TPU v7x, 32 devices: a whole 2x2x4 slice. The times are simulated.
32 devices in a mesh: ctx: 8 (over z, y), head: 4 (over x, core).
Axes of the slice: x: 2, y: 2, z: 4, core: 2. Of those that a mesh axis runs over, the one named last changes fastest.
Arguments:
- query_input: bfloat16 [2048, 4096], P('ctx', 'head'), may hold values from -6 to 6
- key_entries_raw: bfloat16 [2048, 1024], P('ctx', 'head'), may hold values from -6 to 6
- value_entries_raw: bfloat16 [2048, 1024], P('ctx', 'head'), may hold values from -6 to 6
- out_grad: bfloat16 [2048, 4096], P('ctx', 'head'), may hold values from -6 to 6
- attn_out: bfloat16 [2048, 4096], P('ctx', 'head'), may hold values from -3 to 3
- log_sum_exp: float32 [32, 2048], P('head', 'ctx'), may hold values from 4 to 6
- positions: int32 [3, 2048], P(None, ('ctx', 'head')), may hold values from 0 to 4095
- span_map: int32 [8], replicated, may hold values from 0 to 7, each once
Outputs:
- query_grad: bfloat16 [2048, 4096], P('ctx', 'head')
- key_gradient_raw: bfloat16 [2048, 1024], P('ctx', 'head')
- value_gradient_rows: bfloat16 [2048, 1024], P('ctx', 'head')
Inputs may be any that keep to these rules, and one draw needn't show every extreme that they name: Block b of 256 rows holds span span_map[b] of the sequence in its first 128 rows and span 2 * 8 - 1 - span_map[b] in its last 128 rows; each number appears once.
All inputs are finite; a program needn't handle non-finite values.
Results may differ from a plain program's by a relative error of at most 0.019.
The roundings to bfloat16 on the way count: a program that leaves them out, or rounds other values in their place, can miss the bound.
Values may be sent and summed in bfloat16 or wider, within the bound.
No kernel may reach another device: no remote copies, remote signals or barrier semaphores. Data moves between devices by JAX's collectives and lax.ppermute only.
A program may use at most 64 MiB of HBM per device.

v0:
```python
import math

import jax
import jax.numpy as jnp
from jax import lax
from jax.sharding import PartitionSpec as P

HEAD_ENTRIES = 128
WIN = 4


ROPE_BASE = 1000000.0
YARN_FACTOR = 4.0
YARN_INITIAL = 32768.0
BETA_FAST = 32.0
BETA_SLOW = 1.0
YARN_MSCALE = 1.0 + 0.1 * math.log(4.0)


def shifted(value, axis, steps):
    count = lax.axis_size(axis)
    pairs = [(source, (source + steps) % count) for source in range(count)]
    return lax.ppermute(value, axis, pairs)


def rope_tables(positions, head_width):
    half_width = head_width // 2
    pair_index = jnp.arange(half_width, dtype=jnp.float32)
    inverse = jnp.exp(-2.0 * pair_index / head_width * math.log(ROPE_BASE))
    ratio_value = YARN_INITIAL * inverse / (2.0 * math.pi)
    ramp_value = jnp.clip((ratio_value - BETA_SLOW) / (BETA_FAST - BETA_SLOW), 0.0, 1.0)
    frequency = inverse * ((1.0 - ramp_value) / YARN_FACTOR + ramp_value)
    first_cut = head_width // 8
    second_cut = first_cut + 3 * head_width // 16
    spot_values = positions.astype(jnp.float32)
    chosen = jnp.where(
        pair_index < first_cut,
        spot_values[0][:, None],
        jnp.where(pair_index < second_cut, spot_values[1][:, None], spot_values[2][:, None]),
    )
    angles = chosen * frequency
    return (jnp.cos(angles) * YARN_MSCALE, jnp.sin(angles) * YARN_MSCALE)


def apply_rotary(block_rows, cosine_lookup, sine_lookup):
    half_width = block_rows.shape[-1] // 2
    widened = block_rows.astype(jnp.float32)
    first_half = widened[..., :half_width]
    second_half = widened[..., half_width:]
    cosine_rows = cosine_lookup[:, None, :]
    sine_rows = sine_lookup[:, None, :]
    return jnp.concatenate(
        [
            first_half * cosine_rows - second_half * sine_rows,
            second_half * cosine_rows + first_half * sine_rows,
        ],
        axis=-1,
    )


def reverse_rotary(gradient, cosine_lookup, sine_lookup):
    half_width = gradient.shape[-1] // 2
    first_half = gradient[..., :half_width]
    second_half = gradient[..., half_width:]
    cosine_rows = cosine_lookup[:, None, :]
    sine_rows = sine_lookup[:, None, :]
    return jnp.concatenate(
        [
            first_half * cosine_rows + second_half * sine_rows,
            second_half * cosine_rows - first_half * sine_rows,
        ],
        axis=-1,
    )


def slot_order(span_map, slot_index, span_len, cycle_size):
    early_span = span_map[slot_index]
    late_span = 2 * cycle_size - 1 - early_span
    offsets = jnp.arange(span_len, dtype=jnp.int32)
    return jnp.concatenate([early_span * span_len + offsets, late_span * span_len + offsets])


def block_grads(query_side, key_side, query_order, key_order):
    query_rotated, grad_heads, norm_rows, delta_rows = query_side
    key_turned, value_head_split = key_side
    row_count = query_rotated.shape[0]
    key_heads = key_turned.shape[1]
    head_width = key_turned.shape[2]
    group_size = query_rotated.shape[1] // key_heads
    root_scale = 1.0 / math.sqrt(head_width)
    query_groups = query_rotated.reshape(row_count, key_heads, group_size, head_width)
    grad_groups = grad_heads.reshape(row_count, key_heads, group_size, head_width)
    scores = (
        jnp.einsum("qgjd,kgd->gjqk", query_groups, key_turned, preferred_element_type=jnp.float32)
        * root_scale
    )
    visible = key_order[None, :] <= query_order[:, None]
    norm_table = norm_rows.reshape(key_heads, group_size, row_count)[..., None]
    weights = jnp.where(visible, jnp.exp(scores - norm_table), 0.0)
    rounded_weights = weights.astype(jnp.bfloat16)
    value_part = jnp.einsum(
        "gjqk,qgjd->kgd", rounded_weights, grad_groups, preferred_element_type=jnp.float32
    )
    weight_grad = jnp.einsum(
        "qgjd,kgd->gjqk", grad_groups, value_head_split, preferred_element_type=jnp.float32
    )
    score_grad = weights * (
        weight_grad - delta_rows.reshape(key_heads, group_size, row_count)[..., None]
    )
    rounded_grad = score_grad.astype(jnp.bfloat16)
    key_part = (
        jnp.einsum("gjqk,qgjd->kgd", rounded_grad, query_groups, preferred_element_type=jnp.float32)
        * root_scale
    )
    query_part = jnp.einsum(
        "gjqk,kgd->qgjd", rounded_grad, key_turned, preferred_element_type=jnp.float32
    )
    query_part = query_part.reshape(row_count, key_heads * group_size, head_width) * root_scale
    return (query_part, key_part, value_part)


def pair_grads(query_side, key_side, query_order, key_order):
    pieces = block_grads(query_side, key_side, query_order, key_order)
    return pieces


def shards(
    query_input,
    key_entries_raw,
    value_entries_raw,
    out_grad,
    attn_out,
    log_sum_exp,
    positions,
    span_map,
):
    row_count = query_input.shape[0]
    span_len = row_count // 2
    query_heads = query_input.shape[1] // HEAD_ENTRIES
    key_heads = key_entries_raw.shape[1] // HEAD_ENTRIES
    cycle_size = lax.axis_size("ctx")
    self_slot = lax.axis_index("ctx")
    placed = lax.all_gather(positions, "head", axis=1, tiled=True)
    cosine_lookup, sine_lookup = rope_tables(placed, HEAD_ENTRIES)
    query_rotated = apply_rotary(
        query_input.reshape(row_count, query_heads, HEAD_ENTRIES), cosine_lookup, sine_lookup
    ).astype(jnp.bfloat16)
    key_turned = apply_rotary(
        key_entries_raw.reshape(row_count, key_heads, HEAD_ENTRIES), cosine_lookup, sine_lookup
    ).astype(jnp.bfloat16)
    value_head_split = value_entries_raw.reshape(row_count, key_heads, HEAD_ENTRIES)
    grad_heads = out_grad.reshape(row_count, query_heads, HEAD_ENTRIES)
    delta_rows = jnp.sum(
        grad_heads.astype(jnp.float32)
        * attn_out.reshape(row_count, query_heads, HEAD_ENTRIES).astype(jnp.float32),
        axis=2,
    ).T
    self_order = slot_order(span_map, self_slot, span_len, cycle_size)
    moving_query = query_rotated
    moving_grad = grad_heads
    moving_norm = log_sum_exp
    moving_delta = delta_rows
    carried = jnp.zeros((row_count, query_heads, HEAD_ENTRIES), jnp.float32)
    key_overall = jnp.zeros((row_count, key_heads, HEAD_ENTRIES), jnp.float32)
    value_overall = jnp.zeros((row_count, key_heads, HEAD_ENTRIES), jnp.float32)
    for hop_index in range(WIN):
        if hop_index > 0:
            moving_query, moving_grad = shifted((moving_query, moving_grad), "ctx", 1)
            carried, moving_norm, moving_delta = shifted(
                (carried, moving_norm, moving_delta), "ctx", 1
            )
        source = (self_slot - hop_index) % cycle_size
        source_order = slot_order(span_map, source, span_len, cycle_size)
        pieces = pair_grads(
            (moving_query, moving_grad, moving_norm, moving_delta),
            (key_turned, value_head_split),
            source_order,
            self_order,
        )
        carried = carried + pieces[0]
        key_overall = key_overall + pieces[1]
        value_overall = value_overall + pieces[2]
    query_total = shifted(carried, "ctx", 1 - WIN)
    query_grad = (
        reverse_rotary(query_total, cosine_lookup, sine_lookup)
        .reshape(row_count, query_heads * HEAD_ENTRIES)
        .astype(jnp.bfloat16)
    )
    key_gradient_raw = (
        reverse_rotary(key_overall, cosine_lookup, sine_lookup)
        .reshape(row_count, key_heads * HEAD_ENTRIES)
        .astype(jnp.bfloat16)
    )
    value_gradient_rows = value_overall.reshape(row_count, key_heads * HEAD_ENTRIES).astype(
        jnp.bfloat16
    )
    return (query_grad, key_gradient_raw, value_gradient_rows)


def solution(mesh):
    placed = (
        P("ctx", "head"),
        P("ctx", "head"),
        P("ctx", "head"),
        P("ctx", "head"),
        P("ctx", "head"),
        P("head", "ctx"),
        P(None, ("ctx", "head")),
        P(),
    )
    return jax.shard_map(
        shards,
        mesh=mesh,
        in_specs=placed,
        out_specs=(P("ctx", "head"), P("ctx", "head"), P("ctx", "head")),
        check_vma=False,
    )
```

profile of v0, /device:TPU:31, one launch (start us, length us, event | category | flops | bytes accessed | tf_op | source)
XLA Modules:
  0.0 221.6 jit_solution(8977998842255187050)
XLA Ops:
  0.7 1.9 copy.332
  5.1 2.1 multiply_reduce_fusion
  8.5 6.5 %all-gather = s32[4,64,3]{1,2,0:T(4,128)S(1)} all-gather(s32[1,64,3]{1,2,0:T(4,128)S(1)} %bitcast.243), channel_id=1, replica_groups=mesh['ctx'=8,'head'=4] {'head'}, dimensions={0}, use_global_device_ids=true | all-gather | bytes 3840 | tf_op jit(solution)/shard_map/all_gather | solution.py:143
  32.3 1.4 convolution_multiply_fusion.3
  33.7 2.5 %copy.220 = f32[256,8,128]{2,0,1:T(8,128)} copy(f32[256,8,128]{0,2,1:T(8,128)} %bitcast.221) | data formatting | bytes 2097152 | tf_op jit(solution)/shard_map/mul | solution.py:118
  40.0 2.3 %convolution_bitcast_fusion.7 = f32[2,256,128]{1,2,0:T(8,128)} fusion(bf16[256,2,4,128]{0,3,2,1:T(8,128)(2,1)} %bitcast.218, f32[2,4,256,256]{2,3,1,0:T(8,128)S(1)} %fusion.15), kind=kOutput, calls=%fused_computation.38 | convolution fusion | flops 134742016 | bytes 2883584 | tf_op jit(solution)/shard_map/gjqk,qgjd->kgd/dot_general | solution.py:101
  42.3 18.7 %collective-permute-done.7 = f32[8,256]{1,0:T(8,128)S(1)} collective-permute-done((f32[8,256]{1,0:T(8,128)}, f32[8,256]{1,0:T(8,128)S(1)}, u32[]{:S(2)}, u32[]{:S(2)}) %collective-permute-start.7) | collective-permute-done | bytes 8224 | tf_op jit(solution)/shard_map/ppermute | solution.py:23
  61.0 3.9 %collective-permute-start.12 = (f32[8,256]{1,0:T(8,128)S(1)}, f32[8,256]{1,0:T(8,128)S(1)}, u32[]{:S(2)}, u32[]{:S(2)}) collective-permute-start(f32[8,256]{1,0:T(8,128)S(1)} %collective-permute-done.7), channel_id=1, source_target_pairs={{0,4},{4,8},{8,12},{12,16},{16,20},{20,24},{24,28},{28,0},{1,5},{5... | collective-permute-start | bytes 24584 | tf_op jit(solution)/shard_map/ppermute | solution.py:23
  64.9 2.8 %collective-permute-start.14 = (f32[8,256]{0,1:T(8,128)}, f32[8,256]{0,1:T(8,128)S(1)}, u32[]{:S(2)}, u32[]{:S(2)}) collective-permute-start(f32[8,256]{0,1:T(8,128)} %collective-permute-done.9), channel_id=1, source_target_pairs={{0,4},{4,8},{8,12},{12,16},{16,20},{20,24},{24,28},{28,0},{1,5},{5... | collective-permute-start | bytes 24584 | tf_op jit(solution)/shard_map/ppermute | solution.py:23
  73.0 1.5 fusion.69
  74.5 1.5 copy.221
  77.5 1.6 collective-permute-start.8
  79.2 3.2 %fusion.19 = f32[2,256,128]{1,2,0:T(8,128)} fusion(f32[2,256,128]{1,2,0:T(8,128)} %convolution_bitcast_fusion.7, bf16[256,2,4,128]{3,0,2,1:T(8,128)(2,1)} %bitcast.232, f32[2,256,256,4]{2,1,3,0:T(8,128)} %copy-done.7, f32[2,4,256]{2,1,0:T(4,128)} %copy-done.36, pred[256,256]{0,1:T(8,128)(4,1)} %get-tuple-element.36), kind=kOutput, calls=%fused_computation.39 | convolution fusion | flops 136380416 | bytes 3219456 | tf_op jit(solution)/shard_map/gjqk,qgjd->kgd/dot_general | solution.py:101
  82.4 2.4 %add.170 = f32[256,8,128]{2,0,1:T(8,128)} add(f32[256,8,128]{2,0,1:T(8,128)} %collective-permute-done, f32[256,8,128]{2,0,1:T(8,128)S(1)} %copy.226) | non-fusion elementwise | flops 262144 | bytes 3145728 | tf_op jit(solution)/shard_map/add | solution.py:180
  84.7 2.2 fusion.22
  86.9 2.8 %collective-permute-done.8 = bf16[256,8,128]{2,1,0:T(8,128)(2,1)} collective-permute-done((bf16[256,8,128]{2,1,0:T(8,128)(2,1)}, bf16[256,8,128]{2,1,0:T(8,128)(2,1)}, u32[]{:S(2)}, u32[]{:S(2)}) %collective-permute-start.8) | collective-permute-done | bytes 524320 | tf_op jit(solution)/shard_map/ppermute | solution.py:23
  90.8 3.4 %collective-permute-start.13 = (bf16[256,8,128]{2,1,0:T(8,128)(2,1)}, bf16[256,8,128]{2,1,0:T(8,128)(2,1)}, u32[]{:S(2)}, u32[]{:S(2)}) collective-permute-start(bf16[256,8,128]{2,1,0:T(8,128)(2,1)} %collective-permute-done.8), channel_id=1, source_target_pairs={{0,4},{4,8},{8,12},{12,16},{16,20},{20,24},{24,28},{28,0},{1,5},{5... | collective-permute-start | bytes 1572872 | tf_op jit(solution)/shard_map/ppermute | solution.py:23
  94.3 6.7 %collective-permute-done.6 = bf16[256,8,128]{2,0,1:T(8,128)(2,1)} collective-permute-done((bf16[256,8,128]{2,0,1:T(8,128)(2,1)}, bf16[256,8,128]{2,0,1:T(8,128)(2,1)}, u32[]{:S(2)}, u32[]{:S(2)}) %collective-permute-start.6) | collective-permute-done | bytes 524320 | tf_op jit(solution)/shard_map/ppermute | solution.py:23
  100.9 3.4 %collective-permute-start.11 = (bf16[256,8,128]{2,0,1:T(8,128)(2,1)}, bf16[256,8,128]{2,0,1:T(8,128)(2,1)}, u32[]{:S(2)}, u32[]{:S(2)}) collective-permute-start(bf16[256,8,128]{2,0,1:T(8,128)(2,1)} %collective-permute-done.6), channel_id=1, source_target_pairs={{0,4},{4,8},{8,12},{12,16},{16,20},{20,24},{24,28},{28,0},{1,5},{5... | collective-permute-start | bytes 1572872 | tf_op jit(solution)/shard_map/ppermute | solution.py:23
  104.3 1.5 fusion.70
  107.9 15.5 %collective-permute-done.5 = f32[256,8,128]{2,0,1:T(8,128)} collective-permute-done((f32[256,8,128]{2,0,1:T(8,128)}, f32[256,8,128]{2,0,1:T(8,128)}, u32[]{:S(2)}, u32[]{:S(2)}) %collective-permute-start.5) | collective-permute-done | bytes 1048608 | tf_op jit(solution)/shard_map/ppermute | solution.py:23
  123.4 2.3 %add.177 = f32[256,8,128]{2,0,1:T(8,128)} add(f32[256,8,128]{2,0,1:T(8,128)} %collective-permute-done.5, f32[256,8,128]{2,0,1:T(8,128)S(1)} %copy.232) | non-fusion elementwise | flops 262144 | bytes 3145728 | tf_op jit(solution)/shard_map/add | solution.py:180
  125.7 3.4 %collective-permute-start.10 = (f32[256,8,128]{2,0,1:T(8,128)}, f32[256,8,128]{2,0,1:T(8,128)}, u32[]{:S(2)}, u32[]{:S(2)}) collective-permute-start(f32[256,8,128]{2,0,1:T(8,128)} %add.177), channel_id=1, source_target_pairs={{0,4},{4,8},{8,12},{12,16},{16,20},{20,24},{24,28},{28,0},{1,5},{5... | collective-permute-start | bytes 3145736 | tf_op jit(solution)/shard_map/ppermute | solution.py:23
  130.5 4.1 %collective-permute-done.13 = bf16[256,8,128]{2,1,0:T(8,128)(2,1)} collective-permute-done((bf16[256,8,128]{2,1,0:T(8,128)(2,1)}, bf16[256,8,128]{2,1,0:T(8,128)(2,1)}, u32[]{:S(2)}, u32[]{:S(2)}) %collective-permute-start.13) | collective-permute-done | bytes 524320 | tf_op jit(solution)/shard_map/ppermute | solution.py:23
  135.8 10.1 %collective-permute-done.11 = bf16[256,8,128]{2,0,1:T(8,128)(2,1)} collective-permute-done((bf16[256,8,128]{2,0,1:T(8,128)(2,1)}, bf16[256,8,128]{2,0,1:T(8,128)(2,1)}, u32[]{:S(2)}, u32[]{:S(2)}) %collective-permute-start.11) | collective-permute-done | bytes 524320 | tf_op jit(solution)/shard_map/ppermute | solution.py:23
  145.9 1.5 fusion.71
  150.1 1.5 copy.238
  151.6 16.7 %collective-permute-done.10 = f32[256,8,128]{2,0,1:T(8,128)} collective-permute-done((f32[256,8,128]{2,0,1:T(8,128)}, f32[256,8,128]{2,0,1:T(8,128)}, u32[]{:S(2)}, u32[]{:S(2)}) %collective-permute-start.10) | collective-permute-done | bytes 1048608 | tf_op jit(solution)/shard_map/ppermute | solution.py:23
  168.3 2.3 %add.184 = f32[256,8,128]{2,0,1:T(8,128)} add(f32[256,8,128]{2,0,1:T(8,128)} %collective-permute-done.10, f32[256,8,128]{2,0,1:T(8,128)S(1)} %copy.238) | non-fusion elementwise | flops 262144 | bytes 3145728 | tf_op jit(solution)/shard_map/add | solution.py:180
  170.7 2.2 fusion.23
  174.2 1.5 fusion.26
  176.9 43.2 %collective-permute-done.15 = f32[256,8,128]{2,0,1:T(8,128)S(1)} collective-permute-done((f32[256,8,128]{2,0,1:T(8,128)}, f32[256,8,128]{2,0,1:T(8,128)S(1)}, u32[]{:S(2)}, u32[]{:S(2)}) %collective-permute-start.15) | collective-permute-done | bytes 1048608 | tf_op jit(solution)/shard_map/ppermute | solution.py:23
  (165 shorter events, 37.4 us)
Async XLA Ops:
  0.6 36.9 %collective-permute-start.2 = (f32[8,256]{1,0:T(8,128)}, f32[8,256]{1,0:T(8,128)}, u32[]{:S(2)}, u32[]{:S(2)}) collective-permute-start(f32[8,256]{1,0:T(8,128)} %param.13), channel_id=1, source_target_pairs={{0,4},{4,8},{8,12},{12,16},{16,20},{20,24},{24,28},{28,0},{1,5},{5... | collective-permute-start | bytes 24584 | tf_op jit(solution)/shard_map/ppermute | solution.py:23
  2.6 71.8 %collective-permute-start.3 = (bf16[256,8,128]{2,1,0:T(8,128)(2,1)}, bf16[256,8,128]{2,1,0:T(8,128)(2,1)}, u32[]{:S(2)}, u32[]{:S(2)}) collective-permute-start(bf16[256,8,128]{2,1,0:T(8,128)(2,1)} %bitcast.91), channel_id=1, source_target_pairs={{0,4},{4,8},{8,12},{12,16},{16,20},{20,24},{24,28},{28,0},{1,5},{5... | collective-permute-start | bytes 1572872 | tf_op jit(solution)/shard_map/ppermute | solution.py:23
  7.2 31.6 %collective-permute-start.4 = (f32[8,256]{0,1:T(8,128)}, f32[8,256]{0,1:T(8,128)}, u32[]{:S(2)}, u32[]{:S(2)}) collective-permute-start(f32[8,256]{0,1:T(8,128)} %bitcast.20), channel_id=1, source_target_pairs={{0,4},{4,8},{8,12},{12,16},{16,20},{20,24},{24,28},{28,0},{1,5},{5... | collective-permute-start | bytes 24584 | tf_op jit(solution)/shard_map/ppermute | solution.py:23
  17.9 55.1 %collective-permute-start.1 = (bf16[256,8,128]{2,0,1:T(8,128)(2,1)}, bf16[256,8,128]{2,0,1:T(8,128)(2,1)}, u32[]{:S(2)}, u32[]{:S(2)}) collective-permute-start(bf16[256,8,128]{2,0,1:T(8,128)(2,1)} %pad_maximum_fusion.1), channel_id=1, source_target_pairs={{0,4},{4,8},{8,12},{12,16},{16,20},{20,24},{24,28},{28,0},{1,5},{5... | collective-permute-start | bytes 1572872 | tf_op jit(solution)/shard_map/ppermute | solution.py:23
  36.3 31.5 %copy-start.1 = (bf16[256,8,64]{2,0,1:T(8,128)(2,1)S(1)}, bf16[256,8,64]{2,0,1:T(8,128)(2,1)}, u32[]{:S(2)}) copy-start(bf16[256,8,64]{2,0,1:T(8,128)(2,1)} %copy-done) | copy-start | bytes 786436
  36.3 31.5 %copy-start.3 = (bf16[256,8,64]{2,0,1:T(8,128)(2,1)S(1)}, bf16[256,8,64]{2,0,1:T(8,128)(2,1)}, u32[]{:S(2)}) copy-start(bf16[256,8,64]{2,0,1:T(8,128)(2,1)} %copy-done.2) | copy-start | bytes 786436
  36.3 46.1 %collective-permute-start = (f32[256,8,128]{2,0,1:T(8,128)}, f32[256,8,128]{2,0,1:T(8,128)}, u32[]{:S(2)}, u32[]{:S(2)}) collective-permute-start(f32[256,8,128]{2,0,1:T(8,128)} %copy.220), channel_id=1, source_target_pairs={{0,4},{4,8},{8,12},{12,16},{16,20},{20,24},{24,28},{28,0},{1,5},{5... | collective-permute-start | bytes 3145736 | tf_op jit(solution)/shard_map/ppermute | solution.py:23
  37.5 23.5 %collective-permute-start.7 = (f32[8,256]{1,0:T(8,128)}, f32[8,256]{1,0:T(8,128)S(1)}, u32[]{:S(2)}, u32[]{:S(2)}) collective-permute-start(f32[8,256]{1,0:T(8,128)} %collective-permute-done.2), channel_id=1, source_target_pairs={{0,4},{4,8},{8,12},{12,16},{16,20},{20,24},{24,28},{28,0},{1,5},{5... | collective-permute-start | bytes 24584 | tf_op jit(solution)/shard_map/ppermute | solution.py:23
  38.7 26.2 %collective-permute-start.9 = (f32[8,256]{0,1:T(8,128)}, f32[8,256]{0,1:T(8,128)}, u32[]{:S(2)}, u32[]{:S(2)}) collective-permute-start(f32[8,256]{0,1:T(8,128)} %collective-permute-done.4), channel_id=1, source_target_pairs={{0,4},{4,8},{8,12},{12,16},{16,20},{20,24},{24,28},{28,0},{1,5},{5... | collective-permute-start | bytes 24584 | tf_op jit(solution)/shard_map/ppermute | solution.py:23
  61.0 12.0 %collective-permute-start.12 = (f32[8,256]{1,0:T(8,128)S(1)}, f32[8,256]{1,0:T(8,128)S(1)}, u32[]{:S(2)}, u32[]{:S(2)}) collective-permute-start(f32[8,256]{1,0:T(8,128)S(1)} %collective-permute-done.7), channel_id=1, source_target_pairs={{0,4},{4,8},{8,12},{12,16},{16,20},{20,24},{24,28},{28,0},{1,5},{5... | collective-permute-start | bytes 24584 | tf_op jit(solution)/shard_map/ppermute | solution.py:23
  64.9 8.0 %collective-permute-start.14 = (f32[8,256]{0,1:T(8,128)}, f32[8,256]{0,1:T(8,128)S(1)}, u32[]{:S(2)}, u32[]{:S(2)}) collective-permute-start(f32[8,256]{0,1:T(8,128)} %collective-permute-done.9), channel_id=1, source_target_pairs={{0,4},{4,8},{8,12},{12,16},{16,20},{20,24},{24,28},{28,0},{1,5},{5... | collective-permute-start | bytes 24584 | tf_op jit(solution)/shard_map/ppermute | solution.py:23
  77.5 12.2 %collective-permute-start.8 = (bf16[256,8,128]{2,1,0:T(8,128)(2,1)}, bf16[256,8,128]{2,1,0:T(8,128)(2,1)}, u32[]{:S(2)}, u32[]{:S(2)}) collective-permute-start(bf16[256,8,128]{2,1,0:T(8,128)(2,1)} %collective-permute-done.3), channel_id=1, source_target_pairs={{0,4},{4,8},{8,12},{12,16},{16,20},{20,24},{24,28},{28,0},{1,5},{5... | collective-permute-start | bytes 1572872 | tf_op jit(solution)/shard_map/ppermute | solution.py:23
  79.1 21.8 %collective-permute-start.6 = (bf16[256,8,128]{2,0,1:T(8,128)(2,1)}, bf16[256,8,128]{2,0,1:T(8,128)(2,1)}, u32[]{:S(2)}, u32[]{:S(2)}) collective-permute-start(bf16[256,8,128]{2,0,1:T(8,128)(2,1)} %collective-permute-done.1), channel_id=1, source_target_pairs={{0,4},{4,8},{8,12},{12,16},{16,20},{20,24},{24,28},{28,0},{1,5},{5... | collective-permute-start | bytes 1572872 | tf_op jit(solution)/shard_map/ppermute | solution.py:23
  84.7 38.7 %collective-permute-start.5 = (f32[256,8,128]{2,0,1:T(8,128)}, f32[256,8,128]{2,0,1:T(8,128)}, u32[]{:S(2)}, u32[]{:S(2)}) collective-permute-start(f32[256,8,128]{2,0,1:T(8,128)} %add.170), channel_id=1, source_target_pairs={{0,4},{4,8},{8,12},{12,16},{16,20},{20,24},{24,28},{28,0},{1,5},{5... | collective-permute-start | bytes 3145736 | tf_op jit(solution)/shard_map/ppermute | solution.py:23
  86.9 18.9 %copy-start.22 = (bf16[256,2,128]{2,1,0:T(2,128)(2,1)S(1)}, bf16[256,2,128]{2,1,0:T(2,128)(2,1)}, u32[]{:S(2)}) copy-start(bf16[256,2,128]{2,1,0:T(2,128)(2,1)} %reshape.264) | copy-start | bytes 393220
  86.9 18.9 %copy-start.27 = (pred[256,256]{0,1:T(8,128)(4,1)S(1)}, pred[256,256]{0,1:T(8,128)(4,1)}, u32[]{:S(2)}) copy-start(pred[256,256]{0,1:T(8,128)(4,1)} %get-tuple-element.37) | copy-start | bytes 196612
  86.9 19.0 %copy-start.32 = (f32[2,4,256]{2,1,0:T(4,128)S(1)}, f32[2,4,256]{2,1,0:T(4,128)}, u32[]{:S(2)}) copy-start(f32[2,4,256]{2,1,0:T(4,128)} %sub.153) | copy-start | bytes 24580
  86.9 19.0 %copy-start.35 = (f32[2,4,256]{2,1,0:T(4,128)S(1)}, f32[2,4,256]{2,1,0:T(4,128)}, u32[]{:S(2)}) copy-start(f32[2,4,256]{2,1,0:T(4,128)} %sub.156) | copy-start | bytes 24580
  90.8 43.8 %collective-permute-start.13 = (bf16[256,8,128]{2,1,0:T(8,128)(2,1)}, bf16[256,8,128]{2,1,0:T(8,128)(2,1)}, u32[]{:S(2)}, u32[]{:S(2)}) collective-permute-start(bf16[256,8,128]{2,1,0:T(8,128)(2,1)} %collective-permute-done.8), channel_id=1, source_target_pairs={{0,4},{4,8},{8,12},{12,16},{16,20},{20,24},{24,28},{28,0},{1,5},{5... | collective-permute-start | bytes 1572872 | tf_op jit(solution)/shard_map/ppermute | solution.py:23
  100.9 44.9 %collective-permute-start.11 = (bf16[256,8,128]{2,0,1:T(8,128)(2,1)}, bf16[256,8,128]{2,0,1:T(8,128)(2,1)}, u32[]{:S(2)}, u32[]{:S(2)}) collective-permute-start(bf16[256,8,128]{2,0,1:T(8,128)(2,1)} %collective-permute-done.6), channel_id=1, source_target_pairs={{0,4},{4,8},{8,12},{12,16},{16,20},{20,24},{24,28},{28,0},{1,5},{5... | collective-permute-start | bytes 1572872 | tf_op jit(solution)/shard_map/ppermute | solution.py:23
  107.9 21.2 %copy-start.9 = (f32[2,256,256,4]{2,1,3,0:T(8,128)S(1)}, f32[2,256,256,4]{2,1,3,0:T(8,128)}, u32[]{:S(2)}) copy-start(f32[2,256,256,4]{2,1,3,0:T(8,128)} %copy-done.8) | copy-start | bytes 6291460
  107.9 21.2 %copy-start.16 = (bf16[256,8,128]{2,0,1:T(8,128)(2,1)S(1)}, bf16[256,8,128]{2,0,1:T(8,128)(2,1)}, u32[]{:S(2)}) copy-start(bf16[256,8,128]{2,0,1:T(8,128)(2,1)} %copy-done.15) | copy-start | bytes 1572868
  107.9 21.2 %copy-start.28 = (pred[256,256]{0,1:T(8,128)(4,1)S(1)}, pred[256,256]{0,1:T(8,128)(4,1)}, u32[]{:S(2)}) copy-start(pred[256,256]{0,1:T(8,128)(4,1)} %get-tuple-element.37) | copy-start | bytes 196612
  107.9 21.2 %copy-start.33 = (f32[2,4,256]{2,1,0:T(4,128)S(1)}, f32[2,4,256]{2,1,0:T(4,128)}, u32[]{:S(2)}) copy-start(f32[2,4,256]{2,1,0:T(4,128)} %sub.153) | copy-start | bytes 24580
  107.9 21.2 %copy-start.38 = (f32[2,256,128]{1,2,0:T(8,128)S(1)}, f32[2,256,128]{1,2,0:T(8,128)}, u32[]{:S(2)}) copy-start(f32[2,256,128]{1,2,0:T(8,128)} %fusion.19) | copy-start | bytes 786436
  125.7 42.6 %collective-permute-start.10 = (f32[256,8,128]{2,0,1:T(8,128)}, f32[256,8,128]{2,0,1:T(8,128)}, u32[]{:S(2)}, u32[]{:S(2)}) collective-permute-start(f32[256,8,128]{2,0,1:T(8,128)} %add.177), channel_id=1, source_target_pairs={{0,4},{4,8},{8,12},{12,16},{16,20},{20,24},{24,28},{28,0},{1,5},{5... | collective-permute-start | bytes 3145736 | tf_op jit(solution)/shard_map/ppermute | solution.py:23
  130.5 16.9 %copy-start.26 = (pred[256,256]{0,1:T(8,128)(4,1)S(1)}, pred[256,256]{0,1:T(8,128)(4,1)}, u32[]{:S(2)}) copy-start(pred[256,256]{0,1:T(8,128)(4,1)} %get-tuple-element.35) | copy-start | bytes 196612
  151.6 19.1 %copy-start.12 = (f32[2,128,256]{1,2,0:T(8,128)S(1)}, f32[2,128,256]{1,2,0:T(8,128)}, u32[]{:S(2)}) copy-start(f32[2,128,256]{1,2,0:T(8,128)} %fusion.22) | copy-start | bytes 786436
  151.6 21.2 %copy-start.6 = (f32[2,256,256,4]{2,1,3,0:T(8,128)S(1)}, f32[2,256,256,4]{2,1,3,0:T(8,128)}, u32[]{:S(2)}) copy-start(f32[2,256,256,4]{2,1,3,0:T(8,128)} %copy-done.5) | copy-start | bytes 6291460
  151.6 21.2 %copy-start.18 = (bf16[256,8,128]{2,0,1:T(8,128)(2,1)S(1)}, bf16[256,8,128]{2,0,1:T(8,128)(2,1)}, u32[]{:S(2)}) copy-start(bf16[256,8,128]{2,0,1:T(8,128)(2,1)} %copy-done.17) | copy-start | bytes 1572868
  151.6 21.2 %copy-start.39 = (f32[2,256,128]{1,2,0:T(8,128)S(1)}, f32[2,256,128]{1,2,0:T(8,128)}, u32[]{:S(2)}) copy-start(f32[2,256,128]{1,2,0:T(8,128)} %fusion.20) | copy-start | bytes 786436
  170.7 49.4 %collective-permute-start.15 = (f32[256,8,128]{2,0,1:T(8,128)}, f32[256,8,128]{2,0,1:T(8,128)S(1)}, u32[]{:S(2)}, u32[]{:S(2)}) collective-permute-start(f32[256,8,128]{2,0,1:T(8,128)} %add.184), channel_id=1, source_target_pairs={{0,20},{4,24},{8,28},{12,0},{16,4},{20,8},{24,12},{28,16},{1,21},{... | collective-permute-start | bytes 3145736 | tf_op jit(solution)/shard_map/ppermute | solution.py:23
  (24 other events, 169.6 us)
where the time goes:
time: 223 us; the launch traced here: 222 us
  waiting for transfers between devices  118 us (53%)
  starting transfers between devices  26 us (12%)
  matrix products  25.7 us (12%)
  local copies, waits for them, and re-layouts  22.5 us (10%)
  other arithmetic  15.4 us (7%)
  between operations  7.7 us (3%)
  blocking collectives  6.47 us (3%)
    ppermute x16, waiting for transfers between devices, shifted(): return lax.ppermute(value, axis, pairs)  118 us
    ppermute x16, starting transfers between devices, shifted(): return lax.ppermute(value, axis, pairs)  26 us
    dot_general x4, matrix products, block_grads(): jnp.einsum('gjqk,qgjd->kgd', rounded_weights, grad_groups, preferred_elem...  7.43 us
    dot_general x4, matrix products, block_grads(): jnp.einsum('gjqk,qgjd->kgd', rounded_grad, query_groups, preferred_elemen...  7.03 us
    add x3, other arithmetic, shards(): carried = carried + pieces[0]  6.97 us
    all_gather x1, blocking collectives, shards(): placed = lax.all_gather(positions, 'head', axis=1, tiled=True)  6.47 us
    ppermute x6, local copies, waits for them, and re-layouts, shifted(): return lax.ppermute(value, axis, pairs)  5.72 us
    unnamed x88, local copies, waits for them, and re-layouts  5.56 us
  transfers between devices with their start and end apart: 16, of which 8 were waited for; matrix products, arithmetic and copies ran while one was open for 26% of the time, Pallas kernels for 0%

commit v1 on v0

v1 whole, which is shorter than its diff:
```python
import functools
import math

import jax
import jax.numpy as jnp
import numpy as np
from jax import lax
from jax.experimental import pallas as pl
from jax.experimental.pallas import tpu as pltpu
from jax.sharding import PartitionSpec as P

HEAD = 128
HALF = HEAD // 2
WIN = 4
ROPE_BASE = 1000000.0
YARN_FACTOR = 4.0
YARN_INITIAL = 32768.0
BETA_FAST = 32.0
BETA_SLOW = 1.0
YARN_MSCALE = 1.0 + 0.1 * math.log(4.0)
ROOT_SCALE = 1.0 / math.sqrt(HEAD)
LOG2E = math.log2(math.e)
VMEM_LIMIT = 24 * 1024 * 1024

F32 = jnp.float32
BF16 = jnp.bfloat16


def frequencies():
    pair = np.arange(HALF, dtype=np.float64)
    inverse = np.exp(-2.0 * pair / HEAD * math.log(ROPE_BASE))
    ratio = YARN_INITIAL * inverse / (2.0 * math.pi)
    ramp = np.clip((ratio - BETA_SLOW) / (BETA_FAST - BETA_SLOW), 0.0, 1.0)
    return (inverse * ((1.0 - ramp) / YARN_FACTOR + ramp)).astype(np.float32)


def sine_cosine(angle):
    turns = jnp.floor(angle * (2.0 / math.pi) + 0.5)
    r = angle - turns * 1.5703125
    r = r - turns * 4.837512969970703125e-4
    r = r - turns * 7.54978995489188e-8
    r2 = r * r
    s = r + r * r2 * (-1.6666654611e-1 + r2 * (8.3321608736e-3 - r2 * 1.9515295891e-4))
    c = (
        1.0
        - 0.5 * r2
        + r2
        * r2
        * (4.166664568298827e-2 + r2 * (-1.388731625493765e-3 + r2 * 2.443315711809948e-5))
    )
    quadrant = turns.astype(jnp.int32) & 3
    odd = (quadrant & 1) == 1
    sine = jnp.where(odd, c, s)
    cosine = jnp.where(odd, s, c)
    sine = jnp.where(quadrant >= 2, -sine, sine)
    cosine = jnp.where((quadrant == 1) | (quadrant == 2), -cosine, cosine)
    return sine, cosine


def tables_transposed(place, freq):
    place = place.astype(F32)
    pair = lax.broadcasted_iota(jnp.int32, freq.shape, 0)
    first = HEAD // 8
    second = first + 3 * HEAD // 16
    chosen = jnp.where(
        pair < first, place[0:1], jnp.where(pair < second, place[1:2], place[2:3])
    )
    sine, cosine = sine_cosine(chosen * freq)
    return cosine * YARN_MSCALE, sine * YARN_MSCALE


def row_tables(cosine_t, sine_t):
    wide = jnp.concatenate([cosine_t, cosine_t], axis=0).T
    signed = jnp.concatenate([-sine_t, sine_t], axis=0).T
    return wide, signed


def rotated(x, wide, signed):
    return x * wide + pltpu.roll(x, HALF, 1) * signed


def dot_nt(a, b):
    return lax.dot_general(a, b, (((1,), (1,)), ((), ())), preferred_element_type=F32)


def dot_nn(a, b):
    return lax.dot_general(a, b, (((1,), (0,)), ((), ())), preferred_element_type=F32)


def dot_tn(a, b):
    return lax.dot_general(a, b, (((0,), (0,)), ((), ())), preferred_element_type=F32)


def pair_part(key, value, query, grad, norm, delta, causal):
    scores = dot_nt(key, query)
    weights = jnp.exp2(scores * (ROOT_SCALE * LOG2E) - norm)
    if causal:
        at_key = lax.broadcasted_iota(jnp.int32, scores.shape, 0)
        at_query = lax.broadcasted_iota(jnp.int32, scores.shape, 1)
        weights = jnp.where(at_key <= at_query, weights, 0.0)
    value_part = dot_nn(weights.astype(BF16), grad)
    score_grad = (weights * (dot_nt(value, grad) - delta)).astype(BF16)
    key_part = dot_nn(score_grad, query)
    query_part = dot_tn(key, score_grad)
    return value_part, key_part, query_part


def first_kernel(
    slot_ref, pos_ref, freq_ref, q_ref, k_ref, v_ref, do_ref, at_ref, lse_ref,
    qr_ref, delta_ref, wide_ref, signed_ref, dqt_ref, dkv_ref,
):
    heads = q_ref.shape[1] // HEAD
    groups = k_ref.shape[1] // HEAD
    size = heads // groups
    cosine_t, sine_t = tables_transposed(pos_ref[slot_ref[0]], freq_ref[...])
    wide, signed = row_tables(cosine_t, sine_t)
    wide_ref[...] = wide
    signed_ref[...] = signed
    delta = jnp.zeros(delta_ref.shape, F32)
    which = lax.broadcasted_iota(jnp.int32, (heads, HEAD), 0)
    for h in range(heads):
        cols = pl.ds(h * HEAD, HEAD)
        qr_ref[:, cols] = rotated(q_ref[:, cols].astype(F32), wide, signed).astype(BF16)
        product = do_ref[:, cols].astype(F32) * at_ref[:, cols].astype(F32)
        high = product.astype(BF16)
        low = (product - high.astype(F32)).astype(BF16)
        chooser = jnp.where(which == h, 1.0, 0.0).astype(BF16)
        delta = delta + dot_nt(chooser, high) + dot_nt(chooser, low)
    delta_ref[...] = delta
    norm = lse_ref[...] * LOG2E
    for g in range(groups):
        cols = pl.ds(g * HEAD, HEAD)
        key = rotated(k_ref[:, cols].astype(F32), wide, signed).astype(BF16)
        value = v_ref[:, cols]
        dk = dv = None
        for h in range(g * size, (g + 1) * size):
            hc = pl.ds(h * HEAD, HEAD)
            v_part, k_part, q_part = pair_part(
                key, value, qr_ref[:, hc], do_ref[:, hc], norm[h : h + 1], delta[h : h + 1], True
            )
            dqt_ref[hc, :] = q_part
            dv = v_part if dv is None else dv + v_part
            dk = k_part if dk is None else dk + k_part
        dkv_ref[:, cols] = dk
        dkv_ref[:, pl.ds((groups + g) * HEAD, HEAD)] = dv


def hop_body(
    step, slot_ref, span_ref, pos_ref, freq_ref, kv_ref, qr_ref, do_ref, lse_ref, delta_ref,
    dqt_in, dqt_ref, dkv_ref, key_ref,
):
    rows = qr_ref.shape[0]
    half = rows // 2
    heads = qr_ref.shape[1] // HEAD
    groups = kv_ref.shape[1] // HEAD // 2
    size = heads // groups
    count = span_ref.shape[0]
    me = slot_ref[0]
    other = lax.rem(me + step, count)
    cosine_t, sine_t = tables_transposed(pos_ref[other], freq_ref[...])
    wide, signed = row_tables(cosine_t, sine_t)
    for g in range(groups):
        cols = pl.ds(g * HEAD, HEAD)
        key_ref[:, cols] = rotated(kv_ref[:, cols].astype(F32), wide, signed).astype(BF16)
    earlier = span_ref[other] < span_ref[me]
    norm = lse_ref[...] * LOG2E
    delta = delta_ref[...]

    def run(keys, queries):
        for g in range(groups):
            kc = pl.ds(g * HEAD, HEAD)
            vc = pl.ds((groups + g) * HEAD, HEAD)
            dk = dv = None
            for h in range(g * size, (g + 1) * size):
                hc = pl.ds(h * HEAD, HEAD)
                v_part, k_part, q_part = pair_part(
                    key_ref[keys, kc], kv_ref[keys, vc], qr_ref[queries, hc], do_ref[queries, hc],
                    norm[h : h + 1, queries.start :], delta[h : h + 1, queries.start :], False,
                )
                if queries.start:
                    dqt_ref[hc, : queries.start] = dqt_in[hc, : queries.start]
                dqt_ref[hc, queries] = dqt_in[hc, queries] + q_part
                dv = v_part if dv is None else dv + v_part
                dk = k_part if dk is None else dk + k_part
            dkv_ref[keys, kc] = dk.astype(BF16)
            dkv_ref[keys, vc] = dv.astype(BF16)
        if keys.stop < rows:
            dkv_ref[keys.stop :, :] = jnp.zeros((rows - keys.stop, dkv_ref.shape[1]), BF16)

    @pl.when(earlier)
    def _():
        run(slice(0, half), slice(0, rows))

    @pl.when(jnp.logical_not(earlier))
    def _():
        run(slice(0, rows), slice(half, rows))


def middle_kernel(step, *refs):
    hop_body(step, *refs)


def last_kernel(
    step, slot_ref, span_ref, pos_ref, freq_ref, kv_ref, qr_ref, do_ref, lse_ref, delta_ref,
    dqt_in, out_ref, dkv_ref, key_ref, dqt_ref,
):
    hop_body(
        step, slot_ref, span_ref, pos_ref, freq_ref, kv_ref, qr_ref, do_ref, lse_ref, delta_ref,
        dqt_in, dqt_ref, dkv_ref, key_ref,
    )
    cosine_t, sine_t = tables_transposed(pos_ref[slot_ref[0]], freq_ref[...])
    cosine_t = cosine_t * ROOT_SCALE
    sine_t = sine_t * ROOT_SCALE
    for h in range(qr_ref.shape[1] // HEAD):
        y1 = dqt_ref[pl.ds(h * HEAD, HALF), :]
        y2 = dqt_ref[pl.ds(h * HEAD + HALF, HALF), :]
        turned = jnp.concatenate(
            [y1 * cosine_t + y2 * sine_t, y2 * cosine_t - y1 * sine_t], axis=0
        )
        out_ref[:, pl.ds(h * HEAD, HEAD)] = turned.T.astype(BF16)


def final_kernel(wide_ref, signed_ref, own_ref, a_ref, b_ref, c_ref, dk_ref, dv_ref):
    width = dk_ref.shape[1]
    total = (
        own_ref[...] + a_ref[...].astype(F32) + b_ref[...].astype(F32) + c_ref[...].astype(F32)
    )
    wide = wide_ref[...] * ROOT_SCALE
    signed = signed_ref[...] * -ROOT_SCALE
    for g in range(width // HEAD):
        cols = pl.ds(g * HEAD, HEAD)
        dk_ref[:, cols] = rotated(total[:, g * HEAD : (g + 1) * HEAD], wide, signed).astype(BF16)
    dv_ref[...] = total[:, width:].astype(BF16)


def call(kernel, outs, in_smem, n_in, scratch=(), flops=0, bytes_accessed=0, aliases=None):
    vmem = pl.BlockSpec(memory_space=pltpu.VMEM)
    smem = pl.BlockSpec(memory_space=pltpu.SMEM)
    return pl.pallas_call(
        kernel,
        out_shape=[jax.ShapeDtypeStruct(shape, dtype) for shape, dtype in outs],
        in_specs=[smem] * in_smem + [vmem] * n_in,
        out_specs=[vmem] * len(outs),
        scratch_shapes=list(scratch),
        input_output_aliases=aliases or {},
        compiler_params=pltpu.CompilerParams(vmem_limit_bytes=VMEM_LIMIT),
        cost_estimate=pl.CostEstimate(
            flops=flops, bytes_accessed=bytes_accessed, transcendentals=0
        ),
    )


def shifted(value, steps):
    count = lax.axis_size("ctx")
    pairs = [(source, (source + steps) % count) for source in range(count)]
    return lax.ppermute(value, "ctx", pairs)


def shards(q, k, v, do, at, lse, positions, span_map):
    rows = q.shape[0]
    wide_q = q.shape[1]
    wide_k = k.shape[1]
    heads = wide_q // HEAD
    slots = lax.axis_size("ctx")
    slot = lax.axis_index("ctx").astype(jnp.int32).reshape(1)
    freq = jnp.asarray(np.broadcast_to(frequencies()[:, None], (HALF, rows)).copy())

    kv = jnp.concatenate([k, v], axis=1)
    kv1 = shifted(kv, -1)
    kv2 = shifted(kv, -2)
    gathered = lax.all_gather(positions, ("ctx", "head"), axis=0)
    pos = gathered.reshape(slots, -1, 3, positions.shape[1]).transpose(0, 2, 1, 3)
    pos = pos.reshape(slots, 3, rows)
    kv3 = shifted(kv1, -2)

    flops = 10 * rows * rows * wide_q
    qr, delta, wide, signed, dqt, dkv = call(
        first_kernel,
        [
            ((rows, wide_q), BF16),
            ((heads, rows), F32),
            ((rows, HEAD), F32),
            ((rows, HEAD), F32),
            ((wide_q, rows), F32),
            ((rows, 2 * wide_k), F32),
        ],
        1,
        8,
        flops=flops,
        bytes_accessed=5 << 20,
    )(slot, pos, freq, q, k, v, do, at, lse)

    backs = []
    for step, arrived in ((1, kv1), (2, kv2), (3, kv3)):
        last = step == WIN - 1
        scratch = [pltpu.VMEM((rows, wide_k), BF16)]
        if last:
            scratch.append(pltpu.VMEM((wide_q, rows), F32))
        dqt, part = call(
            functools.partial(last_kernel if last else middle_kernel, step),
            [
                ((rows, wide_q), BF16) if last else ((wide_q, rows), F32),
                ((rows, 2 * wide_k), BF16),
            ],
            2,
            8,
            scratch,
            flops=flops // 2,
            bytes_accessed=4 << 20,
        )(slot, span_map, pos, freq, arrived, qr, do, lse, delta, dqt)
        backs.append(shifted(part, step))

    dk, dv = call(
        final_kernel,
        [((rows, wide_k), BF16), ((rows, wide_k), BF16)],
        0,
        6,
        bytes_accessed=2 << 20,
    )(wide, signed, dkv, *backs)
    return dqt, dk, dv


def solution(mesh):
    placed = (
        P("ctx", "head"),
        P("ctx", "head"),
        P("ctx", "head"),
        P("ctx", "head"),
        P("ctx", "head"),
        P("head", "ctx"),
        P(None, ("ctx", "head")),
        P(),
    )
    return jax.shard_map(
        shards,
        mesh=mesh,
        in_specs=placed,
        out_specs=(P("ctx", "head"), P("ctx", "head"), P("ctx", "head")),
        check_vma=False,
    )
```

time: 223 us -> 97.5 us (0.44)
  the two profiles are of different devices: /device:TPU:31 before, /device:TPU:0 now
where the time goes in v1:
time: 97.5 us; the launch traced here: 97.2 us
  blocking collectives  44.4 us (46%)
  waiting for transfers between devices  27.1 us (28%)
  Pallas kernels  12.5 us (13%)
  starting transfers between devices  7.08 us (7%)
  local copies, waits for them, and re-layouts  5.31 us (5%)
    all_gather x1, blocking collectives, shards(): gathered = lax.all_gather(positions, ('ctx', 'head'), axis=0)  44.4 us
    ppermute x6, waiting for transfers between devices, shifted(): return lax.ppermute(value, 'ctx', pairs)  27.1 us
    pallas_call x3, Pallas kernels, shards(): call(functools.partial(last_kernel if last else middle_kernel, step), [((...  8.39 us
    ppermute x6, starting transfers between devices, shifted(): return lax.ppermute(value, 'ctx', pairs)  7.08 us
    unnamed x17, local copies, waits for them, and re-layouts  5.17 us
    pallas_call x1, Pallas kernels, shards(): call(first_kernel, [((rows, wide_q), BF16), ((heads, rows), F32), ((rows,...  3.24 us
  transfers between devices with their start and end apart: 6, of which 4 were waited for; matrix products, arithmetic and copies ran while one was open for 0% of the time, Pallas kernels for 12%

profile of v1, /device:TPU:0, one launch (start us, length us, event | category | flops | bytes accessed | tf_op | source)
XLA Modules:
  0.0 97.2 jit_solution(8959714893199295001)
XLA Ops:
  0.6 0.0 copy-start.3
  0.6 0.0 copy-start
  0.7 1.0 %constant_dynamic-update-slice_fusion.1 = bf16[256,512]{1,0:T(8,128)(2,1)S(1)} fusion(bf16[256,256]{1,0:T(8,128)(2,1)} %k_ref.1), kind=kLoop, calls=%fused_computation.2 | loop fusion | bytes 262144
  1.6 0.0 copy-done.3
  1.7 6.1 %collective-permute-start = (bf16[256,512]{1,0:T(8,128)(2,1)S(1)}, bf16[256,512]{1,0:T(8,128)(2,1)S(1)}, u32[]{:S(2)}, u32[]{:S(2)}) collective-permute-start(bf16[256,512]{1,0:T(8,128)(2,1)S(1)} %constant_dynamic-update-slice_fusion), channel_id=1, source_target_pairs={{0,28},{4,0},{8,4},{12,8},{16,12},{20,16},{24,20},{28,24},{1,29},{... | collective-permute-start | bytes 786440 | tf_op jit(solution)/shard_map/ppermute | solution.py:256
  7.7 0.4 collective-permute-start.2
  8.2 6.3 %collective-permute-done.refs_4_ = bf16[256,512]{1,0:T(8,128)(2,1)S(1)} collective-permute-done((bf16[256,512]{1,0:T(8,128)(2,1)S(1)}, bf16[256,512]{1,0:T(8,128)(2,1)S(1)}, u32[]{:S(2)}, u32[]{:S(2)}) %collective-permute-start) | collective-permute-done | bytes 262176 | tf_op jit(solution)/shard_map/ppermute | solution.py:256
  14.4 0.4 collective-permute-start.1
  14.9 44.4 %all-gather.1 = s32[32,3,64]{2,1,0:T(4,128)S(1)} all-gather(s32[1,3,64]{2,1,0:T(4,128)} %bitcast.10), channel_id=2, replica_groups=mesh['ctx'=8,'head'=4] {'ctx','head'}, dimensions={0}, use_global_device_ids=true | all-gather | bytes 25344 | tf_op jit(solution)/shard_map/all_gather | solution.py:271
  59.3 0.0 copy-start.1
  59.3 0.1 reshape.17
  59.4 0.0 copy-done
  59.5 0.7 copy-done.2
  60.2 0.0 copy-done.1
  60.2 0.7 copy-done.4
  60.9 1.0 %copy-done.6 = bf16[256,1024]{1,0:T(8,128)(2,1)S(1)} copy-done((bf16[256,1024]{1,0:T(8,128)(2,1)S(1)}, bf16[256,1024]{1,0:T(8,128)(2,1)}, u32[]{:S(2)}) %copy-start.6) | copy-done | bytes 524312
  61.9 1.0 %copy-done.7 = bf16[256,1024]{1,0:T(8,128)(2,1)S(1)} copy-done((bf16[256,1024]{1,0:T(8,128)(2,1)S(1)}, bf16[256,1024]{1,0:T(8,128)(2,1)}, u32[]{:S(2)}) %copy-start.7) | copy-done | bytes 524312
  63.0 3.2 %shard_map.112 = (bf16[256,1024]{1,0:T(8,128)(2,1)S(1)}, f32[8,256]{1,0:T(8,128)S(1)}, f32[256,128]{1,0:T(8,128)S(1)}, f32[256,128]{1,0:T(8,128)S(1)}, f32[1024,256]{1,0:T(8,128)S(1)}, /*index=5*/f32[256,512]{1,0:T(8,128)S(1)}) custom-call(s32[1]{0:T(128)} %bitcast.slot_ref.refs_0_, s32[8,3,256]{2,1,0:T(4,128)S(1)} %copy.22.pos_ref.refs_2_, ...), custom_call_target="tpu_custom_call" | custom-call | flops 671088640 | bytes 5242880 | tf_op jit(solution)/shard_map/pallas_call | solution.py:277
  66.2 0.0 copy-start.5
  66.2 0.6 copy-done.5
  66.9 2.4 %shard_map.113 = (f32[1024,256]{1,0:T(8,128)S(1)}, bf16[256,512]{1,0:T(8,128)(2,1)S(1)}) custom-call(s32[1]{0:T(128)} %bitcast.slot_ref.refs_0_, s32[8]{0:T(128)S(1)} %copy-done.5, s32[8,3,256]{2,1,0:T(4,128)S(1)} %copy.22.pos_ref.refs_2_, f32[64,256]{1,0:T(8,128)S(1)} %copy-done.1, bf16[256,512]{1,0:T(8,128)(2,1)S(1)} %collective-permute-done.refs_4_, ...), custom_call_target="tpu_custom_call" | custom-call | flops 335544320 | bytes 4194304 | tf_op jit(solution)/shard_map/pallas_call | solution.py:299
  69.3 0.0 collective-permute-done.2.refs_4_
  69.3 2.4 %shard_map.114 = (f32[1024,256]{1,0:T(8,128)S(1)}, bf16[256,512]{1,0:T(8,128)(2,1)S(1)}) custom-call(s32[1]{0:T(128)} %bitcast.slot_ref.refs_0_, s32[8]{0:T(128)S(1)} %copy-done.5, s32[8,3,256]{2,1,0:T(4,128)S(1)} %copy.22.pos_ref.refs_2_, f32[64,256]{1,0:T(8,128)S(1)} %copy-done.1, bf16[256,512]{1,0:T(8,128)(2,1)S(1)} %collective-permute-done.2.refs_4_, ...), custom_call_target="tpu_custom_call" | custom-call | flops 335544320 | bytes 4194304 | tf_op jit(solution)/shard_map/pallas_call | solution.py:299
  71.7 0.1 collective-permute-start.4
  71.8 0.1 collective-permute-start.3
  71.9 0.0 collective-permute-done.1.kv_ref
  71.9 3.6 %shard_map.115 = (bf16[256,1024]{1,0:T(8,128)(2,1)}, bf16[256,512]{1,0:T(8,128)(2,1)S(1)}) custom-call(s32[1]{0:T(128)} %bitcast.slot_ref.refs_0_, s32[8]{0:T(128)S(1)} %copy-done.5, s32[8,3,256]{2,1,0:T(4,128)S(1)} %copy.22.pos_ref.refs_2_, f32[64,256]{1,0:T(8,128)S(1)} %copy-done.1, bf16[256,512]{1,0:T(8,128)(2,1)S(1)} %collective-permute-done.1.kv_ref, ...), custom_call_target="tpu_custom_call" | custom-call | flops 335544320 | bytes 4194304 | tf_op jit(solution)/shard_map/pallas_call | solution.py:299
  75.4 0.0 collective-permute-start.5
  75.4 7.3 %collective-permute-done.4.b_ref = bf16[256,512]{1,0:T(8,128)(2,1)S(1)} collective-permute-done((bf16[256,512]{1,0:T(8,128)(2,1)S(1)}, bf16[256,512]{1,0:T(8,128)(2,1)S(1)}, u32[]{:S(2)}, u32[]{:S(2)}) %collective-permute-start.4) | collective-permute-done | bytes 262176 | tf_op jit(solution)/shard_map/ppermute | solution.py:256
  82.7 3.0 %collective-permute-done.3.a_ref = bf16[256,512]{1,0:T(8,128)(2,1)S(1)} collective-permute-done((bf16[256,512]{1,0:T(8,128)(2,1)S(1)}, bf16[256,512]{1,0:T(8,128)(2,1)S(1)}, u32[]{:S(2)}, u32[]{:S(2)}) %collective-permute-start.3) | collective-permute-done | bytes 262176 | tf_op jit(solution)/shard_map/ppermute | solution.py:256
  85.7 10.6 %collective-permute-done.5.c_ref = bf16[256,512]{1,0:T(8,128)(2,1)S(1)} collective-permute-done((bf16[256,512]{1,0:T(8,128)(2,1)S(1)}, bf16[256,512]{1,0:T(8,128)(2,1)S(1)}, u32[]{:S(2)}, u32[]{:S(2)}) %collective-permute-start.5) | collective-permute-done | bytes 262176 | tf_op jit(solution)/shard_map/ppermute | solution.py:256
  96.3 0.9 shard_map.116
  (7 shorter events, 0.0 us)
Async XLA Ops:
  0.6 1.0 %copy-start.3 = (bf16[256,256]{1,0:T(8,128)(2,1)S(1)}, bf16[256,256]{1,0:T(8,128)(2,1)}, u32[]{:S(2)}) copy-start(bf16[256,256]{1,0:T(8,128)(2,1)} %v_ref.1) | copy-start | bytes 393220
  0.6 58.8 %copy-start = (bf16[256,1024]{1,0:T(8,128)(2,1)S(1)}, bf16[256,1024]{1,0:T(8,128)(2,1)}, u32[]{:S(2)}) copy-start(bf16[256,1024]{1,0:T(8,128)(2,1)} %do_ref.3) | copy-start | bytes 1572868
  1.7 12.8 %collective-permute-start = (bf16[256,512]{1,0:T(8,128)(2,1)S(1)}, bf16[256,512]{1,0:T(8,128)(2,1)S(1)}, u32[]{:S(2)}, u32[]{:S(2)}) collective-permute-start(bf16[256,512]{1,0:T(8,128)(2,1)S(1)} %constant_dynamic-update-slice_fusion), channel_id=1, source_target_pairs={{0,28},{4,0},{8,4},{12,8},{16,12},{20,16},{24,20},{28,24},{1,29},{... | collective-permute-start | bytes 786440 | tf_op jit(solution)/shard_map/ppermute | solution.py:256
  7.7 61.6 %collective-permute-start.2 = (bf16[256,512]{1,0:T(8,128)(2,1)S(1)}, bf16[256,512]{1,0:T(8,128)(2,1)S(1)}, u32[]{:S(2)}, u32[]{:S(2)}) collective-permute-start(bf16[256,512]{1,0:T(8,128)(2,1)S(1)} %constant_dynamic-update-slice_fusion), channel_id=1, source_target_pairs={{0,24},{4,28},{8,0},{12,4},{16,8},{20,12},{24,16},{28,20},{1,25},{... | collective-permute-start | bytes 786440 | tf_op jit(solution)/shard_map/ppermute | solution.py:256
  14.4 57.4 %collective-permute-start.1 = (bf16[256,512]{1,0:T(8,128)(2,1)S(1)}, bf16[256,512]{1,0:T(8,128)(2,1)S(1)}, u32[]{:S(2)}, u32[]{:S(2)}) collective-permute-start(bf16[256,512]{1,0:T(8,128)(2,1)S(1)} %collective-permute-done.refs_4_), channel_id=1, source_target_pairs={{0,24},{4,28},{8,0},{12,4},{16,8},{20,12},{24,16},{28,20},{1,25},{... | collective-permute-start | bytes 786440 | tf_op jit(solution)/shard_map/ppermute | solution.py:256
  59.3 0.9 copy-start.2
  59.3 0.9 copy-start.1
  60.2 0.7 copy-start.4
  60.9 1.0 %copy-start.6 = (bf16[256,1024]{1,0:T(8,128)(2,1)S(1)}, bf16[256,1024]{1,0:T(8,128)(2,1)}, u32[]{:S(2)}) copy-start(bf16[256,1024]{1,0:T(8,128)(2,1)} %q_ref.1) | copy-start | bytes 1572868
  61.9 1.0 %copy-start.7 = (bf16[256,1024]{1,0:T(8,128)(2,1)S(1)}, bf16[256,1024]{1,0:T(8,128)(2,1)}, u32[]{:S(2)}) copy-start(bf16[256,1024]{1,0:T(8,128)(2,1)} %at_ref.1) | copy-start | bytes 1572868
  66.2 0.7 copy-start.5
  71.7 11.0 %collective-permute-start.4 = (bf16[256,512]{1,0:T(8,128)(2,1)S(1)}, bf16[256,512]{1,0:T(8,128)(2,1)S(1)}, u32[]{:S(2)}, u32[]{:S(2)}) collective-permute-start(bf16[256,512]{1,0:T(8,128)(2,1)S(1)} %get-tuple-element.27), channel_id=1, source_target_pairs={{0,8},{4,12},{8,16},{12,20},{16,24},{20,28},{24,0},{28,4},{1,9},{5... | collective-permute-start | bytes 786440 | tf_op jit(solution)/shard_map/ppermute | solution.py:256
  71.8 13.9 %collective-permute-start.3 = (bf16[256,512]{1,0:T(8,128)(2,1)S(1)}, bf16[256,512]{1,0:T(8,128)(2,1)S(1)}, u32[]{:S(2)}, u32[]{:S(2)}) collective-permute-start(bf16[256,512]{1,0:T(8,128)(2,1)S(1)} %get-tuple-element.26), channel_id=1, source_target_pairs={{0,4},{4,8},{8,12},{12,16},{16,20},{20,24},{24,28},{28,0},{1,5},{5... | collective-permute-start | bytes 786440 | tf_op jit(solution)/shard_map/ppermute | solution.py:256
  75.4 20.9 %collective-permute-start.5 = (bf16[256,512]{1,0:T(8,128)(2,1)S(1)}, bf16[256,512]{1,0:T(8,128)(2,1)S(1)}, u32[]{:S(2)}, u32[]{:S(2)}) collective-permute-start(bf16[256,512]{1,0:T(8,128)(2,1)S(1)} %get-tuple-element.28), channel_id=1, source_target_pairs={{0,12},{4,16},{8,20},{12,24},{16,28},{20,0},{24,4},{28,8},{1,13},{... | collective-permute-start | bytes 786440 | tf_op jit(solution)/shard_map/ppermute | solution.py:256

commit v2 on v1

--- a/solution.py
+++ b/solution.py
@@ -105,38 +105,72 @@
     return value_part, key_part, query_part
 
 
-def first_kernel(
-    slot_ref, pos_ref, freq_ref, q_ref, k_ref, v_ref, do_ref, at_ref, lse_ref,
-    qr_ref, delta_ref, wide_ref, signed_ref, dqt_ref, dkv_ref,
-):
-    heads = q_ref.shape[1] // HEAD
-    groups = k_ref.shape[1] // HEAD
-    size = heads // groups
-    cosine_t, sine_t = tables_transposed(pos_ref[slot_ref[0]], freq_ref[...])
+def key_kernel(pos_ref, freq_ref, k_ref, kr_ref, tables_ref):
+    cosine_t, sine_t = tables_transposed(pos_ref[...], freq_ref[...])
+    tables_ref[:HALF, :] = cosine_t
+    tables_ref[HALF:, :] = sine_t
     wide, signed = row_tables(cosine_t, sine_t)
-    wide_ref[...] = wide
-    signed_ref[...] = signed
+    for g in range(k_ref.shape[1] // HEAD):
+        cols = pl.ds(g * HEAD, HEAD)
+        kr_ref[:, cols] = rotated(k_ref[:, cols].astype(F32), wide, signed).astype(BF16)
+
+
+def delta_kernel(do_hbm, at_hbm, delta_ref, do_ref, at_ref, sems):
+    heads = do_ref.shape[1] // HEAD
+    halves = 2
+    width = do_ref.shape[1] // halves
+    copies = []
+    for part in range(halves):
+        cols = pl.ds(part * width, width)
+        for i, (source, target) in enumerate(((do_hbm, do_ref), (at_hbm, at_ref))):
+            copy = pltpu.make_async_copy(
+                source.at[:, cols], target.at[:, cols], sems.at[2 * part + i]
+            )
+            copy.start()
+            copies.append(copy)
     delta = jnp.zeros(delta_ref.shape, F32)
     which = lax.broadcasted_iota(jnp.int32, (heads, HEAD), 0)
     for h in range(heads):
+        if h % (heads // halves) == 0:
+            part = h // (heads // halves)
+            copies[2 * part].wait()
+            copies[2 * part + 1].wait()
         cols = pl.ds(h * HEAD, HEAD)
-        qr_ref[:, cols] = rotated(q_ref[:, cols].astype(F32), wide, signed).astype(BF16)
         product = do_ref[:, cols].astype(F32) * at_ref[:, cols].astype(F32)
         high = product.astype(BF16)
         low = (product - high.astype(F32)).astype(BF16)
         chooser = jnp.where(which == h, 1.0, 0.0).astype(BF16)
         delta = delta + dot_nt(chooser, high) + dot_nt(chooser, low)
     delta_ref[...] = delta
+
+
+def first_kernel(
+    tables_ref, q_hbm, kr_ref, v_ref, do_ref, lse_ref, delta_ref,
+    qr_ref, dqt_ref, dkv_ref, q_ref, sems,
+):
+    heads = qr_ref.shape[1] // HEAD
+    groups = kr_ref.shape[1] // HEAD
+    size = heads // groups
+    copies = []
+    for g in range(groups):
+        cols = pl.ds(g * size * HEAD, size * HEAD)
+        copy = pltpu.make_async_copy(q_hbm.at[:, cols], q_ref.at[:, cols], sems.at[g])
+        copy.start()
+        copies.append(copy)
+    wide, signed = row_tables(tables_ref[:HALF, :], tables_ref[HALF:, :])
     norm = lse_ref[...] * LOG2E
+    delta = delta_ref[...]
     for g in range(groups):
         cols = pl.ds(g * HEAD, HEAD)
-        key = rotated(k_ref[:, cols].astype(F32), wide, signed).astype(BF16)
-        value = v_ref[:, cols]
         dk = dv = None
+        copies[g].wait()
         for h in range(g * size, (g + 1) * size):
             hc = pl.ds(h * HEAD, HEAD)
+            query = rotated(q_ref[:, hc].astype(F32), wide, signed).astype(BF16)
+            qr_ref[:, hc] = query
             v_part, k_part, q_part = pair_part(
-                key, value, qr_ref[:, hc], do_ref[:, hc], norm[h : h + 1], delta[h : h + 1], True
+                kr_ref[:, cols], v_ref[:, cols], query, do_ref[:, hc],
+                norm[h : h + 1], delta[h : h + 1], True,
             )
             dqt_ref[hc, :] = q_part
             dv = v_part if dv is None else dv + v_part
@@ -146,22 +180,16 @@
 
 
 def hop_body(
-    step, slot_ref, span_ref, pos_ref, freq_ref, kv_ref, qr_ref, do_ref, lse_ref, delta_ref,
-    dqt_in, dqt_ref, dkv_ref, key_ref,
+    step, slot_ref, span_ref, k_ref, v_ref, qr_ref, do_ref, lse_ref, delta_ref,
+    dqt_in, dqt_ref, dkv_ref,
 ):
     rows = qr_ref.shape[0]
     half = rows // 2
     heads = qr_ref.shape[1] // HEAD
-    groups = kv_ref.shape[1] // HEAD // 2
+    groups = k_ref.shape[1] // HEAD
     size = heads // groups
-    count = span_ref.shape[0]
     me = slot_ref[0]
-    other = lax.rem(me + step, count)
-    cosine_t, sine_t = tables_transposed(pos_ref[other], freq_ref[...])
-    wide, signed = row_tables(cosine_t, sine_t)
-    for g in range(groups):
-        cols = pl.ds(g * HEAD, HEAD)
-        key_ref[:, cols] = rotated(kv_ref[:, cols].astype(F32), wide, signed).astype(BF16)
+    other = lax.rem(me + step, span_ref.shape[0])
     earlier = span_ref[other] < span_ref[me]
     norm = lse_ref[...] * LOG2E
     delta = delta_ref[...]
@@ -174,7 +202,7 @@
             for h in range(g * size, (g + 1) * size):
                 hc = pl.ds(h * HEAD, HEAD)
                 v_part, k_part, q_part = pair_part(
-                    key_ref[keys, kc], kv_ref[keys, vc], qr_ref[queries, hc], do_ref[queries, hc],
+                    k_ref[keys, kc], v_ref[keys, kc], qr_ref[queries, hc], do_ref[queries, hc],
                     norm[h : h + 1, queries.start :], delta[h : h + 1, queries.start :], False,
                 )
                 if queries.start:
@@ -196,21 +224,16 @@
         run(slice(0, rows), slice(half, rows))
 
 
-def middle_kernel(step, *refs):
-    hop_body(step, *refs)
-
-
 def last_kernel(
-    step, slot_ref, span_ref, pos_ref, freq_ref, kv_ref, qr_ref, do_ref, lse_ref, delta_ref,
-    dqt_in, out_ref, dkv_ref, key_ref, dqt_ref,
+    step, slot_ref, span_ref, k_ref, v_ref, qr_ref, do_ref, lse_ref, delta_ref, dqt_in, tables_ref,
+    out_ref, dkv_ref, dqt_ref,
 ):
     hop_body(
-        step, slot_ref, span_ref, pos_ref, freq_ref, kv_ref, qr_ref, do_ref, lse_ref, delta_ref,
-        dqt_in, dqt_ref, dkv_ref, key_ref,
-    )
-    cosine_t, sine_t = tables_transposed(pos_ref[slot_ref[0]], freq_ref[...])
-    cosine_t = cosine_t * ROOT_SCALE
-    sine_t = sine_t * ROOT_SCALE
+        step, slot_ref, span_ref, k_ref, v_ref, qr_ref, do_ref, lse_ref, delta_ref,
+        dqt_in, dqt_ref, dkv_ref,
+    )
+    cosine_t = tables_ref[:HALF, :] * ROOT_SCALE
+    sine_t = tables_ref[HALF:, :] * ROOT_SCALE
     for h in range(qr_ref.shape[1] // HEAD):
         y1 = dqt_ref[pl.ds(h * HEAD, HALF), :]
         y2 = dqt_ref[pl.ds(h * HEAD + HALF, HALF), :]
@@ -220,29 +243,32 @@
         out_ref[:, pl.ds(h * HEAD, HEAD)] = turned.T.astype(BF16)
 
 
-def final_kernel(wide_ref, signed_ref, own_ref, a_ref, b_ref, c_ref, dk_ref, dv_ref):
+def final_kernel(tables_ref, own_ref, a_ref, b_ref, c_ref, dk_ref, dv_ref):
     width = dk_ref.shape[1]
+    wide, signed = row_tables(tables_ref[:HALF, :], tables_ref[HALF:, :])
+    wide = wide * ROOT_SCALE
+    signed = signed * -ROOT_SCALE
     total = (
         own_ref[...] + a_ref[...].astype(F32) + b_ref[...].astype(F32) + c_ref[...].astype(F32)
     )
-    wide = wide_ref[...] * ROOT_SCALE
-    signed = signed_ref[...] * -ROOT_SCALE
     for g in range(width // HEAD):
         cols = pl.ds(g * HEAD, HEAD)
         dk_ref[:, cols] = rotated(total[:, g * HEAD : (g + 1) * HEAD], wide, signed).astype(BF16)
     dv_ref[...] = total[:, width:].astype(BF16)
 
 
-def call(kernel, outs, in_smem, n_in, scratch=(), flops=0, bytes_accessed=0, aliases=None):
-    vmem = pl.BlockSpec(memory_space=pltpu.VMEM)
-    smem = pl.BlockSpec(memory_space=pltpu.SMEM)
+SMEM = pl.BlockSpec(memory_space=pltpu.SMEM)
+VMEM = pl.BlockSpec(memory_space=pltpu.VMEM)
+HBM = pl.BlockSpec(memory_space=pltpu.HBM)
+
+
+def call(kernel, outs, specs, scratch=(), flops=0, bytes_accessed=0):
     return pl.pallas_call(
         kernel,
         out_shape=[jax.ShapeDtypeStruct(shape, dtype) for shape, dtype in outs],
-        in_specs=[smem] * in_smem + [vmem] * n_in,
-        out_specs=[vmem] * len(outs),
+        in_specs=specs,
+        out_specs=[VMEM] * len(outs),
         scratch_shapes=list(scratch),
-        input_output_aliases=aliases or {},
         compiler_params=pltpu.CompilerParams(vmem_limit_bytes=VMEM_LIMIT),
         cost_estimate=pl.CostEstimate(
             flops=flops, bytes_accessed=bytes_accessed, transcendentals=0
@@ -261,62 +287,68 @@
     wide_q = q.shape[1]
     wide_k = k.shape[1]
     heads = wide_q // HEAD
-    slots = lax.axis_size("ctx")
     slot = lax.axis_index("ctx").astype(jnp.int32).reshape(1)
     freq = jnp.asarray(np.broadcast_to(frequencies()[:, None], (HALF, rows)).copy())
 
-    kv = jnp.concatenate([k, v], axis=1)
-    kv1 = shifted(kv, -1)
-    kv2 = shifted(kv, -2)
-    gathered = lax.all_gather(positions, ("ctx", "head"), axis=0)
-    pos = gathered.reshape(slots, -1, 3, positions.shape[1]).transpose(0, 2, 1, 3)
-    pos = pos.reshape(slots, 3, rows)
-    kv3 = shifted(kv1, -2)
-
-    flops = 10 * rows * rows * wide_q
-    qr, delta, wide, signed, dqt, dkv = call(
+    v1 = shifted(v, -1)
+    v2 = shifted(v, -2)
+    pos = lax.all_gather(positions, "head", axis=1, tiled=True)
+    (delta,) = call(
+        delta_kernel,
+        [((heads, rows), F32)],
+        [HBM, HBM],
+        [
+            pltpu.VMEM((rows, wide_q), BF16),
+            pltpu.VMEM((rows, wide_q), BF16),
+            pltpu.SemaphoreType.DMA((4,)),
+        ],
+        flops=4 * rows * wide_q,
+        bytes_accessed=4 * rows * wide_q,
+    )(do, at)
+    kr, tables = call(
+        key_kernel,
+        [((rows, wide_k), BF16), ((HEAD, rows), F32)],
+        [VMEM] * 3,
+        flops=100 * rows * HEAD,
+        bytes_accessed=4 * rows * wide_k,
+    )(pos, freq, k)
+    k1 = shifted(kr, -1)
+    k2 = shifted(kr, -2)
+    v3 = shifted(v1, -2)
+    k3 = shifted(k1, -2)
+
+    flops = rows * rows * wide_q
+    qr, dqt, dkv = call(
         first_kernel,
-        [
-            ((rows, wide_q), BF16),
-            ((heads, rows), F32),
-            ((rows, HEAD), F32),
-            ((rows, HEAD), F32),
-            ((wide_q, rows), F32),
-            ((rows, 2 * wide_k), F32),
-        ],
-        1,
-        8,
+        [((rows, wide_q), BF16), ((wide_q, rows), F32), ((rows, 2 * wide_k), F32)],
+        [VMEM, HBM] + [VMEM] * 5,
+        [pltpu.VMEM((rows, wide_q), BF16), pltpu.SemaphoreType.DMA((wide_k // HEAD,))],
         flops=flops,
-        bytes_accessed=5 << 20,
-    )(slot, pos, freq, q, k, v, do, at, lse)
+        bytes_accessed=1 << 20,
+    )(tables, q, kr, v, do, lse, delta)
 
     backs = []
-    for step, arrived in ((1, kv1), (2, kv2), (3, kv3)):
+    for step, key, value in ((1, k1, v1), (2, k2, v2), (3, k3, v3)):
         last = step == WIN - 1
-        scratch = [pltpu.VMEM((rows, wide_k), BF16)]
-        if last:
-            scratch.append(pltpu.VMEM((wide_q, rows), F32))
         dqt, part = call(
-            functools.partial(last_kernel if last else middle_kernel, step),
+            functools.partial(last_kernel if last else hop_body, step),
             [
                 ((rows, wide_q), BF16) if last else ((wide_q, rows), F32),
                 ((rows, 2 * wide_k), BF16),
             ],
-            2,
-            8,
-            scratch,
+            [SMEM, SMEM] + [VMEM] * (8 if last else 7),
+            [pltpu.VMEM((wide_q, rows), F32)] if last else [],
             flops=flops // 2,
-            bytes_accessed=4 << 20,
-        )(slot, span_map, pos, freq, arrived, qr, do, lse, delta, dqt)
+            bytes_accessed=1 << 18,
+        )(slot, span_map, key, value, qr, do, lse, delta, dqt, *([tables] if last else []))
         backs.append(shifted(part, step))
 
     dk, dv = call(
         final_kernel,
         [((rows, wide_k), BF16), ((rows, wide_k), BF16)],
-        0,
-        6,
+        [VMEM] * 5,
         bytes_accessed=2 << 20,
-    )(wide, signed, dkv, *backs)
+    )(tables, dkv, *backs)
     return dqt, dk, dv
 
 

time: 97.5 us -> 61.5 us (0.63)
  blocking collectives: 44.4 us -> 5.28 us
  starting transfers between devices: 7.08 us -> 12.1 us
  waiting for transfers between devices: 27.1 us -> 25.8 us
    all_gather x1, blocking collectives: 44.4 us -> 5.28 us  [shards(): pos = lax.all_gather(positions, 'head', axis=1, tiled=True)]
    ppermute x6 -> x9, starting transfers between devices: 7.08 us -> 12.1 us  [shifted(): return lax.ppermute(value, 'ctx', pairs)]
    ppermute x6 -> x9, waiting for transfers between devices: 27.1 us -> 25.8 us  [shifted(): return lax.ppermute(value, 'ctx', pairs)]
    unnamed x17 -> x19, local copies, waits for them, and re-layouts: 5.17 us -> 4.82 us
    pallas_call x5 -> x7, Pallas kernels: 12.5 us -> 12.4 us  [the longest x3 7.57 us: shards(): call(functools.partial(last_kernel if last else hop_body, step), [((rows,...]
  transfers between devices with their start and end apart: 6 -> 9, of which waited for: 4 -> 4; matrix products, arithmetic and copies ran while one was open for 0% -> 0% of each run, Pallas kernels for 12% -> 19%
where the time goes in v2:
time: 61.5 us; the launch traced here: 61.1 us
  waiting for transfers between devices  25.8 us (42%)
  Pallas kernels  12.4 us (20%)
  starting transfers between devices  12.1 us (20%)
  blocking collectives  5.28 us (9%)
  local copies, waits for them, and re-layouts  4.83 us (8%)
  between operations  0.72 us (1%)
    ppermute x9, waiting for transfers between devices, shifted(): return lax.ppermute(value, 'ctx', pairs)  25.8 us
    ppermute x9, starting transfers between devices, shifted(): return lax.ppermute(value, 'ctx', pairs)  12.1 us
    pallas_call x3, Pallas kernels, shards(): call(functools.partial(last_kernel if last else hop_body, step), [((rows,...  7.57 us
    all_gather x1, blocking collectives, shards(): pos = lax.all_gather(positions, 'head', axis=1, tiled=True)  5.28 us
    unnamed x19, local copies, waits for them, and re-layouts  4.82 us
    pallas_call x1, Pallas kernels, shards(): call(first_kernel, [((rows, wide_q), BF16), ((wide_q, rows), F32), ((rows...  2.69 us
  transfers between devices with their start and end apart: 9, of which 4 were waited for; matrix products, arithmetic and copies ran while one was open for 0% of the time, Pallas kernels for 19%

profile of v2, /device:TPU:0, one launch (start us, length us, event | category | flops | bytes accessed | tf_op | source)
XLA Modules:
  0.0 61.1 jit_solution(10201244802678383348)
XLA Ops:
  0.6 6.1 %collective-permute-start.2 = (bf16[256,256]{1,0:T(8,128)(2,1)}, bf16[256,256]{1,0:T(8,128)(2,1)S(1)}, u32[]{:S(2)}, u32[]{:S(2)}) collective-permute-start(bf16[256,256]{1,0:T(8,128)(2,1)} %v_ref.1), channel_id=1, source_target_pairs={{0,28},{4,0},{8,4},{12,8},{16,12},{20,16},{24,20},{28,24},{1,29},{... | collective-permute-start | bytes 393224 | tf_op jit(solution)/shard_map/ppermute | solution.py:282
  6.7 5.3 %all-gather = s32[4,64,3]{1,2,0:T(4,128)S(1)} all-gather(s32[1,64,3]{1,2,0:T(4,128)} %bitcast.8), channel_id=1, replica_groups=mesh['ctx'=8,'head'=4] {'head'}, dimensions={0}, use_global_device_ids=true | all-gather | bytes 3840 | tf_op jit(solution)/shard_map/all_gather | solution.py:295
  12.0 0.1 reshape.11
  12.1 0.9 %copy-done.6 = bf16[256,256]{1,0:T(8,128)(2,1)S(1)} copy-done((bf16[256,256]{1,0:T(8,128)(2,1)S(1)}, bf16[256,256]{1,0:T(8,128)(2,1)}, u32[]{:S(2)}) %copy-start.6) | copy-done | bytes 131096
  13.0 0.8 %copy-done.7 = f32[64,256]{1,0:T(8,128)S(1)} copy-done((f32[64,256]{1,0:T(8,128)S(1)}, f32[64,256]{1,0:T(8,128)}, u32[]{:S(2)}) %copy-start.7) | copy-done | bytes 65560
  13.8 0.3 shard_map.112
  14.1 0.6 collective-permute-start
  14.7 0.4 collective-permute-start.5
  15.1 0.4 collective-permute-start.4
  15.6 0.0 collective-permute-done.2.v_ref
  15.6 0.0 collective-permute-start.3
  15.6 4.2 %collective-permute-done.k_ref = bf16[256,256]{1,0:T(8,128)(2,1)S(1)} collective-permute-done((bf16[256,256]{1,0:T(8,128)(2,1)S(1)}, bf16[256,256]{1,0:T(8,128)(2,1)S(1)}, u32[]{:S(2)}, u32[]{:S(2)}) %collective-permute-start) | collective-permute-done | bytes 131104 | tf_op jit(solution)/shard_map/ppermute | solution.py:282
  19.8 0.4 collective-permute-start.1
  20.3 1.0 %copy-done = bf16[256,1024]{1,0:T(8,128)(2,1)S(1)} copy-done((bf16[256,1024]{1,0:T(8,128)(2,1)S(1)}, bf16[256,1024]{1,0:T(8,128)(2,1)}, u32[]{:S(2)}) %copy-start) | copy-done | bytes 524312
  21.3 1.0 %copy-done.2 = bf16[256,1024]{1,0:T(8,128)(2,1)S(1)} copy-done((bf16[256,1024]{1,0:T(8,128)(2,1)S(1)}, bf16[256,1024]{1,0:T(8,128)(2,1)}, u32[]{:S(2)}) %copy-start.2) | copy-done | bytes 524312
  22.4 0.9 %shard_map.113.delta_ref = f32[8,256]{1,0:T(8,128)S(1)} custom-call(bf16[256,1024]{1,0:T(8,128)(2,1)S(1)} %copy-done, bf16[256,1024]{1,0:T(8,128)(2,1)S(1)} %copy-done.2), custom_call_target="tpu_custom_call" | custom-call | flops 1048576 | bytes 1048576 | tf_op jit(solution)/shard_map/pallas_call | solution.py:296
  23.3 0.1 copy-done.1
  23.4 0.2 copy-done.3
  23.6 2.7 %shard_map.114 = (bf16[256,1024]{1,0:T(8,128)(2,1)S(1)}, f32[1024,256]{1,0:T(8,128)S(1)}, f32[256,512]{1,0:T(8,128)S(1)}) custom-call(f32[128,256]{1,0:T(8,128)S(1)} %get-tuple-element.17.tables_ref, bf16[256,1024]{1,0:T(8,128)(2,1)S(1)} %copy-done.3, bf16[256,256]{1,0:T(8,128)(2,1)S(1)} %get-tuple-element.16.kr_ref, bf16[256,256]{1,0:T(8,128)(2,1)S(1)} %copy-done.5, ...), custom_call_target="tpu_custom_call" | custom-call | flops 67108864 | bytes 1048576 | tf_op jit(solution)/shard_map/pallas_call | solution.py:321
  26.3 0.0 copy-start.8
  26.3 0.6 %copy-done.8 = s32[8]{0:T(128)S(1)} copy-done((s32[8]{0:T(128)S(1)}, s32[8]{0:T(128)}, u32[]{:S(2)}) %copy-start.8) | copy-done | bytes 56
  26.9 2.2 %shard_map.115 = (f32[1024,256]{1,0:T(8,128)S(1)}, bf16[256,512]{1,0:T(8,128)(2,1)S(1)}) custom-call(s32[1]{0:T(128)} %bitcast.slot_ref, s32[8]{0:T(128)S(1)} %copy-done.8, bf16[256,256]{1,0:T(8,128)(2,1)S(1)} %collective-permute-done.k_ref, bf16[256,256]{1,0:T(8,128)(2,1)S(1)} %collective-permute-done.2.v_ref, ...), custom_call_target="tpu_custom_call" | custom-call | flops 33554432 | bytes 262144 | tf_op jit(solution)/shard_map/pallas_call | solution.py:333
  29.1 2.2 %shard_map.116 = (f32[1024,256]{1,0:T(8,128)S(1)}, bf16[256,512]{1,0:T(8,128)(2,1)S(1)}) custom-call(s32[1]{0:T(128)} %bitcast.slot_ref, s32[8]{0:T(128)S(1)} %copy-done.8, bf16[256,256]{1,0:T(8,128)(2,1)S(1)} %collective-permute-done.4.k_ref, bf16[256,256]{1,0:T(8,128)(2,1)S(1)} %collective-permute-done.5.v_ref, ...), custom_call_target="tpu_custom_call" | custom-call | flops 33554432 | bytes 262144 | tf_op jit(solution)/shard_map/pallas_call | solution.py:333
  31.3 1.6 %collective-permute-start.7 = (bf16[256,512]{1,0:T(8,128)(2,1)S(1)}, bf16[256,512]{1,0:T(8,128)(2,1)S(1)}, u32[]{:S(2)}, u32[]{:S(2)}) collective-permute-start(bf16[256,512]{1,0:T(8,128)(2,1)S(1)} %get-tuple-element.25), channel_id=1, source_target_pairs={{0,8},{4,12},{8,16},{12,20},{16,24},{20,28},{24,0},{28,4},{1,9},{5... | collective-permute-start | bytes 786440 | tf_op jit(solution)/shard_map/ppermute | solution.py:282
  32.9 2.4 %collective-permute-start.6 = (bf16[256,512]{1,0:T(8,128)(2,1)S(1)}, bf16[256,512]{1,0:T(8,128)(2,1)S(1)}, u32[]{:S(2)}, u32[]{:S(2)}) collective-permute-start(bf16[256,512]{1,0:T(8,128)(2,1)S(1)} %get-tuple-element.24), channel_id=1, source_target_pairs={{0,4},{4,8},{8,12},{12,16},{16,20},{20,24},{24,28},{28,0},{1,5},{5... | collective-permute-start | bytes 786440 | tf_op jit(solution)/shard_map/ppermute | solution.py:282
  35.4 0.0 collective-permute-done.3.v_ref
  35.4 0.0 collective-permute-done.1.k_ref
  35.4 3.2 %shard_map.117 = (bf16[256,1024]{1,0:T(8,128)(2,1)}, bf16[256,512]{1,0:T(8,128)(2,1)S(1)}) custom-call(s32[1]{0:T(128)} %bitcast.slot_ref, s32[8]{0:T(128)S(1)} %copy-done.8, bf16[256,256]{1,0:T(8,128)(2,1)S(1)} %collective-permute-done.1.k_ref, bf16[256,256]{1,0:T(8,128)(2,1)S(1)} %collective-permute-done.3.v_ref, ...), custom_call_target="tpu_custom_call" | custom-call | flops 33554432 | bytes 262144 | tf_op jit(solution)/shard_map/pallas_call | solution.py:333
  38.6 2.0 %collective-permute-done.7.b_ref = bf16[256,512]{1,0:T(8,128)(2,1)S(1)} collective-permute-done((bf16[256,512]{1,0:T(8,128)(2,1)S(1)}, bf16[256,512]{1,0:T(8,128)(2,1)S(1)}, u32[]{:S(2)}, u32[]{:S(2)}) %collective-permute-start.7) | collective-permute-done | bytes 262176 | tf_op jit(solution)/shard_map/ppermute | solution.py:282
  40.6 10.9 %collective-permute-done.6.a_ref = bf16[256,512]{1,0:T(8,128)(2,1)S(1)} collective-permute-done((bf16[256,512]{1,0:T(8,128)(2,1)S(1)}, bf16[256,512]{1,0:T(8,128)(2,1)S(1)}, u32[]{:S(2)}, u32[]{:S(2)}) %collective-permute-start.6) | collective-permute-done | bytes 262176 | tf_op jit(solution)/shard_map/ppermute | solution.py:282
  51.5 8.7 %collective-permute-done.8.c_ref = bf16[256,512]{1,0:T(8,128)(2,1)S(1)} collective-permute-done((bf16[256,512]{1,0:T(8,128)(2,1)S(1)}, bf16[256,512]{1,0:T(8,128)(2,1)S(1)}, u32[]{:S(2)}, u32[]{:S(2)}) %collective-permute-start.8) | collective-permute-done | bytes 262176 | tf_op jit(solution)/shard_map/ppermute | solution.py:282
  60.2 1.0 %shard_map.118 = (bf16[256,256]{1,0:T(8,128)(2,1)}, bf16[256,256]{1,0:T(8,128)(2,1)}) custom-call(f32[128,256]{1,0:T(8,128)S(1)} %get-tuple-element.17.tables_ref, f32[256,512]{1,0:T(8,128)S(1)} %get-tuple-element.23.own_ref, bf16[256,512]{1,0:T(8,128)(2,1)S(1)} %collective-permute-done.6.a_ref, bf16[256,512]{1,0:T(8,128)(2,1)S(1)} %collective-permute-done.7.b_ref, ...), custom_call_target="tpu_custom_call" | custom-call | bytes 2097152 | tf_op jit(solution)/shard_map/pallas_call | solution.py:346
  (14 shorter events, 0.0 us)
Async XLA Ops:
  0.6 14.0 %copy-start.5 = (bf16[256,256]{1,0:T(8,128)(2,1)S(1)}, bf16[256,256]{1,0:T(8,128)(2,1)}, u32[]{:S(2)}) copy-start(bf16[256,256]{1,0:T(8,128)(2,1)} %v_ref.1) | copy-start | bytes 393220
  0.6 14.9 %collective-permute-start.2 = (bf16[256,256]{1,0:T(8,128)(2,1)}, bf16[256,256]{1,0:T(8,128)(2,1)S(1)}, u32[]{:S(2)}, u32[]{:S(2)}) collective-permute-start(bf16[256,256]{1,0:T(8,128)(2,1)} %v_ref.1), channel_id=1, source_target_pairs={{0,28},{4,0},{8,4},{12,8},{16,12},{20,16},{24,20},{28,24},{1,29},{... | collective-permute-start | bytes 393224 | tf_op jit(solution)/shard_map/ppermute | solution.py:282
  12.1 0.9 %copy-start.6 = (bf16[256,256]{1,0:T(8,128)(2,1)S(1)}, bf16[256,256]{1,0:T(8,128)(2,1)}, u32[]{:S(2)}) copy-start(bf16[256,256]{1,0:T(8,128)(2,1)} %k_ref.1) | copy-start | bytes 393220
  13.0 0.8 %copy-start.7 = (f32[64,256]{1,0:T(8,128)S(1)}, f32[64,256]{1,0:T(8,128)}, u32[]{:S(2)}) copy-start(f32[64,256]{1,0:T(8,128)} %constant.8.clone.freq_ref) | copy-start | bytes 196612
  14.1 5.8 %collective-permute-start = (bf16[256,256]{1,0:T(8,128)(2,1)S(1)}, bf16[256,256]{1,0:T(8,128)(2,1)S(1)}, u32[]{:S(2)}, u32[]{:S(2)}) collective-permute-start(bf16[256,256]{1,0:T(8,128)(2,1)S(1)} %get-tuple-element.16.kr_ref), channel_id=1, source_target_pairs={{0,28},{4,0},{8,4},{12,8},{16,12},{20,16},{24,20},{28,24},{1,29},{... | collective-permute-start | bytes 393224 | tf_op jit(solution)/shard_map/ppermute | solution.py:282
  14.7 14.5 %collective-permute-start.5 = (bf16[256,256]{1,0:T(8,128)(2,1)S(1)}, bf16[256,256]{1,0:T(8,128)(2,1)S(1)}, u32[]{:S(2)}, u32[]{:S(2)}) collective-permute-start(bf16[256,256]{1,0:T(8,128)(2,1)S(1)} %copy-done.5), channel_id=1, source_target_pairs={{0,24},{4,28},{8,0},{12,4},{16,8},{20,12},{24,16},{28,20},{1,25},{... | collective-permute-start | bytes 393224 | tf_op jit(solution)/shard_map/ppermute | solution.py:282
  15.1 14.0 %collective-permute-start.4 = (bf16[256,256]{1,0:T(8,128)(2,1)S(1)}, bf16[256,256]{1,0:T(8,128)(2,1)S(1)}, u32[]{:S(2)}, u32[]{:S(2)}) collective-permute-start(bf16[256,256]{1,0:T(8,128)(2,1)S(1)} %get-tuple-element.16.kr_ref), channel_id=1, source_target_pairs={{0,24},{4,28},{8,0},{12,4},{16,8},{20,12},{24,16},{28,20},{1,25},{... | collective-permute-start | bytes 393224 | tf_op jit(solution)/shard_map/ppermute | solution.py:282
  15.6 19.8 %collective-permute-start.3 = (bf16[256,256]{1,0:T(8,128)(2,1)S(1)}, bf16[256,256]{1,0:T(8,128)(2,1)S(1)}, u32[]{:S(2)}, u32[]{:S(2)}) collective-permute-start(bf16[256,256]{1,0:T(8,128)(2,1)S(1)} %collective-permute-done.2.v_ref), channel_id=1, source_target_pairs={{0,24},{4,28},{8,0},{12,4},{16,8},{20,12},{24,16},{28,20},{1,25},{... | collective-permute-start | bytes 393224 | tf_op jit(solution)/shard_map/ppermute | solution.py:282
  19.8 15.5 %collective-permute-start.1 = (bf16[256,256]{1,0:T(8,128)(2,1)S(1)}, bf16[256,256]{1,0:T(8,128)(2,1)S(1)}, u32[]{:S(2)}, u32[]{:S(2)}) collective-permute-start(bf16[256,256]{1,0:T(8,128)(2,1)S(1)} %collective-permute-done.k_ref), channel_id=1, source_target_pairs={{0,24},{4,28},{8,0},{12,4},{16,8},{20,12},{24,16},{28,20},{1,25},{... | collective-permute-start | bytes 393224 | tf_op jit(solution)/shard_map/ppermute | solution.py:282
  20.3 1.0 %copy-start = (bf16[256,1024]{1,0:T(8,128)(2,1)S(1)}, bf16[256,1024]{1,0:T(8,128)(2,1)}, u32[]{:S(2)}) copy-start(bf16[256,1024]{1,0:T(8,128)(2,1)} %do_ref.7) | copy-start | bytes 1572868
  21.3 1.0 %copy-start.2 = (bf16[256,1024]{1,0:T(8,128)(2,1)S(1)}, bf16[256,1024]{1,0:T(8,128)(2,1)}, u32[]{:S(2)}) copy-start(bf16[256,1024]{1,0:T(8,128)(2,1)} %at_hbm.1) | copy-start | bytes 1572868
  22.4 1.0 %copy-start.1 = (bf16[256,1024]{1,0:T(8,128)(2,1)S(1)}, bf16[256,1024]{1,0:T(8,128)(2,1)}, u32[]{:S(2)}) copy-start(bf16[256,1024]{1,0:T(8,128)(2,1)} %do_ref.7) | copy-start | bytes 1572868
  22.4 1.2 %copy-start.3 = (bf16[256,1024]{1,0:T(8,128)(2,1)S(1)}, bf16[256,1024]{1,0:T(8,128)(2,1)}, u32[]{:S(2)}) copy-start(bf16[256,1024]{1,0:T(8,128)(2,1)} %q_hbm.1) | copy-start | bytes 1572868
  22.4 1.2 %copy-start.4 = (f32[8,256]{1,0:T(8,128)S(1)}, f32[8,256]{1,0:T(8,128)}, u32[]{:S(2)}) copy-start(f32[8,256]{1,0:T(8,128)} %lse_ref.7) | copy-start | bytes 24580
  26.3 0.7 %copy-start.8 = (s32[8]{0:T(128)S(1)}, s32[8]{0:T(128)}, u32[]{:S(2)}) copy-start(s32[8]{0:T(128)} %span_ref.5) | copy-start | bytes 100
  31.3 9.3 %collective-permute-start.7 = (bf16[256,512]{1,0:T(8,128)(2,1)S(1)}, bf16[256,512]{1,0:T(8,128)(2,1)S(1)}, u32[]{:S(2)}, u32[]{:S(2)}) collective-permute-start(bf16[256,512]{1,0:T(8,128)(2,1)S(1)} %get-tuple-element.25), channel_id=1, source_target_pairs={{0,8},{4,12},{8,16},{12,20},{16,24},{20,28},{24,0},{28,4},{1,9},{5... | collective-permute-start | bytes 786440 | tf_op jit(solution)/shard_map/ppermute | solution.py:282
  32.9 18.5 %collective-permute-start.6 = (bf16[256,512]{1,0:T(8,128)(2,1)S(1)}, bf16[256,512]{1,0:T(8,128)(2,1)S(1)}, u32[]{:S(2)}, u32[]{:S(2)}) collective-permute-start(bf16[256,512]{1,0:T(8,128)(2,1)S(1)} %get-tuple-element.24), channel_id=1, source_target_pairs={{0,4},{4,8},{8,12},{12,16},{16,20},{20,24},{24,28},{28,0},{1,5},{5... | collective-permute-start | bytes 786440 | tf_op jit(solution)/shard_map/ppermute | solution.py:282
  38.6 21.6 %collective-permute-start.8 = (bf16[256,512]{1,0:T(8,128)(2,1)S(1)}, bf16[256,512]{1,0:T(8,128)(2,1)S(1)}, u32[]{:S(2)}, u32[]{:S(2)}) collective-permute-start(bf16[256,512]{1,0:T(8,128)(2,1)S(1)} %get-tuple-element.26), channel_id=1, source_target_pairs={{0,12},{4,16},{8,20},{12,24},{16,28},{20,0},{24,4},{28,8},{1,13},{... | collective-permute-start | bytes 786440 | tf_op jit(solution)/shard_map/ppermute | solution.py:282

commit v3 on v2

v3 whole, which is shorter than its diff:
```python
import functools
import math

import jax
import jax.numpy as jnp
import numpy as np
from jax import lax
from jax.experimental import pallas as pl
from jax.experimental.pallas import tpu as pltpu
from jax.sharding import PartitionSpec as P

HEAD = 128
HALF = HEAD // 2
WIN = 4
ROPE_BASE = 1000000.0
YARN_FACTOR = 4.0
YARN_INITIAL = 32768.0
BETA_FAST = 32.0
BETA_SLOW = 1.0
YARN_MSCALE = 1.0 + 0.1 * math.log(4.0)
ROOT_SCALE = 1.0 / math.sqrt(HEAD)
LOG2E = math.log2(math.e)
VMEM_LIMIT = 24 * 1024 * 1024

F32 = jnp.float32
BF16 = jnp.bfloat16


def frequencies():
    pair = np.arange(HALF, dtype=np.float64)
    inverse = np.exp(-2.0 * pair / HEAD * math.log(ROPE_BASE))
    ratio = YARN_INITIAL * inverse / (2.0 * math.pi)
    ramp = np.clip((ratio - BETA_SLOW) / (BETA_FAST - BETA_SLOW), 0.0, 1.0)
    return inverse * ((1.0 - ramp) / YARN_FACTOR + ramp)


def frequency_rows(lanes):
    values = frequencies()
    row = lax.broadcasted_iota(jnp.int32, (8, lanes), 0)
    tiles = []
    for first in range(0, HALF, 8):
        tile = jnp.full((8, lanes), float(values[first]), F32)
        for j in range(1, 8):
            tile = jnp.where(row == j, float(values[first + j]), tile)
        tiles.append(tile)
    return jnp.concatenate(tiles, axis=0)


def sine_cosine(angle):
    turns = jnp.floor(angle * (2.0 / math.pi) + 0.5)
    r = angle - turns * 1.5703125
    r = r - turns * 4.837512969970703125e-4
    r = r - turns * 7.54978995489188e-8
    r2 = r * r
    s = r + r * r2 * (-1.6666654611e-1 + r2 * (8.3321608736e-3 - r2 * 1.9515295891e-4))
    c = (
        1.0
        - 0.5 * r2
        + r2
        * r2
        * (4.166664568298827e-2 + r2 * (-1.388731625493765e-3 + r2 * 2.443315711809948e-5))
    )
    quadrant = turns.astype(jnp.int32) & 3
    odd = (quadrant & 1) == 1
    sine = jnp.where(odd, c, s)
    cosine = jnp.where(odd, s, c)
    sine = jnp.where(quadrant >= 2, -sine, sine)
    cosine = jnp.where((quadrant == 1) | (quadrant == 2), -cosine, cosine)
    return sine, cosine


def tables_transposed(place):
    place = place.astype(F32)
    freq = frequency_rows(place.shape[1])
    pair = lax.broadcasted_iota(jnp.int32, freq.shape, 0)
    first = HEAD // 8
    second = first + 3 * HEAD // 16
    chosen = jnp.where(
        pair < first, place[0:1], jnp.where(pair < second, place[1:2], place[2:3])
    )
    sine, cosine = sine_cosine(chosen * freq)
    return cosine * YARN_MSCALE, sine * YARN_MSCALE


def row_tables(cosine_t, sine_t):
    wide = jnp.concatenate([cosine_t, cosine_t], axis=0).T
    signed = jnp.concatenate([-sine_t, sine_t], axis=0).T
    return wide, signed


def rotated(x, wide, signed):
    return x * wide + pltpu.roll(x, HALF, 1) * signed


def dot_nt(a, b):
    return lax.dot_general(a, b, (((1,), (1,)), ((), ())), preferred_element_type=F32)


def dot_nn(a, b):
    return lax.dot_general(a, b, (((1,), (0,)), ((), ())), preferred_element_type=F32)


def dot_tn(a, b):
    return lax.dot_general(a, b, (((0,), (0,)), ((), ())), preferred_element_type=F32)


def pair_part(key, value, query, grad, norm, delta, causal):
    scores = dot_nt(key, query)
    weights = jnp.exp2(scores * (ROOT_SCALE * LOG2E) - norm)
    if causal:
        at_key = lax.broadcasted_iota(jnp.int32, scores.shape, 0)
        at_query = lax.broadcasted_iota(jnp.int32, scores.shape, 1)
        weights = jnp.where(at_key <= at_query, weights, 0.0)
    value_part = dot_nn(weights.astype(BF16), grad)
    score_grad = (weights * (dot_nt(value, grad) - delta)).astype(BF16)
    key_part = dot_nn(score_grad, query)
    query_part = dot_tn(key, score_grad)
    return value_part, key_part, query_part


def key_kernel(slot_ref, own_ref, p1_ref, p2_ref, p3_ref, k_ref, kr_ref, tables_ref):
    pieces = (own_ref[...], p1_ref[...], p2_ref[...], p3_ref[...])
    count = len(pieces)
    head = slot_ref[1]
    parts = []
    for j in range(count):
        back = lax.rem(head - j + count, count)
        part = pieces[0]
        for r in range(1, count):
            part = jnp.where(back == r, pieces[r], part)
        parts.append(part)
    cosine_t, sine_t = tables_transposed(jnp.concatenate(parts, axis=1))
    tables_ref[:HALF, :] = cosine_t
    tables_ref[HALF:, :] = sine_t
    wide, signed = row_tables(cosine_t, sine_t)
    for g in range(k_ref.shape[1] // HEAD):
        cols = pl.ds(g * HEAD, HEAD)
        kr_ref[:, cols] = rotated(k_ref[:, cols].astype(F32), wide, signed).astype(BF16)


def first_kernel(
    tables_ref, kr_ref, v_ref, lse_ref, q_hbm, do_hbm, at_hbm,
    qr_ref, do_ref, norm_ref, delta_ref, dqt_ref, dkv_ref, kv_ref, q_ref, at_ref, sems,
):
    heads = qr_ref.shape[1] // HEAD
    groups = kr_ref.shape[1] // HEAD
    size = heads // groups
    copies = []
    for g in range(groups):
        cols = pl.ds(g * size * HEAD, size * HEAD)
        for i, (source, target) in enumerate(
            ((q_hbm, q_ref), (do_hbm, do_ref), (at_hbm, at_ref))
        ):
            copy = pltpu.make_async_copy(
                source.at[:, cols], target.at[:, cols], sems.at[3 * g + i]
            )
            copy.start()
            copies.append(copy)
    wide, signed = row_tables(tables_ref[:HALF, :], tables_ref[HALF:, :])
    norm = lse_ref[...] * LOG2E
    norm_ref[...] = norm
    kv_ref[:, : groups * HEAD] = kr_ref[...]
    kv_ref[:, groups * HEAD :] = v_ref[...]
    chooser = jnp.ones((8, HEAD), BF16)
    for g in range(groups):
        cols = pl.ds(g * HEAD, HEAD)
        dk = dv = None
        for copy in copies[3 * g : 3 * g + 3]:
            copy.wait()
        for h in range(g * size, (g + 1) * size):
            hc = pl.ds(h * HEAD, HEAD)
            grad = do_ref[:, hc]
            query = rotated(q_ref[:, hc].astype(F32), wide, signed).astype(BF16)
            qr_ref[:, hc] = query
            product = grad.astype(F32) * at_ref[:, hc].astype(F32)
            high = product.astype(BF16)
            low = (product - high.astype(F32)).astype(BF16)
            delta = (dot_nt(chooser, high) + dot_nt(chooser, low))[:1]
            delta_ref[h : h + 1, :] = delta
            v_part, k_part, q_part = pair_part(
                kr_ref[:, cols], v_ref[:, cols], query, grad, norm[h : h + 1], delta, True
            )
            dqt_ref[hc, :] = q_part
            dv = v_part if dv is None else dv + v_part
            dk = k_part if dk is None else dk + k_part
        dkv_ref[:, cols] = dk
        dkv_ref[:, pl.ds((groups + g) * HEAD, HEAD)] = dv


def hop_body(
    step, slot_ref, span_ref, k_ref, v_ref, qr_ref, do_ref, norm_ref, delta_ref,
    dqt_in, dqt_ref, dkv_ref,
):
    rows = qr_ref.shape[0]
    half = rows // 2
    heads = qr_ref.shape[1] // HEAD
    groups = k_ref.shape[1] // HEAD
    size = heads // groups
    me = slot_ref[0]
    other = lax.rem(me + step, span_ref.shape[0])
    earlier = span_ref[other] < span_ref[me]
    norm = norm_ref[...]
    delta = delta_ref[...]

    def run(keys, queries):
        for g in range(groups):
            kc = pl.ds(g * HEAD, HEAD)
            vc = pl.ds((groups + g) * HEAD, HEAD)
            dk = dv = None
            for h in range(g * size, (g + 1) * size):
                hc = pl.ds(h * HEAD, HEAD)
                v_part, k_part, q_part = pair_part(
                    k_ref[keys, kc], v_ref[keys, kc], qr_ref[queries, hc], do_ref[queries, hc],
                    norm[h : h + 1, queries.start :], delta[h : h + 1, queries.start :], False,
                )
                if queries.start:
                    dqt_ref[hc, : queries.start] = dqt_in[hc, : queries.start]
                dqt_ref[hc, queries] = dqt_in[hc, queries] + q_part
                dv = v_part if dv is None else dv + v_part
                dk = k_part if dk is None else dk + k_part
            dkv_ref[keys, kc] = dk.astype(BF16)
            dkv_ref[keys, vc] = dv.astype(BF16)
        if keys.stop < rows:
            dkv_ref[keys.stop :, :] = jnp.zeros((rows - keys.stop, dkv_ref.shape[1]), BF16)

    @pl.when(earlier)
    def _():
        run(slice(0, half), slice(0, rows))

    @pl.when(jnp.logical_not(earlier))
    def _():
        run(slice(0, rows), slice(half, rows))


def last_kernel(
    step, slot_ref, span_ref, kv_ref, qr_ref, do_ref, norm_ref, delta_ref, dqt_in, tables_ref,
    out_ref, dkv_ref, dqt_ref,
):
    width = kv_ref.shape[1] // 2
    hop_body(
        step, slot_ref, span_ref, kv_ref.at[:, :width], kv_ref.at[:, width:], qr_ref, do_ref,
        norm_ref, delta_ref, dqt_in, dqt_ref, dkv_ref,
    )
    cosine_t = tables_ref[:HALF, :] * ROOT_SCALE
    sine_t = tables_ref[HALF:, :] * ROOT_SCALE
    for h in range(qr_ref.shape[1] // HEAD):
        y1 = dqt_ref[pl.ds(h * HEAD, HALF), :]
        y2 = dqt_ref[pl.ds(h * HEAD + HALF, HALF), :]
        turned = jnp.concatenate(
            [y1 * cosine_t + y2 * sine_t, y2 * cosine_t - y1 * sine_t], axis=0
        )
        out_ref[:, pl.ds(h * HEAD, HEAD)] = turned.T.astype(BF16)


def add_kernel(a_ref, b_ref, sum_ref):
    sum_ref[...] = (a_ref[...].astype(F32) + b_ref[...].astype(F32)).astype(BF16)


def final_kernel(tables_ref, own_ref, a_ref, b_ref, dk_ref, dv_ref):
    width = dk_ref.shape[1]
    wide, signed = row_tables(tables_ref[:HALF, :], tables_ref[HALF:, :])
    wide = wide * ROOT_SCALE
    signed = signed * -ROOT_SCALE
    total = own_ref[...] + a_ref[...].astype(F32) + b_ref[...].astype(F32)
    for g in range(width // HEAD):
        cols = pl.ds(g * HEAD, HEAD)
        dk_ref[:, cols] = rotated(total[:, g * HEAD : (g + 1) * HEAD], wide, signed).astype(BF16)
    dv_ref[...] = total[:, width:].astype(BF16)


SMEM = pl.BlockSpec(memory_space=pltpu.SMEM)
VMEM = pl.BlockSpec(memory_space=pltpu.VMEM)
HBM = pl.BlockSpec(memory_space=pltpu.HBM)


def call(kernel, outs, specs, scratch=(), moved=1):
    return pl.pallas_call(
        kernel,
        out_shape=[jax.ShapeDtypeStruct(shape, dtype) for shape, dtype in outs],
        in_specs=specs,
        out_specs=[VMEM] * len(outs),
        scratch_shapes=list(scratch),
        compiler_params=pltpu.CompilerParams(vmem_limit_bytes=VMEM_LIMIT),
        cost_estimate=pl.CostEstimate(
            flops=1 << 20, bytes_accessed=moved << 20, transcendentals=0
        ),
    )


def shifted(value, steps, axis="ctx"):
    count = lax.axis_size(axis)
    pairs = [(source, (source + steps) % count) for source in range(count)]
    return lax.ppermute(value, axis, pairs)


def shards(q, k, v, do, at, lse, positions, span_map):
    rows = q.shape[0]
    wide_q = q.shape[1]
    wide_k = k.shape[1]
    heads = wide_q // HEAD
    slot = jnp.stack([lax.axis_index("ctx"), lax.axis_index("head")]).astype(jnp.int32)
    q, do, at, k_here, span_map, own = (
        pltpu.with_memory_space_constraint(x, pltpu.HBM)
        for x in (q, do, at, k, span_map, positions)
    )

    pieces = [own] + [shifted(positions, r, "head") for r in (1, 2, 3)]
    v1 = shifted(v, -1)
    kr, tables = call(
        key_kernel,
        [((rows, wide_k), BF16), ((HEAD, rows), F32)],
        [SMEM] + [VMEM] * 5,
        moved=16,
    )(slot, *pieces, k_here)
    k1 = shifted(kr, -1)
    v3 = shifted(v1, -2)
    qr, grad, norm, delta, dqt, dkv, kv = call(
        first_kernel,
        [
            ((rows, wide_q), BF16),
            ((rows, wide_q), BF16),
            ((heads, rows), F32),
            ((heads, rows), F32),
            ((wide_q, rows), F32),
            ((rows, 2 * wide_k), F32),
            ((rows, 2 * wide_k), BF16),
        ],
        [VMEM] * 4 + [HBM] * 3,
        [
            pltpu.VMEM((rows, wide_q), BF16),
            pltpu.VMEM((rows, wide_q), BF16),
            pltpu.SemaphoreType.DMA((3 * (wide_k // HEAD),)),
        ],
        moved=12,
    )(tables, kr, v, lse, q, do, at)
    held, _ = lax.optimization_barrier((k1, delta))
    k3 = shifted(held, -2)
    kv2 = shifted(kv, -2)

    parts = {}
    for step, key, value in ((1, k1, v1), (3, k3, v3)):
        dqt, parts[step] = call(
            functools.partial(hop_body, step),
            [((wide_q, rows), F32), ((rows, 2 * wide_k), BF16)],
            [SMEM, SMEM] + [VMEM] * 7,
            moved=8,
        )(slot, span_map, key, value, qr, grad, norm, delta, dqt)
    back3 = shifted(parts[3], 2)
    dq, part2 = call(
        functools.partial(last_kernel, 2),
        [((rows, wide_q), BF16), ((rows, 2 * wide_k), BF16)],
        [SMEM, SMEM] + [VMEM] * 7,
        [pltpu.VMEM((wide_q, rows), F32)],
        moved=8,
    )(slot, span_map, kv2, qr, grad, norm, delta, dqt, tables)
    back2 = shifted(part2, 2)
    (part13,) = call(add_kernel, [((rows, 2 * wide_k), BF16)], [VMEM] * 2)(parts[1], back3)
    back1 = shifted(part13, 1)

    dk, dv = call(
        final_kernel,
        [((rows, wide_k), BF16), ((rows, wide_k), BF16)],
        [VMEM] * 4,
    )(tables, dkv, back1, back2)
    return dq, dk, dv


def solution(mesh):
    placed = (
        P("ctx", "head"),
        P("ctx", "head"),
        P("ctx", "head"),
        P("ctx", "head"),
        P("ctx", "head"),
        P("head", "ctx"),
        P(None, ("ctx", "head")),
        P(),
    )
    return jax.shard_map(
        shards,
        mesh=mesh,
        in_specs=placed,
        out_specs=(P("ctx", "head"), P("ctx", "head"), P("ctx", "head")),
        check_vma=False,
    )
```

time: 61.5 us -> 49.8 us (0.81)
  blocking collectives: 5.28 us -> 0 us
  local copies, waits for them, and re-layouts: 4.83 us -> 0.01 us
  waiting for transfers between devices: 25.8 us -> 22.2 us
  Pallas kernels: 12.4 us -> 14.2 us
    all_gather x1 -> x0, blocking collectives: 5.28 us -> none  [shards(): pos = lax.all_gather(positions, 'head', axis=1, tiled=True)]
    unnamed x19 -> x4, local copies, waits for them, and re-layouts: 4.82 us -> 0.01 us
    ppermute x9 -> x11, waiting for transfers between devices: 25.8 us -> 22.2 us  [shifted(): return lax.ppermute(value, axis, pairs)]
    pallas_call x6, Pallas kernels: 11.5 us -> 13.2 us  [the longest x2 4.58 us: shards(): call(functools.partial(hop_body, step), [((wide_q, rows), F32), ((rows, 2...]
    ppermute x9 -> x11, starting transfers between devices: 12.1 us -> 12.4 us  [shifted(): return lax.ppermute(value, axis, pairs)]
  transfers between devices with their start and end apart: 9 -> 11, of which waited for: 4 -> 6; matrix products, arithmetic and copies ran while one was open for 0% -> 0% of each run, Pallas kernels for 19% -> 27%
where the time goes in v3:
time: 49.8 us; the launch traced here: 49.6 us
  waiting for transfers between devices  22.2 us (45%)
  Pallas kernels  14.2 us (29%)
  starting transfers between devices  12.4 us (25%)
  between operations  0.7 us (1%)
    ppermute x11, waiting for transfers between devices, shifted(): return lax.ppermute(value, axis, pairs)  22.2 us
    ppermute x11, starting transfers between devices, shifted(): return lax.ppermute(value, axis, pairs)  12.4 us
    pallas_call x2, Pallas kernels, shards(): call(functools.partial(hop_body, step), [((wide_q, rows), F32), ((rows, 2...  4.58 us
    pallas_call x1, Pallas kernels, shards(): call(first_kernel, [((rows, wide_q), BF16), ((rows, wide_q), BF16), ((hea...  3.95 us
    pallas_call x1, Pallas kernels, shards(): call(functools.partial(last_kernel, 2), [((rows, wide_q), BF16), ((rows,...  3.38 us
    pallas_call x1, Pallas kernels, shards(): call(key_kernel, [((rows, wide_k), BF16), ((HEAD, rows), F32)], [SMEM] +...  1.25 us
  transfers between devices with their start and end apart: 11, of which 6 were waited for; matrix products, arithmetic and copies ran while one was open for 0% of the time, Pallas kernels for 27%

profile of v3, /device:TPU:0, one launch (start us, length us, event | category | flops | bytes accessed | tf_op | source)
XLA Modules:
  0.0 49.6 jit_solution(9834963687424317866)
XLA Ops:
  0.6 3.0 %collective-permute-start.1 = (s32[3,64]{1,0:T(4,128)}, s32[3,64]{1,0:T(4,128)S(1)}, u32[]{:S(2)}, u32[]{:S(2)}) collective-permute-start(s32[3,64]{1,0:T(4,128)} %own_ref.1), channel_id=1, source_target_pairs={{0,2},{1,3},{2,0},{3,1},{4,6},{5,7},{6,4},{7,5},{8,10},{9,11},{10,... | collective-permute-start | bytes 2312 | tf_op jit(solution)/shard_map/ppermute | solution.py:293
  3.6 0.0 collective-permute-start
  3.6 1.7 %collective-permute-start.2 = (s32[3,64]{1,0:T(4,128)}, s32[3,64]{1,0:T(4,128)S(1)}, u32[]{:S(2)}, u32[]{:S(2)}) collective-permute-start(s32[3,64]{1,0:T(4,128)} %own_ref.1), channel_id=1, source_target_pairs={{0,3},{1,0},{2,1},{3,2},{4,7},{5,4},{6,5},{7,6},{8,11},{9,8},{10,9... | collective-permute-start | bytes 2312 | tf_op jit(solution)/shard_map/ppermute | solution.py:293
  5.4 4.6 %collective-permute-start.6 = (bf16[256,256]{1,0:T(8,128)(2,1)}, bf16[256,256]{1,0:T(8,128)(2,1)S(1)}, u32[]{:S(2)}, u32[]{:S(2)}) collective-permute-start(bf16[256,256]{1,0:T(8,128)(2,1)} %v_ref.1), channel_id=1, source_target_pairs={{0,28},{4,0},{8,4},{12,8},{16,12},{20,16},{24,20},{28,24},{1,29},{... | collective-permute-start | bytes 393224 | tf_op jit(solution)/shard_map/ppermute | solution.py:293
  9.9 0.1 pad_add_fusion.slot_ref
  10.0 0.0 collective-permute-done.1.p2_ref
  10.0 0.0 collective-permute-done.p1_ref
  10.0 0.0 collective-permute-done.2.p3_ref
  10.0 0.0 copy-start.1
  10.0 1.2 %shard_map.103 = (bf16[256,256]{1,0:T(8,128)(2,1)S(1)}, f32[128,256]{1,0:T(8,128)S(1)}) custom-call(s32[2]{0:T(128)S(1)} %pad_add_fusion.slot_ref, s32[3,64]{1,0:T(4,128)} %own_ref.1, s32[3,64]{1,0:T(4,128)S(1)} %collective-permute-done.p1_ref, s32[3,64]{1,0:T(4,128)S(1)} %collective-permute-done.1.p2_ref, s32[3,64]{1,0:T(4,128)S(1)} %collective-permute-done.2.p3_ref, ...), custom_call_target="tpu_custom_call" | custom-call | flops 1048576 | bytes 16777216 | tf_op jit(solution)/shard_map/pallas_call | solution.py:309
  11.3 1.5 %collective-permute-start.4 = (bf16[256,256]{1,0:T(8,128)(2,1)S(1)}, bf16[256,256]{1,0:T(8,128)(2,1)S(1)}, u32[]{:S(2)}, u32[]{:S(2)}) collective-permute-start(bf16[256,256]{1,0:T(8,128)(2,1)S(1)} %get-tuple-element.22.kr_ref), channel_id=1, source_target_pairs={{0,28},{4,0},{8,4},{12,8},{16,12},{20,16},{24,20},{28,24},{1,29},{... | collective-permute-start | bytes 393224 | tf_op jit(solution)/shard_map/ppermute | solution.py:293
  12.8 0.0 copy-done.1
  12.8 3.9 %shard_map.104 = (bf16[256,1024]{1,0:T(8,128)(2,1)S(1)}, bf16[256,1024]{1,0:T(8,128)(2,1)S(1)}, f32[8,256]{1,0:T(8,128)S(1)}, f32[8,256]{1,0:T(8,128)S(1)}, f32[...) custom-call(f32[128,256]{1,0:T(8,128)S(1)} %get-tuple-element.21.tables_ref, ...), custom_call_target="tpu_custom_call" | custom-call | flops 1048576 | bytes 12582912 | tf_op jit(solution)/shard_map/pallas_call | solution.py:317
  16.7 0.0 collective-permute-done.6.v_ref
  16.7 0.5 %collective-permute-start.7 = (bf16[256,256]{1,0:T(8,128)(2,1)S(1)}, bf16[256,256]{1,0:T(8,128)(2,1)S(1)}, u32[]{:S(2)}, u32[]{:S(2)}) collective-permute-start(bf16[256,256]{1,0:T(8,128)(2,1)S(1)} %collective-permute-done.6.v_ref), channel_id=1, source_target_pairs={{0,24},{4,28},{8,0},{12,4},{16,8},{20,12},{24,16},{28,20},{1,25},{... | collective-permute-start | bytes 393224 | tf_op jit(solution)/shard_map/ppermute | solution.py:293
  17.2 0.0 collective-permute-done.4.k_ref
  17.2 0.6 %collective-permute-start.5 = (bf16[256,256]{1,0:T(8,128)(2,1)S(1)}, bf16[256,256]{1,0:T(8,128)(2,1)S(1)}, u32[]{:S(2)}, u32[]{:S(2)}) collective-permute-start(bf16[256,256]{1,0:T(8,128)(2,1)S(1)} %collective-permute-done.4.k_ref), channel_id=1, source_target_pairs={{0,24},{4,28},{8,0},{12,4},{16,8},{20,12},{24,16},{28,20},{1,25},{... | collective-permute-start | bytes 393224 | tf_op jit(solution)/shard_map/ppermute | solution.py:293
  17.8 0.4 collective-permute-start.3
  18.3 2.3 %shard_map.105 = (f32[1024,256]{1,0:T(8,128)S(1)}, bf16[256,512]{1,0:T(8,128)(2,1)S(1)}) custom-call(s32[2]{0:T(128)S(1)} %pad_add_fusion.slot_ref, s32[8]{0:T(128)} %span_ref.5, bf16[256,256]{1,0:T(8,128)(2,1)S(1)} %collective-permute-done.4.k_ref, bf16[256,256]{1,0:T(8,128)(2,1)S(1)} %collective-permute-done.6.v_ref, ...), custom_call_target="tpu_custom_call" | custom-call | flops 1048576 | bytes 8388608 | tf_op jit(solution)/shard_map/pallas_call | solution.py:342
  20.6 2.5 %collective-permute-done.7.v_ref = bf16[256,256]{1,0:T(8,128)(2,1)S(1)} collective-permute-done((bf16[256,256]{1,0:T(8,128)(2,1)S(1)}, bf16[256,256]{1,0:T(8,128)(2,1)S(1)}, u32[]{:S(2)}, u32[]{:S(2)}) %collective-permute-start.7) | collective-permute-done | bytes 131104 | tf_op jit(solution)/shard_map/ppermute | solution.py:293
  23.1 2.8 %collective-permute-done.5.k_ref = bf16[256,256]{1,0:T(8,128)(2,1)S(1)} collective-permute-done((bf16[256,256]{1,0:T(8,128)(2,1)S(1)}, bf16[256,256]{1,0:T(8,128)(2,1)S(1)}, u32[]{:S(2)}, u32[]{:S(2)}) %collective-permute-start.5) | collective-permute-done | bytes 131104 | tf_op jit(solution)/shard_map/ppermute | solution.py:293
  25.9 2.3 %shard_map.106 = (f32[1024,256]{1,0:T(8,128)S(1)}, bf16[256,512]{1,0:T(8,128)(2,1)S(1)}) custom-call(s32[2]{0:T(128)S(1)} %pad_add_fusion.slot_ref, s32[8]{0:T(128)} %span_ref.5, bf16[256,256]{1,0:T(8,128)(2,1)S(1)} %collective-permute-done.5.k_ref, bf16[256,256]{1,0:T(8,128)(2,1)S(1)} %collective-permute-done.7.v_ref, ...), custom_call_target="tpu_custom_call" | custom-call | flops 1048576 | bytes 8388608 | tf_op jit(solution)/shard_map/pallas_call | solution.py:342
  28.2 0.1 collective-permute-start.8
  28.3 2.7 %collective-permute-done.3.kv_ref = bf16[256,512]{1,0:T(8,128)(2,1)S(1)} collective-permute-done((bf16[256,512]{1,0:T(8,128)(2,1)S(1)}, bf16[256,512]{1,0:T(8,128)(2,1)S(1)}, u32[]{:S(2)}, u32[]{:S(2)}) %collective-permute-start.3) | collective-permute-done | bytes 262176 | tf_op jit(solution)/shard_map/ppermute | solution.py:293
  31.0 3.4 %shard_map.107 = (bf16[256,1024]{1,0:T(8,128)(2,1)}, bf16[256,512]{1,0:T(8,128)(2,1)S(1)}) custom-call(s32[2]{0:T(128)S(1)} %pad_add_fusion.slot_ref, s32[8]{0:T(128)} %span_ref.5, bf16[256,512]{1,0:T(8,128)(2,1)S(1)} %collective-permute-done.3.kv_ref, bf16[256,1024]{1,0:T(8,128)(2,1)S(1)} %get-tuple-element.24.qr_ref, ...), custom_call_target="tpu_custom_call" | custom-call | flops 1048576 | bytes 8388608 | tf_op jit(solution)/shard_map/pallas_call | solution.py:349
  34.3 0.0 collective-permute-start.10
  34.3 2.9 %collective-permute-done.8.b_ref = bf16[256,512]{1,0:T(8,128)(2,1)S(1)} collective-permute-done((bf16[256,512]{1,0:T(8,128)(2,1)S(1)}, bf16[256,512]{1,0:T(8,128)(2,1)S(1)}, u32[]{:S(2)}, u32[]{:S(2)}) %collective-permute-start.8) | collective-permute-done | bytes 262176 | tf_op jit(solution)/shard_map/ppermute | solution.py:293
  37.2 0.1 shard_map.108
  37.3 0.1 collective-permute-start.9
  37.3 6.5 %collective-permute-done.10.b_ref = bf16[256,512]{1,0:T(8,128)(2,1)S(1)} collective-permute-done((bf16[256,512]{1,0:T(8,128)(2,1)S(1)}, bf16[256,512]{1,0:T(8,128)(2,1)S(1)}, u32[]{:S(2)}, u32[]{:S(2)}) %collective-permute-start.10) | collective-permute-done | bytes 262176 | tf_op jit(solution)/shard_map/ppermute | solution.py:293
  43.9 4.8 %collective-permute-done.9.a_ref = bf16[256,512]{1,0:T(8,128)(2,1)S(1)} collective-permute-done((bf16[256,512]{1,0:T(8,128)(2,1)S(1)}, bf16[256,512]{1,0:T(8,128)(2,1)S(1)}, u32[]{:S(2)}, u32[]{:S(2)}) %collective-permute-start.9) | collective-permute-done | bytes 262176 | tf_op jit(solution)/shard_map/ppermute | solution.py:293
  48.7 1.0 %shard_map.109 = (bf16[256,256]{1,0:T(8,128)(2,1)}, bf16[256,256]{1,0:T(8,128)(2,1)}) custom-call(f32[128,256]{1,0:T(8,128)S(1)} %get-tuple-element.21.tables_ref, f32[256,512]{1,0:T(8,128)S(1)} %get-tuple-element.33.own_ref, bf16[256,512]{1,0:T(8,128)(2,1)S(1)} %collective-permute-done.9.a_ref, bf16[256,512]{1,0:T(8,128)(2,1)S(1)} %collective-permute-done.10.b_ref), custom_call_target="tpu_custom_call" | custom-call | flops 1048576 | bytes 1048576 | tf_op jit(solution)/shard_map/pallas_call | solution.py:360
  (2 shorter events, 0.0 us)
Async XLA Ops:
  0.6 12.1 %copy-start = (bf16[256,256]{1,0:T(8,128)(2,1)S(1)}, bf16[256,256]{1,0:T(8,128)(2,1)}, u32[]{:S(2)}) copy-start(bf16[256,256]{1,0:T(8,128)(2,1)} %v_ref.1) | copy-start | bytes 393220
  0.6 9.4 %collective-permute-start.1 = (s32[3,64]{1,0:T(4,128)}, s32[3,64]{1,0:T(4,128)S(1)}, u32[]{:S(2)}, u32[]{:S(2)}) collective-permute-start(s32[3,64]{1,0:T(4,128)} %own_ref.1), channel_id=1, source_target_pairs={{0,2},{1,3},{2,0},{3,1},{4,6},{5,7},{6,4},{7,5},{8,10},{9,11},{10,... | collective-permute-start | bytes 2312 | tf_op jit(solution)/shard_map/ppermute | solution.py:293
  3.6 6.4 %collective-permute-start = (s32[3,64]{1,0:T(4,128)}, s32[3,64]{1,0:T(4,128)S(1)}, u32[]{:S(2)}, u32[]{:S(2)}) collective-permute-start(s32[3,64]{1,0:T(4,128)} %own_ref.1), channel_id=1, source_target_pairs={{0,1},{1,2},{2,3},{3,0},{4,5},{5,6},{6,7},{7,4},{8,9},{9,10},{10,1... | collective-permute-start | bytes 2312 | tf_op jit(solution)/shard_map/ppermute | solution.py:293
  3.6 6.4 %collective-permute-start.2 = (s32[3,64]{1,0:T(4,128)}, s32[3,64]{1,0:T(4,128)S(1)}, u32[]{:S(2)}, u32[]{:S(2)}) collective-permute-start(s32[3,64]{1,0:T(4,128)} %own_ref.1), channel_id=1, source_target_pairs={{0,3},{1,0},{2,1},{3,2},{4,7},{5,4},{6,5},{7,6},{8,11},{9,8},{10,9... | collective-permute-start | bytes 2312 | tf_op jit(solution)/shard_map/ppermute | solution.py:293
  5.4 11.3 %collective-permute-start.6 = (bf16[256,256]{1,0:T(8,128)(2,1)}, bf16[256,256]{1,0:T(8,128)(2,1)S(1)}, u32[]{:S(2)}, u32[]{:S(2)}) collective-permute-start(bf16[256,256]{1,0:T(8,128)(2,1)} %v_ref.1), channel_id=1, source_target_pairs={{0,28},{4,0},{8,4},{12,8},{16,12},{20,16},{24,20},{28,24},{1,29},{... | collective-permute-start | bytes 393224 | tf_op jit(solution)/shard_map/ppermute | solution.py:293
  10.0 2.7 %copy-start.1 = (f32[8,256]{1,0:T(8,128)S(1)}, f32[8,256]{1,0:T(8,128)}, u32[]{:S(2)}) copy-start(f32[8,256]{1,0:T(8,128)} %lse_ref.1) | copy-start | bytes 24580
  11.3 6.0 %collective-permute-start.4 = (bf16[256,256]{1,0:T(8,128)(2,1)S(1)}, bf16[256,256]{1,0:T(8,128)(2,1)S(1)}, u32[]{:S(2)}, u32[]{:S(2)}) collective-permute-start(bf16[256,256]{1,0:T(8,128)(2,1)S(1)} %get-tuple-element.22.kr_ref), channel_id=1, source_target_pairs={{0,28},{4,0},{8,4},{12,8},{16,12},{20,16},{24,20},{28,24},{1,29},{... | collective-permute-start | bytes 393224 | tf_op jit(solution)/shard_map/ppermute | solution.py:293
  16.7 6.4 %collective-permute-start.7 = (bf16[256,256]{1,0:T(8,128)(2,1)S(1)}, bf16[256,256]{1,0:T(8,128)(2,1)S(1)}, u32[]{:S(2)}, u32[]{:S(2)}) collective-permute-start(bf16[256,256]{1,0:T(8,128)(2,1)S(1)} %collective-permute-done.6.v_ref), channel_id=1, source_target_pairs={{0,24},{4,28},{8,0},{12,4},{16,8},{20,12},{24,16},{28,20},{1,25},{... | collective-permute-start | bytes 393224 | tf_op jit(solution)/shard_map/ppermute | solution.py:293
  17.2 8.7 %collective-permute-start.5 = (bf16[256,256]{1,0:T(8,128)(2,1)S(1)}, bf16[256,256]{1,0:T(8,128)(2,1)S(1)}, u32[]{:S(2)}, u32[]{:S(2)}) collective-permute-start(bf16[256,256]{1,0:T(8,128)(2,1)S(1)} %collective-permute-done.4.k_ref), channel_id=1, source_target_pairs={{0,24},{4,28},{8,0},{12,4},{16,8},{20,12},{24,16},{28,20},{1,25},{... | collective-permute-start | bytes 393224 | tf_op jit(solution)/shard_map/ppermute | solution.py:293
  17.8 13.1 %collective-permute-start.3 = (bf16[256,512]{1,0:T(8,128)(2,1)S(1)}, bf16[256,512]{1,0:T(8,128)(2,1)S(1)}, u32[]{:S(2)}, u32[]{:S(2)}) collective-permute-start(bf16[256,512]{1,0:T(8,128)(2,1)S(1)} %get-tuple-element.23), channel_id=1, source_target_pairs={{0,24},{4,28},{8,0},{12,4},{16,8},{20,12},{24,16},{28,20},{1,25},{... | collective-permute-start | bytes 786440 | tf_op jit(solution)/shard_map/ppermute | solution.py:293
  28.2 9.0 %collective-permute-start.8 = (bf16[256,512]{1,0:T(8,128)(2,1)S(1)}, bf16[256,512]{1,0:T(8,128)(2,1)S(1)}, u32[]{:S(2)}, u32[]{:S(2)}) collective-permute-start(bf16[256,512]{1,0:T(8,128)(2,1)S(1)} %get-tuple-element.35), channel_id=1, source_target_pairs={{0,8},{4,12},{8,16},{12,20},{16,24},{20,28},{24,0},{28,4},{1,9},{5... | collective-permute-start | bytes 786440 | tf_op jit(solution)/shard_map/ppermute | solution.py:293
  34.3 9.5 %collective-permute-start.10 = (bf16[256,512]{1,0:T(8,128)(2,1)S(1)}, bf16[256,512]{1,0:T(8,128)(2,1)S(1)}, u32[]{:S(2)}, u32[]{:S(2)}) collective-permute-start(bf16[256,512]{1,0:T(8,128)(2,1)S(1)} %get-tuple-element.36), channel_id=1, source_target_pairs={{0,8},{4,12},{8,16},{12,20},{16,24},{20,28},{24,0},{28,4},{1,9},{5... | collective-permute-start | bytes 786440 | tf_op jit(solution)/shard_map/ppermute | solution.py:293
  37.3 11.4 %collective-permute-start.9 = (bf16[256,512]{1,0:T(8,128)(2,1)S(1)}, bf16[256,512]{1,0:T(8,128)(2,1)S(1)}, u32[]{:S(2)}, u32[]{:S(2)}) collective-permute-start(bf16[256,512]{1,0:T(8,128)(2,1)S(1)} %shard_map.108), channel_id=1, source_target_pairs={{0,4},{4,8},{8,12},{12,16},{16,20},{20,24},{24,28},{28,0},{1,5},{5... | collective-permute-start | bytes 786440 | tf_op jit(solution)/shard_map/ppermute | solution.py:293

commit v4 on v3

--- a/solution.py
+++ b/solution.py
@@ -70,7 +70,6 @@
 
 
 def tables_transposed(place):
-    place = place.astype(F32)
     freq = frequency_rows(place.shape[1])
     pair = lax.broadcasted_iota(jnp.int32, freq.shape, 0)
     first = HEAD // 8
@@ -118,7 +117,9 @@
     return value_part, key_part, query_part
 
 
-def key_kernel(slot_ref, own_ref, p1_ref, p2_ref, p3_ref, k_ref, kr_ref, tables_ref):
+def key_kernel(
+    slot_ref, own_ref, p1_ref, p2_ref, p3_ref, k_ref, v_ref, tables_ref, kv_ref, packed_ref
+):
     pieces = (own_ref[...], p1_ref[...], p2_ref[...], p3_ref[...])
     count = len(pieces)
     head = slot_ref[1]
@@ -129,21 +130,29 @@
         for r in range(1, count):
             part = jnp.where(back == r, pieces[r], part)
         parts.append(part)
-    cosine_t, sine_t = tables_transposed(jnp.concatenate(parts, axis=1))
+    place = jnp.concatenate(parts, axis=1)
+    rows, width = v_ref.shape
+    packed_ref[:rows, :] = v_ref[...]
+    kv_ref[:, width:] = v_ref[...]
+    spare = jnp.zeros((packed_ref.shape[0] - rows - 6, place.shape[1]), F32)
+    packed_ref[rows:, :] = jnp.concatenate(
+        [(place >> 6).astype(F32), (place & 63).astype(F32), spare], axis=0
+    ).astype(BF16)
+    cosine_t, sine_t = tables_transposed(place.astype(F32))
     tables_ref[:HALF, :] = cosine_t
     tables_ref[HALF:, :] = sine_t
     wide, signed = row_tables(cosine_t, sine_t)
-    for g in range(k_ref.shape[1] // HEAD):
+    for g in range(width // HEAD):
         cols = pl.ds(g * HEAD, HEAD)
-        kr_ref[:, cols] = rotated(k_ref[:, cols].astype(F32), wide, signed).astype(BF16)
+        kv_ref[:, cols] = rotated(k_ref[:, cols].astype(F32), wide, signed).astype(BF16)
 
 
 def first_kernel(
-    tables_ref, kr_ref, v_ref, lse_ref, q_hbm, do_hbm, at_hbm,
-    qr_ref, do_ref, norm_ref, delta_ref, dqt_ref, dkv_ref, kv_ref, q_ref, at_ref, sems,
+    tables_ref, kv_ref, lse_ref, q_hbm, do_hbm, at_hbm,
+    qr_ref, do_ref, norm_ref, delta_ref, dqt_ref, dkv_ref, q_ref, at_ref, sems,
 ):
     heads = qr_ref.shape[1] // HEAD
-    groups = kr_ref.shape[1] // HEAD
+    groups = kv_ref.shape[1] // HEAD // 2
     size = heads // groups
     copies = []
     for g in range(groups):
@@ -159,8 +168,6 @@
     wide, signed = row_tables(tables_ref[:HALF, :], tables_ref[HALF:, :])
     norm = lse_ref[...] * LOG2E
     norm_ref[...] = norm
-    kv_ref[:, : groups * HEAD] = kr_ref[...]
-    kv_ref[:, groups * HEAD :] = v_ref[...]
     chooser = jnp.ones((8, HEAD), BF16)
     for g in range(groups):
         cols = pl.ds(g * HEAD, HEAD)
@@ -178,7 +185,8 @@
             delta = (dot_nt(chooser, high) + dot_nt(chooser, low))[:1]
             delta_ref[h : h + 1, :] = delta
             v_part, k_part, q_part = pair_part(
-                kr_ref[:, cols], v_ref[:, cols], query, grad, norm[h : h + 1], delta, True
+                kv_ref[:, cols], kv_ref[:, pl.ds((groups + g) * HEAD, HEAD)], query, grad,
+                norm[h : h + 1], delta, True,
             )
             dqt_ref[hc, :] = q_part
             dv = v_part if dv is None else dv + v_part
@@ -232,18 +240,42 @@
         run(slice(0, rows), slice(half, rows))
 
 
-def last_kernel(
-    step, slot_ref, span_ref, kv_ref, qr_ref, do_ref, norm_ref, delta_ref, dqt_in, tables_ref,
-    out_ref, dkv_ref, dqt_ref,
+def rotate_arrived(k_ref, packed_ref, key_ref):
+    rows = k_ref.shape[0]
+    tail = packed_ref[rows:, :].astype(F32)
+    wide, signed = row_tables(*tables_transposed(tail[0:3] * 64.0 + tail[3:6]))
+    for g in range(k_ref.shape[1] // HEAD):
+        cols = pl.ds(g * HEAD, HEAD)
+        key_ref[:, cols] = rotated(k_ref[:, cols].astype(F32), wide, signed).astype(BF16)
+
+
+def raw_kernel(
+    step, slot_ref, span_ref, k_ref, packed_ref, qr_ref, do_ref, norm_ref, delta_ref, dqt_in,
+    dqt_ref, dkv_ref, key_ref,
+):
+    rotate_arrived(k_ref, packed_ref, key_ref)
+    hop_body(
+        step, slot_ref, span_ref, key_ref, packed_ref, qr_ref, do_ref, norm_ref, delta_ref,
+        dqt_in, dqt_ref, dkv_ref,
+    )
+
+
+def turned_kernel(
+    step, slot_ref, span_ref, kv_ref, qr_ref, do_ref, norm_ref, delta_ref, dqt_in,
+    dqt_ref, dkv_ref,
 ):
     width = kv_ref.shape[1] // 2
     hop_body(
         step, slot_ref, span_ref, kv_ref.at[:, :width], kv_ref.at[:, width:], qr_ref, do_ref,
         norm_ref, delta_ref, dqt_in, dqt_ref, dkv_ref,
     )
+
+
+def query_kernel(tables_ref, dqt_ref, own_ref, back_ref, out_ref, sum_ref):
+    sum_ref[...] = own_ref[...] + back_ref[...].astype(F32)
     cosine_t = tables_ref[:HALF, :] * ROOT_SCALE
     sine_t = tables_ref[HALF:, :] * ROOT_SCALE
-    for h in range(qr_ref.shape[1] // HEAD):
+    for h in range(out_ref.shape[1] // HEAD):
         y1 = dqt_ref[pl.ds(h * HEAD, HALF), :]
         y2 = dqt_ref[pl.ds(h * HEAD + HALF, HALF), :]
         turned = jnp.concatenate(
@@ -256,12 +288,12 @@
     sum_ref[...] = (a_ref[...].astype(F32) + b_ref[...].astype(F32)).astype(BF16)
 
 
-def final_kernel(tables_ref, own_ref, a_ref, b_ref, dk_ref, dv_ref):
+def final_kernel(tables_ref, own_ref, a_ref, dk_ref, dv_ref):
     width = dk_ref.shape[1]
     wide, signed = row_tables(tables_ref[:HALF, :], tables_ref[HALF:, :])
     wide = wide * ROOT_SCALE
     signed = signed * -ROOT_SCALE
-    total = own_ref[...] + a_ref[...].astype(F32) + b_ref[...].astype(F32)
+    total = own_ref[...] + a_ref[...].astype(F32)
     for g in range(width // HEAD):
         cols = pl.ds(g * HEAD, HEAD)
         dk_ref[:, cols] = rotated(total[:, g * HEAD : (g + 1) * HEAD], wide, signed).astype(BF16)
@@ -299,22 +331,24 @@
     wide_k = k.shape[1]
     heads = wide_q // HEAD
     slot = jnp.stack([lax.axis_index("ctx"), lax.axis_index("head")]).astype(jnp.int32)
-    q, do, at, k_here, span_map, own = (
+    q, do, at, k_here, v_here, span_map, own = (
         pltpu.with_memory_space_constraint(x, pltpu.HBM)
-        for x in (q, do, at, k, span_map, positions)
-    )
-
+        for x in (q, do, at, k, v, span_map, positions)
+    )
+
+    k1 = shifted(k, -1)
     pieces = [own] + [shifted(positions, r, "head") for r in (1, 2, 3)]
-    v1 = shifted(v, -1)
-    kr, tables = call(
+    k1, *pieces = lax.optimization_barrier((k1, *pieces))
+    tables, kv, packed = call(
         key_kernel,
-        [((rows, wide_k), BF16), ((HEAD, rows), F32)],
-        [SMEM] + [VMEM] * 5,
+        [((HEAD, rows), F32), ((rows, 2 * wide_k), BF16), ((rows + 16, wide_k), BF16)],
+        [SMEM] + [VMEM] * 6,
         moved=16,
-    )(slot, *pieces, k_here)
-    k1 = shifted(kr, -1)
-    v3 = shifted(v1, -2)
-    qr, grad, norm, delta, dqt, dkv, kv = call(
+    )(slot, *pieces, k_here, v_here)
+    v1 = shifted(packed, -1)
+    kv2 = shifted(kv, -2)
+    k3 = shifted(k1, -2)
+    qr, grad, norm, delta, dqt, dkv = call(
         first_kernel,
         [
             ((rows, wide_q), BF16),
@@ -323,45 +357,43 @@
             ((heads, rows), F32),
             ((wide_q, rows), F32),
             ((rows, 2 * wide_k), F32),
-            ((rows, 2 * wide_k), BF16),
         ],
-        [VMEM] * 4 + [HBM] * 3,
+        [VMEM] * 3 + [HBM] * 3,
         [
             pltpu.VMEM((rows, wide_q), BF16),
             pltpu.VMEM((rows, wide_q), BF16),
             pltpu.SemaphoreType.DMA((3 * (wide_k // HEAD),)),
         ],
         moved=12,
-    )(tables, kr, v, lse, q, do, at)
-    held, _ = lax.optimization_barrier((k1, delta))
-    k3 = shifted(held, -2)
-    kv2 = shifted(kv, -2)
-
-    parts = {}
-    for step, key, value in ((1, k1, v1), (3, k3, v3)):
-        dqt, parts[step] = call(
-            functools.partial(hop_body, step),
-            [((wide_q, rows), F32), ((rows, 2 * wide_k), BF16)],
-            [SMEM, SMEM] + [VMEM] * 7,
-            moved=8,
-        )(slot, span_map, key, value, qr, grad, norm, delta, dqt)
-    back3 = shifted(parts[3], 2)
-    dq, part2 = call(
-        functools.partial(last_kernel, 2),
-        [((rows, wide_q), BF16), ((rows, 2 * wide_k), BF16)],
-        [SMEM, SMEM] + [VMEM] * 7,
-        [pltpu.VMEM((wide_q, rows), F32)],
-        moved=8,
-    )(slot, span_map, kv2, qr, grad, norm, delta, dqt, tables)
+    )(tables, kv, lse, q, do, at)
+    held, _ = lax.optimization_barrier((v1, delta))
+    v3 = shifted(held, -2)
+
+    outs = [((wide_q, rows), F32), ((rows, 2 * wide_k), BF16)]
+    turned_key = pltpu.VMEM((rows, wide_k), BF16)
+    dqt, part1 = call(
+        functools.partial(raw_kernel, 1), outs, [SMEM] * 2 + [VMEM] * 7, [turned_key], moved=8
+    )(slot, span_map, k1, v1, qr, grad, norm, delta, dqt)
+    dqt, part2 = call(
+        functools.partial(turned_kernel, 2), outs, [SMEM] * 2 + [VMEM] * 6, moved=8
+    )(slot, span_map, kv2, qr, grad, norm, delta, dqt)
     back2 = shifted(part2, 2)
-    (part13,) = call(add_kernel, [((rows, 2 * wide_k), BF16)], [VMEM] * 2)(parts[1], back3)
+    dqt, part3 = call(
+        functools.partial(raw_kernel, 3), outs, [SMEM] * 2 + [VMEM] * 7, [turned_key], moved=8
+    )(slot, span_map, k3, v3, qr, grad, norm, delta, dqt)
+    back3 = shifted(part3, 2)
+    dq, dkv = call(
+        query_kernel, [((rows, wide_q), BF16), ((rows, 2 * wide_k), F32)], [VMEM] * 4, moved=4
+    )(tables, dqt, dkv, back2)
+    part1, _ = lax.optimization_barrier((part1, dkv))
+    (part13,) = call(add_kernel, [((rows, 2 * wide_k), BF16)], [VMEM] * 2)(part1, back3)
     back1 = shifted(part13, 1)
 
     dk, dv = call(
         final_kernel,
         [((rows, wide_k), BF16), ((rows, wide_k), BF16)],
-        [VMEM] * 4,
-    )(tables, dkv, back1, back2)
+        [VMEM] * 3,
+    )(tables, dkv, back1)
     return dq, dk, dv
 
 

time: 49.8 us -> 53.3 us (1.070)
  waiting for transfers between devices: 22.2 us -> 23.8 us
  starting transfers between devices: 12.4 us -> 13.8 us
  Pallas kernels: 14.2 us -> 14.8 us
    ppermute x11, waiting for transfers between devices: 22.2 us -> 23.8 us  [shifted(): return lax.ppermute(value, axis, pairs)]
    ppermute x11, starting transfers between devices: 12.4 us -> 13.8 us  [shifted(): return lax.ppermute(value, axis, pairs)]
    pallas_call x5 -> x6, Pallas kernels: 9.27 us -> 9.92 us  [the longest x1 2.57 us: shards(): call(functools.partial(raw_kernel, 3), outs, [SMEM] * 2 + [VMEM] * 7, [tu...]
  transfers between devices with their start and end apart: 11 -> 11, of which waited for: 6 -> 8; matrix products, arithmetic and copies ran while one was open for 0% -> 0% of each run, Pallas kernels for 27% -> 23%
where the time goes in v4:
time: 53.3 us; the launch traced here: 53.1 us
  waiting for transfers between devices  23.8 us (45%)
  Pallas kernels  14.8 us (28%)
  starting transfers between devices  13.8 us (26%)
  between operations  0.69 us (1%)
    ppermute x11, waiting for transfers between devices, shifted(): return lax.ppermute(value, axis, pairs)  23.8 us
    ppermute x11, starting transfers between devices, shifted(): return lax.ppermute(value, axis, pairs)  13.8 us
    pallas_call x1, Pallas kernels, shards(): call(first_kernel, [((rows, wide_q), BF16), ((rows, wide_q), BF16), ((hea...  3.94 us
    pallas_call x1, Pallas kernels, shards(): call(functools.partial(raw_kernel, 3), outs, [SMEM] * 2 + [VMEM] * 7, [tu...  2.57 us
    pallas_call x1, Pallas kernels, shards(): call(functools.partial(raw_kernel, 1), outs, [SMEM] * 2 + [VMEM] * 7, [tu...  2.56 us
    pallas_call x1, Pallas kernels, shards(): call(functools.partial(turned_kernel, 2), outs, [SMEM] * 2 + [VMEM] * 6,...  2.3 us
    pallas_call x1, Pallas kernels, shards(): call(key_kernel, [((HEAD, rows), F32), ((rows, 2 * wide_k), BF16), ((rows...  1.32 us
    pallas_call x1, Pallas kernels, shards(): call(query_kernel, [((rows, wide_q), BF16), ((rows, 2 * wide_k), F32)], [...  1.1 us
  transfers between devices with their start and end apart: 11, of which 8 were waited for; matrix products, arithmetic and copies ran while one was open for 0% of the time, Pallas kernels for 23%

profile of v4, /device:TPU:0, one launch (start us, length us, event | category | flops | bytes accessed | tf_op | source)
XLA Modules:
  0.0 53.1 jit_solution(10063936673612016430)
XLA Ops:
  0.6 6.1 %collective-permute-start = (bf16[256,256]{1,0:T(8,128)(2,1)}, bf16[256,256]{1,0:T(8,128)(2,1)S(1)}, u32[]{:S(2)}, u32[]{:S(2)}) collective-permute-start(bf16[256,256]{1,0:T(8,128)(2,1)} %k_ref.1), channel_id=1, source_target_pairs={{0,28},{4,0},{8,4},{12,8},{16,12},{20,16},{24,20},{28,24},{1,29},{... | collective-permute-start | bytes 393224 | tf_op jit(solution)/shard_map/ppermute | solution.py:325
  6.7 1.5 %collective-permute-start.2 = (s32[3,64]{1,0:T(4,128)}, s32[3,64]{1,0:T(4,128)S(1)}, u32[]{:S(2)}, u32[]{:S(2)}) collective-permute-start(s32[3,64]{1,0:T(4,128)} %own_ref), channel_id=1, source_target_pairs={{0,2},{1,3},{2,0},{3,1},{4,6},{5,7},{6,4},{7,5},{8,10},{9,11},{10,... | collective-permute-start | bytes 2312 | tf_op jit(solution)/shard_map/ppermute | solution.py:325
  8.2 0.0 collective-permute-start.1
  8.2 1.7 %collective-permute-start.3 = (s32[3,64]{1,0:T(4,128)}, s32[3,64]{1,0:T(4,128)S(1)}, u32[]{:S(2)}, u32[]{:S(2)}) collective-permute-start(s32[3,64]{1,0:T(4,128)} %own_ref), channel_id=1, source_target_pairs={{0,3},{1,0},{2,1},{3,2},{4,7},{5,4},{6,5},{7,6},{8,11},{9,8},{10,9... | collective-permute-start | bytes 2312 | tf_op jit(solution)/shard_map/ppermute | solution.py:325
  9.9 0.1 pad_add_fusion.slot_ref
  10.0 0.5 collective-permute-done.2.p2_ref
  10.5 0.9 %collective-permute-done.1.p1_ref = s32[3,64]{1,0:T(4,128)S(1)} collective-permute-done((s32[3,64]{1,0:T(4,128)}, s32[3,64]{1,0:T(4,128)S(1)}, u32[]{:S(2)}, u32[]{:S(2)}) %collective-permute-start.1) | collective-permute-done | bytes 800 | tf_op jit(solution)/shard_map/ppermute | solution.py:325
  11.4 0.0 collective-permute-done.3.p3_ref
  11.4 0.0 collective-permute-done.k_ref
  11.5 1.3 %shard_map.103 = (f32[128,256]{1,0:T(8,128)S(1)}, bf16[256,512]{1,0:T(8,128)(2,1)S(1)}, bf16[272,256]{1,0:T(8,128)(2,1)S(1)}) custom-call(s32[2]{0:T(128)S(1)} %pad_add_fusion.slot_ref, s32[3,64]{1,0:T(4,128)} %own_ref, s32[3,64]{1,0:T(4,128)S(1)} %collective-permute-done.1.p1_ref, s32[3,64]{1,0:T(4,128)S(1)} %collective-permute-done.2.p2_ref, ...), custom_call_target="tpu_custom_call" | custom-call | flops 1048576 | bytes 16777216 | tf_op jit(solution)/shard_map/pallas_call | solution.py:342
  12.8 3.4 %collective-permute-start.5 = (bf16[272,256]{1,0:T(8,128)(2,1)S(1)}, bf16[272,256]{1,0:T(8,128)(2,1)S(1)}, u32[]{:S(2)}, u32[]{:S(2)}) collective-permute-start(bf16[272,256]{1,0:T(8,128)(2,1)S(1)} %get-tuple-element.35), channel_id=1, source_target_pairs={{0,28},{4,0},{8,4},{12,8},{16,12},{20,16},{24,20},{28,24},{1,29},{... | collective-permute-start | bytes 417800 | tf_op jit(solution)/shard_map/ppermute | solution.py:325
  16.2 0.0 collective-permute-start.7
  16.2 0.0 copy-done
  16.2 3.9 %shard_map.104 = (bf16[256,1024]{1,0:T(8,128)(2,1)S(1)}, bf16[256,1024]{1,0:T(8,128)(2,1)S(1)}, f32[8,256]{1,0:T(8,128)S(1)}, f32[8,256]{1,0:T(8,128)S(1)}, f32[...) custom-call(f32[128,256]{1,0:T(8,128)S(1)} %get-tuple-element.33.tables_ref, bf16[256,512]{1,0:T(8,128)(2,1)S(1)} %get-tuple-element.36.kv_ref, ...), custom_call_target="tpu_custom_call" | custom-call | flops 1048576 | bytes 12582912 | tf_op jit(solution)/shard_map/pallas_call | solution.py:351
  20.2 0.2 collective-permute-done.5.packed_ref
  20.3 0.0 collective-permute-start.6
  20.3 0.0 collective-permute-start.4
  20.3 2.6 %shard_map.105 = (f32[1024,256]{1,0:T(8,128)S(1)}, bf16[256,512]{1,0:T(8,128)(2,1)S(1)}) custom-call(s32[2]{0:T(128)S(1)} %pad_add_fusion.slot_ref, s32[8]{0:T(128)} %span_ref.5, bf16[256,256]{1,0:T(8,128)(2,1)S(1)} %collective-permute-done.k_ref, bf16[272,256]{1,0:T(8,128)(2,1)S(1)} %collective-permute-done.5.packed_ref, ...), custom_call_target="tpu_custom_call" | custom-call | flops 1048576 | bytes 8388608 | tf_op jit(solution)/shard_map/pallas_call | solution.py:374
  22.9 3.0 %collective-permute-done.7.kv_ref = bf16[256,512]{1,0:T(8,128)(2,1)S(1)} collective-permute-done((bf16[256,512]{1,0:T(8,128)(2,1)S(1)}, bf16[256,512]{1,0:T(8,128)(2,1)S(1)}, u32[]{:S(2)}, u32[]{:S(2)}) %collective-permute-start.7) | collective-permute-done | bytes 262176 | tf_op jit(solution)/shard_map/ppermute | solution.py:325
  25.9 2.3 %shard_map.106 = (f32[1024,256]{1,0:T(8,128)S(1)}, bf16[256,512]{1,0:T(8,128)(2,1)S(1)}) custom-call(s32[2]{0:T(128)S(1)} %pad_add_fusion.slot_ref, s32[8]{0:T(128)} %span_ref.5, bf16[256,512]{1,0:T(8,128)(2,1)S(1)} %collective-permute-done.7.kv_ref, bf16[256,1024]{1,0:T(8,128)(2,1)S(1)} %get-tuple-element.39.qr_ref, ...), custom_call_target="tpu_custom_call" | custom-call | flops 1048576 | bytes 8388608 | tf_op jit(solution)/shard_map/pallas_call | solution.py:377
  28.3 0.1 collective-permute-start.8
  28.3 3.4 %collective-permute-done.4.k_ref = bf16[256,256]{1,0:T(8,128)(2,1)S(1)} collective-permute-done((bf16[256,256]{1,0:T(8,128)(2,1)S(1)}, bf16[256,256]{1,0:T(8,128)(2,1)S(1)}, u32[]{:S(2)}, u32[]{:S(2)}) %collective-permute-start.4) | collective-permute-done | bytes 131104 | tf_op jit(solution)/shard_map/ppermute | solution.py:325
  31.7 0.0 collective-permute-done.6.packed_ref
  31.8 2.6 %shard_map.107 = (f32[1024,256]{1,0:T(8,128)S(1)}, bf16[256,512]{1,0:T(8,128)(2,1)S(1)}) custom-call(s32[2]{0:T(128)S(1)} %pad_add_fusion.slot_ref, s32[8]{0:T(128)} %span_ref.5, bf16[256,256]{1,0:T(8,128)(2,1)S(1)} %collective-permute-done.4.k_ref, bf16[272,256]{1,0:T(8,128)(2,1)S(1)} %collective-permute-done.6.packed_ref, ...), custom_call_target="tpu_custom_call" | custom-call | flops 1048576 | bytes 8388608 | tf_op jit(solution)/shard_map/pallas_call | solution.py:381
  34.3 0.1 collective-permute-start.9
  34.4 3.9 %collective-permute-done.8.back_ref = bf16[256,512]{1,0:T(8,128)(2,1)S(1)} collective-permute-done((bf16[256,512]{1,0:T(8,128)(2,1)S(1)}, bf16[256,512]{1,0:T(8,128)(2,1)S(1)}, u32[]{:S(2)}, u32[]{:S(2)}) %collective-permute-start.8) | collective-permute-done | bytes 262176 | tf_op jit(solution)/shard_map/ppermute | solution.py:325
  38.3 1.1 %shard_map.108 = (bf16[256,1024]{1,0:T(8,128)(2,1)}, f32[256,512]{1,0:T(8,128)S(1)}) custom-call(f32[128,256]{1,0:T(8,128)S(1)} %get-tuple-element.33.tables_ref, f32[1024,256]{1,0:T(8,128)S(1)} %get-tuple-element.45.dqt_ref, f32[256,512]{1,0:T(8,128)S(1)} %get-tuple-element.46.own_ref, bf16[256,512]{1,0:T(8,128)(2,1)S(1)} %collective-permute-done.8.back_ref), custom_call_target="tpu_custom_call" | custom-call | flops 1048576 | bytes 4194304 | tf_op jit(solution)/shard_map/pallas_call | solution.py:385
  39.4 3.6 %collective-permute-done.9.b_ref = bf16[256,512]{1,0:T(8,128)(2,1)S(1)} collective-permute-done((bf16[256,512]{1,0:T(8,128)(2,1)S(1)}, bf16[256,512]{1,0:T(8,128)(2,1)S(1)}, u32[]{:S(2)}, u32[]{:S(2)}) %collective-permute-start.9) | collective-permute-done | bytes 262176 | tf_op jit(solution)/shard_map/ppermute | solution.py:325
  43.0 0.1 shard_map.109
  43.1 0.9 %collective-permute-start.10 = (bf16[256,512]{1,0:T(8,128)(2,1)S(1)}, bf16[256,512]{1,0:T(8,128)(2,1)S(1)}, u32[]{:S(2)}, u32[]{:S(2)}) collective-permute-start(bf16[256,512]{1,0:T(8,128)(2,1)S(1)} %shard_map.109), channel_id=1, source_target_pairs={{0,4},{4,8},{8,12},{12,16},{16,20},{20,24},{24,28},{28,0},{1,5},{5... | collective-permute-start | bytes 786440 | tf_op jit(solution)/shard_map/ppermute | solution.py:325
  44.0 8.2 %collective-permute-done.10.a_ref = bf16[256,512]{1,0:T(8,128)(2,1)S(1)} collective-permute-done((bf16[256,512]{1,0:T(8,128)(2,1)S(1)}, bf16[256,512]{1,0:T(8,128)(2,1)S(1)}, u32[]{:S(2)}, u32[]{:S(2)}) %collective-permute-start.10) | collective-permute-done | bytes 262176 | tf_op jit(solution)/shard_map/ppermute | solution.py:325
  52.2 0.9 %shard_map.110 = (bf16[256,256]{1,0:T(8,128)(2,1)}, bf16[256,256]{1,0:T(8,128)(2,1)}) custom-call(f32[128,256]{1,0:T(8,128)S(1)} %get-tuple-element.33.tables_ref, f32[256,512]{1,0:T(8,128)S(1)} %get-tuple-element.49.own_ref, bf16[256,512]{1,0:T(8,128)(2,1)S(1)} %collective-permute-done.10.a_ref), custom_call_target="tpu_custom_call" | custom-call | flops 1048576 | bytes 1048576 | tf_op jit(solution)/shard_map/pallas_call | solution.py:392
  (1 shorter events, 0.0 us)
Async XLA Ops:
  0.6 10.8 %collective-permute-start = (bf16[256,256]{1,0:T(8,128)(2,1)}, bf16[256,256]{1,0:T(8,128)(2,1)S(1)}, u32[]{:S(2)}, u32[]{:S(2)}) collective-permute-start(bf16[256,256]{1,0:T(8,128)(2,1)} %k_ref.1), channel_id=1, source_target_pairs={{0,28},{4,0},{8,4},{12,8},{16,12},{20,16},{24,20},{28,24},{1,29},{... | collective-permute-start | bytes 393224 | tf_op jit(solution)/shard_map/ppermute | solution.py:325
  6.7 3.8 %collective-permute-start.2 = (s32[3,64]{1,0:T(4,128)}, s32[3,64]{1,0:T(4,128)S(1)}, u32[]{:S(2)}, u32[]{:S(2)}) collective-permute-start(s32[3,64]{1,0:T(4,128)} %own_ref), channel_id=1, source_target_pairs={{0,2},{1,3},{2,0},{3,1},{4,6},{5,7},{6,4},{7,5},{8,10},{9,11},{10,... | collective-permute-start | bytes 2312 | tf_op jit(solution)/shard_map/ppermute | solution.py:325
  8.2 3.2 %collective-permute-start.1 = (s32[3,64]{1,0:T(4,128)}, s32[3,64]{1,0:T(4,128)S(1)}, u32[]{:S(2)}, u32[]{:S(2)}) collective-permute-start(s32[3,64]{1,0:T(4,128)} %own_ref), channel_id=1, source_target_pairs={{0,1},{1,2},{2,3},{3,0},{4,5},{5,6},{6,7},{7,4},{8,9},{9,10},{10,1... | collective-permute-start | bytes 2312 | tf_op jit(solution)/shard_map/ppermute | solution.py:325
  8.2 3.3 %collective-permute-start.3 = (s32[3,64]{1,0:T(4,128)}, s32[3,64]{1,0:T(4,128)S(1)}, u32[]{:S(2)}, u32[]{:S(2)}) collective-permute-start(s32[3,64]{1,0:T(4,128)} %own_ref), channel_id=1, source_target_pairs={{0,3},{1,0},{2,1},{3,2},{4,7},{5,4},{6,5},{7,6},{8,11},{9,8},{10,9... | collective-permute-start | bytes 2312 | tf_op jit(solution)/shard_map/ppermute | solution.py:325
  11.4 4.8 %copy-start = (f32[8,256]{1,0:T(8,128)S(1)}, f32[8,256]{1,0:T(8,128)}, u32[]{:S(2)}) copy-start(f32[8,256]{1,0:T(8,128)} %lse_ref.1) | copy-start | bytes 24580
  12.8 7.6 %collective-permute-start.5 = (bf16[272,256]{1,0:T(8,128)(2,1)S(1)}, bf16[272,256]{1,0:T(8,128)(2,1)S(1)}, u32[]{:S(2)}, u32[]{:S(2)}) collective-permute-start(bf16[272,256]{1,0:T(8,128)(2,1)S(1)} %get-tuple-element.35), channel_id=1, source_target_pairs={{0,28},{4,0},{8,4},{12,8},{16,12},{20,16},{24,20},{28,24},{1,29},{... | collective-permute-start | bytes 417800 | tf_op jit(solution)/shard_map/ppermute | solution.py:325
  16.2 9.7 %collective-permute-start.7 = (bf16[256,512]{1,0:T(8,128)(2,1)S(1)}, bf16[256,512]{1,0:T(8,128)(2,1)S(1)}, u32[]{:S(2)}, u32[]{:S(2)}) collective-permute-start(bf16[256,512]{1,0:T(8,128)(2,1)S(1)} %get-tuple-element.36.kv_ref), channel_id=1, source_target_pairs={{0,24},{4,28},{8,0},{12,4},{16,8},{20,12},{24,16},{28,20},{1,25},{... | collective-permute-start | bytes 786440 | tf_op jit(solution)/shard_map/ppermute | solution.py:325
  20.3 11.4 %collective-permute-start.6 = (bf16[272,256]{1,0:T(8,128)(2,1)S(1)}, bf16[272,256]{1,0:T(8,128)(2,1)S(1)}, u32[]{:S(2)}, u32[]{:S(2)}) collective-permute-start(bf16[272,256]{1,0:T(8,128)(2,1)S(1)} %collective-permute-done.5.packed_ref), channel_id=1, source_target_pairs={{0,24},{4,28},{8,0},{12,4},{16,8},{20,12},{24,16},{28,20},{1,25},{... | collective-permute-start | bytes 417800 | tf_op jit(solution)/shard_map/ppermute | solution.py:325
  20.3 11.4 %collective-permute-start.4 = (bf16[256,256]{1,0:T(8,128)(2,1)S(1)}, bf16[256,256]{1,0:T(8,128)(2,1)S(1)}, u32[]{:S(2)}, u32[]{:S(2)}) collective-permute-start(bf16[256,256]{1,0:T(8,128)(2,1)S(1)} %collective-permute-done.k_ref), channel_id=1, source_target_pairs={{0,24},{4,28},{8,0},{12,4},{16,8},{20,12},{24,16},{28,20},{1,25},{... | collective-permute-start | bytes 393224 | tf_op jit(solution)/shard_map/ppermute | solution.py:325
  28.3 10.1 %collective-permute-start.8 = (bf16[256,512]{1,0:T(8,128)(2,1)S(1)}, bf16[256,512]{1,0:T(8,128)(2,1)S(1)}, u32[]{:S(2)}, u32[]{:S(2)}) collective-permute-start(bf16[256,512]{1,0:T(8,128)(2,1)S(1)} %get-tuple-element.47), channel_id=1, source_target_pairs={{0,8},{4,12},{8,16},{12,20},{16,24},{20,28},{24,0},{28,4},{1,9},{5... | collective-permute-start | bytes 786440 | tf_op jit(solution)/shard_map/ppermute | solution.py:325
  34.3 8.7 %collective-permute-start.9 = (bf16[256,512]{1,0:T(8,128)(2,1)S(1)}, bf16[256,512]{1,0:T(8,128)(2,1)S(1)}, u32[]{:S(2)}, u32[]{:S(2)}) collective-permute-start(bf16[256,512]{1,0:T(8,128)(2,1)S(1)} %get-tuple-element.52), channel_id=1, source_target_pairs={{0,8},{4,12},{8,16},{12,20},{16,24},{20,28},{24,0},{28,4},{1,9},{5... | collective-permute-start | bytes 786440 | tf_op jit(solution)/shard_map/ppermute | solution.py:325
  43.1 9.1 %collective-permute-start.10 = (bf16[256,512]{1,0:T(8,128)(2,1)S(1)}, bf16[256,512]{1,0:T(8,128)(2,1)S(1)}, u32[]{:S(2)}, u32[]{:S(2)}) collective-permute-start(bf16[256,512]{1,0:T(8,128)(2,1)S(1)} %shard_map.109), channel_id=1, source_target_pairs={{0,4},{4,8},{8,12},{12,16},{16,20},{20,24},{24,28},{28,0},{1,5},{5... | collective-permute-start | bytes 786440 | tf_op jit(solution)/shard_map/ppermute | solution.py:325

commit v5 on v4

--- a/solution.py
+++ b/solution.py
@@ -117,8 +117,20 @@
     return value_part, key_part, query_part
 
 
+def merge_kernel(k_hbm, v_hbm, kv_ref, sems):
+    width = k_hbm.shape[1]
+    copies = [
+        pltpu.make_async_copy(k_hbm, kv_ref.at[:, :width], sems.at[0]),
+        pltpu.make_async_copy(v_hbm, kv_ref.at[:, width:], sems.at[1]),
+    ]
+    for copy in copies:
+        copy.start()
+    for copy in copies:
+        copy.wait()
+
+
 def key_kernel(
-    slot_ref, own_ref, p1_ref, p2_ref, p3_ref, k_ref, v_ref, tables_ref, kv_ref, packed_ref
+    slot_ref, own_ref, p1_ref, p2_ref, p3_ref, raw_ref, tables_ref, kv_ref, packed_ref
 ):
     pieces = (own_ref[...], p1_ref[...], p2_ref[...], p3_ref[...])
     count = len(pieces)
@@ -131,30 +143,33 @@
             part = jnp.where(back == r, pieces[r], part)
         parts.append(part)
     place = jnp.concatenate(parts, axis=1)
-    rows, width = v_ref.shape
-    packed_ref[:rows, :] = v_ref[...]
-    kv_ref[:, width:] = v_ref[...]
-    spare = jnp.zeros((packed_ref.shape[0] - rows - 6, place.shape[1]), F32)
-    packed_ref[rows:, :] = jnp.concatenate(
+    width = raw_ref.shape[1] // 2
+    spare = jnp.zeros((packed_ref.shape[0] - 6, place.shape[1]), F32)
+    packed_ref[...] = jnp.concatenate(
         [(place >> 6).astype(F32), (place & 63).astype(F32), spare], axis=0
     ).astype(BF16)
     cosine_t, sine_t = tables_transposed(place.astype(F32))
     tables_ref[:HALF, :] = cosine_t
     tables_ref[HALF:, :] = sine_t
     wide, signed = row_tables(cosine_t, sine_t)
+    kv_ref[:, width:] = raw_ref[:, width:]
     for g in range(width // HEAD):
         cols = pl.ds(g * HEAD, HEAD)
-        kv_ref[:, cols] = rotated(k_ref[:, cols].astype(F32), wide, signed).astype(BF16)
+        kv_ref[:, cols] = rotated(raw_ref[:, cols].astype(F32), wide, signed).astype(BF16)
 
 
 def first_kernel(
-    tables_ref, kv_ref, lse_ref, q_hbm, do_hbm, at_hbm,
-    qr_ref, do_ref, norm_ref, delta_ref, dqt_ref, dkv_ref, q_ref, at_ref, sems,
+    tables_ref, kv_ref, lse_hbm, q_hbm, do_hbm, at_hbm,
+    qr_ref, do_ref, norm_ref, delta_ref, *rest,
 ):
     heads = qr_ref.shape[1] // HEAD
     groups = kv_ref.shape[1] // HEAD // 2
+    dqt_refs, part_refs = rest[:groups], rest[groups : 2 * groups]
+    q_ref, at_ref, lse_ref, sems = rest[2 * groups :]
     size = heads // groups
     copies = []
+    lse_copy = pltpu.make_async_copy(lse_hbm, lse_ref, sems.at[3 * groups])
+    lse_copy.start()
     for g in range(groups):
         cols = pl.ds(g * size * HEAD, size * HEAD)
         for i, (source, target) in enumerate(
@@ -166,6 +181,7 @@
             copy.start()
             copies.append(copy)
     wide, signed = row_tables(tables_ref[:HALF, :], tables_ref[HALF:, :])
+    lse_copy.wait()
     norm = lse_ref[...] * LOG2E
     norm_ref[...] = norm
     chooser = jnp.ones((8, HEAD), BF16)
@@ -188,16 +204,16 @@
                 kv_ref[:, cols], kv_ref[:, pl.ds((groups + g) * HEAD, HEAD)], query, grad,
                 norm[h : h + 1], delta, True,
             )
-            dqt_ref[hc, :] = q_part
+            dqt_refs[g][pl.ds((h - g * size) * HEAD, HEAD), :] = q_part
             dv = v_part if dv is None else dv + v_part
             dk = k_part if dk is None else dk + k_part
-        dkv_ref[:, cols] = dk
-        dkv_ref[:, pl.ds((groups + g) * HEAD, HEAD)] = dv
+        part_refs[g][:, :HEAD] = dk
+        part_refs[g][:, HEAD:] = dv
 
 
 def hop_body(
-    step, slot_ref, span_ref, k_ref, v_ref, qr_ref, do_ref, norm_ref, delta_ref,
-    dqt_in, dqt_ref, dkv_ref,
+    step, wanted, slot_ref, span_ref, k_ref, v_ref, qr_ref, do_ref, norm_ref, delta_ref,
+    dqt_ins, dqt_refs, part_refs,
 ):
     rows = qr_ref.shape[0]
     half = rows // 2
@@ -211,25 +227,26 @@
     delta = delta_ref[...]
 
     def run(keys, queries):
-        for g in range(groups):
+        for g, dqt_in, dqt_ref, part_ref in zip(wanted, dqt_ins, dqt_refs, part_refs):
             kc = pl.ds(g * HEAD, HEAD)
-            vc = pl.ds((groups + g) * HEAD, HEAD)
             dk = dv = None
-            for h in range(g * size, (g + 1) * size):
+            for j in range(size):
+                h = g * size + j
                 hc = pl.ds(h * HEAD, HEAD)
+                to = pl.ds(j * HEAD, HEAD)
                 v_part, k_part, q_part = pair_part(
                     k_ref[keys, kc], v_ref[keys, kc], qr_ref[queries, hc], do_ref[queries, hc],
                     norm[h : h + 1, queries.start :], delta[h : h + 1, queries.start :], False,
                 )
                 if queries.start:
-                    dqt_ref[hc, : queries.start] = dqt_in[hc, : queries.start]
-                dqt_ref[hc, queries] = dqt_in[hc, queries] + q_part
+                    dqt_ref[to, : queries.start] = dqt_in[to, : queries.start]
+                dqt_ref[to, queries] = dqt_in[to, queries] + q_part
                 dv = v_part if dv is None else dv + v_part
                 dk = k_part if dk is None else dk + k_part
-            dkv_ref[keys, kc] = dk.astype(BF16)
-            dkv_ref[keys, vc] = dv.astype(BF16)
-        if keys.stop < rows:
-            dkv_ref[keys.stop :, :] = jnp.zeros((rows - keys.stop, dkv_ref.shape[1]), BF16)
+            part_ref[keys, :HEAD] = dk.astype(BF16)
+            part_ref[keys, HEAD:] = dv.astype(BF16)
+            if keys.stop < rows:
+                part_ref[keys.stop :, :] = jnp.zeros((rows - keys.stop, 2 * HEAD), BF16)
 
     @pl.when(earlier)
     def _():
@@ -240,64 +257,76 @@
         run(slice(0, rows), slice(half, rows))
 
 
-def rotate_arrived(k_ref, packed_ref, key_ref):
-    rows = k_ref.shape[0]
-    tail = packed_ref[rows:, :].astype(F32)
-    wide, signed = row_tables(*tables_transposed(tail[0:3] * 64.0 + tail[3:6]))
-    for g in range(k_ref.shape[1] // HEAD):
+def spread(refs, wanted):
+    count = len(wanted)
+    dqt_ins, dqt_refs, part_refs = refs[:count], refs[count : 2 * count], refs[2 * count :]
+    if len(part_refs) < count:
+        (part_ref,) = part_refs
+        part_refs = [part_ref.at[:, 2 * HEAD * i : 2 * HEAD * (i + 1)] for i in range(count)]
+    return dqt_ins, dqt_refs, part_refs
+
+
+def raw_kernel(
+    step, wanted, slot_ref, span_ref, kv_ref, packed_ref, qr_ref, do_ref, norm_ref, delta_ref,
+    *rest,
+):
+    key_ref = rest[-1]
+    width = kv_ref.shape[1] // 2
+    place = packed_ref[...].astype(F32)
+    wide, signed = row_tables(*tables_transposed(place[0:3] * 64.0 + place[3:6]))
+    for g in wanted:
         cols = pl.ds(g * HEAD, HEAD)
-        key_ref[:, cols] = rotated(k_ref[:, cols].astype(F32), wide, signed).astype(BF16)
-
-
-def raw_kernel(
-    step, slot_ref, span_ref, k_ref, packed_ref, qr_ref, do_ref, norm_ref, delta_ref, dqt_in,
-    dqt_ref, dkv_ref, key_ref,
-):
-    rotate_arrived(k_ref, packed_ref, key_ref)
+        key_ref[:, cols] = rotated(kv_ref[:, cols].astype(F32), wide, signed).astype(BF16)
     hop_body(
-        step, slot_ref, span_ref, key_ref, packed_ref, qr_ref, do_ref, norm_ref, delta_ref,
-        dqt_in, dqt_ref, dkv_ref,
+        step, wanted, slot_ref, span_ref, key_ref, kv_ref.at[:, width:], qr_ref, do_ref, norm_ref,
+        delta_ref, *spread(rest[:-1], wanted),
     )
 
 
 def turned_kernel(
-    step, slot_ref, span_ref, kv_ref, qr_ref, do_ref, norm_ref, delta_ref, dqt_in,
-    dqt_ref, dkv_ref,
+    step, wanted, slot_ref, span_ref, kv_ref, qr_ref, do_ref, norm_ref, delta_ref, *rest
 ):
     width = kv_ref.shape[1] // 2
     hop_body(
-        step, slot_ref, span_ref, kv_ref.at[:, :width], kv_ref.at[:, width:], qr_ref, do_ref,
-        norm_ref, delta_ref, dqt_in, dqt_ref, dkv_ref,
-    )
-
-
-def query_kernel(tables_ref, dqt_ref, own_ref, back_ref, out_ref, sum_ref):
-    sum_ref[...] = own_ref[...] + back_ref[...].astype(F32)
+        step, wanted, slot_ref, span_ref, kv_ref.at[:, :width], kv_ref.at[:, width:], qr_ref,
+        do_ref, norm_ref, delta_ref, *spread(rest, wanted),
+    )
+
+
+def query_kernel(groups, tables_ref, *refs):
+    dqt_refs, own_refs, back_ref = refs[:groups], refs[groups : 2 * groups], refs[2 * groups]
+    out_ref, sum_refs = refs[2 * groups + 1], refs[2 * groups + 2 :]
     cosine_t = tables_ref[:HALF, :] * ROOT_SCALE
     sine_t = tables_ref[HALF:, :] * ROOT_SCALE
-    for h in range(out_ref.shape[1] // HEAD):
-        y1 = dqt_ref[pl.ds(h * HEAD, HALF), :]
-        y2 = dqt_ref[pl.ds(h * HEAD + HALF, HALF), :]
-        turned = jnp.concatenate(
-            [y1 * cosine_t + y2 * sine_t, y2 * cosine_t - y1 * sine_t], axis=0
-        )
-        out_ref[:, pl.ds(h * HEAD, HEAD)] = turned.T.astype(BF16)
+    size = dqt_refs[0].shape[0] // HEAD
+    for g in range(groups):
+        sum_refs[g][...] = own_refs[g][...] + back_ref[
+            :, 2 * HEAD * g : 2 * HEAD * (g + 1)
+        ].astype(F32)
+        for j in range(size):
+            y1 = dqt_refs[g][pl.ds(j * HEAD, HALF), :]
+            y2 = dqt_refs[g][pl.ds(j * HEAD + HALF, HALF), :]
+            turned = jnp.concatenate(
+                [y1 * cosine_t + y2 * sine_t, y2 * cosine_t - y1 * sine_t], axis=0
+            )
+            out_ref[:, pl.ds((g * size + j) * HEAD, HEAD)] = turned.T.astype(BF16)
 
 
 def add_kernel(a_ref, b_ref, sum_ref):
     sum_ref[...] = (a_ref[...].astype(F32) + b_ref[...].astype(F32)).astype(BF16)
 
 
-def final_kernel(tables_ref, own_ref, a_ref, dk_ref, dv_ref):
-    width = dk_ref.shape[1]
+def final_kernel(groups, tables_ref, *refs):
+    own, back = refs[:groups], refs[groups : 2 * groups]
+    dk_ref, dv_ref = refs[2 * groups :]
     wide, signed = row_tables(tables_ref[:HALF, :], tables_ref[HALF:, :])
     wide = wide * ROOT_SCALE
     signed = signed * -ROOT_SCALE
-    total = own_ref[...] + a_ref[...].astype(F32)
-    for g in range(width // HEAD):
+    for g in range(groups):
         cols = pl.ds(g * HEAD, HEAD)
-        dk_ref[:, cols] = rotated(total[:, g * HEAD : (g + 1) * HEAD], wide, signed).astype(BF16)
-    dv_ref[...] = total[:, width:].astype(BF16)
+        total = own[g][...] + back[g][...].astype(F32)
+        dk_ref[:, cols] = rotated(total[:, :HEAD], wide, signed).astype(BF16)
+        dv_ref[:, cols] = total[:, HEAD:].astype(BF16)
 
 
 SMEM = pl.BlockSpec(memory_space=pltpu.SMEM)
@@ -305,7 +334,7 @@
 HBM = pl.BlockSpec(memory_space=pltpu.HBM)
 
 
-def call(kernel, outs, specs, scratch=(), moved=1):
+def call(kernel, outs, specs, scratch=()):
     return pl.pallas_call(
         kernel,
         out_shape=[jax.ShapeDtypeStruct(shape, dtype) for shape, dtype in outs],
@@ -314,7 +343,7 @@
         scratch_shapes=list(scratch),
         compiler_params=pltpu.CompilerParams(vmem_limit_bytes=VMEM_LIMIT),
         cost_estimate=pl.CostEstimate(
-            flops=1 << 20, bytes_accessed=moved << 20, transcendentals=0
+            flops=1 << 20, bytes_accessed=1 << 18, transcendentals=0
         ),
     )
 
@@ -331,69 +360,92 @@
     wide_k = k.shape[1]
     heads = wide_q // HEAD
     slot = jnp.stack([lax.axis_index("ctx"), lax.axis_index("head")]).astype(jnp.int32)
-    q, do, at, k_here, v_here, span_map, own = (
+    groups = wide_k // HEAD
+    size = heads // groups
+    q, do, at, k, v, lse, span_map, own = (
         pltpu.with_memory_space_constraint(x, pltpu.HBM)
-        for x in (q, do, at, k, v, span_map, positions)
-    )
-
-    k1 = shifted(k, -1)
+        for x in (q, do, at, k, v, lse, span_map, positions)
+    )
+    dq_out = ((size * HEAD, rows), F32)
+    part_out = ((rows, 2 * HEAD), BF16)
+
+    (raw,) = call(
+        merge_kernel,
+        [((rows, 2 * wide_k), BF16)],
+        [HBM] * 2,
+        [pltpu.SemaphoreType.DMA((2,))],
+    )(k, v)
+    raw1 = shifted(raw, -1)
     pieces = [own] + [shifted(positions, r, "head") for r in (1, 2, 3)]
-    k1, *pieces = lax.optimization_barrier((k1, *pieces))
     tables, kv, packed = call(
         key_kernel,
-        [((HEAD, rows), F32), ((rows, 2 * wide_k), BF16), ((rows + 16, wide_k), BF16)],
-        [SMEM] + [VMEM] * 6,
-        moved=16,
-    )(slot, *pieces, k_here, v_here)
-    v1 = shifted(packed, -1)
-    kv2 = shifted(kv, -2)
-    k3 = shifted(k1, -2)
-    qr, grad, norm, delta, dqt, dkv = call(
+        [((HEAD, rows), F32), ((rows, 2 * wide_k), BF16), ((16, rows), BF16)],
+        [SMEM] + [VMEM] * 5,
+    )(slot, *pieces, raw)
+    packed1 = shifted(packed, -1)
+    raw1, _ = lax.optimization_barrier((raw1, tables))
+    raw3 = shifted(raw1, -2)
+    packed3 = shifted(packed, -3)
+
+    qr, grad, norm, delta, *rest = call(
         first_kernel,
-        [
-            ((rows, wide_q), BF16),
-            ((rows, wide_q), BF16),
-            ((heads, rows), F32),
-            ((heads, rows), F32),
-            ((wide_q, rows), F32),
-            ((rows, 2 * wide_k), F32),
-        ],
-        [VMEM] * 3 + [HBM] * 3,
+        [((rows, wide_q), BF16)] * 2
+        + [((heads, rows), F32)] * 2
+        + [dq_out] * groups
+        + [((rows, 2 * HEAD), F32)] * groups,
+        [VMEM] * 2 + [HBM] * 4,
         [
             pltpu.VMEM((rows, wide_q), BF16),
             pltpu.VMEM((rows, wide_q), BF16),
-            pltpu.SemaphoreType.DMA((3 * (wide_k // HEAD),)),
+            pltpu.VMEM((heads, rows), F32),
+            pltpu.SemaphoreType.DMA((3 * groups + 1,)),
         ],
-        moved=12,
     )(tables, kv, lse, q, do, at)
-    held, _ = lax.optimization_barrier((v1, delta))
-    v3 = shifted(held, -2)
-
-    outs = [((wide_q, rows), F32), ((rows, 2 * wide_k), BF16)]
-    turned_key = pltpu.VMEM((rows, wide_k), BF16)
-    dqt, part1 = call(
-        functools.partial(raw_kernel, 1), outs, [SMEM] * 2 + [VMEM] * 7, [turned_key], moved=8
-    )(slot, span_map, k1, v1, qr, grad, norm, delta, dqt)
-    dqt, part2 = call(
-        functools.partial(turned_kernel, 2), outs, [SMEM] * 2 + [VMEM] * 6, moved=8
-    )(slot, span_map, kv2, qr, grad, norm, delta, dqt)
-    back2 = shifted(part2, 2)
-    dqt, part3 = call(
-        functools.partial(raw_kernel, 3), outs, [SMEM] * 2 + [VMEM] * 7, [turned_key], moved=8
-    )(slot, span_map, k3, v3, qr, grad, norm, delta, dqt)
-    back3 = shifted(part3, 2)
-    dq, dkv = call(
-        query_kernel, [((rows, wide_q), BF16), ((rows, 2 * wide_k), F32)], [VMEM] * 4, moved=4
-    )(tables, dqt, dkv, back2)
-    part1, _ = lax.optimization_barrier((part1, dkv))
-    (part13,) = call(add_kernel, [((rows, 2 * wide_k), BF16)], [VMEM] * 2)(part1, back3)
-    back1 = shifted(part13, 1)
+    dqs, owns = rest[:groups], rest[groups:]
+    held, packed1, packed3, _ = lax.optimization_barrier((kv, packed1, packed3, delta))
+    kv2 = shifted(held, -2)
+
+    shared = (qr, grad, norm, delta)
+    key = pltpu.VMEM((rows, wide_k), BF16)
+
+    def hop(kernel, step, wanted, arrived, dqs, split, scratch=()):
+        count = len(wanted)
+        outs = [part_out] * count if split else [((rows, count * 2 * HEAD), BF16)]
+        results = call(
+            functools.partial(kernel, step, wanted),
+            [dq_out] * count + outs,
+            [SMEM] * 2 + [VMEM] * (4 + len(arrived) + count),
+            scratch,
+        )(slot, span_map, *arrived, *shared, *(dqs[g] for g in wanted))
+        for i, g in enumerate(wanted):
+            dqs[g] = results[i]
+        return results[count:]
+
+    every = tuple(range(groups))
+    dqs = list(dqs)
+    (part1,) = hop(raw_kernel, 1, every, (raw1, packed1), dqs, False, [key])
+    back1 = shifted(part1, 1)
+    backs3 = []
+    for g in every:
+        (part3,) = hop(raw_kernel, 3, (g,), (raw3, packed3), dqs, True, [key])
+        backs3.append(shifted(part3, 1))
+    parts2 = hop(turned_kernel, 2, every, (kv2,), dqs, True)
+    dq, *owns = call(
+        functools.partial(query_kernel, groups),
+        [((rows, wide_q), BF16)] + [((rows, 2 * HEAD), F32)] * groups,
+        [VMEM] * (2 + 2 * groups),
+    )(tables, *dqs, *owns, back1)
+    *parts2, _ = lax.optimization_barrier((*parts2, owns[0]))
+    backs2 = []
+    for part, back in zip(parts2, backs3):
+        (total,) = call(add_kernel, [part_out], [VMEM] * 2)(part, back)
+        backs2.append(shifted(total, 2))
 
     dk, dv = call(
-        final_kernel,
+        functools.partial(final_kernel, groups),
         [((rows, wide_k), BF16), ((rows, wide_k), BF16)],
-        [VMEM] * 3,
-    )(tables, dkv, back1)
+        [VMEM] * (1 + 2 * groups),
+    )(tables, *owns, *backs2)
     return dq, dk, dv
 
 

time: 53.3 us -> 55 us (1.032)
  waiting for transfers between devices: 23.8 us -> 18 us
  starting transfers between devices: 13.8 us -> 19.4 us
  Pallas kernels: 14.8 us -> 16.5 us
    ppermute x11 -> x13, waiting for transfers between devices: 23.8 us -> 18 us  [shifted(): return lax.ppermute(value, axis, pairs)]
    ppermute x11 -> x13, starting transfers between devices: 13.8 us -> 19.4 us  [shifted(): return lax.ppermute(value, axis, pairs)]
    pallas_call x8 -> x11, Pallas kernels: 14.8 us -> 16.5 us  [the longest x4 8.52 us: hop(): call(functools.partial(kernel, step, wanted), [dq_out] * count + outs, [S...]
  transfers between devices with their start and end apart: 11 -> 13, of which waited for: 8 -> 9; matrix products, arithmetic and copies ran while one was open for 0% -> 0% of each run, Pallas kernels for 23% -> 27%
where the time goes in v5:
time: 55 us; the launch traced here: 54.8 us
  starting transfers between devices  19.4 us (35%)
  waiting for transfers between devices  18 us (33%)
  Pallas kernels  16.5 us (30%)
  between operations  0.74 us (1%)
    ppermute x13, starting transfers between devices, shifted(): return lax.ppermute(value, axis, pairs)  19.4 us
    ppermute x13, waiting for transfers between devices, shifted(): return lax.ppermute(value, axis, pairs)  18 us
    pallas_call x4, Pallas kernels, hop(): call(functools.partial(kernel, step, wanted), [dq_out] * count + outs, [S...  8.52 us
    pallas_call x1, Pallas kernels, shards(): call(first_kernel, [((rows, wide_q), BF16)] * 2 + [((heads, rows), F32)]...  3.98 us
  transfers between devices with their start and end apart: 13, of which 9 were waited for; matrix products, arithmetic and copies ran while one was open for 0% of the time, Pallas kernels for 27%

profile of v5, /device:TPU:0, one launch (start us, length us, event | category | flops | bytes accessed | tf_op | source)
XLA Modules:
  0.0 54.8 jit_solution(6021405850250538456)
XLA Ops:
  0.6 0.0 copy-start
  0.6 1.0 %shard_map.103.raw_ref = bf16[256,512]{1,0:T(8,128)(2,1)S(1)} custom-call(bf16[256,256]{1,0:T(8,128)(2,1)} %k_hbm.1, bf16[256,256]{1,0:T(8,128)(2,1)} %v_hbm.1), custom_call_target="tpu_custom_call" | custom-call | flops 1048576 | bytes 262144 | tf_op jit(solution)/shard_map/pallas_call | solution.py:372
  1.6 6.1 %collective-permute-start.6 = (bf16[256,512]{1,0:T(8,128)(2,1)S(1)}, bf16[256,512]{1,0:T(8,128)(2,1)S(1)}, u32[]{:S(2)}, u32[]{:S(2)}) collective-permute-start(bf16[256,512]{1,0:T(8,128)(2,1)S(1)} %shard_map.103.raw_ref), channel_id=1, source_target_pairs={{0,28},{4,0},{8,4},{12,8},{16,12},{20,16},{24,20},{28,24},{1,29},{... | collective-permute-start | bytes 786440 | tf_op jit(solution)/shard_map/ppermute | solution.py:354
  7.7 1.5 %collective-permute-start.1 = (s32[3,64]{1,0:T(4,128)S(1)}, s32[3,64]{1,0:T(4,128)S(1)}, u32[]{:S(2)}, u32[]{:S(2)}) collective-permute-start(s32[3,64]{1,0:T(4,128)S(1)} %copy-done), channel_id=1, source_target_pairs={{0,2},{1,3},{2,0},{3,1},{4,6},{5,7},{6,4},{7,5},{8,10},{9,11},{10,... | collective-permute-start | bytes 2312 | tf_op jit(solution)/shard_map/ppermute | solution.py:354
  9.2 1.4 %collective-permute-start.2 = (s32[3,64]{1,0:T(4,128)S(1)}, s32[3,64]{1,0:T(4,128)S(1)}, u32[]{:S(2)}, u32[]{:S(2)}) collective-permute-start(s32[3,64]{1,0:T(4,128)S(1)} %copy-done), channel_id=1, source_target_pairs={{0,3},{1,0},{2,1},{3,2},{4,7},{5,4},{6,5},{7,6},{8,11},{9,8},{10,9... | collective-permute-start | bytes 2312 | tf_op jit(solution)/shard_map/ppermute | solution.py:354
  10.7 0.1 pad_add_fusion.slot_ref
  10.7 0.6 %collective-permute-done.1.p2_ref = s32[3,64]{1,0:T(4,128)S(1)} collective-permute-done((s32[3,64]{1,0:T(4,128)S(1)}, s32[3,64]{1,0:T(4,128)S(1)}, u32[]{:S(2)}, u32[]{:S(2)}) %collective-permute-start.1) | collective-permute-done | bytes 800 | tf_op jit(solution)/shard_map/ppermute | solution.py:354
  11.3 0.6 %collective-permute-done.2.p3_ref = s32[3,64]{1,0:T(4,128)S(1)} collective-permute-done((s32[3,64]{1,0:T(4,128)S(1)}, s32[3,64]{1,0:T(4,128)S(1)}, u32[]{:S(2)}, u32[]{:S(2)}) %collective-permute-start.2) | collective-permute-done | bytes 800 | tf_op jit(solution)/shard_map/ppermute | solution.py:354
  12.0 1.0 %shard_map.104 = (f32[128,256]{1,0:T(8,128)S(1)}, bf16[256,512]{1,0:T(8,128)(2,1)S(1)}, bf16[16,256]{1,0:T(8,128)(2,1)S(1)}) custom-call(s32[2]{0:T(128)S(1)} %pad_add_fusion.slot_ref, s32[3,64]{1,0:T(4,128)} %own_ref.1, s32[3,64]{1,0:T(4,128)S(1)} %collective-permute-done.p1_ref, s32[3,64]{1,0:T(4,128)S(1)} %collective-permute-done.1.p2_ref, ...), custom_call_target="tpu_custom_call" | custom-call | flops 1048576 | bytes 262144 | tf_op jit(solution)/shard_map/pallas_call | solution.py:380
  13.0 0.3 collective-permute-done.6.kv_ref
  13.3 1.5 %collective-permute-start.7 = (bf16[256,512]{1,0:T(8,128)(2,1)S(1)}, bf16[256,512]{1,0:T(8,128)(2,1)S(1)}, u32[]{:S(2)}, u32[]{:S(2)}) collective-permute-start(bf16[256,512]{1,0:T(8,128)(2,1)S(1)} %collective-permute-done.6.kv_ref), channel_id=1, source_target_pairs={{0,24},{4,28},{8,0},{12,4},{16,8},{20,12},{24,16},{28,20},{1,25},{... | collective-permute-start | bytes 786440 | tf_op jit(solution)/shard_map/ppermute | solution.py:354
  14.8 3.7 %collective-permute-start.3 = (bf16[16,256]{1,0:T(8,128)(2,1)S(1)}, bf16[16,256]{1,0:T(8,128)(2,1)S(1)}, u32[]{:S(2)}, u32[]{:S(2)}) collective-permute-start(bf16[16,256]{1,0:T(8,128)(2,1)S(1)} %get-tuple-element.38), channel_id=1, source_target_pairs={{0,28},{4,0},{8,4},{12,8},{16,12},{20,16},{24,20},{28,24},{1,29},{... | collective-permute-start | bytes 24584 | tf_op jit(solution)/shard_map/ppermute | solution.py:354
  18.4 0.0 collective-permute-start.4
  18.4 4.0 %shard_map.105 = (bf16[256,1024]{1,0:T(8,128)(2,1)S(1)}, bf16[256,1024]{1,0:T(8,128)(2,1)S(1)}, f32[8,256]{1,0:T(8,128)S(1)}, f32[8,256]{1,0:T(8,128)S(1)}, f32[...) custom-call(f32[128,256]{1,0:T(8,128)S(1)} %get-tuple-element.36.tables_ref, ...), custom_call_target="tpu_custom_call" | custom-call | flops 1048576 | bytes 262144 | tf_op jit(solution)/shard_map/pallas_call | solution.py:390
  22.4 0.6 %collective-permute-done.4.packed_ref = bf16[16,256]{1,0:T(8,128)(2,1)S(1)} collective-permute-done((bf16[16,256]{1,0:T(8,128)(2,1)S(1)}, bf16[16,256]{1,0:T(8,128)(2,1)S(1)}, u32[]{:S(2)}, u32[]{:S(2)}) %collective-permute-start.4) | collective-permute-done | bytes 8224 | tf_op jit(solution)/shard_map/ppermute | solution.py:354
  23.0 4.6 %collective-permute-start.5 = (bf16[256,512]{1,0:T(8,128)(2,1)S(1)}, bf16[256,512]{1,0:T(8,128)(2,1)S(1)}, u32[]{:S(2)}, u32[]{:S(2)}) collective-permute-start(bf16[256,512]{1,0:T(8,128)(2,1)S(1)} %get-tuple-element.40.kv_ref), channel_id=1, source_target_pairs={{0,24},{4,28},{8,0},{12,4},{16,8},{20,12},{24,16},{28,20},{1,25},{... | collective-permute-start | bytes 786440 | tf_op jit(solution)/shard_map/ppermute | solution.py:354
  27.6 2.6 %shard_map.106 = (f32[512,256]{1,0:T(8,128)S(1)}, f32[512,256]{1,0:T(8,128)S(1)}, bf16[256,512]{1,0:T(8,128)(2,1)S(1)}) custom-call(s32[2]{0:T(128)S(1)} %pad_add_fusion.slot_ref, s32[8]{0:T(128)} %span_ref.7, bf16[256,512]{1,0:T(8,128)(2,1)S(1)} %collective-permute-done.6.kv_ref, bf16[16,256]{1,0:T(8,128)(2,1)S(1)} %collective-permute-done.3.packed_ref, ...), custom_call_target="tpu_custom_call" | custom-call | flops 1048576 | bytes 262144 | tf_op jit(solution)/shard_map/pallas_call | solution.py:414
  30.2 0.1 collective-permute-start.8
  30.2 1.8 %shard_map.108 = (f32[512,256]{1,0:T(8,128)S(1)}, bf16[256,256]{1,0:T(8,128)(2,1)S(1)}) custom-call(s32[2]{0:T(128)S(1)} %pad_add_fusion.slot_ref, s32[8]{0:T(128)} %span_ref.7, bf16[256,512]{1,0:T(8,128)(2,1)S(1)} %collective-permute-done.7.kv_ref, bf16[16,256]{1,0:T(8,128)(2,1)S(1)} %collective-permute-done.4.packed_ref, ...), custom_call_target="tpu_custom_call" | custom-call | flops 1048576 | bytes 262144 | tf_op jit(solution)/shard_map/pallas_call | solution.py:414
  32.1 0.1 collective-permute-start.11
  32.1 1.8 %shard_map.107 = (f32[512,256]{1,0:T(8,128)S(1)}, bf16[256,256]{1,0:T(8,128)(2,1)S(1)}) custom-call(s32[2]{0:T(128)S(1)} %pad_add_fusion.slot_ref, s32[8]{0:T(128)} %span_ref.7, bf16[256,512]{1,0:T(8,128)(2,1)S(1)} %collective-permute-done.7.kv_ref, bf16[16,256]{1,0:T(8,128)(2,1)S(1)} %collective-permute-done.4.packed_ref, ...), custom_call_target="tpu_custom_call" | custom-call | flops 1048576 | bytes 262144 | tf_op jit(solution)/shard_map/pallas_call | solution.py:414
  34.0 0.4 collective-permute-start.9
  34.3 2.3 %shard_map.109 = (f32[512,256]{1,0:T(8,128)S(1)}, f32[512,256]{1,0:T(8,128)S(1)}, bf16[256,256]{1,0:T(8,128)(2,1)S(1)}, bf16[256,256]{1,0:T(8,128)(2,1)S(1)}) custom-call(s32[2]{0:T(128)S(1)} %pad_add_fusion.slot_ref, s32[8]{0:T(128)} %span_ref.7, bf16[256,512]{1,0:T(8,128)(2,1)S(1)} %collective-permute-done.5.kv_ref, ...), custom_call_target="tpu_custom_call" | custom-call | flops 1048576 | bytes 262144 | tf_op jit(solution)/shard_map/pallas_call | solution.py:414
  36.6 5.5 %collective-permute-done.8.refs_4_ = bf16[256,512]{1,0:T(8,128)(2,1)S(1)} collective-permute-done((bf16[256,512]{1,0:T(8,128)(2,1)S(1)}, bf16[256,512]{1,0:T(8,128)(2,1)S(1)}, u32[]{:S(2)}, u32[]{:S(2)}) %collective-permute-start.8) | collective-permute-done | bytes 262176 | tf_op jit(solution)/shard_map/ppermute | solution.py:354
  42.1 1.1 %shard_map.110 = (bf16[256,1024]{1,0:T(8,128)(2,1)}, f32[256,256]{1,0:T(8,128)S(1)}, f32[256,256]{1,0:T(8,128)S(1)}) custom-call(f32[128,256]{1,0:T(8,128)S(1)} %get-tuple-element.36.tables_ref, f32[512,256]{1,0:T(8,128)S(1)} %get-tuple-element.53.refs_0_, f32[512,256]{1,0:T(8,128)S(1)} %get-tuple-element.54.refs_1_, ...), custom_call_target="tpu_custom_call" | custom-call | flops 1048576 | bytes 262144 | tf_op jit(solution)/shard_map/pallas_call | solution.py:433
  43.2 1.7 %collective-permute-done.11.b_ref = bf16[256,256]{1,0:T(8,128)(2,1)S(1)} collective-permute-done((bf16[256,256]{1,0:T(8,128)(2,1)S(1)}, bf16[256,256]{1,0:T(8,128)(2,1)S(1)}, u32[]{:S(2)}, u32[]{:S(2)}) %collective-permute-start.11) | collective-permute-done | bytes 131104 | tf_op jit(solution)/shard_map/ppermute | solution.py:354
  45.0 0.1 collective-permute-start.12
  45.1 1.9 %collective-permute-done.9.b_ref = bf16[256,256]{1,0:T(8,128)(2,1)S(1)} collective-permute-done((bf16[256,256]{1,0:T(8,128)(2,1)S(1)}, bf16[256,256]{1,0:T(8,128)(2,1)S(1)}, u32[]{:S(2)}, u32[]{:S(2)}) %collective-permute-start.9) | collective-permute-done | bytes 131104 | tf_op jit(solution)/shard_map/ppermute | solution.py:354
  47.0 0.1 collective-permute-start.10
  47.1 4.7 %collective-permute-done.12.refs_3_ = bf16[256,256]{1,0:T(8,128)(2,1)S(1)} collective-permute-done((bf16[256,256]{1,0:T(8,128)(2,1)S(1)}, bf16[256,256]{1,0:T(8,128)(2,1)S(1)}, u32[]{:S(2)}, u32[]{:S(2)}) %collective-permute-start.12) | collective-permute-done | bytes 131104 | tf_op jit(solution)/shard_map/ppermute | solution.py:354
  51.8 2.1 %collective-permute-done.10.refs_2_ = bf16[256,256]{1,0:T(8,128)(2,1)S(1)} collective-permute-done((bf16[256,256]{1,0:T(8,128)(2,1)S(1)}, bf16[256,256]{1,0:T(8,128)(2,1)S(1)}, u32[]{:S(2)}, u32[]{:S(2)}) %collective-permute-start.10) | collective-permute-done | bytes 131104 | tf_op jit(solution)/shard_map/ppermute | solution.py:354
  53.9 0.9 %shard_map.113 = (bf16[256,256]{1,0:T(8,128)(2,1)}, bf16[256,256]{1,0:T(8,128)(2,1)}) custom-call(f32[128,256]{1,0:T(8,128)S(1)} %get-tuple-element.36.tables_ref, f32[256,256]{1,0:T(8,128)S(1)} %get-tuple-element.59.refs_0_, f32[256,256]{1,0:T(8,128)S(1)} %get-tuple-element.60.refs_1_, bf16[256,256]{1,0:T(8,128)(2,1)S(1)} %collective-permute-done.10.refs_2_, ...), custom_call_target="tpu_custom_call" | custom-call | flops 1048576 | bytes 262144 | tf_op jit(solution)/shard_map/pallas_call | solution.py:444
  (8 shorter events, 0.1 us)
Async XLA Ops:
  0.6 7.1 %copy-start = (s32[3,64]{1,0:T(4,128)S(1)}, s32[3,64]{1,0:T(4,128)}, u32[]{:S(2)}) copy-start(s32[3,64]{1,0:T(4,128)} %own_ref.1) | copy-start | bytes 2308
  1.6 11.6 %collective-permute-start.6 = (bf16[256,512]{1,0:T(8,128)(2,1)S(1)}, bf16[256,512]{1,0:T(8,128)(2,1)S(1)}, u32[]{:S(2)}, u32[]{:S(2)}) collective-permute-start(bf16[256,512]{1,0:T(8,128)(2,1)S(1)} %shard_map.103.raw_ref), channel_id=1, source_target_pairs={{0,28},{4,0},{8,4},{12,8},{16,12},{20,16},{24,20},{28,24},{1,29},{... | collective-permute-start | bytes 786440 | tf_op jit(solution)/shard_map/ppermute | solution.py:354
  7.7 3.0 %collective-permute-start = (s32[3,64]{1,0:T(4,128)S(1)}, s32[3,64]{1,0:T(4,128)S(1)}, u32[]{:S(2)}, u32[]{:S(2)}) collective-permute-start(s32[3,64]{1,0:T(4,128)S(1)} %copy-done), channel_id=1, source_target_pairs={{0,1},{1,2},{2,3},{3,0},{4,5},{5,6},{6,7},{7,4},{8,9},{9,10},{10,1... | collective-permute-start | bytes 2312 | tf_op jit(solution)/shard_map/ppermute | solution.py:354
  7.7 3.6 %collective-permute-start.1 = (s32[3,64]{1,0:T(4,128)S(1)}, s32[3,64]{1,0:T(4,128)S(1)}, u32[]{:S(2)}, u32[]{:S(2)}) collective-permute-start(s32[3,64]{1,0:T(4,128)S(1)} %copy-done), channel_id=1, source_target_pairs={{0,2},{1,3},{2,0},{3,1},{4,6},{5,7},{6,4},{7,5},{8,10},{9,11},{10,... | collective-permute-start | bytes 2312 | tf_op jit(solution)/shard_map/ppermute | solution.py:354
  9.2 2.7 %collective-permute-start.2 = (s32[3,64]{1,0:T(4,128)S(1)}, s32[3,64]{1,0:T(4,128)S(1)}, u32[]{:S(2)}, u32[]{:S(2)}) collective-permute-start(s32[3,64]{1,0:T(4,128)S(1)} %copy-done), channel_id=1, source_target_pairs={{0,3},{1,0},{2,1},{3,2},{4,7},{5,4},{6,5},{7,6},{8,11},{9,8},{10,9... | collective-permute-start | bytes 2312 | tf_op jit(solution)/shard_map/ppermute | solution.py:354
  13.3 17.0 %collective-permute-start.7 = (bf16[256,512]{1,0:T(8,128)(2,1)S(1)}, bf16[256,512]{1,0:T(8,128)(2,1)S(1)}, u32[]{:S(2)}, u32[]{:S(2)}) collective-permute-start(bf16[256,512]{1,0:T(8,128)(2,1)S(1)} %collective-permute-done.6.kv_ref), channel_id=1, source_target_pairs={{0,24},{4,28},{8,0},{12,4},{16,8},{20,12},{24,16},{28,20},{1,25},{... | collective-permute-start | bytes 786440 | tf_op jit(solution)/shard_map/ppermute | solution.py:354
  14.8 7.6 %collective-permute-start.3 = (bf16[16,256]{1,0:T(8,128)(2,1)S(1)}, bf16[16,256]{1,0:T(8,128)(2,1)S(1)}, u32[]{:S(2)}, u32[]{:S(2)}) collective-permute-start(bf16[16,256]{1,0:T(8,128)(2,1)S(1)} %get-tuple-element.38), channel_id=1, source_target_pairs={{0,28},{4,0},{8,4},{12,8},{16,12},{20,16},{24,20},{28,24},{1,29},{... | collective-permute-start | bytes 24584 | tf_op jit(solution)/shard_map/ppermute | solution.py:354
  18.4 4.5 %collective-permute-start.4 = (bf16[16,256]{1,0:T(8,128)(2,1)S(1)}, bf16[16,256]{1,0:T(8,128)(2,1)S(1)}, u32[]{:S(2)}, u32[]{:S(2)}) collective-permute-start(bf16[16,256]{1,0:T(8,128)(2,1)S(1)} %get-tuple-element.38), channel_id=1, source_target_pairs={{0,20},{4,24},{8,28},{12,0},{16,4},{20,8},{24,12},{28,16},{1,21},{... | collective-permute-start | bytes 24584 | tf_op jit(solution)/shard_map/ppermute | solution.py:354
  23.0 11.3 %collective-permute-start.5 = (bf16[256,512]{1,0:T(8,128)(2,1)S(1)}, bf16[256,512]{1,0:T(8,128)(2,1)S(1)}, u32[]{:S(2)}, u32[]{:S(2)}) collective-permute-start(bf16[256,512]{1,0:T(8,128)(2,1)S(1)} %get-tuple-element.40.kv_ref), channel_id=1, source_target_pairs={{0,24},{4,28},{8,0},{12,4},{16,8},{20,12},{24,16},{28,20},{1,25},{... | collective-permute-start | bytes 786440 | tf_op jit(solution)/shard_map/ppermute | solution.py:354
  30.2 12.0 %collective-permute-start.8 = (bf16[256,512]{1,0:T(8,128)(2,1)S(1)}, bf16[256,512]{1,0:T(8,128)(2,1)S(1)}, u32[]{:S(2)}, u32[]{:S(2)}) collective-permute-start(bf16[256,512]{1,0:T(8,128)(2,1)S(1)} %get-tuple-element.57), channel_id=1, source_target_pairs={{0,4},{4,8},{8,12},{12,16},{16,20},{20,24},{24,28},{28,0},{1,5},{5... | collective-permute-start | bytes 786440 | tf_op jit(solution)/shard_map/ppermute | solution.py:354
  32.1 12.9 %collective-permute-start.11 = (bf16[256,256]{1,0:T(8,128)(2,1)S(1)}, bf16[256,256]{1,0:T(8,128)(2,1)S(1)}, u32[]{:S(2)}, u32[]{:S(2)}) collective-permute-start(bf16[256,256]{1,0:T(8,128)(2,1)S(1)} %get-tuple-element.66), channel_id=1, source_target_pairs={{0,4},{4,8},{8,12},{12,16},{16,20},{20,24},{24,28},{28,0},{1,5},{5... | collective-permute-start | bytes 393224 | tf_op jit(solution)/shard_map/ppermute | solution.py:354
  34.0 13.0 %collective-permute-start.9 = (bf16[256,256]{1,0:T(8,128)(2,1)S(1)}, bf16[256,256]{1,0:T(8,128)(2,1)S(1)}, u32[]{:S(2)}, u32[]{:S(2)}) collective-permute-start(bf16[256,256]{1,0:T(8,128)(2,1)S(1)} %get-tuple-element.64), channel_id=1, source_target_pairs={{0,4},{4,8},{8,12},{12,16},{16,20},{20,24},{24,28},{28,0},{1,5},{5... | collective-permute-start | bytes 393224 | tf_op jit(solution)/shard_map/ppermute | solution.py:354
  45.0 6.8 %collective-permute-start.12 = (bf16[256,256]{1,0:T(8,128)(2,1)S(1)}, bf16[256,256]{1,0:T(8,128)(2,1)S(1)}, u32[]{:S(2)}, u32[]{:S(2)}) collective-permute-start(bf16[256,256]{1,0:T(8,128)(2,1)S(1)} %shard_map.112), channel_id=1, source_target_pairs={{0,8},{4,12},{8,16},{12,20},{16,24},{20,28},{24,0},{28,4},{1,9},{5... | collective-permute-start | bytes 393224 | tf_op jit(solution)/shard_map/ppermute | solution.py:354
  47.0 6.8 %collective-permute-start.10 = (bf16[256,256]{1,0:T(8,128)(2,1)S(1)}, bf16[256,256]{1,0:T(8,128)(2,1)S(1)}, u32[]{:S(2)}, u32[]{:S(2)}) collective-permute-start(bf16[256,256]{1,0:T(8,128)(2,1)S(1)} %shard_map.111), channel_id=1, source_target_pairs={{0,8},{4,12},{8,16},{12,20},{16,24},{20,28},{24,0},{28,4},{1,9},{5... | collective-permute-start | bytes 393224 | tf_op jit(solution)/shard_map/ppermute | solution.py:354

commit v6 on v3

--- a/solution.py
+++ b/solution.py
@@ -232,18 +232,22 @@
         run(slice(0, rows), slice(half, rows))
 
 
-def last_kernel(
-    step, slot_ref, span_ref, kv_ref, qr_ref, do_ref, norm_ref, delta_ref, dqt_in, tables_ref,
-    out_ref, dkv_ref, dqt_ref,
+def turned_kernel(
+    step, slot_ref, span_ref, kv_ref, qr_ref, do_ref, norm_ref, delta_ref, dqt_in,
+    dqt_ref, dkv_ref,
 ):
     width = kv_ref.shape[1] // 2
     hop_body(
         step, slot_ref, span_ref, kv_ref.at[:, :width], kv_ref.at[:, width:], qr_ref, do_ref,
         norm_ref, delta_ref, dqt_in, dqt_ref, dkv_ref,
     )
+
+
+def query_kernel(tables_ref, dqt_ref, own_ref, back_ref, out_ref, sum_ref):
+    sum_ref[...] = own_ref[...] + back_ref[...].astype(F32)
     cosine_t = tables_ref[:HALF, :] * ROOT_SCALE
     sine_t = tables_ref[HALF:, :] * ROOT_SCALE
-    for h in range(qr_ref.shape[1] // HEAD):
+    for h in range(out_ref.shape[1] // HEAD):
         y1 = dqt_ref[pl.ds(h * HEAD, HALF), :]
         y2 = dqt_ref[pl.ds(h * HEAD + HALF, HALF), :]
         turned = jnp.concatenate(
@@ -256,12 +260,12 @@
     sum_ref[...] = (a_ref[...].astype(F32) + b_ref[...].astype(F32)).astype(BF16)
 
 
-def final_kernel(tables_ref, own_ref, a_ref, b_ref, dk_ref, dv_ref):
+def final_kernel(tables_ref, own_ref, a_ref, dk_ref, dv_ref):
     width = dk_ref.shape[1]
     wide, signed = row_tables(tables_ref[:HALF, :], tables_ref[HALF:, :])
     wide = wide * ROOT_SCALE
     signed = signed * -ROOT_SCALE
-    total = own_ref[...] + a_ref[...].astype(F32) + b_ref[...].astype(F32)
+    total = own_ref[...] + a_ref[...].astype(F32)
     for g in range(width // HEAD):
         cols = pl.ds(g * HEAD, HEAD)
         dk_ref[:, cols] = rotated(total[:, g * HEAD : (g + 1) * HEAD], wide, signed).astype(BF16)
@@ -337,31 +341,30 @@
     k3 = shifted(held, -2)
     kv2 = shifted(kv, -2)
 
-    parts = {}
-    for step, key, value in ((1, k1, v1), (3, k3, v3)):
-        dqt, parts[step] = call(
-            functools.partial(hop_body, step),
-            [((wide_q, rows), F32), ((rows, 2 * wide_k), BF16)],
-            [SMEM, SMEM] + [VMEM] * 7,
-            moved=8,
-        )(slot, span_map, key, value, qr, grad, norm, delta, dqt)
-    back3 = shifted(parts[3], 2)
-    dq, part2 = call(
-        functools.partial(last_kernel, 2),
-        [((rows, wide_q), BF16), ((rows, 2 * wide_k), BF16)],
-        [SMEM, SMEM] + [VMEM] * 7,
-        [pltpu.VMEM((wide_q, rows), F32)],
-        moved=8,
-    )(slot, span_map, kv2, qr, grad, norm, delta, dqt, tables)
-    back2 = shifted(part2, 2)
-    (part13,) = call(add_kernel, [((rows, 2 * wide_k), BF16)], [VMEM] * 2)(parts[1], back3)
-    back1 = shifted(part13, 1)
+    outs = [((wide_q, rows), F32), ((rows, 2 * wide_k), BF16)]
+    dqt, part1 = call(
+        functools.partial(hop_body, 1), outs, [SMEM] * 2 + [VMEM] * 7, moved=8
+    )(slot, span_map, k1, v1, qr, grad, norm, delta, dqt)
+    back1 = shifted(part1, 1)
+    dqt, part3 = call(
+        functools.partial(hop_body, 3), outs, [SMEM] * 2 + [VMEM] * 7, moved=8
+    )(slot, span_map, k3, v3, qr, grad, norm, delta, dqt)
+    back3 = shifted(part3, 1)
+    dqt, part2 = call(
+        functools.partial(turned_kernel, 2), outs, [SMEM] * 2 + [VMEM] * 6, moved=8
+    )(slot, span_map, kv2, qr, grad, norm, delta, dqt)
+    dq, dkv = call(
+        query_kernel, [((rows, wide_q), BF16), ((rows, 2 * wide_k), F32)], [VMEM] * 4, moved=4
+    )(tables, dqt, dkv, back1)
+    part2, _ = lax.optimization_barrier((part2, dkv))
+    (part23,) = call(add_kernel, [((rows, 2 * wide_k), BF16)], [VMEM] * 2)(part2, back3)
+    back2 = shifted(part23, 2)
 
     dk, dv = call(
         final_kernel,
         [((rows, wide_k), BF16), ((rows, wide_k), BF16)],
-        [VMEM] * 4,
-    )(tables, dkv, back1, back2)
+        [VMEM] * 3,
+    )(tables, dkv, back2)
     return dq, dk, dv
 
 

time: 49.8 us -> 53.1 us (1.066)
  starting transfers between devices: 12.4 us -> 18.1 us
  waiting for transfers between devices: 22.2 us -> 19.9 us
    ppermute x11, starting transfers between devices: 12.4 us -> 18.1 us  [shifted(): return lax.ppermute(value, axis, pairs)]
    ppermute x11, waiting for transfers between devices: 22.2 us -> 19.9 us  [shifted(): return lax.ppermute(value, axis, pairs)]
    pallas_call x4 -> x5, Pallas kernels: 8.02 us -> 8.03 us  [the longest x1 2.29 us: shards(): call(functools.partial(turned_kernel, 2), outs, [SMEM] * 2 + [VMEM] * 6,...]
  transfers between devices with their start and end apart: 11 -> 11, of which waited for: 6 -> 5; matrix products, arithmetic and copies ran while one was open for 0% -> 0% of each run, Pallas kernels for 27% -> 25%
where the time goes in v6:
time: 53.1 us; the launch traced here: 52.9 us
  waiting for transfers between devices  19.9 us (37%)
  starting transfers between devices  18.1 us (34%)
  Pallas kernels  14.1 us (27%)
  between operations  0.7 us (1%)
    ppermute x11, waiting for transfers between devices, shifted(): return lax.ppermute(value, axis, pairs)  19.9 us
    ppermute x11, starting transfers between devices, shifted(): return lax.ppermute(value, axis, pairs)  18.1 us
    pallas_call x1, Pallas kernels, shards(): call(first_kernel, [((rows, wide_q), BF16), ((rows, wide_q), BF16), ((hea...  3.95 us
    pallas_call x1, Pallas kernels, shards(): call(functools.partial(turned_kernel, 2), outs, [SMEM] * 2 + [VMEM] * 6,...  2.29 us
    pallas_call x1, Pallas kernels, shards(): call(functools.partial(hop_body, 3), outs, [SMEM] * 2 + [VMEM] * 7, moved=8)  2.29 us
    pallas_call x1, Pallas kernels, shards(): call(functools.partial(hop_body, 1), outs, [SMEM] * 2 + [VMEM] * 7, moved=8)  2.29 us
    pallas_call x1, Pallas kernels, shards(): call(key_kernel, [((rows, wide_k), BF16), ((HEAD, rows), F32)], [SMEM] +...  1.25 us
    pallas_call x1, Pallas kernels, shards(): call(query_kernel, [((rows, wide_q), BF16), ((rows, 2 * wide_k), F32)], [...  1.1 us
  transfers between devices with their start and end apart: 11, of which 5 were waited for; matrix products, arithmetic and copies ran while one was open for 0% of the time, Pallas kernels for 25%

profile of v6, /device:TPU:0, one launch (start us, length us, event | category | flops | bytes accessed | tf_op | source)
XLA Modules:
  0.0 52.9 jit_solution(6710679019188125706)
XLA Ops:
  0.6 3.0 %collective-permute-start.1 = (s32[3,64]{1,0:T(4,128)}, s32[3,64]{1,0:T(4,128)S(1)}, u32[]{:S(2)}, u32[]{:S(2)}) collective-permute-start(s32[3,64]{1,0:T(4,128)} %own_ref.1), channel_id=1, source_target_pairs={{0,2},{1,3},{2,0},{3,1},{4,6},{5,7},{6,4},{7,5},{8,10},{9,11},{10,... | collective-permute-start | bytes 2312 | tf_op jit(solution)/shard_map/ppermute | solution.py:297
  3.6 0.0 collective-permute-start
  3.6 1.7 %collective-permute-start.2 = (s32[3,64]{1,0:T(4,128)}, s32[3,64]{1,0:T(4,128)S(1)}, u32[]{:S(2)}, u32[]{:S(2)}) collective-permute-start(s32[3,64]{1,0:T(4,128)} %own_ref.1), channel_id=1, source_target_pairs={{0,3},{1,0},{2,1},{3,2},{4,7},{5,4},{6,5},{7,6},{8,11},{9,8},{10,9... | collective-permute-start | bytes 2312 | tf_op jit(solution)/shard_map/ppermute | solution.py:297
  5.4 4.6 %collective-permute-start.6 = (bf16[256,256]{1,0:T(8,128)(2,1)}, bf16[256,256]{1,0:T(8,128)(2,1)S(1)}, u32[]{:S(2)}, u32[]{:S(2)}) collective-permute-start(bf16[256,256]{1,0:T(8,128)(2,1)} %v_ref.1), channel_id=1, source_target_pairs={{0,28},{4,0},{8,4},{12,8},{16,12},{20,16},{24,20},{28,24},{1,29},{... | collective-permute-start | bytes 393224 | tf_op jit(solution)/shard_map/ppermute | solution.py:297
  9.9 0.1 pad_add_fusion.slot_ref
  10.0 0.0 collective-permute-done.1.p2_ref
  10.0 0.0 collective-permute-done.p1_ref
  10.0 0.0 collective-permute-done.2.p3_ref
  10.0 0.0 copy-start.1
  10.0 1.2 %shard_map.103 = (bf16[256,256]{1,0:T(8,128)(2,1)S(1)}, f32[128,256]{1,0:T(8,128)S(1)}) custom-call(s32[2]{0:T(128)S(1)} %pad_add_fusion.slot_ref, s32[3,64]{1,0:T(4,128)} %own_ref.1, s32[3,64]{1,0:T(4,128)S(1)} %collective-permute-done.p1_ref, s32[3,64]{1,0:T(4,128)S(1)} %collective-permute-done.1.p2_ref, s32[3,64]{1,0:T(4,128)S(1)} %collective-permute-done.2.p3_ref, ...), custom_call_target="tpu_custom_call" | custom-call | flops 1048576 | bytes 16777216 | tf_op jit(solution)/shard_map/pallas_call | solution.py:313
  11.3 1.5 %collective-permute-start.4 = (bf16[256,256]{1,0:T(8,128)(2,1)S(1)}, bf16[256,256]{1,0:T(8,128)(2,1)S(1)}, u32[]{:S(2)}, u32[]{:S(2)}) collective-permute-start(bf16[256,256]{1,0:T(8,128)(2,1)S(1)} %get-tuple-element.25.kr_ref), channel_id=1, source_target_pairs={{0,28},{4,0},{8,4},{12,8},{16,12},{20,16},{24,20},{28,24},{1,29},{... | collective-permute-start | bytes 393224 | tf_op jit(solution)/shard_map/ppermute | solution.py:297
  12.8 3.9 %shard_map.104 = (bf16[256,1024]{1,0:T(8,128)(2,1)S(1)}, bf16[256,1024]{1,0:T(8,128)(2,1)S(1)}, f32[8,256]{1,0:T(8,128)S(1)}, f32[8,256]{1,0:T(8,128)S(1)}, f32[...) custom-call(f32[128,256]{1,0:T(8,128)S(1)} %get-tuple-element.24.tables_ref, ...), custom_call_target="tpu_custom_call" | custom-call | flops 1048576 | bytes 12582912 | tf_op jit(solution)/shard_map/pallas_call | solution.py:321
  16.7 0.0 collective-permute-done.6.v_ref
  16.7 0.5 collective-permute-start.7
  17.2 0.0 collective-permute-done.4.k_ref
  17.2 0.6 %collective-permute-start.5 = (bf16[256,256]{1,0:T(8,128)(2,1)S(1)}, bf16[256,256]{1,0:T(8,128)(2,1)S(1)}, u32[]{:S(2)}, u32[]{:S(2)}) collective-permute-start(bf16[256,256]{1,0:T(8,128)(2,1)S(1)} %collective-permute-done.4.k_ref), channel_id=1, source_target_pairs={{0,24},{4,28},{8,0},{12,4},{16,8},{20,12},{24,16},{28,20},{1,25},{... | collective-permute-start | bytes 393224 | tf_op jit(solution)/shard_map/ppermute | solution.py:297
  17.8 0.4 collective-permute-start.3
  18.3 2.3 %shard_map.105 = (f32[1024,256]{1,0:T(8,128)S(1)}, bf16[256,512]{1,0:T(8,128)(2,1)S(1)}) custom-call(s32[2]{0:T(128)S(1)} %pad_add_fusion.slot_ref, s32[8]{0:T(128)} %span_ref.5, bf16[256,256]{1,0:T(8,128)(2,1)S(1)} %collective-permute-done.4.k_ref, bf16[256,256]{1,0:T(8,128)(2,1)S(1)} %collective-permute-done.6.v_ref, ...), custom_call_target="tpu_custom_call" | custom-call | flops 1048576 | bytes 8388608 | tf_op jit(solution)/shard_map/pallas_call | solution.py:345
  20.6 3.9 %collective-permute-start.8 = (bf16[256,512]{1,0:T(8,128)(2,1)S(1)}, bf16[256,512]{1,0:T(8,128)(2,1)S(1)}, u32[]{:S(2)}, u32[]{:S(2)}) collective-permute-start(bf16[256,512]{1,0:T(8,128)(2,1)S(1)} %get-tuple-element.37), channel_id=1, source_target_pairs={{0,4},{4,8},{8,12},{12,16},{16,20},{20,24},{24,28},{28,0},{1,5},{5... | collective-permute-start | bytes 786440 | tf_op jit(solution)/shard_map/ppermute | solution.py:297
  24.4 0.0 collective-permute-done.7.v_ref
  24.4 1.5 %collective-permute-done.5.k_ref = bf16[256,256]{1,0:T(8,128)(2,1)S(1)} collective-permute-done((bf16[256,256]{1,0:T(8,128)(2,1)S(1)}, bf16[256,256]{1,0:T(8,128)(2,1)S(1)}, u32[]{:S(2)}, u32[]{:S(2)}) %collective-permute-start.5) | collective-permute-done | bytes 131104 | tf_op jit(solution)/shard_map/ppermute | solution.py:297
  25.9 2.3 %shard_map.106 = (f32[1024,256]{1,0:T(8,128)S(1)}, bf16[256,512]{1,0:T(8,128)(2,1)S(1)}) custom-call(s32[2]{0:T(128)S(1)} %pad_add_fusion.slot_ref, s32[8]{0:T(128)} %span_ref.5, bf16[256,256]{1,0:T(8,128)(2,1)S(1)} %collective-permute-done.5.k_ref, bf16[256,256]{1,0:T(8,128)(2,1)S(1)} %collective-permute-done.7.v_ref, ...), custom_call_target="tpu_custom_call" | custom-call | flops 1048576 | bytes 8388608 | tf_op jit(solution)/shard_map/pallas_call | solution.py:349
  28.2 0.1 collective-permute-start.9
  28.3 2.7 %collective-permute-done.3.kv_ref = bf16[256,512]{1,0:T(8,128)(2,1)S(1)} collective-permute-done((bf16[256,512]{1,0:T(8,128)(2,1)S(1)}, bf16[256,512]{1,0:T(8,128)(2,1)S(1)}, u32[]{:S(2)}, u32[]{:S(2)}) %collective-permute-start.3) | collective-permute-done | bytes 262176 | tf_op jit(solution)/shard_map/ppermute | solution.py:297
  31.0 2.3 %shard_map.107 = (f32[1024,256]{1,0:T(8,128)S(1)}, bf16[256,512]{1,0:T(8,128)(2,1)S(1)}) custom-call(s32[2]{0:T(128)S(1)} %pad_add_fusion.slot_ref, s32[8]{0:T(128)} %span_ref.5, bf16[256,512]{1,0:T(8,128)(2,1)S(1)} %collective-permute-done.3.kv_ref, bf16[256,1024]{1,0:T(8,128)(2,1)S(1)} %get-tuple-element.27.qr_ref, ...), custom_call_target="tpu_custom_call" | custom-call | flops 1048576 | bytes 8388608 | tf_op jit(solution)/shard_map/pallas_call | solution.py:353
  33.3 3.8 %collective-permute-done.8.back_ref = bf16[256,512]{1,0:T(8,128)(2,1)S(1)} collective-permute-done((bf16[256,512]{1,0:T(8,128)(2,1)S(1)}, bf16[256,512]{1,0:T(8,128)(2,1)S(1)}, u32[]{:S(2)}, u32[]{:S(2)}) %collective-permute-start.8) | collective-permute-done | bytes 262176 | tf_op jit(solution)/shard_map/ppermute | solution.py:297
  37.0 1.1 %shard_map.108 = (bf16[256,1024]{1,0:T(8,128)(2,1)}, f32[256,512]{1,0:T(8,128)S(1)}) custom-call(f32[128,256]{1,0:T(8,128)S(1)} %get-tuple-element.24.tables_ref, f32[1024,256]{1,0:T(8,128)S(1)} %get-tuple-element.35.dqt_ref, f32[256,512]{1,0:T(8,128)S(1)} %get-tuple-element.36.own_ref, bf16[256,512]{1,0:T(8,128)(2,1)S(1)} %collective-permute-done.8.back_ref), custom_call_target="tpu_custom_call" | custom-call | flops 1048576 | bytes 4194304 | tf_op jit(solution)/shard_map/pallas_call | solution.py:356
  38.1 3.7 %collective-permute-done.9.b_ref = bf16[256,512]{1,0:T(8,128)(2,1)S(1)} collective-permute-done((bf16[256,512]{1,0:T(8,128)(2,1)S(1)}, bf16[256,512]{1,0:T(8,128)(2,1)S(1)}, u32[]{:S(2)}, u32[]{:S(2)}) %collective-permute-start.9) | collective-permute-done | bytes 262176 | tf_op jit(solution)/shard_map/ppermute | solution.py:297
  41.8 0.1 shard_map.109
  41.9 1.8 %collective-permute-start.10 = (bf16[256,512]{1,0:T(8,128)(2,1)S(1)}, bf16[256,512]{1,0:T(8,128)(2,1)S(1)}, u32[]{:S(2)}, u32[]{:S(2)}) collective-permute-start(bf16[256,512]{1,0:T(8,128)(2,1)S(1)} %shard_map.109), channel_id=1, source_target_pairs={{0,8},{4,12},{8,16},{12,20},{16,24},{20,28},{24,0},{28,4},{1,9},{5... | collective-permute-start | bytes 786440 | tf_op jit(solution)/shard_map/ppermute | solution.py:297
  43.7 8.2 %collective-permute-done.10.a_ref = bf16[256,512]{1,0:T(8,128)(2,1)S(1)} collective-permute-done((bf16[256,512]{1,0:T(8,128)(2,1)S(1)}, bf16[256,512]{1,0:T(8,128)(2,1)S(1)}, u32[]{:S(2)}, u32[]{:S(2)}) %collective-permute-start.10) | collective-permute-done | bytes 262176 | tf_op jit(solution)/shard_map/ppermute | solution.py:297
  52.0 0.9 %shard_map.110 = (bf16[256,256]{1,0:T(8,128)(2,1)}, bf16[256,256]{1,0:T(8,128)(2,1)}) custom-call(f32[128,256]{1,0:T(8,128)S(1)} %get-tuple-element.24.tables_ref, f32[256,512]{1,0:T(8,128)S(1)} %get-tuple-element.39.own_ref, bf16[256,512]{1,0:T(8,128)(2,1)S(1)} %collective-permute-done.10.a_ref), custom_call_target="tpu_custom_call" | custom-call | flops 1048576 | bytes 1048576 | tf_op jit(solution)/shard_map/pallas_call | solution.py:363
  (3 shorter events, 0.0 us)
Async XLA Ops:
  0.6 12.1 %copy-start = (bf16[256,256]{1,0:T(8,128)(2,1)S(1)}, bf16[256,256]{1,0:T(8,128)(2,1)}, u32[]{:S(2)}) copy-start(bf16[256,256]{1,0:T(8,128)(2,1)} %v_ref.1) | copy-start | bytes 393220
  0.6 9.4 %collective-permute-start.1 = (s32[3,64]{1,0:T(4,128)}, s32[3,64]{1,0:T(4,128)S(1)}, u32[]{:S(2)}, u32[]{:S(2)}) collective-permute-start(s32[3,64]{1,0:T(4,128)} %own_ref.1), channel_id=1, source_target_pairs={{0,2},{1,3},{2,0},{3,1},{4,6},{5,7},{6,4},{7,5},{8,10},{9,11},{10,... | collective-permute-start | bytes 2312 | tf_op jit(solution)/shard_map/ppermute | solution.py:297
  3.6 6.4 %collective-permute-start = (s32[3,64]{1,0:T(4,128)}, s32[3,64]{1,0:T(4,128)S(1)}, u32[]{:S(2)}, u32[]{:S(2)}) collective-permute-start(s32[3,64]{1,0:T(4,128)} %own_ref.1), channel_id=1, source_target_pairs={{0,1},{1,2},{2,3},{3,0},{4,5},{5,6},{6,7},{7,4},{8,9},{9,10},{10,1... | collective-permute-start | bytes 2312 | tf_op jit(solution)/shard_map/ppermute | solution.py:297
  3.6 6.4 %collective-permute-start.2 = (s32[3,64]{1,0:T(4,128)}, s32[3,64]{1,0:T(4,128)S(1)}, u32[]{:S(2)}, u32[]{:S(2)}) collective-permute-start(s32[3,64]{1,0:T(4,128)} %own_ref.1), channel_id=1, source_target_pairs={{0,3},{1,0},{2,1},{3,2},{4,7},{5,4},{6,5},{7,6},{8,11},{9,8},{10,9... | collective-permute-start | bytes 2312 | tf_op jit(solution)/shard_map/ppermute | solution.py:297
  5.4 11.3 %collective-permute-start.6 = (bf16[256,256]{1,0:T(8,128)(2,1)}, bf16[256,256]{1,0:T(8,128)(2,1)S(1)}, u32[]{:S(2)}, u32[]{:S(2)}) collective-permute-start(bf16[256,256]{1,0:T(8,128)(2,1)} %v_ref.1), channel_id=1, source_target_pairs={{0,28},{4,0},{8,4},{12,8},{16,12},{20,16},{24,20},{28,24},{1,29},{... | collective-permute-start | bytes 393224 | tf_op jit(solution)/shard_map/ppermute | solution.py:297
  10.0 2.7 %copy-start.1 = (f32[8,256]{1,0:T(8,128)S(1)}, f32[8,256]{1,0:T(8,128)}, u32[]{:S(2)}) copy-start(f32[8,256]{1,0:T(8,128)} %lse_ref.1) | copy-start | bytes 24580
  11.3 6.0 %collective-permute-start.4 = (bf16[256,256]{1,0:T(8,128)(2,1)S(1)}, bf16[256,256]{1,0:T(8,128)(2,1)S(1)}, u32[]{:S(2)}, u32[]{:S(2)}) collective-permute-start(bf16[256,256]{1,0:T(8,128)(2,1)S(1)} %get-tuple-element.25.kr_ref), channel_id=1, source_target_pairs={{0,28},{4,0},{8,4},{12,8},{16,12},{20,16},{24,20},{28,24},{1,29},{... | collective-permute-start | bytes 393224 | tf_op jit(solution)/shard_map/ppermute | solution.py:297
  16.7 7.7 %collective-permute-start.7 = (bf16[256,256]{1,0:T(8,128)(2,1)S(1)}, bf16[256,256]{1,0:T(8,128)(2,1)S(1)}, u32[]{:S(2)}, u32[]{:S(2)}) collective-permute-start(bf16[256,256]{1,0:T(8,128)(2,1)S(1)} %collective-permute-done.6.v_ref), channel_id=1, source_target_pairs={{0,24},{4,28},{8,0},{12,4},{16,8},{20,12},{24,16},{28,20},{1,25},{... | collective-permute-start | bytes 393224 | tf_op jit(solution)/shard_map/ppermute | solution.py:297
  17.2 8.7 %collective-permute-start.5 = (bf16[256,256]{1,0:T(8,128)(2,1)S(1)}, bf16[256,256]{1,0:T(8,128)(2,1)S(1)}, u32[]{:S(2)}, u32[]{:S(2)}) collective-permute-start(bf16[256,256]{1,0:T(8,128)(2,1)S(1)} %collective-permute-done.4.k_ref), channel_id=1, source_target_pairs={{0,24},{4,28},{8,0},{12,4},{16,8},{20,12},{24,16},{28,20},{1,25},{... | collective-permute-start | bytes 393224 | tf_op jit(solution)/shard_map/ppermute | solution.py:297
  17.8 13.1 %collective-permute-start.3 = (bf16[256,512]{1,0:T(8,128)(2,1)S(1)}, bf16[256,512]{1,0:T(8,128)(2,1)S(1)}, u32[]{:S(2)}, u32[]{:S(2)}) collective-permute-start(bf16[256,512]{1,0:T(8,128)(2,1)S(1)} %get-tuple-element.26), channel_id=1, source_target_pairs={{0,24},{4,28},{8,0},{12,4},{16,8},{20,12},{24,16},{28,20},{1,25},{... | collective-permute-start | bytes 786440 | tf_op jit(solution)/shard_map/ppermute | solution.py:297
  20.6 16.5 %collective-permute-start.8 = (bf16[256,512]{1,0:T(8,128)(2,1)S(1)}, bf16[256,512]{1,0:T(8,128)(2,1)S(1)}, u32[]{:S(2)}, u32[]{:S(2)}) collective-permute-start(bf16[256,512]{1,0:T(8,128)(2,1)S(1)} %get-tuple-element.37), channel_id=1, source_target_pairs={{0,4},{4,8},{8,12},{12,16},{16,20},{20,24},{24,28},{28,0},{1,5},{5... | collective-permute-start | bytes 786440 | tf_op jit(solution)/shard_map/ppermute | solution.py:297
  28.2 13.6 %collective-permute-start.9 = (bf16[256,512]{1,0:T(8,128)(2,1)S(1)}, bf16[256,512]{1,0:T(8,128)(2,1)S(1)}, u32[]{:S(2)}, u32[]{:S(2)}) collective-permute-start(bf16[256,512]{1,0:T(8,128)(2,1)S(1)} %get-tuple-element.42), channel_id=1, source_target_pairs={{0,4},{4,8},{8,12},{12,16},{16,20},{20,24},{24,28},{28,0},{1,5},{5... | collective-permute-start | bytes 786440 | tf_op jit(solution)/shard_map/ppermute | solution.py:297
  41.9 10.1 %collective-permute-start.10 = (bf16[256,512]{1,0:T(8,128)(2,1)S(1)}, bf16[256,512]{1,0:T(8,128)(2,1)S(1)}, u32[]{:S(2)}, u32[]{:S(2)}) collective-permute-start(bf16[256,512]{1,0:T(8,128)(2,1)S(1)} %shard_map.109), channel_id=1, source_target_pairs={{0,8},{4,12},{8,16},{12,20},{16,24},{20,28},{24,0},{28,4},{1,9},{5... | collective-permute-start | bytes 786440 | tf_op jit(solution)/shard_map/ppermute | solution.py:297

commit v7 on v6

--- a/solution.py
+++ b/solution.py
@@ -140,7 +140,7 @@
 
 def first_kernel(
     tables_ref, kr_ref, v_ref, lse_ref, q_hbm, do_hbm, at_hbm,
-    qr_ref, do_ref, norm_ref, delta_ref, dqt_ref, dkv_ref, kv_ref, q_ref, at_ref, sems,
+    qr_ref, do_ref, norm_ref, delta_ref, dqt_ref, dkv_ref, q_ref, at_ref, sems,
 ):
     heads = qr_ref.shape[1] // HEAD
     groups = kr_ref.shape[1] // HEAD
@@ -159,8 +159,6 @@
     wide, signed = row_tables(tables_ref[:HALF, :], tables_ref[HALF:, :])
     norm = lse_ref[...] * LOG2E
     norm_ref[...] = norm
-    kv_ref[:, : groups * HEAD] = kr_ref[...]
-    kv_ref[:, groups * HEAD :] = v_ref[...]
     chooser = jnp.ones((8, HEAD), BF16)
     for g in range(groups):
         cols = pl.ds(g * HEAD, HEAD)
@@ -232,19 +230,8 @@
         run(slice(0, rows), slice(half, rows))
 
 
-def turned_kernel(
-    step, slot_ref, span_ref, kv_ref, qr_ref, do_ref, norm_ref, delta_ref, dqt_in,
-    dqt_ref, dkv_ref,
-):
-    width = kv_ref.shape[1] // 2
-    hop_body(
-        step, slot_ref, span_ref, kv_ref.at[:, :width], kv_ref.at[:, width:], qr_ref, do_ref,
-        norm_ref, delta_ref, dqt_in, dqt_ref, dkv_ref,
-    )
-
-
-def query_kernel(tables_ref, dqt_ref, own_ref, back_ref, out_ref, sum_ref):
-    sum_ref[...] = own_ref[...] + back_ref[...].astype(F32)
+def query_kernel(tables_ref, dqt_ref, own_ref, a_ref, b_ref, out_ref, sum_ref):
+    sum_ref[...] = own_ref[...] + a_ref[...].astype(F32) + b_ref[...].astype(F32)
     cosine_t = tables_ref[:HALF, :] * ROOT_SCALE
     sine_t = tables_ref[HALF:, :] * ROOT_SCALE
     for h in range(out_ref.shape[1] // HEAD):
@@ -254,10 +241,6 @@
             [y1 * cosine_t + y2 * sine_t, y2 * cosine_t - y1 * sine_t], axis=0
         )
         out_ref[:, pl.ds(h * HEAD, HEAD)] = turned.T.astype(BF16)
-
-
-def add_kernel(a_ref, b_ref, sum_ref):
-    sum_ref[...] = (a_ref[...].astype(F32) + b_ref[...].astype(F32)).astype(BF16)
 
 
 def final_kernel(tables_ref, own_ref, a_ref, dk_ref, dv_ref):
@@ -277,7 +260,7 @@
 HBM = pl.BlockSpec(memory_space=pltpu.HBM)
 
 
-def call(kernel, outs, specs, scratch=(), moved=1):
+def call(kernel, outs, specs, scratch=()):
     return pl.pallas_call(
         kernel,
         out_shape=[jax.ShapeDtypeStruct(shape, dtype) for shape, dtype in outs],
@@ -286,7 +269,7 @@
         scratch_shapes=list(scratch),
         compiler_params=pltpu.CompilerParams(vmem_limit_bytes=VMEM_LIMIT),
         cost_estimate=pl.CostEstimate(
-            flops=1 << 20, bytes_accessed=moved << 20, transcendentals=0
+            flops=1 << 20, bytes_accessed=1 << 18, transcendentals=0
         ),
     )
 
@@ -303,22 +286,25 @@
     wide_k = k.shape[1]
     heads = wide_q // HEAD
     slot = jnp.stack([lax.axis_index("ctx"), lax.axis_index("head")]).astype(jnp.int32)
-    q, do, at, k_here, span_map, own = (
+    q, do, at, k_here, v_here, lse, span_map, own = (
         pltpu.with_memory_space_constraint(x, pltpu.HBM)
-        for x in (q, do, at, k, span_map, positions)
+        for x in (q, do, at, k, v, lse, span_map, positions)
     )
 
     pieces = [own] + [shifted(positions, r, "head") for r in (1, 2, 3)]
     v1 = shifted(v, -1)
+    v2 = shifted(v, -2)
     kr, tables = call(
         key_kernel,
         [((rows, wide_k), BF16), ((HEAD, rows), F32)],
         [SMEM] + [VMEM] * 5,
-        moved=16,
     )(slot, *pieces, k_here)
-    k1 = shifted(kr, -1)
+    kr1, v1 = lax.optimization_barrier((kr, v1))
+    k1 = shifted(kr1, -1)
     v3 = shifted(v1, -2)
-    qr, grad, norm, delta, dqt, dkv, kv = call(
+    kr2, v2 = lax.optimization_barrier((kr, v2))
+    k2 = shifted(kr2, -2)
+    qr, grad, norm, delta, dqt, dkv = call(
         first_kernel,
         [
             ((rows, wide_q), BF16),
@@ -327,7 +313,6 @@
             ((heads, rows), F32),
             ((wide_q, rows), F32),
             ((rows, 2 * wide_k), F32),
-            ((rows, 2 * wide_k), BF16),
         ],
         [VMEM] * 4 + [HBM] * 3,
         [
@@ -335,36 +320,27 @@
             pltpu.VMEM((rows, wide_q), BF16),
             pltpu.SemaphoreType.DMA((3 * (wide_k // HEAD),)),
         ],
-        moved=12,
-    )(tables, kr, v, lse, q, do, at)
+    )(tables, kr, v_here, lse, q, do, at)
     held, _ = lax.optimization_barrier((k1, delta))
     k3 = shifted(held, -2)
-    kv2 = shifted(kv, -2)
-
-    outs = [((wide_q, rows), F32), ((rows, 2 * wide_k), BF16)]
-    dqt, part1 = call(
-        functools.partial(hop_body, 1), outs, [SMEM] * 2 + [VMEM] * 7, moved=8
-    )(slot, span_map, k1, v1, qr, grad, norm, delta, dqt)
-    back1 = shifted(part1, 1)
-    dqt, part3 = call(
-        functools.partial(hop_body, 3), outs, [SMEM] * 2 + [VMEM] * 7, moved=8
-    )(slot, span_map, k3, v3, qr, grad, norm, delta, dqt)
-    back3 = shifted(part3, 1)
-    dqt, part2 = call(
-        functools.partial(turned_kernel, 2), outs, [SMEM] * 2 + [VMEM] * 6, moved=8
-    )(slot, span_map, kv2, qr, grad, norm, delta, dqt)
+
+    backs = []
+    for step, key, value in ((1, k1, v1), (2, k2, v2), (3, k3, v3)):
+        dqt, part = call(
+            functools.partial(hop_body, step),
+            [((wide_q, rows), F32), ((rows, 2 * wide_k), BF16)],
+            [SMEM] * 2 + [VMEM] * 7,
+        )(slot, span_map, key, value, qr, grad, norm, delta, dqt)
+        backs.append(shifted(part, step))
     dq, dkv = call(
-        query_kernel, [((rows, wide_q), BF16), ((rows, 2 * wide_k), F32)], [VMEM] * 4, moved=4
-    )(tables, dqt, dkv, back1)
-    part2, _ = lax.optimization_barrier((part2, dkv))
-    (part23,) = call(add_kernel, [((rows, 2 * wide_k), BF16)], [VMEM] * 2)(part2, back3)
-    back2 = shifted(part23, 2)
+        query_kernel, [((rows, wide_q), BF16), ((rows, 2 * wide_k), F32)], [VMEM] * 5
+    )(tables, dqt, dkv, backs[1], backs[0])
 
     dk, dv = call(
         final_kernel,
         [((rows, wide_k), BF16), ((rows, wide_k), BF16)],
         [VMEM] * 3,
-    )(tables, dkv, back2)
+    )(tables, dkv, backs[2])
     return dq, dk, dv
 
 

time: 53.1 us -> 52.8 us (level)
  waiting for transfers between devices: 19.9 us -> 17.8 us
  Pallas kernels: 14.1 us -> 15 us
  starting transfers between devices: 18.1 us -> 19 us
    ppermute x11 -> x12, waiting for transfers between devices: 19.9 us -> 17.8 us  [shifted(): return lax.ppermute(value, axis, pairs)]
    ppermute x11 -> x12, starting transfers between devices: 18.1 us -> 19 us  [shifted(): return lax.ppermute(value, axis, pairs)]
    pallas_call x1, Pallas kernels: 3.95 us -> 4.85 us  [shards(): call(first_kernel, [((rows, wide_q), BF16), ((rows, wide_q), BF16), ((hea...]
    pallas_call x4 -> x3, Pallas kernels: 6.93 us -> 6.87 us  [shards(): call(functools.partial(hop_body, step), [((wide_q, rows), F32), ((rows, 2...]
  transfers between devices with their start and end apart: 11 -> 12, of which waited for: 5 -> 5; matrix products, arithmetic and copies ran while one was open for 0% -> 0% of each run, Pallas kernels for 25% -> 27%
where the time goes in v7:
time: 52.8 us; the launch traced here: 52.6 us
  starting transfers between devices  19 us (36%)
  waiting for transfers between devices  17.8 us (34%)
  Pallas kernels  15 us (28%)
  between operations  0.69 us (1%)
    ppermute x12, starting transfers between devices, shifted(): return lax.ppermute(value, axis, pairs)  19 us
    ppermute x12, waiting for transfers between devices, shifted(): return lax.ppermute(value, axis, pairs)  17.8 us
    pallas_call x3, Pallas kernels, shards(): call(functools.partial(hop_body, step), [((wide_q, rows), F32), ((rows, 2...  6.87 us
    pallas_call x1, Pallas kernels, shards(): call(first_kernel, [((rows, wide_q), BF16), ((rows, wide_q), BF16), ((hea...  4.85 us
    pallas_call x1, Pallas kernels, shards(): call(key_kernel, [((rows, wide_k), BF16), ((HEAD, rows), F32)], [SMEM] +...  1.24 us
    pallas_call x1, Pallas kernels, shards(): call(query_kernel, [((rows, wide_q), BF16), ((rows, 2 * wide_k), F32)], [...  1.1 us
  transfers between devices with their start and end apart: 12, of which 5 were waited for; matrix products, arithmetic and copies ran while one was open for 0% of the time, Pallas kernels for 27%

profile of v7, /device:TPU:0, one launch (start us, length us, event | category | flops | bytes accessed | tf_op | source)
XLA Modules:
  0.0 52.6 jit_solution(7160556516835389135)
XLA Ops:
  0.6 6.1 %collective-permute-start.3 = (bf16[256,256]{1,0:T(8,128)(2,1)}, bf16[256,256]{1,0:T(8,128)(2,1)S(1)}, u32[]{:S(2)}, u32[]{:S(2)}) collective-permute-start(bf16[256,256]{1,0:T(8,128)(2,1)} %v_ref.1), channel_id=1, source_target_pairs={{0,28},{4,0},{8,4},{12,8},{16,12},{20,16},{24,20},{28,24},{1,29},{... | collective-permute-start | bytes 393224 | tf_op jit(solution)/shard_map/ppermute | solution.py:280
  6.7 1.5 %collective-permute-start.1 = (s32[3,64]{1,0:T(4,128)}, s32[3,64]{1,0:T(4,128)S(1)}, u32[]{:S(2)}, u32[]{:S(2)}) collective-permute-start(s32[3,64]{1,0:T(4,128)} %own_ref.1), channel_id=1, source_target_pairs={{0,2},{1,3},{2,0},{3,1},{4,6},{5,7},{6,4},{7,5},{8,10},{9,11},{10,... | collective-permute-start | bytes 2312 | tf_op jit(solution)/shard_map/ppermute | solution.py:280
  8.2 0.0 collective-permute-start
  8.2 1.7 %collective-permute-start.2 = (s32[3,64]{1,0:T(4,128)}, s32[3,64]{1,0:T(4,128)S(1)}, u32[]{:S(2)}, u32[]{:S(2)}) collective-permute-start(s32[3,64]{1,0:T(4,128)} %own_ref.1), channel_id=1, source_target_pairs={{0,3},{1,0},{2,1},{3,2},{4,7},{5,4},{6,5},{7,6},{8,11},{9,8},{10,9... | collective-permute-start | bytes 2312 | tf_op jit(solution)/shard_map/ppermute | solution.py:280
  9.9 0.4 collective-permute-start.7
  10.4 0.1 pad_add_fusion.slot_ref
  10.5 0.0 collective-permute-done.1.p2_ref
  10.5 0.9 %collective-permute-done.p1_ref = s32[3,64]{1,0:T(4,128)S(1)} collective-permute-done((s32[3,64]{1,0:T(4,128)}, s32[3,64]{1,0:T(4,128)S(1)}, u32[]{:S(2)}, u32[]{:S(2)}) %collective-permute-start) | collective-permute-done | bytes 800 | tf_op jit(solution)/shard_map/ppermute | solution.py:280
  11.4 0.0 collective-permute-done.2.p3_ref
  11.4 1.2 %shard_map.103 = (bf16[256,256]{1,0:T(8,128)(2,1)S(1)}, f32[128,256]{1,0:T(8,128)S(1)}) custom-call(s32[2]{0:T(128)S(1)} %pad_add_fusion.slot_ref, s32[3,64]{1,0:T(4,128)} %own_ref.1, s32[3,64]{1,0:T(4,128)S(1)} %collective-permute-done.p1_ref, s32[3,64]{1,0:T(4,128)S(1)} %collective-permute-done.1.p2_ref, s32[3,64]{1,0:T(4,128)S(1)} %collective-permute-done.2.p3_ref, ...), custom_call_target="tpu_custom_call" | custom-call | flops 1048576 | bytes 262144 | tf_op jit(solution)/shard_map/pallas_call | solution.py:297
  12.7 0.0 collective-permute-done.3.v_ref
  12.7 2.1 %collective-permute-start.4 = (bf16[256,256]{1,0:T(8,128)(2,1)S(1)}, bf16[256,256]{1,0:T(8,128)(2,1)S(1)}, u32[]{:S(2)}, u32[]{:S(2)}) collective-permute-start(bf16[256,256]{1,0:T(8,128)(2,1)S(1)} %get-tuple-element.35.kr_ref), channel_id=1, source_target_pairs={{0,28},{4,0},{8,4},{12,8},{16,12},{20,16},{24,20},{28,24},{1,29},{... | collective-permute-start | bytes 393224 | tf_op jit(solution)/shard_map/ppermute | solution.py:280
  14.8 1.0 %collective-permute-done.7.v_ref = bf16[256,256]{1,0:T(8,128)(2,1)S(1)} collective-permute-done((bf16[256,256]{1,0:T(8,128)(2,1)}, bf16[256,256]{1,0:T(8,128)(2,1)S(1)}, u32[]{:S(2)}, u32[]{:S(2)}) %collective-permute-start.7) | collective-permute-done | bytes 131104 | tf_op jit(solution)/shard_map/ppermute | solution.py:280
  15.9 1.5 %collective-permute-start.8 = (bf16[256,256]{1,0:T(8,128)(2,1)S(1)}, bf16[256,256]{1,0:T(8,128)(2,1)S(1)}, u32[]{:S(2)}, u32[]{:S(2)}) collective-permute-start(bf16[256,256]{1,0:T(8,128)(2,1)S(1)} %get-tuple-element.35.kr_ref), channel_id=1, source_target_pairs={{0,24},{4,28},{8,0},{12,4},{16,8},{20,12},{24,16},{28,20},{1,25},{... | collective-permute-start | bytes 393224 | tf_op jit(solution)/shard_map/ppermute | solution.py:280
  17.4 4.8 %shard_map.104 = (bf16[256,1024]{1,0:T(8,128)(2,1)S(1)}, bf16[256,1024]{1,0:T(8,128)(2,1)S(1)}, f32[8,256]{1,0:T(8,128)S(1)}, f32[8,256]{1,0:T(8,128)S(1)}, f32[...) custom-call(f32[128,256]{1,0:T(8,128)S(1)} %get-tuple-element.26.tables_ref, bf16[256,256]{1,0:T(8,128)(2,1)S(1)} %get-tuple-element.35.kr_ref, ...), custom_call_target="tpu_custom_call" | custom-call | flops 1048576 | bytes 262144 | tf_op jit(solution)/shard_map/pallas_call | solution.py:307
  22.2 0.1 collective-permute-start.6
  22.3 0.0 collective-permute-done.4.k_ref
  22.3 1.1 %collective-permute-start.5 = (bf16[256,256]{1,0:T(8,128)(2,1)S(1)}, bf16[256,256]{1,0:T(8,128)(2,1)S(1)}, u32[]{:S(2)}, u32[]{:S(2)}) collective-permute-start(bf16[256,256]{1,0:T(8,128)(2,1)S(1)} %collective-permute-done.4.k_ref), channel_id=1, source_target_pairs={{0,24},{4,28},{8,0},{12,4},{16,8},{20,12},{24,16},{28,20},{1,25},{... | collective-permute-start | bytes 393224 | tf_op jit(solution)/shard_map/ppermute | solution.py:280
  23.3 2.3 %shard_map.105 = (f32[1024,256]{1,0:T(8,128)S(1)}, bf16[256,512]{1,0:T(8,128)(2,1)S(1)}) custom-call(s32[2]{0:T(128)S(1)} %pad_add_fusion.slot_ref, s32[8]{0:T(128)} %span_ref.5, bf16[256,256]{1,0:T(8,128)(2,1)S(1)} %collective-permute-done.4.k_ref, bf16[256,256]{1,0:T(8,128)(2,1)S(1)} %collective-permute-done.3.v_ref, ...), custom_call_target="tpu_custom_call" | custom-call | flops 1048576 | bytes 262144 | tf_op jit(solution)/shard_map/pallas_call | solution.py:329
  25.6 0.0 collective-permute-done.8.k_ref
  25.6 2.3 %shard_map.106 = (f32[1024,256]{1,0:T(8,128)S(1)}, bf16[256,512]{1,0:T(8,128)(2,1)S(1)}) custom-call(s32[2]{0:T(128)S(1)} %pad_add_fusion.slot_ref, s32[8]{0:T(128)} %span_ref.5, bf16[256,256]{1,0:T(8,128)(2,1)S(1)} %collective-permute-done.8.k_ref, bf16[256,256]{1,0:T(8,128)(2,1)S(1)} %collective-permute-done.7.v_ref, ...), custom_call_target="tpu_custom_call" | custom-call | flops 1048576 | bytes 262144 | tf_op jit(solution)/shard_map/pallas_call | solution.py:329
  27.9 1.1 %collective-permute-start.9 = (bf16[256,512]{1,0:T(8,128)(2,1)S(1)}, bf16[256,512]{1,0:T(8,128)(2,1)S(1)}, u32[]{:S(2)}, u32[]{:S(2)}) collective-permute-start(bf16[256,512]{1,0:T(8,128)(2,1)S(1)} %get-tuple-element.42), channel_id=1, source_target_pairs={{0,8},{4,12},{8,16},{12,20},{16,24},{20,28},{24,0},{28,4},{1,9},{5... | collective-permute-start | bytes 786440 | tf_op jit(solution)/shard_map/ppermute | solution.py:280
  29.0 0.6 %collective-permute-start.10 = (bf16[256,512]{1,0:T(8,128)(2,1)S(1)}, bf16[256,512]{1,0:T(8,128)(2,1)S(1)}, u32[]{:S(2)}, u32[]{:S(2)}) collective-permute-start(bf16[256,512]{1,0:T(8,128)(2,1)S(1)} %get-tuple-element.43), channel_id=1, source_target_pairs={{0,4},{4,8},{8,12},{12,16},{16,20},{20,24},{24,28},{28,0},{1,5},{5... | collective-permute-start | bytes 786440 | tf_op jit(solution)/shard_map/ppermute | solution.py:280
  29.7 0.0 collective-permute-done.6.v_ref
  29.7 0.0 collective-permute-done.5.k_ref
  29.7 2.3 %shard_map.107 = (f32[1024,256]{1,0:T(8,128)S(1)}, bf16[256,512]{1,0:T(8,128)(2,1)S(1)}) custom-call(s32[2]{0:T(128)S(1)} %pad_add_fusion.slot_ref, s32[8]{0:T(128)} %span_ref.5, bf16[256,256]{1,0:T(8,128)(2,1)S(1)} %collective-permute-done.5.k_ref, bf16[256,256]{1,0:T(8,128)(2,1)S(1)} %collective-permute-done.6.v_ref, ...), custom_call_target="tpu_custom_call" | custom-call | flops 1048576 | bytes 262144 | tf_op jit(solution)/shard_map/pallas_call | solution.py:329
  32.0 2.8 %collective-permute-start.11 = (bf16[256,512]{1,0:T(8,128)(2,1)S(1)}, bf16[256,512]{1,0:T(8,128)(2,1)S(1)}, u32[]{:S(2)}, u32[]{:S(2)}) collective-permute-start(bf16[256,512]{1,0:T(8,128)(2,1)S(1)} %get-tuple-element.46), channel_id=1, source_target_pairs={{0,12},{4,16},{8,20},{12,24},{16,28},{20,0},{24,4},{28,8},{1,13},{... | collective-permute-start | bytes 786440 | tf_op jit(solution)/shard_map/ppermute | solution.py:280
  34.8 2.5 %collective-permute-done.9.a_ref = bf16[256,512]{1,0:T(8,128)(2,1)S(1)} collective-permute-done((bf16[256,512]{1,0:T(8,128)(2,1)S(1)}, bf16[256,512]{1,0:T(8,128)(2,1)S(1)}, u32[]{:S(2)}, u32[]{:S(2)}) %collective-permute-start.9) | collective-permute-done | bytes 262176 | tf_op jit(solution)/shard_map/ppermute | solution.py:280
  37.2 6.1 %collective-permute-done.10.b_ref = bf16[256,512]{1,0:T(8,128)(2,1)S(1)} collective-permute-done((bf16[256,512]{1,0:T(8,128)(2,1)S(1)}, bf16[256,512]{1,0:T(8,128)(2,1)S(1)}, u32[]{:S(2)}, u32[]{:S(2)}) %collective-permute-start.10) | collective-permute-done | bytes 262176 | tf_op jit(solution)/shard_map/ppermute | solution.py:280
  43.3 1.1 %shard_map.108 = (bf16[256,1024]{1,0:T(8,128)(2,1)}, f32[256,512]{1,0:T(8,128)S(1)}) custom-call(f32[128,256]{1,0:T(8,128)S(1)} %get-tuple-element.26.tables_ref, f32[1024,256]{1,0:T(8,128)S(1)} %get-tuple-element.40.dqt_ref, f32[256,512]{1,0:T(8,128)S(1)} %get-tuple-element.41.own_ref, bf16[256,512]{1,0:T(8,128)(2,1)S(1)} %collective-permute-done.9.a_ref, ...), custom_call_target="tpu_custom_call" | custom-call | flops 1048576 | bytes 262144 | tf_op jit(solution)/shard_map/pallas_call | solution.py:335
  44.5 7.2 %collective-permute-done.11.a_ref = bf16[256,512]{1,0:T(8,128)(2,1)S(1)} collective-permute-done((bf16[256,512]{1,0:T(8,128)(2,1)S(1)}, bf16[256,512]{1,0:T(8,128)(2,1)S(1)}, u32[]{:S(2)}, u32[]{:S(2)}) %collective-permute-start.11) | collective-permute-done | bytes 262176 | tf_op jit(solution)/shard_map/ppermute | solution.py:280
  51.7 0.9 %shard_map.109 = (bf16[256,256]{1,0:T(8,128)(2,1)}, bf16[256,256]{1,0:T(8,128)(2,1)}) custom-call(f32[128,256]{1,0:T(8,128)S(1)} %get-tuple-element.26.tables_ref, f32[256,512]{1,0:T(8,128)S(1)} %get-tuple-element.45.own_ref, bf16[256,512]{1,0:T(8,128)(2,1)S(1)} %collective-permute-done.11.a_ref), custom_call_target="tpu_custom_call" | custom-call | flops 1048576 | bytes 262144 | tf_op jit(solution)/shard_map/pallas_call | solution.py:339
Async XLA Ops:
  0.6 12.1 %collective-permute-start.3 = (bf16[256,256]{1,0:T(8,128)(2,1)}, bf16[256,256]{1,0:T(8,128)(2,1)S(1)}, u32[]{:S(2)}, u32[]{:S(2)}) collective-permute-start(bf16[256,256]{1,0:T(8,128)(2,1)} %v_ref.1), channel_id=1, source_target_pairs={{0,28},{4,0},{8,4},{12,8},{16,12},{20,16},{24,20},{28,24},{1,29},{... | collective-permute-start | bytes 393224 | tf_op jit(solution)/shard_map/ppermute | solution.py:280
  6.7 3.8 %collective-permute-start.1 = (s32[3,64]{1,0:T(4,128)}, s32[3,64]{1,0:T(4,128)S(1)}, u32[]{:S(2)}, u32[]{:S(2)}) collective-permute-start(s32[3,64]{1,0:T(4,128)} %own_ref.1), channel_id=1, source_target_pairs={{0,2},{1,3},{2,0},{3,1},{4,6},{5,7},{6,4},{7,5},{8,10},{9,11},{10,... | collective-permute-start | bytes 2312 | tf_op jit(solution)/shard_map/ppermute | solution.py:280
  8.2 3.2 %collective-permute-start = (s32[3,64]{1,0:T(4,128)}, s32[3,64]{1,0:T(4,128)S(1)}, u32[]{:S(2)}, u32[]{:S(2)}) collective-permute-start(s32[3,64]{1,0:T(4,128)} %own_ref.1), channel_id=1, source_target_pairs={{0,1},{1,2},{2,3},{3,0},{4,5},{5,6},{6,7},{7,4},{8,9},{9,10},{10,1... | collective-permute-start | bytes 2312 | tf_op jit(solution)/shard_map/ppermute | solution.py:280
  8.2 3.3 %collective-permute-start.2 = (s32[3,64]{1,0:T(4,128)}, s32[3,64]{1,0:T(4,128)S(1)}, u32[]{:S(2)}, u32[]{:S(2)}) collective-permute-start(s32[3,64]{1,0:T(4,128)} %own_ref.1), channel_id=1, source_target_pairs={{0,3},{1,0},{2,1},{3,2},{4,7},{5,4},{6,5},{7,6},{8,11},{9,8},{10,9... | collective-permute-start | bytes 2312 | tf_op jit(solution)/shard_map/ppermute | solution.py:280
  9.9 5.9 %collective-permute-start.7 = (bf16[256,256]{1,0:T(8,128)(2,1)}, bf16[256,256]{1,0:T(8,128)(2,1)S(1)}, u32[]{:S(2)}, u32[]{:S(2)}) collective-permute-start(bf16[256,256]{1,0:T(8,128)(2,1)} %v_ref.1), channel_id=1, source_target_pairs={{0,24},{4,28},{8,0},{12,4},{16,8},{20,12},{24,16},{28,20},{1,25},{... | collective-permute-start | bytes 393224 | tf_op jit(solution)/shard_map/ppermute | solution.py:280
  12.7 9.6 %collective-permute-start.4 = (bf16[256,256]{1,0:T(8,128)(2,1)S(1)}, bf16[256,256]{1,0:T(8,128)(2,1)S(1)}, u32[]{:S(2)}, u32[]{:S(2)}) collective-permute-start(bf16[256,256]{1,0:T(8,128)(2,1)S(1)} %get-tuple-element.35.kr_ref), channel_id=1, source_target_pairs={{0,28},{4,0},{8,4},{12,8},{16,12},{20,16},{24,20},{28,24},{1,29},{... | collective-permute-start | bytes 393224 | tf_op jit(solution)/shard_map/ppermute | solution.py:280
  15.9 9.8 %collective-permute-start.8 = (bf16[256,256]{1,0:T(8,128)(2,1)S(1)}, bf16[256,256]{1,0:T(8,128)(2,1)S(1)}, u32[]{:S(2)}, u32[]{:S(2)}) collective-permute-start(bf16[256,256]{1,0:T(8,128)(2,1)S(1)} %get-tuple-element.35.kr_ref), channel_id=1, source_target_pairs={{0,24},{4,28},{8,0},{12,4},{16,8},{20,12},{24,16},{28,20},{1,25},{... | collective-permute-start | bytes 393224 | tf_op jit(solution)/shard_map/ppermute | solution.py:280
  22.2 7.4 %collective-permute-start.6 = (bf16[256,256]{1,0:T(8,128)(2,1)S(1)}, bf16[256,256]{1,0:T(8,128)(2,1)S(1)}, u32[]{:S(2)}, u32[]{:S(2)}) collective-permute-start(bf16[256,256]{1,0:T(8,128)(2,1)S(1)} %collective-permute-done.3.v_ref), channel_id=1, source_target_pairs={{0,24},{4,28},{8,0},{12,4},{16,8},{20,12},{24,16},{28,20},{1,25},{... | collective-permute-start | bytes 393224 | tf_op jit(solution)/shard_map/ppermute | solution.py:280
  22.3 7.4 %collective-permute-start.5 = (bf16[256,256]{1,0:T(8,128)(2,1)S(1)}, bf16[256,256]{1,0:T(8,128)(2,1)S(1)}, u32[]{:S(2)}, u32[]{:S(2)}) collective-permute-start(bf16[256,256]{1,0:T(8,128)(2,1)S(1)} %collective-permute-done.4.k_ref), channel_id=1, source_target_pairs={{0,24},{4,28},{8,0},{12,4},{16,8},{20,12},{24,16},{28,20},{1,25},{... | collective-permute-start | bytes 393224 | tf_op jit(solution)/shard_map/ppermute | solution.py:280
  27.9 9.3 %collective-permute-start.9 = (bf16[256,512]{1,0:T(8,128)(2,1)S(1)}, bf16[256,512]{1,0:T(8,128)(2,1)S(1)}, u32[]{:S(2)}, u32[]{:S(2)}) collective-permute-start(bf16[256,512]{1,0:T(8,128)(2,1)S(1)} %get-tuple-element.42), channel_id=1, source_target_pairs={{0,8},{4,12},{8,16},{12,20},{16,24},{20,28},{24,0},{28,4},{1,9},{5... | collective-permute-start | bytes 786440 | tf_op jit(solution)/shard_map/ppermute | solution.py:280
  29.0 14.3 %collective-permute-start.10 = (bf16[256,512]{1,0:T(8,128)(2,1)S(1)}, bf16[256,512]{1,0:T(8,128)(2,1)S(1)}, u32[]{:S(2)}, u32[]{:S(2)}) collective-permute-start(bf16[256,512]{1,0:T(8,128)(2,1)S(1)} %get-tuple-element.43), channel_id=1, source_target_pairs={{0,4},{4,8},{8,12},{12,16},{16,20},{20,24},{24,28},{28,0},{1,5},{5... | collective-permute-start | bytes 786440 | tf_op jit(solution)/shard_map/ppermute | solution.py:280
  32.0 19.7 %collective-permute-start.11 = (bf16[256,512]{1,0:T(8,128)(2,1)S(1)}, bf16[256,512]{1,0:T(8,128)(2,1)S(1)}, u32[]{:S(2)}, u32[]{:S(2)}) collective-permute-start(bf16[256,512]{1,0:T(8,128)(2,1)S(1)} %get-tuple-element.46), channel_id=1, source_target_pairs={{0,12},{4,16},{8,20},{12,24},{16,28},{20,0},{24,4},{28,8},{1,13},{... | collective-permute-start | bytes 786440 | tf_op jit(solution)/shard_map/ppermute | solution.py:280

commit v8 on v7

--- a/solution.py
+++ b/solution.py
@@ -138,12 +138,11 @@
         kr_ref[:, cols] = rotated(k_ref[:, cols].astype(F32), wide, signed).astype(BF16)
 
 
-def first_kernel(
-    tables_ref, kr_ref, v_ref, lse_ref, q_hbm, do_hbm, at_hbm,
-    qr_ref, do_ref, norm_ref, delta_ref, dqt_ref, dkv_ref, q_ref, at_ref, sems,
+def prep_kernel(
+    groups, tables_ref, lse_hbm, q_hbm, do_hbm, at_hbm,
+    qr_ref, do_ref, norm_ref, delta_ref, q_ref, at_ref, lse_ref, sems,
 ):
     heads = qr_ref.shape[1] // HEAD
-    groups = kr_ref.shape[1] // HEAD
     size = heads // groups
     copies = []
     for g in range(groups):
@@ -156,39 +155,29 @@
             )
             copy.start()
             copies.append(copy)
+    lse_copy = pltpu.make_async_copy(lse_hbm, lse_ref, sems.at[3 * groups])
+    lse_copy.start()
     wide, signed = row_tables(tables_ref[:HALF, :], tables_ref[HALF:, :])
-    norm = lse_ref[...] * LOG2E
-    norm_ref[...] = norm
     chooser = jnp.ones((8, HEAD), BF16)
-    for g in range(groups):
-        cols = pl.ds(g * HEAD, HEAD)
-        dk = dv = None
-        for copy in copies[3 * g : 3 * g + 3]:
-            copy.wait()
-        for h in range(g * size, (g + 1) * size):
-            hc = pl.ds(h * HEAD, HEAD)
-            grad = do_ref[:, hc]
-            query = rotated(q_ref[:, hc].astype(F32), wide, signed).astype(BF16)
-            qr_ref[:, hc] = query
-            product = grad.astype(F32) * at_ref[:, hc].astype(F32)
-            high = product.astype(BF16)
-            low = (product - high.astype(F32)).astype(BF16)
-            delta = (dot_nt(chooser, high) + dot_nt(chooser, low))[:1]
-            delta_ref[h : h + 1, :] = delta
-            v_part, k_part, q_part = pair_part(
-                kr_ref[:, cols], v_ref[:, cols], query, grad, norm[h : h + 1], delta, True
-            )
-            dqt_ref[hc, :] = q_part
-            dv = v_part if dv is None else dv + v_part
-            dk = k_part if dk is None else dk + k_part
-        dkv_ref[:, cols] = dk
-        dkv_ref[:, pl.ds((groups + g) * HEAD, HEAD)] = dv
+    for h in range(heads):
+        if h % size == 0:
+            for copy in copies[3 * (h // size) : 3 * (h // size) + 3]:
+                copy.wait()
+        hc = pl.ds(h * HEAD, HEAD)
+        qr_ref[:, hc] = rotated(q_ref[:, hc].astype(F32), wide, signed).astype(BF16)
+        product = do_ref[:, hc].astype(F32) * at_ref[:, hc].astype(F32)
+        high = product.astype(BF16)
+        low = (product - high.astype(F32)).astype(BF16)
+        delta_ref[h : h + 1, :] = (dot_nt(chooser, high) + dot_nt(chooser, low))[:1]
+    lse_copy.wait()
+    norm_ref[...] = lse_ref[...] * LOG2E
 
 
 def hop_body(
-    step, slot_ref, span_ref, k_ref, v_ref, qr_ref, do_ref, norm_ref, delta_ref,
-    dqt_in, dqt_ref, dkv_ref,
+    step, slot_ref, span_ref, k_ref, v_ref, qr_ref, do_ref, norm_ref, delta_ref, *refs
 ):
+    dqt_ref, dkv_ref = refs[-2:]
+    dqt_in = refs[0] if len(refs) > 2 else None
     rows = qr_ref.shape[0]
     half = rows // 2
     heads = qr_ref.shape[1] // HEAD
@@ -212,8 +201,11 @@
                     norm[h : h + 1, queries.start :], delta[h : h + 1, queries.start :], False,
                 )
                 if queries.start:
-                    dqt_ref[hc, : queries.start] = dqt_in[hc, : queries.start]
-                dqt_ref[hc, queries] = dqt_in[hc, queries] + q_part
+                    before = jnp.zeros((HEAD, queries.start), F32)
+                    if dqt_in is not None:
+                        before = dqt_in[hc, : queries.start]
+                    dqt_ref[hc, : queries.start] = before
+                dqt_ref[hc, queries] = q_part if dqt_in is None else dqt_in[hc, queries] + q_part
                 dv = v_part if dv is None else dv + v_part
                 dk = k_part if dk is None else dk + k_part
             dkv_ref[keys, kc] = dk.astype(BF16)
@@ -230,25 +222,46 @@
         run(slice(0, rows), slice(half, rows))
 
 
-def query_kernel(tables_ref, dqt_ref, own_ref, a_ref, b_ref, out_ref, sum_ref):
-    sum_ref[...] = own_ref[...] + a_ref[...].astype(F32) + b_ref[...].astype(F32)
+def own_kernel(
+    tables_ref, k_ref, v_ref, qr_ref, do_ref, norm_ref, delta_ref, dqt_ref, back_ref,
+    out_ref, sum_ref,
+):
+    heads = qr_ref.shape[1] // HEAD
+    groups = k_ref.shape[1] // HEAD
+    size = heads // groups
     cosine_t = tables_ref[:HALF, :] * ROOT_SCALE
     sine_t = tables_ref[HALF:, :] * ROOT_SCALE
-    for h in range(out_ref.shape[1] // HEAD):
-        y1 = dqt_ref[pl.ds(h * HEAD, HALF), :]
-        y2 = dqt_ref[pl.ds(h * HEAD + HALF, HALF), :]
-        turned = jnp.concatenate(
-            [y1 * cosine_t + y2 * sine_t, y2 * cosine_t - y1 * sine_t], axis=0
-        )
-        out_ref[:, pl.ds(h * HEAD, HEAD)] = turned.T.astype(BF16)
-
-
-def final_kernel(tables_ref, own_ref, a_ref, dk_ref, dv_ref):
+    norm = norm_ref[...]
+    delta = delta_ref[...]
+    for g in range(groups):
+        kc = pl.ds(g * HEAD, HEAD)
+        vc = pl.ds((groups + g) * HEAD, HEAD)
+        dk = back_ref[:, kc].astype(F32)
+        dv = back_ref[:, vc].astype(F32)
+        for h in range(g * size, (g + 1) * size):
+            hc = pl.ds(h * HEAD, HEAD)
+            v_part, k_part, q_part = pair_part(
+                k_ref[:, kc], v_ref[:, kc], qr_ref[:, hc], do_ref[:, hc],
+                norm[h : h + 1], delta[h : h + 1], True,
+            )
+            dk = dk + k_part
+            dv = dv + v_part
+            total = dqt_ref[hc, :] + q_part
+            y1, y2 = total[:HALF], total[HALF:]
+            turned = jnp.concatenate(
+                [y1 * cosine_t + y2 * sine_t, y2 * cosine_t - y1 * sine_t], axis=0
+            )
+            out_ref[:, hc] = turned.T.astype(BF16)
+        sum_ref[:, kc] = dk
+        sum_ref[:, vc] = dv
+
+
+def final_kernel(tables_ref, own_ref, a_ref, b_ref, dk_ref, dv_ref):
     width = dk_ref.shape[1]
     wide, signed = row_tables(tables_ref[:HALF, :], tables_ref[HALF:, :])
     wide = wide * ROOT_SCALE
     signed = signed * -ROOT_SCALE
-    total = own_ref[...] + a_ref[...].astype(F32)
+    total = own_ref[...] + a_ref[...].astype(F32) + b_ref[...].astype(F32)
     for g in range(width // HEAD):
         cols = pl.ds(g * HEAD, HEAD)
         dk_ref[:, cols] = rotated(total[:, g * HEAD : (g + 1) * HEAD], wide, signed).astype(BF16)
@@ -302,45 +315,41 @@
     kr1, v1 = lax.optimization_barrier((kr, v1))
     k1 = shifted(kr1, -1)
     v3 = shifted(v1, -2)
-    kr2, v2 = lax.optimization_barrier((kr, v2))
-    k2 = shifted(kr2, -2)
-    qr, grad, norm, delta, dqt, dkv = call(
-        first_kernel,
-        [
-            ((rows, wide_q), BF16),
-            ((rows, wide_q), BF16),
-            ((heads, rows), F32),
-            ((heads, rows), F32),
-            ((wide_q, rows), F32),
-            ((rows, 2 * wide_k), F32),
-        ],
-        [VMEM] * 4 + [HBM] * 3,
+    k2 = shifted(kr, -2)
+    turned, v2 = lax.optimization_barrier((tables, v2))
+    groups = wide_k // HEAD
+    qr, grad, norm, delta = call(
+        functools.partial(prep_kernel, groups),
+        [((rows, wide_q), BF16)] * 2 + [((heads, rows), F32)] * 2,
+        [VMEM] + [HBM] * 4,
         [
             pltpu.VMEM((rows, wide_q), BF16),
             pltpu.VMEM((rows, wide_q), BF16),
-            pltpu.SemaphoreType.DMA((3 * (wide_k // HEAD),)),
+            pltpu.VMEM((heads, rows), F32),
+            pltpu.SemaphoreType.DMA((3 * groups + 1,)),
         ],
-    )(tables, kr, v_here, lse, q, do, at)
+    )(turned, lse, q, do, at)
     held, _ = lax.optimization_barrier((k1, delta))
     k3 = shifted(held, -2)
 
+    dqt = ()
     backs = []
     for step, key, value in ((1, k1, v1), (2, k2, v2), (3, k3, v3)):
-        dqt, part = call(
+        *dqt, part = call(
             functools.partial(hop_body, step),
             [((wide_q, rows), F32), ((rows, 2 * wide_k), BF16)],
-            [SMEM] * 2 + [VMEM] * 7,
-        )(slot, span_map, key, value, qr, grad, norm, delta, dqt)
+            [SMEM] * 2 + [VMEM] * (6 + len(dqt)),
+        )(slot, span_map, key, value, qr, grad, norm, delta, *dqt)
         backs.append(shifted(part, step))
     dq, dkv = call(
-        query_kernel, [((rows, wide_q), BF16), ((rows, 2 * wide_k), F32)], [VMEM] * 5
-    )(tables, dqt, dkv, backs[1], backs[0])
+        own_kernel, [((rows, wide_q), BF16), ((rows, 2 * wide_k), F32)], [VMEM] * 9
+    )(tables, kr, v_here, qr, grad, norm, delta, *dqt, backs[0])
 
     dk, dv = call(
         final_kernel,
         [((rows, wide_k), BF16), ((rows, wide_k), BF16)],
-        [VMEM] * 3,
-    )(tables, dkv, backs[2])
+        [VMEM] * 4,
+    )(tables, dkv, backs[1], backs[2])
     return dq, dk, dv
 
 

time: 52.8 us -> 52.8 us (level)
  waiting for transfers between devices: 17.8 us -> 16.6 us
  starting transfers between devices: 19 us -> 20.1 us
    ppermute x12, waiting for transfers between devices: 17.8 us -> 16.6 us  [shifted(): return lax.ppermute(value, axis, pairs)]
    ppermute x12, starting transfers between devices: 19 us -> 20.1 us  [shifted(): return lax.ppermute(value, axis, pairs)]
where the time goes in v8:
time: 52.8 us; the launch traced here: 52.6 us
  starting transfers between devices  20.1 us (38%)
  waiting for transfers between devices  16.6 us (31%)
  Pallas kernels  15.1 us (29%)
  between operations  0.68 us (1%)
    ppermute x12, starting transfers between devices, shifted(): return lax.ppermute(value, axis, pairs)  20.1 us
    ppermute x12, waiting for transfers between devices, shifted(): return lax.ppermute(value, axis, pairs)  16.6 us
    pallas_call x3, Pallas kernels, shards(): call(functools.partial(hop_body, step), [((wide_q, rows), F32), ((rows, 2...  6.89 us
    pallas_call x1, Pallas kernels, shards(): call(own_kernel, [((rows, wide_q), BF16), ((rows, 2 * wide_k), F32)], [VM...  4.29 us
    pallas_call x1, Pallas kernels, shards(): call(functools.partial(prep_kernel, groups), [((rows, wide_q), BF16)] * 2...  1.74 us
    pallas_call x1, Pallas kernels, shards(): call(key_kernel, [((rows, wide_k), BF16), ((HEAD, rows), F32)], [SMEM] +...  1.24 us
  transfers between devices with their start and end apart: 12, of which 5 were waited for; matrix products, arithmetic and copies ran while one was open for 0% of the time, Pallas kernels for 27%

profile of v8, /device:TPU:0, one launch (start us, length us, event | category | flops | bytes accessed | tf_op | source)
XLA Modules:
  0.0 52.6 jit_solution(9936943539347090164)
XLA Ops:
  0.6 6.1 %collective-permute-start.4 = (bf16[256,256]{1,0:T(8,128)(2,1)}, bf16[256,256]{1,0:T(8,128)(2,1)S(1)}, u32[]{:S(2)}, u32[]{:S(2)}) collective-permute-start(bf16[256,256]{1,0:T(8,128)(2,1)} %v_ref.1), channel_id=1, source_target_pairs={{0,28},{4,0},{8,4},{12,8},{16,12},{20,16},{24,20},{28,24},{1,29},{... | collective-permute-start | bytes 393224 | tf_op jit(solution)/shard_map/ppermute | solution.py:293
  6.7 1.5 %collective-permute-start.1 = (s32[3,64]{1,0:T(4,128)}, s32[3,64]{1,0:T(4,128)S(1)}, u32[]{:S(2)}, u32[]{:S(2)}) collective-permute-start(s32[3,64]{1,0:T(4,128)} %own_ref.1), channel_id=1, source_target_pairs={{0,2},{1,3},{2,0},{3,1},{4,6},{5,7},{6,4},{7,5},{8,10},{9,11},{10,... | collective-permute-start | bytes 2312 | tf_op jit(solution)/shard_map/ppermute | solution.py:293
  8.2 0.0 collective-permute-start
  8.2 1.7 %collective-permute-start.2 = (s32[3,64]{1,0:T(4,128)}, s32[3,64]{1,0:T(4,128)S(1)}, u32[]{:S(2)}, u32[]{:S(2)}) collective-permute-start(s32[3,64]{1,0:T(4,128)} %own_ref.1), channel_id=1, source_target_pairs={{0,3},{1,0},{2,1},{3,2},{4,7},{5,4},{6,5},{7,6},{8,11},{9,8},{10,9... | collective-permute-start | bytes 2312 | tf_op jit(solution)/shard_map/ppermute | solution.py:293
  9.9 0.4 collective-permute-start.3
  10.4 0.1 pad_add_fusion.slot_ref
  10.5 0.0 collective-permute-done.1.p2_ref
  10.5 0.9 %collective-permute-done.p1_ref = s32[3,64]{1,0:T(4,128)S(1)} collective-permute-done((s32[3,64]{1,0:T(4,128)}, s32[3,64]{1,0:T(4,128)S(1)}, u32[]{:S(2)}, u32[]{:S(2)}) %collective-permute-start) | collective-permute-done | bytes 800 | tf_op jit(solution)/shard_map/ppermute | solution.py:293
  11.4 0.0 collective-permute-done.2.p3_ref
  11.4 1.2 %shard_map.103 = (bf16[256,256]{1,0:T(8,128)(2,1)S(1)}, f32[128,256]{1,0:T(8,128)S(1)}) custom-call(s32[2]{0:T(128)S(1)} %pad_add_fusion.slot_ref, s32[3,64]{1,0:T(4,128)} %own_ref.1, s32[3,64]{1,0:T(4,128)S(1)} %collective-permute-done.p1_ref, s32[3,64]{1,0:T(4,128)S(1)} %collective-permute-done.1.p2_ref, s32[3,64]{1,0:T(4,128)S(1)} %collective-permute-done.2.p3_ref, ...), custom_call_target="tpu_custom_call" | custom-call | flops 1048576 | bytes 262144 | tf_op jit(solution)/shard_map/pallas_call | solution.py:310
  12.7 0.0 collective-permute-done.4.v_ref
  12.7 2.1 %collective-permute-start.5 = (bf16[256,256]{1,0:T(8,128)(2,1)S(1)}, bf16[256,256]{1,0:T(8,128)(2,1)S(1)}, u32[]{:S(2)}, u32[]{:S(2)}) collective-permute-start(bf16[256,256]{1,0:T(8,128)(2,1)S(1)} %get-tuple-element.31.k_ref), channel_id=1, source_target_pairs={{0,28},{4,0},{8,4},{12,8},{16,12},{20,16},{24,20},{28,24},{1,29},{... | collective-permute-start | bytes 393224 | tf_op jit(solution)/shard_map/ppermute | solution.py:293
  14.8 0.0 collective-permute-start.8
  14.8 1.0 %collective-permute-done.3.v_ref = bf16[256,256]{1,0:T(8,128)(2,1)S(1)} collective-permute-done((bf16[256,256]{1,0:T(8,128)(2,1)}, bf16[256,256]{1,0:T(8,128)(2,1)S(1)}, u32[]{:S(2)}, u32[]{:S(2)}) %collective-permute-start.3) | collective-permute-done | bytes 131104 | tf_op jit(solution)/shard_map/ppermute | solution.py:293
  15.9 1.5 %collective-permute-start.7 = (bf16[256,256]{1,0:T(8,128)(2,1)S(1)}, bf16[256,256]{1,0:T(8,128)(2,1)S(1)}, u32[]{:S(2)}, u32[]{:S(2)}) collective-permute-start(bf16[256,256]{1,0:T(8,128)(2,1)S(1)} %collective-permute-done.4.v_ref), channel_id=1, source_target_pairs={{0,24},{4,28},{8,0},{12,4},{16,8},{20,12},{24,16},{28,20},{1,25},{... | collective-permute-start | bytes 393224 | tf_op jit(solution)/shard_map/ppermute | solution.py:293
  17.4 1.7 %shard_map.104 = (bf16[256,1024]{1,0:T(8,128)(2,1)S(1)}, bf16[256,1024]{1,0:T(8,128)(2,1)S(1)}, f32[8,256]{1,0:T(8,128)S(1)}, f32[8,256]{1,0:T(8,128)S(1)}) custom-call(f32[128,256]{1,0:T(8,128)S(1)} %get-tuple-element.26.tables_ref, f32[8,256]{1,0:T(8,128)} %lse_hbm.1, bf16[256,1024]{1,0:T(8,128)(2,1)} %q_hbm.1, bf16[256,1024]{1,0:T(8,128)(2,1)} %do_hbm.1, ...), custom_call_target="tpu_custom_call" | custom-call | flops 1048576 | bytes 262144 | tf_op jit(solution)/shard_map/pallas_call | solution.py:321
  19.1 0.0 collective-permute-done.5.k_ref
  19.1 0.1 collective-permute-start.6
  19.2 2.3 %shard_map.105 = (f32[1024,256]{1,0:T(8,128)S(1)}, bf16[256,512]{1,0:T(8,128)(2,1)S(1)}) custom-call(s32[2]{0:T(128)S(1)} %pad_add_fusion.slot_ref, s32[8]{0:T(128)} %span_ref.5, bf16[256,256]{1,0:T(8,128)(2,1)S(1)} %collective-permute-done.5.k_ref, bf16[256,256]{1,0:T(8,128)(2,1)S(1)} %collective-permute-done.4.v_ref, ...), custom_call_target="tpu_custom_call" | custom-call | flops 1048576 | bytes 262144 | tf_op jit(solution)/shard_map/pallas_call | solution.py:338
  21.5 0.1 collective-permute-done.8.k_ref
  21.6 2.3 %shard_map.106 = (f32[1024,256]{1,0:T(8,128)S(1)}, bf16[256,512]{1,0:T(8,128)(2,1)S(1)}) custom-call(s32[2]{0:T(128)S(1)} %pad_add_fusion.slot_ref, s32[8]{0:T(128)} %span_ref.5, bf16[256,256]{1,0:T(8,128)(2,1)S(1)} %collective-permute-done.8.k_ref, bf16[256,256]{1,0:T(8,128)(2,1)S(1)} %collective-permute-done.3.v_ref, ...), custom_call_target="tpu_custom_call" | custom-call | flops 1048576 | bytes 262144 | tf_op jit(solution)/shard_map/pallas_call | solution.py:338
  23.9 1.9 %collective-permute-start.10 = (bf16[256,512]{1,0:T(8,128)(2,1)S(1)}, bf16[256,512]{1,0:T(8,128)(2,1)S(1)}, u32[]{:S(2)}, u32[]{:S(2)}) collective-permute-start(bf16[256,512]{1,0:T(8,128)(2,1)S(1)} %get-tuple-element.41), channel_id=1, source_target_pairs={{0,8},{4,12},{8,16},{12,20},{16,24},{20,28},{24,0},{28,4},{1,9},{5... | collective-permute-start | bytes 786440 | tf_op jit(solution)/shard_map/ppermute | solution.py:293
  25.8 3.4 %collective-permute-start.9 = (bf16[256,512]{1,0:T(8,128)(2,1)S(1)}, bf16[256,512]{1,0:T(8,128)(2,1)S(1)}, u32[]{:S(2)}, u32[]{:S(2)}) collective-permute-start(bf16[256,512]{1,0:T(8,128)(2,1)S(1)} %get-tuple-element.38), channel_id=1, source_target_pairs={{0,4},{4,8},{8,12},{12,16},{16,20},{20,24},{24,28},{28,0},{1,5},{5... | collective-permute-start | bytes 786440 | tf_op jit(solution)/shard_map/ppermute | solution.py:293
  29.2 0.0 collective-permute-done.7.v_ref
  29.2 0.0 collective-permute-done.6.k_ref
  29.2 2.3 %shard_map.107 = (f32[1024,256]{1,0:T(8,128)S(1)}, bf16[256,512]{1,0:T(8,128)(2,1)S(1)}) custom-call(s32[2]{0:T(128)S(1)} %pad_add_fusion.slot_ref, s32[8]{0:T(128)} %span_ref.5, bf16[256,256]{1,0:T(8,128)(2,1)S(1)} %collective-permute-done.6.k_ref, bf16[256,256]{1,0:T(8,128)(2,1)S(1)} %collective-permute-done.7.v_ref, ...), custom_call_target="tpu_custom_call" | custom-call | flops 1048576 | bytes 262144 | tf_op jit(solution)/shard_map/pallas_call | solution.py:338
  31.6 1.2 %collective-permute-start.11 = (bf16[256,512]{1,0:T(8,128)(2,1)S(1)}, bf16[256,512]{1,0:T(8,128)(2,1)S(1)}, u32[]{:S(2)}, u32[]{:S(2)}) collective-permute-start(bf16[256,512]{1,0:T(8,128)(2,1)S(1)} %get-tuple-element.42), channel_id=1, source_target_pairs={{0,12},{4,16},{8,20},{12,24},{16,28},{20,0},{24,4},{28,8},{1,13},{... | collective-permute-start | bytes 786440 | tf_op jit(solution)/shard_map/ppermute | solution.py:293
  32.8 10.5 %collective-permute-done.9.back_ref = bf16[256,512]{1,0:T(8,128)(2,1)S(1)} collective-permute-done((bf16[256,512]{1,0:T(8,128)(2,1)S(1)}, bf16[256,512]{1,0:T(8,128)(2,1)S(1)}, u32[]{:S(2)}, u32[]{:S(2)}) %collective-permute-start.9) | collective-permute-done | bytes 262176 | tf_op jit(solution)/shard_map/ppermute | solution.py:293
  43.3 4.3 %shard_map.108 = (bf16[256,1024]{1,0:T(8,128)(2,1)}, f32[256,512]{1,0:T(8,128)S(1)}) custom-call(f32[128,256]{1,0:T(8,128)S(1)} %get-tuple-element.26.tables_ref, bf16[256,256]{1,0:T(8,128)(2,1)S(1)} %get-tuple-element.31.k_ref, bf16[256,256]{1,0:T(8,128)(2,1)} %v_ref.1, bf16[256,1024]{1,0:T(8,128)(2,1)S(1)} %get-tuple-element.27.qr_ref, ...), custom_call_target="tpu_custom_call" | custom-call | flops 1048576 | bytes 262144 | tf_op jit(solution)/shard_map/pallas_call | solution.py:344
  47.6 0.0 collective-permute-done.10.a_ref
  47.6 4.0 %collective-permute-done.11.b_ref = bf16[256,512]{1,0:T(8,128)(2,1)S(1)} collective-permute-done((bf16[256,512]{1,0:T(8,128)(2,1)S(1)}, bf16[256,512]{1,0:T(8,128)(2,1)S(1)}, u32[]{:S(2)}, u32[]{:S(2)}) %collective-permute-start.11) | collective-permute-done | bytes 262176 | tf_op jit(solution)/shard_map/ppermute | solution.py:293
  51.6 1.0 %shard_map.109 = (bf16[256,256]{1,0:T(8,128)(2,1)}, bf16[256,256]{1,0:T(8,128)(2,1)}) custom-call(f32[128,256]{1,0:T(8,128)S(1)} %get-tuple-element.26.tables_ref, f32[256,512]{1,0:T(8,128)S(1)} %get-tuple-element.40.own_ref, bf16[256,512]{1,0:T(8,128)(2,1)S(1)} %collective-permute-done.10.a_ref, bf16[256,512]{1,0:T(8,128)(2,1)S(1)} %collective-permute-done.11.b_ref), custom_call_target="tpu_custom_call" | custom-call | flops 1048576 | bytes 262144 | tf_op jit(solution)/shard_map/pallas_call | solution.py:348
Async XLA Ops:
  0.6 12.1 %collective-permute-start.4 = (bf16[256,256]{1,0:T(8,128)(2,1)}, bf16[256,256]{1,0:T(8,128)(2,1)S(1)}, u32[]{:S(2)}, u32[]{:S(2)}) collective-permute-start(bf16[256,256]{1,0:T(8,128)(2,1)} %v_ref.1), channel_id=1, source_target_pairs={{0,28},{4,0},{8,4},{12,8},{16,12},{20,16},{24,20},{28,24},{1,29},{... | collective-permute-start | bytes 393224 | tf_op jit(solution)/shard_map/ppermute | solution.py:293
  6.7 3.8 %collective-permute-start.1 = (s32[3,64]{1,0:T(4,128)}, s32[3,64]{1,0:T(4,128)S(1)}, u32[]{:S(2)}, u32[]{:S(2)}) collective-permute-start(s32[3,64]{1,0:T(4,128)} %own_ref.1), channel_id=1, source_target_pairs={{0,2},{1,3},{2,0},{3,1},{4,6},{5,7},{6,4},{7,5},{8,10},{9,11},{10,... | collective-permute-start | bytes 2312 | tf_op jit(solution)/shard_map/ppermute | solution.py:293
  8.2 3.2 %collective-permute-start = (s32[3,64]{1,0:T(4,128)}, s32[3,64]{1,0:T(4,128)S(1)}, u32[]{:S(2)}, u32[]{:S(2)}) collective-permute-start(s32[3,64]{1,0:T(4,128)} %own_ref.1), channel_id=1, source_target_pairs={{0,1},{1,2},{2,3},{3,0},{4,5},{5,6},{6,7},{7,4},{8,9},{9,10},{10,1... | collective-permute-start | bytes 2312 | tf_op jit(solution)/shard_map/ppermute | solution.py:293
  8.2 3.3 %collective-permute-start.2 = (s32[3,64]{1,0:T(4,128)}, s32[3,64]{1,0:T(4,128)S(1)}, u32[]{:S(2)}, u32[]{:S(2)}) collective-permute-start(s32[3,64]{1,0:T(4,128)} %own_ref.1), channel_id=1, source_target_pairs={{0,3},{1,0},{2,1},{3,2},{4,7},{5,4},{6,5},{7,6},{8,11},{9,8},{10,9... | collective-permute-start | bytes 2312 | tf_op jit(solution)/shard_map/ppermute | solution.py:293
  9.9 5.9 %collective-permute-start.3 = (bf16[256,256]{1,0:T(8,128)(2,1)}, bf16[256,256]{1,0:T(8,128)(2,1)S(1)}, u32[]{:S(2)}, u32[]{:S(2)}) collective-permute-start(bf16[256,256]{1,0:T(8,128)(2,1)} %v_ref.1), channel_id=1, source_target_pairs={{0,24},{4,28},{8,0},{12,4},{16,8},{20,12},{24,16},{28,20},{1,25},{... | collective-permute-start | bytes 393224 | tf_op jit(solution)/shard_map/ppermute | solution.py:293
  12.7 6.4 %collective-permute-start.5 = (bf16[256,256]{1,0:T(8,128)(2,1)S(1)}, bf16[256,256]{1,0:T(8,128)(2,1)S(1)}, u32[]{:S(2)}, u32[]{:S(2)}) collective-permute-start(bf16[256,256]{1,0:T(8,128)(2,1)S(1)} %get-tuple-element.31.k_ref), channel_id=1, source_target_pairs={{0,28},{4,0},{8,4},{12,8},{16,12},{20,16},{24,20},{28,24},{1,29},{... | collective-permute-start | bytes 393224 | tf_op jit(solution)/shard_map/ppermute | solution.py:293
  14.8 6.8 %collective-permute-start.8 = (bf16[256,256]{1,0:T(8,128)(2,1)S(1)}, bf16[256,256]{1,0:T(8,128)(2,1)S(1)}, u32[]{:S(2)}, u32[]{:S(2)}) collective-permute-start(bf16[256,256]{1,0:T(8,128)(2,1)S(1)} %get-tuple-element.31.k_ref), channel_id=1, source_target_pairs={{0,24},{4,28},{8,0},{12,4},{16,8},{20,12},{24,16},{28,20},{1,25},{... | collective-permute-start | bytes 393224 | tf_op jit(solution)/shard_map/ppermute | solution.py:293
  15.9 13.4 %collective-permute-start.7 = (bf16[256,256]{1,0:T(8,128)(2,1)S(1)}, bf16[256,256]{1,0:T(8,128)(2,1)S(1)}, u32[]{:S(2)}, u32[]{:S(2)}) collective-permute-start(bf16[256,256]{1,0:T(8,128)(2,1)S(1)} %collective-permute-done.4.v_ref), channel_id=1, source_target_pairs={{0,24},{4,28},{8,0},{12,4},{16,8},{20,12},{24,16},{28,20},{1,25},{... | collective-permute-start | bytes 393224 | tf_op jit(solution)/shard_map/ppermute | solution.py:293
  19.1 10.1 %collective-permute-start.6 = (bf16[256,256]{1,0:T(8,128)(2,1)S(1)}, bf16[256,256]{1,0:T(8,128)(2,1)S(1)}, u32[]{:S(2)}, u32[]{:S(2)}) collective-permute-start(bf16[256,256]{1,0:T(8,128)(2,1)S(1)} %collective-permute-done.5.k_ref), channel_id=1, source_target_pairs={{0,24},{4,28},{8,0},{12,4},{16,8},{20,12},{24,16},{28,20},{1,25},{... | collective-permute-start | bytes 393224 | tf_op jit(solution)/shard_map/ppermute | solution.py:293
  23.9 23.7 %collective-permute-start.10 = (bf16[256,512]{1,0:T(8,128)(2,1)S(1)}, bf16[256,512]{1,0:T(8,128)(2,1)S(1)}, u32[]{:S(2)}, u32[]{:S(2)}) collective-permute-start(bf16[256,512]{1,0:T(8,128)(2,1)S(1)} %get-tuple-element.41), channel_id=1, source_target_pairs={{0,8},{4,12},{8,16},{12,20},{16,24},{20,28},{24,0},{28,4},{1,9},{5... | collective-permute-start | bytes 786440 | tf_op jit(solution)/shard_map/ppermute | solution.py:293
  25.8 17.4 %collective-permute-start.9 = (bf16[256,512]{1,0:T(8,128)(2,1)S(1)}, bf16[256,512]{1,0:T(8,128)(2,1)S(1)}, u32[]{:S(2)}, u32[]{:S(2)}) collective-permute-start(bf16[256,512]{1,0:T(8,128)(2,1)S(1)} %get-tuple-element.38), channel_id=1, source_target_pairs={{0,4},{4,8},{8,12},{12,16},{16,20},{20,24},{24,28},{28,0},{1,5},{5... | collective-permute-start | bytes 786440 | tf_op jit(solution)/shard_map/ppermute | solution.py:293
  31.6 20.1 %collective-permute-start.11 = (bf16[256,512]{1,0:T(8,128)(2,1)S(1)}, bf16[256,512]{1,0:T(8,128)(2,1)S(1)}, u32[]{:S(2)}, u32[]{:S(2)}) collective-permute-start(bf16[256,512]{1,0:T(8,128)(2,1)S(1)} %get-tuple-element.42), channel_id=1, source_target_pairs={{0,12},{4,16},{8,20},{12,24},{16,28},{20,0},{24,4},{28,8},{1,13},{... | collective-permute-start | bytes 786440 | tf_op jit(solution)/shard_map/ppermute | solution.py:293

commit v9 on v8

--- a/solution.py
+++ b/solution.py
@@ -223,9 +223,10 @@
 
 
 def own_kernel(
-    tables_ref, k_ref, v_ref, qr_ref, do_ref, norm_ref, delta_ref, dqt_ref, back_ref,
+    slot_ref, tables_ref, k_ref, v_ref, qr_ref, do_ref, norm_ref, delta_ref, dqt_ref, back_ref,
     out_ref, sum_ref,
 ):
+    odd = (slot_ref[0] & 1) == 1
     heads = qr_ref.shape[1] // HEAD
     groups = k_ref.shape[1] // HEAD
     size = heads // groups
@@ -236,8 +237,8 @@
     for g in range(groups):
         kc = pl.ds(g * HEAD, HEAD)
         vc = pl.ds((groups + g) * HEAD, HEAD)
-        dk = back_ref[:, kc].astype(F32)
-        dv = back_ref[:, vc].astype(F32)
+        dk = jnp.where(odd, back_ref[:, kc].astype(F32), 0.0)
+        dv = jnp.where(odd, back_ref[:, vc].astype(F32), 0.0)
         for h in range(g * size, (g + 1) * size):
             hc = pl.ds(h * HEAD, HEAD)
             v_part, k_part, q_part = pair_part(
@@ -256,12 +257,18 @@
         sum_ref[:, vc] = dv
 
 
-def final_kernel(tables_ref, own_ref, a_ref, b_ref, dk_ref, dv_ref):
+def add_kernel(slot_ref, two_ref, three_ref, swapped_ref, sum_ref):
+    even = (slot_ref[0] & 1) == 0
+    total = two_ref[...].astype(F32) + three_ref[...].astype(F32)
+    sum_ref[...] = (total + jnp.where(even, swapped_ref[...].astype(F32), 0.0)).astype(BF16)
+
+
+def final_kernel(tables_ref, own_ref, a_ref, dk_ref, dv_ref):
     width = dk_ref.shape[1]
     wide, signed = row_tables(tables_ref[:HALF, :], tables_ref[HALF:, :])
     wide = wide * ROOT_SCALE
     signed = signed * -ROOT_SCALE
-    total = own_ref[...] + a_ref[...].astype(F32) + b_ref[...].astype(F32)
+    total = own_ref[...] + a_ref[...].astype(F32)
     for g in range(width // HEAD):
         cols = pl.ds(g * HEAD, HEAD)
         dk_ref[:, cols] = rotated(total[:, g * HEAD : (g + 1) * HEAD], wide, signed).astype(BF16)
@@ -291,6 +298,11 @@
     count = lax.axis_size(axis)
     pairs = [(source, (source + steps) % count) for source in range(count)]
     return lax.ppermute(value, axis, pairs)
+
+
+def exchanged(value):
+    count = lax.axis_size("ctx")
+    return lax.ppermute(value, "ctx", [(source, source ^ 1) for source in range(count)])
 
 
 def shards(q, k, v, do, at, lse, positions, span_map):
@@ -333,23 +345,30 @@
     k3 = shifted(held, -2)
 
     dqt = ()
-    backs = []
+    parts = []
     for step, key, value in ((1, k1, v1), (2, k2, v2), (3, k3, v3)):
         *dqt, part = call(
             functools.partial(hop_body, step),
             [((wide_q, rows), F32), ((rows, 2 * wide_k), BF16)],
             [SMEM] * 2 + [VMEM] * (6 + len(dqt)),
         )(slot, span_map, key, value, qr, grad, norm, delta, *dqt)
-        backs.append(shifted(part, step))
+        parts.append(part)
+    swapped = exchanged(parts[0])
+    moved = shifted(parts[2], 1)
     dq, dkv = call(
-        own_kernel, [((rows, wide_q), BF16), ((rows, 2 * wide_k), F32)], [VMEM] * 9
-    )(tables, kr, v_here, qr, grad, norm, delta, *dqt, backs[0])
+        own_kernel, [((rows, wide_q), BF16), ((rows, 2 * wide_k), F32)], [SMEM] + [VMEM] * 9
+    )(slot, tables, kr, v_here, qr, grad, norm, delta, *dqt, swapped)
+    part2, _ = lax.optimization_barrier((parts[1], dkv))
+    (total,) = call(add_kernel, [((rows, 2 * wide_k), BF16)], [SMEM] + [VMEM] * 3)(
+        slot, part2, moved, swapped
+    )
+    home = shifted(total, 2)
 
     dk, dv = call(
         final_kernel,
         [((rows, wide_k), BF16), ((rows, wide_k), BF16)],
-        [VMEM] * 4,
-    )(tables, dkv, backs[1], backs[2])
+        [VMEM] * 3,
+    )(tables, dkv, home)
     return dq, dk, dv
 
 

time: 52.8 us -> 50.8 us (0.962)
  waiting for transfers between devices: 16.6 us -> 14.9 us
  starting transfers between devices: 20.1 us -> 19.2 us
  Pallas kernels: 15.1 us -> 15.7 us
    ppermute x12 -> x11, starting transfers between devices: 20.1 us -> 13.8 us  [shifted(): return lax.ppermute(value, axis, pairs)]
    ppermute x0 -> x1, starting transfers between devices: none -> 5.39 us  [exchanged(): lax.ppermute(value, 'ctx', [(source, source ^ 1) for source in range(coun...]
    ppermute x12 -> x11, waiting for transfers between devices: 16.6 us -> 13.4 us  [shifted(): return lax.ppermute(value, axis, pairs)]
    ppermute x0 -> x1, waiting for transfers between devices: none -> 1.52 us  [exchanged(): lax.ppermute(value, 'ctx', [(source, source ^ 1) for source in range(coun...]
    pallas_call x1 -> x2, Pallas kernels: 4.29 us -> 4.94 us  [the longest x1 4.28 us: shards(): call(own_kernel, [((rows, wide_q), BF16), ((rows, 2 * wide_k), F32)], [SM...]
  transfers between devices with their start and end apart: 12 -> 12, of which waited for: 5 -> 5; matrix products, arithmetic and copies ran while one was open for 0% -> 0% of each run, Pallas kernels for 27% -> 28%
where the time goes in v9:
time: 50.8 us; the launch traced here: 50.6 us
  starting transfers between devices  19.2 us (38%)
  Pallas kernels  15.7 us (31%)
  waiting for transfers between devices  14.9 us (29%)
  between operations  0.72 us (1%)
    ppermute x11, starting transfers between devices, shifted(): return lax.ppermute(value, axis, pairs)  13.8 us
    ppermute x11, waiting for transfers between devices, shifted(): return lax.ppermute(value, axis, pairs)  13.4 us
    pallas_call x3, Pallas kernels, shards(): call(functools.partial(hop_body, step), [((wide_q, rows), F32), ((rows, 2...  6.86 us
    ppermute x1, starting transfers between devices, exchanged(): lax.ppermute(value, 'ctx', [(source, source ^ 1) for source in range(coun...  5.39 us
    pallas_call x1, Pallas kernels, shards(): call(own_kernel, [((rows, wide_q), BF16), ((rows, 2 * wide_k), F32)], [SM...  4.28 us
    pallas_call x1, Pallas kernels, shards(): call(functools.partial(prep_kernel, groups), [((rows, wide_q), BF16)] * 2...  1.74 us
    ppermute x1, waiting for transfers between devices, exchanged(): lax.ppermute(value, 'ctx', [(source, source ^ 1) for source in range(coun...  1.52 us
    pallas_call x1, Pallas kernels, shards(): call(key_kernel, [((rows, wide_k), BF16), ((HEAD, rows), F32)], [SMEM] +...  1.24 us
  transfers between devices with their start and end apart: 12, of which 5 were waited for; matrix products, arithmetic and copies ran while one was open for 0% of the time, Pallas kernels for 28%

profile of v9, /device:TPU:0, one launch (start us, length us, event | category | flops | bytes accessed | tf_op | source)
XLA Modules:
  0.0 50.6 jit_solution(18019445085408009685)
XLA Ops:
  0.6 6.1 %collective-permute-start.4 = (bf16[256,256]{1,0:T(8,128)(2,1)}, bf16[256,256]{1,0:T(8,128)(2,1)S(1)}, u32[]{:S(2)}, u32[]{:S(2)}) collective-permute-start(bf16[256,256]{1,0:T(8,128)(2,1)} %v_ref.1), channel_id=1, source_target_pairs={{0,28},{4,0},{8,4},{12,8},{16,12},{20,16},{24,20},{28,24},{1,29},{... | collective-permute-start | bytes 393224 | tf_op jit(solution)/shard_map/ppermute | solution.py:300
  6.7 1.5 %collective-permute-start.1 = (s32[3,64]{1,0:T(4,128)}, s32[3,64]{1,0:T(4,128)S(1)}, u32[]{:S(2)}, u32[]{:S(2)}) collective-permute-start(s32[3,64]{1,0:T(4,128)} %own_ref.1), channel_id=1, source_target_pairs={{0,2},{1,3},{2,0},{3,1},{4,6},{5,7},{6,4},{7,5},{8,10},{9,11},{10,... | collective-permute-start | bytes 2312 | tf_op jit(solution)/shard_map/ppermute | solution.py:300
  8.2 0.0 collective-permute-start
  8.2 1.7 %collective-permute-start.2 = (s32[3,64]{1,0:T(4,128)}, s32[3,64]{1,0:T(4,128)S(1)}, u32[]{:S(2)}, u32[]{:S(2)}) collective-permute-start(s32[3,64]{1,0:T(4,128)} %own_ref.1), channel_id=1, source_target_pairs={{0,3},{1,0},{2,1},{3,2},{4,7},{5,4},{6,5},{7,6},{8,11},{9,8},{10,9... | collective-permute-start | bytes 2312 | tf_op jit(solution)/shard_map/ppermute | solution.py:300
  9.9 0.4 collective-permute-start.3
  10.4 0.1 pad_add_fusion.slot_ref
  10.5 0.0 collective-permute-done.1.p2_ref
  10.5 0.9 %collective-permute-done.p1_ref = s32[3,64]{1,0:T(4,128)S(1)} collective-permute-done((s32[3,64]{1,0:T(4,128)}, s32[3,64]{1,0:T(4,128)S(1)}, u32[]{:S(2)}, u32[]{:S(2)}) %collective-permute-start) | collective-permute-done | bytes 800 | tf_op jit(solution)/shard_map/ppermute | solution.py:300
  11.4 0.0 collective-permute-done.2.p3_ref
  11.4 1.2 %shard_map.103 = (bf16[256,256]{1,0:T(8,128)(2,1)S(1)}, f32[128,256]{1,0:T(8,128)S(1)}) custom-call(s32[2]{0:T(128)S(1)} %pad_add_fusion.slot_ref, s32[3,64]{1,0:T(4,128)} %own_ref.1, s32[3,64]{1,0:T(4,128)S(1)} %collective-permute-done.p1_ref, s32[3,64]{1,0:T(4,128)S(1)} %collective-permute-done.1.p2_ref, s32[3,64]{1,0:T(4,128)S(1)} %collective-permute-done.2.p3_ref, ...), custom_call_target="tpu_custom_call" | custom-call | flops 1048576 | bytes 262144 | tf_op jit(solution)/shard_map/pallas_call | solution.py:322
  12.7 0.0 collective-permute-done.4.v_ref
  12.7 2.1 %collective-permute-start.5 = (bf16[256,256]{1,0:T(8,128)(2,1)S(1)}, bf16[256,256]{1,0:T(8,128)(2,1)S(1)}, u32[]{:S(2)}, u32[]{:S(2)}) collective-permute-start(bf16[256,256]{1,0:T(8,128)(2,1)S(1)} %get-tuple-element.32.k_ref), channel_id=1, source_target_pairs={{0,28},{4,0},{8,4},{12,8},{16,12},{20,16},{24,20},{28,24},{1,29},{... | collective-permute-start | bytes 393224 | tf_op jit(solution)/shard_map/ppermute | solution.py:300
  14.8 0.0 collective-permute-start.8
  14.8 1.0 %collective-permute-done.3.v_ref = bf16[256,256]{1,0:T(8,128)(2,1)S(1)} collective-permute-done((bf16[256,256]{1,0:T(8,128)(2,1)}, bf16[256,256]{1,0:T(8,128)(2,1)S(1)}, u32[]{:S(2)}, u32[]{:S(2)}) %collective-permute-start.3) | collective-permute-done | bytes 131104 | tf_op jit(solution)/shard_map/ppermute | solution.py:300
  15.9 1.5 %collective-permute-start.7 = (bf16[256,256]{1,0:T(8,128)(2,1)S(1)}, bf16[256,256]{1,0:T(8,128)(2,1)S(1)}, u32[]{:S(2)}, u32[]{:S(2)}) collective-permute-start(bf16[256,256]{1,0:T(8,128)(2,1)S(1)} %collective-permute-done.4.v_ref), channel_id=1, source_target_pairs={{0,24},{4,28},{8,0},{12,4},{16,8},{20,12},{24,16},{28,20},{1,25},{... | collective-permute-start | bytes 393224 | tf_op jit(solution)/shard_map/ppermute | solution.py:300
  17.4 1.7 %shard_map.104 = (bf16[256,1024]{1,0:T(8,128)(2,1)S(1)}, bf16[256,1024]{1,0:T(8,128)(2,1)S(1)}, f32[8,256]{1,0:T(8,128)S(1)}, f32[8,256]{1,0:T(8,128)S(1)}) custom-call(f32[128,256]{1,0:T(8,128)S(1)} %get-tuple-element.27.tables_ref, f32[8,256]{1,0:T(8,128)} %lse_hbm.1, bf16[256,1024]{1,0:T(8,128)(2,1)} %q_hbm.1, bf16[256,1024]{1,0:T(8,128)(2,1)} %do_hbm.1, ...), custom_call_target="tpu_custom_call" | custom-call | flops 1048576 | bytes 262144 | tf_op jit(solution)/shard_map/pallas_call | solution.py:333
  19.1 0.1 collective-permute-start.6
  19.2 2.3 %shard_map.105 = (f32[1024,256]{1,0:T(8,128)S(1)}, bf16[256,512]{1,0:T(8,128)(2,1)S(1)}) custom-call(s32[2]{0:T(128)S(1)} %pad_add_fusion.slot_ref, s32[8]{0:T(128)} %span_ref.5, bf16[256,256]{1,0:T(8,128)(2,1)S(1)} %collective-permute-done.5.k_ref, bf16[256,256]{1,0:T(8,128)(2,1)S(1)} %collective-permute-done.4.v_ref, ...), custom_call_target="tpu_custom_call" | custom-call | flops 1048576 | bytes 262144 | tf_op jit(solution)/shard_map/pallas_call | solution.py:350
  21.5 5.4 %collective-permute-start.9 = (bf16[256,512]{1,0:T(8,128)(2,1)S(1)}, bf16[256,512]{1,0:T(8,128)(2,1)S(1)}, u32[]{:S(2)}, u32[]{:S(2)}) collective-permute-start(bf16[256,512]{1,0:T(8,128)(2,1)S(1)} %get-tuple-element.39), channel_id=1, source_target_pairs={{0,4},{4,0},{8,12},{12,8},{16,20},{20,16},{24,28},{28,24},{1,5},{5... | collective-permute-start | bytes 786440 | tf_op jit(solution)/shard_map/ppermute | solution.py:305
  26.9 0.0 collective-permute-done.8.k_ref
  26.9 2.3 %shard_map.106 = (f32[1024,256]{1,0:T(8,128)S(1)}, bf16[256,512]{1,0:T(8,128)(2,1)S(1)}) custom-call(s32[2]{0:T(128)S(1)} %pad_add_fusion.slot_ref, s32[8]{0:T(128)} %span_ref.5, bf16[256,256]{1,0:T(8,128)(2,1)S(1)} %collective-permute-done.8.k_ref, bf16[256,256]{1,0:T(8,128)(2,1)S(1)} %collective-permute-done.3.v_ref, ...), custom_call_target="tpu_custom_call" | custom-call | flops 1048576 | bytes 262144 | tf_op jit(solution)/shard_map/pallas_call | solution.py:350
  29.2 0.0 collective-permute-done.7.v_ref
  29.2 0.0 collective-permute-done.6.k_ref
  29.2 2.3 %shard_map.107 = (f32[1024,256]{1,0:T(8,128)S(1)}, bf16[256,512]{1,0:T(8,128)(2,1)S(1)}) custom-call(s32[2]{0:T(128)S(1)} %pad_add_fusion.slot_ref, s32[8]{0:T(128)} %span_ref.5, bf16[256,256]{1,0:T(8,128)(2,1)S(1)} %collective-permute-done.6.k_ref, bf16[256,256]{1,0:T(8,128)(2,1)S(1)} %collective-permute-done.7.v_ref, ...), custom_call_target="tpu_custom_call" | custom-call | flops 1048576 | bytes 262144 | tf_op jit(solution)/shard_map/pallas_call | solution.py:350
  31.5 0.3 collective-permute-start.10
  31.8 1.5 %collective-permute-done.9.back_ref.swapped_ref = bf16[256,512]{1,0:T(8,128)(2,1)S(1)} collective-permute-done((bf16[256,512]{1,0:T(8,128)(2,1)S(1)}, bf16[256,512]{1,0:T(8,128)(2,1)S(1)}, u32[]{:S(2)}, u32[]{:S(2)}) %collective-permute-start.9) | collective-permute-done | bytes 262176 | tf_op jit(solution)/shard_map/ppermute | solution.py:305
  33.3 4.3 %shard_map.108 = (bf16[256,1024]{1,0:T(8,128)(2,1)}, f32[256,512]{1,0:T(8,128)S(1)}) custom-call(s32[2]{0:T(128)S(1)} %pad_add_fusion.slot_ref, f32[128,256]{1,0:T(8,128)S(1)} %get-tuple-element.27.tables_ref, bf16[256,256]{1,0:T(8,128)(2,1)S(1)} %get-tuple-element.32.k_ref, bf16[256,256]{1,0:T(8,128)(2,1)} %v_ref.1, ...), custom_call_target="tpu_custom_call" | custom-call | flops 1048576 | bytes 262144 | tf_op jit(solution)/shard_map/pallas_call | solution.py:358
  37.6 3.2 %collective-permute-done.10.three_ref = bf16[256,512]{1,0:T(8,128)(2,1)S(1)} collective-permute-done((bf16[256,512]{1,0:T(8,128)(2,1)S(1)}, bf16[256,512]{1,0:T(8,128)(2,1)S(1)}, u32[]{:S(2)}, u32[]{:S(2)}) %collective-permute-start.10) | collective-permute-done | bytes 262176 | tf_op jit(solution)/shard_map/ppermute | solution.py:300
  40.8 0.7 %shard_map.109 = bf16[256,512]{1,0:T(8,128)(2,1)S(1)} custom-call(s32[2]{0:T(128)S(1)} %pad_add_fusion.slot_ref, bf16[256,512]{1,0:T(8,128)(2,1)S(1)} %get-tuple-element.43.two_ref, bf16[256,512]{1,0:T(8,128)(2,1)S(1)} %collective-permute-done.10.three_ref, bf16[256,512]{1,0:T(8,128)(2,1)S(1)} %collective-permute-done.9.back_ref.swapped_ref), custom_call_target="tpu_custom_call" | custom-call | flops 1048576 | bytes 262144 | tf_op jit(solution)/shard_map/pallas_call | solution.py:362
  41.5 0.1 collective-permute-start.11
  41.5 8.2 %collective-permute-done.11.a_ref = bf16[256,512]{1,0:T(8,128)(2,1)S(1)} collective-permute-done((bf16[256,512]{1,0:T(8,128)(2,1)S(1)}, bf16[256,512]{1,0:T(8,128)(2,1)S(1)}, u32[]{:S(2)}, u32[]{:S(2)}) %collective-permute-start.11) | collective-permute-done | bytes 262176 | tf_op jit(solution)/shard_map/ppermute | solution.py:300
  49.7 0.9 %shard_map.110 = (bf16[256,256]{1,0:T(8,128)(2,1)}, bf16[256,256]{1,0:T(8,128)(2,1)}) custom-call(f32[128,256]{1,0:T(8,128)S(1)} %get-tuple-element.27.tables_ref, f32[256,512]{1,0:T(8,128)S(1)} %get-tuple-element.41.own_ref, bf16[256,512]{1,0:T(8,128)(2,1)S(1)} %collective-permute-done.11.a_ref), custom_call_target="tpu_custom_call" | custom-call | flops 1048576 | bytes 262144 | tf_op jit(solution)/shard_map/pallas_call | solution.py:367
  (1 shorter events, 0.0 us)
Async XLA Ops:
  0.6 12.1 %collective-permute-start.4 = (bf16[256,256]{1,0:T(8,128)(2,1)}, bf16[256,256]{1,0:T(8,128)(2,1)S(1)}, u32[]{:S(2)}, u32[]{:S(2)}) collective-permute-start(bf16[256,256]{1,0:T(8,128)(2,1)} %v_ref.1), channel_id=1, source_target_pairs={{0,28},{4,0},{8,4},{12,8},{16,12},{20,16},{24,20},{28,24},{1,29},{... | collective-permute-start | bytes 393224 | tf_op jit(solution)/shard_map/ppermute | solution.py:300
  6.7 3.8 %collective-permute-start.1 = (s32[3,64]{1,0:T(4,128)}, s32[3,64]{1,0:T(4,128)S(1)}, u32[]{:S(2)}, u32[]{:S(2)}) collective-permute-start(s32[3,64]{1,0:T(4,128)} %own_ref.1), channel_id=1, source_target_pairs={{0,2},{1,3},{2,0},{3,1},{4,6},{5,7},{6,4},{7,5},{8,10},{9,11},{10,... | collective-permute-start | bytes 2312 | tf_op jit(solution)/shard_map/ppermute | solution.py:300
  8.2 3.2 %collective-permute-start = (s32[3,64]{1,0:T(4,128)}, s32[3,64]{1,0:T(4,128)S(1)}, u32[]{:S(2)}, u32[]{:S(2)}) collective-permute-start(s32[3,64]{1,0:T(4,128)} %own_ref.1), channel_id=1, source_target_pairs={{0,1},{1,2},{2,3},{3,0},{4,5},{5,6},{6,7},{7,4},{8,9},{9,10},{10,1... | collective-permute-start | bytes 2312 | tf_op jit(solution)/shard_map/ppermute | solution.py:300
  8.2 3.3 %collective-permute-start.2 = (s32[3,64]{1,0:T(4,128)}, s32[3,64]{1,0:T(4,128)S(1)}, u32[]{:S(2)}, u32[]{:S(2)}) collective-permute-start(s32[3,64]{1,0:T(4,128)} %own_ref.1), channel_id=1, source_target_pairs={{0,3},{1,0},{2,1},{3,2},{4,7},{5,4},{6,5},{7,6},{8,11},{9,8},{10,9... | collective-permute-start | bytes 2312 | tf_op jit(solution)/shard_map/ppermute | solution.py:300
  9.9 5.9 %collective-permute-start.3 = (bf16[256,256]{1,0:T(8,128)(2,1)}, bf16[256,256]{1,0:T(8,128)(2,1)S(1)}, u32[]{:S(2)}, u32[]{:S(2)}) collective-permute-start(bf16[256,256]{1,0:T(8,128)(2,1)} %v_ref.1), channel_id=1, source_target_pairs={{0,24},{4,28},{8,0},{12,4},{16,8},{20,12},{24,16},{28,20},{1,25},{... | collective-permute-start | bytes 393224 | tf_op jit(solution)/shard_map/ppermute | solution.py:300
  12.7 6.4 %collective-permute-start.5 = (bf16[256,256]{1,0:T(8,128)(2,1)S(1)}, bf16[256,256]{1,0:T(8,128)(2,1)S(1)}, u32[]{:S(2)}, u32[]{:S(2)}) collective-permute-start(bf16[256,256]{1,0:T(8,128)(2,1)S(1)} %get-tuple-element.32.k_ref), channel_id=1, source_target_pairs={{0,28},{4,0},{8,4},{12,8},{16,12},{20,16},{24,20},{28,24},{1,29},{... | collective-permute-start | bytes 393224 | tf_op jit(solution)/shard_map/ppermute | solution.py:300
  14.8 12.1 %collective-permute-start.8 = (bf16[256,256]{1,0:T(8,128)(2,1)S(1)}, bf16[256,256]{1,0:T(8,128)(2,1)S(1)}, u32[]{:S(2)}, u32[]{:S(2)}) collective-permute-start(bf16[256,256]{1,0:T(8,128)(2,1)S(1)} %get-tuple-element.32.k_ref), channel_id=1, source_target_pairs={{0,24},{4,28},{8,0},{12,4},{16,8},{20,12},{24,16},{28,20},{1,25},{... | collective-permute-start | bytes 393224 | tf_op jit(solution)/shard_map/ppermute | solution.py:300
  15.9 13.3 %collective-permute-start.7 = (bf16[256,256]{1,0:T(8,128)(2,1)S(1)}, bf16[256,256]{1,0:T(8,128)(2,1)S(1)}, u32[]{:S(2)}, u32[]{:S(2)}) collective-permute-start(bf16[256,256]{1,0:T(8,128)(2,1)S(1)} %collective-permute-done.4.v_ref), channel_id=1, source_target_pairs={{0,24},{4,28},{8,0},{12,4},{16,8},{20,12},{24,16},{28,20},{1,25},{... | collective-permute-start | bytes 393224 | tf_op jit(solution)/shard_map/ppermute | solution.py:300
  19.1 10.1 %collective-permute-start.6 = (bf16[256,256]{1,0:T(8,128)(2,1)S(1)}, bf16[256,256]{1,0:T(8,128)(2,1)S(1)}, u32[]{:S(2)}, u32[]{:S(2)}) collective-permute-start(bf16[256,256]{1,0:T(8,128)(2,1)S(1)} %collective-permute-done.5.k_ref), channel_id=1, source_target_pairs={{0,24},{4,28},{8,0},{12,4},{16,8},{20,12},{24,16},{28,20},{1,25},{... | collective-permute-start | bytes 393224 | tf_op jit(solution)/shard_map/ppermute | solution.py:300
  21.5 11.8 %collective-permute-start.9 = (bf16[256,512]{1,0:T(8,128)(2,1)S(1)}, bf16[256,512]{1,0:T(8,128)(2,1)S(1)}, u32[]{:S(2)}, u32[]{:S(2)}) collective-permute-start(bf16[256,512]{1,0:T(8,128)(2,1)S(1)} %get-tuple-element.39), channel_id=1, source_target_pairs={{0,4},{4,0},{8,12},{12,8},{16,20},{20,16},{24,28},{28,24},{1,5},{5... | collective-permute-start | bytes 786440 | tf_op jit(solution)/shard_map/ppermute | solution.py:305
  31.5 9.3 %collective-permute-start.10 = (bf16[256,512]{1,0:T(8,128)(2,1)S(1)}, bf16[256,512]{1,0:T(8,128)(2,1)S(1)}, u32[]{:S(2)}, u32[]{:S(2)}) collective-permute-start(bf16[256,512]{1,0:T(8,128)(2,1)S(1)} %get-tuple-element.44), channel_id=1, source_target_pairs={{0,4},{4,8},{8,12},{12,16},{16,20},{20,24},{24,28},{28,0},{1,5},{5... | collective-permute-start | bytes 786440 | tf_op jit(solution)/shard_map/ppermute | solution.py:300
  41.5 8.2 %collective-permute-start.11 = (bf16[256,512]{1,0:T(8,128)(2,1)S(1)}, bf16[256,512]{1,0:T(8,128)(2,1)S(1)}, u32[]{:S(2)}, u32[]{:S(2)}) collective-permute-start(bf16[256,512]{1,0:T(8,128)(2,1)S(1)} %shard_map.109), channel_id=1, source_target_pairs={{0,8},{4,12},{8,16},{12,20},{16,24},{20,28},{24,0},{28,4},{1,9},{5... | collective-permute-start | bytes 786440 | tf_op jit(solution)/shard_map/ppermute | solution.py:300

commit v10 on v8

--- a/solution.py
+++ b/solution.py
@@ -118,7 +118,7 @@
     return value_part, key_part, query_part
 
 
-def key_kernel(slot_ref, own_ref, p1_ref, p2_ref, p3_ref, k_ref, kr_ref, tables_ref):
+def key_kernel(slot_ref, own_ref, p1_ref, p2_ref, p3_ref, k_ref, v_ref, kr_ref, kv_ref, tables_ref):
     pieces = (own_ref[...], p1_ref[...], p2_ref[...], p3_ref[...])
     count = len(pieces)
     head = slot_ref[1]
@@ -135,7 +135,10 @@
     wide, signed = row_tables(cosine_t, sine_t)
     for g in range(k_ref.shape[1] // HEAD):
         cols = pl.ds(g * HEAD, HEAD)
-        kr_ref[:, cols] = rotated(k_ref[:, cols].astype(F32), wide, signed).astype(BF16)
+        key = rotated(k_ref[:, cols].astype(F32), wide, signed).astype(BF16)
+        kr_ref[:, cols] = key
+        kv_ref[:, cols] = key
+    kv_ref[:, k_ref.shape[1] :] = v_ref[...]
 
 
 def prep_kernel(
@@ -173,11 +176,11 @@
     norm_ref[...] = lse_ref[...] * LOG2E
 
 
-def hop_body(
-    step, slot_ref, span_ref, k_ref, v_ref, qr_ref, do_ref, norm_ref, delta_ref, *refs
-):
-    dqt_ref, dkv_ref = refs[-2:]
-    dqt_in = refs[0] if len(refs) > 2 else None
+def hop_kernel(step, wanted, started, slot_ref, span_ref, k_ref, v_ref, *refs):
+    qr_ref, do_ref, norm_ref, delta_ref = refs[:4]
+    count = len(wanted)
+    dqt_ins = refs[4 : 4 + count] if started else [None] * count
+    dqt_refs, part_ref = refs[-count - 1 : -1], refs[-1]
     rows = qr_ref.shape[0]
     half = rows // 2
     heads = qr_ref.shape[1] // HEAD
@@ -190,12 +193,13 @@
     delta = delta_ref[...]
 
     def run(keys, queries):
-        for g in range(groups):
+        for i, (g, dqt_in, dqt_ref) in enumerate(zip(wanted, dqt_ins, dqt_refs)):
             kc = pl.ds(g * HEAD, HEAD)
-            vc = pl.ds((groups + g) * HEAD, HEAD)
             dk = dv = None
-            for h in range(g * size, (g + 1) * size):
+            for j in range(size):
+                h = g * size + j
                 hc = pl.ds(h * HEAD, HEAD)
+                to = pl.ds(j * HEAD, HEAD)
                 v_part, k_part, q_part = pair_part(
                     k_ref[keys, kc], v_ref[keys, kc], qr_ref[queries, hc], do_ref[queries, hc],
                     norm[h : h + 1, queries.start :], delta[h : h + 1, queries.start :], False,
@@ -203,15 +207,15 @@
                 if queries.start:
                     before = jnp.zeros((HEAD, queries.start), F32)
                     if dqt_in is not None:
-                        before = dqt_in[hc, : queries.start]
-                    dqt_ref[hc, : queries.start] = before
-                dqt_ref[hc, queries] = q_part if dqt_in is None else dqt_in[hc, queries] + q_part
+                        before = dqt_in[to, : queries.start]
+                    dqt_ref[to, : queries.start] = before
+                dqt_ref[to, queries] = q_part if dqt_in is None else dqt_in[to, queries] + q_part
                 dv = v_part if dv is None else dv + v_part
                 dk = k_part if dk is None else dk + k_part
-            dkv_ref[keys, kc] = dk.astype(BF16)
-            dkv_ref[keys, vc] = dv.astype(BF16)
+            part_ref[keys, pl.ds(2 * i * HEAD, HEAD)] = dk.astype(BF16)
+            part_ref[keys, pl.ds((2 * i + 1) * HEAD, HEAD)] = dv.astype(BF16)
         if keys.stop < rows:
-            dkv_ref[keys.stop :, :] = jnp.zeros((rows - keys.stop, dkv_ref.shape[1]), BF16)
+            part_ref[keys.stop :, :] = jnp.zeros((rows - keys.stop, part_ref.shape[1]), BF16)
 
     @pl.when(earlier)
     def _():
@@ -222,50 +226,71 @@
         run(slice(0, rows), slice(half, rows))
 
 
-def own_kernel(
-    tables_ref, k_ref, v_ref, qr_ref, do_ref, norm_ref, delta_ref, dqt_ref, back_ref,
-    out_ref, sum_ref,
-):
-    heads = qr_ref.shape[1] // HEAD
-    groups = k_ref.shape[1] // HEAD
-    size = heads // groups
-    cosine_t = tables_ref[:HALF, :] * ROOT_SCALE
-    sine_t = tables_ref[HALF:, :] * ROOT_SCALE
+def merged_kernel(step, wanted, started, slot_ref, span_ref, kv_ref, *refs):
+    width = kv_ref.shape[1] // 2
+    hop_kernel(
+        step, wanted, started, slot_ref, span_ref, kv_ref.at[:, :width], kv_ref.at[:, width:],
+        *refs,
+    )
+
+
+def own_kernel(groups, k_ref, v_ref, qr_ref, do_ref, norm_ref, delta_ref, *refs):
+    dqt_ins, dqt_refs, part_ref = refs[:groups], refs[groups : 2 * groups], refs[2 * groups]
+    size = qr_ref.shape[1] // HEAD // groups
     norm = norm_ref[...]
     delta = delta_ref[...]
     for g in range(groups):
         kc = pl.ds(g * HEAD, HEAD)
-        vc = pl.ds((groups + g) * HEAD, HEAD)
-        dk = back_ref[:, kc].astype(F32)
-        dv = back_ref[:, vc].astype(F32)
-        for h in range(g * size, (g + 1) * size):
+        dk = dv = None
+        for j in range(size):
+            h = g * size + j
             hc = pl.ds(h * HEAD, HEAD)
+            to = pl.ds(j * HEAD, HEAD)
             v_part, k_part, q_part = pair_part(
                 k_ref[:, kc], v_ref[:, kc], qr_ref[:, hc], do_ref[:, hc],
                 norm[h : h + 1], delta[h : h + 1], True,
             )
-            dk = dk + k_part
-            dv = dv + v_part
-            total = dqt_ref[hc, :] + q_part
-            y1, y2 = total[:HALF], total[HALF:]
+            dqt_refs[g][to, :] = dqt_ins[g][to, :] + q_part
+            dv = v_part if dv is None else dv + v_part
+            dk = k_part if dk is None else dk + k_part
+        part_ref[:, pl.ds(2 * g * HEAD, HEAD)] = dk
+        part_ref[:, pl.ds((2 * g + 1) * HEAD, HEAD)] = dv
+
+
+def query_kernel(groups, slot_ref, tables_ref, own_ref, swapped_ref, *refs):
+    dqt_refs, out_ref, sum_ref = refs[:groups], refs[groups], refs[groups + 1]
+    odd = (slot_ref[0] & 1) == 1
+    sum_ref[...] = own_ref[...] + jnp.where(odd, swapped_ref[...].astype(F32), 0.0)
+    cosine_t = tables_ref[:HALF, :] * ROOT_SCALE
+    sine_t = tables_ref[HALF:, :] * ROOT_SCALE
+    size = dqt_refs[0].shape[0] // HEAD
+    for g in range(groups):
+        for j in range(size):
+            y1 = dqt_refs[g][pl.ds(j * HEAD, HALF), :]
+            y2 = dqt_refs[g][pl.ds(j * HEAD + HALF, HALF), :]
             turned = jnp.concatenate(
                 [y1 * cosine_t + y2 * sine_t, y2 * cosine_t - y1 * sine_t], axis=0
             )
-            out_ref[:, hc] = turned.T.astype(BF16)
-        sum_ref[:, kc] = dk
-        sum_ref[:, vc] = dv
-
-
-def final_kernel(tables_ref, own_ref, a_ref, b_ref, dk_ref, dv_ref):
-    width = dk_ref.shape[1]
+            out_ref[:, pl.ds((g * size + j) * HEAD, HEAD)] = turned.T.astype(BF16)
+
+
+def add_kernel(g, slot_ref, two_ref, swapped_ref, three_ref, sum_ref):
+    even = (slot_ref[0] & 1) == 0
+    cols = pl.ds(2 * g * HEAD, 2 * HEAD)
+    total = two_ref[:, cols].astype(F32) + three_ref[...].astype(F32)
+    sum_ref[...] = (total + jnp.where(even, swapped_ref[:, cols].astype(F32), 0.0)).astype(BF16)
+
+
+def final_kernel(groups, tables_ref, own_ref, *refs):
+    dk_ref, dv_ref = refs[groups:]
     wide, signed = row_tables(tables_ref[:HALF, :], tables_ref[HALF:, :])
     wide = wide * ROOT_SCALE
     signed = signed * -ROOT_SCALE
-    total = own_ref[...] + a_ref[...].astype(F32) + b_ref[...].astype(F32)
-    for g in range(width // HEAD):
+    for g in range(groups):
         cols = pl.ds(g * HEAD, HEAD)
-        dk_ref[:, cols] = rotated(total[:, g * HEAD : (g + 1) * HEAD], wide, signed).astype(BF16)
-    dv_ref[...] = total[:, width:].astype(BF16)
+        total = own_ref[:, pl.ds(2 * g * HEAD, 2 * HEAD)] + refs[g][...].astype(F32)
+        dk_ref[:, cols] = rotated(total[:, :HEAD], wide, signed).astype(BF16)
+        dv_ref[:, cols] = total[:, HEAD:].astype(BF16)
 
 
 SMEM = pl.BlockSpec(memory_space=pltpu.SMEM)
@@ -293,6 +318,11 @@
     return lax.ppermute(value, axis, pairs)
 
 
+def exchanged(value):
+    count = lax.axis_size("ctx")
+    return lax.ppermute(value, "ctx", [(source, source ^ 1) for source in range(count)])
+
+
 def shards(q, k, v, do, at, lse, positions, span_map):
     rows = q.shape[0]
     wide_q = q.shape[1]
@@ -305,19 +335,16 @@
     )
 
     pieces = [own] + [shifted(positions, r, "head") for r in (1, 2, 3)]
+    groups = wide_k // HEAD
+    every = tuple(range(groups))
+
     v1 = shifted(v, -1)
-    v2 = shifted(v, -2)
-    kr, tables = call(
+    kr, kv, tables = call(
         key_kernel,
-        [((rows, wide_k), BF16), ((HEAD, rows), F32)],
-        [SMEM] + [VMEM] * 5,
-    )(slot, *pieces, k_here)
-    kr1, v1 = lax.optimization_barrier((kr, v1))
-    k1 = shifted(kr1, -1)
-    v3 = shifted(v1, -2)
-    k2 = shifted(kr, -2)
-    turned, v2 = lax.optimization_barrier((tables, v2))
-    groups = wide_k // HEAD
+        [((rows, wide_k), BF16), ((rows, 2 * wide_k), BF16), ((HEAD, rows), F32)],
+        [SMEM] + [VMEM] * 6,
+    )(slot, *pieces, k_here, v_here)
+    k1 = shifted(kr, -1)
     qr, grad, norm, delta = call(
         functools.partial(prep_kernel, groups),
         [((rows, wide_q), BF16)] * 2 + [((heads, rows), F32)] * 2,
@@ -328,28 +355,58 @@
             pltpu.VMEM((heads, rows), F32),
             pltpu.SemaphoreType.DMA((3 * groups + 1,)),
         ],
-    )(turned, lse, q, do, at)
-    held, _ = lax.optimization_barrier((k1, delta))
+    )(tables, lse, q, do, at)
+    held, _ = lax.optimization_barrier((kv, delta))
+    kv2 = shifted(held, -2)
+    v3 = shifted(v1, -2)
+
+    shared = (qr, grad, norm, delta)
+    dqs = [None] * groups
+
+    def hop(kernel, step, wanted, *arrived):
+        count = len(wanted)
+        started = dqs[wanted[0]] is not None
+        before = [dqs[g] for g in wanted] if started else []
+        *new, part = call(
+            functools.partial(kernel, step, wanted, started),
+            [((wide_q // groups, rows), F32)] * count + [((rows, 2 * HEAD * count), BF16)],
+            [SMEM] * 2 + [VMEM] * (4 + len(arrived) + len(before)),
+        )(slot, span_map, *arrived, *shared, *before)
+        for g, dq in zip(wanted, new):
+            dqs[g] = dq
+        return part
+
+    part1 = hop(hop_kernel, 1, every, k1, v1)
+    swapped = exchanged(part1)
+    held, _ = lax.optimization_barrier((k1, part1))
     k3 = shifted(held, -2)
-
-    dqt = ()
-    backs = []
-    for step, key, value in ((1, k1, v1), (2, k2, v2), (3, k3, v3)):
-        *dqt, part = call(
-            functools.partial(hop_body, step),
-            [((wide_q, rows), F32), ((rows, 2 * wide_k), BF16)],
-            [SMEM] * 2 + [VMEM] * (6 + len(dqt)),
-        )(slot, span_map, key, value, qr, grad, norm, delta, *dqt)
-        backs.append(shifted(part, step))
-    dq, dkv = call(
-        own_kernel, [((rows, wide_q), BF16), ((rows, 2 * wide_k), F32)], [VMEM] * 9
-    )(tables, kr, v_here, qr, grad, norm, delta, *dqt, backs[0])
+    *dqs, own = call(
+        functools.partial(own_kernel, groups),
+        [((wide_q // groups, rows), F32)] * groups + [((rows, 2 * wide_k), F32)],
+        [VMEM] * (6 + groups),
+    )(kr, v_here, *shared, *dqs)
+    part2 = hop(merged_kernel, 2, every, kv2)
+    moved = [shifted(hop(hop_kernel, 3, (g,), k3, v3), 1) for g in every]
+    dq, own = call(
+        functools.partial(query_kernel, groups),
+        [((rows, wide_q), BF16), ((rows, 2 * wide_k), F32)],
+        [SMEM] + [VMEM] * (3 + groups),
+    )(slot, tables, own, swapped, *dqs)
+    part2, _ = lax.optimization_barrier((part2, own))
+    home = []
+    for g in every:
+        (total,) = call(
+            functools.partial(add_kernel, g),
+            [((rows, 2 * HEAD), BF16)],
+            [SMEM] + [VMEM] * 3,
+        )(slot, part2, swapped, moved[g])
+        home.append(shifted(total, 2))
 
     dk, dv = call(
-        final_kernel,
+        functools.partial(final_kernel, groups),
         [((rows, wide_k), BF16), ((rows, wide_k), BF16)],
-        [VMEM] * 4,
-    )(tables, dkv, backs[1], backs[2])
+        [VMEM] * (2 + groups),
+    )(tables, own, *home)
     return dq, dk, dv
 
 

time: 52.8 us -> 50.9 us (0.964)
  waiting for transfers between devices: 16.6 us -> 10.1 us
  Pallas kernels: 15.1 us -> 17.6 us
  starting transfers between devices: 20.1 us -> 22.3 us
    ppermute x12, waiting for transfers between devices: 16.6 us -> 10.1 us  [shifted(): return lax.ppermute(value, axis, pairs)]
    pallas_call x6 -> x10, Pallas kernels: 13.4 us -> 15.8 us  [the longest x4 7.72 us: hop(): call(functools.partial(kernel, step, wanted, started), [((wide_q // group...]
    ppermute x12, starting transfers between devices: 20.1 us -> 22.2 us  [shifted(): return lax.ppermute(value, axis, pairs)]
  transfers between devices with their start and end apart: 12 -> 13, of which waited for: 5 -> 5; matrix products, arithmetic and copies ran while one was open for 0% -> 0% of each run, Pallas kernels for 27% -> 33%
where the time goes in v10:
time: 50.9 us; the launch traced here: 50.7 us
  starting transfers between devices  22.3 us (44%)
  Pallas kernels  17.6 us (35%)
  waiting for transfers between devices  10.1 us (20%)
  between operations  0.72 us (1%)
    ppermute x12, starting transfers between devices, shifted(): return lax.ppermute(value, axis, pairs)  22.2 us
    ppermute x12, waiting for transfers between devices, shifted(): return lax.ppermute(value, axis, pairs)  10.1 us
    pallas_call x4, Pallas kernels, hop(): call(functools.partial(kernel, step, wanted, started), [((wide_q // group...  7.72 us
    pallas_call x1, Pallas kernels, shards(): call(functools.partial(own_kernel, groups), [((wide_q // groups, rows), F...  3.05 us
    pallas_call x1, Pallas kernels, shards(): call(functools.partial(prep_kernel, groups), [((rows, wide_q), BF16)] * 2...  1.74 us
    pallas_call x1, Pallas kernels, shards(): call(functools.partial(query_kernel, groups), [((rows, wide_q), BF16), ((...  1.64 us
    pallas_call x1, Pallas kernels, shards(): call(key_kernel, [((rows, wide_k), BF16), ((rows, 2 * wide_k), BF16), ((H...  1.31 us
    pallas_call x2, Pallas kernels, shards(): call(functools.partial(add_kernel, g), [((rows, 2 * HEAD), BF16)], [SMEM]...  1.2 us
  transfers between devices with their start and end apart: 13, of which 5 were waited for; matrix products, arithmetic and copies ran while one was open for 0% of the time, Pallas kernels for 33%

profile of v10, /device:TPU:0, one launch (start us, length us, event | category | flops | bytes accessed | tf_op | source)
XLA Modules:
  0.0 50.7 jit_solution(89935301822945060)
XLA Ops:
  0.6 3.0 %collective-permute-start.1 = (s32[3,64]{1,0:T(4,128)}, s32[3,64]{1,0:T(4,128)S(1)}, u32[]{:S(2)}, u32[]{:S(2)}) collective-permute-start(s32[3,64]{1,0:T(4,128)} %own_ref.1), channel_id=1, source_target_pairs={{0,2},{1,3},{2,0},{3,1},{4,6},{5,7},{6,4},{7,5},{8,10},{9,11},{10,... | collective-permute-start | bytes 2312 | tf_op jit(solution)/shard_map/ppermute | solution.py:318
  3.6 1.7 %collective-permute-start.2 = (s32[3,64]{1,0:T(4,128)}, s32[3,64]{1,0:T(4,128)S(1)}, u32[]{:S(2)}, u32[]{:S(2)}) collective-permute-start(s32[3,64]{1,0:T(4,128)} %own_ref.1), channel_id=1, source_target_pairs={{0,3},{1,0},{2,1},{3,2},{4,7},{5,4},{6,5},{7,6},{8,11},{9,8},{10,9... | collective-permute-start | bytes 2312 | tf_op jit(solution)/shard_map/ppermute | solution.py:318
  5.4 4.6 %collective-permute-start.4 = (bf16[256,256]{1,0:T(8,128)(2,1)}, bf16[256,256]{1,0:T(8,128)(2,1)S(1)}, u32[]{:S(2)}, u32[]{:S(2)}) collective-permute-start(bf16[256,256]{1,0:T(8,128)(2,1)} %v_ref.3), channel_id=1, source_target_pairs={{0,28},{4,0},{8,4},{12,8},{16,12},{20,16},{24,20},{28,24},{1,29},{... | collective-permute-start | bytes 393224 | tf_op jit(solution)/shard_map/ppermute | solution.py:318
  9.9 0.1 pad_add_fusion.slot_ref
  10.0 1.3 %shard_map.103 = (bf16[256,256]{1,0:T(8,128)(2,1)S(1)}, bf16[256,512]{1,0:T(8,128)(2,1)S(1)}, f32[128,256]{1,0:T(8,128)S(1)}) custom-call(s32[2]{0:T(128)S(1)} %pad_add_fusion.slot_ref, s32[3,64]{1,0:T(4,128)} %own_ref.1, s32[3,64]{1,0:T(4,128)S(1)} %collective-permute-done.p1_ref, s32[3,64]{1,0:T(4,128)S(1)} %collective-permute-done.1.p2_ref, ...), custom_call_target="tpu_custom_call" | custom-call | flops 1048576 | bytes 262144 | tf_op jit(solution)/shard_map/pallas_call | solution.py:342
  11.3 1.5 %collective-permute-start.3 = (bf16[256,256]{1,0:T(8,128)(2,1)S(1)}, bf16[256,256]{1,0:T(8,128)(2,1)S(1)}, u32[]{:S(2)}, u32[]{:S(2)}) collective-permute-start(bf16[256,256]{1,0:T(8,128)(2,1)S(1)} %get-tuple-element.31.k_ref), channel_id=1, source_target_pairs={{0,28},{4,0},{8,4},{12,8},{16,12},{20,16},{24,20},{28,24},{1,29},{... | collective-permute-start | bytes 393224 | tf_op jit(solution)/shard_map/ppermute | solution.py:318
  12.8 1.7 %shard_map.104 = (bf16[256,1024]{1,0:T(8,128)(2,1)S(1)}, bf16[256,1024]{1,0:T(8,128)(2,1)S(1)}, f32[8,256]{1,0:T(8,128)S(1)}, f32[8,256]{1,0:T(8,128)S(1)}) custom-call(f32[128,256]{1,0:T(8,128)S(1)} %get-tuple-element.30.tables_ref, f32[8,256]{1,0:T(8,128)} %lse_hbm.1, bf16[256,1024]{1,0:T(8,128)(2,1)} %q_hbm.1, bf16[256,1024]{1,0:T(8,128)(2,1)} %do_hbm.1, ...), custom_call_target="tpu_custom_call" | custom-call | flops 1048576 | bytes 262144 | tf_op jit(solution)/shard_map/pallas_call | solution.py:348
  14.6 0.5 collective-permute-start.8
  15.1 0.0 collective-permute-done.4.v_ref
  15.1 1.5 %collective-permute-done.3.k_ref = bf16[256,256]{1,0:T(8,128)(2,1)S(1)} collective-permute-done((bf16[256,256]{1,0:T(8,128)(2,1)S(1)}, bf16[256,256]{1,0:T(8,128)(2,1)S(1)}, u32[]{:S(2)}, u32[]{:S(2)}) %collective-permute-start.3) | collective-permute-done | bytes 131104 | tf_op jit(solution)/shard_map/ppermute | solution.py:318
  16.6 2.3 %shard_map.105 = (f32[512,256]{1,0:T(8,128)S(1)}, f32[512,256]{1,0:T(8,128)S(1)}, bf16[256,512]{1,0:T(8,128)(2,1)S(1)}) custom-call(s32[2]{0:T(128)S(1)} %pad_add_fusion.slot_ref, s32[8]{0:T(128)} %span_ref.7, bf16[256,256]{1,0:T(8,128)(2,1)S(1)} %collective-permute-done.3.k_ref, bf16[256,256]{1,0:T(8,128)(2,1)S(1)} %collective-permute-done.4.v_ref, ...), custom_call_target="tpu_custom_call" | custom-call | flops 1048576 | bytes 262144 | tf_op jit(solution)/shard_map/pallas_call | solution.py:370
  18.9 0.1 collective-permute-start.5
  19.0 5.7 %collective-permute-start.7 = (bf16[256,256]{1,0:T(8,128)(2,1)S(1)}, bf16[256,256]{1,0:T(8,128)(2,1)S(1)}, u32[]{:S(2)}, u32[]{:S(2)}) collective-permute-start(bf16[256,256]{1,0:T(8,128)(2,1)S(1)} %collective-permute-done.4.v_ref), channel_id=1, source_target_pairs={{0,24},{4,28},{8,0},{12,4},{16,8},{20,12},{24,16},{28,20},{1,25},{... | collective-permute-start | bytes 393224 | tf_op jit(solution)/shard_map/ppermute | solution.py:318
  24.7 0.0 collective-permute-start.6
  24.7 3.1 %shard_map.106 = (f32[512,256]{1,0:T(8,128)S(1)}, f32[512,256]{1,0:T(8,128)S(1)}, f32[256,512]{1,0:T(8,128)S(1)}) custom-call(bf16[256,256]{1,0:T(8,128)(2,1)S(1)} %get-tuple-element.31.k_ref, bf16[256,256]{1,0:T(8,128)(2,1)} %v_ref.3, bf16[256,1024]{1,0:T(8,128)(2,1)S(1)} %get-tuple-element.32.refs_0_.qr_ref, ...), custom_call_target="tpu_custom_call" | custom-call | flops 1048576 | bytes 262144 | tf_op jit(solution)/shard_map/pallas_call | solution.py:383
  27.8 0.0 collective-permute-done.8.kv_ref
  27.8 2.3 %shard_map.107 = (f32[512,256]{1,0:T(8,128)S(1)}, f32[512,256]{1,0:T(8,128)S(1)}, bf16[256,512]{1,0:T(8,128)(2,1)S(1)}) custom-call(s32[2]{0:T(128)S(1)} %pad_add_fusion.slot_ref, s32[8]{0:T(128)} %span_ref.7, bf16[256,512]{1,0:T(8,128)(2,1)S(1)} %collective-permute-done.8.kv_ref, bf16[256,1024]{1,0:T(8,128)(2,1)S(1)} %get-tuple-element.32.refs_0_.qr_ref, ...), custom_call_target="tpu_custom_call" | custom-call | flops 1048576 | bytes 262144 | tf_op jit(solution)/shard_map/pallas_call | solution.py:370
  30.1 0.0 collective-permute-done.6.k_ref
  30.1 1.6 %shard_map.108 = (f32[512,256]{1,0:T(8,128)S(1)}, bf16[256,256]{1,0:T(8,128)(2,1)S(1)}) custom-call(s32[2]{0:T(128)S(1)} %pad_add_fusion.slot_ref, s32[8]{0:T(128)} %span_ref.7, bf16[256,256]{1,0:T(8,128)(2,1)S(1)} %collective-permute-done.6.k_ref, bf16[256,256]{1,0:T(8,128)(2,1)S(1)} %collective-permute-done.7.v_ref, ...), custom_call_target="tpu_custom_call" | custom-call | flops 1048576 | bytes 262144 | tf_op jit(solution)/shard_map/pallas_call | solution.py:370
  31.7 0.1 collective-permute-start.9
  31.9 1.6 %shard_map.109 = (f32[512,256]{1,0:T(8,128)S(1)}, bf16[256,256]{1,0:T(8,128)(2,1)S(1)}) custom-call(s32[2]{0:T(128)S(1)} %pad_add_fusion.slot_ref, s32[8]{0:T(128)} %span_ref.7, bf16[256,256]{1,0:T(8,128)(2,1)S(1)} %collective-permute-done.6.k_ref, bf16[256,256]{1,0:T(8,128)(2,1)S(1)} %collective-permute-done.7.v_ref, ...), custom_call_target="tpu_custom_call" | custom-call | flops 1048576 | bytes 262144 | tf_op jit(solution)/shard_map/pallas_call | solution.py:370
  33.4 3.4 %collective-permute-start.11 = (bf16[256,256]{1,0:T(8,128)(2,1)S(1)}, bf16[256,256]{1,0:T(8,128)(2,1)S(1)}, u32[]{:S(2)}, u32[]{:S(2)}) collective-permute-start(bf16[256,256]{1,0:T(8,128)(2,1)S(1)} %get-tuple-element.54), channel_id=1, source_target_pairs={{0,4},{4,8},{8,12},{12,16},{16,20},{20,24},{24,28},{28,0},{1,5},{5... | collective-permute-start | bytes 393224 | tf_op jit(solution)/shard_map/ppermute | solution.py:318
  36.9 1.6 %shard_map.110 = (bf16[256,1024]{1,0:T(8,128)(2,1)}, f32[256,512]{1,0:T(8,128)S(1)}) custom-call(s32[2]{0:T(128)S(1)} %pad_add_fusion.slot_ref, f32[128,256]{1,0:T(8,128)S(1)} %get-tuple-element.30.tables_ref, f32[256,512]{1,0:T(8,128)S(1)} %get-tuple-element.38.own_ref, bf16[256,512]{1,0:T(8,128)(2,1)S(1)} %collective-permute-done.5.swapped_ref, ...), custom_call_target="tpu_custom_call" | custom-call | flops 1048576 | bytes 262144 | tf_op jit(solution)/shard_map/pallas_call | solution.py:390
  38.5 2.1 %collective-permute-done.9.three_ref = bf16[256,256]{1,0:T(8,128)(2,1)S(1)} collective-permute-done((bf16[256,256]{1,0:T(8,128)(2,1)S(1)}, bf16[256,256]{1,0:T(8,128)(2,1)S(1)}, u32[]{:S(2)}, u32[]{:S(2)}) %collective-permute-start.9) | collective-permute-done | bytes 131104 | tf_op jit(solution)/shard_map/ppermute | solution.py:318
  40.6 0.6 %shard_map.111 = bf16[256,256]{1,0:T(8,128)(2,1)S(1)} custom-call(s32[2]{0:T(128)S(1)} %pad_add_fusion.slot_ref, bf16[256,512]{1,0:T(8,128)(2,1)S(1)} %get-tuple-element.52.two_ref, bf16[256,512]{1,0:T(8,128)(2,1)S(1)} %collective-permute-done.5.swapped_ref, bf16[256,256]{1,0:T(8,128)(2,1)S(1)} %collective-permute-done.9.three_ref), custom_call_target="tpu_custom_call" | custom-call | flops 1048576 | bytes 262144 | tf_op jit(solution)/shard_map/pallas_call | solution.py:398
  41.2 0.4 collective-permute-start.10
  41.6 0.8 %collective-permute-done.11.three_ref = bf16[256,256]{1,0:T(8,128)(2,1)S(1)} collective-permute-done((bf16[256,256]{1,0:T(8,128)(2,1)S(1)}, bf16[256,256]{1,0:T(8,128)(2,1)S(1)}, u32[]{:S(2)}, u32[]{:S(2)}) %collective-permute-start.11) | collective-permute-done | bytes 131104 | tf_op jit(solution)/shard_map/ppermute | solution.py:318
  42.4 0.6 %shard_map.112 = bf16[256,256]{1,0:T(8,128)(2,1)S(1)} custom-call(s32[2]{0:T(128)S(1)} %pad_add_fusion.slot_ref, bf16[256,512]{1,0:T(8,128)(2,1)S(1)} %get-tuple-element.52.two_ref, bf16[256,512]{1,0:T(8,128)(2,1)S(1)} %collective-permute-done.5.swapped_ref, bf16[256,256]{1,0:T(8,128)(2,1)S(1)} %collective-permute-done.11.three_ref), custom_call_target="tpu_custom_call" | custom-call | flops 1048576 | bytes 262144 | tf_op jit(solution)/shard_map/pallas_call | solution.py:398
  43.0 1.2 %collective-permute-start.12 = (bf16[256,256]{1,0:T(8,128)(2,1)S(1)}, bf16[256,256]{1,0:T(8,128)(2,1)S(1)}, u32[]{:S(2)}, u32[]{:S(2)}) collective-permute-start(bf16[256,256]{1,0:T(8,128)(2,1)S(1)} %shard_map.112), channel_id=1, source_target_pairs={{0,8},{4,12},{8,16},{12,20},{16,24},{20,28},{24,0},{28,4},{1,9},{5... | collective-permute-start | bytes 393224 | tf_op jit(solution)/shard_map/ppermute | solution.py:318
  44.2 4.1 %collective-permute-done.10.refs_0_ = bf16[256,256]{1,0:T(8,128)(2,1)S(1)} collective-permute-done((bf16[256,256]{1,0:T(8,128)(2,1)S(1)}, bf16[256,256]{1,0:T(8,128)(2,1)S(1)}, u32[]{:S(2)}, u32[]{:S(2)}) %collective-permute-start.10) | collective-permute-done | bytes 131104 | tf_op jit(solution)/shard_map/ppermute | solution.py:318
  48.3 1.5 %collective-permute-done.12.refs_1_ = bf16[256,256]{1,0:T(8,128)(2,1)S(1)} collective-permute-done((bf16[256,256]{1,0:T(8,128)(2,1)S(1)}, bf16[256,256]{1,0:T(8,128)(2,1)S(1)}, u32[]{:S(2)}, u32[]{:S(2)}) %collective-permute-start.12) | collective-permute-done | bytes 131104 | tf_op jit(solution)/shard_map/ppermute | solution.py:318
  49.8 0.9 %shard_map.113 = (bf16[256,256]{1,0:T(8,128)(2,1)}, bf16[256,256]{1,0:T(8,128)(2,1)}) custom-call(f32[128,256]{1,0:T(8,128)S(1)} %get-tuple-element.30.tables_ref, f32[256,512]{1,0:T(8,128)S(1)} %get-tuple-element.50.own_ref, bf16[256,256]{1,0:T(8,128)(2,1)S(1)} %collective-permute-done.10.refs_0_, bf16[256,256]{1,0:T(8,128)(2,1)S(1)} %collective-permute-done.12.refs_1_), custom_call_target="tpu_custom_call" | custom-call | flops 1048576 | bytes 262144 | tf_op jit(solution)/shard_map/pallas_call | solution.py:405
  (6 shorter events, 0.0 us)
Async XLA Ops:
  0.6 9.4 %collective-permute-start.1 = (s32[3,64]{1,0:T(4,128)}, s32[3,64]{1,0:T(4,128)S(1)}, u32[]{:S(2)}, u32[]{:S(2)}) collective-permute-start(s32[3,64]{1,0:T(4,128)} %own_ref.1), channel_id=1, source_target_pairs={{0,2},{1,3},{2,0},{3,1},{4,6},{5,7},{6,4},{7,5},{8,10},{9,11},{10,... | collective-permute-start | bytes 2312 | tf_op jit(solution)/shard_map/ppermute | solution.py:318
  3.6 6.4 %collective-permute-start = (s32[3,64]{1,0:T(4,128)}, s32[3,64]{1,0:T(4,128)S(1)}, u32[]{:S(2)}, u32[]{:S(2)}) collective-permute-start(s32[3,64]{1,0:T(4,128)} %own_ref.1), channel_id=1, source_target_pairs={{0,1},{1,2},{2,3},{3,0},{4,5},{5,6},{6,7},{7,4},{8,9},{9,10},{10,1... | collective-permute-start | bytes 2312 | tf_op jit(solution)/shard_map/ppermute | solution.py:318
  3.6 6.4 %collective-permute-start.2 = (s32[3,64]{1,0:T(4,128)}, s32[3,64]{1,0:T(4,128)S(1)}, u32[]{:S(2)}, u32[]{:S(2)}) collective-permute-start(s32[3,64]{1,0:T(4,128)} %own_ref.1), channel_id=1, source_target_pairs={{0,3},{1,0},{2,1},{3,2},{4,7},{5,4},{6,5},{7,6},{8,11},{9,8},{10,9... | collective-permute-start | bytes 2312 | tf_op jit(solution)/shard_map/ppermute | solution.py:318
  5.4 9.7 %collective-permute-start.4 = (bf16[256,256]{1,0:T(8,128)(2,1)}, bf16[256,256]{1,0:T(8,128)(2,1)S(1)}, u32[]{:S(2)}, u32[]{:S(2)}) collective-permute-start(bf16[256,256]{1,0:T(8,128)(2,1)} %v_ref.3), channel_id=1, source_target_pairs={{0,28},{4,0},{8,4},{12,8},{16,12},{20,16},{24,20},{28,24},{1,29},{... | collective-permute-start | bytes 393224 | tf_op jit(solution)/shard_map/ppermute | solution.py:318
  11.3 5.3 %collective-permute-start.3 = (bf16[256,256]{1,0:T(8,128)(2,1)S(1)}, bf16[256,256]{1,0:T(8,128)(2,1)S(1)}, u32[]{:S(2)}, u32[]{:S(2)}) collective-permute-start(bf16[256,256]{1,0:T(8,128)(2,1)S(1)} %get-tuple-element.31.k_ref), channel_id=1, source_target_pairs={{0,28},{4,0},{8,4},{12,8},{16,12},{20,16},{24,20},{28,24},{1,29},{... | collective-permute-start | bytes 393224 | tf_op jit(solution)/shard_map/ppermute | solution.py:318
  14.6 13.2 %collective-permute-start.8 = (bf16[256,512]{1,0:T(8,128)(2,1)S(1)}, bf16[256,512]{1,0:T(8,128)(2,1)S(1)}, u32[]{:S(2)}, u32[]{:S(2)}) collective-permute-start(bf16[256,512]{1,0:T(8,128)(2,1)S(1)} %get-tuple-element.42), channel_id=1, source_target_pairs={{0,24},{4,28},{8,0},{12,4},{16,8},{20,12},{24,16},{28,20},{1,25},{... | collective-permute-start | bytes 786440 | tf_op jit(solution)/shard_map/ppermute | solution.py:318
  18.9 17.9 %collective-permute-start.5 = (bf16[256,512]{1,0:T(8,128)(2,1)S(1)}, bf16[256,512]{1,0:T(8,128)(2,1)S(1)}, u32[]{:S(2)}, u32[]{:S(2)}) collective-permute-start(bf16[256,512]{1,0:T(8,128)(2,1)S(1)} %get-tuple-element.39), channel_id=1, source_target_pairs={{0,4},{4,0},{8,12},{12,8},{16,20},{20,16},{24,28},{28,24},{1,5},{5... | collective-permute-start | bytes 786440 | tf_op jit(solution)/shard_map/ppermute | solution.py:323
  19.0 11.1 %collective-permute-start.7 = (bf16[256,256]{1,0:T(8,128)(2,1)S(1)}, bf16[256,256]{1,0:T(8,128)(2,1)S(1)}, u32[]{:S(2)}, u32[]{:S(2)}) collective-permute-start(bf16[256,256]{1,0:T(8,128)(2,1)S(1)} %collective-permute-done.4.v_ref), channel_id=1, source_target_pairs={{0,24},{4,28},{8,0},{12,4},{16,8},{20,12},{24,16},{28,20},{1,25},{... | collective-permute-start | bytes 393224 | tf_op jit(solution)/shard_map/ppermute | solution.py:318
  24.7 5.4 %collective-permute-start.6 = (bf16[256,256]{1,0:T(8,128)(2,1)S(1)}, bf16[256,256]{1,0:T(8,128)(2,1)S(1)}, u32[]{:S(2)}, u32[]{:S(2)}) collective-permute-start(bf16[256,256]{1,0:T(8,128)(2,1)S(1)} %collective-permute-done.3.k_ref), channel_id=1, source_target_pairs={{0,24},{4,28},{8,0},{12,4},{16,8},{20,12},{24,16},{28,20},{1,25},{... | collective-permute-start | bytes 393224 | tf_op jit(solution)/shard_map/ppermute | solution.py:318
  31.7 8.9 %collective-permute-start.9 = (bf16[256,256]{1,0:T(8,128)(2,1)S(1)}, bf16[256,256]{1,0:T(8,128)(2,1)S(1)}, u32[]{:S(2)}, u32[]{:S(2)}) collective-permute-start(bf16[256,256]{1,0:T(8,128)(2,1)S(1)} %get-tuple-element.53), channel_id=1, source_target_pairs={{0,4},{4,8},{8,12},{12,16},{16,20},{20,24},{24,28},{28,0},{1,5},{5... | collective-permute-start | bytes 393224 | tf_op jit(solution)/shard_map/ppermute | solution.py:318
  33.4 9.0 %collective-permute-start.11 = (bf16[256,256]{1,0:T(8,128)(2,1)S(1)}, bf16[256,256]{1,0:T(8,128)(2,1)S(1)}, u32[]{:S(2)}, u32[]{:S(2)}) collective-permute-start(bf16[256,256]{1,0:T(8,128)(2,1)S(1)} %get-tuple-element.54), channel_id=1, source_target_pairs={{0,4},{4,8},{8,12},{12,16},{16,20},{20,24},{24,28},{28,0},{1,5},{5... | collective-permute-start | bytes 393224 | tf_op jit(solution)/shard_map/ppermute | solution.py:318
  41.2 7.1 %collective-permute-start.10 = (bf16[256,256]{1,0:T(8,128)(2,1)S(1)}, bf16[256,256]{1,0:T(8,128)(2,1)S(1)}, u32[]{:S(2)}, u32[]{:S(2)}) collective-permute-start(bf16[256,256]{1,0:T(8,128)(2,1)S(1)} %shard_map.111), channel_id=1, source_target_pairs={{0,8},{4,12},{8,16},{12,20},{16,24},{20,28},{24,0},{28,4},{1,9},{5... | collective-permute-start | bytes 393224 | tf_op jit(solution)/shard_map/ppermute | solution.py:318
  43.0 6.8 %collective-permute-start.12 = (bf16[256,256]{1,0:T(8,128)(2,1)S(1)}, bf16[256,256]{1,0:T(8,128)(2,1)S(1)}, u32[]{:S(2)}, u32[]{:S(2)}) collective-permute-start(bf16[256,256]{1,0:T(8,128)(2,1)S(1)} %shard_map.112), channel_id=1, source_target_pairs={{0,8},{4,12},{8,16},{12,20},{16,24},{20,28},{24,0},{28,4},{1,9},{5... | collective-permute-start | bytes 393224 | tf_op jit(solution)/shard_map/ppermute | solution.py:318

commit v11 on v10

--- a/solution.py
+++ b/solution.py
@@ -118,10 +118,10 @@
     return value_part, key_part, query_part
 
 
-def key_kernel(slot_ref, own_ref, p1_ref, p2_ref, p3_ref, k_ref, v_ref, kr_ref, kv_ref, tables_ref):
+def key_kernel(own_ref, p1_ref, p2_ref, p3_ref, k_ref, v_ref, kr_ref, kv_ref, tables_ref):
     pieces = (own_ref[...], p1_ref[...], p2_ref[...], p3_ref[...])
     count = len(pieces)
-    head = slot_ref[1]
+    head = lax.axis_index("head")
     parts = []
     for j in range(count):
         back = lax.rem(head - j + count, count)
@@ -142,8 +142,8 @@
 
 
 def prep_kernel(
-    groups, tables_ref, lse_hbm, q_hbm, do_hbm, at_hbm,
-    qr_ref, do_ref, norm_ref, delta_ref, q_ref, at_ref, lse_ref, sems,
+    groups, span_ref, tables_ref, lse_hbm, q_hbm, do_hbm, at_hbm,
+    qr_ref, do_ref, norm_ref, delta_ref, flag_ref, q_ref, at_ref, lse_ref, sems,
 ):
     heads = qr_ref.shape[1] // HEAD
     size = heads // groups
@@ -160,6 +160,14 @@
             copies.append(copy)
     lse_copy = pltpu.make_async_copy(lse_hbm, lse_ref, sems.at[3 * groups])
     lse_copy.start()
+    me = lax.axis_index("ctx")
+    step_row = lax.broadcasted_iota(jnp.int32, flag_ref.shape, 0)
+    flags = jnp.zeros(flag_ref.shape, jnp.int32)
+    for step in range(1, WIN):
+        other = lax.rem(me + step, span_ref.shape[0])
+        earlier = jnp.where(span_ref[other] < span_ref[me], 1, 0)
+        flags = jnp.where(step_row == step, earlier, flags)
+    flag_ref[...] = flags
     wide, signed = row_tables(tables_ref[:HALF, :], tables_ref[HALF:, :])
     chooser = jnp.ones((8, HEAD), BF16)
     for h in range(heads):
@@ -176,19 +184,17 @@
     norm_ref[...] = lse_ref[...] * LOG2E
 
 
-def hop_kernel(step, wanted, started, slot_ref, span_ref, k_ref, v_ref, *refs):
-    qr_ref, do_ref, norm_ref, delta_ref = refs[:4]
+def hop_kernel(step, wanted, started, k_ref, v_ref, *refs):
+    qr_ref, do_ref, norm_ref, delta_ref, flag_ref = refs[:5]
     count = len(wanted)
-    dqt_ins = refs[4 : 4 + count] if started else [None] * count
+    dqt_ins = refs[5 : 5 + count] if started else [None] * count
     dqt_refs, part_ref = refs[-count - 1 : -1], refs[-1]
     rows = qr_ref.shape[0]
     half = rows // 2
     heads = qr_ref.shape[1] // HEAD
     groups = k_ref.shape[1] // HEAD
     size = heads // groups
-    me = slot_ref[0]
-    other = lax.rem(me + step, span_ref.shape[0])
-    earlier = span_ref[other] < span_ref[me]
+    earlier = flag_ref[step, 0] == 1
     norm = norm_ref[...]
     delta = delta_ref[...]
 
@@ -226,16 +232,13 @@
         run(slice(0, rows), slice(half, rows))
 
 
-def merged_kernel(step, wanted, started, slot_ref, span_ref, kv_ref, *refs):
+def merged_kernel(step, wanted, started, kv_ref, *refs):
     width = kv_ref.shape[1] // 2
-    hop_kernel(
-        step, wanted, started, slot_ref, span_ref, kv_ref.at[:, :width], kv_ref.at[:, width:],
-        *refs,
-    )
+    hop_kernel(step, wanted, started, kv_ref.at[:, :width], kv_ref.at[:, width:], *refs)
 
 
 def own_kernel(groups, k_ref, v_ref, qr_ref, do_ref, norm_ref, delta_ref, *refs):
-    dqt_ins, dqt_refs, part_ref = refs[:groups], refs[groups : 2 * groups], refs[2 * groups]
+    dqt_refs, part_ref = refs[:groups], refs[groups]
     size = qr_ref.shape[1] // HEAD // groups
     norm = norm_ref[...]
     delta = delta_ref[...]
@@ -250,16 +253,16 @@
                 k_ref[:, kc], v_ref[:, kc], qr_ref[:, hc], do_ref[:, hc],
                 norm[h : h + 1], delta[h : h + 1], True,
             )
-            dqt_refs[g][to, :] = dqt_ins[g][to, :] + q_part
+            dqt_refs[g][to, :] = q_part
             dv = v_part if dv is None else dv + v_part
             dk = k_part if dk is None else dk + k_part
         part_ref[:, pl.ds(2 * g * HEAD, HEAD)] = dk
         part_ref[:, pl.ds((2 * g + 1) * HEAD, HEAD)] = dv
 
 
-def query_kernel(groups, slot_ref, tables_ref, own_ref, swapped_ref, *refs):
+def query_kernel(groups, tables_ref, own_ref, swapped_ref, *refs):
     dqt_refs, out_ref, sum_ref = refs[:groups], refs[groups], refs[groups + 1]
-    odd = (slot_ref[0] & 1) == 1
+    odd = (lax.axis_index("ctx") & 1) == 1
     sum_ref[...] = own_ref[...] + jnp.where(odd, swapped_ref[...].astype(F32), 0.0)
     cosine_t = tables_ref[:HALF, :] * ROOT_SCALE
     sine_t = tables_ref[HALF:, :] * ROOT_SCALE
@@ -274,8 +277,8 @@
             out_ref[:, pl.ds((g * size + j) * HEAD, HEAD)] = turned.T.astype(BF16)
 
 
-def add_kernel(g, slot_ref, two_ref, swapped_ref, three_ref, sum_ref):
-    even = (slot_ref[0] & 1) == 0
+def add_kernel(g, two_ref, swapped_ref, three_ref, sum_ref):
+    even = (lax.axis_index("ctx") & 1) == 0
     cols = pl.ds(2 * g * HEAD, 2 * HEAD)
     total = two_ref[:, cols].astype(F32) + three_ref[...].astype(F32)
     sum_ref[...] = (total + jnp.where(even, swapped_ref[:, cols].astype(F32), 0.0)).astype(BF16)
@@ -298,7 +301,7 @@
 HBM = pl.BlockSpec(memory_space=pltpu.HBM)
 
 
-def call(kernel, outs, specs, scratch=()):
+def call(kernel, outs, specs, scratch=(), micros=1):
     return pl.pallas_call(
         kernel,
         out_shape=[jax.ShapeDtypeStruct(shape, dtype) for shape, dtype in outs],
@@ -307,7 +310,7 @@
         scratch_shapes=list(scratch),
         compiler_params=pltpu.CompilerParams(vmem_limit_bytes=VMEM_LIMIT),
         cost_estimate=pl.CostEstimate(
-            flops=1 << 20, bytes_accessed=1 << 18, transcendentals=0
+            flops=1 << 20, bytes_accessed=micros * 3690000, transcendentals=0
         ),
     )
 
@@ -328,13 +331,15 @@
     wide_q = q.shape[1]
     wide_k = k.shape[1]
     heads = wide_q // HEAD
-    slot = jnp.stack([lax.axis_index("ctx"), lax.axis_index("head")]).astype(jnp.int32)
     q, do, at, k_here, v_here, lse, span_map, own = (
         pltpu.with_memory_space_constraint(x, pltpu.HBM)
         for x in (q, do, at, k, v, lse, span_map, positions)
     )
 
     pieces = [own] + [shifted(positions, r, "head") for r in (1, 2, 3)]
+    groups = wide_k // HEAD
+    every = tuple(range(groups))
+
     groups = wide_k // HEAD
     every = tuple(range(groups))
 
@@ -342,64 +347,62 @@
     kr, kv, tables = call(
         key_kernel,
         [((rows, wide_k), BF16), ((rows, 2 * wide_k), BF16), ((HEAD, rows), F32)],
-        [SMEM] + [VMEM] * 6,
-    )(slot, *pieces, k_here, v_here)
+        [VMEM] * 6,
+    )(*pieces, k_here, v_here)
     k1 = shifted(kr, -1)
-    qr, grad, norm, delta = call(
+    shared = call(
         functools.partial(prep_kernel, groups),
-        [((rows, wide_q), BF16)] * 2 + [((heads, rows), F32)] * 2,
-        [VMEM] + [HBM] * 4,
+        [((rows, wide_q), BF16)] * 2 + [((heads, rows), F32)] * 2 + [((8, HEAD), jnp.int32)],
+        [SMEM, VMEM] + [HBM] * 4,
         [
             pltpu.VMEM((rows, wide_q), BF16),
             pltpu.VMEM((rows, wide_q), BF16),
             pltpu.VMEM((heads, rows), F32),
             pltpu.SemaphoreType.DMA((3 * groups + 1,)),
         ],
-    )(tables, lse, q, do, at)
-    held, _ = lax.optimization_barrier((kv, delta))
-    kv2 = shifted(held, -2)
-    v3 = shifted(v1, -2)
-
-    shared = (qr, grad, norm, delta)
-    dqs = [None] * groups
+        micros=2,
+    )(span_map, tables, lse, q, do, at)
+    *dqs, own = call(
+        functools.partial(own_kernel, groups),
+        [((wide_q // groups, rows), F32)] * groups + [((rows, 2 * wide_k), F32)],
+        [VMEM] * 6,
+        micros=3,
+    )(kr, v_here, *shared[:4])
 
     def hop(kernel, step, wanted, *arrived):
         count = len(wanted)
-        started = dqs[wanted[0]] is not None
-        before = [dqs[g] for g in wanted] if started else []
+        before = [dqs[g] for g in wanted]
         *new, part = call(
-            functools.partial(kernel, step, wanted, started),
+            functools.partial(kernel, step, wanted, True),
             [((wide_q // groups, rows), F32)] * count + [((rows, 2 * HEAD * count), BF16)],
-            [SMEM] * 2 + [VMEM] * (4 + len(arrived) + len(before)),
-        )(slot, span_map, *arrived, *shared, *before)
+            [VMEM] * (5 + len(arrived) + count),
+            micros=count,
+        )(*arrived, *shared, *before)
         for g, dq in zip(wanted, new):
             dqs[g] = dq
         return part
 
+    v1, k1, _ = lax.optimization_barrier((v1, k1, own))
+    v3 = shifted(v1, -2)
+    k3 = shifted(k1, -2)
     part1 = hop(hop_kernel, 1, every, k1, v1)
+    held, _ = lax.optimization_barrier((kv, part1))
+    kv2 = shifted(held, -2)
+    part1, k3, v3 = lax.optimization_barrier((part1, k3, v3))
     swapped = exchanged(part1)
-    held, _ = lax.optimization_barrier((k1, part1))
-    k3 = shifted(held, -2)
-    *dqs, own = call(
-        functools.partial(own_kernel, groups),
-        [((wide_q // groups, rows), F32)] * groups + [((rows, 2 * wide_k), F32)],
-        [VMEM] * (6 + groups),
-    )(kr, v_here, *shared, *dqs)
+    moved = [shifted(hop(hop_kernel, 3, (g,), k3, v3), 1) for g in every]
     part2 = hop(merged_kernel, 2, every, kv2)
-    moved = [shifted(hop(hop_kernel, 3, (g,), k3, v3), 1) for g in every]
     dq, own = call(
         functools.partial(query_kernel, groups),
         [((rows, wide_q), BF16), ((rows, 2 * wide_k), F32)],
-        [SMEM] + [VMEM] * (3 + groups),
-    )(slot, tables, own, swapped, *dqs)
+        [VMEM] * (3 + groups),
+    )(tables, own, swapped, *dqs)
     part2, _ = lax.optimization_barrier((part2, own))
     home = []
     for g in every:
         (total,) = call(
-            functools.partial(add_kernel, g),
-            [((rows, 2 * HEAD), BF16)],
-            [SMEM] + [VMEM] * 3,
-        )(slot, part2, swapped, moved[g])
+            functools.partial(add_kernel, g), [((rows, 2 * HEAD), BF16)], [VMEM] * 3
+        )(part2, swapped, moved[g])
         home.append(shifted(total, 2))
 
     dk, dv = call(

time: 50.9 us -> 51.6 us (1.014)
  the two profiles are of different devices: /device:TPU:0 before, /device:TPU:2 now
where the time goes in v11:
time: 51.6 us; the launch traced here: 51.4 us
  waiting for transfers between devices  24.5 us (47%)
  Pallas kernels  14 us (27%)
  starting transfers between devices  12.2 us (24%)
  between operations  0.74 us (1%)
    ppermute x12, waiting for transfers between devices, shifted(): return lax.ppermute(value, axis, pairs)  17.2 us
    ppermute x12, starting transfers between devices, shifted(): return lax.ppermute(value, axis, pairs)  10.9 us
    ppermute x1, waiting for transfers between devices, exchanged(): lax.ppermute(value, 'ctx', [(source, source ^ 1) for source in range(coun...  7.29 us
    pallas_call x4, Pallas kernels, hop(): call(functools.partial(kernel, step, wanted, True), [((wide_q // groups,...  5.13 us
    pallas_call x1, Pallas kernels, shards(): call(functools.partial(own_kernel, groups), [((wide_q // groups, rows), F...  3.06 us
    pallas_call x1, Pallas kernels, shards(): call(functools.partial(prep_kernel, groups), [((rows, wide_q), BF16)] * 2...  2.42 us
    ppermute x1, starting transfers between devices, exchanged(): lax.ppermute(value, 'ctx', [(source, source ^ 1) for source in range(coun...  1.33 us
    pallas_call x1, Pallas kernels, shards(): call(key_kernel, [((rows, wide_k), BF16), ((rows, 2 * wide_k), BF16), ((H...  1.3 us
  transfers between devices with their start and end apart: 13, of which 6 were waited for; matrix products, arithmetic and copies ran while one was open for 0% of the time, Pallas kernels for 26%

profile of v11, /device:TPU:2, one launch (start us, length us, event | category | flops | bytes accessed | tf_op | source)
XLA Modules:
  0.0 51.4 jit_solution(16412975169047365271)
XLA Ops:
  0.6 0.1 collective-permute-start.1
  0.7 0.1 collective-permute-start
  0.8 1.7 %collective-permute-start.2 = (s32[3,64]{1,0:T(4,128)}, s32[3,64]{1,0:T(4,128)S(1)}, u32[]{:S(2)}, u32[]{:S(2)}) collective-permute-start(s32[3,64]{1,0:T(4,128)} %own_ref.1), channel_id=1, source_target_pairs={{0,3},{1,0},{2,1},{3,2},{4,7},{5,4},{6,5},{7,6},{8,11},{9,8},{10,9... | collective-permute-start | bytes 2312 | tf_op jit(solution)/shard_map/ppermute | solution.py:321
  2.5 5.0 %collective-permute-start.3 = (bf16[256,256]{1,0:T(8,128)(2,1)}, bf16[256,256]{1,0:T(8,128)(2,1)S(1)}, u32[]{:S(2)}, u32[]{:S(2)}) collective-permute-start(bf16[256,256]{1,0:T(8,128)(2,1)} %v_ref.3), channel_id=1, source_target_pairs={{0,28},{4,0},{8,4},{12,8},{16,12},{20,16},{24,20},{28,24},{1,29},{... | collective-permute-start | bytes 393224 | tf_op jit(solution)/shard_map/ppermute | solution.py:321
  7.5 0.0 collective-permute-done.1.p2_ref
  7.5 1.3 %shard_map.103 = (bf16[256,256]{1,0:T(8,128)(2,1)S(1)}, bf16[256,512]{1,0:T(8,128)(2,1)S(1)}, f32[128,256]{1,0:T(8,128)S(1)}) custom-call(s32[3,64]{1,0:T(4,128)} %own_ref.1, s32[3,64]{1,0:T(4,128)S(1)} %collective-permute-done.p1_ref, s32[3,64]{1,0:T(4,128)S(1)} %collective-permute-done.1.p2_ref, s32[3,64]{1,0:T(4,128)S(1)} %collective-permute-done.2.p3_ref, ...), custom_call_target="tpu_custom_call" | custom-call | flops 1048576 | bytes 3690000 | tf_op jit(solution)/shard_map/pallas_call | solution.py:347
  8.8 1.6 %collective-permute-start.4 = (bf16[256,256]{1,0:T(8,128)(2,1)S(1)}, bf16[256,256]{1,0:T(8,128)(2,1)S(1)}, u32[]{:S(2)}, u32[]{:S(2)}) collective-permute-start(bf16[256,256]{1,0:T(8,128)(2,1)S(1)} %get-tuple-element.36.k_ref), channel_id=1, source_target_pairs={{0,28},{4,0},{8,4},{12,8},{16,12},{20,16},{24,20},{28,24},{1,29},{... | collective-permute-start | bytes 393224 | tf_op jit(solution)/shard_map/ppermute | solution.py:321
  10.4 2.4 %shard_map.104 = (bf16[256,1024]{1,0:T(8,128)(2,1)S(1)}, bf16[256,1024]{1,0:T(8,128)(2,1)S(1)}, f32[8,256]{1,0:T(8,128)S(1)}, f32[8,256]{1,0:T(8,128)S(1)}, s32[8,128]{1,0:T(8,128)S(1)}) custom-call(s32[8]{0:T(128)} %span_ref.1, f32[128,256]{1,0:T(8,128)S(1)} %get-tuple-element.35.tables_ref, f32[8,256]{1,0:T(8,128)} %lse_hbm.1, bf16[256,1024]{1,0:T(8,128)(2,1)} %q_hbm.1, ...), custom_call_target="tpu_custom_call" | custom-call | flops 1048576 | bytes 7380000 | tf_op jit(solution)/shard_map/pallas_call | solution.py:353
  12.8 3.1 %shard_map.105 = (f32[512,256]{1,0:T(8,128)S(1)}, f32[512,256]{1,0:T(8,128)S(1)}, f32[256,512]{1,0:T(8,128)S(1)}) custom-call(bf16[256,256]{1,0:T(8,128)(2,1)S(1)} %get-tuple-element.36.k_ref, bf16[256,256]{1,0:T(8,128)(2,1)} %v_ref.3, bf16[256,1024]{1,0:T(8,128)(2,1)S(1)} %get-tuple-element.37.qr_ref.refs_0_, ...), custom_call_target="tpu_custom_call" | custom-call | flops 1048576 | bytes 11070000 | tf_op jit(solution)/shard_map/pallas_call | solution.py:365
  15.9 0.0 collective-permute-done.4.k_ref
  15.9 0.5 collective-permute-start.5
  16.4 0.4 collective-permute-start.6
  16.9 1.6 %shard_map.106 = (f32[512,256]{1,0:T(8,128)S(1)}, f32[512,256]{1,0:T(8,128)S(1)}, bf16[256,512]{1,0:T(8,128)(2,1)S(1)}) custom-call(bf16[256,256]{1,0:T(8,128)(2,1)S(1)} %collective-permute-done.4.k_ref, bf16[256,256]{1,0:T(8,128)(2,1)S(1)} %collective-permute-done.3.v_ref, bf16[256,1024]{1,0:T(8,128)(2,1)S(1)} %get-tuple-element.37.qr_ref.refs_0_, ...), custom_call_target="tpu_custom_call" | custom-call | flops 1048576 | bytes 7380000 | tf_op jit(solution)/shard_map/pallas_call | solution.py:375
  18.5 0.5 collective-permute-start.8
  19.0 3.0 %collective-permute-done.5.k_ref = bf16[256,256]{1,0:T(8,128)(2,1)S(1)} collective-permute-done((bf16[256,256]{1,0:T(8,128)(2,1)S(1)}, bf16[256,256]{1,0:T(8,128)(2,1)S(1)}, u32[]{:S(2)}, u32[]{:S(2)}) %collective-permute-start.5) | collective-permute-done | bytes 131104 | tf_op jit(solution)/shard_map/ppermute | solution.py:321
  22.0 2.8 %collective-permute-done.6.v_ref = bf16[256,256]{1,0:T(8,128)(2,1)S(1)} collective-permute-done((bf16[256,256]{1,0:T(8,128)(2,1)S(1)}, bf16[256,256]{1,0:T(8,128)(2,1)S(1)}, u32[]{:S(2)}, u32[]{:S(2)}) %collective-permute-start.6) | collective-permute-done | bytes 131104 | tf_op jit(solution)/shard_map/ppermute | solution.py:321
  24.8 1.3 %collective-permute-start.7 = (bf16[256,512]{1,0:T(8,128)(2,1)S(1)}, bf16[256,512]{1,0:T(8,128)(2,1)S(1)}, u32[]{:S(2)}, u32[]{:S(2)}) collective-permute-start(bf16[256,512]{1,0:T(8,128)(2,1)S(1)} %get-tuple-element.48), channel_id=1, source_target_pairs={{0,4},{4,0},{8,12},{12,8},{16,20},{20,16},{24,28},{28,24},{1,5},{5... | collective-permute-start | bytes 786440 | tf_op jit(solution)/shard_map/ppermute | solution.py:326
  26.2 0.9 %shard_map.107 = (f32[512,256]{1,0:T(8,128)S(1)}, bf16[256,256]{1,0:T(8,128)(2,1)S(1)}) custom-call(bf16[256,256]{1,0:T(8,128)(2,1)S(1)} %collective-permute-done.5.k_ref, bf16[256,256]{1,0:T(8,128)(2,1)S(1)} %collective-permute-done.6.v_ref, bf16[256,1024]{1,0:T(8,128)(2,1)S(1)} %get-tuple-element.37.qr_ref.refs_0_, ...), custom_call_target="tpu_custom_call" | custom-call | flops 1048576 | bytes 3690000 | tf_op jit(solution)/shard_map/pallas_call | solution.py:375
  27.1 0.8 %collective-permute-start.9 = (bf16[256,256]{1,0:T(8,128)(2,1)S(1)}, bf16[256,256]{1,0:T(8,128)(2,1)S(1)}, u32[]{:S(2)}, u32[]{:S(2)}) collective-permute-start(bf16[256,256]{1,0:T(8,128)(2,1)S(1)} %get-tuple-element.63), channel_id=1, source_target_pairs={{0,4},{4,8},{8,12},{12,16},{16,20},{20,24},{24,28},{28,0},{1,5},{5... | collective-permute-start | bytes 393224 | tf_op jit(solution)/shard_map/ppermute | solution.py:321
  27.9 0.9 %shard_map.108 = (f32[512,256]{1,0:T(8,128)S(1)}, bf16[256,256]{1,0:T(8,128)(2,1)S(1)}) custom-call(bf16[256,256]{1,0:T(8,128)(2,1)S(1)} %collective-permute-done.5.k_ref, bf16[256,256]{1,0:T(8,128)(2,1)S(1)} %collective-permute-done.6.v_ref, bf16[256,1024]{1,0:T(8,128)(2,1)S(1)} %get-tuple-element.37.qr_ref.refs_0_, ...), custom_call_target="tpu_custom_call" | custom-call | flops 1048576 | bytes 3690000 | tf_op jit(solution)/shard_map/pallas_call | solution.py:375
  28.8 0.1 collective-permute-start.11
  28.9 1.6 %collective-permute-done.8.kv_ref = bf16[256,512]{1,0:T(8,128)(2,1)S(1)} collective-permute-done((bf16[256,512]{1,0:T(8,128)(2,1)S(1)}, bf16[256,512]{1,0:T(8,128)(2,1)S(1)}, u32[]{:S(2)}, u32[]{:S(2)}) %collective-permute-start.8) | collective-permute-done | bytes 262176 | tf_op jit(solution)/shard_map/ppermute | solution.py:321
  30.5 1.7 %shard_map.109 = (f32[512,256]{1,0:T(8,128)S(1)}, f32[512,256]{1,0:T(8,128)S(1)}, bf16[256,512]{1,0:T(8,128)(2,1)S(1)}) custom-call(bf16[256,512]{1,0:T(8,128)(2,1)S(1)} %collective-permute-done.8.kv_ref, bf16[256,1024]{1,0:T(8,128)(2,1)S(1)} %get-tuple-element.37.qr_ref.refs_0_, bf16[256,1024]{1,0:T(8,128)(2,1)S(1)} %get-tuple-element.38.do_ref.refs_1_, ...), custom_call_target="tpu_custom_call" | custom-call | flops 1048576 | bytes 7380000 | tf_op jit(solution)/shard_map/pallas_call | solution.py:375
  32.1 7.3 %collective-permute-done.7.swapped_ref = bf16[256,512]{1,0:T(8,128)(2,1)S(1)} collective-permute-done((bf16[256,512]{1,0:T(8,128)(2,1)S(1)}, bf16[256,512]{1,0:T(8,128)(2,1)S(1)}, u32[]{:S(2)}, u32[]{:S(2)}) %collective-permute-start.7) | collective-permute-done | bytes 262176 | tf_op jit(solution)/shard_map/ppermute | solution.py:326
  39.4 1.1 %shard_map.110 = (bf16[256,1024]{1,0:T(8,128)(2,1)}, f32[256,512]{1,0:T(8,128)S(1)}) custom-call(f32[128,256]{1,0:T(8,128)S(1)} %get-tuple-element.35.tables_ref, f32[256,512]{1,0:T(8,128)S(1)} %get-tuple-element.41.own_ref, bf16[256,512]{1,0:T(8,128)(2,1)S(1)} %collective-permute-done.7.swapped_ref, f32[512,256]{1,0:T(8,128)S(1)} %get-tuple-element.57.refs_0_, ...), custom_call_target="tpu_custom_call" | custom-call | flops 1048576 | bytes 3690000 | tf_op jit(solution)/shard_map/pallas_call | solution.py:395
  40.5 0.1 shard_map.111
  40.6 0.1 collective-permute-start.10
  40.7 0.1 shard_map.112
  40.7 0.1 collective-permute-start.12
  40.8 8.0 %collective-permute-done.10.refs_0_ = bf16[256,256]{1,0:T(8,128)(2,1)S(1)} collective-permute-done((bf16[256,256]{1,0:T(8,128)(2,1)S(1)}, bf16[256,256]{1,0:T(8,128)(2,1)S(1)}, u32[]{:S(2)}, u32[]{:S(2)}) %collective-permute-start.10) | collective-permute-done | bytes 131104 | tf_op jit(solution)/shard_map/ppermute | solution.py:321
  48.8 1.7 %collective-permute-done.12.refs_1_ = bf16[256,256]{1,0:T(8,128)(2,1)S(1)} collective-permute-done((bf16[256,256]{1,0:T(8,128)(2,1)S(1)}, bf16[256,256]{1,0:T(8,128)(2,1)S(1)}, u32[]{:S(2)}, u32[]{:S(2)}) %collective-permute-start.12) | collective-permute-done | bytes 131104 | tf_op jit(solution)/shard_map/ppermute | solution.py:321
  50.5 0.9 %shard_map.113 = (bf16[256,256]{1,0:T(8,128)(2,1)}, bf16[256,256]{1,0:T(8,128)(2,1)}) custom-call(f32[128,256]{1,0:T(8,128)S(1)} %get-tuple-element.35.tables_ref, f32[256,512]{1,0:T(8,128)S(1)} %get-tuple-element.60.own_ref, bf16[256,256]{1,0:T(8,128)(2,1)S(1)} %collective-permute-done.10.refs_0_, bf16[256,256]{1,0:T(8,128)(2,1)S(1)} %collective-permute-done.12.refs_1_), custom_call_target="tpu_custom_call" | custom-call | flops 1048576 | bytes 3690000 | tf_op jit(solution)/shard_map/pallas_call | solution.py:408
  (5 shorter events, 0.0 us)
Async XLA Ops:
  0.6 6.9 %collective-permute-start.1 = (s32[3,64]{1,0:T(4,128)}, s32[3,64]{1,0:T(4,128)S(1)}, u32[]{:S(2)}, u32[]{:S(2)}) collective-permute-start(s32[3,64]{1,0:T(4,128)} %own_ref.1), channel_id=1, source_target_pairs={{0,2},{1,3},{2,0},{3,1},{4,6},{5,7},{6,4},{7,5},{8,10},{9,11},{10,... | collective-permute-start | bytes 2312 | tf_op jit(solution)/shard_map/ppermute | solution.py:321
  0.7 6.8 %collective-permute-start = (s32[3,64]{1,0:T(4,128)}, s32[3,64]{1,0:T(4,128)S(1)}, u32[]{:S(2)}, u32[]{:S(2)}) collective-permute-start(s32[3,64]{1,0:T(4,128)} %own_ref.1), channel_id=1, source_target_pairs={{0,1},{1,2},{2,3},{3,0},{4,5},{5,6},{6,7},{7,4},{8,9},{9,10},{10,1... | collective-permute-start | bytes 2312 | tf_op jit(solution)/shard_map/ppermute | solution.py:321
  0.8 6.8 %collective-permute-start.2 = (s32[3,64]{1,0:T(4,128)}, s32[3,64]{1,0:T(4,128)S(1)}, u32[]{:S(2)}, u32[]{:S(2)}) collective-permute-start(s32[3,64]{1,0:T(4,128)} %own_ref.1), channel_id=1, source_target_pairs={{0,3},{1,0},{2,1},{3,2},{4,7},{5,4},{6,5},{7,6},{8,11},{9,8},{10,9... | collective-permute-start | bytes 2312 | tf_op jit(solution)/shard_map/ppermute | solution.py:321
  2.5 13.4 %collective-permute-start.3 = (bf16[256,256]{1,0:T(8,128)(2,1)}, bf16[256,256]{1,0:T(8,128)(2,1)S(1)}, u32[]{:S(2)}, u32[]{:S(2)}) collective-permute-start(bf16[256,256]{1,0:T(8,128)(2,1)} %v_ref.3), channel_id=1, source_target_pairs={{0,28},{4,0},{8,4},{12,8},{16,12},{20,16},{24,20},{28,24},{1,29},{... | collective-permute-start | bytes 393224 | tf_op jit(solution)/shard_map/ppermute | solution.py:321
  8.8 7.1 %collective-permute-start.4 = (bf16[256,256]{1,0:T(8,128)(2,1)S(1)}, bf16[256,256]{1,0:T(8,128)(2,1)S(1)}, u32[]{:S(2)}, u32[]{:S(2)}) collective-permute-start(bf16[256,256]{1,0:T(8,128)(2,1)S(1)} %get-tuple-element.36.k_ref), channel_id=1, source_target_pairs={{0,28},{4,0},{8,4},{12,8},{16,12},{20,16},{24,20},{28,24},{1,29},{... | collective-permute-start | bytes 393224 | tf_op jit(solution)/shard_map/ppermute | solution.py:321
  15.9 6.1 %collective-permute-start.5 = (bf16[256,256]{1,0:T(8,128)(2,1)S(1)}, bf16[256,256]{1,0:T(8,128)(2,1)S(1)}, u32[]{:S(2)}, u32[]{:S(2)}) collective-permute-start(bf16[256,256]{1,0:T(8,128)(2,1)S(1)} %collective-permute-done.4.k_ref), channel_id=1, source_target_pairs={{0,24},{4,28},{8,0},{12,4},{16,8},{20,12},{24,16},{28,20},{1,25},{... | collective-permute-start | bytes 393224 | tf_op jit(solution)/shard_map/ppermute | solution.py:321
  16.4 8.4 %collective-permute-start.6 = (bf16[256,256]{1,0:T(8,128)(2,1)S(1)}, bf16[256,256]{1,0:T(8,128)(2,1)S(1)}, u32[]{:S(2)}, u32[]{:S(2)}) collective-permute-start(bf16[256,256]{1,0:T(8,128)(2,1)S(1)} %collective-permute-done.3.v_ref), channel_id=1, source_target_pairs={{0,24},{4,28},{8,0},{12,4},{16,8},{20,12},{24,16},{28,20},{1,25},{... | collective-permute-start | bytes 393224 | tf_op jit(solution)/shard_map/ppermute | solution.py:321
  18.5 11.9 %collective-permute-start.8 = (bf16[256,512]{1,0:T(8,128)(2,1)S(1)}, bf16[256,512]{1,0:T(8,128)(2,1)S(1)}, u32[]{:S(2)}, u32[]{:S(2)}) collective-permute-start(bf16[256,512]{1,0:T(8,128)(2,1)S(1)} %get-tuple-element.50), channel_id=1, source_target_pairs={{0,24},{4,28},{8,0},{12,4},{16,8},{20,12},{24,16},{28,20},{1,25},{... | collective-permute-start | bytes 786440 | tf_op jit(solution)/shard_map/ppermute | solution.py:321
  24.8 14.6 %collective-permute-start.7 = (bf16[256,512]{1,0:T(8,128)(2,1)S(1)}, bf16[256,512]{1,0:T(8,128)(2,1)S(1)}, u32[]{:S(2)}, u32[]{:S(2)}) collective-permute-start(bf16[256,512]{1,0:T(8,128)(2,1)S(1)} %get-tuple-element.48), channel_id=1, source_target_pairs={{0,4},{4,0},{8,12},{12,8},{16,20},{20,16},{24,28},{28,24},{1,5},{5... | collective-permute-start | bytes 786440 | tf_op jit(solution)/shard_map/ppermute | solution.py:326
  27.1 13.4 %collective-permute-start.9 = (bf16[256,256]{1,0:T(8,128)(2,1)S(1)}, bf16[256,256]{1,0:T(8,128)(2,1)S(1)}, u32[]{:S(2)}, u32[]{:S(2)}) collective-permute-start(bf16[256,256]{1,0:T(8,128)(2,1)S(1)} %get-tuple-element.63), channel_id=1, source_target_pairs={{0,4},{4,8},{8,12},{12,16},{16,20},{20,24},{24,28},{28,0},{1,5},{5... | collective-permute-start | bytes 393224 | tf_op jit(solution)/shard_map/ppermute | solution.py:321
  28.8 11.9 %collective-permute-start.11 = (bf16[256,256]{1,0:T(8,128)(2,1)S(1)}, bf16[256,256]{1,0:T(8,128)(2,1)S(1)}, u32[]{:S(2)}, u32[]{:S(2)}) collective-permute-start(bf16[256,256]{1,0:T(8,128)(2,1)S(1)} %get-tuple-element.64), channel_id=1, source_target_pairs={{0,4},{4,8},{8,12},{12,16},{16,20},{20,24},{24,28},{28,0},{1,5},{5... | collective-permute-start | bytes 393224 | tf_op jit(solution)/shard_map/ppermute | solution.py:321
  40.6 8.2 %collective-permute-start.10 = (bf16[256,256]{1,0:T(8,128)(2,1)S(1)}, bf16[256,256]{1,0:T(8,128)(2,1)S(1)}, u32[]{:S(2)}, u32[]{:S(2)}) collective-permute-start(bf16[256,256]{1,0:T(8,128)(2,1)S(1)} %shard_map.111), channel_id=1, source_target_pairs={{0,8},{4,12},{8,16},{12,20},{16,24},{20,28},{24,0},{28,4},{1,9},{5... | collective-permute-start | bytes 393224 | tf_op jit(solution)/shard_map/ppermute | solution.py:321
  40.7 9.8 %collective-permute-start.12 = (bf16[256,256]{1,0:T(8,128)(2,1)S(1)}, bf16[256,256]{1,0:T(8,128)(2,1)S(1)}, u32[]{:S(2)}, u32[]{:S(2)}) collective-permute-start(bf16[256,256]{1,0:T(8,128)(2,1)S(1)} %shard_map.112), channel_id=1, source_target_pairs={{0,8},{4,12},{8,16},{12,20},{16,24},{20,28},{24,0},{28,4},{1,9},{5... | collective-permute-start | bytes 393224 | tf_op jit(solution)/shard_map/ppermute | solution.py:321

commit v12 on v11

--- a/solution.py
+++ b/solution.py
@@ -184,11 +184,10 @@
     norm_ref[...] = lse_ref[...] * LOG2E
 
 
-def hop_kernel(step, wanted, started, k_ref, v_ref, *refs):
-    qr_ref, do_ref, norm_ref, delta_ref, flag_ref = refs[:5]
+def hop_kernel(step, wanted, *refs):
     count = len(wanted)
-    dqt_ins = refs[5 : 5 + count] if started else [None] * count
-    dqt_refs, part_ref = refs[-count - 1 : -1], refs[-1]
+    dqt_ins, dqt_refs, part_ref = refs[:count], refs[-count - 1 : -1], refs[-1]
+    k_ref, v_ref, qr_ref, do_ref, norm_ref, delta_ref, flag_ref = refs[count : -count - 1]
     rows = qr_ref.shape[0]
     half = rows // 2
     heads = qr_ref.shape[1] // HEAD
@@ -211,11 +210,8 @@
                     norm[h : h + 1, queries.start :], delta[h : h + 1, queries.start :], False,
                 )
                 if queries.start:
-                    before = jnp.zeros((HEAD, queries.start), F32)
-                    if dqt_in is not None:
-                        before = dqt_in[to, : queries.start]
-                    dqt_ref[to, : queries.start] = before
-                dqt_ref[to, queries] = q_part if dqt_in is None else dqt_in[to, queries] + q_part
+                    dqt_ref[to, : queries.start] = dqt_in[to, : queries.start]
+                dqt_ref[to, queries] = dqt_in[to, queries] + q_part
                 dv = v_part if dv is None else dv + v_part
                 dk = k_part if dk is None else dk + k_part
             part_ref[keys, pl.ds(2 * i * HEAD, HEAD)] = dk.astype(BF16)
@@ -232,9 +228,19 @@
         run(slice(0, rows), slice(half, rows))
 
 
-def merged_kernel(step, wanted, started, kv_ref, *refs):
+def merged_kernel(step, wanted, *refs):
+    count = len(wanted)
+    kv_ref = refs[count]
     width = kv_ref.shape[1] // 2
-    hop_kernel(step, wanted, started, kv_ref.at[:, :width], kv_ref.at[:, width:], *refs)
+    hop_kernel(
+        step, wanted, *refs[:count], kv_ref.at[:, :width], kv_ref.at[:, width:], *refs[count + 1 :]
+    )
+
+
+def beside_kernel(k_ref, v_ref, kv_ref):
+    width = k_ref.shape[1]
+    kv_ref[:, :width] = k_ref[...]
+    kv_ref[:, width:] = v_ref[...]
 
 
 def own_kernel(groups, k_ref, v_ref, qr_ref, do_ref, norm_ref, delta_ref, *refs):
@@ -260,8 +266,9 @@
         part_ref[:, pl.ds((2 * g + 1) * HEAD, HEAD)] = dv
 
 
-def query_kernel(groups, tables_ref, own_ref, swapped_ref, *refs):
-    dqt_refs, out_ref, sum_ref = refs[:groups], refs[groups], refs[groups + 1]
+def query_kernel(groups, tables_ref, *refs):
+    dqt_refs = refs[:groups]
+    own_ref, swapped_ref, out_ref, sum_ref = refs[groups:]
     odd = (lax.axis_index("ctx") & 1) == 1
     sum_ref[...] = own_ref[...] + jnp.where(odd, swapped_ref[...].astype(F32), 0.0)
     cosine_t = tables_ref[:HALF, :] * ROOT_SCALE
@@ -373,30 +380,29 @@
         count = len(wanted)
         before = [dqs[g] for g in wanted]
         *new, part = call(
-            functools.partial(kernel, step, wanted, True),
+            functools.partial(kernel, step, wanted),
             [((wide_q // groups, rows), F32)] * count + [((rows, 2 * HEAD * count), BF16)],
             [VMEM] * (5 + len(arrived) + count),
             micros=count,
-        )(*arrived, *shared, *before)
+        )(*before, *arrived, *shared)
         for g, dq in zip(wanted, new):
             dqs[g] = dq
         return part
 
-    v1, k1, _ = lax.optimization_barrier((v1, k1, own))
-    v3 = shifted(v1, -2)
-    k3 = shifted(k1, -2)
-    part1 = hop(hop_kernel, 1, every, k1, v1)
+    k1, _ = lax.optimization_barrier((k1, own))
+    (kv1,) = call(beside_kernel, [((rows, 2 * wide_k), BF16)], [VMEM] * 2)(k1, v1)
+    kv3 = shifted(kv1, -2)
+    part1 = hop(merged_kernel, 1, every, kv1)
     held, _ = lax.optimization_barrier((kv, part1))
     kv2 = shifted(held, -2)
-    part1, k3, v3 = lax.optimization_barrier((part1, k3, v3))
     swapped = exchanged(part1)
-    moved = [shifted(hop(hop_kernel, 3, (g,), k3, v3), 1) for g in every]
+    moved = [shifted(hop(merged_kernel, 3, (g,), kv3), 1) for g in every]
     part2 = hop(merged_kernel, 2, every, kv2)
     dq, own = call(
         functools.partial(query_kernel, groups),
         [((rows, wide_q), BF16), ((rows, 2 * wide_k), F32)],
         [VMEM] * (3 + groups),
-    )(tables, own, swapped, *dqs)
+    )(tables, *dqs, own, swapped)
     part2, _ = lax.optimization_barrier((part2, own))
     home = []
     for g in every:

time: 51.6 us -> 51.3 us (level)
  the two profiles are of different devices: /device:TPU:2 before, /device:TPU:0 now
where the time goes in v12:
time: 51.3 us; the launch traced here: 51.1 us
  starting transfers between devices  23.6 us (46%)
  Pallas kernels  14.1 us (27%)
  waiting for transfers between devices  12.8 us (25%)
  between operations  0.72 us (1%)
    ppermute x11, starting transfers between devices, shifted(): return lax.ppermute(value, axis, pairs)  19.7 us
    ppermute x11, waiting for transfers between devices, shifted(): return lax.ppermute(value, axis, pairs)  12.8 us
    pallas_call x4, Pallas kernels, hop(): call(functools.partial(kernel, step, wanted), [((wide_q // groups, rows),...  5.16 us
    ppermute x1, starting transfers between devices, exchanged(): lax.ppermute(value, 'ctx', [(source, source ^ 1) for source in range(coun...  3.84 us
    pallas_call x1, Pallas kernels, shards(): call(functools.partial(own_kernel, groups), [((wide_q // groups, rows), F...  3.07 us
    pallas_call x1, Pallas kernels, shards(): call(functools.partial(prep_kernel, groups), [((rows, wide_q), BF16)] * 2...  2.42 us
    pallas_call x1, Pallas kernels, shards(): call(key_kernel, [((rows, wide_k), BF16), ((rows, 2 * wide_k), BF16), ((H...  1.3 us
    pallas_call x1, Pallas kernels, shards(): call(functools.partial(query_kernel, groups), [((rows, wide_q), BF16), ((...  1.1 us
  transfers between devices with their start and end apart: 12, of which 6 were waited for; matrix products, arithmetic and copies ran while one was open for 0% of the time, Pallas kernels for 23%

profile of v12, /device:TPU:0, one launch (start us, length us, event | category | flops | bytes accessed | tf_op | source)
XLA Modules:
  0.0 51.1 jit_solution(8224209204319731396)
XLA Ops:
  0.6 0.0 copy-start
  0.6 3.0 %collective-permute-start.1 = (s32[3,64]{1,0:T(4,128)}, s32[3,64]{1,0:T(4,128)S(1)}, u32[]{:S(2)}, u32[]{:S(2)}) collective-permute-start(s32[3,64]{1,0:T(4,128)} %own_ref.1), channel_id=1, source_target_pairs={{0,2},{1,3},{2,0},{3,1},{4,6},{5,7},{6,4},{7,5},{8,10},{9,11},{10,... | collective-permute-start | bytes 2312 | tf_op jit(solution)/shard_map/ppermute | solution.py:328
  3.6 0.0 collective-permute-start
  3.6 1.7 %collective-permute-start.2 = (s32[3,64]{1,0:T(4,128)}, s32[3,64]{1,0:T(4,128)S(1)}, u32[]{:S(2)}, u32[]{:S(2)}) collective-permute-start(s32[3,64]{1,0:T(4,128)} %own_ref.1), channel_id=1, source_target_pairs={{0,3},{1,0},{2,1},{3,2},{4,7},{5,4},{6,5},{7,6},{8,11},{9,8},{10,9... | collective-permute-start | bytes 2312 | tf_op jit(solution)/shard_map/ppermute | solution.py:328
  5.4 0.0 collective-permute-done.1.p2_ref
  5.4 1.4 %collective-permute-done.p1_ref = s32[3,64]{1,0:T(4,128)S(1)} collective-permute-done((s32[3,64]{1,0:T(4,128)}, s32[3,64]{1,0:T(4,128)S(1)}, u32[]{:S(2)}, u32[]{:S(2)}) %collective-permute-start) | collective-permute-done | bytes 800 | tf_op jit(solution)/shard_map/ppermute | solution.py:328
  6.9 0.0 collective-permute-done.2.p3_ref
  6.9 1.3 %shard_map.103 = (bf16[256,256]{1,0:T(8,128)(2,1)S(1)}, bf16[256,512]{1,0:T(8,128)(2,1)S(1)}, f32[128,256]{1,0:T(8,128)S(1)}) custom-call(s32[3,64]{1,0:T(4,128)} %own_ref.1, s32[3,64]{1,0:T(4,128)S(1)} %collective-permute-done.p1_ref, s32[3,64]{1,0:T(4,128)S(1)} %collective-permute-done.1.p2_ref, s32[3,64]{1,0:T(4,128)S(1)} %collective-permute-done.2.p3_ref, ...), custom_call_target="tpu_custom_call" | custom-call | flops 1048576 | bytes 3690000 | tf_op jit(solution)/shard_map/pallas_call | solution.py:354
  8.2 4.6 %collective-permute-start.3 = (bf16[256,256]{1,0:T(8,128)(2,1)S(1)}, bf16[256,256]{1,0:T(8,128)(2,1)S(1)}, u32[]{:S(2)}, u32[]{:S(2)}) collective-permute-start(bf16[256,256]{1,0:T(8,128)(2,1)S(1)} %get-tuple-element.32.k_ref), channel_id=1, source_target_pairs={{0,28},{4,0},{8,4},{12,8},{16,12},{20,16},{24,20},{28,24},{1,29},{... | collective-permute-start | bytes 393224 | tf_op jit(solution)/shard_map/ppermute | solution.py:328
  12.8 0.5 collective-permute-start.4
  13.3 2.4 %shard_map.104 = (bf16[256,1024]{1,0:T(8,128)(2,1)S(1)}, bf16[256,1024]{1,0:T(8,128)(2,1)S(1)}, f32[8,256]{1,0:T(8,128)S(1)}, f32[8,256]{1,0:T(8,128)S(1)}, s32[8,128]{1,0:T(8,128)S(1)}) custom-call(s32[8]{0:T(128)} %span_ref.1, f32[128,256]{1,0:T(8,128)S(1)} %get-tuple-element.31.tables_ref, f32[8,256]{1,0:T(8,128)} %lse_hbm.1, bf16[256,1024]{1,0:T(8,128)(2,1)} %q_hbm.1, ...), custom_call_target="tpu_custom_call" | custom-call | flops 1048576 | bytes 7380000 | tf_op jit(solution)/shard_map/pallas_call | solution.py:360
  15.8 3.1 %shard_map.105 = (f32[512,256]{1,0:T(8,128)S(1)}, f32[512,256]{1,0:T(8,128)S(1)}, f32[256,512]{1,0:T(8,128)S(1)}) custom-call(bf16[256,256]{1,0:T(8,128)(2,1)S(1)} %get-tuple-element.32.k_ref, bf16[256,256]{1,0:T(8,128)(2,1)} %v_ref.3, bf16[256,1024]{1,0:T(8,128)(2,1)S(1)} %get-tuple-element.33.qr_ref.refs_3_.refs_2_, ...), custom_call_target="tpu_custom_call" | custom-call | flops 1048576 | bytes 11070000 | tf_op jit(solution)/shard_map/pallas_call | solution.py:372
  18.8 0.3 collective-permute-done.4.v_ref
  19.2 1.6 %collective-permute-start.5 = (bf16[256,512]{1,0:T(8,128)(2,1)S(1)}, bf16[256,512]{1,0:T(8,128)(2,1)S(1)}, u32[]{:S(2)}, u32[]{:S(2)}) collective-permute-start(bf16[256,512]{1,0:T(8,128)(2,1)S(1)} %shard_map.106.refs_2_), channel_id=1, source_target_pairs={{0,24},{4,28},{8,0},{12,4},{16,8},{20,12},{24,16},{28,20},{1,25},{... | collective-permute-start | bytes 786440 | tf_op jit(solution)/shard_map/ppermute | solution.py:328
  20.8 1.6 %shard_map.107 = (f32[512,256]{1,0:T(8,128)S(1)}, f32[512,256]{1,0:T(8,128)S(1)}, bf16[256,512]{1,0:T(8,128)(2,1)S(1)}) custom-call(f32[512,256]{1,0:T(8,128)S(1)} %get-tuple-element.37.refs_0_, f32[512,256]{1,0:T(8,128)S(1)} %get-tuple-element.38.refs_1_, bf16[256,512]{1,0:T(8,128)(2,1)S(1)} %shard_map.106.refs_2_, ...), custom_call_target="tpu_custom_call" | custom-call | flops 1048576 | bytes 7380000 | tf_op jit(solution)/shard_map/pallas_call | solution.py:382
  22.4 0.5 collective-permute-start.6
  22.9 3.8 %collective-permute-start.7 = (bf16[256,512]{1,0:T(8,128)(2,1)S(1)}, bf16[256,512]{1,0:T(8,128)(2,1)S(1)}, u32[]{:S(2)}, u32[]{:S(2)}) collective-permute-start(bf16[256,512]{1,0:T(8,128)(2,1)S(1)} %get-tuple-element.47), channel_id=1, source_target_pairs={{0,4},{4,0},{8,12},{12,8},{16,20},{20,16},{24,28},{28,24},{1,5},{5... | collective-permute-start | bytes 786440 | tf_op jit(solution)/shard_map/ppermute | solution.py:333
  26.8 1.7 %collective-permute-done.5.refs_1_ = bf16[256,512]{1,0:T(8,128)(2,1)S(1)} collective-permute-done((bf16[256,512]{1,0:T(8,128)(2,1)S(1)}, bf16[256,512]{1,0:T(8,128)(2,1)S(1)}, u32[]{:S(2)}, u32[]{:S(2)}) %collective-permute-start.5) | collective-permute-done | bytes 262176 | tf_op jit(solution)/shard_map/ppermute | solution.py:328
  28.4 0.9 %shard_map.109 = (f32[512,256]{1,0:T(8,128)S(1)}, bf16[256,256]{1,0:T(8,128)(2,1)S(1)}) custom-call(f32[512,256]{1,0:T(8,128)S(1)} %get-tuple-element.44.refs_0_, bf16[256,512]{1,0:T(8,128)(2,1)S(1)} %collective-permute-done.5.refs_1_, bf16[256,1024]{1,0:T(8,128)(2,1)S(1)} %get-tuple-element.33.qr_ref.refs_3_.refs_2_, ...), custom_call_target="tpu_custom_call" | custom-call | flops 1048576 | bytes 3690000 | tf_op jit(solution)/shard_map/pallas_call | solution.py:382
  29.4 3.4 %collective-permute-start.10 = (bf16[256,256]{1,0:T(8,128)(2,1)S(1)}, bf16[256,256]{1,0:T(8,128)(2,1)S(1)}, u32[]{:S(2)}, u32[]{:S(2)}) collective-permute-start(bf16[256,256]{1,0:T(8,128)(2,1)S(1)} %get-tuple-element.56), channel_id=1, source_target_pairs={{0,4},{4,8},{8,12},{12,16},{16,20},{20,24},{24,28},{28,0},{1,5},{5... | collective-permute-start | bytes 393224 | tf_op jit(solution)/shard_map/ppermute | solution.py:328
  32.7 0.9 %shard_map.108 = (f32[512,256]{1,0:T(8,128)S(1)}, bf16[256,256]{1,0:T(8,128)(2,1)S(1)}) custom-call(f32[512,256]{1,0:T(8,128)S(1)} %get-tuple-element.42.refs_0_, bf16[256,512]{1,0:T(8,128)(2,1)S(1)} %collective-permute-done.5.refs_1_, bf16[256,1024]{1,0:T(8,128)(2,1)S(1)} %get-tuple-element.33.qr_ref.refs_3_.refs_2_, ...), custom_call_target="tpu_custom_call" | custom-call | flops 1048576 | bytes 3690000 | tf_op jit(solution)/shard_map/pallas_call | solution.py:382
  33.7 0.1 collective-permute-start.8
  33.7 1.7 %shard_map.110 = (f32[512,256]{1,0:T(8,128)S(1)}, f32[512,256]{1,0:T(8,128)S(1)}, bf16[256,512]{1,0:T(8,128)(2,1)S(1)}) custom-call(f32[512,256]{1,0:T(8,128)S(1)} %get-tuple-element.43.refs_0_, f32[512,256]{1,0:T(8,128)S(1)} %get-tuple-element.45.refs_1_, bf16[256,512]{1,0:T(8,128)(2,1)S(1)} %collective-permute-done.6.refs_2_, ...), custom_call_target="tpu_custom_call" | custom-call | flops 1048576 | bytes 7380000 | tf_op jit(solution)/shard_map/pallas_call | solution.py:382
  35.4 1.1 %shard_map.111 = (bf16[256,1024]{1,0:T(8,128)(2,1)}, f32[256,512]{1,0:T(8,128)S(1)}) custom-call(f32[128,256]{1,0:T(8,128)S(1)} %get-tuple-element.31.tables_ref, f32[512,256]{1,0:T(8,128)S(1)} %get-tuple-element.49.refs_0_, f32[512,256]{1,0:T(8,128)S(1)} %get-tuple-element.50.refs_1_, f32[256,512]{1,0:T(8,128)S(1)} %get-tuple-element.39.refs_2_, ...), custom_call_target="tpu_custom_call" | custom-call | flops 1048576 | bytes 3690000 | tf_op jit(solution)/shard_map/pallas_call | solution.py:401
  36.5 4.1 %collective-permute-done.10.three_ref = bf16[256,256]{1,0:T(8,128)(2,1)S(1)} collective-permute-done((bf16[256,256]{1,0:T(8,128)(2,1)S(1)}, bf16[256,256]{1,0:T(8,128)(2,1)S(1)}, u32[]{:S(2)}, u32[]{:S(2)}) %collective-permute-start.10) | collective-permute-done | bytes 131104 | tf_op jit(solution)/shard_map/ppermute | solution.py:328
  40.6 0.1 shard_map.113
  40.6 1.6 %collective-permute-start.11 = (bf16[256,256]{1,0:T(8,128)(2,1)S(1)}, bf16[256,256]{1,0:T(8,128)(2,1)S(1)}, u32[]{:S(2)}, u32[]{:S(2)}) collective-permute-start(bf16[256,256]{1,0:T(8,128)(2,1)S(1)} %shard_map.113), channel_id=1, source_target_pairs={{0,8},{4,12},{8,16},{12,20},{16,24},{20,28},{24,0},{28,4},{1,9},{5... | collective-permute-start | bytes 393224 | tf_op jit(solution)/shard_map/ppermute | solution.py:328
  42.2 0.1 shard_map.112
  42.3 2.7 %collective-permute-start.9 = (bf16[256,256]{1,0:T(8,128)(2,1)S(1)}, bf16[256,256]{1,0:T(8,128)(2,1)S(1)}, u32[]{:S(2)}, u32[]{:S(2)}) collective-permute-start(bf16[256,256]{1,0:T(8,128)(2,1)S(1)} %shard_map.112), channel_id=1, source_target_pairs={{0,8},{4,12},{8,16},{12,20},{16,24},{20,28},{24,0},{28,4},{1,9},{5... | collective-permute-start | bytes 393224 | tf_op jit(solution)/shard_map/ppermute | solution.py:328
  45.0 3.3 %collective-permute-done.11.refs_1_ = bf16[256,256]{1,0:T(8,128)(2,1)S(1)} collective-permute-done((bf16[256,256]{1,0:T(8,128)(2,1)S(1)}, bf16[256,256]{1,0:T(8,128)(2,1)S(1)}, u32[]{:S(2)}, u32[]{:S(2)}) %collective-permute-start.11) | collective-permute-done | bytes 131104 | tf_op jit(solution)/shard_map/ppermute | solution.py:328
  48.4 1.9 %collective-permute-done.9.refs_0_ = bf16[256,256]{1,0:T(8,128)(2,1)S(1)} collective-permute-done((bf16[256,256]{1,0:T(8,128)(2,1)S(1)}, bf16[256,256]{1,0:T(8,128)(2,1)S(1)}, u32[]{:S(2)}, u32[]{:S(2)}) %collective-permute-start.9) | collective-permute-done | bytes 131104 | tf_op jit(solution)/shard_map/ppermute | solution.py:328
  50.2 0.9 %shard_map.114 = (bf16[256,256]{1,0:T(8,128)(2,1)}, bf16[256,256]{1,0:T(8,128)(2,1)}) custom-call(f32[128,256]{1,0:T(8,128)S(1)} %get-tuple-element.31.tables_ref, f32[256,512]{1,0:T(8,128)S(1)} %get-tuple-element.52.own_ref, bf16[256,256]{1,0:T(8,128)(2,1)S(1)} %collective-permute-done.9.refs_0_, bf16[256,256]{1,0:T(8,128)(2,1)S(1)} %collective-permute-done.11.refs_1_), custom_call_target="tpu_custom_call" | custom-call | flops 1048576 | bytes 3690000 | tf_op jit(solution)/shard_map/pallas_call | solution.py:414
  (6 shorter events, 0.0 us)
Async XLA Ops:
  0.6 12.2 %copy-start = (bf16[256,256]{1,0:T(8,128)(2,1)S(1)}, bf16[256,256]{1,0:T(8,128)(2,1)}, u32[]{:S(2)}) copy-start(bf16[256,256]{1,0:T(8,128)(2,1)} %v_ref.3) | copy-start | bytes 393220
  0.6 4.8 %collective-permute-start.1 = (s32[3,64]{1,0:T(4,128)}, s32[3,64]{1,0:T(4,128)S(1)}, u32[]{:S(2)}, u32[]{:S(2)}) collective-permute-start(s32[3,64]{1,0:T(4,128)} %own_ref.1), channel_id=1, source_target_pairs={{0,2},{1,3},{2,0},{3,1},{4,6},{5,7},{6,4},{7,5},{8,10},{9,11},{10,... | collective-permute-start | bytes 2312 | tf_op jit(solution)/shard_map/ppermute | solution.py:328
  3.6 3.2 %collective-permute-start = (s32[3,64]{1,0:T(4,128)}, s32[3,64]{1,0:T(4,128)S(1)}, u32[]{:S(2)}, u32[]{:S(2)}) collective-permute-start(s32[3,64]{1,0:T(4,128)} %own_ref.1), channel_id=1, source_target_pairs={{0,1},{1,2},{2,3},{3,0},{4,5},{5,6},{6,7},{7,4},{8,9},{9,10},{10,1... | collective-permute-start | bytes 2312 | tf_op jit(solution)/shard_map/ppermute | solution.py:328
  3.6 3.3 %collective-permute-start.2 = (s32[3,64]{1,0:T(4,128)}, s32[3,64]{1,0:T(4,128)S(1)}, u32[]{:S(2)}, u32[]{:S(2)}) collective-permute-start(s32[3,64]{1,0:T(4,128)} %own_ref.1), channel_id=1, source_target_pairs={{0,3},{1,0},{2,1},{3,2},{4,7},{5,4},{6,5},{7,6},{8,11},{9,8},{10,9... | collective-permute-start | bytes 2312 | tf_op jit(solution)/shard_map/ppermute | solution.py:328
  8.2 10.6 %collective-permute-start.3 = (bf16[256,256]{1,0:T(8,128)(2,1)S(1)}, bf16[256,256]{1,0:T(8,128)(2,1)S(1)}, u32[]{:S(2)}, u32[]{:S(2)}) collective-permute-start(bf16[256,256]{1,0:T(8,128)(2,1)S(1)} %get-tuple-element.32.k_ref), channel_id=1, source_target_pairs={{0,28},{4,0},{8,4},{12,8},{16,12},{20,16},{24,20},{28,24},{1,29},{... | collective-permute-start | bytes 393224 | tf_op jit(solution)/shard_map/ppermute | solution.py:328
  12.8 6.3 %collective-permute-start.4 = (bf16[256,256]{1,0:T(8,128)(2,1)S(1)}, bf16[256,256]{1,0:T(8,128)(2,1)S(1)}, u32[]{:S(2)}, u32[]{:S(2)}) collective-permute-start(bf16[256,256]{1,0:T(8,128)(2,1)S(1)} %copy-done), channel_id=1, source_target_pairs={{0,28},{4,0},{8,4},{12,8},{16,12},{20,16},{24,20},{28,24},{1,29},{... | collective-permute-start | bytes 393224 | tf_op jit(solution)/shard_map/ppermute | solution.py:328
  19.2 9.2 %collective-permute-start.5 = (bf16[256,512]{1,0:T(8,128)(2,1)S(1)}, bf16[256,512]{1,0:T(8,128)(2,1)S(1)}, u32[]{:S(2)}, u32[]{:S(2)}) collective-permute-start(bf16[256,512]{1,0:T(8,128)(2,1)S(1)} %shard_map.106.refs_2_), channel_id=1, source_target_pairs={{0,24},{4,28},{8,0},{12,4},{16,8},{20,12},{24,16},{28,20},{1,25},{... | collective-permute-start | bytes 786440 | tf_op jit(solution)/shard_map/ppermute | solution.py:328
  22.4 11.3 %collective-permute-start.6 = (bf16[256,512]{1,0:T(8,128)(2,1)S(1)}, bf16[256,512]{1,0:T(8,128)(2,1)S(1)}, u32[]{:S(2)}, u32[]{:S(2)}) collective-permute-start(bf16[256,512]{1,0:T(8,128)(2,1)S(1)} %get-tuple-element.48), channel_id=1, source_target_pairs={{0,24},{4,28},{8,0},{12,4},{16,8},{20,12},{24,16},{28,20},{1,25},{... | collective-permute-start | bytes 786440 | tf_op jit(solution)/shard_map/ppermute | solution.py:328
  22.9 12.5 %collective-permute-start.7 = (bf16[256,512]{1,0:T(8,128)(2,1)S(1)}, bf16[256,512]{1,0:T(8,128)(2,1)S(1)}, u32[]{:S(2)}, u32[]{:S(2)}) collective-permute-start(bf16[256,512]{1,0:T(8,128)(2,1)S(1)} %get-tuple-element.47), channel_id=1, source_target_pairs={{0,4},{4,0},{8,12},{12,8},{16,20},{20,16},{24,28},{28,24},{1,5},{5... | collective-permute-start | bytes 786440 | tf_op jit(solution)/shard_map/ppermute | solution.py:333
  29.4 11.2 %collective-permute-start.10 = (bf16[256,256]{1,0:T(8,128)(2,1)S(1)}, bf16[256,256]{1,0:T(8,128)(2,1)S(1)}, u32[]{:S(2)}, u32[]{:S(2)}) collective-permute-start(bf16[256,256]{1,0:T(8,128)(2,1)S(1)} %get-tuple-element.56), channel_id=1, source_target_pairs={{0,4},{4,8},{8,12},{12,16},{16,20},{20,24},{24,28},{28,0},{1,5},{5... | collective-permute-start | bytes 393224 | tf_op jit(solution)/shard_map/ppermute | solution.py:328
  33.7 8.6 %collective-permute-start.8 = (bf16[256,256]{1,0:T(8,128)(2,1)S(1)}, bf16[256,256]{1,0:T(8,128)(2,1)S(1)}, u32[]{:S(2)}, u32[]{:S(2)}) collective-permute-start(bf16[256,256]{1,0:T(8,128)(2,1)S(1)} %get-tuple-element.55), channel_id=1, source_target_pairs={{0,4},{4,8},{8,12},{12,16},{16,20},{20,24},{24,28},{28,0},{1,5},{5... | collective-permute-start | bytes 393224 | tf_op jit(solution)/shard_map/ppermute | solution.py:328
  40.6 7.7 %collective-permute-start.11 = (bf16[256,256]{1,0:T(8,128)(2,1)S(1)}, bf16[256,256]{1,0:T(8,128)(2,1)S(1)}, u32[]{:S(2)}, u32[]{:S(2)}) collective-permute-start(bf16[256,256]{1,0:T(8,128)(2,1)S(1)} %shard_map.113), channel_id=1, source_target_pairs={{0,8},{4,12},{8,16},{12,20},{16,24},{20,28},{24,0},{28,4},{1,9},{5... | collective-permute-start | bytes 393224 | tf_op jit(solution)/shard_map/ppermute | solution.py:328
  42.3 7.9 %collective-permute-start.9 = (bf16[256,256]{1,0:T(8,128)(2,1)S(1)}, bf16[256,256]{1,0:T(8,128)(2,1)S(1)}, u32[]{:S(2)}, u32[]{:S(2)}) collective-permute-start(bf16[256,256]{1,0:T(8,128)(2,1)S(1)} %shard_map.112), channel_id=1, source_target_pairs={{0,8},{4,12},{8,16},{12,20},{16,24},{20,28},{24,0},{28,4},{1,9},{5... | collective-permute-start | bytes 393224 | tf_op jit(solution)/shard_map/ppermute | solution.py:328

commit v13 on v12

--- a/solution.py
+++ b/solution.py
@@ -118,7 +118,9 @@
     return value_part, key_part, query_part
 
 
-def key_kernel(own_ref, p1_ref, p2_ref, p3_ref, k_ref, v_ref, kr_ref, kv_ref, tables_ref):
+def key_kernel(
+    own_ref, p1_ref, p2_ref, p3_ref, k_ref, v_ref, kr_ref, kv_ref, tables_ref, packed_ref
+):
     pieces = (own_ref[...], p1_ref[...], p2_ref[...], p3_ref[...])
     count = len(pieces)
     head = lax.axis_index("head")
@@ -129,7 +131,12 @@
         for r in range(1, count):
             part = jnp.where(back == r, pieces[r], part)
         parts.append(part)
-    cosine_t, sine_t = tables_transposed(jnp.concatenate(parts, axis=1))
+    place = jnp.concatenate(parts, axis=1)
+    spare = jnp.zeros((packed_ref.shape[0] - 6, place.shape[1]), F32)
+    packed_ref[...] = jnp.concatenate(
+        [(place >> 6).astype(F32), (place & 63).astype(F32), spare], axis=0
+    ).astype(BF16)
+    cosine_t, sine_t = tables_transposed(place.astype(F32))
     tables_ref[:HALF, :] = cosine_t
     tables_ref[HALF:, :] = sine_t
     wide, signed = row_tables(cosine_t, sine_t)
@@ -237,6 +244,21 @@
     )
 
 
+def raw_kernel(step, wanted, *refs):
+    *refs, key_ref = refs
+    count = len(wanted)
+    kv_ref, packed_ref = refs[count : count + 2]
+    width = kv_ref.shape[1] // 2
+    place = packed_ref[...].astype(F32)
+    wide, signed = row_tables(*tables_transposed(place[0:3] * 64.0 + place[3:6]))
+    for g in wanted:
+        cols = pl.ds(g * HEAD, HEAD)
+        key_ref[:, cols] = rotated(kv_ref[:, cols].astype(F32), wide, signed).astype(BF16)
+    hop_kernel(
+        step, wanted, *refs[:count], key_ref, kv_ref.at[:, width:], *refs[count + 2 :]
+    )
+
+
 def beside_kernel(k_ref, v_ref, kv_ref):
     width = k_ref.shape[1]
     kv_ref[:, :width] = k_ref[...]
@@ -350,13 +372,25 @@
     groups = wide_k // HEAD
     every = tuple(range(groups))
 
+    k1 = shifted(k, -1)
     v1 = shifted(v, -1)
-    kr, kv, tables = call(
+    kr, kv, tables, packed = call(
         key_kernel,
-        [((rows, wide_k), BF16), ((rows, 2 * wide_k), BF16), ((HEAD, rows), F32)],
+        [
+            ((rows, wide_k), BF16),
+            ((rows, 2 * wide_k), BF16),
+            ((HEAD, rows), F32),
+            ((16, rows), BF16),
+        ],
         [VMEM] * 6,
     )(*pieces, k_here, v_here)
-    k1 = shifted(kr, -1)
+    packed1 = shifted(packed, -1)
+    packed3 = shifted(packed, -3)
+    turned, k1, v1, packed1, packed3 = lax.optimization_barrier(
+        (tables, k1, v1, packed1, packed3)
+    )
+    (kv1,) = call(beside_kernel, [((rows, 2 * wide_k), BF16)], [VMEM] * 2)(k1, v1)
+    kv3 = shifted(kv1, -2)
     shared = call(
         functools.partial(prep_kernel, groups),
         [((rows, wide_q), BF16)] * 2 + [((heads, rows), F32)] * 2 + [((8, HEAD), jnp.int32)],
@@ -368,7 +402,7 @@
             pltpu.SemaphoreType.DMA((3 * groups + 1,)),
         ],
         micros=2,
-    )(span_map, tables, lse, q, do, at)
+    )(span_map, turned, lse, q, do, at)
     *dqs, own = call(
         functools.partial(own_kernel, groups),
         [((wide_q // groups, rows), F32)] * groups + [((rows, 2 * wide_k), F32)],
@@ -376,28 +410,27 @@
         micros=3,
     )(kr, v_here, *shared[:4])
 
-    def hop(kernel, step, wanted, *arrived):
+    def hop(kernel, step, wanted, arrived, scratch=()):
         count = len(wanted)
         before = [dqs[g] for g in wanted]
         *new, part = call(
             functools.partial(kernel, step, wanted),
             [((wide_q // groups, rows), F32)] * count + [((rows, 2 * HEAD * count), BF16)],
             [VMEM] * (5 + len(arrived) + count),
+            scratch,
             micros=count,
         )(*before, *arrived, *shared)
         for g, dq in zip(wanted, new):
             dqs[g] = dq
         return part
 
-    k1, _ = lax.optimization_barrier((k1, own))
-    (kv1,) = call(beside_kernel, [((rows, 2 * wide_k), BF16)], [VMEM] * 2)(k1, v1)
-    kv3 = shifted(kv1, -2)
-    part1 = hop(merged_kernel, 1, every, kv1)
-    held, _ = lax.optimization_barrier((kv, part1))
+    held, _ = lax.optimization_barrier((kv, own))
     kv2 = shifted(held, -2)
+    turned_key = [pltpu.VMEM((rows, wide_k), BF16)]
+    part1 = hop(raw_kernel, 1, every, (kv1, packed1), turned_key)
     swapped = exchanged(part1)
-    moved = [shifted(hop(merged_kernel, 3, (g,), kv3), 1) for g in every]
-    part2 = hop(merged_kernel, 2, every, kv2)
+    moved = [shifted(hop(raw_kernel, 3, (g,), (kv3, packed3), turned_key), 1) for g in every]
+    part2 = hop(merged_kernel, 2, every, (kv2,))
     dq, own = call(
         functools.partial(query_kernel, groups),
         [((rows, wide_q), BF16), ((rows, 2 * wide_k), F32)],

time: 51.3 us -> 52.8 us (1.029)
  waiting for transfers between devices: 12.8 us -> 17.9 us
  starting transfers between devices: 23.6 us -> 19.2 us
  Pallas kernels: 14.1 us -> 14.8 us
    ppermute x1, waiting for transfers between devices: 0.01 us -> 5.04 us  [exchanged(): lax.ppermute(value, 'ctx', [(source, source ^ 1) for source in range(coun...]
    ppermute x1, starting transfers between devices: 3.84 us -> 0.93 us  [exchanged(): lax.ppermute(value, 'ctx', [(source, source ^ 1) for source in range(coun...]
    ppermute x11 -> x13, starting transfers between devices: 19.7 us -> 18.3 us  [shifted(): return lax.ppermute(value, axis, pairs)]
    pallas_call x4, Pallas kernels: 5.16 us -> 5.88 us  [hop(): call(functools.partial(kernel, step, wanted), [((wide_q // groups, rows),...]
    ppermute x11 -> x13, waiting for transfers between devices: 12.8 us -> 12.8 us  [shifted(): return lax.ppermute(value, axis, pairs)]
  transfers between devices with their start and end apart: 12 -> 14, of which waited for: 6 -> 8; matrix products, arithmetic and copies ran while one was open for 0% -> 0% of each run, Pallas kernels for 23% -> 26%
where the time goes in v13:
time: 52.8 us; the launch traced here: 52.6 us
  starting transfers between devices  19.2 us (36%)
  waiting for transfers between devices  17.9 us (34%)
  Pallas kernels  14.8 us (28%)
  between operations  0.7 us (1%)
    ppermute x13, starting transfers between devices, shifted(): return lax.ppermute(value, axis, pairs)  18.3 us
    ppermute x13, waiting for transfers between devices, shifted(): return lax.ppermute(value, axis, pairs)  12.8 us
    pallas_call x4, Pallas kernels, hop(): call(functools.partial(kernel, step, wanted), [((wide_q // groups, rows),...  5.88 us
    ppermute x1, waiting for transfers between devices, exchanged(): lax.ppermute(value, 'ctx', [(source, source ^ 1) for source in range(coun...  5.04 us
    pallas_call x1, Pallas kernels, shards(): call(functools.partial(own_kernel, groups), [((wide_q // groups, rows), F...  3.06 us
    pallas_call x1, Pallas kernels, shards(): call(functools.partial(prep_kernel, groups), [((rows, wide_q), BF16)] * 2...  2.42 us
    pallas_call x1, Pallas kernels, shards(): call(key_kernel, [((rows, wide_k), BF16), ((rows, 2 * wide_k), BF16), ((H...  1.3 us
    pallas_call x1, Pallas kernels, shards(): call(functools.partial(query_kernel, groups), [((rows, wide_q), BF16), ((...  1.11 us
  transfers between devices with their start and end apart: 14, of which 8 were waited for; matrix products, arithmetic and copies ran while one was open for 0% of the time, Pallas kernels for 26%

profile of v13, /device:TPU:0, one launch (start us, length us, event | category | flops | bytes accessed | tf_op | source)
XLA Modules:
  0.0 52.6 jit_solution(14712159916275528726)
XLA Ops:
  0.6 6.1 %collective-permute-start.3 = (bf16[256,256]{1,0:T(8,128)(2,1)}, bf16[256,256]{1,0:T(8,128)(2,1)S(1)}, u32[]{:S(2)}, u32[]{:S(2)}) collective-permute-start(bf16[256,256]{1,0:T(8,128)(2,1)} %k_ref.1), channel_id=1, source_target_pairs={{0,28},{4,0},{8,4},{12,8},{16,12},{20,16},{24,20},{28,24},{1,29},{... | collective-permute-start | bytes 393224 | tf_op jit(solution)/shard_map/ppermute | solution.py:350
  6.7 0.5 collective-permute-start.4
  7.2 1.5 %collective-permute-start.1 = (s32[3,64]{1,0:T(4,128)}, s32[3,64]{1,0:T(4,128)S(1)}, u32[]{:S(2)}, u32[]{:S(2)}) collective-permute-start(s32[3,64]{1,0:T(4,128)} %own_ref.1), channel_id=1, source_target_pairs={{0,2},{1,3},{2,0},{3,1},{4,6},{5,7},{6,4},{7,5},{8,10},{9,11},{10,... | collective-permute-start | bytes 2312 | tf_op jit(solution)/shard_map/ppermute | solution.py:350
  8.7 1.4 %collective-permute-start.2 = (s32[3,64]{1,0:T(4,128)}, s32[3,64]{1,0:T(4,128)S(1)}, u32[]{:S(2)}, u32[]{:S(2)}) collective-permute-start(s32[3,64]{1,0:T(4,128)} %own_ref.1), channel_id=1, source_target_pairs={{0,3},{1,0},{2,1},{3,2},{4,7},{5,4},{6,5},{7,6},{8,11},{9,8},{10,9... | collective-permute-start | bytes 2312 | tf_op jit(solution)/shard_map/ppermute | solution.py:350
  10.2 0.3 collective-permute-done.p1_ref
  10.4 0.6 %collective-permute-done.1.p2_ref = s32[3,64]{1,0:T(4,128)S(1)} collective-permute-done((s32[3,64]{1,0:T(4,128)}, s32[3,64]{1,0:T(4,128)S(1)}, u32[]{:S(2)}, u32[]{:S(2)}) %collective-permute-start.1) | collective-permute-done | bytes 800 | tf_op jit(solution)/shard_map/ppermute | solution.py:350
  11.0 0.6 %collective-permute-done.2.p3_ref = s32[3,64]{1,0:T(4,128)S(1)} collective-permute-done((s32[3,64]{1,0:T(4,128)}, s32[3,64]{1,0:T(4,128)S(1)}, u32[]{:S(2)}, u32[]{:S(2)}) %collective-permute-start.2) | collective-permute-done | bytes 800 | tf_op jit(solution)/shard_map/ppermute | solution.py:350
  11.7 1.3 %shard_map.103 = (bf16[256,256]{1,0:T(8,128)(2,1)S(1)}, bf16[256,512]{1,0:T(8,128)(2,1)S(1)}, f32[128,256]{1,0:T(8,128)S(1)}, bf16[16,256]{1,0:T(8,128)(2,1)S(1)}) custom-call(s32[3,64]{1,0:T(4,128)} %own_ref.1, s32[3,64]{1,0:T(4,128)S(1)} %collective-permute-done.p1_ref, s32[3,64]{1,0:T(4,128)S(1)} %collective-permute-done.1.p2_ref, ...), custom_call_target="tpu_custom_call" | custom-call | flops 1048576 | bytes 3690000 | tf_op jit(solution)/shard_map/pallas_call | solution.py:377
  13.0 1.5 %collective-permute-start.5 = (bf16[16,256]{1,0:T(8,128)(2,1)S(1)}, bf16[16,256]{1,0:T(8,128)(2,1)S(1)}, u32[]{:S(2)}, u32[]{:S(2)}) collective-permute-start(bf16[16,256]{1,0:T(8,128)(2,1)S(1)} %get-tuple-element.38), channel_id=1, source_target_pairs={{0,28},{4,0},{8,4},{12,8},{16,12},{20,16},{24,20},{28,24},{1,29},{... | collective-permute-start | bytes 24584 | tf_op jit(solution)/shard_map/ppermute | solution.py:350
  14.4 0.0 collective-permute-start.6
  14.4 2.2 %collective-permute-done.5.refs_3_ = bf16[16,256]{1,0:T(8,128)(2,1)S(1)} collective-permute-done((bf16[16,256]{1,0:T(8,128)(2,1)S(1)}, bf16[16,256]{1,0:T(8,128)(2,1)S(1)}, u32[]{:S(2)}, u32[]{:S(2)}) %collective-permute-start.5) | collective-permute-done | bytes 8224 | tf_op jit(solution)/shard_map/ppermute | solution.py:350
  16.7 2.3 %collective-permute-done.6.refs_2_ = bf16[16,256]{1,0:T(8,128)(2,1)S(1)} collective-permute-done((bf16[16,256]{1,0:T(8,128)(2,1)S(1)}, bf16[16,256]{1,0:T(8,128)(2,1)S(1)}, u32[]{:S(2)}, u32[]{:S(2)}) %collective-permute-start.6) | collective-permute-done | bytes 8224 | tf_op jit(solution)/shard_map/ppermute | solution.py:350
  19.0 2.3 %collective-permute-start.7 = (bf16[256,512]{1,0:T(8,128)(2,1)S(1)}, bf16[256,512]{1,0:T(8,128)(2,1)S(1)}, u32[]{:S(2)}, u32[]{:S(2)}) collective-permute-start(bf16[256,512]{1,0:T(8,128)(2,1)S(1)} %shard_map.106.refs_2_), channel_id=1, source_target_pairs={{0,24},{4,28},{8,0},{12,4},{16,8},{20,12},{24,16},{28,20},{1,25},{... | collective-permute-start | bytes 786440 | tf_op jit(solution)/shard_map/ppermute | solution.py:350
  21.3 2.4 %shard_map.104 = (bf16[256,1024]{1,0:T(8,128)(2,1)S(1)}, bf16[256,1024]{1,0:T(8,128)(2,1)S(1)}, f32[8,256]{1,0:T(8,128)S(1)}, f32[8,256]{1,0:T(8,128)S(1)}, s32[8,128]{1,0:T(8,128)S(1)}) custom-call(s32[8]{0:T(128)} %span_ref.1, f32[128,256]{1,0:T(8,128)S(1)} %get-tuple-element.39.tables_ref, f32[8,256]{1,0:T(8,128)} %lse_hbm.1, bf16[256,1024]{1,0:T(8,128)(2,1)} %q_hbm.1, ...), custom_call_target="tpu_custom_call" | custom-call | flops 1048576 | bytes 7380000 | tf_op jit(solution)/shard_map/pallas_call | solution.py:394
  23.7 3.1 %shard_map.105 = (f32[512,256]{1,0:T(8,128)S(1)}, f32[512,256]{1,0:T(8,128)S(1)}, f32[256,512]{1,0:T(8,128)S(1)}) custom-call(bf16[256,256]{1,0:T(8,128)(2,1)S(1)} %get-tuple-element.37.k_ref, bf16[256,256]{1,0:T(8,128)(2,1)} %v_ref.3, bf16[256,1024]{1,0:T(8,128)(2,1)S(1)} %get-tuple-element.40.qr_ref.refs_4_.refs_3_, ...), custom_call_target="tpu_custom_call" | custom-call | flops 1048576 | bytes 11070000 | tf_op jit(solution)/shard_map/pallas_call | solution.py:406
  26.8 0.1 collective-permute-start.8
  26.9 1.9 %shard_map.107 = (f32[512,256]{1,0:T(8,128)S(1)}, f32[512,256]{1,0:T(8,128)S(1)}, bf16[256,512]{1,0:T(8,128)(2,1)S(1)}) custom-call(f32[512,256]{1,0:T(8,128)S(1)} %get-tuple-element.44.refs_0_, f32[512,256]{1,0:T(8,128)S(1)} %get-tuple-element.45.refs_1_, bf16[256,512]{1,0:T(8,128)(2,1)S(1)} %shard_map.106.refs_2_, ...), custom_call_target="tpu_custom_call" | custom-call | flops 1048576 | bytes 7380000 | tf_op jit(solution)/shard_map/pallas_call | solution.py:416
  28.8 0.9 %collective-permute-start.9 = (bf16[256,512]{1,0:T(8,128)(2,1)S(1)}, bf16[256,512]{1,0:T(8,128)(2,1)S(1)}, u32[]{:S(2)}, u32[]{:S(2)}) collective-permute-start(bf16[256,512]{1,0:T(8,128)(2,1)S(1)} %get-tuple-element.60), channel_id=1, source_target_pairs={{0,4},{4,0},{8,12},{12,8},{16,20},{20,16},{24,28},{28,24},{1,5},{5... | collective-permute-start | bytes 786440 | tf_op jit(solution)/shard_map/ppermute | solution.py:355
  29.7 1.2 %shard_map.109 = (f32[512,256]{1,0:T(8,128)S(1)}, bf16[256,256]{1,0:T(8,128)(2,1)S(1)}) custom-call(f32[512,256]{1,0:T(8,128)S(1)} %get-tuple-element.53.refs_0_, bf16[256,512]{1,0:T(8,128)(2,1)S(1)} %collective-permute-done.7.refs_1_, bf16[16,256]{1,0:T(8,128)(2,1)S(1)} %collective-permute-done.6.refs_2_, ...), custom_call_target="tpu_custom_call" | custom-call | flops 1048576 | bytes 3690000 | tf_op jit(solution)/shard_map/pallas_call | solution.py:416
  30.9 1.2 %collective-permute-start.12 = (bf16[256,256]{1,0:T(8,128)(2,1)S(1)}, bf16[256,256]{1,0:T(8,128)(2,1)S(1)}, u32[]{:S(2)}, u32[]{:S(2)}) collective-permute-start(bf16[256,256]{1,0:T(8,128)(2,1)S(1)} %get-tuple-element.66), channel_id=1, source_target_pairs={{0,4},{4,8},{8,12},{12,16},{16,20},{20,24},{24,28},{28,0},{1,5},{5... | collective-permute-start | bytes 393224 | tf_op jit(solution)/shard_map/ppermute | solution.py:350
  32.1 1.2 %shard_map.108 = (f32[512,256]{1,0:T(8,128)S(1)}, bf16[256,256]{1,0:T(8,128)(2,1)S(1)}) custom-call(f32[512,256]{1,0:T(8,128)S(1)} %get-tuple-element.50.refs_0_, bf16[256,512]{1,0:T(8,128)(2,1)S(1)} %collective-permute-done.7.refs_1_, bf16[16,256]{1,0:T(8,128)(2,1)S(1)} %collective-permute-done.6.refs_2_, ...), custom_call_target="tpu_custom_call" | custom-call | flops 1048576 | bytes 3690000 | tf_op jit(solution)/shard_map/pallas_call | solution.py:416
  33.3 1.9 %collective-permute-start.10 = (bf16[256,256]{1,0:T(8,128)(2,1)S(1)}, bf16[256,256]{1,0:T(8,128)(2,1)S(1)}, u32[]{:S(2)}, u32[]{:S(2)}) collective-permute-start(bf16[256,256]{1,0:T(8,128)(2,1)S(1)} %get-tuple-element.65), channel_id=1, source_target_pairs={{0,4},{4,8},{8,12},{12,16},{16,20},{20,24},{24,28},{28,0},{1,5},{5... | collective-permute-start | bytes 393224 | tf_op jit(solution)/shard_map/ppermute | solution.py:350
  35.2 1.7 %shard_map.110 = (f32[512,256]{1,0:T(8,128)S(1)}, f32[512,256]{1,0:T(8,128)S(1)}, bf16[256,512]{1,0:T(8,128)(2,1)S(1)}) custom-call(f32[512,256]{1,0:T(8,128)S(1)} %get-tuple-element.52.refs_0_, f32[512,256]{1,0:T(8,128)S(1)} %get-tuple-element.54.refs_1_, bf16[256,512]{1,0:T(8,128)(2,1)S(1)} %collective-permute-done.8.refs_2_, ...), custom_call_target="tpu_custom_call" | custom-call | flops 1048576 | bytes 7380000 | tf_op jit(solution)/shard_map/pallas_call | solution.py:416
  36.8 5.0 %collective-permute-done.9.refs_3_.swapped_ref = bf16[256,512]{1,0:T(8,128)(2,1)S(1)} collective-permute-done((bf16[256,512]{1,0:T(8,128)(2,1)S(1)}, bf16[256,512]{1,0:T(8,128)(2,1)S(1)}, u32[]{:S(2)}, u32[]{:S(2)}) %collective-permute-start.9) | collective-permute-done | bytes 262176 | tf_op jit(solution)/shard_map/ppermute | solution.py:355
  41.9 1.1 %shard_map.111 = (bf16[256,1024]{1,0:T(8,128)(2,1)}, f32[256,512]{1,0:T(8,128)S(1)}) custom-call(f32[128,256]{1,0:T(8,128)S(1)} %get-tuple-element.39.tables_ref, f32[512,256]{1,0:T(8,128)S(1)} %get-tuple-element.58.refs_0_, f32[512,256]{1,0:T(8,128)S(1)} %get-tuple-element.59.refs_1_, f32[256,512]{1,0:T(8,128)S(1)} %get-tuple-element.56.refs_2_, ...), custom_call_target="tpu_custom_call" | custom-call | flops 1048576 | bytes 3690000 | tf_op jit(solution)/shard_map/pallas_call | solution.py:434
  43.0 0.1 shard_map.113
  43.1 1.8 %collective-permute-start.13 = (bf16[256,256]{1,0:T(8,128)(2,1)S(1)}, bf16[256,256]{1,0:T(8,128)(2,1)S(1)}, u32[]{:S(2)}, u32[]{:S(2)}) collective-permute-start(bf16[256,256]{1,0:T(8,128)(2,1)S(1)} %shard_map.113), channel_id=1, source_target_pairs={{0,8},{4,12},{8,16},{12,20},{16,24},{20,28},{24,0},{28,4},{1,9},{5... | collective-permute-start | bytes 393224 | tf_op jit(solution)/shard_map/ppermute | solution.py:350
  44.8 0.1 shard_map.112
  44.9 0.1 collective-permute-start.11
  45.0 4.9 %collective-permute-done.13.refs_1_ = bf16[256,256]{1,0:T(8,128)(2,1)S(1)} collective-permute-done((bf16[256,256]{1,0:T(8,128)(2,1)S(1)}, bf16[256,256]{1,0:T(8,128)(2,1)S(1)}, u32[]{:S(2)}, u32[]{:S(2)}) %collective-permute-start.13) | collective-permute-done | bytes 131104 | tf_op jit(solution)/shard_map/ppermute | solution.py:350
  49.9 1.8 %collective-permute-done.11.refs_0_ = bf16[256,256]{1,0:T(8,128)(2,1)S(1)} collective-permute-done((bf16[256,256]{1,0:T(8,128)(2,1)S(1)}, bf16[256,256]{1,0:T(8,128)(2,1)S(1)}, u32[]{:S(2)}, u32[]{:S(2)}) %collective-permute-start.11) | collective-permute-done | bytes 131104 | tf_op jit(solution)/shard_map/ppermute | solution.py:350
  51.7 0.9 %shard_map.114 = (bf16[256,256]{1,0:T(8,128)(2,1)}, bf16[256,256]{1,0:T(8,128)(2,1)}) custom-call(f32[128,256]{1,0:T(8,128)S(1)} %get-tuple-element.39.tables_ref, f32[256,512]{1,0:T(8,128)S(1)} %get-tuple-element.62.own_ref, bf16[256,256]{1,0:T(8,128)(2,1)S(1)} %collective-permute-done.11.refs_0_, bf16[256,256]{1,0:T(8,128)(2,1)S(1)} %collective-permute-done.13.refs_1_), custom_call_target="tpu_custom_call" | custom-call | flops 1048576 | bytes 3690000 | tf_op jit(solution)/shard_map/pallas_call | solution.py:447
  (8 shorter events, 0.0 us)
Async XLA Ops:
  0.6 18.4 %collective-permute-start.3 = (bf16[256,256]{1,0:T(8,128)(2,1)}, bf16[256,256]{1,0:T(8,128)(2,1)S(1)}, u32[]{:S(2)}, u32[]{:S(2)}) collective-permute-start(bf16[256,256]{1,0:T(8,128)(2,1)} %k_ref.1), channel_id=1, source_target_pairs={{0,28},{4,0},{8,4},{12,8},{16,12},{20,16},{24,20},{28,24},{1,29},{... | collective-permute-start | bytes 393224 | tf_op jit(solution)/shard_map/ppermute | solution.py:350
  6.7 12.3 %collective-permute-start.4 = (bf16[256,256]{1,0:T(8,128)(2,1)}, bf16[256,256]{1,0:T(8,128)(2,1)S(1)}, u32[]{:S(2)}, u32[]{:S(2)}) collective-permute-start(bf16[256,256]{1,0:T(8,128)(2,1)} %v_ref.3), channel_id=1, source_target_pairs={{0,28},{4,0},{8,4},{12,8},{16,12},{20,16},{24,20},{28,24},{1,29},{... | collective-permute-start | bytes 393224 | tf_op jit(solution)/shard_map/ppermute | solution.py:350
  7.2 3.2 %collective-permute-start = (s32[3,64]{1,0:T(4,128)}, s32[3,64]{1,0:T(4,128)S(1)}, u32[]{:S(2)}, u32[]{:S(2)}) collective-permute-start(s32[3,64]{1,0:T(4,128)} %own_ref.1), channel_id=1, source_target_pairs={{0,1},{1,2},{2,3},{3,0},{4,5},{5,6},{6,7},{7,4},{8,9},{9,10},{10,1... | collective-permute-start | bytes 2312 | tf_op jit(solution)/shard_map/ppermute | solution.py:350
  7.2 3.8 %collective-permute-start.1 = (s32[3,64]{1,0:T(4,128)}, s32[3,64]{1,0:T(4,128)S(1)}, u32[]{:S(2)}, u32[]{:S(2)}) collective-permute-start(s32[3,64]{1,0:T(4,128)} %own_ref.1), channel_id=1, source_target_pairs={{0,2},{1,3},{2,0},{3,1},{4,6},{5,7},{6,4},{7,5},{8,10},{9,11},{10,... | collective-permute-start | bytes 2312 | tf_op jit(solution)/shard_map/ppermute | solution.py:350
  8.7 3.0 %collective-permute-start.2 = (s32[3,64]{1,0:T(4,128)}, s32[3,64]{1,0:T(4,128)S(1)}, u32[]{:S(2)}, u32[]{:S(2)}) collective-permute-start(s32[3,64]{1,0:T(4,128)} %own_ref.1), channel_id=1, source_target_pairs={{0,3},{1,0},{2,1},{3,2},{4,7},{5,4},{6,5},{7,6},{8,11},{9,8},{10,9... | collective-permute-start | bytes 2312 | tf_op jit(solution)/shard_map/ppermute | solution.py:350
  13.0 3.7 %collective-permute-start.5 = (bf16[16,256]{1,0:T(8,128)(2,1)S(1)}, bf16[16,256]{1,0:T(8,128)(2,1)S(1)}, u32[]{:S(2)}, u32[]{:S(2)}) collective-permute-start(bf16[16,256]{1,0:T(8,128)(2,1)S(1)} %get-tuple-element.38), channel_id=1, source_target_pairs={{0,28},{4,0},{8,4},{12,8},{16,12},{20,16},{24,20},{28,24},{1,29},{... | collective-permute-start | bytes 24584 | tf_op jit(solution)/shard_map/ppermute | solution.py:350
  14.4 4.5 %collective-permute-start.6 = (bf16[16,256]{1,0:T(8,128)(2,1)S(1)}, bf16[16,256]{1,0:T(8,128)(2,1)S(1)}, u32[]{:S(2)}, u32[]{:S(2)}) collective-permute-start(bf16[16,256]{1,0:T(8,128)(2,1)S(1)} %get-tuple-element.38), channel_id=1, source_target_pairs={{0,20},{4,24},{8,28},{12,0},{16,4},{20,8},{24,12},{28,16},{1,21},{... | collective-permute-start | bytes 24584 | tf_op jit(solution)/shard_map/ppermute | solution.py:350
  19.0 10.7 %collective-permute-start.7 = (bf16[256,512]{1,0:T(8,128)(2,1)S(1)}, bf16[256,512]{1,0:T(8,128)(2,1)S(1)}, u32[]{:S(2)}, u32[]{:S(2)}) collective-permute-start(bf16[256,512]{1,0:T(8,128)(2,1)S(1)} %shard_map.106.refs_2_), channel_id=1, source_target_pairs={{0,24},{4,28},{8,0},{12,4},{16,8},{20,12},{24,16},{28,20},{1,25},{... | collective-permute-start | bytes 786440 | tf_op jit(solution)/shard_map/ppermute | solution.py:350
  26.8 8.4 %collective-permute-start.8 = (bf16[256,512]{1,0:T(8,128)(2,1)S(1)}, bf16[256,512]{1,0:T(8,128)(2,1)S(1)}, u32[]{:S(2)}, u32[]{:S(2)}) collective-permute-start(bf16[256,512]{1,0:T(8,128)(2,1)S(1)} %get-tuple-element.57), channel_id=1, source_target_pairs={{0,24},{4,28},{8,0},{12,4},{16,8},{20,12},{24,16},{28,20},{1,25},{... | collective-permute-start | bytes 786440 | tf_op jit(solution)/shard_map/ppermute | solution.py:350
  28.8 13.1 %collective-permute-start.9 = (bf16[256,512]{1,0:T(8,128)(2,1)S(1)}, bf16[256,512]{1,0:T(8,128)(2,1)S(1)}, u32[]{:S(2)}, u32[]{:S(2)}) collective-permute-start(bf16[256,512]{1,0:T(8,128)(2,1)S(1)} %get-tuple-element.60), channel_id=1, source_target_pairs={{0,4},{4,0},{8,12},{12,8},{16,20},{20,16},{24,28},{28,24},{1,5},{5... | collective-permute-start | bytes 786440 | tf_op jit(solution)/shard_map/ppermute | solution.py:355
  30.9 12.1 %collective-permute-start.12 = (bf16[256,256]{1,0:T(8,128)(2,1)S(1)}, bf16[256,256]{1,0:T(8,128)(2,1)S(1)}, u32[]{:S(2)}, u32[]{:S(2)}) collective-permute-start(bf16[256,256]{1,0:T(8,128)(2,1)S(1)} %get-tuple-element.66), channel_id=1, source_target_pairs={{0,4},{4,8},{8,12},{12,16},{16,20},{20,24},{24,28},{28,0},{1,5},{5... | collective-permute-start | bytes 393224 | tf_op jit(solution)/shard_map/ppermute | solution.py:350
  33.3 11.6 %collective-permute-start.10 = (bf16[256,256]{1,0:T(8,128)(2,1)S(1)}, bf16[256,256]{1,0:T(8,128)(2,1)S(1)}, u32[]{:S(2)}, u32[]{:S(2)}) collective-permute-start(bf16[256,256]{1,0:T(8,128)(2,1)S(1)} %get-tuple-element.65), channel_id=1, source_target_pairs={{0,4},{4,8},{8,12},{12,16},{16,20},{20,24},{24,28},{28,0},{1,5},{5... | collective-permute-start | bytes 393224 | tf_op jit(solution)/shard_map/ppermute | solution.py:350
  43.1 6.8 %collective-permute-start.13 = (bf16[256,256]{1,0:T(8,128)(2,1)S(1)}, bf16[256,256]{1,0:T(8,128)(2,1)S(1)}, u32[]{:S(2)}, u32[]{:S(2)}) collective-permute-start(bf16[256,256]{1,0:T(8,128)(2,1)S(1)} %shard_map.113), channel_id=1, source_target_pairs={{0,8},{4,12},{8,16},{12,20},{16,24},{20,28},{24,0},{28,4},{1,9},{5... | collective-permute-start | bytes 393224 | tf_op jit(solution)/shard_map/ppermute | solution.py:350
  44.9 6.8 %collective-permute-start.11 = (bf16[256,256]{1,0:T(8,128)(2,1)S(1)}, bf16[256,256]{1,0:T(8,128)(2,1)S(1)}, u32[]{:S(2)}, u32[]{:S(2)}) collective-permute-start(bf16[256,256]{1,0:T(8,128)(2,1)S(1)} %shard_map.112), channel_id=1, source_target_pairs={{0,8},{4,12},{8,16},{12,20},{16,24},{20,28},{24,0},{28,4},{1,9},{5... | collective-permute-start | bytes 393224 | tf_op jit(solution)/shard_map/ppermute | solution.py:350

commit v14 on v13

--- a/solution.py
+++ b/solution.py
@@ -191,10 +191,10 @@
     norm_ref[...] = lse_ref[...] * LOG2E
 
 
-def hop_kernel(step, wanted, *refs):
+def hop_kernel(step, wanted, started, *refs):
     count = len(wanted)
     dqt_ins, dqt_refs, part_ref = refs[:count], refs[-count - 1 : -1], refs[-1]
-    k_ref, v_ref, qr_ref, do_ref, norm_ref, delta_ref, flag_ref = refs[count : -count - 1]
+    k_ref, v_ref, qr_ref, do_ref, norm_ref, delta_ref, flag_ref = refs[count * started : -count - 1]
     rows = qr_ref.shape[0]
     half = rows // 2
     heads = qr_ref.shape[1] // HEAD
@@ -217,8 +217,11 @@
                     norm[h : h + 1, queries.start :], delta[h : h + 1, queries.start :], False,
                 )
                 if queries.start:
-                    dqt_ref[to, : queries.start] = dqt_in[to, : queries.start]
-                dqt_ref[to, queries] = dqt_in[to, queries] + q_part
+                    zeros = jnp.zeros((HEAD, queries.start), F32)
+                    dqt_ref[to, : queries.start] = (
+                        dqt_in[to, : queries.start] if started else zeros
+                    )
+                dqt_ref[to, queries] = dqt_in[to, queries] + q_part if started else q_part
                 dv = v_part if dv is None else dv + v_part
                 dk = k_part if dk is None else dk + k_part
             part_ref[keys, pl.ds(2 * i * HEAD, HEAD)] = dk.astype(BF16)
@@ -235,18 +238,19 @@
         run(slice(0, rows), slice(half, rows))
 
 
-def merged_kernel(step, wanted, *refs):
-    count = len(wanted)
+def merged_kernel(step, wanted, started, *refs):
+    count = len(wanted) * started
     kv_ref = refs[count]
     width = kv_ref.shape[1] // 2
     hop_kernel(
-        step, wanted, *refs[:count], kv_ref.at[:, :width], kv_ref.at[:, width:], *refs[count + 1 :]
-    )
-
-
-def raw_kernel(step, wanted, *refs):
+        step, wanted, started, *refs[:count], kv_ref.at[:, :width], kv_ref.at[:, width:],
+        *refs[count + 1 :],
+    )
+
+
+def raw_kernel(step, wanted, started, *refs):
     *refs, key_ref = refs
-    count = len(wanted)
+    count = len(wanted) * started
     kv_ref, packed_ref = refs[count : count + 2]
     width = kv_ref.shape[1] // 2
     place = packed_ref[...].astype(F32)
@@ -255,7 +259,7 @@
         cols = pl.ds(g * HEAD, HEAD)
         key_ref[:, cols] = rotated(kv_ref[:, cols].astype(F32), wide, signed).astype(BF16)
     hop_kernel(
-        step, wanted, *refs[:count], key_ref, kv_ref.at[:, width:], *refs[count + 2 :]
+        step, wanted, started, *refs[:count], key_ref, kv_ref.at[:, width:], *refs[count + 2 :]
     )
 
 
@@ -266,7 +270,7 @@
 
 
 def own_kernel(groups, k_ref, v_ref, qr_ref, do_ref, norm_ref, delta_ref, *refs):
-    dqt_refs, part_ref = refs[:groups], refs[groups]
+    dqt_ins, dqt_refs, part_ref = refs[:groups], refs[groups : 2 * groups], refs[2 * groups]
     size = qr_ref.shape[1] // HEAD // groups
     norm = norm_ref[...]
     delta = delta_ref[...]
@@ -281,7 +285,7 @@
                 k_ref[:, kc], v_ref[:, kc], qr_ref[:, hc], do_ref[:, hc],
                 norm[h : h + 1], delta[h : h + 1], True,
             )
-            dqt_refs[g][to, :] = q_part
+            dqt_refs[g][to, :] = dqt_ins[g][to, :] + q_part
             dv = v_part if dv is None else dv + v_part
             dk = k_part if dk is None else dk + k_part
         part_ref[:, pl.ds(2 * g * HEAD, HEAD)] = dk
@@ -386,9 +390,7 @@
     )(*pieces, k_here, v_here)
     packed1 = shifted(packed, -1)
     packed3 = shifted(packed, -3)
-    turned, k1, v1, packed1, packed3 = lax.optimization_barrier(
-        (tables, k1, v1, packed1, packed3)
-    )
+    turned, k1, v1 = lax.optimization_barrier((tables, k1, v1))
     (kv1,) = call(beside_kernel, [((rows, 2 * wide_k), BF16)], [VMEM] * 2)(k1, v1)
     kv3 = shifted(kv1, -2)
     shared = call(
@@ -403,32 +405,37 @@
         ],
         micros=2,
     )(span_map, turned, lse, q, do, at)
+    dqs = []
+
+    def hop(kernel, step, wanted, arrived, scratch=()):
+        count = len(wanted)
+        started = len(dqs) > 0
+        before = [dqs[g] for g in wanted] if started else []
+        *new, part = call(
+            functools.partial(kernel, step, wanted, started),
+            [((wide_q // groups, rows), F32)] * count + [((rows, 2 * HEAD * count), BF16)],
+            [VMEM] * (5 + len(arrived) + len(before)),
+            scratch,
+            micros=count,
+        )(*before, *arrived, *shared)
+        if not started:
+            dqs.extend(new)
+        for g, dq in zip(wanted, new):
+            dqs[g] = dq
+        return part
+
+    turned_key = [pltpu.VMEM((rows, wide_k), BF16)]
+    part1 = hop(raw_kernel, 1, every, (kv1, packed1), turned_key)
+    swapped = exchanged(part1)
+    held, _ = lax.optimization_barrier((kv, part1))
+    kv2 = shifted(held, -2)
     *dqs, own = call(
         functools.partial(own_kernel, groups),
         [((wide_q // groups, rows), F32)] * groups + [((rows, 2 * wide_k), F32)],
-        [VMEM] * 6,
+        [VMEM] * (6 + groups),
         micros=3,
-    )(kr, v_here, *shared[:4])
-
-    def hop(kernel, step, wanted, arrived, scratch=()):
-        count = len(wanted)
-        before = [dqs[g] for g in wanted]
-        *new, part = call(
-            functools.partial(kernel, step, wanted),
-            [((wide_q // groups, rows), F32)] * count + [((rows, 2 * HEAD * count), BF16)],
-            [VMEM] * (5 + len(arrived) + count),
-            scratch,
-            micros=count,
-        )(*before, *arrived, *shared)
-        for g, dq in zip(wanted, new):
-            dqs[g] = dq
-        return part
-
-    held, _ = lax.optimization_barrier((kv, own))
-    kv2 = shifted(held, -2)
-    turned_key = [pltpu.VMEM((rows, wide_k), BF16)]
-    part1 = hop(raw_kernel, 1, every, (kv1, packed1), turned_key)
-    swapped = exchanged(part1)
+    )(kr, v_here, *shared[:4], *dqs)
+
     moved = [shifted(hop(raw_kernel, 3, (g,), (kv3, packed3), turned_key), 1) for g in every]
     part2 = hop(merged_kernel, 2, every, (kv2,))
     dq, own = call(

time: 52.8 us -> 52.3 us (level)
  waiting for transfers between devices: 17.9 us -> 14.7 us
  starting transfers between devices: 19.2 us -> 21.9 us
    ppermute x1, waiting for transfers between devices: 5.04 us -> 0.01 us  [exchanged(): lax.ppermute(value, 'ctx', [(source, source ^ 1) for source in range(coun...]
    ppermute x1, starting transfers between devices: 0.93 us -> 5.29 us  [exchanged(): lax.ppermute(value, 'ctx', [(source, source ^ 1) for source in range(coun...]
    ppermute x13, waiting for transfers between devices: 12.8 us -> 14.7 us  [shifted(): return lax.ppermute(value, axis, pairs)]
    ppermute x13, starting transfers between devices: 18.3 us -> 16.6 us  [shifted(): return lax.ppermute(value, axis, pairs)]
  transfers between devices with their start and end apart: 14 -> 14, of which waited for: 8 -> 8; matrix products, arithmetic and copies ran while one was open for 0% -> 0% of each run, Pallas kernels for 26% -> 27%
where the time goes in v14:
time: 52.3 us; the launch traced here: 52.1 us
  starting transfers between devices  21.9 us (42%)
  waiting for transfers between devices  14.7 us (28%)
  Pallas kernels  14.7 us (28%)
  between operations  0.73 us (1%)
    ppermute x13, starting transfers between devices, shifted(): return lax.ppermute(value, axis, pairs)  16.6 us
    ppermute x13, waiting for transfers between devices, shifted(): return lax.ppermute(value, axis, pairs)  14.7 us
    pallas_call x4, Pallas kernels, hop(): call(functools.partial(kernel, step, wanted, started), [((wide_q // group...  5.83 us
    ppermute x1, starting transfers between devices, exchanged(): lax.ppermute(value, 'ctx', [(source, source ^ 1) for source in range(coun...  5.29 us
    pallas_call x1, Pallas kernels, shards(): call(functools.partial(own_kernel, groups), [((wide_q // groups, rows), F...  3.04 us
    pallas_call x1, Pallas kernels, shards(): call(functools.partial(prep_kernel, groups), [((rows, wide_q), BF16)] * 2...  2.41 us
    pallas_call x1, Pallas kernels, shards(): call(key_kernel, [((rows, wide_k), BF16), ((rows, 2 * wide_k), BF16), ((H...  1.3 us
    pallas_call x1, Pallas kernels, shards(): call(functools.partial(query_kernel, groups), [((rows, wide_q), BF16), ((...  1.11 us
  transfers between devices with their start and end apart: 14, of which 8 were waited for; matrix products, arithmetic and copies ran while one was open for 0% of the time, Pallas kernels for 27%

profile of v14, /device:TPU:0, one launch (start us, length us, event | category | flops | bytes accessed | tf_op | source)
XLA Modules:
  0.0 52.1 jit_solution(10651064483563944448)
XLA Ops:
  0.6 6.1 %collective-permute-start.3 = (bf16[256,256]{1,0:T(8,128)(2,1)}, bf16[256,256]{1,0:T(8,128)(2,1)S(1)}, u32[]{:S(2)}, u32[]{:S(2)}) collective-permute-start(bf16[256,256]{1,0:T(8,128)(2,1)} %k_ref.1), channel_id=1, source_target_pairs={{0,28},{4,0},{8,4},{12,8},{16,12},{20,16},{24,20},{28,24},{1,29},{... | collective-permute-start | bytes 393224 | tf_op jit(solution)/shard_map/ppermute | solution.py:354
  6.7 0.5 collective-permute-start.4
  7.2 1.5 %collective-permute-start.1 = (s32[3,64]{1,0:T(4,128)}, s32[3,64]{1,0:T(4,128)S(1)}, u32[]{:S(2)}, u32[]{:S(2)}) collective-permute-start(s32[3,64]{1,0:T(4,128)} %own_ref.1), channel_id=1, source_target_pairs={{0,2},{1,3},{2,0},{3,1},{4,6},{5,7},{6,4},{7,5},{8,10},{9,11},{10,... | collective-permute-start | bytes 2312 | tf_op jit(solution)/shard_map/ppermute | solution.py:354
  8.7 1.7 %collective-permute-start.2 = (s32[3,64]{1,0:T(4,128)}, s32[3,64]{1,0:T(4,128)S(1)}, u32[]{:S(2)}, u32[]{:S(2)}) collective-permute-start(s32[3,64]{1,0:T(4,128)} %own_ref.1), channel_id=1, source_target_pairs={{0,3},{1,0},{2,1},{3,2},{4,7},{5,4},{6,5},{7,6},{8,11},{9,8},{10,9... | collective-permute-start | bytes 2312 | tf_op jit(solution)/shard_map/ppermute | solution.py:354
  10.4 0.6 %collective-permute-done.1.p2_ref = s32[3,64]{1,0:T(4,128)S(1)} collective-permute-done((s32[3,64]{1,0:T(4,128)}, s32[3,64]{1,0:T(4,128)S(1)}, u32[]{:S(2)}, u32[]{:S(2)}) %collective-permute-start.1) | collective-permute-done | bytes 800 | tf_op jit(solution)/shard_map/ppermute | solution.py:354
  11.0 0.9 %collective-permute-done.p1_ref = s32[3,64]{1,0:T(4,128)S(1)} collective-permute-done((s32[3,64]{1,0:T(4,128)}, s32[3,64]{1,0:T(4,128)S(1)}, u32[]{:S(2)}, u32[]{:S(2)}) %collective-permute-start) | collective-permute-done | bytes 800 | tf_op jit(solution)/shard_map/ppermute | solution.py:354
  11.9 0.0 collective-permute-done.2.p3_ref
  12.0 1.3 %shard_map.103 = (bf16[256,256]{1,0:T(8,128)(2,1)S(1)}, bf16[256,512]{1,0:T(8,128)(2,1)S(1)}, f32[128,256]{1,0:T(8,128)S(1)}, bf16[16,256]{1,0:T(8,128)(2,1)S(1)}) custom-call(s32[3,64]{1,0:T(4,128)} %own_ref.1, s32[3,64]{1,0:T(4,128)S(1)} %collective-permute-done.p1_ref, s32[3,64]{1,0:T(4,128)S(1)} %collective-permute-done.1.p2_ref, ...), custom_call_target="tpu_custom_call" | custom-call | flops 1048576 | bytes 3690000 | tf_op jit(solution)/shard_map/pallas_call | solution.py:381
  13.3 0.8 %collective-permute-start.6 = (bf16[256,512]{1,0:T(8,128)(2,1)S(1)}, bf16[256,512]{1,0:T(8,128)(2,1)S(1)}, u32[]{:S(2)}, u32[]{:S(2)}) collective-permute-start(bf16[256,512]{1,0:T(8,128)(2,1)S(1)} %shard_map.105.refs_0_), channel_id=1, source_target_pairs={{0,24},{4,28},{8,0},{12,4},{16,8},{20,12},{24,16},{28,20},{1,25},{... | collective-permute-start | bytes 786440 | tf_op jit(solution)/shard_map/ppermute | solution.py:354
  14.1 3.7 %collective-permute-start.5 = (bf16[16,256]{1,0:T(8,128)(2,1)S(1)}, bf16[16,256]{1,0:T(8,128)(2,1)S(1)}, u32[]{:S(2)}, u32[]{:S(2)}) collective-permute-start(bf16[16,256]{1,0:T(8,128)(2,1)S(1)} %get-tuple-element.43), channel_id=1, source_target_pairs={{0,28},{4,0},{8,4},{12,8},{16,12},{20,16},{24,20},{28,24},{1,29},{... | collective-permute-start | bytes 24584 | tf_op jit(solution)/shard_map/ppermute | solution.py:354
  17.8 2.4 %shard_map.104 = (bf16[256,1024]{1,0:T(8,128)(2,1)S(1)}, bf16[256,1024]{1,0:T(8,128)(2,1)S(1)}, f32[8,256]{1,0:T(8,128)S(1)}, f32[8,256]{1,0:T(8,128)S(1)}, s32[8,128]{1,0:T(8,128)S(1)}) custom-call(s32[8]{0:T(128)} %span_ref.1, f32[128,256]{1,0:T(8,128)S(1)} %get-tuple-element.36.tables_ref, f32[8,256]{1,0:T(8,128)} %lse_hbm.1, bf16[256,1024]{1,0:T(8,128)(2,1)} %q_hbm.1, ...), custom_call_target="tpu_custom_call" | custom-call | flops 1048576 | bytes 7380000 | tf_op jit(solution)/shard_map/pallas_call | solution.py:396
  20.2 0.4 collective-permute-done.5.refs_1_
  20.6 1.9 %shard_map.106 = (f32[512,256]{1,0:T(8,128)S(1)}, f32[512,256]{1,0:T(8,128)S(1)}, bf16[256,512]{1,0:T(8,128)(2,1)S(1)}) custom-call(bf16[256,512]{1,0:T(8,128)(2,1)S(1)} %shard_map.105.refs_0_, bf16[16,256]{1,0:T(8,128)(2,1)S(1)} %collective-permute-done.5.refs_1_, bf16[256,1024]{1,0:T(8,128)(2,1)S(1)} %get-tuple-element.37.refs_2_.qr_ref.refs_3_, ...), custom_call_target="tpu_custom_call" | custom-call | flops 1048576 | bytes 7380000 | tf_op jit(solution)/shard_map/pallas_call | solution.py:414
  22.5 0.5 collective-permute-start.8
  23.0 5.3 %collective-permute-start.9 = (bf16[256,512]{1,0:T(8,128)(2,1)S(1)}, bf16[256,512]{1,0:T(8,128)(2,1)S(1)}, u32[]{:S(2)}, u32[]{:S(2)}) collective-permute-start(bf16[256,512]{1,0:T(8,128)(2,1)S(1)} %get-tuple-element.52), channel_id=1, source_target_pairs={{0,4},{4,0},{8,12},{12,8},{16,20},{20,16},{24,28},{28,24},{1,5},{5... | collective-permute-start | bytes 786440 | tf_op jit(solution)/shard_map/ppermute | solution.py:359
  28.3 3.0 %shard_map.107 = (f32[512,256]{1,0:T(8,128)S(1)}, f32[512,256]{1,0:T(8,128)S(1)}, f32[256,512]{1,0:T(8,128)S(1)}) custom-call(bf16[256,256]{1,0:T(8,128)(2,1)S(1)} %get-tuple-element.35.k_ref, bf16[256,256]{1,0:T(8,128)(2,1)} %v_ref.3, bf16[256,1024]{1,0:T(8,128)(2,1)S(1)} %get-tuple-element.37.refs_2_.qr_ref.refs_3_, ...), custom_call_target="tpu_custom_call" | custom-call | flops 1048576 | bytes 11070000 | tf_op jit(solution)/shard_map/pallas_call | solution.py:432
  31.3 1.9 %collective-permute-done.7.refs_2_ = bf16[16,256]{1,0:T(8,128)(2,1)S(1)} collective-permute-done((bf16[16,256]{1,0:T(8,128)(2,1)S(1)}, bf16[16,256]{1,0:T(8,128)(2,1)S(1)}, u32[]{:S(2)}, u32[]{:S(2)}) %collective-permute-start.7) | collective-permute-done | bytes 8224 | tf_op jit(solution)/shard_map/ppermute | solution.py:354
  33.2 1.2 %shard_map.108 = (f32[512,256]{1,0:T(8,128)S(1)}, bf16[256,256]{1,0:T(8,128)(2,1)S(1)}) custom-call(f32[512,256]{1,0:T(8,128)S(1)} %get-tuple-element.47.refs_0_, bf16[256,512]{1,0:T(8,128)(2,1)S(1)} %collective-permute-done.6.refs_1_, bf16[16,256]{1,0:T(8,128)(2,1)S(1)} %collective-permute-done.7.refs_2_, ...), custom_call_target="tpu_custom_call" | custom-call | flops 1048576 | bytes 3690000 | tf_op jit(solution)/shard_map/pallas_call | solution.py:414
  34.4 0.7 %collective-permute-start.10 = (bf16[256,256]{1,0:T(8,128)(2,1)S(1)}, bf16[256,256]{1,0:T(8,128)(2,1)S(1)}, u32[]{:S(2)}, u32[]{:S(2)}) collective-permute-start(bf16[256,256]{1,0:T(8,128)(2,1)S(1)} %get-tuple-element.61), channel_id=1, source_target_pairs={{0,4},{4,8},{8,12},{12,16},{16,20},{20,24},{24,28},{28,0},{1,5},{5... | collective-permute-start | bytes 393224 | tf_op jit(solution)/shard_map/ppermute | solution.py:354
  35.1 1.2 %shard_map.109 = (f32[512,256]{1,0:T(8,128)S(1)}, bf16[256,256]{1,0:T(8,128)(2,1)S(1)}) custom-call(f32[512,256]{1,0:T(8,128)S(1)} %get-tuple-element.49.refs_0_, bf16[256,512]{1,0:T(8,128)(2,1)S(1)} %collective-permute-done.6.refs_1_, bf16[16,256]{1,0:T(8,128)(2,1)S(1)} %collective-permute-done.7.refs_2_, ...), custom_call_target="tpu_custom_call" | custom-call | flops 1048576 | bytes 3690000 | tf_op jit(solution)/shard_map/pallas_call | solution.py:414
  36.2 0.1 collective-permute-start.12
  36.3 1.6 %shard_map.110 = (f32[512,256]{1,0:T(8,128)S(1)}, f32[512,256]{1,0:T(8,128)S(1)}, bf16[256,512]{1,0:T(8,128)(2,1)S(1)}) custom-call(f32[512,256]{1,0:T(8,128)S(1)} %get-tuple-element.48.refs_0_, f32[512,256]{1,0:T(8,128)S(1)} %get-tuple-element.50.refs_1_, bf16[256,512]{1,0:T(8,128)(2,1)S(1)} %collective-permute-done.8.refs_2_, ...), custom_call_target="tpu_custom_call" | custom-call | flops 1048576 | bytes 7380000 | tf_op jit(solution)/shard_map/pallas_call | solution.py:414
  38.0 1.1 %shard_map.111 = (bf16[256,1024]{1,0:T(8,128)(2,1)}, f32[256,512]{1,0:T(8,128)S(1)}) custom-call(f32[128,256]{1,0:T(8,128)S(1)} %get-tuple-element.36.tables_ref, f32[512,256]{1,0:T(8,128)S(1)} %get-tuple-element.54.refs_0_, f32[512,256]{1,0:T(8,128)S(1)} %get-tuple-element.55.refs_1_, f32[256,512]{1,0:T(8,128)S(1)} %get-tuple-element.56.refs_2_, ...), custom_call_target="tpu_custom_call" | custom-call | flops 1048576 | bytes 3690000 | tf_op jit(solution)/shard_map/pallas_call | solution.py:441
  39.1 3.4 %collective-permute-done.10.three_ref = bf16[256,256]{1,0:T(8,128)(2,1)S(1)} collective-permute-done((bf16[256,256]{1,0:T(8,128)(2,1)S(1)}, bf16[256,256]{1,0:T(8,128)(2,1)S(1)}, u32[]{:S(2)}, u32[]{:S(2)}) %collective-permute-start.10) | collective-permute-done | bytes 131104 | tf_op jit(solution)/shard_map/ppermute | solution.py:354
  42.5 0.1 shard_map.112
  42.6 0.1 collective-permute-start.11
  42.6 1.7 %collective-permute-done.12.three_ref = bf16[256,256]{1,0:T(8,128)(2,1)S(1)} collective-permute-done((bf16[256,256]{1,0:T(8,128)(2,1)S(1)}, bf16[256,256]{1,0:T(8,128)(2,1)S(1)}, u32[]{:S(2)}, u32[]{:S(2)}) %collective-permute-start.12) | collective-permute-done | bytes 131104 | tf_op jit(solution)/shard_map/ppermute | solution.py:354
  44.3 0.1 shard_map.113
  44.4 1.0 %collective-permute-start.13 = (bf16[256,256]{1,0:T(8,128)(2,1)S(1)}, bf16[256,256]{1,0:T(8,128)(2,1)S(1)}, u32[]{:S(2)}, u32[]{:S(2)}) collective-permute-start(bf16[256,256]{1,0:T(8,128)(2,1)S(1)} %shard_map.113), channel_id=1, source_target_pairs={{0,8},{4,12},{8,16},{12,20},{16,24},{20,28},{24,0},{28,4},{1,9},{5... | collective-permute-start | bytes 393224 | tf_op jit(solution)/shard_map/ppermute | solution.py:354
  45.4 3.9 %collective-permute-done.11.refs_0_ = bf16[256,256]{1,0:T(8,128)(2,1)S(1)} collective-permute-done((bf16[256,256]{1,0:T(8,128)(2,1)S(1)}, bf16[256,256]{1,0:T(8,128)(2,1)S(1)}, u32[]{:S(2)}, u32[]{:S(2)}) %collective-permute-start.11) | collective-permute-done | bytes 131104 | tf_op jit(solution)/shard_map/ppermute | solution.py:354
  49.4 1.8 %collective-permute-done.13.refs_1_ = bf16[256,256]{1,0:T(8,128)(2,1)S(1)} collective-permute-done((bf16[256,256]{1,0:T(8,128)(2,1)S(1)}, bf16[256,256]{1,0:T(8,128)(2,1)S(1)}, u32[]{:S(2)}, u32[]{:S(2)}) %collective-permute-start.13) | collective-permute-done | bytes 131104 | tf_op jit(solution)/shard_map/ppermute | solution.py:354
  51.2 0.9 %shard_map.114 = (bf16[256,256]{1,0:T(8,128)(2,1)}, bf16[256,256]{1,0:T(8,128)(2,1)}) custom-call(f32[128,256]{1,0:T(8,128)S(1)} %get-tuple-element.36.tables_ref, f32[256,512]{1,0:T(8,128)S(1)} %get-tuple-element.58.own_ref, bf16[256,256]{1,0:T(8,128)(2,1)S(1)} %collective-permute-done.11.refs_0_, bf16[256,256]{1,0:T(8,128)(2,1)S(1)} %collective-permute-done.13.refs_1_), custom_call_target="tpu_custom_call" | custom-call | flops 1048576 | bytes 3690000 | tf_op jit(solution)/shard_map/pallas_call | solution.py:454
  (8 shorter events, 0.0 us)
Async XLA Ops:
  0.6 12.6 %collective-permute-start.3 = (bf16[256,256]{1,0:T(8,128)(2,1)}, bf16[256,256]{1,0:T(8,128)(2,1)S(1)}, u32[]{:S(2)}, u32[]{:S(2)}) collective-permute-start(bf16[256,256]{1,0:T(8,128)(2,1)} %k_ref.1), channel_id=1, source_target_pairs={{0,28},{4,0},{8,4},{12,8},{16,12},{20,16},{24,20},{28,24},{1,29},{... | collective-permute-start | bytes 393224 | tf_op jit(solution)/shard_map/ppermute | solution.py:354
  6.7 6.6 %collective-permute-start.4 = (bf16[256,256]{1,0:T(8,128)(2,1)}, bf16[256,256]{1,0:T(8,128)(2,1)S(1)}, u32[]{:S(2)}, u32[]{:S(2)}) collective-permute-start(bf16[256,256]{1,0:T(8,128)(2,1)} %v_ref.3), channel_id=1, source_target_pairs={{0,28},{4,0},{8,4},{12,8},{16,12},{20,16},{24,20},{28,24},{1,29},{... | collective-permute-start | bytes 393224 | tf_op jit(solution)/shard_map/ppermute | solution.py:354
  7.2 3.8 %collective-permute-start.1 = (s32[3,64]{1,0:T(4,128)}, s32[3,64]{1,0:T(4,128)S(1)}, u32[]{:S(2)}, u32[]{:S(2)}) collective-permute-start(s32[3,64]{1,0:T(4,128)} %own_ref.1), channel_id=1, source_target_pairs={{0,2},{1,3},{2,0},{3,1},{4,6},{5,7},{6,4},{7,5},{8,10},{9,11},{10,... | collective-permute-start | bytes 2312 | tf_op jit(solution)/shard_map/ppermute | solution.py:354
  8.7 3.2 %collective-permute-start = (s32[3,64]{1,0:T(4,128)}, s32[3,64]{1,0:T(4,128)S(1)}, u32[]{:S(2)}, u32[]{:S(2)}) collective-permute-start(s32[3,64]{1,0:T(4,128)} %own_ref.1), channel_id=1, source_target_pairs={{0,1},{1,2},{2,3},{3,0},{4,5},{5,6},{6,7},{7,4},{8,9},{9,10},{10,1... | collective-permute-start | bytes 2312 | tf_op jit(solution)/shard_map/ppermute | solution.py:354
  8.7 3.3 %collective-permute-start.2 = (s32[3,64]{1,0:T(4,128)}, s32[3,64]{1,0:T(4,128)S(1)}, u32[]{:S(2)}, u32[]{:S(2)}) collective-permute-start(s32[3,64]{1,0:T(4,128)} %own_ref.1), channel_id=1, source_target_pairs={{0,3},{1,0},{2,1},{3,2},{4,7},{5,4},{6,5},{7,6},{8,11},{9,8},{10,9... | collective-permute-start | bytes 2312 | tf_op jit(solution)/shard_map/ppermute | solution.py:354
  13.3 19.9 %collective-permute-start.6 = (bf16[256,512]{1,0:T(8,128)(2,1)S(1)}, bf16[256,512]{1,0:T(8,128)(2,1)S(1)}, u32[]{:S(2)}, u32[]{:S(2)}) collective-permute-start(bf16[256,512]{1,0:T(8,128)(2,1)S(1)} %shard_map.105.refs_0_), channel_id=1, source_target_pairs={{0,24},{4,28},{8,0},{12,4},{16,8},{20,12},{24,16},{28,20},{1,25},{... | collective-permute-start | bytes 786440 | tf_op jit(solution)/shard_map/ppermute | solution.py:354
  14.1 6.5 %collective-permute-start.5 = (bf16[16,256]{1,0:T(8,128)(2,1)S(1)}, bf16[16,256]{1,0:T(8,128)(2,1)S(1)}, u32[]{:S(2)}, u32[]{:S(2)}) collective-permute-start(bf16[16,256]{1,0:T(8,128)(2,1)S(1)} %get-tuple-element.43), channel_id=1, source_target_pairs={{0,28},{4,0},{8,4},{12,8},{16,12},{20,16},{24,20},{28,24},{1,29},{... | collective-permute-start | bytes 24584 | tf_op jit(solution)/shard_map/ppermute | solution.py:354
  22.5 13.8 %collective-permute-start.8 = (bf16[256,512]{1,0:T(8,128)(2,1)S(1)}, bf16[256,512]{1,0:T(8,128)(2,1)S(1)}, u32[]{:S(2)}, u32[]{:S(2)}) collective-permute-start(bf16[256,512]{1,0:T(8,128)(2,1)S(1)} %get-tuple-element.53), channel_id=1, source_target_pairs={{0,24},{4,28},{8,0},{12,4},{16,8},{20,12},{24,16},{28,20},{1,25},{... | collective-permute-start | bytes 786440 | tf_op jit(solution)/shard_map/ppermute | solution.py:354
  23.0 15.0 %collective-permute-start.9 = (bf16[256,512]{1,0:T(8,128)(2,1)S(1)}, bf16[256,512]{1,0:T(8,128)(2,1)S(1)}, u32[]{:S(2)}, u32[]{:S(2)}) collective-permute-start(bf16[256,512]{1,0:T(8,128)(2,1)S(1)} %get-tuple-element.52), channel_id=1, source_target_pairs={{0,4},{4,0},{8,12},{12,8},{16,20},{20,16},{24,28},{28,24},{1,5},{5... | collective-permute-start | bytes 786440 | tf_op jit(solution)/shard_map/ppermute | solution.py:359
  28.3 4.9 %collective-permute-start.7 = (bf16[16,256]{1,0:T(8,128)(2,1)S(1)}, bf16[16,256]{1,0:T(8,128)(2,1)S(1)}, u32[]{:S(2)}, u32[]{:S(2)}) collective-permute-start(bf16[16,256]{1,0:T(8,128)(2,1)S(1)} %get-tuple-element.43), channel_id=1, source_target_pairs={{0,20},{4,24},{8,28},{12,0},{16,4},{20,8},{24,12},{28,16},{1,21},{... | collective-permute-start | bytes 24584 | tf_op jit(solution)/shard_map/ppermute | solution.py:354
  34.4 8.1 %collective-permute-start.10 = (bf16[256,256]{1,0:T(8,128)(2,1)S(1)}, bf16[256,256]{1,0:T(8,128)(2,1)S(1)}, u32[]{:S(2)}, u32[]{:S(2)}) collective-permute-start(bf16[256,256]{1,0:T(8,128)(2,1)S(1)} %get-tuple-element.61), channel_id=1, source_target_pairs={{0,4},{4,8},{8,12},{12,16},{16,20},{20,24},{24,28},{28,0},{1,5},{5... | collective-permute-start | bytes 393224 | tf_op jit(solution)/shard_map/ppermute | solution.py:354
  36.2 8.1 %collective-permute-start.12 = (bf16[256,256]{1,0:T(8,128)(2,1)S(1)}, bf16[256,256]{1,0:T(8,128)(2,1)S(1)}, u32[]{:S(2)}, u32[]{:S(2)}) collective-permute-start(bf16[256,256]{1,0:T(8,128)(2,1)S(1)} %get-tuple-element.62), channel_id=1, source_target_pairs={{0,4},{4,8},{8,12},{12,16},{16,20},{20,24},{24,28},{28,0},{1,5},{5... | collective-permute-start | bytes 393224 | tf_op jit(solution)/shard_map/ppermute | solution.py:354
  42.6 6.8 %collective-permute-start.11 = (bf16[256,256]{1,0:T(8,128)(2,1)S(1)}, bf16[256,256]{1,0:T(8,128)(2,1)S(1)}, u32[]{:S(2)}, u32[]{:S(2)}) collective-permute-start(bf16[256,256]{1,0:T(8,128)(2,1)S(1)} %shard_map.112), channel_id=1, source_target_pairs={{0,8},{4,12},{8,16},{12,20},{16,24},{20,28},{24,0},{28,4},{1,9},{5... | collective-permute-start | bytes 393224 | tf_op jit(solution)/shard_map/ppermute | solution.py:354
  44.4 6.8 %collective-permute-start.13 = (bf16[256,256]{1,0:T(8,128)(2,1)S(1)}, bf16[256,256]{1,0:T(8,128)(2,1)S(1)}, u32[]{:S(2)}, u32[]{:S(2)}) collective-permute-start(bf16[256,256]{1,0:T(8,128)(2,1)S(1)} %shard_map.113), channel_id=1, source_target_pairs={{0,8},{4,12},{8,16},{12,20},{16,24},{20,28},{24,0},{28,4},{1,9},{5... | collective-permute-start | bytes 393224 | tf_op jit(solution)/shard_map/ppermute | solution.py:354

commit v15 on v12

--- a/solution.py
+++ b/solution.py
@@ -184,10 +184,10 @@
     norm_ref[...] = lse_ref[...] * LOG2E
 
 
-def hop_kernel(step, wanted, *refs):
+def hop_kernel(step, wanted, started, *refs):
     count = len(wanted)
     dqt_ins, dqt_refs, part_ref = refs[:count], refs[-count - 1 : -1], refs[-1]
-    k_ref, v_ref, qr_ref, do_ref, norm_ref, delta_ref, flag_ref = refs[count : -count - 1]
+    k_ref, v_ref, qr_ref, do_ref, norm_ref, delta_ref, flag_ref = refs[count * started : -count - 1]
     rows = qr_ref.shape[0]
     half = rows // 2
     heads = qr_ref.shape[1] // HEAD
@@ -210,8 +210,11 @@
                     norm[h : h + 1, queries.start :], delta[h : h + 1, queries.start :], False,
                 )
                 if queries.start:
-                    dqt_ref[to, : queries.start] = dqt_in[to, : queries.start]
-                dqt_ref[to, queries] = dqt_in[to, queries] + q_part
+                    zeros = jnp.zeros((HEAD, queries.start), F32)
+                    dqt_ref[to, : queries.start] = (
+                        dqt_in[to, : queries.start] if started else zeros
+                    )
+                dqt_ref[to, queries] = dqt_in[to, queries] + q_part if started else q_part
                 dv = v_part if dv is None else dv + v_part
                 dk = k_part if dk is None else dk + k_part
             part_ref[keys, pl.ds(2 * i * HEAD, HEAD)] = dk.astype(BF16)
@@ -228,12 +231,13 @@
         run(slice(0, rows), slice(half, rows))
 
 
-def merged_kernel(step, wanted, *refs):
-    count = len(wanted)
+def merged_kernel(step, wanted, started, *refs):
+    count = len(wanted) * started
     kv_ref = refs[count]
     width = kv_ref.shape[1] // 2
     hop_kernel(
-        step, wanted, *refs[:count], kv_ref.at[:, :width], kv_ref.at[:, width:], *refs[count + 1 :]
+        step, wanted, started, *refs[:count], kv_ref.at[:, :width], kv_ref.at[:, width:],
+        *refs[count + 1 :],
     )
 
 
@@ -244,7 +248,7 @@
 
 
 def own_kernel(groups, k_ref, v_ref, qr_ref, do_ref, norm_ref, delta_ref, *refs):
-    dqt_refs, part_ref = refs[:groups], refs[groups]
+    dqt_ins, dqt_refs, part_ref = refs[:groups], refs[groups : 2 * groups], refs[2 * groups]
     size = qr_ref.shape[1] // HEAD // groups
     norm = norm_ref[...]
     delta = delta_ref[...]
@@ -259,7 +263,7 @@
                 k_ref[:, kc], v_ref[:, kc], qr_ref[:, hc], do_ref[:, hc],
                 norm[h : h + 1], delta[h : h + 1], True,
             )
-            dqt_refs[g][to, :] = q_part
+            dqt_refs[g][to, :] = dqt_ins[g][to, :] + q_part
             dv = v_part if dv is None else dv + v_part
             dk = k_part if dk is None else dk + k_part
         part_ref[:, pl.ds(2 * g * HEAD, HEAD)] = dk
@@ -369,35 +373,40 @@
         ],
         micros=2,
     )(span_map, tables, lse, q, do, at)
+    held, _, v1 = lax.optimization_barrier((kv, shared[3], v1))
+    kv2 = shifted(held, -2)
+    (kv1,) = call(beside_kernel, [((rows, 2 * wide_k), BF16)], [VMEM] * 2)(k1, v1)
+    kv3 = shifted(kv1, -2)
+    dqs = []
+
+    def hop(step, wanted, arrived):
+        count = len(wanted)
+        started = len(dqs) > 0
+        before = [dqs[g] for g in wanted] if started else []
+        *new, part = call(
+            functools.partial(merged_kernel, step, wanted, started),
+            [((wide_q // groups, rows), F32)] * count + [((rows, 2 * HEAD * count), BF16)],
+            [VMEM] * (6 + len(before)),
+            micros=count,
+        )(*before, arrived, *shared)
+        if not started:
+            dqs.extend(new)
+        for g, dq in zip(wanted, new):
+            dqs[g] = dq
+        return part
+
+    part1 = hop(1, every, kv1)
+    swapped = exchanged(part1)
+    kr, kv2 = lax.optimization_barrier((kr, kv2))
     *dqs, own = call(
         functools.partial(own_kernel, groups),
         [((wide_q // groups, rows), F32)] * groups + [((rows, 2 * wide_k), F32)],
-        [VMEM] * 6,
+        [VMEM] * (6 + groups),
         micros=3,
-    )(kr, v_here, *shared[:4])
-
-    def hop(kernel, step, wanted, *arrived):
-        count = len(wanted)
-        before = [dqs[g] for g in wanted]
-        *new, part = call(
-            functools.partial(kernel, step, wanted),
-            [((wide_q // groups, rows), F32)] * count + [((rows, 2 * HEAD * count), BF16)],
-            [VMEM] * (5 + len(arrived) + count),
-            micros=count,
-        )(*before, *arrived, *shared)
-        for g, dq in zip(wanted, new):
-            dqs[g] = dq
-        return part
-
-    k1, _ = lax.optimization_barrier((k1, own))
-    (kv1,) = call(beside_kernel, [((rows, 2 * wide_k), BF16)], [VMEM] * 2)(k1, v1)
-    kv3 = shifted(kv1, -2)
-    part1 = hop(merged_kernel, 1, every, kv1)
-    held, _ = lax.optimization_barrier((kv, part1))
-    kv2 = shifted(held, -2)
-    swapped = exchanged(part1)
-    moved = [shifted(hop(merged_kernel, 3, (g,), kv3), 1) for g in every]
-    part2 = hop(merged_kernel, 2, every, kv2)
+    )(kr, v_here, *shared[:4], *dqs)
+
+    moved = [shifted(hop(3, (g,), kv3), 1) for g in every]
+    part2 = hop(2, every, kv2)
     dq, own = call(
         functools.partial(query_kernel, groups),
         [((rows, wide_q), BF16), ((rows, 2 * wide_k), F32)],

time: 51.3 us -> 50.3 us (0.981)
  starting transfers between devices: 23.6 us -> 18.4 us
  waiting for transfers between devices: 12.8 us -> 16.9 us
    ppermute x11, starting transfers between devices: 19.7 us -> 14.1 us  [shifted(): return lax.ppermute(value, axis, pairs)]
    ppermute x11, waiting for transfers between devices: 12.8 us -> 16.9 us  [shifted(): return lax.ppermute(value, axis, pairs)]
    ppermute x1, starting transfers between devices: 3.84 us -> 4.37 us  [exchanged(): lax.ppermute(value, 'ctx', [(source, source ^ 1) for source in range(coun...]
  transfers between devices with their start and end apart: 12 -> 12, of which waited for: 6 -> 7; matrix products, arithmetic and copies ran while one was open for 0% -> 0% of each run, Pallas kernels for 23% -> 26%
where the time goes in v15:
time: 50.3 us; the launch traced here: 50.1 us
  starting transfers between devices  18.4 us (37%)
  waiting for transfers between devices  16.9 us (34%)
  Pallas kernels  14 us (28%)
  between operations  0.73 us (1%)
    ppermute x11, waiting for transfers between devices, shifted(): return lax.ppermute(value, axis, pairs)  16.9 us
    ppermute x11, starting transfers between devices, shifted(): return lax.ppermute(value, axis, pairs)  14.1 us
    pallas_call x4, Pallas kernels, hop(): call(functools.partial(merged_kernel, step, wanted, started), [((wide_q /...  5.11 us
    ppermute x1, starting transfers between devices, exchanged(): lax.ppermute(value, 'ctx', [(source, source ^ 1) for source in range(coun...  4.37 us
    pallas_call x1, Pallas kernels, shards(): call(functools.partial(own_kernel, groups), [((wide_q // groups, rows), F...  3.04 us
    pallas_call x1, Pallas kernels, shards(): call(functools.partial(prep_kernel, groups), [((rows, wide_q), BF16)] * 2...  2.41 us
    pallas_call x1, Pallas kernels, shards(): call(key_kernel, [((rows, wide_k), BF16), ((rows, 2 * wide_k), BF16), ((H...  1.3 us
    pallas_call x1, Pallas kernels, shards(): call(functools.partial(query_kernel, groups), [((rows, wide_q), BF16), ((...  1.11 us
  transfers between devices with their start and end apart: 12, of which 7 were waited for; matrix products, arithmetic and copies ran while one was open for 0% of the time, Pallas kernels for 26%

profile of v15, /device:TPU:0, one launch (start us, length us, event | category | flops | bytes accessed | tf_op | source)
XLA Modules:
  0.0 50.1 jit_solution(2851693359283828723)
XLA Ops:
  0.6 3.0 %collective-permute-start.1 = (s32[3,64]{1,0:T(4,128)}, s32[3,64]{1,0:T(4,128)S(1)}, u32[]{:S(2)}, u32[]{:S(2)}) collective-permute-start(s32[3,64]{1,0:T(4,128)} %own_ref.1), channel_id=1, source_target_pairs={{0,2},{1,3},{2,0},{3,1},{4,6},{5,7},{6,4},{7,5},{8,10},{9,11},{10,... | collective-permute-start | bytes 2312 | tf_op jit(solution)/shard_map/ppermute | solution.py:332
  3.6 0.0 collective-permute-start
  3.6 1.7 %collective-permute-start.2 = (s32[3,64]{1,0:T(4,128)}, s32[3,64]{1,0:T(4,128)S(1)}, u32[]{:S(2)}, u32[]{:S(2)}) collective-permute-start(s32[3,64]{1,0:T(4,128)} %own_ref.1), channel_id=1, source_target_pairs={{0,3},{1,0},{2,1},{3,2},{4,7},{5,4},{6,5},{7,6},{8,11},{9,8},{10,9... | collective-permute-start | bytes 2312 | tf_op jit(solution)/shard_map/ppermute | solution.py:332
  5.4 4.6 %collective-permute-start.3 = (bf16[256,256]{1,0:T(8,128)(2,1)}, bf16[256,256]{1,0:T(8,128)(2,1)S(1)}, u32[]{:S(2)}, u32[]{:S(2)}) collective-permute-start(bf16[256,256]{1,0:T(8,128)(2,1)} %v_ref.3), channel_id=1, source_target_pairs={{0,28},{4,0},{8,4},{12,8},{16,12},{20,16},{24,20},{28,24},{1,29},{... | collective-permute-start | bytes 393224 | tf_op jit(solution)/shard_map/ppermute | solution.py:332
  10.0 1.3 %shard_map.103 = (bf16[256,256]{1,0:T(8,128)(2,1)S(1)}, bf16[256,512]{1,0:T(8,128)(2,1)S(1)}, f32[128,256]{1,0:T(8,128)S(1)}) custom-call(s32[3,64]{1,0:T(4,128)} %own_ref.1, s32[3,64]{1,0:T(4,128)S(1)} %collective-permute-done.p1_ref, s32[3,64]{1,0:T(4,128)S(1)} %collective-permute-done.1.p2_ref, s32[3,64]{1,0:T(4,128)S(1)} %collective-permute-done.2.p3_ref, ...), custom_call_target="tpu_custom_call" | custom-call | flops 1048576 | bytes 3690000 | tf_op jit(solution)/shard_map/pallas_call | solution.py:358
  11.3 1.6 %collective-permute-start.5 = (bf16[256,256]{1,0:T(8,128)(2,1)S(1)}, bf16[256,256]{1,0:T(8,128)(2,1)S(1)}, u32[]{:S(2)}, u32[]{:S(2)}) collective-permute-start(bf16[256,256]{1,0:T(8,128)(2,1)S(1)} %get-tuple-element.38.k_ref), channel_id=1, source_target_pairs={{0,28},{4,0},{8,4},{12,8},{16,12},{20,16},{24,20},{28,24},{1,29},{... | collective-permute-start | bytes 393224 | tf_op jit(solution)/shard_map/ppermute | solution.py:332
  12.8 2.4 %shard_map.104 = (bf16[256,1024]{1,0:T(8,128)(2,1)S(1)}, bf16[256,1024]{1,0:T(8,128)(2,1)S(1)}, f32[8,256]{1,0:T(8,128)S(1)}, f32[8,256]{1,0:T(8,128)S(1)}, s32[8,128]{1,0:T(8,128)S(1)}) custom-call(s32[8]{0:T(128)} %span_ref.1, f32[128,256]{1,0:T(8,128)S(1)} %get-tuple-element.33.tables_ref, f32[8,256]{1,0:T(8,128)} %lse_hbm.1, bf16[256,1024]{1,0:T(8,128)(2,1)} %q_hbm.1, ...), custom_call_target="tpu_custom_call" | custom-call | flops 1048576 | bytes 7380000 | tf_op jit(solution)/shard_map/pallas_call | solution.py:364
  15.2 0.0 collective-permute-done.3.v_ref
  15.2 0.5 %collective-permute-start.4 = (bf16[256,512]{1,0:T(8,128)(2,1)S(1)}, bf16[256,512]{1,0:T(8,128)(2,1)S(1)}, u32[]{:S(2)}, u32[]{:S(2)}) collective-permute-start(bf16[256,512]{1,0:T(8,128)(2,1)S(1)} %get-tuple-element.37), channel_id=1, source_target_pairs={{0,24},{4,28},{8,0},{12,4},{16,8},{20,12},{24,16},{28,20},{1,25},{... | collective-permute-start | bytes 786440 | tf_op jit(solution)/shard_map/ppermute | solution.py:332
  15.7 0.7 %collective-permute-done.5.k_ref = bf16[256,256]{1,0:T(8,128)(2,1)S(1)} collective-permute-done((bf16[256,256]{1,0:T(8,128)(2,1)S(1)}, bf16[256,256]{1,0:T(8,128)(2,1)S(1)}, u32[]{:S(2)}, u32[]{:S(2)}) %collective-permute-start.5) | collective-permute-done | bytes 131104 | tf_op jit(solution)/shard_map/ppermute | solution.py:332
  16.4 1.5 %collective-permute-start.6 = (bf16[256,512]{1,0:T(8,128)(2,1)S(1)}, bf16[256,512]{1,0:T(8,128)(2,1)S(1)}, u32[]{:S(2)}, u32[]{:S(2)}) collective-permute-start(bf16[256,512]{1,0:T(8,128)(2,1)S(1)} %shard_map.105.refs_0_), channel_id=1, source_target_pairs={{0,24},{4,28},{8,0},{12,4},{16,8},{20,12},{24,16},{28,20},{1,25},{... | collective-permute-start | bytes 786440 | tf_op jit(solution)/shard_map/ppermute | solution.py:332
  17.9 1.6 %shard_map.106 = (f32[512,256]{1,0:T(8,128)S(1)}, f32[512,256]{1,0:T(8,128)S(1)}, bf16[256,512]{1,0:T(8,128)(2,1)S(1)}) custom-call(bf16[256,512]{1,0:T(8,128)(2,1)S(1)} %shard_map.105.refs_0_, bf16[256,1024]{1,0:T(8,128)(2,1)S(1)} %get-tuple-element.39.refs_1_.qr_ref.refs_2_.refs_3_, bf16[256,1024]{1,0:T(8,128)(2,1)S(1)} %get-tuple-element.40.refs_2_.do_ref.refs_3_.refs_4_, ...), custom_call_target="tpu_custom_call" | custom-call | flops 1048576 | bytes 7380000 | tf_op jit(solution)/shard_map/pallas_call | solution.py:386
  19.6 4.4 %collective-permute-start.7 = (bf16[256,512]{1,0:T(8,128)(2,1)S(1)}, bf16[256,512]{1,0:T(8,128)(2,1)S(1)}, u32[]{:S(2)}, u32[]{:S(2)}) collective-permute-start(bf16[256,512]{1,0:T(8,128)(2,1)S(1)} %get-tuple-element.54), channel_id=1, source_target_pairs={{0,4},{4,0},{8,12},{12,8},{16,20},{20,16},{24,28},{28,24},{1,5},{5... | collective-permute-start | bytes 786440 | tf_op jit(solution)/shard_map/ppermute | solution.py:337
  23.9 0.5 collective-permute-done.4.refs_2_
  24.4 3.0 %shard_map.107 = (f32[512,256]{1,0:T(8,128)S(1)}, f32[512,256]{1,0:T(8,128)S(1)}, f32[256,512]{1,0:T(8,128)S(1)}) custom-call(bf16[256,256]{1,0:T(8,128)(2,1)S(1)} %get-tuple-element.38.k_ref, bf16[256,256]{1,0:T(8,128)(2,1)} %v_ref.3, bf16[256,1024]{1,0:T(8,128)(2,1)S(1)} %get-tuple-element.39.refs_1_.qr_ref.refs_2_.refs_3_, ...), custom_call_target="tpu_custom_call" | custom-call | flops 1048576 | bytes 11070000 | tf_op jit(solution)/shard_map/pallas_call | solution.py:401
  27.5 2.0 %collective-permute-done.6.refs_1_ = bf16[256,512]{1,0:T(8,128)(2,1)S(1)} collective-permute-done((bf16[256,512]{1,0:T(8,128)(2,1)S(1)}, bf16[256,512]{1,0:T(8,128)(2,1)S(1)}, u32[]{:S(2)}, u32[]{:S(2)}) %collective-permute-start.6) | collective-permute-done | bytes 262176 | tf_op jit(solution)/shard_map/ppermute | solution.py:332
  29.4 0.9 %shard_map.108 = (f32[512,256]{1,0:T(8,128)S(1)}, bf16[256,256]{1,0:T(8,128)(2,1)S(1)}) custom-call(f32[512,256]{1,0:T(8,128)S(1)} %get-tuple-element.46.refs_0_, bf16[256,512]{1,0:T(8,128)(2,1)S(1)} %collective-permute-done.6.refs_1_, bf16[256,1024]{1,0:T(8,128)(2,1)S(1)} %get-tuple-element.39.refs_1_.qr_ref.refs_2_.refs_3_, ...), custom_call_target="tpu_custom_call" | custom-call | flops 1048576 | bytes 3690000 | tf_op jit(solution)/shard_map/pallas_call | solution.py:386
  30.4 0.1 collective-permute-start.8
  30.4 0.9 %shard_map.109 = (f32[512,256]{1,0:T(8,128)S(1)}, bf16[256,256]{1,0:T(8,128)(2,1)S(1)}) custom-call(f32[512,256]{1,0:T(8,128)S(1)} %get-tuple-element.48.refs_0_, bf16[256,512]{1,0:T(8,128)(2,1)S(1)} %collective-permute-done.6.refs_1_, bf16[256,1024]{1,0:T(8,128)(2,1)S(1)} %get-tuple-element.39.refs_1_.qr_ref.refs_2_.refs_3_, ...), custom_call_target="tpu_custom_call" | custom-call | flops 1048576 | bytes 3690000 | tf_op jit(solution)/shard_map/pallas_call | solution.py:386
  31.4 1.0 %collective-permute-start.10 = (bf16[256,256]{1,0:T(8,128)(2,1)S(1)}, bf16[256,256]{1,0:T(8,128)(2,1)S(1)}, u32[]{:S(2)}, u32[]{:S(2)}) collective-permute-start(bf16[256,256]{1,0:T(8,128)(2,1)S(1)} %get-tuple-element.60), channel_id=1, source_target_pairs={{0,4},{4,8},{8,12},{12,16},{16,20},{20,24},{24,28},{28,0},{1,5},{5... | collective-permute-start | bytes 393224 | tf_op jit(solution)/shard_map/ppermute | solution.py:332
  32.4 1.6 %shard_map.110 = (f32[512,256]{1,0:T(8,128)S(1)}, f32[512,256]{1,0:T(8,128)S(1)}, bf16[256,512]{1,0:T(8,128)(2,1)S(1)}) custom-call(f32[512,256]{1,0:T(8,128)S(1)} %get-tuple-element.47.refs_0_, f32[512,256]{1,0:T(8,128)S(1)} %get-tuple-element.49.refs_1_, bf16[256,512]{1,0:T(8,128)(2,1)S(1)} %collective-permute-done.4.refs_2_, ...), custom_call_target="tpu_custom_call" | custom-call | flops 1048576 | bytes 7380000 | tf_op jit(solution)/shard_map/pallas_call | solution.py:386
  34.1 0.0 collective-permute-done.7.refs_3_.swapped_ref
  34.1 1.1 %shard_map.111 = (bf16[256,1024]{1,0:T(8,128)(2,1)}, f32[256,512]{1,0:T(8,128)S(1)}) custom-call(f32[128,256]{1,0:T(8,128)S(1)} %get-tuple-element.33.tables_ref, f32[512,256]{1,0:T(8,128)S(1)} %get-tuple-element.51.refs_0_, f32[512,256]{1,0:T(8,128)S(1)} %get-tuple-element.52.refs_1_, f32[256,512]{1,0:T(8,128)S(1)} %get-tuple-element.53.refs_2_, ...), custom_call_target="tpu_custom_call" | custom-call | flops 1048576 | bytes 3690000 | tf_op jit(solution)/shard_map/pallas_call | solution.py:410
  35.2 4.4 %collective-permute-done.8.three_ref = bf16[256,256]{1,0:T(8,128)(2,1)S(1)} collective-permute-done((bf16[256,256]{1,0:T(8,128)(2,1)S(1)}, bf16[256,256]{1,0:T(8,128)(2,1)S(1)}, u32[]{:S(2)}, u32[]{:S(2)}) %collective-permute-start.8) | collective-permute-done | bytes 131104 | tf_op jit(solution)/shard_map/ppermute | solution.py:332
  39.5 0.1 shard_map.112
  39.6 0.1 collective-permute-start.9
  39.7 2.7 %collective-permute-done.10.three_ref = bf16[256,256]{1,0:T(8,128)(2,1)S(1)} collective-permute-done((bf16[256,256]{1,0:T(8,128)(2,1)S(1)}, bf16[256,256]{1,0:T(8,128)(2,1)S(1)}, u32[]{:S(2)}, u32[]{:S(2)}) %collective-permute-start.10) | collective-permute-done | bytes 131104 | tf_op jit(solution)/shard_map/ppermute | solution.py:332
  42.4 0.1 shard_map.113
  42.4 0.1 collective-permute-start.11
  42.5 4.3 %collective-permute-done.9.refs_0_ = bf16[256,256]{1,0:T(8,128)(2,1)S(1)} collective-permute-done((bf16[256,256]{1,0:T(8,128)(2,1)S(1)}, bf16[256,256]{1,0:T(8,128)(2,1)S(1)}, u32[]{:S(2)}, u32[]{:S(2)}) %collective-permute-start.9) | collective-permute-done | bytes 131104 | tf_op jit(solution)/shard_map/ppermute | solution.py:332
  46.8 2.5 %collective-permute-done.11.refs_1_ = bf16[256,256]{1,0:T(8,128)(2,1)S(1)} collective-permute-done((bf16[256,256]{1,0:T(8,128)(2,1)S(1)}, bf16[256,256]{1,0:T(8,128)(2,1)S(1)}, u32[]{:S(2)}, u32[]{:S(2)}) %collective-permute-start.11) | collective-permute-done | bytes 131104 | tf_op jit(solution)/shard_map/ppermute | solution.py:332
  49.2 0.9 %shard_map.114 = (bf16[256,256]{1,0:T(8,128)(2,1)}, bf16[256,256]{1,0:T(8,128)(2,1)}) custom-call(f32[128,256]{1,0:T(8,128)S(1)} %get-tuple-element.33.tables_ref, f32[256,512]{1,0:T(8,128)S(1)} %get-tuple-element.56.own_ref, bf16[256,256]{1,0:T(8,128)(2,1)S(1)} %collective-permute-done.9.refs_0_, bf16[256,256]{1,0:T(8,128)(2,1)S(1)} %collective-permute-done.11.refs_1_), custom_call_target="tpu_custom_call" | custom-call | flops 1048576 | bytes 3690000 | tf_op jit(solution)/shard_map/pallas_call | solution.py:423
  (4 shorter events, 0.0 us)
Async XLA Ops:
  0.6 9.3 %collective-permute-start.1 = (s32[3,64]{1,0:T(4,128)}, s32[3,64]{1,0:T(4,128)S(1)}, u32[]{:S(2)}, u32[]{:S(2)}) collective-permute-start(s32[3,64]{1,0:T(4,128)} %own_ref.1), channel_id=1, source_target_pairs={{0,2},{1,3},{2,0},{3,1},{4,6},{5,7},{6,4},{7,5},{8,10},{9,11},{10,... | collective-permute-start | bytes 2312 | tf_op jit(solution)/shard_map/ppermute | solution.py:332
  3.6 6.3 %collective-permute-start = (s32[3,64]{1,0:T(4,128)}, s32[3,64]{1,0:T(4,128)S(1)}, u32[]{:S(2)}, u32[]{:S(2)}) collective-permute-start(s32[3,64]{1,0:T(4,128)} %own_ref.1), channel_id=1, source_target_pairs={{0,1},{1,2},{2,3},{3,0},{4,5},{5,6},{6,7},{7,4},{8,9},{9,10},{10,1... | collective-permute-start | bytes 2312 | tf_op jit(solution)/shard_map/ppermute | solution.py:332
  3.6 6.3 %collective-permute-start.2 = (s32[3,64]{1,0:T(4,128)}, s32[3,64]{1,0:T(4,128)S(1)}, u32[]{:S(2)}, u32[]{:S(2)}) collective-permute-start(s32[3,64]{1,0:T(4,128)} %own_ref.1), channel_id=1, source_target_pairs={{0,3},{1,0},{2,1},{3,2},{4,7},{5,4},{6,5},{7,6},{8,11},{9,8},{10,9... | collective-permute-start | bytes 2312 | tf_op jit(solution)/shard_map/ppermute | solution.py:332
  5.4 9.9 %collective-permute-start.3 = (bf16[256,256]{1,0:T(8,128)(2,1)}, bf16[256,256]{1,0:T(8,128)(2,1)S(1)}, u32[]{:S(2)}, u32[]{:S(2)}) collective-permute-start(bf16[256,256]{1,0:T(8,128)(2,1)} %v_ref.3), channel_id=1, source_target_pairs={{0,28},{4,0},{8,4},{12,8},{16,12},{20,16},{24,20},{28,24},{1,29},{... | collective-permute-start | bytes 393224 | tf_op jit(solution)/shard_map/ppermute | solution.py:332
  11.3 5.2 %collective-permute-start.5 = (bf16[256,256]{1,0:T(8,128)(2,1)S(1)}, bf16[256,256]{1,0:T(8,128)(2,1)S(1)}, u32[]{:S(2)}, u32[]{:S(2)}) collective-permute-start(bf16[256,256]{1,0:T(8,128)(2,1)S(1)} %get-tuple-element.38.k_ref), channel_id=1, source_target_pairs={{0,28},{4,0},{8,4},{12,8},{16,12},{20,16},{24,20},{28,24},{1,29},{... | collective-permute-start | bytes 393224 | tf_op jit(solution)/shard_map/ppermute | solution.py:332
  15.2 9.2 %collective-permute-start.4 = (bf16[256,512]{1,0:T(8,128)(2,1)S(1)}, bf16[256,512]{1,0:T(8,128)(2,1)S(1)}, u32[]{:S(2)}, u32[]{:S(2)}) collective-permute-start(bf16[256,512]{1,0:T(8,128)(2,1)S(1)} %get-tuple-element.37), channel_id=1, source_target_pairs={{0,24},{4,28},{8,0},{12,4},{16,8},{20,12},{24,16},{28,20},{1,25},{... | collective-permute-start | bytes 786440 | tf_op jit(solution)/shard_map/ppermute | solution.py:332
  16.4 13.0 %collective-permute-start.6 = (bf16[256,512]{1,0:T(8,128)(2,1)S(1)}, bf16[256,512]{1,0:T(8,128)(2,1)S(1)}, u32[]{:S(2)}, u32[]{:S(2)}) collective-permute-start(bf16[256,512]{1,0:T(8,128)(2,1)S(1)} %shard_map.105.refs_0_), channel_id=1, source_target_pairs={{0,24},{4,28},{8,0},{12,4},{16,8},{20,12},{24,16},{28,20},{1,25},{... | collective-permute-start | bytes 786440 | tf_op jit(solution)/shard_map/ppermute | solution.py:332
  19.6 14.5 %collective-permute-start.7 = (bf16[256,512]{1,0:T(8,128)(2,1)S(1)}, bf16[256,512]{1,0:T(8,128)(2,1)S(1)}, u32[]{:S(2)}, u32[]{:S(2)}) collective-permute-start(bf16[256,512]{1,0:T(8,128)(2,1)S(1)} %get-tuple-element.54), channel_id=1, source_target_pairs={{0,4},{4,0},{8,12},{12,8},{16,20},{20,16},{24,28},{28,24},{1,5},{5... | collective-permute-start | bytes 786440 | tf_op jit(solution)/shard_map/ppermute | solution.py:337
  30.4 9.2 %collective-permute-start.8 = (bf16[256,256]{1,0:T(8,128)(2,1)S(1)}, bf16[256,256]{1,0:T(8,128)(2,1)S(1)}, u32[]{:S(2)}, u32[]{:S(2)}) collective-permute-start(bf16[256,256]{1,0:T(8,128)(2,1)S(1)} %get-tuple-element.59), channel_id=1, source_target_pairs={{0,4},{4,8},{8,12},{12,16},{16,20},{20,24},{24,28},{28,0},{1,5},{5... | collective-permute-start | bytes 393224 | tf_op jit(solution)/shard_map/ppermute | solution.py:332
  31.4 11.0 %collective-permute-start.10 = (bf16[256,256]{1,0:T(8,128)(2,1)S(1)}, bf16[256,256]{1,0:T(8,128)(2,1)S(1)}, u32[]{:S(2)}, u32[]{:S(2)}) collective-permute-start(bf16[256,256]{1,0:T(8,128)(2,1)S(1)} %get-tuple-element.60), channel_id=1, source_target_pairs={{0,4},{4,8},{8,12},{12,16},{16,20},{20,24},{24,28},{28,0},{1,5},{5... | collective-permute-start | bytes 393224 | tf_op jit(solution)/shard_map/ppermute | solution.py:332
  39.6 7.2 %collective-permute-start.9 = (bf16[256,256]{1,0:T(8,128)(2,1)S(1)}, bf16[256,256]{1,0:T(8,128)(2,1)S(1)}, u32[]{:S(2)}, u32[]{:S(2)}) collective-permute-start(bf16[256,256]{1,0:T(8,128)(2,1)S(1)} %shard_map.112), channel_id=1, source_target_pairs={{0,8},{4,12},{8,16},{12,20},{16,24},{20,28},{24,0},{28,4},{1,9},{5... | collective-permute-start | bytes 393224 | tf_op jit(solution)/shard_map/ppermute | solution.py:332
  42.4 6.8 %collective-permute-start.11 = (bf16[256,256]{1,0:T(8,128)(2,1)S(1)}, bf16[256,256]{1,0:T(8,128)(2,1)S(1)}, u32[]{:S(2)}, u32[]{:S(2)}) collective-permute-start(bf16[256,256]{1,0:T(8,128)(2,1)S(1)} %shard_map.113), channel_id=1, source_target_pairs={{0,8},{4,12},{8,16},{12,20},{16,24},{20,28},{24,0},{28,4},{1,9},{5... | collective-permute-start | bytes 393224 | tf_op jit(solution)/shard_map/ppermute | solution.py:332

commit v16 on v15

--- a/solution.py
+++ b/solution.py
@@ -373,8 +373,7 @@
         ],
         micros=2,
     )(span_map, tables, lse, q, do, at)
-    held, _, v1 = lax.optimization_barrier((kv, shared[3], v1))
-    kv2 = shifted(held, -2)
+    k1, _, v1 = lax.optimization_barrier((k1, shared[3], v1))
     (kv1,) = call(beside_kernel, [((rows, 2 * wide_k), BF16)], [VMEM] * 2)(k1, v1)
     kv3 = shifted(kv1, -2)
     dqs = []
@@ -397,7 +396,8 @@
 
     part1 = hop(1, every, kv1)
     swapped = exchanged(part1)
-    kr, kv2 = lax.optimization_barrier((kr, kv2))
+    held, _ = lax.optimization_barrier((kv, part1))
+    kv2 = shifted(held, -2)
     *dqs, own = call(
         functools.partial(own_kernel, groups),
         [((wide_q // groups, rows), F32)] * groups + [((rows, 2 * wide_k), F32)],

time: 50.3 us -> 48.5 us (0.964)
  waiting for transfers between devices: 16.9 us -> 9.03 us
  starting transfers between devices: 18.4 us -> 24.5 us
    ppermute x11, waiting for transfers between devices: 16.9 us -> 9.03 us  [shifted(): return lax.ppermute(value, axis, pairs)]
    ppermute x11, starting transfers between devices: 14.1 us -> 20.7 us  [shifted(): return lax.ppermute(value, axis, pairs)]
    ppermute x1, starting transfers between devices: 4.37 us -> 3.85 us  [exchanged(): lax.ppermute(value, 'ctx', [(source, source ^ 1) for source in range(coun...]
  transfers between devices with their start and end apart: 12 -> 12, of which waited for: 7 -> 4; matrix products, arithmetic and copies ran while one was open for 0% -> 0% of each run, Pallas kernels for 26% -> 27%
where the time goes in v16:
time: 48.5 us; the launch traced here: 48.3 us
  starting transfers between devices  24.5 us (51%)
  Pallas kernels  14 us (29%)
  waiting for transfers between devices  9.03 us (19%)
  between operations  0.72 us (1%)
    ppermute x11, starting transfers between devices, shifted(): return lax.ppermute(value, axis, pairs)  20.7 us
    ppermute x11, waiting for transfers between devices, shifted(): return lax.ppermute(value, axis, pairs)  9.03 us
    pallas_call x4, Pallas kernels, hop(): call(functools.partial(merged_kernel, step, wanted, started), [((wide_q /...  5.12 us
    ppermute x1, starting transfers between devices, exchanged(): lax.ppermute(value, 'ctx', [(source, source ^ 1) for source in range(coun...  3.85 us
    pallas_call x1, Pallas kernels, shards(): call(functools.partial(own_kernel, groups), [((wide_q // groups, rows), F...  3.04 us
    pallas_call x1, Pallas kernels, shards(): call(functools.partial(prep_kernel, groups), [((rows, wide_q), BF16)] * 2...  2.41 us
    pallas_call x1, Pallas kernels, shards(): call(key_kernel, [((rows, wide_k), BF16), ((rows, 2 * wide_k), BF16), ((H...  1.3 us
    pallas_call x1, Pallas kernels, shards(): call(functools.partial(query_kernel, groups), [((rows, wide_q), BF16), ((...  1.11 us
  transfers between devices with their start and end apart: 12, of which 4 were waited for; matrix products, arithmetic and copies ran while one was open for 0% of the time, Pallas kernels for 27%

profile of v16, /device:TPU:0, one launch (start us, length us, event | category | flops | bytes accessed | tf_op | source)
XLA Modules:
  0.0 48.3 jit_solution(10709199208173269519)
XLA Ops:
  0.6 3.0 %collective-permute-start.1 = (s32[3,64]{1,0:T(4,128)}, s32[3,64]{1,0:T(4,128)S(1)}, u32[]{:S(2)}, u32[]{:S(2)}) collective-permute-start(s32[3,64]{1,0:T(4,128)} %own_ref.1), channel_id=1, source_target_pairs={{0,2},{1,3},{2,0},{3,1},{4,6},{5,7},{6,4},{7,5},{8,10},{9,11},{10,... | collective-permute-start | bytes 2312 | tf_op jit(solution)/shard_map/ppermute | solution.py:332
  3.6 0.0 collective-permute-start
  3.6 1.7 %collective-permute-start.2 = (s32[3,64]{1,0:T(4,128)}, s32[3,64]{1,0:T(4,128)S(1)}, u32[]{:S(2)}, u32[]{:S(2)}) collective-permute-start(s32[3,64]{1,0:T(4,128)} %own_ref.1), channel_id=1, source_target_pairs={{0,3},{1,0},{2,1},{3,2},{4,7},{5,4},{6,5},{7,6},{8,11},{9,8},{10,9... | collective-permute-start | bytes 2312 | tf_op jit(solution)/shard_map/ppermute | solution.py:332
  5.4 4.6 %collective-permute-start.4 = (bf16[256,256]{1,0:T(8,128)(2,1)}, bf16[256,256]{1,0:T(8,128)(2,1)S(1)}, u32[]{:S(2)}, u32[]{:S(2)}) collective-permute-start(bf16[256,256]{1,0:T(8,128)(2,1)} %v_ref.3), channel_id=1, source_target_pairs={{0,28},{4,0},{8,4},{12,8},{16,12},{20,16},{24,20},{28,24},{1,29},{... | collective-permute-start | bytes 393224 | tf_op jit(solution)/shard_map/ppermute | solution.py:332
  9.9 0.0 collective-permute-done.1.p2_ref
  9.9 0.0 collective-permute-done.p1_ref
  10.0 1.3 %shard_map.103 = (bf16[256,256]{1,0:T(8,128)(2,1)S(1)}, bf16[256,512]{1,0:T(8,128)(2,1)S(1)}, f32[128,256]{1,0:T(8,128)S(1)}) custom-call(s32[3,64]{1,0:T(4,128)} %own_ref.1, s32[3,64]{1,0:T(4,128)S(1)} %collective-permute-done.p1_ref, s32[3,64]{1,0:T(4,128)S(1)} %collective-permute-done.1.p2_ref, s32[3,64]{1,0:T(4,128)S(1)} %collective-permute-done.2.p3_ref, ...), custom_call_target="tpu_custom_call" | custom-call | flops 1048576 | bytes 3690000 | tf_op jit(solution)/shard_map/pallas_call | solution.py:358
  11.3 1.6 %collective-permute-start.3 = (bf16[256,256]{1,0:T(8,128)(2,1)S(1)}, bf16[256,256]{1,0:T(8,128)(2,1)S(1)}, u32[]{:S(2)}, u32[]{:S(2)}) collective-permute-start(bf16[256,256]{1,0:T(8,128)(2,1)S(1)} %get-tuple-element.33.k_ref), channel_id=1, source_target_pairs={{0,28},{4,0},{8,4},{12,8},{16,12},{20,16},{24,20},{28,24},{1,29},{... | collective-permute-start | bytes 393224 | tf_op jit(solution)/shard_map/ppermute | solution.py:332
  12.8 2.4 %shard_map.104 = (bf16[256,1024]{1,0:T(8,128)(2,1)S(1)}, bf16[256,1024]{1,0:T(8,128)(2,1)S(1)}, f32[8,256]{1,0:T(8,128)S(1)}, f32[8,256]{1,0:T(8,128)S(1)}, s32[8,128]{1,0:T(8,128)S(1)}) custom-call(s32[8]{0:T(128)} %span_ref.1, f32[128,256]{1,0:T(8,128)S(1)} %get-tuple-element.32.tables_ref, f32[8,256]{1,0:T(8,128)} %lse_hbm.1, bf16[256,1024]{1,0:T(8,128)(2,1)} %q_hbm.1, ...), custom_call_target="tpu_custom_call" | custom-call | flops 1048576 | bytes 7380000 | tf_op jit(solution)/shard_map/pallas_call | solution.py:364
  15.2 0.0 collective-permute-done.4.v_ref
  15.2 1.1 %collective-permute-done.3.k_ref = bf16[256,256]{1,0:T(8,128)(2,1)S(1)} collective-permute-done((bf16[256,256]{1,0:T(8,128)(2,1)S(1)}, bf16[256,256]{1,0:T(8,128)(2,1)S(1)}, u32[]{:S(2)}, u32[]{:S(2)}) %collective-permute-start.3) | collective-permute-done | bytes 131104 | tf_op jit(solution)/shard_map/ppermute | solution.py:332
  16.4 1.6 %collective-permute-start.5 = (bf16[256,512]{1,0:T(8,128)(2,1)S(1)}, bf16[256,512]{1,0:T(8,128)(2,1)S(1)}, u32[]{:S(2)}, u32[]{:S(2)}) collective-permute-start(bf16[256,512]{1,0:T(8,128)(2,1)S(1)} %shard_map.105.refs_0_), channel_id=1, source_target_pairs={{0,24},{4,28},{8,0},{12,4},{16,8},{20,12},{24,16},{28,20},{1,25},{... | collective-permute-start | bytes 786440 | tf_op jit(solution)/shard_map/ppermute | solution.py:332
  17.9 1.6 %shard_map.106 = (f32[512,256]{1,0:T(8,128)S(1)}, f32[512,256]{1,0:T(8,128)S(1)}, bf16[256,512]{1,0:T(8,128)(2,1)S(1)}) custom-call(bf16[256,512]{1,0:T(8,128)(2,1)S(1)} %shard_map.105.refs_0_, bf16[256,1024]{1,0:T(8,128)(2,1)S(1)} %get-tuple-element.34.refs_1_.qr_ref.refs_2_.refs_3_, bf16[256,1024]{1,0:T(8,128)(2,1)S(1)} %get-tuple-element.35.refs_2_.do_ref.refs_3_.refs_4_, ...), custom_call_target="tpu_custom_call" | custom-call | flops 1048576 | bytes 7380000 | tf_op jit(solution)/shard_map/pallas_call | solution.py:385
  19.6 0.5 %collective-permute-start.6 = (bf16[256,512]{1,0:T(8,128)(2,1)S(1)}, bf16[256,512]{1,0:T(8,128)(2,1)S(1)}, u32[]{:S(2)}, u32[]{:S(2)}) collective-permute-start(bf16[256,512]{1,0:T(8,128)(2,1)S(1)} %get-tuple-element.49), channel_id=1, source_target_pairs={{0,24},{4,28},{8,0},{12,4},{16,8},{20,12},{24,16},{28,20},{1,25},{... | collective-permute-start | bytes 786440 | tf_op jit(solution)/shard_map/ppermute | solution.py:332
  20.1 3.8 %collective-permute-start.7 = (bf16[256,512]{1,0:T(8,128)(2,1)S(1)}, bf16[256,512]{1,0:T(8,128)(2,1)S(1)}, u32[]{:S(2)}, u32[]{:S(2)}) collective-permute-start(bf16[256,512]{1,0:T(8,128)(2,1)S(1)} %get-tuple-element.48), channel_id=1, source_target_pairs={{0,4},{4,0},{8,12},{12,8},{16,20},{20,16},{24,28},{28,24},{1,5},{5... | collective-permute-start | bytes 786440 | tf_op jit(solution)/shard_map/ppermute | solution.py:337
  23.9 3.0 %shard_map.107 = (f32[512,256]{1,0:T(8,128)S(1)}, f32[512,256]{1,0:T(8,128)S(1)}, f32[256,512]{1,0:T(8,128)S(1)}) custom-call(bf16[256,256]{1,0:T(8,128)(2,1)S(1)} %get-tuple-element.33.k_ref, bf16[256,256]{1,0:T(8,128)(2,1)} %v_ref.3, bf16[256,1024]{1,0:T(8,128)(2,1)S(1)} %get-tuple-element.34.refs_1_.qr_ref.refs_2_.refs_3_, ...), custom_call_target="tpu_custom_call" | custom-call | flops 1048576 | bytes 11070000 | tf_op jit(solution)/shard_map/pallas_call | solution.py:401
  27.0 0.0 collective-permute-done.5.refs_1_
  27.0 0.9 %shard_map.108 = (f32[512,256]{1,0:T(8,128)S(1)}, bf16[256,256]{1,0:T(8,128)(2,1)S(1)}) custom-call(f32[512,256]{1,0:T(8,128)S(1)} %get-tuple-element.43.refs_0_, bf16[256,512]{1,0:T(8,128)(2,1)S(1)} %collective-permute-done.5.refs_1_, bf16[256,1024]{1,0:T(8,128)(2,1)S(1)} %get-tuple-element.34.refs_1_.qr_ref.refs_2_.refs_3_, ...), custom_call_target="tpu_custom_call" | custom-call | flops 1048576 | bytes 3690000 | tf_op jit(solution)/shard_map/pallas_call | solution.py:385
  27.9 1.9 %collective-permute-start.8 = (bf16[256,256]{1,0:T(8,128)(2,1)S(1)}, bf16[256,256]{1,0:T(8,128)(2,1)S(1)}, u32[]{:S(2)}, u32[]{:S(2)}) collective-permute-start(bf16[256,256]{1,0:T(8,128)(2,1)S(1)} %get-tuple-element.57), channel_id=1, source_target_pairs={{0,4},{4,8},{8,12},{12,16},{16,20},{20,24},{24,28},{28,0},{1,5},{5... | collective-permute-start | bytes 393224 | tf_op jit(solution)/shard_map/ppermute | solution.py:332
  29.8 0.9 %shard_map.109 = (f32[512,256]{1,0:T(8,128)S(1)}, bf16[256,256]{1,0:T(8,128)(2,1)S(1)}) custom-call(f32[512,256]{1,0:T(8,128)S(1)} %get-tuple-element.45.refs_0_, bf16[256,512]{1,0:T(8,128)(2,1)S(1)} %collective-permute-done.5.refs_1_, bf16[256,1024]{1,0:T(8,128)(2,1)S(1)} %get-tuple-element.34.refs_1_.qr_ref.refs_2_.refs_3_, ...), custom_call_target="tpu_custom_call" | custom-call | flops 1048576 | bytes 3690000 | tf_op jit(solution)/shard_map/pallas_call | solution.py:385
  30.8 1.6 %collective-permute-start.10 = (bf16[256,256]{1,0:T(8,128)(2,1)S(1)}, bf16[256,256]{1,0:T(8,128)(2,1)S(1)}, u32[]{:S(2)}, u32[]{:S(2)}) collective-permute-start(bf16[256,256]{1,0:T(8,128)(2,1)S(1)} %get-tuple-element.58), channel_id=1, source_target_pairs={{0,4},{4,8},{8,12},{12,16},{16,20},{20,24},{24,28},{28,0},{1,5},{5... | collective-permute-start | bytes 393224 | tf_op jit(solution)/shard_map/ppermute | solution.py:332
  32.4 1.6 %shard_map.110 = (f32[512,256]{1,0:T(8,128)S(1)}, f32[512,256]{1,0:T(8,128)S(1)}, bf16[256,512]{1,0:T(8,128)(2,1)S(1)}) custom-call(f32[512,256]{1,0:T(8,128)S(1)} %get-tuple-element.44.refs_0_, f32[512,256]{1,0:T(8,128)S(1)} %get-tuple-element.46.refs_1_, bf16[256,512]{1,0:T(8,128)(2,1)S(1)} %collective-permute-done.6.refs_2_, ...), custom_call_target="tpu_custom_call" | custom-call | flops 1048576 | bytes 7380000 | tf_op jit(solution)/shard_map/pallas_call | solution.py:385
  34.0 1.1 %shard_map.111 = (bf16[256,1024]{1,0:T(8,128)(2,1)}, f32[256,512]{1,0:T(8,128)S(1)}) custom-call(f32[128,256]{1,0:T(8,128)S(1)} %get-tuple-element.32.tables_ref, f32[512,256]{1,0:T(8,128)S(1)} %get-tuple-element.50.refs_0_, f32[512,256]{1,0:T(8,128)S(1)} %get-tuple-element.51.refs_1_, f32[256,512]{1,0:T(8,128)S(1)} %get-tuple-element.52.refs_2_, ...), custom_call_target="tpu_custom_call" | custom-call | flops 1048576 | bytes 3690000 | tf_op jit(solution)/shard_map/pallas_call | solution.py:410
  35.1 2.6 %collective-permute-done.8.three_ref = bf16[256,256]{1,0:T(8,128)(2,1)S(1)} collective-permute-done((bf16[256,256]{1,0:T(8,128)(2,1)S(1)}, bf16[256,256]{1,0:T(8,128)(2,1)S(1)}, u32[]{:S(2)}, u32[]{:S(2)}) %collective-permute-start.8) | collective-permute-done | bytes 131104 | tf_op jit(solution)/shard_map/ppermute | solution.py:332
  37.7 0.1 shard_map.112
  37.8 1.6 %collective-permute-start.9 = (bf16[256,256]{1,0:T(8,128)(2,1)S(1)}, bf16[256,256]{1,0:T(8,128)(2,1)S(1)}, u32[]{:S(2)}, u32[]{:S(2)}) collective-permute-start(bf16[256,256]{1,0:T(8,128)(2,1)S(1)} %shard_map.112), channel_id=1, source_target_pairs={{0,8},{4,12},{8,16},{12,20},{16,24},{20,28},{24,0},{28,4},{1,9},{5... | collective-permute-start | bytes 393224 | tf_op jit(solution)/shard_map/ppermute | solution.py:332
  39.4 0.0 collective-permute-done.10.three_ref
  39.4 0.1 shard_map.113
  39.4 2.7 %collective-permute-start.11 = (bf16[256,256]{1,0:T(8,128)(2,1)S(1)}, bf16[256,256]{1,0:T(8,128)(2,1)S(1)}, u32[]{:S(2)}, u32[]{:S(2)}) collective-permute-start(bf16[256,256]{1,0:T(8,128)(2,1)S(1)} %shard_map.113), channel_id=1, source_target_pairs={{0,8},{4,12},{8,16},{12,20},{16,24},{20,28},{24,0},{28,4},{1,9},{5... | collective-permute-start | bytes 393224 | tf_op jit(solution)/shard_map/ppermute | solution.py:332
  42.1 3.5 %collective-permute-done.9.refs_0_ = bf16[256,256]{1,0:T(8,128)(2,1)S(1)} collective-permute-done((bf16[256,256]{1,0:T(8,128)(2,1)S(1)}, bf16[256,256]{1,0:T(8,128)(2,1)S(1)}, u32[]{:S(2)}, u32[]{:S(2)}) %collective-permute-start.9) | collective-permute-done | bytes 131104 | tf_op jit(solution)/shard_map/ppermute | solution.py:332
  45.6 1.8 %collective-permute-done.11.refs_1_ = bf16[256,256]{1,0:T(8,128)(2,1)S(1)} collective-permute-done((bf16[256,256]{1,0:T(8,128)(2,1)S(1)}, bf16[256,256]{1,0:T(8,128)(2,1)S(1)}, u32[]{:S(2)}, u32[]{:S(2)}) %collective-permute-start.11) | collective-permute-done | bytes 131104 | tf_op jit(solution)/shard_map/ppermute | solution.py:332
  47.4 0.9 %shard_map.114 = (bf16[256,256]{1,0:T(8,128)(2,1)}, bf16[256,256]{1,0:T(8,128)(2,1)}) custom-call(f32[128,256]{1,0:T(8,128)S(1)} %get-tuple-element.32.tables_ref, f32[256,512]{1,0:T(8,128)S(1)} %get-tuple-element.54.own_ref, bf16[256,256]{1,0:T(8,128)(2,1)S(1)} %collective-permute-done.9.refs_0_, bf16[256,256]{1,0:T(8,128)(2,1)S(1)} %collective-permute-done.11.refs_1_), custom_call_target="tpu_custom_call" | custom-call | flops 1048576 | bytes 3690000 | tf_op jit(solution)/shard_map/pallas_call | solution.py:423
  (4 shorter events, 0.0 us)
Async XLA Ops:
  0.6 9.3 %collective-permute-start.1 = (s32[3,64]{1,0:T(4,128)}, s32[3,64]{1,0:T(4,128)S(1)}, u32[]{:S(2)}, u32[]{:S(2)}) collective-permute-start(s32[3,64]{1,0:T(4,128)} %own_ref.1), channel_id=1, source_target_pairs={{0,2},{1,3},{2,0},{3,1},{4,6},{5,7},{6,4},{7,5},{8,10},{9,11},{10,... | collective-permute-start | bytes 2312 | tf_op jit(solution)/shard_map/ppermute | solution.py:332
  3.6 6.3 %collective-permute-start = (s32[3,64]{1,0:T(4,128)}, s32[3,64]{1,0:T(4,128)S(1)}, u32[]{:S(2)}, u32[]{:S(2)}) collective-permute-start(s32[3,64]{1,0:T(4,128)} %own_ref.1), channel_id=1, source_target_pairs={{0,1},{1,2},{2,3},{3,0},{4,5},{5,6},{6,7},{7,4},{8,9},{9,10},{10,1... | collective-permute-start | bytes 2312 | tf_op jit(solution)/shard_map/ppermute | solution.py:332
  3.6 6.3 %collective-permute-start.2 = (s32[3,64]{1,0:T(4,128)}, s32[3,64]{1,0:T(4,128)S(1)}, u32[]{:S(2)}, u32[]{:S(2)}) collective-permute-start(s32[3,64]{1,0:T(4,128)} %own_ref.1), channel_id=1, source_target_pairs={{0,3},{1,0},{2,1},{3,2},{4,7},{5,4},{6,5},{7,6},{8,11},{9,8},{10,9... | collective-permute-start | bytes 2312 | tf_op jit(solution)/shard_map/ppermute | solution.py:332
  5.4 9.9 %collective-permute-start.4 = (bf16[256,256]{1,0:T(8,128)(2,1)}, bf16[256,256]{1,0:T(8,128)(2,1)S(1)}, u32[]{:S(2)}, u32[]{:S(2)}) collective-permute-start(bf16[256,256]{1,0:T(8,128)(2,1)} %v_ref.3), channel_id=1, source_target_pairs={{0,28},{4,0},{8,4},{12,8},{16,12},{20,16},{24,20},{28,24},{1,29},{... | collective-permute-start | bytes 393224 | tf_op jit(solution)/shard_map/ppermute | solution.py:332
  11.3 5.1 %collective-permute-start.3 = (bf16[256,256]{1,0:T(8,128)(2,1)S(1)}, bf16[256,256]{1,0:T(8,128)(2,1)S(1)}, u32[]{:S(2)}, u32[]{:S(2)}) collective-permute-start(bf16[256,256]{1,0:T(8,128)(2,1)S(1)} %get-tuple-element.33.k_ref), channel_id=1, source_target_pairs={{0,28},{4,0},{8,4},{12,8},{16,12},{20,16},{24,20},{28,24},{1,29},{... | collective-permute-start | bytes 393224 | tf_op jit(solution)/shard_map/ppermute | solution.py:332
  16.4 10.6 %collective-permute-start.5 = (bf16[256,512]{1,0:T(8,128)(2,1)S(1)}, bf16[256,512]{1,0:T(8,128)(2,1)S(1)}, u32[]{:S(2)}, u32[]{:S(2)}) collective-permute-start(bf16[256,512]{1,0:T(8,128)(2,1)S(1)} %shard_map.105.refs_0_), channel_id=1, source_target_pairs={{0,24},{4,28},{8,0},{12,4},{16,8},{20,12},{24,16},{28,20},{1,25},{... | collective-permute-start | bytes 786440 | tf_op jit(solution)/shard_map/ppermute | solution.py:332
  19.6 12.8 %collective-permute-start.6 = (bf16[256,512]{1,0:T(8,128)(2,1)S(1)}, bf16[256,512]{1,0:T(8,128)(2,1)S(1)}, u32[]{:S(2)}, u32[]{:S(2)}) collective-permute-start(bf16[256,512]{1,0:T(8,128)(2,1)S(1)} %get-tuple-element.49), channel_id=1, source_target_pairs={{0,24},{4,28},{8,0},{12,4},{16,8},{20,12},{24,16},{28,20},{1,25},{... | collective-permute-start | bytes 786440 | tf_op jit(solution)/shard_map/ppermute | solution.py:332
  20.1 13.9 %collective-permute-start.7 = (bf16[256,512]{1,0:T(8,128)(2,1)S(1)}, bf16[256,512]{1,0:T(8,128)(2,1)S(1)}, u32[]{:S(2)}, u32[]{:S(2)}) collective-permute-start(bf16[256,512]{1,0:T(8,128)(2,1)S(1)} %get-tuple-element.48), channel_id=1, source_target_pairs={{0,4},{4,0},{8,12},{12,8},{16,20},{20,16},{24,28},{28,24},{1,5},{5... | collective-permute-start | bytes 786440 | tf_op jit(solution)/shard_map/ppermute | solution.py:337
  27.9 9.8 %collective-permute-start.8 = (bf16[256,256]{1,0:T(8,128)(2,1)S(1)}, bf16[256,256]{1,0:T(8,128)(2,1)S(1)}, u32[]{:S(2)}, u32[]{:S(2)}) collective-permute-start(bf16[256,256]{1,0:T(8,128)(2,1)S(1)} %get-tuple-element.57), channel_id=1, source_target_pairs={{0,4},{4,8},{8,12},{12,16},{16,20},{20,24},{24,28},{28,0},{1,5},{5... | collective-permute-start | bytes 393224 | tf_op jit(solution)/shard_map/ppermute | solution.py:332
  30.8 8.6 %collective-permute-start.10 = (bf16[256,256]{1,0:T(8,128)(2,1)S(1)}, bf16[256,256]{1,0:T(8,128)(2,1)S(1)}, u32[]{:S(2)}, u32[]{:S(2)}) collective-permute-start(bf16[256,256]{1,0:T(8,128)(2,1)S(1)} %get-tuple-element.58), channel_id=1, source_target_pairs={{0,4},{4,8},{8,12},{12,16},{16,20},{20,24},{24,28},{28,0},{1,5},{5... | collective-permute-start | bytes 393224 | tf_op jit(solution)/shard_map/ppermute | solution.py:332
  37.8 7.8 %collective-permute-start.9 = (bf16[256,256]{1,0:T(8,128)(2,1)S(1)}, bf16[256,256]{1,0:T(8,128)(2,1)S(1)}, u32[]{:S(2)}, u32[]{:S(2)}) collective-permute-start(bf16[256,256]{1,0:T(8,128)(2,1)S(1)} %shard_map.112), channel_id=1, source_target_pairs={{0,8},{4,12},{8,16},{12,20},{16,24},{20,28},{24,0},{28,4},{1,9},{5... | collective-permute-start | bytes 393224 | tf_op jit(solution)/shard_map/ppermute | solution.py:332
  39.4 8.0 %collective-permute-start.11 = (bf16[256,256]{1,0:T(8,128)(2,1)S(1)}, bf16[256,256]{1,0:T(8,128)(2,1)S(1)}, u32[]{:S(2)}, u32[]{:S(2)}) collective-permute-start(bf16[256,256]{1,0:T(8,128)(2,1)S(1)} %shard_map.113), channel_id=1, source_target_pairs={{0,8},{4,12},{8,16},{12,20},{16,24},{20,28},{24,0},{28,4},{1,9},{5... | collective-permute-start | bytes 393224 | tf_op jit(solution)/shard_map/ppermute | solution.py:332

commit v17 on v16

--- a/solution.py
+++ b/solution.py
@@ -118,7 +118,7 @@
     return value_part, key_part, query_part
 
 
-def key_kernel(own_ref, p1_ref, p2_ref, p3_ref, k_ref, v_ref, kr_ref, kv_ref, tables_ref):
+def key_kernel(own_ref, p1_ref, p2_ref, p3_ref, k_ref, kr_ref, tables_ref):
     pieces = (own_ref[...], p1_ref[...], p2_ref[...], p3_ref[...])
     count = len(pieces)
     head = lax.axis_index("head")
@@ -135,10 +135,7 @@
     wide, signed = row_tables(cosine_t, sine_t)
     for g in range(k_ref.shape[1] // HEAD):
         cols = pl.ds(g * HEAD, HEAD)
-        key = rotated(k_ref[:, cols].astype(F32), wide, signed).astype(BF16)
-        kr_ref[:, cols] = key
-        kv_ref[:, cols] = key
-    kv_ref[:, k_ref.shape[1] :] = v_ref[...]
+        kr_ref[:, cols] = rotated(k_ref[:, cols].astype(F32), wide, signed).astype(BF16)
 
 
 def prep_kernel(
@@ -186,8 +183,10 @@
 
 def hop_kernel(step, wanted, started, *refs):
     count = len(wanted)
-    dqt_ins, dqt_refs, part_ref = refs[:count], refs[-count - 1 : -1], refs[-1]
-    k_ref, v_ref, qr_ref, do_ref, norm_ref, delta_ref, flag_ref = refs[count * started : -count - 1]
+    dqt_ins, dqt_refs, part_refs = refs[:count], refs[-2 * count : -count], refs[-count:]
+    k_ref, v_ref, qr_ref, do_ref, norm_ref, delta_ref, flag_ref = refs[
+        count * started : -2 * count
+    ]
     rows = qr_ref.shape[0]
     half = rows // 2
     heads = qr_ref.shape[1] // HEAD
@@ -198,7 +197,7 @@
     delta = delta_ref[...]
 
     def run(keys, queries):
-        for i, (g, dqt_in, dqt_ref) in enumerate(zip(wanted, dqt_ins, dqt_refs)):
+        for g, dqt_in, dqt_ref, part_ref in zip(wanted, dqt_ins, dqt_refs, part_refs):
             kc = pl.ds(g * HEAD, HEAD)
             dk = dv = None
             for j in range(size):
@@ -217,10 +216,10 @@
                 dqt_ref[to, queries] = dqt_in[to, queries] + q_part if started else q_part
                 dv = v_part if dv is None else dv + v_part
                 dk = k_part if dk is None else dk + k_part
-            part_ref[keys, pl.ds(2 * i * HEAD, HEAD)] = dk.astype(BF16)
-            part_ref[keys, pl.ds((2 * i + 1) * HEAD, HEAD)] = dv.astype(BF16)
-        if keys.stop < rows:
-            part_ref[keys.stop :, :] = jnp.zeros((rows - keys.stop, part_ref.shape[1]), BF16)
+            part_ref[keys, :HEAD] = dk.astype(BF16)
+            part_ref[keys, HEAD:] = dv.astype(BF16)
+            if keys.stop < rows:
+                part_ref[keys.stop :, :] = jnp.zeros((rows - keys.stop, 2 * HEAD), BF16)
 
     @pl.when(earlier)
     def _():
@@ -231,24 +230,8 @@
         run(slice(0, rows), slice(half, rows))
 
 
-def merged_kernel(step, wanted, started, *refs):
-    count = len(wanted) * started
-    kv_ref = refs[count]
-    width = kv_ref.shape[1] // 2
-    hop_kernel(
-        step, wanted, started, *refs[:count], kv_ref.at[:, :width], kv_ref.at[:, width:],
-        *refs[count + 1 :],
-    )
-
-
-def beside_kernel(k_ref, v_ref, kv_ref):
-    width = k_ref.shape[1]
-    kv_ref[:, :width] = k_ref[...]
-    kv_ref[:, width:] = v_ref[...]
-
-
 def own_kernel(groups, k_ref, v_ref, qr_ref, do_ref, norm_ref, delta_ref, *refs):
-    dqt_ins, dqt_refs, part_ref = refs[:groups], refs[groups : 2 * groups], refs[2 * groups]
+    dqt_ins, dqt_refs, part_refs = refs[:groups], refs[groups : 2 * groups], refs[2 * groups :]
     size = qr_ref.shape[1] // HEAD // groups
     norm = norm_ref[...]
     delta = delta_ref[...]
@@ -266,15 +249,19 @@
             dqt_refs[g][to, :] = dqt_ins[g][to, :] + q_part
             dv = v_part if dv is None else dv + v_part
             dk = k_part if dk is None else dk + k_part
-        part_ref[:, pl.ds(2 * g * HEAD, HEAD)] = dk
-        part_ref[:, pl.ds((2 * g + 1) * HEAD, HEAD)] = dv
+        part_refs[g][:, :HEAD] = dk
+        part_refs[g][:, HEAD:] = dv
 
 
 def query_kernel(groups, tables_ref, *refs):
-    dqt_refs = refs[:groups]
-    own_ref, swapped_ref, out_ref, sum_ref = refs[groups:]
+    dqt_refs, own_refs = refs[:groups], refs[groups : 2 * groups]
+    swapped_refs, out_ref = refs[2 * groups : 3 * groups], refs[3 * groups]
+    sum_refs = refs[3 * groups + 1 :]
     odd = (lax.axis_index("ctx") & 1) == 1
-    sum_ref[...] = own_ref[...] + jnp.where(odd, swapped_ref[...].astype(F32), 0.0)
+    for g in range(groups):
+        sum_refs[g][...] = own_refs[g][...] + jnp.where(
+            odd, swapped_refs[g][...].astype(F32), 0.0
+        )
     cosine_t = tables_ref[:HALF, :] * ROOT_SCALE
     sine_t = tables_ref[HALF:, :] * ROOT_SCALE
     size = dqt_refs[0].shape[0] // HEAD
@@ -288,21 +275,20 @@
             out_ref[:, pl.ds((g * size + j) * HEAD, HEAD)] = turned.T.astype(BF16)
 
 
-def add_kernel(g, two_ref, swapped_ref, three_ref, sum_ref):
+def add_kernel(two_ref, swapped_ref, three_ref, sum_ref):
     even = (lax.axis_index("ctx") & 1) == 0
-    cols = pl.ds(2 * g * HEAD, 2 * HEAD)
-    total = two_ref[:, cols].astype(F32) + three_ref[...].astype(F32)
-    sum_ref[...] = (total + jnp.where(even, swapped_ref[:, cols].astype(F32), 0.0)).astype(BF16)
-
-
-def final_kernel(groups, tables_ref, own_ref, *refs):
-    dk_ref, dv_ref = refs[groups:]
+    total = two_ref[...].astype(F32) + three_ref[...].astype(F32)
+    sum_ref[...] = (total + jnp.where(even, swapped_ref[...].astype(F32), 0.0)).astype(BF16)
+
+
+def final_kernel(groups, tables_ref, *refs):
+    own_refs, home_refs, (dk_ref, dv_ref) = refs[:groups], refs[groups : 2 * groups], refs[-2:]
     wide, signed = row_tables(tables_ref[:HALF, :], tables_ref[HALF:, :])
     wide = wide * ROOT_SCALE
     signed = signed * -ROOT_SCALE
     for g in range(groups):
         cols = pl.ds(g * HEAD, HEAD)
-        total = own_ref[:, pl.ds(2 * g * HEAD, 2 * HEAD)] + refs[g][...].astype(F32)
+        total = own_refs[g][...] + home_refs[g][...].astype(F32)
         dk_ref[:, cols] = rotated(total[:, :HEAD], wide, signed).astype(BF16)
         dv_ref[:, cols] = total[:, HEAD:].astype(BF16)
 
@@ -355,11 +341,9 @@
     every = tuple(range(groups))
 
     v1 = shifted(v, -1)
-    kr, kv, tables = call(
-        key_kernel,
-        [((rows, wide_k), BF16), ((rows, 2 * wide_k), BF16), ((HEAD, rows), F32)],
-        [VMEM] * 6,
-    )(*pieces, k_here, v_here)
+    kr, tables = call(
+        key_kernel, [((rows, wide_k), BF16), ((HEAD, rows), F32)], [VMEM] * 5
+    )(*pieces, k_here)
     k1 = shifted(kr, -1)
     shared = call(
         functools.partial(prep_kernel, groups),
@@ -373,58 +357,59 @@
         ],
         micros=2,
     )(span_map, tables, lse, q, do, at)
-    k1, _, v1 = lax.optimization_barrier((k1, shared[3], v1))
-    (kv1,) = call(beside_kernel, [((rows, 2 * wide_k), BF16)], [VMEM] * 2)(k1, v1)
-    kv3 = shifted(kv1, -2)
+    v1, _ = lax.optimization_barrier((v1, shared[3]))
+    v3 = shifted(v1, -2)
+    k3 = shifted(k1, -2)
     dqs = []
-
-    def hop(step, wanted, arrived):
+    dq_out = ((wide_q // groups, rows), F32)
+    part_out = ((rows, 2 * HEAD), BF16)
+
+    def hop(step, wanted, key, value):
         count = len(wanted)
         started = len(dqs) > 0
         before = [dqs[g] for g in wanted] if started else []
-        *new, part = call(
-            functools.partial(merged_kernel, step, wanted, started),
-            [((wide_q // groups, rows), F32)] * count + [((rows, 2 * HEAD * count), BF16)],
-            [VMEM] * (6 + len(before)),
+        results = call(
+            functools.partial(hop_kernel, step, wanted, started),
+            [dq_out] * count + [part_out] * count,
+            [VMEM] * (7 + len(before)),
             micros=count,
-        )(*before, arrived, *shared)
+        )(*before, key, value, *shared)
         if not started:
-            dqs.extend(new)
-        for g, dq in zip(wanted, new):
-            dqs[g] = dq
-        return part
-
-    part1 = hop(1, every, kv1)
-    swapped = exchanged(part1)
-    held, _ = lax.optimization_barrier((kv, part1))
-    kv2 = shifted(held, -2)
-    *dqs, own = call(
+            dqs.extend(results[:count])
+        for i, g in enumerate(wanted):
+            dqs[g] = results[i]
+        return results[count:]
+
+    parts1 = hop(1, every, k1, v1)
+    swapped = [exchanged(part) for part in parts1]
+    kr2, v_far, _ = lax.optimization_barrier((kr, v, parts1[0]))
+    k2 = shifted(kr2, -2)
+    v2 = shifted(v_far, -2)
+    moved = [shifted(*hop(3, (g,), k3, v3), 1) for g in every]
+    results = call(
         functools.partial(own_kernel, groups),
-        [((wide_q // groups, rows), F32)] * groups + [((rows, 2 * wide_k), F32)],
+        [dq_out] * groups + [((rows, 2 * HEAD), F32)] * groups,
         [VMEM] * (6 + groups),
         micros=3,
     )(kr, v_here, *shared[:4], *dqs)
-
-    moved = [shifted(hop(3, (g,), kv3), 1) for g in every]
-    part2 = hop(2, every, kv2)
-    dq, own = call(
+    dqs, owns = list(results[:groups]), results[groups:]
+    parts2 = hop(2, every, k2, v2)
+    dq, *owns = call(
         functools.partial(query_kernel, groups),
-        [((rows, wide_q), BF16), ((rows, 2 * wide_k), F32)],
-        [VMEM] * (3 + groups),
-    )(tables, *dqs, own, swapped)
-    part2, _ = lax.optimization_barrier((part2, own))
+        [((rows, wide_q), BF16)] + [((rows, 2 * HEAD), F32)] * groups,
+        [VMEM] * (1 + 3 * groups),
+    )(tables, *dqs, *owns, *swapped)
+    *parts2, _ = lax.optimization_barrier((*parts2, owns[0]))
     home = []
     for g in every:
-        (total,) = call(
-            functools.partial(add_kernel, g), [((rows, 2 * HEAD), BF16)], [VMEM] * 3
-        )(part2, swapped, moved[g])
+        (total,) = call(add_kernel, [part_out], [VMEM] * 3)(parts2[g], swapped[g], moved[g])
         home.append(shifted(total, 2))
 
     dk, dv = call(
         functools.partial(final_kernel, groups),
         [((rows, wide_k), BF16), ((rows, wide_k), BF16)],
-        [VMEM] * (2 + groups),
-    )(tables, own, *home)
+        [VMEM] * (1 + 2 * groups),
+    )(tables, *owns, *home)
     return dq, dk, dv
 
 

time: 48.5 us -> 46.3 us (0.955)
  starting transfers between devices: 24.5 us -> 23.3 us
  waiting for transfers between devices: 9.03 us -> 7.88 us
    ppermute x1 -> x2, starting transfers between devices: 3.85 us -> 2.16 us  [exchanged(): lax.ppermute(value, 'ctx', [(source, source ^ 1) for source in range(coun...]
    ppermute x11 -> x13, waiting for transfers between devices: 9.03 us -> 7.87 us  [shifted(): return lax.ppermute(value, axis, pairs)]
    ppermute x11 -> x13, starting transfers between devices: 20.7 us -> 21.1 us  [shifted(): return lax.ppermute(value, axis, pairs)]
    pallas_call x10 -> x9, Pallas kernels: 10.7 us -> 10.6 us  [the longest x4 5.11 us: hop(): call(functools.partial(hop_kernel, step, wanted, started), [dq_out] * cou...]
  transfers between devices with their start and end apart: 12 -> 15, of which waited for: 4 -> 4; matrix products, arithmetic and copies ran while one was open for 0% -> 0% of each run, Pallas kernels for 27% -> 28%
where the time goes in v17:
time: 46.3 us; the launch traced here: 45.8 us
  starting transfers between devices  23.3 us (50%)
  Pallas kernels  13.9 us (30%)
  waiting for transfers between devices  7.88 us (17%)
  between operations  0.73 us (2%)
    ppermute x13, starting transfers between devices, shifted(): return lax.ppermute(value, axis, pairs)  21.1 us
    ppermute x13, waiting for transfers between devices, shifted(): return lax.ppermute(value, axis, pairs)  7.87 us
    pallas_call x4, Pallas kernels, hop(): call(functools.partial(hop_kernel, step, wanted, started), [dq_out] * cou...  5.11 us
    pallas_call x1, Pallas kernels, shards(): call(functools.partial(own_kernel, groups), [dq_out] * groups + [((rows,...  3.04 us
    pallas_call x1, Pallas kernels, shards(): call(functools.partial(prep_kernel, groups), [((rows, wide_q), BF16)] * 2...  2.41 us
    ppermute x2, starting transfers between devices, exchanged(): lax.ppermute(value, 'ctx', [(source, source ^ 1) for source in range(coun...  2.16 us
    pallas_call x1, Pallas kernels, shards(): call(key_kernel, [((rows, wide_k), BF16), ((HEAD, rows), F32)], [VMEM] * 5)  1.24 us
    pallas_call x1, Pallas kernels, shards(): call(functools.partial(query_kernel, groups), [((rows, wide_q), BF16)] +...  1.1 us
  transfers between devices with their start and end apart: 15, of which 4 were waited for; matrix products, arithmetic and copies ran while one was open for 0% of the time, Pallas kernels for 28%

profile of v17, /device:TPU:0, one launch (start us, length us, event | category | flops | bytes accessed | tf_op | source)
XLA Modules:
  0.0 45.8 jit_solution(11604523030498898844)
XLA Ops:
  0.6 3.0 %collective-permute-start.1 = (s32[3,64]{1,0:T(4,128)}, s32[3,64]{1,0:T(4,128)S(1)}, u32[]{:S(2)}, u32[]{:S(2)}) collective-permute-start(s32[3,64]{1,0:T(4,128)} %own_ref.1), channel_id=1, source_target_pairs={{0,2},{1,3},{2,0},{3,1},{4,6},{5,7},{6,4},{7,5},{8,10},{9,11},{10,... | collective-permute-start | bytes 2312 | tf_op jit(solution)/shard_map/ppermute | solution.py:318
  3.6 0.0 collective-permute-start
  3.6 1.7 %collective-permute-start.2 = (s32[3,64]{1,0:T(4,128)}, s32[3,64]{1,0:T(4,128)S(1)}, u32[]{:S(2)}, u32[]{:S(2)}) collective-permute-start(s32[3,64]{1,0:T(4,128)} %own_ref.1), channel_id=1, source_target_pairs={{0,3},{1,0},{2,1},{3,2},{4,7},{5,4},{6,5},{7,6},{8,11},{9,8},{10,9... | collective-permute-start | bytes 2312 | tf_op jit(solution)/shard_map/ppermute | solution.py:318
  5.4 4.6 %collective-permute-start.4 = (bf16[256,256]{1,0:T(8,128)(2,1)}, bf16[256,256]{1,0:T(8,128)(2,1)S(1)}, u32[]{:S(2)}, u32[]{:S(2)}) collective-permute-start(bf16[256,256]{1,0:T(8,128)(2,1)} %v_ref.1), channel_id=1, source_target_pairs={{0,28},{4,0},{8,4},{12,8},{16,12},{20,16},{24,20},{28,24},{1,29},{... | collective-permute-start | bytes 393224 | tf_op jit(solution)/shard_map/ppermute | solution.py:318
  9.9 0.0 collective-permute-done.1.p2_ref
  9.9 0.0 collective-permute-done.p1_ref
  10.0 1.2 %shard_map.103 = (bf16[256,256]{1,0:T(8,128)(2,1)S(1)}, f32[128,256]{1,0:T(8,128)S(1)}) custom-call(s32[3,64]{1,0:T(4,128)} %own_ref.1, s32[3,64]{1,0:T(4,128)S(1)} %collective-permute-done.p1_ref, s32[3,64]{1,0:T(4,128)S(1)} %collective-permute-done.1.p2_ref, s32[3,64]{1,0:T(4,128)S(1)} %collective-permute-done.2.p3_ref, bf16[256,256]{1,0:T(8,128)(2,1)} %k_ref.1), custom_call_target="tpu_custom_call" | custom-call | flops 1048576 | bytes 3690000 | tf_op jit(solution)/shard_map/pallas_call | solution.py:344
  11.2 1.6 %collective-permute-start.3 = (bf16[256,256]{1,0:T(8,128)(2,1)S(1)}, bf16[256,256]{1,0:T(8,128)(2,1)S(1)}, u32[]{:S(2)}, u32[]{:S(2)}) collective-permute-start(bf16[256,256]{1,0:T(8,128)(2,1)S(1)} %get-tuple-element.51.k_ref), channel_id=1, source_target_pairs={{0,28},{4,0},{8,4},{12,8},{16,12},{20,16},{24,20},{28,24},{1,29},{... | collective-permute-start | bytes 393224 | tf_op jit(solution)/shard_map/ppermute | solution.py:318
  12.7 2.4 %shard_map.104 = (bf16[256,1024]{1,0:T(8,128)(2,1)S(1)}, bf16[256,1024]{1,0:T(8,128)(2,1)S(1)}, f32[8,256]{1,0:T(8,128)S(1)}, f32[8,256]{1,0:T(8,128)S(1)}, s32[8,128]{1,0:T(8,128)S(1)}) custom-call(s32[8]{0:T(128)} %span_ref.1, f32[128,256]{1,0:T(8,128)S(1)} %get-tuple-element.36.tables_ref, f32[8,256]{1,0:T(8,128)} %lse_hbm.1, bf16[256,1024]{1,0:T(8,128)(2,1)} %q_hbm.1, ...), custom_call_target="tpu_custom_call" | custom-call | flops 1048576 | bytes 7380000 | tf_op jit(solution)/shard_map/pallas_call | solution.py:348
  15.2 0.5 %collective-permute-start.6 = (bf16[256,256]{1,0:T(8,128)(2,1)S(1)}, bf16[256,256]{1,0:T(8,128)(2,1)S(1)}, u32[]{:S(2)}, u32[]{:S(2)}) collective-permute-start(bf16[256,256]{1,0:T(8,128)(2,1)S(1)} %collective-permute-done.4.refs_1_), channel_id=1, source_target_pairs={{0,24},{4,28},{8,0},{12,4},{16,8},{20,12},{24,16},{28,20},{1,25},{... | collective-permute-start | bytes 393224 | tf_op jit(solution)/shard_map/ppermute | solution.py:318
  15.7 0.7 %collective-permute-done.3.refs_0_ = bf16[256,256]{1,0:T(8,128)(2,1)S(1)} collective-permute-done((bf16[256,256]{1,0:T(8,128)(2,1)S(1)}, bf16[256,256]{1,0:T(8,128)(2,1)S(1)}, u32[]{:S(2)}, u32[]{:S(2)}) %collective-permute-start.3) | collective-permute-done | bytes 131104 | tf_op jit(solution)/shard_map/ppermute | solution.py:318
  16.4 1.4 %collective-permute-start.5 = (bf16[256,256]{1,0:T(8,128)(2,1)S(1)}, bf16[256,256]{1,0:T(8,128)(2,1)S(1)}, u32[]{:S(2)}, u32[]{:S(2)}) collective-permute-start(bf16[256,256]{1,0:T(8,128)(2,1)S(1)} %collective-permute-done.3.refs_0_), channel_id=1, source_target_pairs={{0,24},{4,28},{8,0},{12,4},{16,8},{20,12},{24,16},{28,20},{1,25},{... | collective-permute-start | bytes 393224 | tf_op jit(solution)/shard_map/ppermute | solution.py:318
  17.8 1.6 %shard_map.105 = (f32[512,256]{1,0:T(8,128)S(1)}, f32[512,256]{1,0:T(8,128)S(1)}, bf16[256,256]{1,0:T(8,128)(2,1)S(1)}, bf16[256,256]{1,0:T(8,128)(2,1)S(1)}) custom-call(bf16[256,256]{1,0:T(8,128)(2,1)S(1)} %collective-permute-done.3.refs_0_, bf16[256,256]{1,0:T(8,128)(2,1)S(1)} %collective-permute-done.4.refs_1_, ...), custom_call_target="tpu_custom_call" | custom-call | flops 1048576 | bytes 7380000 | tf_op jit(solution)/shard_map/pallas_call | solution.py:371
  19.4 0.5 %collective-permute-start.7 = (bf16[256,256]{1,0:T(8,128)(2,1)S(1)}, bf16[256,256]{1,0:T(8,128)(2,1)S(1)}, u32[]{:S(2)}, u32[]{:S(2)}) collective-permute-start(bf16[256,256]{1,0:T(8,128)(2,1)S(1)} %get-tuple-element.51.k_ref), channel_id=1, source_target_pairs={{0,24},{4,28},{8,0},{12,4},{16,8},{20,12},{24,16},{28,20},{1,25},{... | collective-permute-start | bytes 393224 | tf_op jit(solution)/shard_map/ppermute | solution.py:318
  19.9 1.9 %collective-permute-start.8 = (bf16[256,256]{1,0:T(8,128)(2,1)S(1)}, bf16[256,256]{1,0:T(8,128)(2,1)S(1)}, u32[]{:S(2)}, u32[]{:S(2)}) collective-permute-start(bf16[256,256]{1,0:T(8,128)(2,1)S(1)} %copy-done), channel_id=1, source_target_pairs={{0,24},{4,28},{8,0},{12,4},{16,8},{20,12},{24,16},{28,20},{1,25},{... | collective-permute-start | bytes 393224 | tf_op jit(solution)/shard_map/ppermute | solution.py:318
  21.9 2.1 %collective-permute-start.10 = (bf16[256,256]{1,0:T(8,128)(2,1)S(1)}, bf16[256,256]{1,0:T(8,128)(2,1)S(1)}, u32[]{:S(2)}, u32[]{:S(2)}) collective-permute-start(bf16[256,256]{1,0:T(8,128)(2,1)S(1)} %get-tuple-element.57), channel_id=1, source_target_pairs={{0,4},{4,0},{8,12},{12,8},{16,20},{20,16},{24,28},{28,24},{1,5},{5... | collective-permute-start | bytes 393224 | tf_op jit(solution)/shard_map/ppermute | solution.py:323
  24.0 0.1 collective-permute-start.9
  24.0 0.3 collective-permute-done.5.refs_1_
  24.4 0.9 %shard_map.106 = (f32[512,256]{1,0:T(8,128)S(1)}, bf16[256,256]{1,0:T(8,128)(2,1)S(1)}) custom-call(f32[512,256]{1,0:T(8,128)S(1)} %get-tuple-element.44.refs_0_, bf16[256,256]{1,0:T(8,128)(2,1)S(1)} %collective-permute-done.5.refs_1_, bf16[256,256]{1,0:T(8,128)(2,1)S(1)} %collective-permute-done.6.refs_2_, ...), custom_call_target="tpu_custom_call" | custom-call | flops 1048576 | bytes 3690000 | tf_op jit(solution)/shard_map/pallas_call | solution.py:371
  25.3 1.7 %collective-permute-start.11 = (bf16[256,256]{1,0:T(8,128)(2,1)S(1)}, bf16[256,256]{1,0:T(8,128)(2,1)S(1)}, u32[]{:S(2)}, u32[]{:S(2)}) collective-permute-start(bf16[256,256]{1,0:T(8,128)(2,1)S(1)} %get-tuple-element.64), channel_id=1, source_target_pairs={{0,4},{4,8},{8,12},{12,16},{16,20},{20,24},{24,28},{28,0},{1,5},{5... | collective-permute-start | bytes 393224 | tf_op jit(solution)/shard_map/ppermute | solution.py:318
  27.0 0.9 %shard_map.107 = (f32[512,256]{1,0:T(8,128)S(1)}, bf16[256,256]{1,0:T(8,128)(2,1)S(1)}) custom-call(f32[512,256]{1,0:T(8,128)S(1)} %get-tuple-element.46.refs_0_, bf16[256,256]{1,0:T(8,128)(2,1)S(1)} %collective-permute-done.5.refs_1_, bf16[256,256]{1,0:T(8,128)(2,1)S(1)} %collective-permute-done.6.refs_2_, ...), custom_call_target="tpu_custom_call" | custom-call | flops 1048576 | bytes 3690000 | tf_op jit(solution)/shard_map/pallas_call | solution.py:371
  27.9 2.2 %collective-permute-start.13 = (bf16[256,256]{1,0:T(8,128)(2,1)S(1)}, bf16[256,256]{1,0:T(8,128)(2,1)S(1)}, u32[]{:S(2)}, u32[]{:S(2)}) collective-permute-start(bf16[256,256]{1,0:T(8,128)(2,1)S(1)} %get-tuple-element.66), channel_id=1, source_target_pairs={{0,4},{4,8},{8,12},{12,16},{16,20},{20,24},{24,28},{28,0},{1,5},{5... | collective-permute-start | bytes 393224 | tf_op jit(solution)/shard_map/ppermute | solution.py:318
  30.1 3.0 %shard_map.108 = (f32[512,256]{1,0:T(8,128)S(1)}, f32[512,256]{1,0:T(8,128)S(1)}, f32[256,256]{1,0:T(8,128)S(1)}, f32[256,256]{1,0:T(8,128)S(1)}) custom-call(bf16[256,256]{1,0:T(8,128)(2,1)S(1)} %get-tuple-element.51.k_ref, bf16[256,256]{1,0:T(8,128)(2,1)} %v_ref.1, bf16[256,1024]{1,0:T(8,128)(2,1)S(1)} %get-tuple-element.38.refs_2_.refs_3_.qr_ref.refs_4_, ...), custom_call_target="tpu_custom_call" | custom-call | flops 1048576 | bytes 11070000 | tf_op jit(solution)/shard_map/pallas_call | solution.py:389
  33.1 1.6 %shard_map.109 = (f32[512,256]{1,0:T(8,128)S(1)}, f32[512,256]{1,0:T(8,128)S(1)}, bf16[256,256]{1,0:T(8,128)(2,1)S(1)}, bf16[256,256]{1,0:T(8,128)(2,1)S(1)}) custom-call(f32[512,256]{1,0:T(8,128)S(1)} %get-tuple-element.48.refs_0_, f32[512,256]{1,0:T(8,128)S(1)} %get-tuple-element.49.refs_1_, bf16[256,256]{1,0:T(8,128)(2,1)S(1)} %collective-permute-done.7.refs_2_, ...), custom_call_target="tpu_custom_call" | custom-call | flops 1048576 | bytes 7380000 | tf_op jit(solution)/shard_map/pallas_call | solution.py:371
  34.8 1.1 %shard_map.110 = (bf16[256,1024]{1,0:T(8,128)(2,1)}, f32[256,256]{1,0:T(8,128)S(1)}, f32[256,256]{1,0:T(8,128)S(1)}) custom-call(f32[128,256]{1,0:T(8,128)S(1)} %get-tuple-element.36.tables_ref, f32[512,256]{1,0:T(8,128)S(1)} %get-tuple-element.53.refs_0_, f32[512,256]{1,0:T(8,128)S(1)} %get-tuple-element.54.refs_1_, ...), custom_call_target="tpu_custom_call" | custom-call | flops 1048576 | bytes 3690000 | tf_op jit(solution)/shard_map/pallas_call | solution.py:397
  35.9 0.1 shard_map.111
  36.0 1.3 %collective-permute-start.12 = (bf16[256,256]{1,0:T(8,128)(2,1)S(1)}, bf16[256,256]{1,0:T(8,128)(2,1)S(1)}, u32[]{:S(2)}, u32[]{:S(2)}) collective-permute-start(bf16[256,256]{1,0:T(8,128)(2,1)S(1)} %shard_map.111), channel_id=1, source_target_pairs={{0,8},{4,12},{8,16},{12,20},{16,24},{20,28},{24,0},{28,4},{1,9},{5... | collective-permute-start | bytes 393224 | tf_op jit(solution)/shard_map/ppermute | solution.py:318
  37.3 0.1 shard_map.112
  37.3 0.7 %collective-permute-start.14 = (bf16[256,256]{1,0:T(8,128)(2,1)S(1)}, bf16[256,256]{1,0:T(8,128)(2,1)S(1)}, u32[]{:S(2)}, u32[]{:S(2)}) collective-permute-start(bf16[256,256]{1,0:T(8,128)(2,1)S(1)} %shard_map.112), channel_id=1, source_target_pairs={{0,8},{4,12},{8,16},{12,20},{16,24},{20,28},{24,0},{28,4},{1,9},{5... | collective-permute-start | bytes 393224 | tf_op jit(solution)/shard_map/ppermute | solution.py:318
  38.1 5.5 %collective-permute-done.12.refs_2_ = bf16[256,256]{1,0:T(8,128)(2,1)S(1)} collective-permute-done((bf16[256,256]{1,0:T(8,128)(2,1)S(1)}, bf16[256,256]{1,0:T(8,128)(2,1)S(1)}, u32[]{:S(2)}, u32[]{:S(2)}) %collective-permute-start.12) | collective-permute-done | bytes 131104 | tf_op jit(solution)/shard_map/ppermute | solution.py:318
  43.5 1.4 %collective-permute-done.14.refs_3_ = bf16[256,256]{1,0:T(8,128)(2,1)S(1)} collective-permute-done((bf16[256,256]{1,0:T(8,128)(2,1)S(1)}, bf16[256,256]{1,0:T(8,128)(2,1)S(1)}, u32[]{:S(2)}, u32[]{:S(2)}) %collective-permute-start.14) | collective-permute-done | bytes 131104 | tf_op jit(solution)/shard_map/ppermute | solution.py:318
  44.9 0.9 %shard_map.113 = (bf16[256,256]{1,0:T(8,128)(2,1)}, bf16[256,256]{1,0:T(8,128)(2,1)}) custom-call(f32[128,256]{1,0:T(8,128)S(1)} %get-tuple-element.36.tables_ref, f32[256,256]{1,0:T(8,128)S(1)} %get-tuple-element.59.refs_0_, f32[256,256]{1,0:T(8,128)S(1)} %get-tuple-element.60.refs_1_, bf16[256,256]{1,0:T(8,128)(2,1)S(1)} %collective-permute-done.12.refs_2_, ...), custom_call_target="tpu_custom_call" | custom-call | flops 1048576 | bytes 3690000 | tf_op jit(solution)/shard_map/pallas_call | solution.py:408
  (11 shorter events, 0.0 us)
Async XLA Ops:
  0.6 9.3 %collective-permute-start.1 = (s32[3,64]{1,0:T(4,128)}, s32[3,64]{1,0:T(4,128)S(1)}, u32[]{:S(2)}, u32[]{:S(2)}) collective-permute-start(s32[3,64]{1,0:T(4,128)} %own_ref.1), channel_id=1, source_target_pairs={{0,2},{1,3},{2,0},{3,1},{4,6},{5,7},{6,4},{7,5},{8,10},{9,11},{10,... | collective-permute-start | bytes 2312 | tf_op jit(solution)/shard_map/ppermute | solution.py:318
  3.6 6.3 %collective-permute-start = (s32[3,64]{1,0:T(4,128)}, s32[3,64]{1,0:T(4,128)S(1)}, u32[]{:S(2)}, u32[]{:S(2)}) collective-permute-start(s32[3,64]{1,0:T(4,128)} %own_ref.1), channel_id=1, source_target_pairs={{0,1},{1,2},{2,3},{3,0},{4,5},{5,6},{6,7},{7,4},{8,9},{9,10},{10,1... | collective-permute-start | bytes 2312 | tf_op jit(solution)/shard_map/ppermute | solution.py:318
  3.6 6.3 %collective-permute-start.2 = (s32[3,64]{1,0:T(4,128)}, s32[3,64]{1,0:T(4,128)S(1)}, u32[]{:S(2)}, u32[]{:S(2)}) collective-permute-start(s32[3,64]{1,0:T(4,128)} %own_ref.1), channel_id=1, source_target_pairs={{0,3},{1,0},{2,1},{3,2},{4,7},{5,4},{6,5},{7,6},{8,11},{9,8},{10,9... | collective-permute-start | bytes 2312 | tf_op jit(solution)/shard_map/ppermute | solution.py:318
  5.4 9.8 %collective-permute-start.4 = (bf16[256,256]{1,0:T(8,128)(2,1)}, bf16[256,256]{1,0:T(8,128)(2,1)S(1)}, u32[]{:S(2)}, u32[]{:S(2)}) collective-permute-start(bf16[256,256]{1,0:T(8,128)(2,1)} %v_ref.1), channel_id=1, source_target_pairs={{0,28},{4,0},{8,4},{12,8},{16,12},{20,16},{24,20},{28,24},{1,29},{... | collective-permute-start | bytes 393224 | tf_op jit(solution)/shard_map/ppermute | solution.py:318
  11.2 5.2 %collective-permute-start.3 = (bf16[256,256]{1,0:T(8,128)(2,1)S(1)}, bf16[256,256]{1,0:T(8,128)(2,1)S(1)}, u32[]{:S(2)}, u32[]{:S(2)}) collective-permute-start(bf16[256,256]{1,0:T(8,128)(2,1)S(1)} %get-tuple-element.51.k_ref), channel_id=1, source_target_pairs={{0,28},{4,0},{8,4},{12,8},{16,12},{20,16},{24,20},{28,24},{1,29},{... | collective-permute-start | bytes 393224 | tf_op jit(solution)/shard_map/ppermute | solution.py:318
  15.2 8.8 %collective-permute-start.6 = (bf16[256,256]{1,0:T(8,128)(2,1)S(1)}, bf16[256,256]{1,0:T(8,128)(2,1)S(1)}, u32[]{:S(2)}, u32[]{:S(2)}) collective-permute-start(bf16[256,256]{1,0:T(8,128)(2,1)S(1)} %collective-permute-done.4.refs_1_), channel_id=1, source_target_pairs={{0,24},{4,28},{8,0},{12,4},{16,8},{20,12},{24,16},{28,20},{1,25},{... | collective-permute-start | bytes 393224 | tf_op jit(solution)/shard_map/ppermute | solution.py:318
  16.4 8.0 %collective-permute-start.5 = (bf16[256,256]{1,0:T(8,128)(2,1)S(1)}, bf16[256,256]{1,0:T(8,128)(2,1)S(1)}, u32[]{:S(2)}, u32[]{:S(2)}) collective-permute-start(bf16[256,256]{1,0:T(8,128)(2,1)S(1)} %collective-permute-done.3.refs_0_), channel_id=1, source_target_pairs={{0,24},{4,28},{8,0},{12,4},{16,8},{20,12},{24,16},{28,20},{1,25},{... | collective-permute-start | bytes 393224 | tf_op jit(solution)/shard_map/ppermute | solution.py:318
  17.8 2.1 %copy-start = (bf16[256,256]{1,0:T(8,128)(2,1)S(1)}, bf16[256,256]{1,0:T(8,128)(2,1)}, u32[]{:S(2)}) copy-start(bf16[256,256]{1,0:T(8,128)(2,1)} %v_ref.1) | copy-start | bytes 393220
  19.4 8.5 %collective-permute-start.7 = (bf16[256,256]{1,0:T(8,128)(2,1)S(1)}, bf16[256,256]{1,0:T(8,128)(2,1)S(1)}, u32[]{:S(2)}, u32[]{:S(2)}) collective-permute-start(bf16[256,256]{1,0:T(8,128)(2,1)S(1)} %get-tuple-element.51.k_ref), channel_id=1, source_target_pairs={{0,24},{4,28},{8,0},{12,4},{16,8},{20,12},{24,16},{28,20},{1,25},{... | collective-permute-start | bytes 393224 | tf_op jit(solution)/shard_map/ppermute | solution.py:318
  19.9 13.2 %collective-permute-start.8 = (bf16[256,256]{1,0:T(8,128)(2,1)S(1)}, bf16[256,256]{1,0:T(8,128)(2,1)S(1)}, u32[]{:S(2)}, u32[]{:S(2)}) collective-permute-start(bf16[256,256]{1,0:T(8,128)(2,1)S(1)} %copy-done), channel_id=1, source_target_pairs={{0,24},{4,28},{8,0},{12,4},{16,8},{20,12},{24,16},{28,20},{1,25},{... | collective-permute-start | bytes 393224 | tf_op jit(solution)/shard_map/ppermute | solution.py:318
  21.9 12.9 %collective-permute-start.10 = (bf16[256,256]{1,0:T(8,128)(2,1)S(1)}, bf16[256,256]{1,0:T(8,128)(2,1)S(1)}, u32[]{:S(2)}, u32[]{:S(2)}) collective-permute-start(bf16[256,256]{1,0:T(8,128)(2,1)S(1)} %get-tuple-element.57), channel_id=1, source_target_pairs={{0,4},{4,0},{8,12},{12,8},{16,20},{20,16},{24,28},{28,24},{1,5},{5... | collective-permute-start | bytes 393224 | tf_op jit(solution)/shard_map/ppermute | solution.py:323
  24.0 10.8 %collective-permute-start.9 = (bf16[256,256]{1,0:T(8,128)(2,1)S(1)}, bf16[256,256]{1,0:T(8,128)(2,1)S(1)}, u32[]{:S(2)}, u32[]{:S(2)}) collective-permute-start(bf16[256,256]{1,0:T(8,128)(2,1)S(1)} %get-tuple-element.50), channel_id=1, source_target_pairs={{0,4},{4,0},{8,12},{12,8},{16,20},{20,16},{24,28},{28,24},{1,5},{5... | collective-permute-start | bytes 393224 | tf_op jit(solution)/shard_map/ppermute | solution.py:323
  25.3 10.6 %collective-permute-start.11 = (bf16[256,256]{1,0:T(8,128)(2,1)S(1)}, bf16[256,256]{1,0:T(8,128)(2,1)S(1)}, u32[]{:S(2)}, u32[]{:S(2)}) collective-permute-start(bf16[256,256]{1,0:T(8,128)(2,1)S(1)} %get-tuple-element.64), channel_id=1, source_target_pairs={{0,4},{4,8},{8,12},{12,16},{16,20},{20,24},{24,28},{28,0},{1,5},{5... | collective-permute-start | bytes 393224 | tf_op jit(solution)/shard_map/ppermute | solution.py:318
  27.9 9.4 %collective-permute-start.13 = (bf16[256,256]{1,0:T(8,128)(2,1)S(1)}, bf16[256,256]{1,0:T(8,128)(2,1)S(1)}, u32[]{:S(2)}, u32[]{:S(2)}) collective-permute-start(bf16[256,256]{1,0:T(8,128)(2,1)S(1)} %get-tuple-element.66), channel_id=1, source_target_pairs={{0,4},{4,8},{8,12},{12,16},{16,20},{20,24},{24,28},{28,0},{1,5},{5... | collective-permute-start | bytes 393224 | tf_op jit(solution)/shard_map/ppermute | solution.py:318
  36.0 7.5 %collective-permute-start.12 = (bf16[256,256]{1,0:T(8,128)(2,1)S(1)}, bf16[256,256]{1,0:T(8,128)(2,1)S(1)}, u32[]{:S(2)}, u32[]{:S(2)}) collective-permute-start(bf16[256,256]{1,0:T(8,128)(2,1)S(1)} %shard_map.111), channel_id=1, source_target_pairs={{0,8},{4,12},{8,16},{12,20},{16,24},{20,28},{24,0},{28,4},{1,9},{5... | collective-permute-start | bytes 393224 | tf_op jit(solution)/shard_map/ppermute | solution.py:318
  37.3 7.6 %collective-permute-start.14 = (bf16[256,256]{1,0:T(8,128)(2,1)S(1)}, bf16[256,256]{1,0:T(8,128)(2,1)S(1)}, u32[]{:S(2)}, u32[]{:S(2)}) collective-permute-start(bf16[256,256]{1,0:T(8,128)(2,1)S(1)} %shard_map.112), channel_id=1, source_target_pairs={{0,8},{4,12},{8,16},{12,20},{16,24},{20,28},{24,0},{28,4},{1,9},{5... | collective-permute-start | bytes 393224 | tf_op jit(solution)/shard_map/ppermute | solution.py:318

commit v18 on v17

--- a/solution.py
+++ b/solution.py
@@ -359,6 +359,8 @@
     )(span_map, tables, lse, q, do, at)
     v1, _ = lax.optimization_barrier((v1, shared[3]))
     v3 = shifted(v1, -2)
+    v_far, _ = lax.optimization_barrier((v, shared[3]))
+    v2 = shifted(v_far, -2)
     k3 = shifted(k1, -2)
     dqs = []
     dq_out = ((wide_q // groups, rows), F32)
@@ -382,10 +384,10 @@
 
     parts1 = hop(1, every, k1, v1)
     swapped = [exchanged(part) for part in parts1]
-    kr2, v_far, _ = lax.optimization_barrier((kr, v, parts1[0]))
+    kr2, _ = lax.optimization_barrier((kr, parts1[0]))
     k2 = shifted(kr2, -2)
-    v2 = shifted(v_far, -2)
     moved = [shifted(*hop(3, (g,), k3, v3), 1) for g in every]
+    parts2 = hop(2, every, k2, v2)
     results = call(
         functools.partial(own_kernel, groups),
         [dq_out] * groups + [((rows, 2 * HEAD), F32)] * groups,
@@ -393,13 +395,11 @@
         micros=3,
     )(kr, v_here, *shared[:4], *dqs)
     dqs, owns = list(results[:groups]), results[groups:]
-    parts2 = hop(2, every, k2, v2)
     dq, *owns = call(
         functools.partial(query_kernel, groups),
         [((rows, wide_q), BF16)] + [((rows, 2 * HEAD), F32)] * groups,
         [VMEM] * (1 + 3 * groups),
     )(tables, *dqs, *owns, *swapped)
-    *parts2, _ = lax.optimization_barrier((*parts2, owns[0]))
     home = []
     for g in every:
         (total,) = call(add_kernel, [part_out], [VMEM] * 3)(parts2[g], swapped[g], moved[g])

time: 46.3 us -> 45.3 us (0.978)
  waiting for transfers between devices: 7.88 us -> 5.62 us
  starting transfers between devices: 23.3 us -> 24.7 us
    ppermute x13, waiting for transfers between devices: 7.87 us -> 5.61 us  [shifted(): return lax.ppermute(value, axis, pairs)]
    ppermute x2, starting transfers between devices: 2.16 us -> 4.15 us  [exchanged(): lax.ppermute(value, 'ctx', [(source, source ^ 1) for source in range(coun...]
    ppermute x13, starting transfers between devices: 21.1 us -> 20.5 us  [shifted(): return lax.ppermute(value, axis, pairs)]
  transfers between devices with their start and end apart: 15 -> 15, of which waited for: 4 -> 5; matrix products, arithmetic and copies ran while one was open for 0% -> 0% of each run, Pallas kernels for 28% -> 29%
where the time goes in v18:
time: 45.3 us; the launch traced here: 45.1 us
  starting transfers between devices  24.7 us (55%)
  Pallas kernels  14.1 us (31%)
  waiting for transfers between devices  5.62 us (12%)
  between operations  0.72 us (2%)
    ppermute x13, starting transfers between devices, shifted(): return lax.ppermute(value, axis, pairs)  20.5 us
    ppermute x13, waiting for transfers between devices, shifted(): return lax.ppermute(value, axis, pairs)  5.61 us
    pallas_call x4, Pallas kernels, hop(): call(functools.partial(hop_kernel, step, wanted, started), [dq_out] * cou...  5.13 us
    ppermute x2, starting transfers between devices, exchanged(): lax.ppermute(value, 'ctx', [(source, source ^ 1) for source in range(coun...  4.15 us
    pallas_call x1, Pallas kernels, shards(): call(functools.partial(own_kernel, groups), [dq_out] * groups + [((rows,...  3.05 us
    pallas_call x1, Pallas kernels, shards(): call(functools.partial(prep_kernel, groups), [((rows, wide_q), BF16)] * 2...  2.55 us
    pallas_call x1, Pallas kernels, shards(): call(key_kernel, [((rows, wide_k), BF16), ((HEAD, rows), F32)], [VMEM] * 5)  1.24 us
    pallas_call x1, Pallas kernels, shards(): call(functools.partial(query_kernel, groups), [((rows, wide_q), BF16)] +...  1.1 us
  transfers between devices with their start and end apart: 15, of which 5 were waited for; matrix products, arithmetic and copies ran while one was open for 0% of the time, Pallas kernels for 29%

profile of v18, /device:TPU:0, one launch (start us, length us, event | category | flops | bytes accessed | tf_op | source)
XLA Modules:
  0.0 45.1 jit_solution(15975465707037878869)
XLA Ops:
  0.6 0.5 %collective-permute-start = (s32[3,64]{1,0:T(4,128)}, s32[3,64]{1,0:T(4,128)S(1)}, u32[]{:S(2)}, u32[]{:S(2)}) collective-permute-start(s32[3,64]{1,0:T(4,128)} %own_ref.1), channel_id=1, source_target_pairs={{0,1},{1,2},{2,3},{3,0},{4,5},{5,6},{6,7},{7,4},{8,9},{9,10},{10,1... | collective-permute-start | bytes 2312 | tf_op jit(solution)/shard_map/ppermute | solution.py:318
  1.1 2.6 %collective-permute-start.1 = (s32[3,64]{1,0:T(4,128)}, s32[3,64]{1,0:T(4,128)S(1)}, u32[]{:S(2)}, u32[]{:S(2)}) collective-permute-start(s32[3,64]{1,0:T(4,128)} %own_ref.1), channel_id=1, source_target_pairs={{0,2},{1,3},{2,0},{3,1},{4,6},{5,7},{6,4},{7,5},{8,10},{9,11},{10,... | collective-permute-start | bytes 2312 | tf_op jit(solution)/shard_map/ppermute | solution.py:318
  3.7 1.4 %collective-permute-start.2 = (s32[3,64]{1,0:T(4,128)}, s32[3,64]{1,0:T(4,128)S(1)}, u32[]{:S(2)}, u32[]{:S(2)}) collective-permute-start(s32[3,64]{1,0:T(4,128)} %own_ref.1), channel_id=1, source_target_pairs={{0,3},{1,0},{2,1},{3,2},{4,7},{5,4},{6,5},{7,6},{8,11},{9,8},{10,9... | collective-permute-start | bytes 2312 | tf_op jit(solution)/shard_map/ppermute | solution.py:318
  5.1 4.6 %collective-permute-start.4 = (bf16[256,256]{1,0:T(8,128)(2,1)}, bf16[256,256]{1,0:T(8,128)(2,1)S(1)}, u32[]{:S(2)}, u32[]{:S(2)}) collective-permute-start(bf16[256,256]{1,0:T(8,128)(2,1)} %v_ref.1), channel_id=1, source_target_pairs={{0,28},{4,0},{8,4},{12,8},{16,12},{20,16},{24,20},{28,24},{1,29},{... | collective-permute-start | bytes 393224 | tf_op jit(solution)/shard_map/ppermute | solution.py:318
  9.6 0.0 collective-permute-done.p1_ref
  9.6 0.0 collective-permute-done.1.p2_ref
  9.7 1.2 %shard_map.103 = (bf16[256,256]{1,0:T(8,128)(2,1)S(1)}, f32[128,256]{1,0:T(8,128)S(1)}) custom-call(s32[3,64]{1,0:T(4,128)} %own_ref.1, s32[3,64]{1,0:T(4,128)S(1)} %collective-permute-done.p1_ref, s32[3,64]{1,0:T(4,128)S(1)} %collective-permute-done.1.p2_ref, s32[3,64]{1,0:T(4,128)S(1)} %collective-permute-done.2.p3_ref, bf16[256,256]{1,0:T(8,128)(2,1)} %k_ref.1), custom_call_target="tpu_custom_call" | custom-call | flops 1048576 | bytes 3690000 | tf_op jit(solution)/shard_map/pallas_call | solution.py:344
  10.9 1.6 %collective-permute-start.3 = (bf16[256,256]{1,0:T(8,128)(2,1)S(1)}, bf16[256,256]{1,0:T(8,128)(2,1)S(1)}, u32[]{:S(2)}, u32[]{:S(2)}) collective-permute-start(bf16[256,256]{1,0:T(8,128)(2,1)S(1)} %get-tuple-element.47.k_ref), channel_id=1, source_target_pairs={{0,28},{4,0},{8,4},{12,8},{16,12},{20,16},{24,20},{28,24},{1,29},{... | collective-permute-start | bytes 393224 | tf_op jit(solution)/shard_map/ppermute | solution.py:318
  12.5 2.5 %shard_map.104 = (bf16[256,1024]{1,0:T(8,128)(2,1)S(1)}, bf16[256,1024]{1,0:T(8,128)(2,1)S(1)}, f32[8,256]{1,0:T(8,128)S(1)}, f32[8,256]{1,0:T(8,128)S(1)}, s32[8,128]{1,0:T(8,128)S(1)}) custom-call(s32[8]{0:T(128)} %span_ref.1, f32[128,256]{1,0:T(8,128)S(1)} %get-tuple-element.34.tables_ref, f32[8,256]{1,0:T(8,128)} %lse_hbm.1, bf16[256,1024]{1,0:T(8,128)(2,1)} %q_hbm.1, ...), custom_call_target="tpu_custom_call" | custom-call | flops 1048576 | bytes 7380000 | tf_op jit(solution)/shard_map/pallas_call | solution.py:348
  15.0 0.5 %collective-permute-start.6 = (bf16[256,256]{1,0:T(8,128)(2,1)S(1)}, bf16[256,256]{1,0:T(8,128)(2,1)S(1)}, u32[]{:S(2)}, u32[]{:S(2)}) collective-permute-start(bf16[256,256]{1,0:T(8,128)(2,1)S(1)} %collective-permute-done.4.refs_1_), channel_id=1, source_target_pairs={{0,24},{4,28},{8,0},{12,4},{16,8},{20,12},{24,16},{28,20},{1,25},{... | collective-permute-start | bytes 393224 | tf_op jit(solution)/shard_map/ppermute | solution.py:318
  15.5 0.5 %collective-permute-done.3.refs_0_ = bf16[256,256]{1,0:T(8,128)(2,1)S(1)} collective-permute-done((bf16[256,256]{1,0:T(8,128)(2,1)S(1)}, bf16[256,256]{1,0:T(8,128)(2,1)S(1)}, u32[]{:S(2)}, u32[]{:S(2)}) %collective-permute-start.3) | collective-permute-done | bytes 131104 | tf_op jit(solution)/shard_map/ppermute | solution.py:318
  16.0 1.5 %collective-permute-start.5 = (bf16[256,256]{1,0:T(8,128)(2,1)S(1)}, bf16[256,256]{1,0:T(8,128)(2,1)S(1)}, u32[]{:S(2)}, u32[]{:S(2)}) collective-permute-start(bf16[256,256]{1,0:T(8,128)(2,1)S(1)} %collective-permute-done.3.refs_0_), channel_id=1, source_target_pairs={{0,24},{4,28},{8,0},{12,4},{16,8},{20,12},{24,16},{28,20},{1,25},{... | collective-permute-start | bytes 393224 | tf_op jit(solution)/shard_map/ppermute | solution.py:318
  17.5 0.4 collective-permute-start.8
  18.0 1.6 %shard_map.105 = (f32[512,256]{1,0:T(8,128)S(1)}, f32[512,256]{1,0:T(8,128)S(1)}, bf16[256,256]{1,0:T(8,128)(2,1)S(1)}, bf16[256,256]{1,0:T(8,128)(2,1)S(1)}) custom-call(bf16[256,256]{1,0:T(8,128)(2,1)S(1)} %collective-permute-done.3.refs_0_, bf16[256,256]{1,0:T(8,128)(2,1)S(1)} %collective-permute-done.4.refs_1_, ...), custom_call_target="tpu_custom_call" | custom-call | flops 1048576 | bytes 7380000 | tf_op jit(solution)/shard_map/pallas_call | solution.py:373
  19.6 3.9 %collective-permute-start.9 = (bf16[256,256]{1,0:T(8,128)(2,1)S(1)}, bf16[256,256]{1,0:T(8,128)(2,1)S(1)}, u32[]{:S(2)}, u32[]{:S(2)}) collective-permute-start(bf16[256,256]{1,0:T(8,128)(2,1)S(1)} %get-tuple-element.46), channel_id=1, source_target_pairs={{0,4},{4,0},{8,12},{12,8},{16,20},{20,16},{24,28},{28,24},{1,5},{5... | collective-permute-start | bytes 393224 | tf_op jit(solution)/shard_map/ppermute | solution.py:323
  23.5 0.3 collective-permute-start.10
  23.8 0.4 collective-permute-done.5.refs_1_
  24.2 0.9 %shard_map.107 = (f32[512,256]{1,0:T(8,128)S(1)}, bf16[256,256]{1,0:T(8,128)(2,1)S(1)}) custom-call(f32[512,256]{1,0:T(8,128)S(1)} %get-tuple-element.44.refs_0_, bf16[256,256]{1,0:T(8,128)(2,1)S(1)} %collective-permute-done.5.refs_1_, bf16[256,256]{1,0:T(8,128)(2,1)S(1)} %collective-permute-done.6.refs_2_, ...), custom_call_target="tpu_custom_call" | custom-call | flops 1048576 | bytes 3690000 | tf_op jit(solution)/shard_map/pallas_call | solution.py:373
  25.1 1.5 %collective-permute-start.13 = (bf16[256,256]{1,0:T(8,128)(2,1)S(1)}, bf16[256,256]{1,0:T(8,128)(2,1)S(1)}, u32[]{:S(2)}, u32[]{:S(2)}) collective-permute-start(bf16[256,256]{1,0:T(8,128)(2,1)S(1)} %get-tuple-element.62), channel_id=1, source_target_pairs={{0,4},{4,8},{8,12},{12,16},{16,20},{20,24},{24,28},{28,0},{1,5},{5... | collective-permute-start | bytes 393224 | tf_op jit(solution)/shard_map/ppermute | solution.py:318
  26.6 0.9 %shard_map.106 = (f32[512,256]{1,0:T(8,128)S(1)}, bf16[256,256]{1,0:T(8,128)(2,1)S(1)}) custom-call(f32[512,256]{1,0:T(8,128)S(1)} %get-tuple-element.42.refs_0_, bf16[256,256]{1,0:T(8,128)(2,1)S(1)} %collective-permute-done.5.refs_1_, bf16[256,256]{1,0:T(8,128)(2,1)S(1)} %collective-permute-done.6.refs_2_, ...), custom_call_target="tpu_custom_call" | custom-call | flops 1048576 | bytes 3690000 | tf_op jit(solution)/shard_map/pallas_call | solution.py:373
  27.5 1.5 %collective-permute-start.11 = (bf16[256,256]{1,0:T(8,128)(2,1)S(1)}, bf16[256,256]{1,0:T(8,128)(2,1)S(1)}, u32[]{:S(2)}, u32[]{:S(2)}) collective-permute-start(bf16[256,256]{1,0:T(8,128)(2,1)S(1)} %get-tuple-element.60), channel_id=1, source_target_pairs={{0,4},{4,8},{8,12},{12,16},{16,20},{20,24},{24,28},{28,0},{1,5},{5... | collective-permute-start | bytes 393224 | tf_op jit(solution)/shard_map/ppermute | solution.py:318
  29.1 0.2 collective-permute-done.7.refs_2_
  29.2 1.6 %shard_map.108 = (f32[512,256]{1,0:T(8,128)S(1)}, f32[512,256]{1,0:T(8,128)S(1)}, bf16[256,256]{1,0:T(8,128)(2,1)S(1)}, bf16[256,256]{1,0:T(8,128)(2,1)S(1)}) custom-call(f32[512,256]{1,0:T(8,128)S(1)} %get-tuple-element.43.refs_0_, f32[512,256]{1,0:T(8,128)S(1)} %get-tuple-element.45.refs_1_, bf16[256,256]{1,0:T(8,128)(2,1)S(1)} %collective-permute-done.7.refs_2_, ...), custom_call_target="tpu_custom_call" | custom-call | flops 1048576 | bytes 7380000 | tf_op jit(solution)/shard_map/pallas_call | solution.py:373
  30.9 3.6 %collective-permute-done.13.three_ref = bf16[256,256]{1,0:T(8,128)(2,1)S(1)} collective-permute-done((bf16[256,256]{1,0:T(8,128)(2,1)S(1)}, bf16[256,256]{1,0:T(8,128)(2,1)S(1)}, u32[]{:S(2)}, u32[]{:S(2)}) %collective-permute-start.13) | collective-permute-done | bytes 131104 | tf_op jit(solution)/shard_map/ppermute | solution.py:318
  34.5 0.1 shard_map.112
  34.6 1.5 %collective-permute-start.14 = (bf16[256,256]{1,0:T(8,128)(2,1)S(1)}, bf16[256,256]{1,0:T(8,128)(2,1)S(1)}, u32[]{:S(2)}, u32[]{:S(2)}) collective-permute-start(bf16[256,256]{1,0:T(8,128)(2,1)S(1)} %shard_map.112), channel_id=1, source_target_pairs={{0,8},{4,12},{8,16},{12,20},{16,24},{20,28},{24,0},{28,4},{1,9},{5... | collective-permute-start | bytes 393224 | tf_op jit(solution)/shard_map/ppermute | solution.py:318
  36.1 0.1 shard_map.111
  36.2 2.9 %collective-permute-start.12 = (bf16[256,256]{1,0:T(8,128)(2,1)S(1)}, bf16[256,256]{1,0:T(8,128)(2,1)S(1)}, u32[]{:S(2)}, u32[]{:S(2)}) collective-permute-start(bf16[256,256]{1,0:T(8,128)(2,1)S(1)} %shard_map.111), channel_id=1, source_target_pairs={{0,8},{4,12},{8,16},{12,20},{16,24},{20,28},{24,0},{28,4},{1,9},{5... | collective-permute-start | bytes 393224 | tf_op jit(solution)/shard_map/ppermute | solution.py:318
  39.1 3.0 %shard_map.109 = (f32[512,256]{1,0:T(8,128)S(1)}, f32[512,256]{1,0:T(8,128)S(1)}, f32[256,256]{1,0:T(8,128)S(1)}, f32[256,256]{1,0:T(8,128)S(1)}) custom-call(bf16[256,256]{1,0:T(8,128)(2,1)S(1)} %get-tuple-element.47.k_ref, bf16[256,256]{1,0:T(8,128)(2,1)} %v_ref.1, bf16[256,1024]{1,0:T(8,128)(2,1)S(1)} %get-tuple-element.36.refs_2_.refs_3_.refs_4_.qr_ref, ...), custom_call_target="tpu_custom_call" | custom-call | flops 1048576 | bytes 11070000 | tf_op jit(solution)/shard_map/pallas_call | solution.py:391
  42.1 1.1 %shard_map.110 = (bf16[256,1024]{1,0:T(8,128)(2,1)}, f32[256,256]{1,0:T(8,128)S(1)}, f32[256,256]{1,0:T(8,128)S(1)}) custom-call(f32[128,256]{1,0:T(8,128)S(1)} %get-tuple-element.34.tables_ref, f32[512,256]{1,0:T(8,128)S(1)} %get-tuple-element.51.refs_0_, f32[512,256]{1,0:T(8,128)S(1)} %get-tuple-element.52.refs_1_, ...), custom_call_target="tpu_custom_call" | custom-call | flops 1048576 | bytes 3690000 | tf_op jit(solution)/shard_map/pallas_call | solution.py:398
  43.2 0.9 %collective-permute-done.12.refs_2_ = bf16[256,256]{1,0:T(8,128)(2,1)S(1)} collective-permute-done((bf16[256,256]{1,0:T(8,128)(2,1)S(1)}, bf16[256,256]{1,0:T(8,128)(2,1)S(1)}, u32[]{:S(2)}, u32[]{:S(2)}) %collective-permute-start.12) | collective-permute-done | bytes 131104 | tf_op jit(solution)/shard_map/ppermute | solution.py:318
  44.2 0.9 %shard_map.113 = (bf16[256,256]{1,0:T(8,128)(2,1)}, bf16[256,256]{1,0:T(8,128)(2,1)}) custom-call(f32[128,256]{1,0:T(8,128)S(1)} %get-tuple-element.34.tables_ref, f32[256,256]{1,0:T(8,128)S(1)} %get-tuple-element.57.refs_0_, f32[256,256]{1,0:T(8,128)S(1)} %get-tuple-element.58.refs_1_, bf16[256,256]{1,0:T(8,128)(2,1)S(1)} %collective-permute-done.12.refs_2_, ...), custom_call_target="tpu_custom_call" | custom-call | flops 1048576 | bytes 3690000 | tf_op jit(solution)/shard_map/pallas_call | solution.py:408
  (11 shorter events, 0.0 us)
Async XLA Ops:
  0.6 9.0 %collective-permute-start = (s32[3,64]{1,0:T(4,128)}, s32[3,64]{1,0:T(4,128)S(1)}, u32[]{:S(2)}, u32[]{:S(2)}) collective-permute-start(s32[3,64]{1,0:T(4,128)} %own_ref.1), channel_id=1, source_target_pairs={{0,1},{1,2},{2,3},{3,0},{4,5},{5,6},{6,7},{7,4},{8,9},{9,10},{10,1... | collective-permute-start | bytes 2312 | tf_op jit(solution)/shard_map/ppermute | solution.py:318
  1.1 8.5 %collective-permute-start.1 = (s32[3,64]{1,0:T(4,128)}, s32[3,64]{1,0:T(4,128)S(1)}, u32[]{:S(2)}, u32[]{:S(2)}) collective-permute-start(s32[3,64]{1,0:T(4,128)} %own_ref.1), channel_id=1, source_target_pairs={{0,2},{1,3},{2,0},{3,1},{4,6},{5,7},{6,4},{7,5},{8,10},{9,11},{10,... | collective-permute-start | bytes 2312 | tf_op jit(solution)/shard_map/ppermute | solution.py:318
  3.7 6.0 %collective-permute-start.2 = (s32[3,64]{1,0:T(4,128)}, s32[3,64]{1,0:T(4,128)S(1)}, u32[]{:S(2)}, u32[]{:S(2)}) collective-permute-start(s32[3,64]{1,0:T(4,128)} %own_ref.1), channel_id=1, source_target_pairs={{0,3},{1,0},{2,1},{3,2},{4,7},{5,4},{6,5},{7,6},{8,11},{9,8},{10,9... | collective-permute-start | bytes 2312 | tf_op jit(solution)/shard_map/ppermute | solution.py:318
  5.1 9.9 %collective-permute-start.4 = (bf16[256,256]{1,0:T(8,128)(2,1)}, bf16[256,256]{1,0:T(8,128)(2,1)S(1)}, u32[]{:S(2)}, u32[]{:S(2)}) collective-permute-start(bf16[256,256]{1,0:T(8,128)(2,1)} %v_ref.1), channel_id=1, source_target_pairs={{0,28},{4,0},{8,4},{12,8},{16,12},{20,16},{24,20},{28,24},{1,29},{... | collective-permute-start | bytes 393224 | tf_op jit(solution)/shard_map/ppermute | solution.py:318
  10.9 5.1 %collective-permute-start.3 = (bf16[256,256]{1,0:T(8,128)(2,1)S(1)}, bf16[256,256]{1,0:T(8,128)(2,1)S(1)}, u32[]{:S(2)}, u32[]{:S(2)}) collective-permute-start(bf16[256,256]{1,0:T(8,128)(2,1)S(1)} %get-tuple-element.47.k_ref), channel_id=1, source_target_pairs={{0,28},{4,0},{8,4},{12,8},{16,12},{20,16},{24,20},{28,24},{1,29},{... | collective-permute-start | bytes 393224 | tf_op jit(solution)/shard_map/ppermute | solution.py:318
  12.5 5.1 %copy-start = (bf16[256,256]{1,0:T(8,128)(2,1)S(1)}, bf16[256,256]{1,0:T(8,128)(2,1)}, u32[]{:S(2)}) copy-start(bf16[256,256]{1,0:T(8,128)(2,1)} %v_ref.1) | copy-start | bytes 393220
  15.0 8.5 %collective-permute-start.6 = (bf16[256,256]{1,0:T(8,128)(2,1)S(1)}, bf16[256,256]{1,0:T(8,128)(2,1)S(1)}, u32[]{:S(2)}, u32[]{:S(2)}) collective-permute-start(bf16[256,256]{1,0:T(8,128)(2,1)S(1)} %collective-permute-done.4.refs_1_), channel_id=1, source_target_pairs={{0,24},{4,28},{8,0},{12,4},{16,8},{20,12},{24,16},{28,20},{1,25},{... | collective-permute-start | bytes 393224 | tf_op jit(solution)/shard_map/ppermute | solution.py:318
  16.0 8.2 %collective-permute-start.5 = (bf16[256,256]{1,0:T(8,128)(2,1)S(1)}, bf16[256,256]{1,0:T(8,128)(2,1)S(1)}, u32[]{:S(2)}, u32[]{:S(2)}) collective-permute-start(bf16[256,256]{1,0:T(8,128)(2,1)S(1)} %collective-permute-done.3.refs_0_), channel_id=1, source_target_pairs={{0,24},{4,28},{8,0},{12,4},{16,8},{20,12},{24,16},{28,20},{1,25},{... | collective-permute-start | bytes 393224 | tf_op jit(solution)/shard_map/ppermute | solution.py:318
  17.5 10.0 %collective-permute-start.8 = (bf16[256,256]{1,0:T(8,128)(2,1)S(1)}, bf16[256,256]{1,0:T(8,128)(2,1)S(1)}, u32[]{:S(2)}, u32[]{:S(2)}) collective-permute-start(bf16[256,256]{1,0:T(8,128)(2,1)S(1)} %copy-done), channel_id=1, source_target_pairs={{0,24},{4,28},{8,0},{12,4},{16,8},{20,12},{24,16},{28,20},{1,25},{... | collective-permute-start | bytes 393224 | tf_op jit(solution)/shard_map/ppermute | solution.py:318
  19.6 16.5 %collective-permute-start.9 = (bf16[256,256]{1,0:T(8,128)(2,1)S(1)}, bf16[256,256]{1,0:T(8,128)(2,1)S(1)}, u32[]{:S(2)}, u32[]{:S(2)}) collective-permute-start(bf16[256,256]{1,0:T(8,128)(2,1)S(1)} %get-tuple-element.46), channel_id=1, source_target_pairs={{0,4},{4,0},{8,12},{12,8},{16,20},{20,16},{24,28},{28,24},{1,5},{5... | collective-permute-start | bytes 393224 | tf_op jit(solution)/shard_map/ppermute | solution.py:323
  23.5 5.8 %collective-permute-start.7 = (bf16[256,256]{1,0:T(8,128)(2,1)S(1)}, bf16[256,256]{1,0:T(8,128)(2,1)S(1)}, u32[]{:S(2)}, u32[]{:S(2)}) collective-permute-start(bf16[256,256]{1,0:T(8,128)(2,1)S(1)} %get-tuple-element.47.k_ref), channel_id=1, source_target_pairs={{0,24},{4,28},{8,0},{12,4},{16,8},{20,12},{24,16},{28,20},{1,25},{... | collective-permute-start | bytes 393224 | tf_op jit(solution)/shard_map/ppermute | solution.py:318
  23.5 7.4 %collective-permute-start.10 = (bf16[256,256]{1,0:T(8,128)(2,1)S(1)}, bf16[256,256]{1,0:T(8,128)(2,1)S(1)}, u32[]{:S(2)}, u32[]{:S(2)}) collective-permute-start(bf16[256,256]{1,0:T(8,128)(2,1)S(1)} %get-tuple-element.55), channel_id=1, source_target_pairs={{0,4},{4,0},{8,12},{12,8},{16,20},{20,16},{24,28},{28,24},{1,5},{5... | collective-permute-start | bytes 393224 | tf_op jit(solution)/shard_map/ppermute | solution.py:323
  25.1 9.4 %collective-permute-start.13 = (bf16[256,256]{1,0:T(8,128)(2,1)S(1)}, bf16[256,256]{1,0:T(8,128)(2,1)S(1)}, u32[]{:S(2)}, u32[]{:S(2)}) collective-permute-start(bf16[256,256]{1,0:T(8,128)(2,1)S(1)} %get-tuple-element.62), channel_id=1, source_target_pairs={{0,4},{4,8},{8,12},{12,16},{16,20},{20,24},{24,28},{28,0},{1,5},{5... | collective-permute-start | bytes 393224 | tf_op jit(solution)/shard_map/ppermute | solution.py:318
  27.5 8.6 %collective-permute-start.11 = (bf16[256,256]{1,0:T(8,128)(2,1)S(1)}, bf16[256,256]{1,0:T(8,128)(2,1)S(1)}, u32[]{:S(2)}, u32[]{:S(2)}) collective-permute-start(bf16[256,256]{1,0:T(8,128)(2,1)S(1)} %get-tuple-element.60), channel_id=1, source_target_pairs={{0,4},{4,8},{8,12},{12,16},{16,20},{20,24},{24,28},{28,0},{1,5},{5... | collective-permute-start | bytes 393224 | tf_op jit(solution)/shard_map/ppermute | solution.py:318
  34.6 8.7 %collective-permute-start.14 = (bf16[256,256]{1,0:T(8,128)(2,1)S(1)}, bf16[256,256]{1,0:T(8,128)(2,1)S(1)}, u32[]{:S(2)}, u32[]{:S(2)}) collective-permute-start(bf16[256,256]{1,0:T(8,128)(2,1)S(1)} %shard_map.112), channel_id=1, source_target_pairs={{0,8},{4,12},{8,16},{12,20},{16,24},{20,28},{24,0},{28,4},{1,9},{5... | collective-permute-start | bytes 393224 | tf_op jit(solution)/shard_map/ppermute | solution.py:318
  36.2 8.0 %collective-permute-start.12 = (bf16[256,256]{1,0:T(8,128)(2,1)S(1)}, bf16[256,256]{1,0:T(8,128)(2,1)S(1)}, u32[]{:S(2)}, u32[]{:S(2)}) collective-permute-start(bf16[256,256]{1,0:T(8,128)(2,1)S(1)} %shard_map.111), channel_id=1, source_target_pairs={{0,8},{4,12},{8,16},{12,20},{16,24},{20,28},{24,0},{28,4},{1,9},{5... | collective-permute-start | bytes 393224 | tf_op jit(solution)/shard_map/ppermute | solution.py:318

commit v19 on v18

--- a/solution.py
+++ b/solution.py
@@ -181,8 +181,11 @@
     norm_ref[...] = lse_ref[...] * LOG2E
 
 
-def hop_kernel(step, wanted, started, *refs):
+def hop_kernel(step, wanted, started, joined, *refs):
     count = len(wanted)
+    if joined:
+        *refs, part_ref = refs
+        refs += [part_ref.at[:, 2 * HEAD * i : 2 * HEAD * (i + 1)] for i in range(count)]
     dqt_ins, dqt_refs, part_refs = refs[:count], refs[-2 * count : -count], refs[-count:]
     k_ref, v_ref, qr_ref, do_ref, norm_ref, delta_ref, flag_ref = refs[
         count * started : -2 * count
@@ -255,12 +258,11 @@
 
 def query_kernel(groups, tables_ref, *refs):
     dqt_refs, own_refs = refs[:groups], refs[groups : 2 * groups]
-    swapped_refs, out_ref = refs[2 * groups : 3 * groups], refs[3 * groups]
-    sum_refs = refs[3 * groups + 1 :]
+    swapped_ref, out_ref, *sum_refs = refs[2 * groups :]
     odd = (lax.axis_index("ctx") & 1) == 1
     for g in range(groups):
         sum_refs[g][...] = own_refs[g][...] + jnp.where(
-            odd, swapped_refs[g][...].astype(F32), 0.0
+            odd, swapped_ref[:, 2 * HEAD * g : 2 * HEAD * (g + 1)].astype(F32), 0.0
         )
     cosine_t = tables_ref[:HALF, :] * ROOT_SCALE
     sine_t = tables_ref[HALF:, :] * ROOT_SCALE
@@ -275,10 +277,11 @@
             out_ref[:, pl.ds((g * size + j) * HEAD, HEAD)] = turned.T.astype(BF16)
 
 
-def add_kernel(two_ref, swapped_ref, three_ref, sum_ref):
+def add_kernel(g, two_ref, swapped_ref, three_ref, sum_ref):
     even = (lax.axis_index("ctx") & 1) == 0
     total = two_ref[...].astype(F32) + three_ref[...].astype(F32)
-    sum_ref[...] = (total + jnp.where(even, swapped_ref[...].astype(F32), 0.0)).astype(BF16)
+    swapped = swapped_ref[:, 2 * HEAD * g : 2 * HEAD * (g + 1)].astype(F32)
+    sum_ref[...] = (total + jnp.where(even, swapped, 0.0)).astype(BF16)
 
 
 def final_kernel(groups, tables_ref, *refs):
@@ -359,20 +362,18 @@
     )(span_map, tables, lse, q, do, at)
     v1, _ = lax.optimization_barrier((v1, shared[3]))
     v3 = shifted(v1, -2)
-    v_far, _ = lax.optimization_barrier((v, shared[3]))
-    v2 = shifted(v_far, -2)
-    k3 = shifted(k1, -2)
     dqs = []
     dq_out = ((wide_q // groups, rows), F32)
     part_out = ((rows, 2 * HEAD), BF16)
 
-    def hop(step, wanted, key, value):
+    def hop(step, wanted, key, value, joined=False):
         count = len(wanted)
         started = len(dqs) > 0
         before = [dqs[g] for g in wanted] if started else []
         results = call(
-            functools.partial(hop_kernel, step, wanted, started),
-            [dq_out] * count + [part_out] * count,
+            functools.partial(hop_kernel, step, wanted, started, joined),
+            [dq_out] * count
+            + ([((rows, 2 * HEAD * count), BF16)] if joined else [part_out] * count),
             [VMEM] * (7 + len(before)),
             micros=count,
         )(*before, key, value, *shared)
@@ -382,11 +383,14 @@
             dqs[g] = results[i]
         return results[count:]
 
-    parts1 = hop(1, every, k1, v1)
-    swapped = [exchanged(part) for part in parts1]
-    kr2, _ = lax.optimization_barrier((kr, parts1[0]))
+    (part1,) = hop(1, every, k1, v1, joined=True)
+    swapped = exchanged(part1)
+    held, kr2, v_far, _ = lax.optimization_barrier((k1, kr, v, part1))
+    k3 = shifted(held, -2)
     k2 = shifted(kr2, -2)
+    v2 = shifted(v_far, -2)
     moved = [shifted(*hop(3, (g,), k3, v3), 1) for g in every]
+    k2, swapped = lax.optimization_barrier((k2, swapped))
     parts2 = hop(2, every, k2, v2)
     results = call(
         functools.partial(own_kernel, groups),
@@ -398,11 +402,13 @@
     dq, *owns = call(
         functools.partial(query_kernel, groups),
         [((rows, wide_q), BF16)] + [((rows, 2 * HEAD), F32)] * groups,
-        [VMEM] * (1 + 3 * groups),
-    )(tables, *dqs, *owns, *swapped)
+        [VMEM] * (2 + 2 * groups),
+    )(tables, *dqs, *owns, swapped)
     home = []
     for g in every:
-        (total,) = call(add_kernel, [part_out], [VMEM] * 3)(parts2[g], swapped[g], moved[g])
+        (total,) = call(functools.partial(add_kernel, g), [part_out], [VMEM] * 3)(
+            parts2[g], swapped, moved[g]
+        )
         home.append(shifted(total, 2))
 
     dk, dv = call(

time: 45.3 us -> 47.5 us (1.049)
  waiting for transfers between devices: 5.62 us -> 10.7 us
  starting transfers between devices: 24.7 us -> 22 us
    ppermute x13, waiting for transfers between devices: 5.61 us -> 10.7 us  [shifted(): return lax.ppermute(value, axis, pairs)]
    ppermute x2 -> x1, starting transfers between devices: 4.15 us -> 2.08 us  [exchanged(): lax.ppermute(value, 'ctx', [(source, source ^ 1) for source in range(coun...]
    ppermute x13, starting transfers between devices: 20.5 us -> 19.9 us  [shifted(): return lax.ppermute(value, axis, pairs)]
  transfers between devices with their start and end apart: 15 -> 14, of which waited for: 5 -> 6; matrix products, arithmetic and copies ran while one was open for 0% -> 0% of each run, Pallas kernels for 29% -> 28%
where the time goes in v19:
time: 47.5 us; the launch traced here: 47.3 us
  starting transfers between devices  22 us (46%)
  Pallas kernels  13.9 us (29%)
  waiting for transfers between devices  10.7 us (23%)
  between operations  0.71 us (1%)
    ppermute x13, starting transfers between devices, shifted(): return lax.ppermute(value, axis, pairs)  19.9 us
    ppermute x13, waiting for transfers between devices, shifted(): return lax.ppermute(value, axis, pairs)  10.7 us
    pallas_call x4, Pallas kernels, hop(): call(functools.partial(hop_kernel, step, wanted, started, joined), [dq_ou...  5.12 us
    pallas_call x1, Pallas kernels, shards(): call(functools.partial(own_kernel, groups), [dq_out] * groups + [((rows,...  3.05 us
    pallas_call x1, Pallas kernels, shards(): call(functools.partial(prep_kernel, groups), [((rows, wide_q), BF16)] * 2...  2.41 us
    ppermute x1, starting transfers between devices, exchanged(): lax.ppermute(value, 'ctx', [(source, source ^ 1) for source in range(coun...  2.08 us
    pallas_call x1, Pallas kernels, shards(): call(key_kernel, [((rows, wide_k), BF16), ((HEAD, rows), F32)], [VMEM] * 5)  1.24 us
    pallas_call x1, Pallas kernels, shards(): call(functools.partial(query_kernel, groups), [((rows, wide_q), BF16)] +...  1.1 us
  transfers between devices with their start and end apart: 14, of which 6 were waited for; matrix products, arithmetic and copies ran while one was open for 0% of the time, Pallas kernels for 28%

profile of v19, /device:TPU:0, one launch (start us, length us, event | category | flops | bytes accessed | tf_op | source)
XLA Modules:
  0.0 47.3 jit_solution(2760789613741467933)
XLA Ops:
  0.6 3.0 %collective-permute-start.1 = (s32[3,64]{1,0:T(4,128)}, s32[3,64]{1,0:T(4,128)S(1)}, u32[]{:S(2)}, u32[]{:S(2)}) collective-permute-start(s32[3,64]{1,0:T(4,128)} %own_ref.1), channel_id=1, source_target_pairs={{0,2},{1,3},{2,0},{3,1},{4,6},{5,7},{6,4},{7,5},{8,10},{9,11},{10,... | collective-permute-start | bytes 2312 | tf_op jit(solution)/shard_map/ppermute | solution.py:321
  3.6 0.0 collective-permute-start
  3.6 1.7 %collective-permute-start.2 = (s32[3,64]{1,0:T(4,128)}, s32[3,64]{1,0:T(4,128)S(1)}, u32[]{:S(2)}, u32[]{:S(2)}) collective-permute-start(s32[3,64]{1,0:T(4,128)} %own_ref.1), channel_id=1, source_target_pairs={{0,3},{1,0},{2,1},{3,2},{4,7},{5,4},{6,5},{7,6},{8,11},{9,8},{10,9... | collective-permute-start | bytes 2312 | tf_op jit(solution)/shard_map/ppermute | solution.py:321
  5.4 4.6 %collective-permute-start.4 = (bf16[256,256]{1,0:T(8,128)(2,1)}, bf16[256,256]{1,0:T(8,128)(2,1)S(1)}, u32[]{:S(2)}, u32[]{:S(2)}) collective-permute-start(bf16[256,256]{1,0:T(8,128)(2,1)} %v_ref.1), channel_id=1, source_target_pairs={{0,28},{4,0},{8,4},{12,8},{16,12},{20,16},{24,20},{28,24},{1,29},{... | collective-permute-start | bytes 393224 | tf_op jit(solution)/shard_map/ppermute | solution.py:321
  10.0 1.2 %shard_map.103 = (bf16[256,256]{1,0:T(8,128)(2,1)S(1)}, f32[128,256]{1,0:T(8,128)S(1)}) custom-call(s32[3,64]{1,0:T(4,128)} %own_ref.1, s32[3,64]{1,0:T(4,128)S(1)} %collective-permute-done.p1_ref, s32[3,64]{1,0:T(4,128)S(1)} %collective-permute-done.1.p2_ref, s32[3,64]{1,0:T(4,128)S(1)} %collective-permute-done.2.p3_ref, bf16[256,256]{1,0:T(8,128)(2,1)} %k_ref.1), custom_call_target="tpu_custom_call" | custom-call | flops 1048576 | bytes 3690000 | tf_op jit(solution)/shard_map/pallas_call | solution.py:347
  11.2 1.6 %collective-permute-start.3 = (bf16[256,256]{1,0:T(8,128)(2,1)S(1)}, bf16[256,256]{1,0:T(8,128)(2,1)S(1)}, u32[]{:S(2)}, u32[]{:S(2)}) collective-permute-start(bf16[256,256]{1,0:T(8,128)(2,1)S(1)} %get-tuple-element.50.k_ref), channel_id=1, source_target_pairs={{0,28},{4,0},{8,4},{12,8},{16,12},{20,16},{24,20},{28,24},{1,29},{... | collective-permute-start | bytes 393224 | tf_op jit(solution)/shard_map/ppermute | solution.py:321
  12.7 2.4 %shard_map.104 = (bf16[256,1024]{1,0:T(8,128)(2,1)S(1)}, bf16[256,1024]{1,0:T(8,128)(2,1)S(1)}, f32[8,256]{1,0:T(8,128)S(1)}, f32[8,256]{1,0:T(8,128)S(1)}, s32[8,128]{1,0:T(8,128)S(1)}) custom-call(s32[8]{0:T(128)} %span_ref.1, f32[128,256]{1,0:T(8,128)S(1)} %get-tuple-element.36.tables_ref, f32[8,256]{1,0:T(8,128)} %lse_hbm.1, bf16[256,1024]{1,0:T(8,128)(2,1)} %q_hbm.1, ...), custom_call_target="tpu_custom_call" | custom-call | flops 1048576 | bytes 7380000 | tf_op jit(solution)/shard_map/pallas_call | solution.py:351
  15.2 0.5 %collective-permute-start.6 = (bf16[256,256]{1,0:T(8,128)(2,1)S(1)}, bf16[256,256]{1,0:T(8,128)(2,1)S(1)}, u32[]{:S(2)}, u32[]{:S(2)}) collective-permute-start(bf16[256,256]{1,0:T(8,128)(2,1)S(1)} %collective-permute-done.4.refs_1_), channel_id=1, source_target_pairs={{0,24},{4,28},{8,0},{12,4},{16,8},{20,12},{24,16},{28,20},{1,25},{... | collective-permute-start | bytes 393224 | tf_op jit(solution)/shard_map/ppermute | solution.py:321
  15.7 0.7 %collective-permute-done.3.refs_0_ = bf16[256,256]{1,0:T(8,128)(2,1)S(1)} collective-permute-done((bf16[256,256]{1,0:T(8,128)(2,1)S(1)}, bf16[256,256]{1,0:T(8,128)(2,1)S(1)}, u32[]{:S(2)}, u32[]{:S(2)}) %collective-permute-start.3) | collective-permute-done | bytes 131104 | tf_op jit(solution)/shard_map/ppermute | solution.py:321
  16.4 1.6 %shard_map.105 = (f32[512,256]{1,0:T(8,128)S(1)}, f32[512,256]{1,0:T(8,128)S(1)}, bf16[256,512]{1,0:T(8,128)(2,1)S(1)}) custom-call(bf16[256,256]{1,0:T(8,128)(2,1)S(1)} %collective-permute-done.3.refs_0_, bf16[256,256]{1,0:T(8,128)(2,1)S(1)} %collective-permute-done.4.refs_1_, bf16[256,1024]{1,0:T(8,128)(2,1)S(1)} %get-tuple-element.38.refs_2_.refs_3_.refs_4_.qr_ref, ...), custom_call_target="tpu_custom_call" | custom-call | flops 1048576 | bytes 7380000 | tf_op jit(solution)/shard_map/pallas_call | solution.py:373
  18.0 2.1 %collective-permute-start.8 = (bf16[256,512]{1,0:T(8,128)(2,1)S(1)}, bf16[256,512]{1,0:T(8,128)(2,1)S(1)}, u32[]{:S(2)}, u32[]{:S(2)}) collective-permute-start(bf16[256,512]{1,0:T(8,128)(2,1)S(1)} %get-tuple-element.45), channel_id=1, source_target_pairs={{0,4},{4,0},{8,12},{12,8},{16,20},{20,16},{24,28},{28,24},{1,5},{5... | collective-permute-start | bytes 786440 | tf_op jit(solution)/shard_map/ppermute | solution.py:326
  20.1 3.7 %collective-permute-start.5 = (bf16[256,256]{1,0:T(8,128)(2,1)S(1)}, bf16[256,256]{1,0:T(8,128)(2,1)S(1)}, u32[]{:S(2)}, u32[]{:S(2)}) collective-permute-start(bf16[256,256]{1,0:T(8,128)(2,1)S(1)} %collective-permute-done.3.refs_0_), channel_id=1, source_target_pairs={{0,24},{4,28},{8,0},{12,4},{16,8},{20,12},{24,16},{28,20},{1,25},{... | collective-permute-start | bytes 393224 | tf_op jit(solution)/shard_map/ppermute | solution.py:321
  23.8 0.0 collective-permute-start.7
  23.9 0.0 collective-permute-start.9
  23.9 0.0 collective-permute-done.6.refs_2_
  23.9 3.9 %collective-permute-done.5.refs_1_ = bf16[256,256]{1,0:T(8,128)(2,1)S(1)} collective-permute-done((bf16[256,256]{1,0:T(8,128)(2,1)S(1)}, bf16[256,256]{1,0:T(8,128)(2,1)S(1)}, u32[]{:S(2)}, u32[]{:S(2)}) %collective-permute-start.5) | collective-permute-done | bytes 131104 | tf_op jit(solution)/shard_map/ppermute | solution.py:321
  27.8 0.9 %shard_map.106 = (f32[512,256]{1,0:T(8,128)S(1)}, bf16[256,256]{1,0:T(8,128)(2,1)S(1)}) custom-call(f32[512,256]{1,0:T(8,128)S(1)} %get-tuple-element.44.refs_0_, bf16[256,256]{1,0:T(8,128)(2,1)S(1)} %collective-permute-done.5.refs_1_, bf16[256,256]{1,0:T(8,128)(2,1)S(1)} %collective-permute-done.6.refs_2_, ...), custom_call_target="tpu_custom_call" | custom-call | flops 1048576 | bytes 3690000 | tf_op jit(solution)/shard_map/pallas_call | solution.py:373
  28.7 0.1 collective-permute-start.10
  28.8 0.9 %shard_map.107 = (f32[512,256]{1,0:T(8,128)S(1)}, bf16[256,256]{1,0:T(8,128)(2,1)S(1)}) custom-call(f32[512,256]{1,0:T(8,128)S(1)} %get-tuple-element.48.refs_0_, bf16[256,256]{1,0:T(8,128)(2,1)S(1)} %collective-permute-done.5.refs_1_, bf16[256,256]{1,0:T(8,128)(2,1)S(1)} %collective-permute-done.6.refs_2_, ...), custom_call_target="tpu_custom_call" | custom-call | flops 1048576 | bytes 3690000 | tf_op jit(solution)/shard_map/pallas_call | solution.py:373
  29.7 0.1 collective-permute-start.12
  29.8 0.6 %collective-permute-done.7.refs_2_ = bf16[256,256]{1,0:T(8,128)(2,1)S(1)} collective-permute-done((bf16[256,256]{1,0:T(8,128)(2,1)S(1)}, bf16[256,256]{1,0:T(8,128)(2,1)S(1)}, u32[]{:S(2)}, u32[]{:S(2)}) %collective-permute-start.7) | collective-permute-done | bytes 131104 | tf_op jit(solution)/shard_map/ppermute | solution.py:321
  30.4 1.4 %collective-permute-done.9.refs_3_ = bf16[256,256]{1,0:T(8,128)(2,1)S(1)} collective-permute-done((bf16[256,256]{1,0:T(8,128)(2,1)S(1)}, bf16[256,256]{1,0:T(8,128)(2,1)S(1)}, u32[]{:S(2)}, u32[]{:S(2)}) %collective-permute-start.9) | collective-permute-done | bytes 131104 | tf_op jit(solution)/shard_map/ppermute | solution.py:321
  31.8 1.6 %shard_map.108 = (f32[512,256]{1,0:T(8,128)S(1)}, f32[512,256]{1,0:T(8,128)S(1)}, bf16[256,256]{1,0:T(8,128)(2,1)S(1)}, bf16[256,256]{1,0:T(8,128)(2,1)S(1)}) custom-call(f32[512,256]{1,0:T(8,128)S(1)} %get-tuple-element.47.refs_0_, f32[512,256]{1,0:T(8,128)S(1)} %get-tuple-element.49.refs_1_, bf16[256,256]{1,0:T(8,128)(2,1)S(1)} %collective-permute-done.7.refs_2_, ...), custom_call_target="tpu_custom_call" | custom-call | flops 1048576 | bytes 7380000 | tf_op jit(solution)/shard_map/pallas_call | solution.py:373
  33.5 3.1 %collective-permute-done.10.three_ref = bf16[256,256]{1,0:T(8,128)(2,1)S(1)} collective-permute-done((bf16[256,256]{1,0:T(8,128)(2,1)S(1)}, bf16[256,256]{1,0:T(8,128)(2,1)S(1)}, u32[]{:S(2)}, u32[]{:S(2)}) %collective-permute-start.10) | collective-permute-done | bytes 131104 | tf_op jit(solution)/shard_map/ppermute | solution.py:321
  36.6 0.1 shard_map.111
  36.6 1.7 %collective-permute-start.11 = (bf16[256,256]{1,0:T(8,128)(2,1)S(1)}, bf16[256,256]{1,0:T(8,128)(2,1)S(1)}, u32[]{:S(2)}, u32[]{:S(2)}) collective-permute-start(bf16[256,256]{1,0:T(8,128)(2,1)S(1)} %shard_map.111), channel_id=1, source_target_pairs={{0,8},{4,12},{8,16},{12,20},{16,24},{20,28},{24,0},{28,4},{1,9},{5... | collective-permute-start | bytes 393224 | tf_op jit(solution)/shard_map/ppermute | solution.py:321
  38.3 0.1 shard_map.112
  38.4 2.9 %collective-permute-start.13 = (bf16[256,256]{1,0:T(8,128)(2,1)S(1)}, bf16[256,256]{1,0:T(8,128)(2,1)S(1)}, u32[]{:S(2)}, u32[]{:S(2)}) collective-permute-start(bf16[256,256]{1,0:T(8,128)(2,1)S(1)} %shard_map.112), channel_id=1, source_target_pairs={{0,8},{4,12},{8,16},{12,20},{16,24},{20,28},{24,0},{28,4},{1,9},{5... | collective-permute-start | bytes 393224 | tf_op jit(solution)/shard_map/ppermute | solution.py:321
  41.3 3.0 %shard_map.109 = (f32[512,256]{1,0:T(8,128)S(1)}, f32[512,256]{1,0:T(8,128)S(1)}, f32[256,256]{1,0:T(8,128)S(1)}, f32[256,256]{1,0:T(8,128)S(1)}) custom-call(bf16[256,256]{1,0:T(8,128)(2,1)S(1)} %get-tuple-element.50.k_ref, bf16[256,256]{1,0:T(8,128)(2,1)} %v_ref.1, bf16[256,1024]{1,0:T(8,128)(2,1)S(1)} %get-tuple-element.38.refs_2_.refs_3_.refs_4_.qr_ref, ...), custom_call_target="tpu_custom_call" | custom-call | flops 1048576 | bytes 11070000 | tf_op jit(solution)/shard_map/pallas_call | solution.py:395
  44.4 1.1 %shard_map.110 = (bf16[256,1024]{1,0:T(8,128)(2,1)}, f32[256,256]{1,0:T(8,128)S(1)}, f32[256,256]{1,0:T(8,128)S(1)}) custom-call(f32[128,256]{1,0:T(8,128)S(1)} %get-tuple-element.36.tables_ref, f32[512,256]{1,0:T(8,128)S(1)} %get-tuple-element.55.refs_0_, f32[512,256]{1,0:T(8,128)S(1)} %get-tuple-element.56.refs_1_, ...), custom_call_target="tpu_custom_call" | custom-call | flops 1048576 | bytes 3690000 | tf_op jit(solution)/shard_map/pallas_call | solution.py:402
  45.5 1.0 %collective-permute-done.13.refs_3_ = bf16[256,256]{1,0:T(8,128)(2,1)S(1)} collective-permute-done((bf16[256,256]{1,0:T(8,128)(2,1)S(1)}, bf16[256,256]{1,0:T(8,128)(2,1)S(1)}, u32[]{:S(2)}, u32[]{:S(2)}) %collective-permute-start.13) | collective-permute-done | bytes 131104 | tf_op jit(solution)/shard_map/ppermute | solution.py:321
  46.4 0.9 %shard_map.113 = (bf16[256,256]{1,0:T(8,128)(2,1)}, bf16[256,256]{1,0:T(8,128)(2,1)}) custom-call(f32[128,256]{1,0:T(8,128)S(1)} %get-tuple-element.36.tables_ref, f32[256,256]{1,0:T(8,128)S(1)} %get-tuple-element.61.refs_0_, f32[256,256]{1,0:T(8,128)S(1)} %get-tuple-element.62.refs_1_, bf16[256,256]{1,0:T(8,128)(2,1)S(1)} %collective-permute-done.11.refs_2_, ...), custom_call_target="tpu_custom_call" | custom-call | flops 1048576 | bytes 3690000 | tf_op jit(solution)/shard_map/pallas_call | solution.py:414
  (9 shorter events, 0.0 us)
Async XLA Ops:
  0.6 9.3 %collective-permute-start.1 = (s32[3,64]{1,0:T(4,128)}, s32[3,64]{1,0:T(4,128)S(1)}, u32[]{:S(2)}, u32[]{:S(2)}) collective-permute-start(s32[3,64]{1,0:T(4,128)} %own_ref.1), channel_id=1, source_target_pairs={{0,2},{1,3},{2,0},{3,1},{4,6},{5,7},{6,4},{7,5},{8,10},{9,11},{10,... | collective-permute-start | bytes 2312 | tf_op jit(solution)/shard_map/ppermute | solution.py:321
  3.6 6.3 %collective-permute-start = (s32[3,64]{1,0:T(4,128)}, s32[3,64]{1,0:T(4,128)S(1)}, u32[]{:S(2)}, u32[]{:S(2)}) collective-permute-start(s32[3,64]{1,0:T(4,128)} %own_ref.1), channel_id=1, source_target_pairs={{0,1},{1,2},{2,3},{3,0},{4,5},{5,6},{6,7},{7,4},{8,9},{9,10},{10,1... | collective-permute-start | bytes 2312 | tf_op jit(solution)/shard_map/ppermute | solution.py:321
  3.6 6.3 %collective-permute-start.2 = (s32[3,64]{1,0:T(4,128)}, s32[3,64]{1,0:T(4,128)S(1)}, u32[]{:S(2)}, u32[]{:S(2)}) collective-permute-start(s32[3,64]{1,0:T(4,128)} %own_ref.1), channel_id=1, source_target_pairs={{0,3},{1,0},{2,1},{3,2},{4,7},{5,4},{6,5},{7,6},{8,11},{9,8},{10,9... | collective-permute-start | bytes 2312 | tf_op jit(solution)/shard_map/ppermute | solution.py:321
  5.4 9.8 %collective-permute-start.4 = (bf16[256,256]{1,0:T(8,128)(2,1)}, bf16[256,256]{1,0:T(8,128)(2,1)S(1)}, u32[]{:S(2)}, u32[]{:S(2)}) collective-permute-start(bf16[256,256]{1,0:T(8,128)(2,1)} %v_ref.1), channel_id=1, source_target_pairs={{0,28},{4,0},{8,4},{12,8},{16,12},{20,16},{24,20},{28,24},{1,29},{... | collective-permute-start | bytes 393224 | tf_op jit(solution)/shard_map/ppermute | solution.py:321
  11.2 5.2 %collective-permute-start.3 = (bf16[256,256]{1,0:T(8,128)(2,1)S(1)}, bf16[256,256]{1,0:T(8,128)(2,1)S(1)}, u32[]{:S(2)}, u32[]{:S(2)}) collective-permute-start(bf16[256,256]{1,0:T(8,128)(2,1)S(1)} %get-tuple-element.50.k_ref), channel_id=1, source_target_pairs={{0,28},{4,0},{8,4},{12,8},{16,12},{20,16},{24,20},{28,24},{1,29},{... | collective-permute-start | bytes 393224 | tf_op jit(solution)/shard_map/ppermute | solution.py:321
  15.2 8.7 %collective-permute-start.6 = (bf16[256,256]{1,0:T(8,128)(2,1)S(1)}, bf16[256,256]{1,0:T(8,128)(2,1)S(1)}, u32[]{:S(2)}, u32[]{:S(2)}) collective-permute-start(bf16[256,256]{1,0:T(8,128)(2,1)S(1)} %collective-permute-done.4.refs_1_), channel_id=1, source_target_pairs={{0,24},{4,28},{8,0},{12,4},{16,8},{20,12},{24,16},{28,20},{1,25},{... | collective-permute-start | bytes 393224 | tf_op jit(solution)/shard_map/ppermute | solution.py:321
  16.4 7.5 %copy-start = (bf16[256,256]{1,0:T(8,128)(2,1)S(1)}, bf16[256,256]{1,0:T(8,128)(2,1)}, u32[]{:S(2)}) copy-start(bf16[256,256]{1,0:T(8,128)(2,1)} %v_ref.1) | copy-start | bytes 393220
  18.0 12.4 %collective-permute-start.8 = (bf16[256,512]{1,0:T(8,128)(2,1)S(1)}, bf16[256,512]{1,0:T(8,128)(2,1)S(1)}, u32[]{:S(2)}, u32[]{:S(2)}) collective-permute-start(bf16[256,512]{1,0:T(8,128)(2,1)S(1)} %get-tuple-element.45), channel_id=1, source_target_pairs={{0,4},{4,0},{8,12},{12,8},{16,20},{20,16},{24,28},{28,24},{1,5},{5... | collective-permute-start | bytes 786440 | tf_op jit(solution)/shard_map/ppermute | solution.py:326
  20.1 7.7 %collective-permute-start.5 = (bf16[256,256]{1,0:T(8,128)(2,1)S(1)}, bf16[256,256]{1,0:T(8,128)(2,1)S(1)}, u32[]{:S(2)}, u32[]{:S(2)}) collective-permute-start(bf16[256,256]{1,0:T(8,128)(2,1)S(1)} %collective-permute-done.3.refs_0_), channel_id=1, source_target_pairs={{0,24},{4,28},{8,0},{12,4},{16,8},{20,12},{24,16},{28,20},{1,25},{... | collective-permute-start | bytes 393224 | tf_op jit(solution)/shard_map/ppermute | solution.py:321
  23.8 6.6 %collective-permute-start.7 = (bf16[256,256]{1,0:T(8,128)(2,1)S(1)}, bf16[256,256]{1,0:T(8,128)(2,1)S(1)}, u32[]{:S(2)}, u32[]{:S(2)}) collective-permute-start(bf16[256,256]{1,0:T(8,128)(2,1)S(1)} %get-tuple-element.50.k_ref), channel_id=1, source_target_pairs={{0,24},{4,28},{8,0},{12,4},{16,8},{20,12},{24,16},{28,20},{1,25},{... | collective-permute-start | bytes 393224 | tf_op jit(solution)/shard_map/ppermute | solution.py:321
  23.9 8.0 %collective-permute-start.9 = (bf16[256,256]{1,0:T(8,128)(2,1)S(1)}, bf16[256,256]{1,0:T(8,128)(2,1)S(1)}, u32[]{:S(2)}, u32[]{:S(2)}) collective-permute-start(bf16[256,256]{1,0:T(8,128)(2,1)S(1)} %copy-done), channel_id=1, source_target_pairs={{0,24},{4,28},{8,0},{12,4},{16,8},{20,12},{24,16},{28,20},{1,25},{... | collective-permute-start | bytes 393224 | tf_op jit(solution)/shard_map/ppermute | solution.py:321
  28.7 7.9 %collective-permute-start.10 = (bf16[256,256]{1,0:T(8,128)(2,1)S(1)}, bf16[256,256]{1,0:T(8,128)(2,1)S(1)}, u32[]{:S(2)}, u32[]{:S(2)}) collective-permute-start(bf16[256,256]{1,0:T(8,128)(2,1)S(1)} %get-tuple-element.64), channel_id=1, source_target_pairs={{0,4},{4,8},{8,12},{12,16},{16,20},{20,24},{24,28},{28,0},{1,5},{5... | collective-permute-start | bytes 393224 | tf_op jit(solution)/shard_map/ppermute | solution.py:321
  29.7 8.6 %collective-permute-start.12 = (bf16[256,256]{1,0:T(8,128)(2,1)S(1)}, bf16[256,256]{1,0:T(8,128)(2,1)S(1)}, u32[]{:S(2)}, u32[]{:S(2)}) collective-permute-start(bf16[256,256]{1,0:T(8,128)(2,1)S(1)} %get-tuple-element.66), channel_id=1, source_target_pairs={{0,4},{4,8},{8,12},{12,16},{16,20},{20,24},{24,28},{28,0},{1,5},{5... | collective-permute-start | bytes 393224 | tf_op jit(solution)/shard_map/ppermute | solution.py:321
  36.6 8.8 %collective-permute-start.11 = (bf16[256,256]{1,0:T(8,128)(2,1)S(1)}, bf16[256,256]{1,0:T(8,128)(2,1)S(1)}, u32[]{:S(2)}, u32[]{:S(2)}) collective-permute-start(bf16[256,256]{1,0:T(8,128)(2,1)S(1)} %shard_map.111), channel_id=1, source_target_pairs={{0,8},{4,12},{8,16},{12,20},{16,24},{20,28},{24,0},{28,4},{1,9},{5... | collective-permute-start | bytes 393224 | tf_op jit(solution)/shard_map/ppermute | solution.py:321
  38.4 8.0 %collective-permute-start.13 = (bf16[256,256]{1,0:T(8,128)(2,1)S(1)}, bf16[256,256]{1,0:T(8,128)(2,1)S(1)}, u32[]{:S(2)}, u32[]{:S(2)}) collective-permute-start(bf16[256,256]{1,0:T(8,128)(2,1)S(1)} %shard_map.112), channel_id=1, source_target_pairs={{0,8},{4,12},{8,16},{12,20},{16,24},{20,28},{24,0},{28,4},{1,9},{5... | collective-permute-start | bytes 393224 | tf_op jit(solution)/shard_map/ppermute | solution.py:321

commit v20 on v19

--- a/solution.py
+++ b/solution.py
@@ -362,6 +362,7 @@
     )(span_map, tables, lse, q, do, at)
     v1, _ = lax.optimization_barrier((v1, shared[3]))
     v3 = shifted(v1, -2)
+    k3 = shifted(k1, -2)
     dqs = []
     dq_out = ((wide_q // groups, rows), F32)
     part_out = ((rows, 2 * HEAD), BF16)
@@ -385,12 +386,10 @@
 
     (part1,) = hop(1, every, k1, v1, joined=True)
     swapped = exchanged(part1)
-    held, kr2, v_far, _ = lax.optimization_barrier((k1, kr, v, part1))
-    k3 = shifted(held, -2)
+    kr2, v_far, _ = lax.optimization_barrier((kr, v, part1))
     k2 = shifted(kr2, -2)
     v2 = shifted(v_far, -2)
     moved = [shifted(*hop(3, (g,), k3, v3), 1) for g in every]
-    k2, swapped = lax.optimization_barrier((k2, swapped))
     parts2 = hop(2, every, k2, v2)
     results = call(
         functools.partial(own_kernel, groups),

time: 47.5 us -> 45.4 us (0.956)
  waiting for transfers between devices: 10.7 us -> 5.71 us
  starting transfers between devices: 22 us -> 24.8 us
    ppermute x13, waiting for transfers between devices: 10.7 us -> 5.71 us  [shifted(): return lax.ppermute(value, axis, pairs)]
    ppermute x1, starting transfers between devices: 2.08 us -> 4.36 us  [exchanged(): lax.ppermute(value, 'ctx', [(source, source ^ 1) for source in range(coun...]
    ppermute x13, starting transfers between devices: 19.9 us -> 20.5 us  [shifted(): return lax.ppermute(value, axis, pairs)]
  transfers between devices with their start and end apart: 14 -> 14, of which waited for: 6 -> 5; matrix products, arithmetic and copies ran while one was open for 0% -> 0% of each run, Pallas kernels for 28% -> 29%
where the time goes in v20:
time: 45.4 us; the launch traced here: 45.2 us
  starting transfers between devices  24.8 us (55%)
  Pallas kernels  13.9 us (31%)
  waiting for transfers between devices  5.71 us (13%)
  between operations  0.7 us (2%)
    ppermute x13, starting transfers between devices, shifted(): return lax.ppermute(value, axis, pairs)  20.5 us
    ppermute x13, waiting for transfers between devices, shifted(): return lax.ppermute(value, axis, pairs)  5.71 us
    pallas_call x4, Pallas kernels, hop(): call(functools.partial(hop_kernel, step, wanted, started, joined), [dq_ou...  5.12 us
    ppermute x1, starting transfers between devices, exchanged(): lax.ppermute(value, 'ctx', [(source, source ^ 1) for source in range(coun...  4.36 us
    pallas_call x1, Pallas kernels, shards(): call(functools.partial(own_kernel, groups), [dq_out] * groups + [((rows,...  3.05 us
    pallas_call x1, Pallas kernels, shards(): call(functools.partial(prep_kernel, groups), [((rows, wide_q), BF16)] * 2...  2.41 us
    pallas_call x1, Pallas kernels, shards(): call(key_kernel, [((rows, wide_k), BF16), ((HEAD, rows), F32)], [VMEM] * 5)  1.24 us
    pallas_call x1, Pallas kernels, shards(): call(functools.partial(query_kernel, groups), [((rows, wide_q), BF16)] +...  1.1 us
  transfers between devices with their start and end apart: 14, of which 5 were waited for; matrix products, arithmetic and copies ran while one was open for 0% of the time, Pallas kernels for 29%

profile of v20, /device:TPU:0, one launch (start us, length us, event | category | flops | bytes accessed | tf_op | source)
XLA Modules:
  0.0 45.2 jit_solution(18370275811794271713)
XLA Ops:
  0.6 0.5 %collective-permute-start = (s32[3,64]{1,0:T(4,128)}, s32[3,64]{1,0:T(4,128)S(1)}, u32[]{:S(2)}, u32[]{:S(2)}) collective-permute-start(s32[3,64]{1,0:T(4,128)} %own_ref.1), channel_id=1, source_target_pairs={{0,1},{1,2},{2,3},{3,0},{4,5},{5,6},{6,7},{7,4},{8,9},{9,10},{10,1... | collective-permute-start | bytes 2312 | tf_op jit(solution)/shard_map/ppermute | solution.py:321
  1.1 2.6 %collective-permute-start.1 = (s32[3,64]{1,0:T(4,128)}, s32[3,64]{1,0:T(4,128)S(1)}, u32[]{:S(2)}, u32[]{:S(2)}) collective-permute-start(s32[3,64]{1,0:T(4,128)} %own_ref.1), channel_id=1, source_target_pairs={{0,2},{1,3},{2,0},{3,1},{4,6},{5,7},{6,4},{7,5},{8,10},{9,11},{10,... | collective-permute-start | bytes 2312 | tf_op jit(solution)/shard_map/ppermute | solution.py:321
  3.7 1.4 %collective-permute-start.2 = (s32[3,64]{1,0:T(4,128)}, s32[3,64]{1,0:T(4,128)S(1)}, u32[]{:S(2)}, u32[]{:S(2)}) collective-permute-start(s32[3,64]{1,0:T(4,128)} %own_ref.1), channel_id=1, source_target_pairs={{0,3},{1,0},{2,1},{3,2},{4,7},{5,4},{6,5},{7,6},{8,11},{9,8},{10,9... | collective-permute-start | bytes 2312 | tf_op jit(solution)/shard_map/ppermute | solution.py:321
  5.1 4.6 %collective-permute-start.4 = (bf16[256,256]{1,0:T(8,128)(2,1)}, bf16[256,256]{1,0:T(8,128)(2,1)S(1)}, u32[]{:S(2)}, u32[]{:S(2)}) collective-permute-start(bf16[256,256]{1,0:T(8,128)(2,1)} %v_ref.1), channel_id=1, source_target_pairs={{0,28},{4,0},{8,4},{12,8},{16,12},{20,16},{24,20},{28,24},{1,29},{... | collective-permute-start | bytes 393224 | tf_op jit(solution)/shard_map/ppermute | solution.py:321
  9.6 0.0 collective-permute-done.p1_ref
  9.6 0.0 collective-permute-done.1.p2_ref
  9.7 1.2 %shard_map.103 = (bf16[256,256]{1,0:T(8,128)(2,1)S(1)}, f32[128,256]{1,0:T(8,128)S(1)}) custom-call(s32[3,64]{1,0:T(4,128)} %own_ref.1, s32[3,64]{1,0:T(4,128)S(1)} %collective-permute-done.p1_ref, s32[3,64]{1,0:T(4,128)S(1)} %collective-permute-done.1.p2_ref, s32[3,64]{1,0:T(4,128)S(1)} %collective-permute-done.2.p3_ref, bf16[256,256]{1,0:T(8,128)(2,1)} %k_ref.1), custom_call_target="tpu_custom_call" | custom-call | flops 1048576 | bytes 3690000 | tf_op jit(solution)/shard_map/pallas_call | solution.py:347
  10.9 1.6 %collective-permute-start.3 = (bf16[256,256]{1,0:T(8,128)(2,1)S(1)}, bf16[256,256]{1,0:T(8,128)(2,1)S(1)}, u32[]{:S(2)}, u32[]{:S(2)}) collective-permute-start(bf16[256,256]{1,0:T(8,128)(2,1)S(1)} %get-tuple-element.46.k_ref), channel_id=1, source_target_pairs={{0,28},{4,0},{8,4},{12,8},{16,12},{20,16},{24,20},{28,24},{1,29},{... | collective-permute-start | bytes 393224 | tf_op jit(solution)/shard_map/ppermute | solution.py:321
  12.5 2.4 %shard_map.104 = (bf16[256,1024]{1,0:T(8,128)(2,1)S(1)}, bf16[256,1024]{1,0:T(8,128)(2,1)S(1)}, f32[8,256]{1,0:T(8,128)S(1)}, f32[8,256]{1,0:T(8,128)S(1)}, s32[8,128]{1,0:T(8,128)S(1)}) custom-call(s32[8]{0:T(128)} %span_ref.1, f32[128,256]{1,0:T(8,128)S(1)} %get-tuple-element.33.tables_ref, f32[8,256]{1,0:T(8,128)} %lse_hbm.1, bf16[256,1024]{1,0:T(8,128)(2,1)} %q_hbm.1, ...), custom_call_target="tpu_custom_call" | custom-call | flops 1048576 | bytes 7380000 | tf_op jit(solution)/shard_map/pallas_call | solution.py:351
  14.9 0.5 %collective-permute-start.6 = (bf16[256,256]{1,0:T(8,128)(2,1)S(1)}, bf16[256,256]{1,0:T(8,128)(2,1)S(1)}, u32[]{:S(2)}, u32[]{:S(2)}) collective-permute-start(bf16[256,256]{1,0:T(8,128)(2,1)S(1)} %collective-permute-done.4.refs_1_), channel_id=1, source_target_pairs={{0,24},{4,28},{8,0},{12,4},{16,8},{20,12},{24,16},{28,20},{1,25},{... | collective-permute-start | bytes 393224 | tf_op jit(solution)/shard_map/ppermute | solution.py:321
  15.4 0.7 %collective-permute-done.3.refs_0_ = bf16[256,256]{1,0:T(8,128)(2,1)S(1)} collective-permute-done((bf16[256,256]{1,0:T(8,128)(2,1)S(1)}, bf16[256,256]{1,0:T(8,128)(2,1)S(1)}, u32[]{:S(2)}, u32[]{:S(2)}) %collective-permute-start.3) | collective-permute-done | bytes 131104 | tf_op jit(solution)/shard_map/ppermute | solution.py:321
  16.1 1.4 %collective-permute-start.5 = (bf16[256,256]{1,0:T(8,128)(2,1)S(1)}, bf16[256,256]{1,0:T(8,128)(2,1)S(1)}, u32[]{:S(2)}, u32[]{:S(2)}) collective-permute-start(bf16[256,256]{1,0:T(8,128)(2,1)S(1)} %collective-permute-done.3.refs_0_), channel_id=1, source_target_pairs={{0,24},{4,28},{8,0},{12,4},{16,8},{20,12},{24,16},{28,20},{1,25},{... | collective-permute-start | bytes 393224 | tf_op jit(solution)/shard_map/ppermute | solution.py:321
  17.5 1.6 %shard_map.105 = (f32[512,256]{1,0:T(8,128)S(1)}, f32[512,256]{1,0:T(8,128)S(1)}, bf16[256,512]{1,0:T(8,128)(2,1)S(1)}) custom-call(bf16[256,256]{1,0:T(8,128)(2,1)S(1)} %collective-permute-done.3.refs_0_, bf16[256,256]{1,0:T(8,128)(2,1)S(1)} %collective-permute-done.4.refs_1_, bf16[256,1024]{1,0:T(8,128)(2,1)S(1)} %get-tuple-element.35.refs_2_.refs_3_.refs_4_.qr_ref, ...), custom_call_target="tpu_custom_call" | custom-call | flops 1048576 | bytes 7380000 | tf_op jit(solution)/shard_map/pallas_call | solution.py:374
  19.2 4.4 %collective-permute-start.9 = (bf16[256,512]{1,0:T(8,128)(2,1)S(1)}, bf16[256,512]{1,0:T(8,128)(2,1)S(1)}, u32[]{:S(2)}, u32[]{:S(2)}) collective-permute-start(bf16[256,512]{1,0:T(8,128)(2,1)S(1)} %get-tuple-element.45), channel_id=1, source_target_pairs={{0,4},{4,0},{8,12},{12,8},{16,20},{20,16},{24,28},{28,24},{1,5},{5... | collective-permute-start | bytes 786440 | tf_op jit(solution)/shard_map/ppermute | solution.py:326
  23.5 0.0 collective-permute-start.7
  23.5 0.0 collective-permute-start.8
  23.6 0.9 %shard_map.107 = (f32[512,256]{1,0:T(8,128)S(1)}, bf16[256,256]{1,0:T(8,128)(2,1)S(1)}) custom-call(f32[512,256]{1,0:T(8,128)S(1)} %get-tuple-element.43.refs_0_, bf16[256,256]{1,0:T(8,128)(2,1)S(1)} %collective-permute-done.5.refs_1_, bf16[256,256]{1,0:T(8,128)(2,1)S(1)} %collective-permute-done.6.refs_2_, ...), custom_call_target="tpu_custom_call" | custom-call | flops 1048576 | bytes 3690000 | tf_op jit(solution)/shard_map/pallas_call | solution.py:374
  24.5 2.1 %collective-permute-start.12 = (bf16[256,256]{1,0:T(8,128)(2,1)S(1)}, bf16[256,256]{1,0:T(8,128)(2,1)S(1)}, u32[]{:S(2)}, u32[]{:S(2)}) collective-permute-start(bf16[256,256]{1,0:T(8,128)(2,1)S(1)} %get-tuple-element.60), channel_id=1, source_target_pairs={{0,4},{4,8},{8,12},{12,16},{16,20},{20,24},{24,28},{28,0},{1,5},{5... | collective-permute-start | bytes 393224 | tf_op jit(solution)/shard_map/ppermute | solution.py:321
  26.6 0.9 %shard_map.106 = (f32[512,256]{1,0:T(8,128)S(1)}, bf16[256,256]{1,0:T(8,128)(2,1)S(1)}) custom-call(f32[512,256]{1,0:T(8,128)S(1)} %get-tuple-element.41.refs_0_, bf16[256,256]{1,0:T(8,128)(2,1)S(1)} %collective-permute-done.5.refs_1_, bf16[256,256]{1,0:T(8,128)(2,1)S(1)} %collective-permute-done.6.refs_2_, ...), custom_call_target="tpu_custom_call" | custom-call | flops 1048576 | bytes 3690000 | tf_op jit(solution)/shard_map/pallas_call | solution.py:374
  27.5 1.5 %collective-permute-start.10 = (bf16[256,256]{1,0:T(8,128)(2,1)S(1)}, bf16[256,256]{1,0:T(8,128)(2,1)S(1)}, u32[]{:S(2)}, u32[]{:S(2)}) collective-permute-start(bf16[256,256]{1,0:T(8,128)(2,1)S(1)} %get-tuple-element.58), channel_id=1, source_target_pairs={{0,4},{4,8},{8,12},{12,16},{16,20},{20,24},{24,28},{28,0},{1,5},{5... | collective-permute-start | bytes 393224 | tf_op jit(solution)/shard_map/ppermute | solution.py:321
  29.0 0.5 %collective-permute-done.7.refs_2_ = bf16[256,256]{1,0:T(8,128)(2,1)S(1)} collective-permute-done((bf16[256,256]{1,0:T(8,128)(2,1)S(1)}, bf16[256,256]{1,0:T(8,128)(2,1)S(1)}, u32[]{:S(2)}, u32[]{:S(2)}) %collective-permute-start.7) | collective-permute-done | bytes 131104 | tf_op jit(solution)/shard_map/ppermute | solution.py:321
  29.5 1.4 %collective-permute-done.8.refs_3_ = bf16[256,256]{1,0:T(8,128)(2,1)S(1)} collective-permute-done((bf16[256,256]{1,0:T(8,128)(2,1)S(1)}, bf16[256,256]{1,0:T(8,128)(2,1)S(1)}, u32[]{:S(2)}, u32[]{:S(2)}) %collective-permute-start.8) | collective-permute-done | bytes 131104 | tf_op jit(solution)/shard_map/ppermute | solution.py:321
  30.9 1.6 %shard_map.108 = (f32[512,256]{1,0:T(8,128)S(1)}, f32[512,256]{1,0:T(8,128)S(1)}, bf16[256,256]{1,0:T(8,128)(2,1)S(1)}, bf16[256,256]{1,0:T(8,128)(2,1)S(1)}) custom-call(f32[512,256]{1,0:T(8,128)S(1)} %get-tuple-element.42.refs_0_, f32[512,256]{1,0:T(8,128)S(1)} %get-tuple-element.44.refs_1_, bf16[256,256]{1,0:T(8,128)(2,1)S(1)} %collective-permute-done.7.refs_2_, ...), custom_call_target="tpu_custom_call" | custom-call | flops 1048576 | bytes 7380000 | tf_op jit(solution)/shard_map/pallas_call | solution.py:374
  32.6 2.0 %collective-permute-done.12.three_ref = bf16[256,256]{1,0:T(8,128)(2,1)S(1)} collective-permute-done((bf16[256,256]{1,0:T(8,128)(2,1)S(1)}, bf16[256,256]{1,0:T(8,128)(2,1)S(1)}, u32[]{:S(2)}, u32[]{:S(2)}) %collective-permute-start.12) | collective-permute-done | bytes 131104 | tf_op jit(solution)/shard_map/ppermute | solution.py:321
  34.6 0.1 shard_map.112
  34.7 1.4 %collective-permute-start.13 = (bf16[256,256]{1,0:T(8,128)(2,1)S(1)}, bf16[256,256]{1,0:T(8,128)(2,1)S(1)}, u32[]{:S(2)}, u32[]{:S(2)}) collective-permute-start(bf16[256,256]{1,0:T(8,128)(2,1)S(1)} %shard_map.112), channel_id=1, source_target_pairs={{0,8},{4,12},{8,16},{12,20},{16,24},{20,28},{24,0},{28,4},{1,9},{5... | collective-permute-start | bytes 393224 | tf_op jit(solution)/shard_map/ppermute | solution.py:321
  36.1 0.1 shard_map.111
  36.1 2.9 %collective-permute-start.11 = (bf16[256,256]{1,0:T(8,128)(2,1)S(1)}, bf16[256,256]{1,0:T(8,128)(2,1)S(1)}, u32[]{:S(2)}, u32[]{:S(2)}) collective-permute-start(bf16[256,256]{1,0:T(8,128)(2,1)S(1)} %shard_map.111), channel_id=1, source_target_pairs={{0,8},{4,12},{8,16},{12,20},{16,24},{20,28},{24,0},{28,4},{1,9},{5... | collective-permute-start | bytes 393224 | tf_op jit(solution)/shard_map/ppermute | solution.py:321
  39.1 3.0 %shard_map.109 = (f32[512,256]{1,0:T(8,128)S(1)}, f32[512,256]{1,0:T(8,128)S(1)}, f32[256,256]{1,0:T(8,128)S(1)}, f32[256,256]{1,0:T(8,128)S(1)}) custom-call(bf16[256,256]{1,0:T(8,128)(2,1)S(1)} %get-tuple-element.46.k_ref, bf16[256,256]{1,0:T(8,128)(2,1)} %v_ref.1, bf16[256,1024]{1,0:T(8,128)(2,1)S(1)} %get-tuple-element.35.refs_2_.refs_3_.refs_4_.qr_ref, ...), custom_call_target="tpu_custom_call" | custom-call | flops 1048576 | bytes 11070000 | tf_op jit(solution)/shard_map/pallas_call | solution.py:394
  42.1 1.1 %shard_map.110 = (bf16[256,1024]{1,0:T(8,128)(2,1)}, f32[256,256]{1,0:T(8,128)S(1)}, f32[256,256]{1,0:T(8,128)S(1)}) custom-call(f32[128,256]{1,0:T(8,128)S(1)} %get-tuple-element.33.tables_ref, f32[512,256]{1,0:T(8,128)S(1)} %get-tuple-element.50.refs_0_, f32[512,256]{1,0:T(8,128)S(1)} %get-tuple-element.51.refs_1_, ...), custom_call_target="tpu_custom_call" | custom-call | flops 1048576 | bytes 3690000 | tf_op jit(solution)/shard_map/pallas_call | solution.py:401
  43.2 1.1 %collective-permute-done.11.refs_2_ = bf16[256,256]{1,0:T(8,128)(2,1)S(1)} collective-permute-done((bf16[256,256]{1,0:T(8,128)(2,1)S(1)}, bf16[256,256]{1,0:T(8,128)(2,1)S(1)}, u32[]{:S(2)}, u32[]{:S(2)}) %collective-permute-start.11) | collective-permute-done | bytes 131104 | tf_op jit(solution)/shard_map/ppermute | solution.py:321
  44.3 0.9 %shard_map.113 = (bf16[256,256]{1,0:T(8,128)(2,1)}, bf16[256,256]{1,0:T(8,128)(2,1)}) custom-call(f32[128,256]{1,0:T(8,128)S(1)} %get-tuple-element.33.tables_ref, f32[256,256]{1,0:T(8,128)S(1)} %get-tuple-element.55.refs_0_, f32[256,256]{1,0:T(8,128)S(1)} %get-tuple-element.56.refs_1_, bf16[256,256]{1,0:T(8,128)(2,1)S(1)} %collective-permute-done.11.refs_2_, ...), custom_call_target="tpu_custom_call" | custom-call | flops 1048576 | bytes 3690000 | tf_op jit(solution)/shard_map/pallas_call | solution.py:413
  (9 shorter events, 0.0 us)
Async XLA Ops:
  0.6 9.0 %collective-permute-start = (s32[3,64]{1,0:T(4,128)}, s32[3,64]{1,0:T(4,128)S(1)}, u32[]{:S(2)}, u32[]{:S(2)}) collective-permute-start(s32[3,64]{1,0:T(4,128)} %own_ref.1), channel_id=1, source_target_pairs={{0,1},{1,2},{2,3},{3,0},{4,5},{5,6},{6,7},{7,4},{8,9},{9,10},{10,1... | collective-permute-start | bytes 2312 | tf_op jit(solution)/shard_map/ppermute | solution.py:321
  1.1 8.5 %collective-permute-start.1 = (s32[3,64]{1,0:T(4,128)}, s32[3,64]{1,0:T(4,128)S(1)}, u32[]{:S(2)}, u32[]{:S(2)}) collective-permute-start(s32[3,64]{1,0:T(4,128)} %own_ref.1), channel_id=1, source_target_pairs={{0,2},{1,3},{2,0},{3,1},{4,6},{5,7},{6,4},{7,5},{8,10},{9,11},{10,... | collective-permute-start | bytes 2312 | tf_op jit(solution)/shard_map/ppermute | solution.py:321
  3.7 6.0 %collective-permute-start.2 = (s32[3,64]{1,0:T(4,128)}, s32[3,64]{1,0:T(4,128)S(1)}, u32[]{:S(2)}, u32[]{:S(2)}) collective-permute-start(s32[3,64]{1,0:T(4,128)} %own_ref.1), channel_id=1, source_target_pairs={{0,3},{1,0},{2,1},{3,2},{4,7},{5,4},{6,5},{7,6},{8,11},{9,8},{10,9... | collective-permute-start | bytes 2312 | tf_op jit(solution)/shard_map/ppermute | solution.py:321
  5.1 9.8 %collective-permute-start.4 = (bf16[256,256]{1,0:T(8,128)(2,1)}, bf16[256,256]{1,0:T(8,128)(2,1)S(1)}, u32[]{:S(2)}, u32[]{:S(2)}) collective-permute-start(bf16[256,256]{1,0:T(8,128)(2,1)} %v_ref.1), channel_id=1, source_target_pairs={{0,28},{4,0},{8,4},{12,8},{16,12},{20,16},{24,20},{28,24},{1,29},{... | collective-permute-start | bytes 393224 | tf_op jit(solution)/shard_map/ppermute | solution.py:321
  10.9 5.2 %collective-permute-start.3 = (bf16[256,256]{1,0:T(8,128)(2,1)S(1)}, bf16[256,256]{1,0:T(8,128)(2,1)S(1)}, u32[]{:S(2)}, u32[]{:S(2)}) collective-permute-start(bf16[256,256]{1,0:T(8,128)(2,1)S(1)} %get-tuple-element.46.k_ref), channel_id=1, source_target_pairs={{0,28},{4,0},{8,4},{12,8},{16,12},{20,16},{24,20},{28,24},{1,29},{... | collective-permute-start | bytes 393224 | tf_op jit(solution)/shard_map/ppermute | solution.py:321
  14.9 8.7 %collective-permute-start.6 = (bf16[256,256]{1,0:T(8,128)(2,1)S(1)}, bf16[256,256]{1,0:T(8,128)(2,1)S(1)}, u32[]{:S(2)}, u32[]{:S(2)}) collective-permute-start(bf16[256,256]{1,0:T(8,128)(2,1)S(1)} %collective-permute-done.4.refs_1_), channel_id=1, source_target_pairs={{0,24},{4,28},{8,0},{12,4},{16,8},{20,12},{24,16},{28,20},{1,25},{... | collective-permute-start | bytes 393224 | tf_op jit(solution)/shard_map/ppermute | solution.py:321
  16.1 7.5 %collective-permute-start.5 = (bf16[256,256]{1,0:T(8,128)(2,1)S(1)}, bf16[256,256]{1,0:T(8,128)(2,1)S(1)}, u32[]{:S(2)}, u32[]{:S(2)}) collective-permute-start(bf16[256,256]{1,0:T(8,128)(2,1)S(1)} %collective-permute-done.3.refs_0_), channel_id=1, source_target_pairs={{0,24},{4,28},{8,0},{12,4},{16,8},{20,12},{24,16},{28,20},{1,25},{... | collective-permute-start | bytes 393224 | tf_op jit(solution)/shard_map/ppermute | solution.py:321
  17.5 6.0 %copy-start = (bf16[256,256]{1,0:T(8,128)(2,1)S(1)}, bf16[256,256]{1,0:T(8,128)(2,1)}, u32[]{:S(2)}) copy-start(bf16[256,256]{1,0:T(8,128)(2,1)} %v_ref.1) | copy-start | bytes 393220
  19.2 15.4 %collective-permute-start.9 = (bf16[256,512]{1,0:T(8,128)(2,1)S(1)}, bf16[256,512]{1,0:T(8,128)(2,1)S(1)}, u32[]{:S(2)}, u32[]{:S(2)}) collective-permute-start(bf16[256,512]{1,0:T(8,128)(2,1)S(1)} %get-tuple-element.45), channel_id=1, source_target_pairs={{0,4},{4,0},{8,12},{12,8},{16,20},{20,16},{24,28},{28,24},{1,5},{5... | collective-permute-start | bytes 786440 | tf_op jit(solution)/shard_map/ppermute | solution.py:326
  23.5 6.0 %collective-permute-start.7 = (bf16[256,256]{1,0:T(8,128)(2,1)S(1)}, bf16[256,256]{1,0:T(8,128)(2,1)S(1)}, u32[]{:S(2)}, u32[]{:S(2)}) collective-permute-start(bf16[256,256]{1,0:T(8,128)(2,1)S(1)} %get-tuple-element.46.k_ref), channel_id=1, source_target_pairs={{0,24},{4,28},{8,0},{12,4},{16,8},{20,12},{24,16},{28,20},{1,25},{... | collective-permute-start | bytes 393224 | tf_op jit(solution)/shard_map/ppermute | solution.py:321
  23.5 7.4 %collective-permute-start.8 = (bf16[256,256]{1,0:T(8,128)(2,1)S(1)}, bf16[256,256]{1,0:T(8,128)(2,1)S(1)}, u32[]{:S(2)}, u32[]{:S(2)}) collective-permute-start(bf16[256,256]{1,0:T(8,128)(2,1)S(1)} %copy-done), channel_id=1, source_target_pairs={{0,24},{4,28},{8,0},{12,4},{16,8},{20,12},{24,16},{28,20},{1,25},{... | collective-permute-start | bytes 393224 | tf_op jit(solution)/shard_map/ppermute | solution.py:321
  24.5 10.1 %collective-permute-start.12 = (bf16[256,256]{1,0:T(8,128)(2,1)S(1)}, bf16[256,256]{1,0:T(8,128)(2,1)S(1)}, u32[]{:S(2)}, u32[]{:S(2)}) collective-permute-start(bf16[256,256]{1,0:T(8,128)(2,1)S(1)} %get-tuple-element.60), channel_id=1, source_target_pairs={{0,4},{4,8},{8,12},{12,16},{16,20},{20,24},{24,28},{28,0},{1,5},{5... | collective-permute-start | bytes 393224 | tf_op jit(solution)/shard_map/ppermute | solution.py:321
  27.5 8.6 %collective-permute-start.10 = (bf16[256,256]{1,0:T(8,128)(2,1)S(1)}, bf16[256,256]{1,0:T(8,128)(2,1)S(1)}, u32[]{:S(2)}, u32[]{:S(2)}) collective-permute-start(bf16[256,256]{1,0:T(8,128)(2,1)S(1)} %get-tuple-element.58), channel_id=1, source_target_pairs={{0,4},{4,8},{8,12},{12,16},{16,20},{20,24},{24,28},{28,0},{1,5},{5... | collective-permute-start | bytes 393224 | tf_op jit(solution)/shard_map/ppermute | solution.py:321
  34.7 8.6 %collective-permute-start.13 = (bf16[256,256]{1,0:T(8,128)(2,1)S(1)}, bf16[256,256]{1,0:T(8,128)(2,1)S(1)}, u32[]{:S(2)}, u32[]{:S(2)}) collective-permute-start(bf16[256,256]{1,0:T(8,128)(2,1)S(1)} %shard_map.112), channel_id=1, source_target_pairs={{0,8},{4,12},{8,16},{12,20},{16,24},{20,28},{24,0},{28,4},{1,9},{5... | collective-permute-start | bytes 393224 | tf_op jit(solution)/shard_map/ppermute | solution.py:321
  36.1 8.2 %collective-permute-start.11 = (bf16[256,256]{1,0:T(8,128)(2,1)S(1)}, bf16[256,256]{1,0:T(8,128)(2,1)S(1)}, u32[]{:S(2)}, u32[]{:S(2)}) collective-permute-start(bf16[256,256]{1,0:T(8,128)(2,1)S(1)} %shard_map.111), channel_id=1, source_target_pairs={{0,8},{4,12},{8,16},{12,20},{16,24},{20,28},{24,0},{28,4},{1,9},{5... | collective-permute-start | bytes 393224 | tf_op jit(solution)/shard_map/ppermute | solution.py:321

commit v21 on v20

--- a/solution.py
+++ b/solution.py
@@ -362,7 +362,7 @@
     )(span_map, tables, lse, q, do, at)
     v1, _ = lax.optimization_barrier((v1, shared[3]))
     v3 = shifted(v1, -2)
-    k3 = shifted(k1, -2)
+    k3 = shifted(kr, -3)
     dqs = []
     dq_out = ((wide_q // groups, rows), F32)
     part_out = ((rows, 2 * HEAD), BF16)

time: 45.4 us -> 49.6 us (1.093)
  waiting for transfers between devices: 5.71 us -> 8.48 us
  starting transfers between devices: 24.8 us -> 26.2 us
    ppermute x13, starting transfers between devices: 20.5 us -> 24.4 us  [shifted(): return lax.ppermute(value, axis, pairs)]
    ppermute x13, waiting for transfers between devices: 5.71 us -> 8.48 us  [shifted(): return lax.ppermute(value, axis, pairs)]
    ppermute x1, starting transfers between devices: 4.36 us -> 1.86 us  [exchanged(): lax.ppermute(value, 'ctx', [(source, source ^ 1) for source in range(coun...]
  transfers between devices with their start and end apart: 14 -> 14, of which waited for: 5 -> 5; matrix products, arithmetic and copies ran while one was open for 0% -> 0% of each run, Pallas kernels for 29% -> 26%
where the time goes in v21:
time: 49.6 us; the launch traced here: 49.4 us
  starting transfers between devices  26.2 us (53%)
  Pallas kernels  13.9 us (28%)
  waiting for transfers between devices  8.48 us (17%)
  between operations  0.72 us (1%)
    ppermute x13, starting transfers between devices, shifted(): return lax.ppermute(value, axis, pairs)  24.4 us
    ppermute x13, waiting for transfers between devices, shifted(): return lax.ppermute(value, axis, pairs)  8.48 us
    pallas_call x4, Pallas kernels, hop(): call(functools.partial(hop_kernel, step, wanted, started, joined), [dq_ou...  5.13 us
    pallas_call x1, Pallas kernels, shards(): call(functools.partial(own_kernel, groups), [dq_out] * groups + [((rows,...  3.05 us
    pallas_call x1, Pallas kernels, shards(): call(functools.partial(prep_kernel, groups), [((rows, wide_q), BF16)] * 2...  2.41 us
    ppermute x1, starting transfers between devices, exchanged(): lax.ppermute(value, 'ctx', [(source, source ^ 1) for source in range(coun...  1.86 us
    pallas_call x1, Pallas kernels, shards(): call(key_kernel, [((rows, wide_k), BF16), ((HEAD, rows), F32)], [VMEM] * 5)  1.24 us
    pallas_call x1, Pallas kernels, shards(): call(functools.partial(query_kernel, groups), [((rows, wide_q), BF16)] +...  1.1 us
  transfers between devices with their start and end apart: 14, of which 5 were waited for; matrix products, arithmetic and copies ran while one was open for 0% of the time, Pallas kernels for 26%

profile of v21, /device:TPU:0, one launch (start us, length us, event | category | flops | bytes accessed | tf_op | source)
XLA Modules:
  0.0 49.4 jit_solution(9165049223728835588)
XLA Ops:
  0.6 0.5 %collective-permute-start = (s32[3,64]{1,0:T(4,128)}, s32[3,64]{1,0:T(4,128)S(1)}, u32[]{:S(2)}, u32[]{:S(2)}) collective-permute-start(s32[3,64]{1,0:T(4,128)} %own_ref.1), channel_id=1, source_target_pairs={{0,1},{1,2},{2,3},{3,0},{4,5},{5,6},{6,7},{7,4},{8,9},{9,10},{10,1... | collective-permute-start | bytes 2312 | tf_op jit(solution)/shard_map/ppermute | solution.py:321
  1.1 2.6 %collective-permute-start.1 = (s32[3,64]{1,0:T(4,128)}, s32[3,64]{1,0:T(4,128)S(1)}, u32[]{:S(2)}, u32[]{:S(2)}) collective-permute-start(s32[3,64]{1,0:T(4,128)} %own_ref.1), channel_id=1, source_target_pairs={{0,2},{1,3},{2,0},{3,1},{4,6},{5,7},{6,4},{7,5},{8,10},{9,11},{10,... | collective-permute-start | bytes 2312 | tf_op jit(solution)/shard_map/ppermute | solution.py:321
  3.7 1.4 %collective-permute-start.2 = (s32[3,64]{1,0:T(4,128)}, s32[3,64]{1,0:T(4,128)S(1)}, u32[]{:S(2)}, u32[]{:S(2)}) collective-permute-start(s32[3,64]{1,0:T(4,128)} %own_ref.1), channel_id=1, source_target_pairs={{0,3},{1,0},{2,1},{3,2},{4,7},{5,4},{6,5},{7,6},{8,11},{9,8},{10,9... | collective-permute-start | bytes 2312 | tf_op jit(solution)/shard_map/ppermute | solution.py:321
  5.1 4.6 %collective-permute-start.4 = (bf16[256,256]{1,0:T(8,128)(2,1)}, bf16[256,256]{1,0:T(8,128)(2,1)S(1)}, u32[]{:S(2)}, u32[]{:S(2)}) collective-permute-start(bf16[256,256]{1,0:T(8,128)(2,1)} %v_ref.1), channel_id=1, source_target_pairs={{0,28},{4,0},{8,4},{12,8},{16,12},{20,16},{24,20},{28,24},{1,29},{... | collective-permute-start | bytes 393224 | tf_op jit(solution)/shard_map/ppermute | solution.py:321
  9.6 0.0 collective-permute-done.p1_ref
  9.6 0.0 collective-permute-done.1.p2_ref
  9.7 0.0 collective-permute-done.2.p3_ref
  9.7 1.2 %shard_map.103 = (bf16[256,256]{1,0:T(8,128)(2,1)S(1)}, f32[128,256]{1,0:T(8,128)S(1)}) custom-call(s32[3,64]{1,0:T(4,128)} %own_ref.1, s32[3,64]{1,0:T(4,128)S(1)} %collective-permute-done.p1_ref, s32[3,64]{1,0:T(4,128)S(1)} %collective-permute-done.1.p2_ref, s32[3,64]{1,0:T(4,128)S(1)} %collective-permute-done.2.p3_ref, bf16[256,256]{1,0:T(8,128)(2,1)} %k_ref.1), custom_call_target="tpu_custom_call" | custom-call | flops 1048576 | bytes 3690000 | tf_op jit(solution)/shard_map/pallas_call | solution.py:347
  10.9 1.6 %collective-permute-start.3 = (bf16[256,256]{1,0:T(8,128)(2,1)S(1)}, bf16[256,256]{1,0:T(8,128)(2,1)S(1)}, u32[]{:S(2)}, u32[]{:S(2)}) collective-permute-start(bf16[256,256]{1,0:T(8,128)(2,1)S(1)} %get-tuple-element.46.k_ref), channel_id=1, source_target_pairs={{0,28},{4,0},{8,4},{12,8},{16,12},{20,16},{24,20},{28,24},{1,29},{... | collective-permute-start | bytes 393224 | tf_op jit(solution)/shard_map/ppermute | solution.py:321
  12.5 2.4 %shard_map.104 = (bf16[256,1024]{1,0:T(8,128)(2,1)S(1)}, bf16[256,1024]{1,0:T(8,128)(2,1)S(1)}, f32[8,256]{1,0:T(8,128)S(1)}, f32[8,256]{1,0:T(8,128)S(1)}, s32[8,128]{1,0:T(8,128)S(1)}) custom-call(s32[8]{0:T(128)} %span_ref.1, f32[128,256]{1,0:T(8,128)S(1)} %get-tuple-element.33.tables_ref, f32[8,256]{1,0:T(8,128)} %lse_hbm.1, bf16[256,1024]{1,0:T(8,128)(2,1)} %q_hbm.1, ...), custom_call_target="tpu_custom_call" | custom-call | flops 1048576 | bytes 7380000 | tf_op jit(solution)/shard_map/pallas_call | solution.py:351
  14.9 0.9 %collective-permute-start.6 = (bf16[256,256]{1,0:T(8,128)(2,1)S(1)}, bf16[256,256]{1,0:T(8,128)(2,1)S(1)}, u32[]{:S(2)}, u32[]{:S(2)}) collective-permute-start(bf16[256,256]{1,0:T(8,128)(2,1)S(1)} %collective-permute-done.4.refs_1_), channel_id=1, source_target_pairs={{0,24},{4,28},{8,0},{12,4},{16,8},{20,12},{24,16},{28,20},{1,25},{... | collective-permute-start | bytes 393224 | tf_op jit(solution)/shard_map/ppermute | solution.py:321
  15.8 0.5 %collective-permute-done.3.refs_0_ = bf16[256,256]{1,0:T(8,128)(2,1)S(1)} collective-permute-done((bf16[256,256]{1,0:T(8,128)(2,1)S(1)}, bf16[256,256]{1,0:T(8,128)(2,1)S(1)}, u32[]{:S(2)}, u32[]{:S(2)}) %collective-permute-start.3) | collective-permute-done | bytes 131104 | tf_op jit(solution)/shard_map/ppermute | solution.py:321
  16.3 1.6 %shard_map.105 = (f32[512,256]{1,0:T(8,128)S(1)}, f32[512,256]{1,0:T(8,128)S(1)}, bf16[256,512]{1,0:T(8,128)(2,1)S(1)}) custom-call(bf16[256,256]{1,0:T(8,128)(2,1)S(1)} %collective-permute-done.3.refs_0_, bf16[256,256]{1,0:T(8,128)(2,1)S(1)} %collective-permute-done.4.refs_1_, bf16[256,1024]{1,0:T(8,128)(2,1)S(1)} %get-tuple-element.35.refs_2_.refs_3_.refs_4_.qr_ref, ...), custom_call_target="tpu_custom_call" | custom-call | flops 1048576 | bytes 7380000 | tf_op jit(solution)/shard_map/pallas_call | solution.py:374
  17.9 1.9 %collective-permute-start.9 = (bf16[256,512]{1,0:T(8,128)(2,1)S(1)}, bf16[256,512]{1,0:T(8,128)(2,1)S(1)}, u32[]{:S(2)}, u32[]{:S(2)}) collective-permute-start(bf16[256,512]{1,0:T(8,128)(2,1)S(1)} %get-tuple-element.45), channel_id=1, source_target_pairs={{0,4},{4,0},{8,12},{12,8},{16,20},{20,16},{24,28},{28,24},{1,5},{5... | collective-permute-start | bytes 786440 | tf_op jit(solution)/shard_map/ppermute | solution.py:326
  19.8 4.0 %collective-permute-start.7 = (bf16[256,256]{1,0:T(8,128)(2,1)S(1)}, bf16[256,256]{1,0:T(8,128)(2,1)S(1)}, u32[]{:S(2)}, u32[]{:S(2)}) collective-permute-start(bf16[256,256]{1,0:T(8,128)(2,1)S(1)} %get-tuple-element.46.k_ref), channel_id=1, source_target_pairs={{0,24},{4,28},{8,0},{12,4},{16,8},{20,12},{24,16},{28,20},{1,25},{... | collective-permute-start | bytes 393224 | tf_op jit(solution)/shard_map/ppermute | solution.py:321
  23.8 0.0 collective-permute-start.8
  23.8 0.9 %shard_map.107 = (f32[512,256]{1,0:T(8,128)S(1)}, bf16[256,256]{1,0:T(8,128)(2,1)S(1)}) custom-call(f32[512,256]{1,0:T(8,128)S(1)} %get-tuple-element.43.refs_0_, bf16[256,256]{1,0:T(8,128)(2,1)S(1)} %collective-permute-done.5.refs_1_, bf16[256,256]{1,0:T(8,128)(2,1)S(1)} %collective-permute-done.6.refs_2_, ...), custom_call_target="tpu_custom_call" | custom-call | flops 1048576 | bytes 3690000 | tf_op jit(solution)/shard_map/pallas_call | solution.py:374
  24.8 0.7 %collective-permute-start.12 = (bf16[256,256]{1,0:T(8,128)(2,1)S(1)}, bf16[256,256]{1,0:T(8,128)(2,1)S(1)}, u32[]{:S(2)}, u32[]{:S(2)}) collective-permute-start(bf16[256,256]{1,0:T(8,128)(2,1)S(1)} %get-tuple-element.60), channel_id=1, source_target_pairs={{0,4},{4,8},{8,12},{12,16},{16,20},{20,24},{24,28},{28,0},{1,5},{5... | collective-permute-start | bytes 393224 | tf_op jit(solution)/shard_map/ppermute | solution.py:321
  25.5 0.9 %shard_map.106 = (f32[512,256]{1,0:T(8,128)S(1)}, bf16[256,256]{1,0:T(8,128)(2,1)S(1)}) custom-call(f32[512,256]{1,0:T(8,128)S(1)} %get-tuple-element.41.refs_0_, bf16[256,256]{1,0:T(8,128)(2,1)S(1)} %collective-permute-done.5.refs_1_, bf16[256,256]{1,0:T(8,128)(2,1)S(1)} %collective-permute-done.6.refs_2_, ...), custom_call_target="tpu_custom_call" | custom-call | flops 1048576 | bytes 3690000 | tf_op jit(solution)/shard_map/pallas_call | solution.py:374
  26.4 7.8 %collective-permute-start.10 = (bf16[256,256]{1,0:T(8,128)(2,1)S(1)}, bf16[256,256]{1,0:T(8,128)(2,1)S(1)}, u32[]{:S(2)}, u32[]{:S(2)}) collective-permute-start(bf16[256,256]{1,0:T(8,128)(2,1)S(1)} %get-tuple-element.58), channel_id=1, source_target_pairs={{0,4},{4,8},{8,12},{12,16},{16,20},{20,24},{24,28},{28,0},{1,5},{5... | collective-permute-start | bytes 393224 | tf_op jit(solution)/shard_map/ppermute | solution.py:321
  34.3 1.6 %shard_map.108 = (f32[512,256]{1,0:T(8,128)S(1)}, f32[512,256]{1,0:T(8,128)S(1)}, bf16[256,256]{1,0:T(8,128)(2,1)S(1)}, bf16[256,256]{1,0:T(8,128)(2,1)S(1)}) custom-call(f32[512,256]{1,0:T(8,128)S(1)} %get-tuple-element.42.refs_0_, f32[512,256]{1,0:T(8,128)S(1)} %get-tuple-element.44.refs_1_, bf16[256,256]{1,0:T(8,128)(2,1)S(1)} %collective-permute-done.7.refs_2_, ...), custom_call_target="tpu_custom_call" | custom-call | flops 1048576 | bytes 7380000 | tf_op jit(solution)/shard_map/pallas_call | solution.py:374
  35.9 3.9 %collective-permute-done.12.three_ref = bf16[256,256]{1,0:T(8,128)(2,1)S(1)} collective-permute-done((bf16[256,256]{1,0:T(8,128)(2,1)S(1)}, bf16[256,256]{1,0:T(8,128)(2,1)S(1)}, u32[]{:S(2)}, u32[]{:S(2)}) %collective-permute-start.12) | collective-permute-done | bytes 131104 | tf_op jit(solution)/shard_map/ppermute | solution.py:321
  39.8 0.1 shard_map.112
  39.9 0.1 collective-permute-start.13
  40.0 1.4 %collective-permute-done.10.three_ref = bf16[256,256]{1,0:T(8,128)(2,1)S(1)} collective-permute-done((bf16[256,256]{1,0:T(8,128)(2,1)S(1)}, bf16[256,256]{1,0:T(8,128)(2,1)S(1)}, u32[]{:S(2)}, u32[]{:S(2)}) %collective-permute-start.10) | collective-permute-done | bytes 131104 | tf_op jit(solution)/shard_map/ppermute | solution.py:321
  41.4 0.1 shard_map.111
  41.5 0.2 collective-permute-start.11
  41.7 3.1 %shard_map.109 = (f32[512,256]{1,0:T(8,128)S(1)}, f32[512,256]{1,0:T(8,128)S(1)}, f32[256,256]{1,0:T(8,128)S(1)}, f32[256,256]{1,0:T(8,128)S(1)}) custom-call(bf16[256,256]{1,0:T(8,128)(2,1)S(1)} %get-tuple-element.46.k_ref, bf16[256,256]{1,0:T(8,128)(2,1)} %v_ref.1, bf16[256,1024]{1,0:T(8,128)(2,1)S(1)} %get-tuple-element.35.refs_2_.refs_3_.refs_4_.qr_ref, ...), custom_call_target="tpu_custom_call" | custom-call | flops 1048576 | bytes 11070000 | tf_op jit(solution)/shard_map/pallas_call | solution.py:394
  44.8 1.1 %shard_map.110 = (bf16[256,1024]{1,0:T(8,128)(2,1)}, f32[256,256]{1,0:T(8,128)S(1)}, f32[256,256]{1,0:T(8,128)S(1)}) custom-call(f32[128,256]{1,0:T(8,128)S(1)} %get-tuple-element.33.tables_ref, f32[512,256]{1,0:T(8,128)S(1)} %get-tuple-element.50.refs_0_, f32[512,256]{1,0:T(8,128)S(1)} %get-tuple-element.51.refs_1_, ...), custom_call_target="tpu_custom_call" | custom-call | flops 1048576 | bytes 3690000 | tf_op jit(solution)/shard_map/pallas_call | solution.py:401
  45.9 0.8 %collective-permute-done.13.refs_3_ = bf16[256,256]{1,0:T(8,128)(2,1)S(1)} collective-permute-done((bf16[256,256]{1,0:T(8,128)(2,1)S(1)}, bf16[256,256]{1,0:T(8,128)(2,1)S(1)}, u32[]{:S(2)}, u32[]{:S(2)}) %collective-permute-start.13) | collective-permute-done | bytes 131104 | tf_op jit(solution)/shard_map/ppermute | solution.py:321
  46.7 1.8 %collective-permute-done.11.refs_2_ = bf16[256,256]{1,0:T(8,128)(2,1)S(1)} collective-permute-done((bf16[256,256]{1,0:T(8,128)(2,1)S(1)}, bf16[256,256]{1,0:T(8,128)(2,1)S(1)}, u32[]{:S(2)}, u32[]{:S(2)}) %collective-permute-start.11) | collective-permute-done | bytes 131104 | tf_op jit(solution)/shard_map/ppermute | solution.py:321
  48.5 0.9 %shard_map.113 = (bf16[256,256]{1,0:T(8,128)(2,1)}, bf16[256,256]{1,0:T(8,128)(2,1)}) custom-call(f32[128,256]{1,0:T(8,128)S(1)} %get-tuple-element.33.tables_ref, f32[256,256]{1,0:T(8,128)S(1)} %get-tuple-element.55.refs_0_, f32[256,256]{1,0:T(8,128)S(1)} %get-tuple-element.56.refs_1_, bf16[256,256]{1,0:T(8,128)(2,1)S(1)} %collective-permute-done.11.refs_2_, ...), custom_call_target="tpu_custom_call" | custom-call | flops 1048576 | bytes 3690000 | tf_op jit(solution)/shard_map/pallas_call | solution.py:413
  (9 shorter events, 0.0 us)
Async XLA Ops:
  0.6 9.0 %collective-permute-start = (s32[3,64]{1,0:T(4,128)}, s32[3,64]{1,0:T(4,128)S(1)}, u32[]{:S(2)}, u32[]{:S(2)}) collective-permute-start(s32[3,64]{1,0:T(4,128)} %own_ref.1), channel_id=1, source_target_pairs={{0,1},{1,2},{2,3},{3,0},{4,5},{5,6},{6,7},{7,4},{8,9},{9,10},{10,1... | collective-permute-start | bytes 2312 | tf_op jit(solution)/shard_map/ppermute | solution.py:321
  1.1 8.5 %collective-permute-start.1 = (s32[3,64]{1,0:T(4,128)}, s32[3,64]{1,0:T(4,128)S(1)}, u32[]{:S(2)}, u32[]{:S(2)}) collective-permute-start(s32[3,64]{1,0:T(4,128)} %own_ref.1), channel_id=1, source_target_pairs={{0,2},{1,3},{2,0},{3,1},{4,6},{5,7},{6,4},{7,5},{8,10},{9,11},{10,... | collective-permute-start | bytes 2312 | tf_op jit(solution)/shard_map/ppermute | solution.py:321
  3.7 6.0 %collective-permute-start.2 = (s32[3,64]{1,0:T(4,128)}, s32[3,64]{1,0:T(4,128)S(1)}, u32[]{:S(2)}, u32[]{:S(2)}) collective-permute-start(s32[3,64]{1,0:T(4,128)} %own_ref.1), channel_id=1, source_target_pairs={{0,3},{1,0},{2,1},{3,2},{4,7},{5,4},{6,5},{7,6},{8,11},{9,8},{10,9... | collective-permute-start | bytes 2312 | tf_op jit(solution)/shard_map/ppermute | solution.py:321
  5.1 9.8 %collective-permute-start.4 = (bf16[256,256]{1,0:T(8,128)(2,1)}, bf16[256,256]{1,0:T(8,128)(2,1)S(1)}, u32[]{:S(2)}, u32[]{:S(2)}) collective-permute-start(bf16[256,256]{1,0:T(8,128)(2,1)} %v_ref.1), channel_id=1, source_target_pairs={{0,28},{4,0},{8,4},{12,8},{16,12},{20,16},{24,20},{28,24},{1,29},{... | collective-permute-start | bytes 393224 | tf_op jit(solution)/shard_map/ppermute | solution.py:321
  10.9 5.4 %collective-permute-start.3 = (bf16[256,256]{1,0:T(8,128)(2,1)S(1)}, bf16[256,256]{1,0:T(8,128)(2,1)S(1)}, u32[]{:S(2)}, u32[]{:S(2)}) collective-permute-start(bf16[256,256]{1,0:T(8,128)(2,1)S(1)} %get-tuple-element.46.k_ref), channel_id=1, source_target_pairs={{0,28},{4,0},{8,4},{12,8},{16,12},{20,16},{24,20},{28,24},{1,29},{... | collective-permute-start | bytes 393224 | tf_op jit(solution)/shard_map/ppermute | solution.py:321
  12.5 11.4 %collective-permute-start.5 = (bf16[256,256]{1,0:T(8,128)(2,1)S(1)}, bf16[256,256]{1,0:T(8,128)(2,1)S(1)}, u32[]{:S(2)}, u32[]{:S(2)}) collective-permute-start(bf16[256,256]{1,0:T(8,128)(2,1)S(1)} %get-tuple-element.46.k_ref), channel_id=1, source_target_pairs={{0,20},{4,24},{8,28},{12,0},{16,4},{20,8},{24,12},{28,16},{1,21},{... | collective-permute-start | bytes 393224 | tf_op jit(solution)/shard_map/ppermute | solution.py:321
  14.9 9.0 %collective-permute-start.6 = (bf16[256,256]{1,0:T(8,128)(2,1)S(1)}, bf16[256,256]{1,0:T(8,128)(2,1)S(1)}, u32[]{:S(2)}, u32[]{:S(2)}) collective-permute-start(bf16[256,256]{1,0:T(8,128)(2,1)S(1)} %collective-permute-done.4.refs_1_), channel_id=1, source_target_pairs={{0,24},{4,28},{8,0},{12,4},{16,8},{20,12},{24,16},{28,20},{1,25},{... | collective-permute-start | bytes 393224 | tf_op jit(solution)/shard_map/ppermute | solution.py:321
  16.3 7.5 %copy-start = (bf16[256,256]{1,0:T(8,128)(2,1)S(1)}, bf16[256,256]{1,0:T(8,128)(2,1)}, u32[]{:S(2)}) copy-start(bf16[256,256]{1,0:T(8,128)(2,1)} %v_ref.1) | copy-start | bytes 393220
  17.9 21.9 %collective-permute-start.9 = (bf16[256,512]{1,0:T(8,128)(2,1)S(1)}, bf16[256,512]{1,0:T(8,128)(2,1)S(1)}, u32[]{:S(2)}, u32[]{:S(2)}) collective-permute-start(bf16[256,512]{1,0:T(8,128)(2,1)S(1)} %get-tuple-element.45), channel_id=1, source_target_pairs={{0,4},{4,0},{8,12},{12,8},{16,20},{20,16},{24,28},{28,24},{1,5},{5... | collective-permute-start | bytes 786440 | tf_op jit(solution)/shard_map/ppermute | solution.py:326
  19.8 14.5 %collective-permute-start.7 = (bf16[256,256]{1,0:T(8,128)(2,1)S(1)}, bf16[256,256]{1,0:T(8,128)(2,1)S(1)}, u32[]{:S(2)}, u32[]{:S(2)}) collective-permute-start(bf16[256,256]{1,0:T(8,128)(2,1)S(1)} %get-tuple-element.46.k_ref), channel_id=1, source_target_pairs={{0,24},{4,28},{8,0},{12,4},{16,8},{20,12},{24,16},{28,20},{1,25},{... | collective-permute-start | bytes 393224 | tf_op jit(solution)/shard_map/ppermute | solution.py:321
  23.8 10.5 %collective-permute-start.8 = (bf16[256,256]{1,0:T(8,128)(2,1)S(1)}, bf16[256,256]{1,0:T(8,128)(2,1)S(1)}, u32[]{:S(2)}, u32[]{:S(2)}) collective-permute-start(bf16[256,256]{1,0:T(8,128)(2,1)S(1)} %copy-done), channel_id=1, source_target_pairs={{0,24},{4,28},{8,0},{12,4},{16,8},{20,12},{24,16},{28,20},{1,25},{... | collective-permute-start | bytes 393224 | tf_op jit(solution)/shard_map/ppermute | solution.py:321
  24.8 15.1 %collective-permute-start.12 = (bf16[256,256]{1,0:T(8,128)(2,1)S(1)}, bf16[256,256]{1,0:T(8,128)(2,1)S(1)}, u32[]{:S(2)}, u32[]{:S(2)}) collective-permute-start(bf16[256,256]{1,0:T(8,128)(2,1)S(1)} %get-tuple-element.60), channel_id=1, source_target_pairs={{0,4},{4,8},{8,12},{12,16},{16,20},{20,24},{24,28},{28,0},{1,5},{5... | collective-permute-start | bytes 393224 | tf_op jit(solution)/shard_map/ppermute | solution.py:321
  26.4 15.0 %collective-permute-start.10 = (bf16[256,256]{1,0:T(8,128)(2,1)S(1)}, bf16[256,256]{1,0:T(8,128)(2,1)S(1)}, u32[]{:S(2)}, u32[]{:S(2)}) collective-permute-start(bf16[256,256]{1,0:T(8,128)(2,1)S(1)} %get-tuple-element.58), channel_id=1, source_target_pairs={{0,4},{4,8},{8,12},{12,16},{16,20},{20,24},{24,28},{28,0},{1,5},{5... | collective-permute-start | bytes 393224 | tf_op jit(solution)/shard_map/ppermute | solution.py:321
  39.9 6.8 %collective-permute-start.13 = (bf16[256,256]{1,0:T(8,128)(2,1)S(1)}, bf16[256,256]{1,0:T(8,128)(2,1)S(1)}, u32[]{:S(2)}, u32[]{:S(2)}) collective-permute-start(bf16[256,256]{1,0:T(8,128)(2,1)S(1)} %shard_map.112), channel_id=1, source_target_pairs={{0,8},{4,12},{8,16},{12,20},{16,24},{20,28},{24,0},{28,4},{1,9},{5... | collective-permute-start | bytes 393224 | tf_op jit(solution)/shard_map/ppermute | solution.py:321
  41.5 7.0 %collective-permute-start.11 = (bf16[256,256]{1,0:T(8,128)(2,1)S(1)}, bf16[256,256]{1,0:T(8,128)(2,1)S(1)}, u32[]{:S(2)}, u32[]{:S(2)}) collective-permute-start(bf16[256,256]{1,0:T(8,128)(2,1)S(1)} %shard_map.111), channel_id=1, source_target_pairs={{0,8},{4,12},{8,16},{12,20},{16,24},{20,28},{24,0},{28,4},{1,9},{5... | collective-permute-start | bytes 393224 | tf_op jit(solution)/shard_map/ppermute | solution.py:321

commit v22 on v20

--- a/solution.py
+++ b/solution.py
@@ -258,12 +258,9 @@
 
 def query_kernel(groups, tables_ref, *refs):
     dqt_refs, own_refs = refs[:groups], refs[groups : 2 * groups]
-    swapped_ref, out_ref, *sum_refs = refs[2 * groups :]
-    odd = (lax.axis_index("ctx") & 1) == 1
+    back_refs, (out_ref, *sum_refs) = refs[2 * groups : 3 * groups], refs[3 * groups :]
     for g in range(groups):
-        sum_refs[g][...] = own_refs[g][...] + jnp.where(
-            odd, swapped_ref[:, 2 * HEAD * g : 2 * HEAD * (g + 1)].astype(F32), 0.0
-        )
+        sum_refs[g][...] = own_refs[g][...] + back_refs[g][...].astype(F32)
     cosine_t = tables_ref[:HALF, :] * ROOT_SCALE
     sine_t = tables_ref[HALF:, :] * ROOT_SCALE
     size = dqt_refs[0].shape[0] // HEAD
@@ -277,11 +274,8 @@
             out_ref[:, pl.ds((g * size + j) * HEAD, HEAD)] = turned.T.astype(BF16)
 
 
-def add_kernel(g, two_ref, swapped_ref, three_ref, sum_ref):
-    even = (lax.axis_index("ctx") & 1) == 0
-    total = two_ref[...].astype(F32) + three_ref[...].astype(F32)
-    swapped = swapped_ref[:, 2 * HEAD * g : 2 * HEAD * (g + 1)].astype(F32)
-    sum_ref[...] = (total + jnp.where(even, swapped, 0.0)).astype(BF16)
+def add_kernel(a_ref, b_ref, sum_ref):
+    sum_ref[...] = (a_ref[...].astype(F32) + b_ref[...].astype(F32)).astype(BF16)
 
 
 def final_kernel(groups, tables_ref, *refs):
@@ -319,11 +313,6 @@
     count = lax.axis_size(axis)
     pairs = [(source, (source + steps) % count) for source in range(count)]
     return lax.ppermute(value, axis, pairs)
-
-
-def exchanged(value):
-    count = lax.axis_size("ctx")
-    return lax.ppermute(value, "ctx", [(source, source ^ 1) for source in range(count)])
 
 
 def shards(q, k, v, do, at, lse, positions, span_map):
@@ -384,13 +373,12 @@
             dqs[g] = results[i]
         return results[count:]
 
-    (part1,) = hop(1, every, k1, v1, joined=True)
-    swapped = exchanged(part1)
-    kr2, v_far, _ = lax.optimization_barrier((kr, v, part1))
+    parts1 = hop(1, every, k1, v1)
+    kr2, v_far, _ = lax.optimization_barrier((kr, v, parts1[0]))
     k2 = shifted(kr2, -2)
     v2 = shifted(v_far, -2)
-    moved = [shifted(*hop(3, (g,), k3, v3), 1) for g in every]
-    parts2 = hop(2, every, k2, v2)
+    moved = [shifted(*hop(3, (g,), k3, v3), 2) for g in every]
+    back2 = [shifted(part, 2) for part in hop(2, every, k2, v2)]
     results = call(
         functools.partial(own_kernel, groups),
         [dq_out] * groups + [((rows, 2 * HEAD), F32)] * groups,
@@ -401,14 +389,12 @@
     dq, *owns = call(
         functools.partial(query_kernel, groups),
         [((rows, wide_q), BF16)] + [((rows, 2 * HEAD), F32)] * groups,
-        [VMEM] * (2 + 2 * groups),
-    )(tables, *dqs, *owns, swapped)
+        [VMEM] * (1 + 3 * groups),
+    )(tables, *dqs, *owns, *back2)
     home = []
     for g in every:
-        (total,) = call(functools.partial(add_kernel, g), [part_out], [VMEM] * 3)(
-            parts2[g], swapped, moved[g]
-        )
-        home.append(shifted(total, 2))
+        (total,) = call(add_kernel, [part_out], [VMEM] * 2)(parts1[g], moved[g])
+        home.append(shifted(total, 1))
 
     dk, dv = call(
         functools.partial(final_kernel, groups),

time: 45.4 us -> 53.1 us (1.17)
  waiting for transfers between devices: 5.71 us -> 17.6 us
  starting transfers between devices: 24.8 us -> 20.7 us
    ppermute x13 -> x15, waiting for transfers between devices: 5.71 us -> 17.6 us  [shifted(): return lax.ppermute(value, axis, pairs)]
    ppermute x1 -> x0, starting transfers between devices: 4.36 us -> none  [exchanged(): lax.ppermute(value, 'ctx', [(source, source ^ 1) for source in range(coun...]
    ppermute x13 -> x15, starting transfers between devices: 20.5 us -> 20.7 us  [shifted(): return lax.ppermute(value, axis, pairs)]
  transfers between devices with their start and end apart: 14 -> 15, of which waited for: 5 -> 7; matrix products, arithmetic and copies ran while one was open for 0% -> 0% of each run, Pallas kernels for 29% -> 25%
where the time goes in v22:
time: 53.1 us; the launch traced here: 52.9 us
  starting transfers between devices  20.7 us (39%)
  waiting for transfers between devices  17.6 us (33%)
  Pallas kernels  13.9 us (26%)
  between operations  0.75 us (1%)
    ppermute x15, starting transfers between devices, shifted(): return lax.ppermute(value, axis, pairs)  20.7 us
    ppermute x15, waiting for transfers between devices, shifted(): return lax.ppermute(value, axis, pairs)  17.6 us
    pallas_call x4, Pallas kernels, hop(): call(functools.partial(hop_kernel, step, wanted, started, joined), [dq_ou...  5.12 us
    pallas_call x1, Pallas kernels, shards(): call(functools.partial(own_kernel, groups), [dq_out] * groups + [((rows,...  3.05 us
    pallas_call x1, Pallas kernels, shards(): call(functools.partial(prep_kernel, groups), [((rows, wide_q), BF16)] * 2...  2.41 us
    pallas_call x1, Pallas kernels, shards(): call(key_kernel, [((rows, wide_k), BF16), ((HEAD, rows), F32)], [VMEM] * 5)  1.24 us
    pallas_call x1, Pallas kernels, shards(): call(functools.partial(query_kernel, groups), [((rows, wide_q), BF16)] +...  1.1 us
  transfers between devices with their start and end apart: 15, of which 7 were waited for; matrix products, arithmetic and copies ran while one was open for 0% of the time, Pallas kernels for 25%

profile of v22, /device:TPU:0, one launch (start us, length us, event | category | flops | bytes accessed | tf_op | source)
XLA Modules:
  0.0 52.9 jit_solution(9523846843729582558)
XLA Ops:
  0.6 3.0 %collective-permute-start.1 = (s32[3,64]{1,0:T(4,128)}, s32[3,64]{1,0:T(4,128)S(1)}, u32[]{:S(2)}, u32[]{:S(2)}) collective-permute-start(s32[3,64]{1,0:T(4,128)} %own_ref.1), channel_id=1, source_target_pairs={{0,2},{1,3},{2,0},{3,1},{4,6},{5,7},{6,4},{7,5},{8,10},{9,11},{10,... | collective-permute-start | bytes 2312 | tf_op jit(solution)/shard_map/ppermute | solution.py:315
  3.6 0.0 collective-permute-start
  3.6 1.7 %collective-permute-start.2 = (s32[3,64]{1,0:T(4,128)}, s32[3,64]{1,0:T(4,128)S(1)}, u32[]{:S(2)}, u32[]{:S(2)}) collective-permute-start(s32[3,64]{1,0:T(4,128)} %own_ref.1), channel_id=1, source_target_pairs={{0,3},{1,0},{2,1},{3,2},{4,7},{5,4},{6,5},{7,6},{8,11},{9,8},{10,9... | collective-permute-start | bytes 2312 | tf_op jit(solution)/shard_map/ppermute | solution.py:315
  5.4 4.6 %collective-permute-start.4 = (bf16[256,256]{1,0:T(8,128)(2,1)}, bf16[256,256]{1,0:T(8,128)(2,1)S(1)}, u32[]{:S(2)}, u32[]{:S(2)}) collective-permute-start(bf16[256,256]{1,0:T(8,128)(2,1)} %v_ref.1), channel_id=1, source_target_pairs={{0,28},{4,0},{8,4},{12,8},{16,12},{20,16},{24,20},{28,24},{1,29},{... | collective-permute-start | bytes 393224 | tf_op jit(solution)/shard_map/ppermute | solution.py:315
  9.9 0.0 collective-permute-done.1.p2_ref
  10.0 1.2 %shard_map.103 = (bf16[256,256]{1,0:T(8,128)(2,1)S(1)}, f32[128,256]{1,0:T(8,128)S(1)}) custom-call(s32[3,64]{1,0:T(4,128)} %own_ref.1, s32[3,64]{1,0:T(4,128)S(1)} %collective-permute-done.p1_ref, s32[3,64]{1,0:T(4,128)S(1)} %collective-permute-done.1.p2_ref, s32[3,64]{1,0:T(4,128)S(1)} %collective-permute-done.2.p3_ref, bf16[256,256]{1,0:T(8,128)(2,1)} %k_ref.1), custom_call_target="tpu_custom_call" | custom-call | flops 1048576 | bytes 3690000 | tf_op jit(solution)/shard_map/pallas_call | solution.py:336
  11.2 1.6 %collective-permute-start.3 = (bf16[256,256]{1,0:T(8,128)(2,1)S(1)}, bf16[256,256]{1,0:T(8,128)(2,1)S(1)}, u32[]{:S(2)}, u32[]{:S(2)}) collective-permute-start(bf16[256,256]{1,0:T(8,128)(2,1)S(1)} %get-tuple-element.47.k_ref), channel_id=1, source_target_pairs={{0,28},{4,0},{8,4},{12,8},{16,12},{20,16},{24,20},{28,24},{1,29},{... | collective-permute-start | bytes 393224 | tf_op jit(solution)/shard_map/ppermute | solution.py:315
  12.7 2.4 %shard_map.104 = (bf16[256,1024]{1,0:T(8,128)(2,1)S(1)}, bf16[256,1024]{1,0:T(8,128)(2,1)S(1)}, f32[8,256]{1,0:T(8,128)S(1)}, f32[8,256]{1,0:T(8,128)S(1)}, s32[8,128]{1,0:T(8,128)S(1)}) custom-call(s32[8]{0:T(128)} %span_ref.1, f32[128,256]{1,0:T(8,128)S(1)} %get-tuple-element.34.tables_ref, f32[8,256]{1,0:T(8,128)} %lse_hbm.1, bf16[256,1024]{1,0:T(8,128)(2,1)} %q_hbm.1, ...), custom_call_target="tpu_custom_call" | custom-call | flops 1048576 | bytes 7380000 | tf_op jit(solution)/shard_map/pallas_call | solution.py:340
  15.2 0.5 collective-permute-start.6
  15.7 0.7 %collective-permute-done.3.refs_0_ = bf16[256,256]{1,0:T(8,128)(2,1)S(1)} collective-permute-done((bf16[256,256]{1,0:T(8,128)(2,1)S(1)}, bf16[256,256]{1,0:T(8,128)(2,1)S(1)}, u32[]{:S(2)}, u32[]{:S(2)}) %collective-permute-start.3) | collective-permute-done | bytes 131104 | tf_op jit(solution)/shard_map/ppermute | solution.py:315
  16.4 1.4 %collective-permute-start.5 = (bf16[256,256]{1,0:T(8,128)(2,1)S(1)}, bf16[256,256]{1,0:T(8,128)(2,1)S(1)}, u32[]{:S(2)}, u32[]{:S(2)}) collective-permute-start(bf16[256,256]{1,0:T(8,128)(2,1)S(1)} %collective-permute-done.3.refs_0_), channel_id=1, source_target_pairs={{0,24},{4,28},{8,0},{12,4},{16,8},{20,12},{24,16},{28,20},{1,25},{... | collective-permute-start | bytes 393224 | tf_op jit(solution)/shard_map/ppermute | solution.py:315
  17.8 1.6 %shard_map.105 = (f32[512,256]{1,0:T(8,128)S(1)}, f32[512,256]{1,0:T(8,128)S(1)}, bf16[256,256]{1,0:T(8,128)(2,1)S(1)}, bf16[256,256]{1,0:T(8,128)(2,1)S(1)}) custom-call(bf16[256,256]{1,0:T(8,128)(2,1)S(1)} %collective-permute-done.3.refs_0_, bf16[256,256]{1,0:T(8,128)(2,1)S(1)} %collective-permute-done.4.refs_1_, ...), custom_call_target="tpu_custom_call" | custom-call | flops 1048576 | bytes 7380000 | tf_op jit(solution)/shard_map/pallas_call | solution.py:363
  19.4 0.5 collective-permute-start.7
  19.9 1.9 %collective-permute-start.8 = (bf16[256,256]{1,0:T(8,128)(2,1)S(1)}, bf16[256,256]{1,0:T(8,128)(2,1)S(1)}, u32[]{:S(2)}, u32[]{:S(2)}) collective-permute-start(bf16[256,256]{1,0:T(8,128)(2,1)S(1)} %copy-done), channel_id=1, source_target_pairs={{0,24},{4,28},{8,0},{12,4},{16,8},{20,12},{24,16},{28,20},{1,25},{... | collective-permute-start | bytes 393224 | tf_op jit(solution)/shard_map/ppermute | solution.py:315
  21.9 2.5 %collective-permute-done.5.refs_1_ = bf16[256,256]{1,0:T(8,128)(2,1)S(1)} collective-permute-done((bf16[256,256]{1,0:T(8,128)(2,1)S(1)}, bf16[256,256]{1,0:T(8,128)(2,1)S(1)}, u32[]{:S(2)}, u32[]{:S(2)}) %collective-permute-start.5) | collective-permute-done | bytes 131104 | tf_op jit(solution)/shard_map/ppermute | solution.py:315
  24.4 0.9 %shard_map.106 = (f32[512,256]{1,0:T(8,128)S(1)}, bf16[256,256]{1,0:T(8,128)(2,1)S(1)}) custom-call(f32[512,256]{1,0:T(8,128)S(1)} %get-tuple-element.42.refs_0_, bf16[256,256]{1,0:T(8,128)(2,1)S(1)} %collective-permute-done.5.refs_1_, bf16[256,256]{1,0:T(8,128)(2,1)S(1)} %collective-permute-done.6.refs_2_, ...), custom_call_target="tpu_custom_call" | custom-call | flops 1048576 | bytes 3690000 | tf_op jit(solution)/shard_map/pallas_call | solution.py:363
  25.3 0.1 collective-permute-start.11
  25.3 0.9 %shard_map.107 = (f32[512,256]{1,0:T(8,128)S(1)}, bf16[256,256]{1,0:T(8,128)(2,1)S(1)}) custom-call(f32[512,256]{1,0:T(8,128)S(1)} %get-tuple-element.44.refs_0_, bf16[256,256]{1,0:T(8,128)(2,1)S(1)} %collective-permute-done.5.refs_1_, bf16[256,256]{1,0:T(8,128)(2,1)S(1)} %collective-permute-done.6.refs_2_, ...), custom_call_target="tpu_custom_call" | custom-call | flops 1048576 | bytes 3690000 | tf_op jit(solution)/shard_map/pallas_call | solution.py:363
  26.3 0.1 collective-permute-start.13
  26.3 0.8 %collective-permute-done.7.refs_2_ = bf16[256,256]{1,0:T(8,128)(2,1)S(1)} collective-permute-done((bf16[256,256]{1,0:T(8,128)(2,1)S(1)}, bf16[256,256]{1,0:T(8,128)(2,1)S(1)}, u32[]{:S(2)}, u32[]{:S(2)}) %collective-permute-start.7) | collective-permute-done | bytes 131104 | tf_op jit(solution)/shard_map/ppermute | solution.py:315
  27.2 7.8 %collective-permute-done.8.refs_3_ = bf16[256,256]{1,0:T(8,128)(2,1)S(1)} collective-permute-done((bf16[256,256]{1,0:T(8,128)(2,1)S(1)}, bf16[256,256]{1,0:T(8,128)(2,1)S(1)}, u32[]{:S(2)}, u32[]{:S(2)}) %collective-permute-start.8) | collective-permute-done | bytes 131104 | tf_op jit(solution)/shard_map/ppermute | solution.py:315
  35.0 1.6 %shard_map.108 = (f32[512,256]{1,0:T(8,128)S(1)}, f32[512,256]{1,0:T(8,128)S(1)}, bf16[256,256]{1,0:T(8,128)(2,1)S(1)}, bf16[256,256]{1,0:T(8,128)(2,1)S(1)}) custom-call(f32[512,256]{1,0:T(8,128)S(1)} %get-tuple-element.43.refs_0_, f32[512,256]{1,0:T(8,128)S(1)} %get-tuple-element.45.refs_1_, bf16[256,256]{1,0:T(8,128)(2,1)S(1)} %collective-permute-done.7.refs_2_, ...), custom_call_target="tpu_custom_call" | custom-call | flops 1048576 | bytes 7380000 | tf_op jit(solution)/shard_map/pallas_call | solution.py:363
  36.7 0.1 collective-permute-start.9
  36.7 0.1 collective-permute-start.10
  36.8 5.0 %collective-permute-start.12 = (bf16[256,256]{1,0:T(8,128)(2,1)S(1)}, bf16[256,256]{1,0:T(8,128)(2,1)S(1)}, u32[]{:S(2)}, u32[]{:S(2)}) collective-permute-start(bf16[256,256]{1,0:T(8,128)(2,1)S(1)} %shard_map.111), channel_id=1, source_target_pairs={{0,4},{4,8},{8,12},{12,16},{16,20},{20,24},{24,28},{28,0},{1,5},{5... | collective-permute-start | bytes 393224 | tf_op jit(solution)/shard_map/ppermute | solution.py:315
  41.8 0.3 collective-permute-start.14
  42.1 3.0 %shard_map.109 = (f32[512,256]{1,0:T(8,128)S(1)}, f32[512,256]{1,0:T(8,128)S(1)}, f32[256,256]{1,0:T(8,128)S(1)}, f32[256,256]{1,0:T(8,128)S(1)}) custom-call(bf16[256,256]{1,0:T(8,128)(2,1)S(1)} %get-tuple-element.47.k_ref, bf16[256,256]{1,0:T(8,128)(2,1)} %v_ref.1, bf16[256,1024]{1,0:T(8,128)(2,1)S(1)} %get-tuple-element.36.refs_2_.refs_3_.refs_4_.qr_ref, ...), custom_call_target="tpu_custom_call" | custom-call | flops 1048576 | bytes 11070000 | tf_op jit(solution)/shard_map/pallas_call | solution.py:382
  45.2 1.1 %collective-permute-done.10.refs_5_ = bf16[256,256]{1,0:T(8,128)(2,1)S(1)} collective-permute-done((bf16[256,256]{1,0:T(8,128)(2,1)S(1)}, bf16[256,256]{1,0:T(8,128)(2,1)S(1)}, u32[]{:S(2)}, u32[]{:S(2)}) %collective-permute-start.10) | collective-permute-done | bytes 131104 | tf_op jit(solution)/shard_map/ppermute | solution.py:315
  46.2 1.1 %shard_map.110 = (bf16[256,1024]{1,0:T(8,128)(2,1)}, f32[256,256]{1,0:T(8,128)S(1)}, f32[256,256]{1,0:T(8,128)S(1)}) custom-call(f32[128,256]{1,0:T(8,128)S(1)} %get-tuple-element.34.tables_ref, f32[512,256]{1,0:T(8,128)S(1)} %get-tuple-element.51.refs_0_, f32[512,256]{1,0:T(8,128)S(1)} %get-tuple-element.52.refs_1_, ...), custom_call_target="tpu_custom_call" | custom-call | flops 1048576 | bytes 3690000 | tf_op jit(solution)/shard_map/pallas_call | solution.py:389
  47.3 3.3 %collective-permute-done.12.refs_2_ = bf16[256,256]{1,0:T(8,128)(2,1)S(1)} collective-permute-done((bf16[256,256]{1,0:T(8,128)(2,1)S(1)}, bf16[256,256]{1,0:T(8,128)(2,1)S(1)}, u32[]{:S(2)}, u32[]{:S(2)}) %collective-permute-start.12) | collective-permute-done | bytes 131104 | tf_op jit(solution)/shard_map/ppermute | solution.py:315
  50.6 1.4 %collective-permute-done.14.refs_3_ = bf16[256,256]{1,0:T(8,128)(2,1)S(1)} collective-permute-done((bf16[256,256]{1,0:T(8,128)(2,1)S(1)}, bf16[256,256]{1,0:T(8,128)(2,1)S(1)}, u32[]{:S(2)}, u32[]{:S(2)}) %collective-permute-start.14) | collective-permute-done | bytes 131104 | tf_op jit(solution)/shard_map/ppermute | solution.py:315
  52.0 0.9 %shard_map.113 = (bf16[256,256]{1,0:T(8,128)(2,1)}, bf16[256,256]{1,0:T(8,128)(2,1)}) custom-call(f32[128,256]{1,0:T(8,128)S(1)} %get-tuple-element.34.tables_ref, f32[256,256]{1,0:T(8,128)S(1)} %get-tuple-element.58.refs_0_, f32[256,256]{1,0:T(8,128)S(1)} %get-tuple-element.59.refs_1_, bf16[256,256]{1,0:T(8,128)(2,1)S(1)} %collective-permute-done.12.refs_2_, ...), custom_call_target="tpu_custom_call" | custom-call | flops 1048576 | bytes 3690000 | tf_op jit(solution)/shard_map/pallas_call | solution.py:399
  (11 shorter events, 0.1 us)
Async XLA Ops:
  0.6 9.3 %collective-permute-start.1 = (s32[3,64]{1,0:T(4,128)}, s32[3,64]{1,0:T(4,128)S(1)}, u32[]{:S(2)}, u32[]{:S(2)}) collective-permute-start(s32[3,64]{1,0:T(4,128)} %own_ref.1), channel_id=1, source_target_pairs={{0,2},{1,3},{2,0},{3,1},{4,6},{5,7},{6,4},{7,5},{8,10},{9,11},{10,... | collective-permute-start | bytes 2312 | tf_op jit(solution)/shard_map/ppermute | solution.py:315
  3.6 6.3 %collective-permute-start = (s32[3,64]{1,0:T(4,128)}, s32[3,64]{1,0:T(4,128)S(1)}, u32[]{:S(2)}, u32[]{:S(2)}) collective-permute-start(s32[3,64]{1,0:T(4,128)} %own_ref.1), channel_id=1, source_target_pairs={{0,1},{1,2},{2,3},{3,0},{4,5},{5,6},{6,7},{7,4},{8,9},{9,10},{10,1... | collective-permute-start | bytes 2312 | tf_op jit(solution)/shard_map/ppermute | solution.py:315
  3.6 6.3 %collective-permute-start.2 = (s32[3,64]{1,0:T(4,128)}, s32[3,64]{1,0:T(4,128)S(1)}, u32[]{:S(2)}, u32[]{:S(2)}) collective-permute-start(s32[3,64]{1,0:T(4,128)} %own_ref.1), channel_id=1, source_target_pairs={{0,3},{1,0},{2,1},{3,2},{4,7},{5,4},{6,5},{7,6},{8,11},{9,8},{10,9... | collective-permute-start | bytes 2312 | tf_op jit(solution)/shard_map/ppermute | solution.py:315
  5.4 9.8 %collective-permute-start.4 = (bf16[256,256]{1,0:T(8,128)(2,1)}, bf16[256,256]{1,0:T(8,128)(2,1)S(1)}, u32[]{:S(2)}, u32[]{:S(2)}) collective-permute-start(bf16[256,256]{1,0:T(8,128)(2,1)} %v_ref.1), channel_id=1, source_target_pairs={{0,28},{4,0},{8,4},{12,8},{16,12},{20,16},{24,20},{28,24},{1,29},{... | collective-permute-start | bytes 393224 | tf_op jit(solution)/shard_map/ppermute | solution.py:315
  11.2 5.2 %collective-permute-start.3 = (bf16[256,256]{1,0:T(8,128)(2,1)S(1)}, bf16[256,256]{1,0:T(8,128)(2,1)S(1)}, u32[]{:S(2)}, u32[]{:S(2)}) collective-permute-start(bf16[256,256]{1,0:T(8,128)(2,1)S(1)} %get-tuple-element.47.k_ref), channel_id=1, source_target_pairs={{0,28},{4,0},{8,4},{12,8},{16,12},{20,16},{24,20},{28,24},{1,29},{... | collective-permute-start | bytes 393224 | tf_op jit(solution)/shard_map/ppermute | solution.py:315
  15.2 6.7 %collective-permute-start.6 = (bf16[256,256]{1,0:T(8,128)(2,1)S(1)}, bf16[256,256]{1,0:T(8,128)(2,1)S(1)}, u32[]{:S(2)}, u32[]{:S(2)}) collective-permute-start(bf16[256,256]{1,0:T(8,128)(2,1)S(1)} %collective-permute-done.4.refs_1_), channel_id=1, source_target_pairs={{0,24},{4,28},{8,0},{12,4},{16,8},{20,12},{24,16},{28,20},{1,25},{... | collective-permute-start | bytes 393224 | tf_op jit(solution)/shard_map/ppermute | solution.py:315
  16.4 8.0 %collective-permute-start.5 = (bf16[256,256]{1,0:T(8,128)(2,1)S(1)}, bf16[256,256]{1,0:T(8,128)(2,1)S(1)}, u32[]{:S(2)}, u32[]{:S(2)}) collective-permute-start(bf16[256,256]{1,0:T(8,128)(2,1)S(1)} %collective-permute-done.3.refs_0_), channel_id=1, source_target_pairs={{0,24},{4,28},{8,0},{12,4},{16,8},{20,12},{24,16},{28,20},{1,25},{... | collective-permute-start | bytes 393224 | tf_op jit(solution)/shard_map/ppermute | solution.py:315
  17.8 2.1 %copy-start = (bf16[256,256]{1,0:T(8,128)(2,1)S(1)}, bf16[256,256]{1,0:T(8,128)(2,1)}, u32[]{:S(2)}) copy-start(bf16[256,256]{1,0:T(8,128)(2,1)} %v_ref.1) | copy-start | bytes 393220
  19.4 7.7 %collective-permute-start.7 = (bf16[256,256]{1,0:T(8,128)(2,1)S(1)}, bf16[256,256]{1,0:T(8,128)(2,1)S(1)}, u32[]{:S(2)}, u32[]{:S(2)}) collective-permute-start(bf16[256,256]{1,0:T(8,128)(2,1)S(1)} %get-tuple-element.47.k_ref), channel_id=1, source_target_pairs={{0,24},{4,28},{8,0},{12,4},{16,8},{20,12},{24,16},{28,20},{1,25},{... | collective-permute-start | bytes 393224 | tf_op jit(solution)/shard_map/ppermute | solution.py:315
  19.9 15.1 %collective-permute-start.8 = (bf16[256,256]{1,0:T(8,128)(2,1)S(1)}, bf16[256,256]{1,0:T(8,128)(2,1)S(1)}, u32[]{:S(2)}, u32[]{:S(2)}) collective-permute-start(bf16[256,256]{1,0:T(8,128)(2,1)S(1)} %copy-done), channel_id=1, source_target_pairs={{0,24},{4,28},{8,0},{12,4},{16,8},{20,12},{24,16},{28,20},{1,25},{... | collective-permute-start | bytes 393224 | tf_op jit(solution)/shard_map/ppermute | solution.py:315
  25.3 11.5 %collective-permute-start.11 = (bf16[256,256]{1,0:T(8,128)(2,1)S(1)}, bf16[256,256]{1,0:T(8,128)(2,1)S(1)}, u32[]{:S(2)}, u32[]{:S(2)}) collective-permute-start(bf16[256,256]{1,0:T(8,128)(2,1)S(1)} %get-tuple-element.60), channel_id=1, source_target_pairs={{0,8},{4,12},{8,16},{12,20},{16,24},{20,28},{24,0},{28,4},{1,9},{5... | collective-permute-start | bytes 393224 | tf_op jit(solution)/shard_map/ppermute | solution.py:315
  26.3 15.5 %collective-permute-start.13 = (bf16[256,256]{1,0:T(8,128)(2,1)S(1)}, bf16[256,256]{1,0:T(8,128)(2,1)S(1)}, u32[]{:S(2)}, u32[]{:S(2)}) collective-permute-start(bf16[256,256]{1,0:T(8,128)(2,1)S(1)} %get-tuple-element.62), channel_id=1, source_target_pairs={{0,8},{4,12},{8,16},{12,20},{16,24},{20,28},{24,0},{28,4},{1,9},{5... | collective-permute-start | bytes 393224 | tf_op jit(solution)/shard_map/ppermute | solution.py:315
  36.7 8.5 %collective-permute-start.9 = (bf16[256,256]{1,0:T(8,128)(2,1)S(1)}, bf16[256,256]{1,0:T(8,128)(2,1)S(1)}, u32[]{:S(2)}, u32[]{:S(2)}) collective-permute-start(bf16[256,256]{1,0:T(8,128)(2,1)S(1)} %get-tuple-element.55), channel_id=1, source_target_pairs={{0,8},{4,12},{8,16},{12,20},{16,24},{20,28},{24,0},{28,4},{1,9},{5... | collective-permute-start | bytes 393224 | tf_op jit(solution)/shard_map/ppermute | solution.py:315
  36.7 9.5 %collective-permute-start.10 = (bf16[256,256]{1,0:T(8,128)(2,1)S(1)}, bf16[256,256]{1,0:T(8,128)(2,1)S(1)}, u32[]{:S(2)}, u32[]{:S(2)}) collective-permute-start(bf16[256,256]{1,0:T(8,128)(2,1)S(1)} %get-tuple-element.56), channel_id=1, source_target_pairs={{0,8},{4,12},{8,16},{12,20},{16,24},{20,28},{24,0},{28,4},{1,9},{5... | collective-permute-start | bytes 393224 | tf_op jit(solution)/shard_map/ppermute | solution.py:315
  36.8 13.8 %collective-permute-start.12 = (bf16[256,256]{1,0:T(8,128)(2,1)S(1)}, bf16[256,256]{1,0:T(8,128)(2,1)S(1)}, u32[]{:S(2)}, u32[]{:S(2)}) collective-permute-start(bf16[256,256]{1,0:T(8,128)(2,1)S(1)} %shard_map.111), channel_id=1, source_target_pairs={{0,4},{4,8},{8,12},{12,16},{16,20},{20,24},{24,28},{28,0},{1,5},{5... | collective-permute-start | bytes 393224 | tf_op jit(solution)/shard_map/ppermute | solution.py:315
  41.8 10.2 %collective-permute-start.14 = (bf16[256,256]{1,0:T(8,128)(2,1)S(1)}, bf16[256,256]{1,0:T(8,128)(2,1)S(1)}, u32[]{:S(2)}, u32[]{:S(2)}) collective-permute-start(bf16[256,256]{1,0:T(8,128)(2,1)S(1)} %shard_map.112), channel_id=1, source_target_pairs={{0,4},{4,8},{8,12},{12,16},{16,20},{20,24},{24,28},{28,0},{1,5},{5... | collective-permute-start | bytes 393224 | tf_op jit(solution)/shard_map/ppermute | solution.py:315

commit v23 on v22

--- a/solution.py
+++ b/solution.py
@@ -351,6 +351,8 @@
     )(span_map, tables, lse, q, do, at)
     v1, _ = lax.optimization_barrier((v1, shared[3]))
     v3 = shifted(v1, -2)
+    v_far, _ = lax.optimization_barrier((v, shared[3]))
+    v2 = shifted(v_far, -2)
     k3 = shifted(k1, -2)
     dqs = []
     dq_out = ((wide_q // groups, rows), F32)
@@ -374,9 +376,8 @@
         return results[count:]
 
     parts1 = hop(1, every, k1, v1)
-    kr2, v_far, _ = lax.optimization_barrier((kr, v, parts1[0]))
+    kr2, _ = lax.optimization_barrier((kr, parts1[0]))
     k2 = shifted(kr2, -2)
-    v2 = shifted(v_far, -2)
     moved = [shifted(*hop(3, (g,), k3, v3), 2) for g in every]
     back2 = [shifted(part, 2) for part in hop(2, every, k2, v2)]
     results = call(

time: 53.1 us -> 48.5 us (0.913)
  starting transfers between devices: 20.7 us -> 17 us
  waiting for transfers between devices: 17.6 us -> 16.6 us
    ppermute x15, starting transfers between devices: 20.7 us -> 17 us  [shifted(): return lax.ppermute(value, axis, pairs)]
    ppermute x15, waiting for transfers between devices: 17.6 us -> 16.6 us  [shifted(): return lax.ppermute(value, axis, pairs)]
  transfers between devices with their start and end apart: 15 -> 15, of which waited for: 7 -> 6; matrix products, arithmetic and copies ran while one was open for 0% -> 0% of each run, Pallas kernels for 25% -> 27%
where the time goes in v23:
time: 48.5 us; the launch traced here: 48.4 us
  starting transfers between devices  17 us (35%)
  waiting for transfers between devices  16.6 us (34%)
  Pallas kernels  14 us (29%)
  between operations  0.77 us (2%)
    ppermute x15, starting transfers between devices, shifted(): return lax.ppermute(value, axis, pairs)  17 us
    ppermute x15, waiting for transfers between devices, shifted(): return lax.ppermute(value, axis, pairs)  16.6 us
    pallas_call x4, Pallas kernels, hop(): call(functools.partial(hop_kernel, step, wanted, started, joined), [dq_ou...  5.13 us
    pallas_call x1, Pallas kernels, shards(): call(functools.partial(own_kernel, groups), [dq_out] * groups + [((rows,...  3.05 us
    pallas_call x1, Pallas kernels, shards(): call(functools.partial(prep_kernel, groups), [((rows, wide_q), BF16)] * 2...  2.55 us
    pallas_call x1, Pallas kernels, shards(): call(key_kernel, [((rows, wide_k), BF16), ((HEAD, rows), F32)], [VMEM] * 5)  1.24 us
    pallas_call x1, Pallas kernels, shards(): call(functools.partial(query_kernel, groups), [((rows, wide_q), BF16)] +...  1.1 us
  transfers between devices with their start and end apart: 15, of which 6 were waited for; matrix products, arithmetic and copies ran while one was open for 0% of the time, Pallas kernels for 27%

profile of v23, /device:TPU:0, one launch (start us, length us, event | category | flops | bytes accessed | tf_op | source)
XLA Modules:
  0.0 48.4 jit_solution(9217854903375666569)
XLA Ops:
  0.6 3.0 %collective-permute-start.1 = (s32[3,64]{1,0:T(4,128)}, s32[3,64]{1,0:T(4,128)S(1)}, u32[]{:S(2)}, u32[]{:S(2)}) collective-permute-start(s32[3,64]{1,0:T(4,128)} %own_ref.1), channel_id=1, source_target_pairs={{0,2},{1,3},{2,0},{3,1},{4,6},{5,7},{6,4},{7,5},{8,10},{9,11},{10,... | collective-permute-start | bytes 2312 | tf_op jit(solution)/shard_map/ppermute | solution.py:315
  3.6 0.0 collective-permute-start
  3.6 1.7 %collective-permute-start.2 = (s32[3,64]{1,0:T(4,128)}, s32[3,64]{1,0:T(4,128)S(1)}, u32[]{:S(2)}, u32[]{:S(2)}) collective-permute-start(s32[3,64]{1,0:T(4,128)} %own_ref.1), channel_id=1, source_target_pairs={{0,3},{1,0},{2,1},{3,2},{4,7},{5,4},{6,5},{7,6},{8,11},{9,8},{10,9... | collective-permute-start | bytes 2312 | tf_op jit(solution)/shard_map/ppermute | solution.py:315
  5.4 4.6 %collective-permute-start.4 = (bf16[256,256]{1,0:T(8,128)(2,1)}, bf16[256,256]{1,0:T(8,128)(2,1)S(1)}, u32[]{:S(2)}, u32[]{:S(2)}) collective-permute-start(bf16[256,256]{1,0:T(8,128)(2,1)} %v_ref.1), channel_id=1, source_target_pairs={{0,28},{4,0},{8,4},{12,8},{16,12},{20,16},{24,20},{28,24},{1,29},{... | collective-permute-start | bytes 393224 | tf_op jit(solution)/shard_map/ppermute | solution.py:315
  9.9 0.0 collective-permute-done.1.p2_ref
  10.0 1.2 %shard_map.103 = (bf16[256,256]{1,0:T(8,128)(2,1)S(1)}, f32[128,256]{1,0:T(8,128)S(1)}) custom-call(s32[3,64]{1,0:T(4,128)} %own_ref.1, s32[3,64]{1,0:T(4,128)S(1)} %collective-permute-done.p1_ref, s32[3,64]{1,0:T(4,128)S(1)} %collective-permute-done.1.p2_ref, s32[3,64]{1,0:T(4,128)S(1)} %collective-permute-done.2.p3_ref, bf16[256,256]{1,0:T(8,128)(2,1)} %k_ref.1), custom_call_target="tpu_custom_call" | custom-call | flops 1048576 | bytes 3690000 | tf_op jit(solution)/shard_map/pallas_call | solution.py:336
  11.2 1.6 %collective-permute-start.3 = (bf16[256,256]{1,0:T(8,128)(2,1)S(1)}, bf16[256,256]{1,0:T(8,128)(2,1)S(1)}, u32[]{:S(2)}, u32[]{:S(2)}) collective-permute-start(bf16[256,256]{1,0:T(8,128)(2,1)S(1)} %get-tuple-element.47.k_ref), channel_id=1, source_target_pairs={{0,28},{4,0},{8,4},{12,8},{16,12},{20,16},{24,20},{28,24},{1,29},{... | collective-permute-start | bytes 393224 | tf_op jit(solution)/shard_map/ppermute | solution.py:315
  12.7 2.5 %shard_map.104 = (bf16[256,1024]{1,0:T(8,128)(2,1)S(1)}, bf16[256,1024]{1,0:T(8,128)(2,1)S(1)}, f32[8,256]{1,0:T(8,128)S(1)}, f32[8,256]{1,0:T(8,128)S(1)}, s32[8,128]{1,0:T(8,128)S(1)}) custom-call(s32[8]{0:T(128)} %span_ref.1, f32[128,256]{1,0:T(8,128)S(1)} %get-tuple-element.34.tables_ref, f32[8,256]{1,0:T(8,128)} %lse_hbm.1, bf16[256,1024]{1,0:T(8,128)(2,1)} %q_hbm.1, ...), custom_call_target="tpu_custom_call" | custom-call | flops 1048576 | bytes 7380000 | tf_op jit(solution)/shard_map/pallas_call | solution.py:340
  15.3 0.5 %collective-permute-start.6 = (bf16[256,256]{1,0:T(8,128)(2,1)S(1)}, bf16[256,256]{1,0:T(8,128)(2,1)S(1)}, u32[]{:S(2)}, u32[]{:S(2)}) collective-permute-start(bf16[256,256]{1,0:T(8,128)(2,1)S(1)} %collective-permute-done.4.refs_1_), channel_id=1, source_target_pairs={{0,24},{4,28},{8,0},{12,4},{16,8},{20,12},{24,16},{28,20},{1,25},{... | collective-permute-start | bytes 393224 | tf_op jit(solution)/shard_map/ppermute | solution.py:315
  15.8 0.5 collective-permute-done.3.refs_0_
  16.3 1.5 %collective-permute-start.5 = (bf16[256,256]{1,0:T(8,128)(2,1)S(1)}, bf16[256,256]{1,0:T(8,128)(2,1)S(1)}, u32[]{:S(2)}, u32[]{:S(2)}) collective-permute-start(bf16[256,256]{1,0:T(8,128)(2,1)S(1)} %collective-permute-done.3.refs_0_), channel_id=1, source_target_pairs={{0,24},{4,28},{8,0},{12,4},{16,8},{20,12},{24,16},{28,20},{1,25},{... | collective-permute-start | bytes 393224 | tf_op jit(solution)/shard_map/ppermute | solution.py:315
  17.8 0.4 collective-permute-start.8
  18.3 1.6 %shard_map.105 = (f32[512,256]{1,0:T(8,128)S(1)}, f32[512,256]{1,0:T(8,128)S(1)}, bf16[256,256]{1,0:T(8,128)(2,1)S(1)}, bf16[256,256]{1,0:T(8,128)(2,1)S(1)}) custom-call(bf16[256,256]{1,0:T(8,128)(2,1)S(1)} %collective-permute-done.3.refs_0_, bf16[256,256]{1,0:T(8,128)(2,1)S(1)} %collective-permute-done.4.refs_1_, ...), custom_call_target="tpu_custom_call" | custom-call | flops 1048576 | bytes 7380000 | tf_op jit(solution)/shard_map/pallas_call | solution.py:365
  19.9 2.1 %collective-permute-start.7 = (bf16[256,256]{1,0:T(8,128)(2,1)S(1)}, bf16[256,256]{1,0:T(8,128)(2,1)S(1)}, u32[]{:S(2)}, u32[]{:S(2)}) collective-permute-start(bf16[256,256]{1,0:T(8,128)(2,1)S(1)} %get-tuple-element.47.k_ref), channel_id=1, source_target_pairs={{0,24},{4,28},{8,0},{12,4},{16,8},{20,12},{24,16},{28,20},{1,25},{... | collective-permute-start | bytes 393224 | tf_op jit(solution)/shard_map/ppermute | solution.py:315
  22.0 0.0 collective-permute-done.6.refs_2_
  22.0 2.5 %collective-permute-done.5.refs_1_ = bf16[256,256]{1,0:T(8,128)(2,1)S(1)} collective-permute-done((bf16[256,256]{1,0:T(8,128)(2,1)S(1)}, bf16[256,256]{1,0:T(8,128)(2,1)S(1)}, u32[]{:S(2)}, u32[]{:S(2)}) %collective-permute-start.5) | collective-permute-done | bytes 131104 | tf_op jit(solution)/shard_map/ppermute | solution.py:315
  24.5 0.9 %shard_map.106 = (f32[512,256]{1,0:T(8,128)S(1)}, bf16[256,256]{1,0:T(8,128)(2,1)S(1)}) custom-call(f32[512,256]{1,0:T(8,128)S(1)} %get-tuple-element.42.refs_0_, bf16[256,256]{1,0:T(8,128)(2,1)S(1)} %collective-permute-done.5.refs_1_, bf16[256,256]{1,0:T(8,128)(2,1)S(1)} %collective-permute-done.6.refs_2_, ...), custom_call_target="tpu_custom_call" | custom-call | flops 1048576 | bytes 3690000 | tf_op jit(solution)/shard_map/pallas_call | solution.py:365
  25.4 0.1 collective-permute-start.11
  25.5 0.9 %shard_map.107 = (f32[512,256]{1,0:T(8,128)S(1)}, bf16[256,256]{1,0:T(8,128)(2,1)S(1)}) custom-call(f32[512,256]{1,0:T(8,128)S(1)} %get-tuple-element.44.refs_0_, bf16[256,256]{1,0:T(8,128)(2,1)S(1)} %collective-permute-done.5.refs_1_, bf16[256,256]{1,0:T(8,128)(2,1)S(1)} %collective-permute-done.6.refs_2_, ...), custom_call_target="tpu_custom_call" | custom-call | flops 1048576 | bytes 3690000 | tf_op jit(solution)/shard_map/pallas_call | solution.py:365
  26.4 0.1 collective-permute-start.13
  26.5 0.8 %collective-permute-done.8.refs_3_ = bf16[256,256]{1,0:T(8,128)(2,1)S(1)} collective-permute-done((bf16[256,256]{1,0:T(8,128)(2,1)S(1)}, bf16[256,256]{1,0:T(8,128)(2,1)S(1)}, u32[]{:S(2)}, u32[]{:S(2)}) %collective-permute-start.8) | collective-permute-done | bytes 131104 | tf_op jit(solution)/shard_map/ppermute | solution.py:315
  27.3 7.8 %collective-permute-done.7.refs_2_ = bf16[256,256]{1,0:T(8,128)(2,1)S(1)} collective-permute-done((bf16[256,256]{1,0:T(8,128)(2,1)S(1)}, bf16[256,256]{1,0:T(8,128)(2,1)S(1)}, u32[]{:S(2)}, u32[]{:S(2)}) %collective-permute-start.7) | collective-permute-done | bytes 131104 | tf_op jit(solution)/shard_map/ppermute | solution.py:315
  35.1 1.6 %shard_map.108 = (f32[512,256]{1,0:T(8,128)S(1)}, f32[512,256]{1,0:T(8,128)S(1)}, bf16[256,256]{1,0:T(8,128)(2,1)S(1)}, bf16[256,256]{1,0:T(8,128)(2,1)S(1)}) custom-call(f32[512,256]{1,0:T(8,128)S(1)} %get-tuple-element.43.refs_0_, f32[512,256]{1,0:T(8,128)S(1)} %get-tuple-element.45.refs_1_, bf16[256,256]{1,0:T(8,128)(2,1)S(1)} %collective-permute-done.7.refs_2_, ...), custom_call_target="tpu_custom_call" | custom-call | flops 1048576 | bytes 7380000 | tf_op jit(solution)/shard_map/pallas_call | solution.py:365
  36.8 0.1 collective-permute-start.9
  36.9 0.1 collective-permute-start.10
  37.0 0.1 collective-permute-start.12
  37.1 1.2 %collective-permute-start.14 = (bf16[256,256]{1,0:T(8,128)(2,1)S(1)}, bf16[256,256]{1,0:T(8,128)(2,1)S(1)}, u32[]{:S(2)}, u32[]{:S(2)}) collective-permute-start(bf16[256,256]{1,0:T(8,128)(2,1)S(1)} %shard_map.112), channel_id=1, source_target_pairs={{0,4},{4,8},{8,12},{12,16},{16,20},{20,24},{24,28},{28,0},{1,5},{5... | collective-permute-start | bytes 393224 | tf_op jit(solution)/shard_map/ppermute | solution.py:315
  38.3 3.0 %shard_map.109 = (f32[512,256]{1,0:T(8,128)S(1)}, f32[512,256]{1,0:T(8,128)S(1)}, f32[256,256]{1,0:T(8,128)S(1)}, f32[256,256]{1,0:T(8,128)S(1)}) custom-call(bf16[256,256]{1,0:T(8,128)(2,1)S(1)} %get-tuple-element.47.k_ref, bf16[256,256]{1,0:T(8,128)(2,1)} %v_ref.1, bf16[256,1024]{1,0:T(8,128)(2,1)S(1)} %get-tuple-element.36.refs_2_.refs_3_.refs_4_.qr_ref, ...), custom_call_target="tpu_custom_call" | custom-call | flops 1048576 | bytes 11070000 | tf_op jit(solution)/shard_map/pallas_call | solution.py:383
  41.4 3.6 %collective-permute-done.9.refs_4_ = bf16[256,256]{1,0:T(8,128)(2,1)S(1)} collective-permute-done((bf16[256,256]{1,0:T(8,128)(2,1)S(1)}, bf16[256,256]{1,0:T(8,128)(2,1)S(1)}, u32[]{:S(2)}, u32[]{:S(2)}) %collective-permute-start.9) | collective-permute-done | bytes 131104 | tf_op jit(solution)/shard_map/ppermute | solution.py:315
  45.0 1.4 %collective-permute-done.10.refs_5_ = bf16[256,256]{1,0:T(8,128)(2,1)S(1)} collective-permute-done((bf16[256,256]{1,0:T(8,128)(2,1)S(1)}, bf16[256,256]{1,0:T(8,128)(2,1)S(1)}, u32[]{:S(2)}, u32[]{:S(2)}) %collective-permute-start.10) | collective-permute-done | bytes 131104 | tf_op jit(solution)/shard_map/ppermute | solution.py:315
  46.4 1.1 %shard_map.110 = (bf16[256,1024]{1,0:T(8,128)(2,1)}, f32[256,256]{1,0:T(8,128)S(1)}, f32[256,256]{1,0:T(8,128)S(1)}) custom-call(f32[128,256]{1,0:T(8,128)S(1)} %get-tuple-element.34.tables_ref, f32[512,256]{1,0:T(8,128)S(1)} %get-tuple-element.51.refs_0_, f32[512,256]{1,0:T(8,128)S(1)} %get-tuple-element.52.refs_1_, ...), custom_call_target="tpu_custom_call" | custom-call | flops 1048576 | bytes 3690000 | tf_op jit(solution)/shard_map/pallas_call | solution.py:390
  47.5 0.9 %shard_map.113 = (bf16[256,256]{1,0:T(8,128)(2,1)}, bf16[256,256]{1,0:T(8,128)(2,1)}) custom-call(f32[128,256]{1,0:T(8,128)S(1)} %get-tuple-element.34.tables_ref, f32[256,256]{1,0:T(8,128)S(1)} %get-tuple-element.58.refs_0_, f32[256,256]{1,0:T(8,128)S(1)} %get-tuple-element.59.refs_1_, bf16[256,256]{1,0:T(8,128)(2,1)S(1)} %collective-permute-done.12.refs_2_, ...), custom_call_target="tpu_custom_call" | custom-call | flops 1048576 | bytes 3690000 | tf_op jit(solution)/shard_map/pallas_call | solution.py:400
  (11 shorter events, 0.1 us)
Async XLA Ops:
  0.6 9.3 %collective-permute-start.1 = (s32[3,64]{1,0:T(4,128)}, s32[3,64]{1,0:T(4,128)S(1)}, u32[]{:S(2)}, u32[]{:S(2)}) collective-permute-start(s32[3,64]{1,0:T(4,128)} %own_ref.1), channel_id=1, source_target_pairs={{0,2},{1,3},{2,0},{3,1},{4,6},{5,7},{6,4},{7,5},{8,10},{9,11},{10,... | collective-permute-start | bytes 2312 | tf_op jit(solution)/shard_map/ppermute | solution.py:315
  3.6 6.3 %collective-permute-start = (s32[3,64]{1,0:T(4,128)}, s32[3,64]{1,0:T(4,128)S(1)}, u32[]{:S(2)}, u32[]{:S(2)}) collective-permute-start(s32[3,64]{1,0:T(4,128)} %own_ref.1), channel_id=1, source_target_pairs={{0,1},{1,2},{2,3},{3,0},{4,5},{5,6},{6,7},{7,4},{8,9},{9,10},{10,1... | collective-permute-start | bytes 2312 | tf_op jit(solution)/shard_map/ppermute | solution.py:315
  3.6 6.3 %collective-permute-start.2 = (s32[3,64]{1,0:T(4,128)}, s32[3,64]{1,0:T(4,128)S(1)}, u32[]{:S(2)}, u32[]{:S(2)}) collective-permute-start(s32[3,64]{1,0:T(4,128)} %own_ref.1), channel_id=1, source_target_pairs={{0,3},{1,0},{2,1},{3,2},{4,7},{5,4},{6,5},{7,6},{8,11},{9,8},{10,9... | collective-permute-start | bytes 2312 | tf_op jit(solution)/shard_map/ppermute | solution.py:315
  5.4 9.9 %collective-permute-start.4 = (bf16[256,256]{1,0:T(8,128)(2,1)}, bf16[256,256]{1,0:T(8,128)(2,1)S(1)}, u32[]{:S(2)}, u32[]{:S(2)}) collective-permute-start(bf16[256,256]{1,0:T(8,128)(2,1)} %v_ref.1), channel_id=1, source_target_pairs={{0,28},{4,0},{8,4},{12,8},{16,12},{20,16},{24,20},{28,24},{1,29},{... | collective-permute-start | bytes 393224 | tf_op jit(solution)/shard_map/ppermute | solution.py:315
  11.2 5.1 %collective-permute-start.3 = (bf16[256,256]{1,0:T(8,128)(2,1)S(1)}, bf16[256,256]{1,0:T(8,128)(2,1)S(1)}, u32[]{:S(2)}, u32[]{:S(2)}) collective-permute-start(bf16[256,256]{1,0:T(8,128)(2,1)S(1)} %get-tuple-element.47.k_ref), channel_id=1, source_target_pairs={{0,28},{4,0},{8,4},{12,8},{16,12},{20,16},{24,20},{28,24},{1,29},{... | collective-permute-start | bytes 393224 | tf_op jit(solution)/shard_map/ppermute | solution.py:315
  12.7 5.1 %copy-start = (bf16[256,256]{1,0:T(8,128)(2,1)S(1)}, bf16[256,256]{1,0:T(8,128)(2,1)}, u32[]{:S(2)}) copy-start(bf16[256,256]{1,0:T(8,128)(2,1)} %v_ref.1) | copy-start | bytes 393220
  15.3 6.7 %collective-permute-start.6 = (bf16[256,256]{1,0:T(8,128)(2,1)S(1)}, bf16[256,256]{1,0:T(8,128)(2,1)S(1)}, u32[]{:S(2)}, u32[]{:S(2)}) collective-permute-start(bf16[256,256]{1,0:T(8,128)(2,1)S(1)} %collective-permute-done.4.refs_1_), channel_id=1, source_target_pairs={{0,24},{4,28},{8,0},{12,4},{16,8},{20,12},{24,16},{28,20},{1,25},{... | collective-permute-start | bytes 393224 | tf_op jit(solution)/shard_map/ppermute | solution.py:315
  16.3 8.2 %collective-permute-start.5 = (bf16[256,256]{1,0:T(8,128)(2,1)S(1)}, bf16[256,256]{1,0:T(8,128)(2,1)S(1)}, u32[]{:S(2)}, u32[]{:S(2)}) collective-permute-start(bf16[256,256]{1,0:T(8,128)(2,1)S(1)} %collective-permute-done.3.refs_0_), channel_id=1, source_target_pairs={{0,24},{4,28},{8,0},{12,4},{16,8},{20,12},{24,16},{28,20},{1,25},{... | collective-permute-start | bytes 393224 | tf_op jit(solution)/shard_map/ppermute | solution.py:315
  17.8 9.5 %collective-permute-start.8 = (bf16[256,256]{1,0:T(8,128)(2,1)S(1)}, bf16[256,256]{1,0:T(8,128)(2,1)S(1)}, u32[]{:S(2)}, u32[]{:S(2)}) collective-permute-start(bf16[256,256]{1,0:T(8,128)(2,1)S(1)} %copy-done), channel_id=1, source_target_pairs={{0,24},{4,28},{8,0},{12,4},{16,8},{20,12},{24,16},{28,20},{1,25},{... | collective-permute-start | bytes 393224 | tf_op jit(solution)/shard_map/ppermute | solution.py:315
  19.9 15.2 %collective-permute-start.7 = (bf16[256,256]{1,0:T(8,128)(2,1)S(1)}, bf16[256,256]{1,0:T(8,128)(2,1)S(1)}, u32[]{:S(2)}, u32[]{:S(2)}) collective-permute-start(bf16[256,256]{1,0:T(8,128)(2,1)S(1)} %get-tuple-element.47.k_ref), channel_id=1, source_target_pairs={{0,24},{4,28},{8,0},{12,4},{16,8},{20,12},{24,16},{28,20},{1,25},{... | collective-permute-start | bytes 393224 | tf_op jit(solution)/shard_map/ppermute | solution.py:315
  25.4 11.5 %collective-permute-start.11 = (bf16[256,256]{1,0:T(8,128)(2,1)S(1)}, bf16[256,256]{1,0:T(8,128)(2,1)S(1)}, u32[]{:S(2)}, u32[]{:S(2)}) collective-permute-start(bf16[256,256]{1,0:T(8,128)(2,1)S(1)} %get-tuple-element.60), channel_id=1, source_target_pairs={{0,8},{4,12},{8,16},{12,20},{16,24},{20,28},{24,0},{28,4},{1,9},{5... | collective-permute-start | bytes 393224 | tf_op jit(solution)/shard_map/ppermute | solution.py:315
  26.4 10.6 %collective-permute-start.13 = (bf16[256,256]{1,0:T(8,128)(2,1)S(1)}, bf16[256,256]{1,0:T(8,128)(2,1)S(1)}, u32[]{:S(2)}, u32[]{:S(2)}) collective-permute-start(bf16[256,256]{1,0:T(8,128)(2,1)S(1)} %get-tuple-element.62), channel_id=1, source_target_pairs={{0,8},{4,12},{8,16},{12,20},{16,24},{20,28},{24,0},{28,4},{1,9},{5... | collective-permute-start | bytes 393224 | tf_op jit(solution)/shard_map/ppermute | solution.py:315
  36.8 8.2 %collective-permute-start.9 = (bf16[256,256]{1,0:T(8,128)(2,1)S(1)}, bf16[256,256]{1,0:T(8,128)(2,1)S(1)}, u32[]{:S(2)}, u32[]{:S(2)}) collective-permute-start(bf16[256,256]{1,0:T(8,128)(2,1)S(1)} %get-tuple-element.55), channel_id=1, source_target_pairs={{0,8},{4,12},{8,16},{12,20},{16,24},{20,28},{24,0},{28,4},{1,9},{5... | collective-permute-start | bytes 393224 | tf_op jit(solution)/shard_map/ppermute | solution.py:315
  36.9 9.5 %collective-permute-start.10 = (bf16[256,256]{1,0:T(8,128)(2,1)S(1)}, bf16[256,256]{1,0:T(8,128)(2,1)S(1)}, u32[]{:S(2)}, u32[]{:S(2)}) collective-permute-start(bf16[256,256]{1,0:T(8,128)(2,1)S(1)} %get-tuple-element.56), channel_id=1, source_target_pairs={{0,8},{4,12},{8,16},{12,20},{16,24},{20,28},{24,0},{28,4},{1,9},{5... | collective-permute-start | bytes 393224 | tf_op jit(solution)/shard_map/ppermute | solution.py:315
  37.0 10.5 %collective-permute-start.12 = (bf16[256,256]{1,0:T(8,128)(2,1)S(1)}, bf16[256,256]{1,0:T(8,128)(2,1)S(1)}, u32[]{:S(2)}, u32[]{:S(2)}) collective-permute-start(bf16[256,256]{1,0:T(8,128)(2,1)S(1)} %shard_map.111), channel_id=1, source_target_pairs={{0,4},{4,8},{8,12},{12,16},{16,20},{20,24},{24,28},{28,0},{1,5},{5... | collective-permute-start | bytes 393224 | tf_op jit(solution)/shard_map/ppermute | solution.py:315
  37.1 10.4 %collective-permute-start.14 = (bf16[256,256]{1,0:T(8,128)(2,1)S(1)}, bf16[256,256]{1,0:T(8,128)(2,1)S(1)}, u32[]{:S(2)}, u32[]{:S(2)}) collective-permute-start(bf16[256,256]{1,0:T(8,128)(2,1)S(1)} %shard_map.112), channel_id=1, source_target_pairs={{0,4},{4,8},{8,12},{12,16},{16,20},{20,24},{24,28},{28,0},{1,5},{5... | collective-permute-start | bytes 393224 | tf_op jit(solution)/shard_map/ppermute | solution.py:315

commit v24 on v23

--- a/solution.py
+++ b/solution.py
@@ -351,8 +351,9 @@
     )(span_map, tables, lse, q, do, at)
     v1, _ = lax.optimization_barrier((v1, shared[3]))
     v3 = shifted(v1, -2)
-    v_far, _ = lax.optimization_barrier((v, shared[3]))
+    v_far, kr_far, _ = lax.optimization_barrier((v, kr, shared[3]))
     v2 = shifted(v_far, -2)
+    k2 = shifted(kr_far, -2)
     k3 = shifted(k1, -2)
     dqs = []
     dq_out = ((wide_q // groups, rows), F32)
@@ -376,8 +377,6 @@
         return results[count:]
 
     parts1 = hop(1, every, k1, v1)
-    kr2, _ = lax.optimization_barrier((kr, parts1[0]))
-    k2 = shifted(kr2, -2)
     moved = [shifted(*hop(3, (g,), k3, v3), 2) for g in every]
     back2 = [shifted(part, 2) for part in hop(2, every, k2, v2)]
     results = call(

time: 48.5 us -> 48.5 us (level)
  no operation moved by 1% of the time
where the time goes in v24:
time: 48.5 us; the launch traced here: 48.4 us
  starting transfers between devices  16.9 us (35%)
  waiting for transfers between devices  16.7 us (34%)
  Pallas kernels  14 us (29%)
  between operations  0.77 us (2%)
    ppermute x15, starting transfers between devices, shifted(): return lax.ppermute(value, axis, pairs)  16.9 us
    ppermute x15, waiting for transfers between devices, shifted(): return lax.ppermute(value, axis, pairs)  16.7 us
    pallas_call x4, Pallas kernels, hop(): call(functools.partial(hop_kernel, step, wanted, started, joined), [dq_ou...  5.12 us
    pallas_call x1, Pallas kernels, shards(): call(functools.partial(own_kernel, groups), [dq_out] * groups + [((rows,...  3.05 us
    pallas_call x1, Pallas kernels, shards(): call(functools.partial(prep_kernel, groups), [((rows, wide_q), BF16)] * 2...  2.55 us
    pallas_call x1, Pallas kernels, shards(): call(key_kernel, [((rows, wide_k), BF16), ((HEAD, rows), F32)], [VMEM] * 5)  1.24 us
    pallas_call x1, Pallas kernels, shards(): call(functools.partial(query_kernel, groups), [((rows, wide_q), BF16)] +...  1.1 us
  transfers between devices with their start and end apart: 15, of which 6 were waited for; matrix products, arithmetic and copies ran while one was open for 0% of the time, Pallas kernels for 27%

profile of v24, /device:TPU:0, one launch (start us, length us, event | category | flops | bytes accessed | tf_op | source)
XLA Modules:
  0.0 48.4 jit_solution(12663807430258207527)
XLA Ops:
  0.6 3.0 %collective-permute-start.1 = (s32[3,64]{1,0:T(4,128)}, s32[3,64]{1,0:T(4,128)S(1)}, u32[]{:S(2)}, u32[]{:S(2)}) collective-permute-start(s32[3,64]{1,0:T(4,128)} %own_ref.1), channel_id=1, source_target_pairs={{0,2},{1,3},{2,0},{3,1},{4,6},{5,7},{6,4},{7,5},{8,10},{9,11},{10,... | collective-permute-start | bytes 2312 | tf_op jit(solution)/shard_map/ppermute | solution.py:315
  3.6 0.0 collective-permute-start
  3.6 1.7 %collective-permute-start.2 = (s32[3,64]{1,0:T(4,128)}, s32[3,64]{1,0:T(4,128)S(1)}, u32[]{:S(2)}, u32[]{:S(2)}) collective-permute-start(s32[3,64]{1,0:T(4,128)} %own_ref.1), channel_id=1, source_target_pairs={{0,3},{1,0},{2,1},{3,2},{4,7},{5,4},{6,5},{7,6},{8,11},{9,8},{10,9... | collective-permute-start | bytes 2312 | tf_op jit(solution)/shard_map/ppermute | solution.py:315
  5.4 4.6 %collective-permute-start.4 = (bf16[256,256]{1,0:T(8,128)(2,1)}, bf16[256,256]{1,0:T(8,128)(2,1)S(1)}, u32[]{:S(2)}, u32[]{:S(2)}) collective-permute-start(bf16[256,256]{1,0:T(8,128)(2,1)} %v_ref.1), channel_id=1, source_target_pairs={{0,28},{4,0},{8,4},{12,8},{16,12},{20,16},{24,20},{28,24},{1,29},{... | collective-permute-start | bytes 393224 | tf_op jit(solution)/shard_map/ppermute | solution.py:315
  9.9 0.0 collective-permute-done.1.p2_ref
  9.9 0.0 collective-permute-done.p1_ref
  10.0 1.2 %shard_map.103 = (bf16[256,256]{1,0:T(8,128)(2,1)S(1)}, f32[128,256]{1,0:T(8,128)S(1)}) custom-call(s32[3,64]{1,0:T(4,128)} %own_ref.1, s32[3,64]{1,0:T(4,128)S(1)} %collective-permute-done.p1_ref, s32[3,64]{1,0:T(4,128)S(1)} %collective-permute-done.1.p2_ref, s32[3,64]{1,0:T(4,128)S(1)} %collective-permute-done.2.p3_ref, bf16[256,256]{1,0:T(8,128)(2,1)} %k_ref.1), custom_call_target="tpu_custom_call" | custom-call | flops 1048576 | bytes 3690000 | tf_op jit(solution)/shard_map/pallas_call | solution.py:336
  11.2 1.6 %collective-permute-start.3 = (bf16[256,256]{1,0:T(8,128)(2,1)S(1)}, bf16[256,256]{1,0:T(8,128)(2,1)S(1)}, u32[]{:S(2)}, u32[]{:S(2)}) collective-permute-start(bf16[256,256]{1,0:T(8,128)(2,1)S(1)} %get-tuple-element.46.k_ref), channel_id=1, source_target_pairs={{0,28},{4,0},{8,4},{12,8},{16,12},{20,16},{24,20},{28,24},{1,29},{... | collective-permute-start | bytes 393224 | tf_op jit(solution)/shard_map/ppermute | solution.py:315
  12.7 2.5 %shard_map.104 = (bf16[256,1024]{1,0:T(8,128)(2,1)S(1)}, bf16[256,1024]{1,0:T(8,128)(2,1)S(1)}, f32[8,256]{1,0:T(8,128)S(1)}, f32[8,256]{1,0:T(8,128)S(1)}, s32[8,128]{1,0:T(8,128)S(1)}) custom-call(s32[8]{0:T(128)} %span_ref.1, f32[128,256]{1,0:T(8,128)S(1)} %get-tuple-element.34.tables_ref, f32[8,256]{1,0:T(8,128)} %lse_hbm.1, bf16[256,1024]{1,0:T(8,128)(2,1)} %q_hbm.1, ...), custom_call_target="tpu_custom_call" | custom-call | flops 1048576 | bytes 7380000 | tf_op jit(solution)/shard_map/pallas_call | solution.py:340
  15.3 0.5 %collective-permute-start.6 = (bf16[256,256]{1,0:T(8,128)(2,1)S(1)}, bf16[256,256]{1,0:T(8,128)(2,1)S(1)}, u32[]{:S(2)}, u32[]{:S(2)}) collective-permute-start(bf16[256,256]{1,0:T(8,128)(2,1)S(1)} %collective-permute-done.4.refs_1_), channel_id=1, source_target_pairs={{0,24},{4,28},{8,0},{12,4},{16,8},{20,12},{24,16},{28,20},{1,25},{... | collective-permute-start | bytes 393224 | tf_op jit(solution)/shard_map/ppermute | solution.py:315
  15.8 0.5 collective-permute-done.3.refs_0_
  16.3 1.5 %collective-permute-start.5 = (bf16[256,256]{1,0:T(8,128)(2,1)S(1)}, bf16[256,256]{1,0:T(8,128)(2,1)S(1)}, u32[]{:S(2)}, u32[]{:S(2)}) collective-permute-start(bf16[256,256]{1,0:T(8,128)(2,1)S(1)} %collective-permute-done.3.refs_0_), channel_id=1, source_target_pairs={{0,24},{4,28},{8,0},{12,4},{16,8},{20,12},{24,16},{28,20},{1,25},{... | collective-permute-start | bytes 393224 | tf_op jit(solution)/shard_map/ppermute | solution.py:315
  17.8 0.4 collective-permute-start.7
  18.3 2.1 %collective-permute-start.8 = (bf16[256,256]{1,0:T(8,128)(2,1)S(1)}, bf16[256,256]{1,0:T(8,128)(2,1)S(1)}, u32[]{:S(2)}, u32[]{:S(2)}) collective-permute-start(bf16[256,256]{1,0:T(8,128)(2,1)S(1)} %copy-done), channel_id=1, source_target_pairs={{0,24},{4,28},{8,0},{12,4},{16,8},{20,12},{24,16},{28,20},{1,25},{... | collective-permute-start | bytes 393224 | tf_op jit(solution)/shard_map/ppermute | solution.py:315
  20.3 1.6 %shard_map.105 = (f32[512,256]{1,0:T(8,128)S(1)}, f32[512,256]{1,0:T(8,128)S(1)}, bf16[256,256]{1,0:T(8,128)(2,1)S(1)}, bf16[256,256]{1,0:T(8,128)(2,1)S(1)}) custom-call(bf16[256,256]{1,0:T(8,128)(2,1)S(1)} %collective-permute-done.3.refs_0_, bf16[256,256]{1,0:T(8,128)(2,1)S(1)} %collective-permute-done.4.refs_1_, ...), custom_call_target="tpu_custom_call" | custom-call | flops 1048576 | bytes 7380000 | tf_op jit(solution)/shard_map/pallas_call | solution.py:366
  22.0 2.5 %collective-permute-done.5.refs_1_ = bf16[256,256]{1,0:T(8,128)(2,1)S(1)} collective-permute-done((bf16[256,256]{1,0:T(8,128)(2,1)S(1)}, bf16[256,256]{1,0:T(8,128)(2,1)S(1)}, u32[]{:S(2)}, u32[]{:S(2)}) %collective-permute-start.5) | collective-permute-done | bytes 131104 | tf_op jit(solution)/shard_map/ppermute | solution.py:315
  24.5 0.9 %shard_map.106 = (f32[512,256]{1,0:T(8,128)S(1)}, bf16[256,256]{1,0:T(8,128)(2,1)S(1)}) custom-call(f32[512,256]{1,0:T(8,128)S(1)} %get-tuple-element.42.refs_0_, bf16[256,256]{1,0:T(8,128)(2,1)S(1)} %collective-permute-done.5.refs_1_, bf16[256,256]{1,0:T(8,128)(2,1)S(1)} %collective-permute-done.6.refs_2_, ...), custom_call_target="tpu_custom_call" | custom-call | flops 1048576 | bytes 3690000 | tf_op jit(solution)/shard_map/pallas_call | solution.py:366
  25.4 0.1 collective-permute-start.11
  25.5 0.9 %shard_map.107 = (f32[512,256]{1,0:T(8,128)S(1)}, bf16[256,256]{1,0:T(8,128)(2,1)S(1)}) custom-call(f32[512,256]{1,0:T(8,128)S(1)} %get-tuple-element.44.refs_0_, bf16[256,256]{1,0:T(8,128)(2,1)S(1)} %collective-permute-done.5.refs_1_, bf16[256,256]{1,0:T(8,128)(2,1)S(1)} %collective-permute-done.6.refs_2_, ...), custom_call_target="tpu_custom_call" | custom-call | flops 1048576 | bytes 3690000 | tf_op jit(solution)/shard_map/pallas_call | solution.py:366
  26.4 0.1 collective-permute-start.13
  26.5 0.8 %collective-permute-done.7.refs_2_ = bf16[256,256]{1,0:T(8,128)(2,1)S(1)} collective-permute-done((bf16[256,256]{1,0:T(8,128)(2,1)S(1)}, bf16[256,256]{1,0:T(8,128)(2,1)S(1)}, u32[]{:S(2)}, u32[]{:S(2)}) %collective-permute-start.7) | collective-permute-done | bytes 131104 | tf_op jit(solution)/shard_map/ppermute | solution.py:315
  27.3 7.8 %collective-permute-done.8.refs_3_ = bf16[256,256]{1,0:T(8,128)(2,1)S(1)} collective-permute-done((bf16[256,256]{1,0:T(8,128)(2,1)S(1)}, bf16[256,256]{1,0:T(8,128)(2,1)S(1)}, u32[]{:S(2)}, u32[]{:S(2)}) %collective-permute-start.8) | collective-permute-done | bytes 131104 | tf_op jit(solution)/shard_map/ppermute | solution.py:315
  35.1 1.6 %shard_map.108 = (f32[512,256]{1,0:T(8,128)S(1)}, f32[512,256]{1,0:T(8,128)S(1)}, bf16[256,256]{1,0:T(8,128)(2,1)S(1)}, bf16[256,256]{1,0:T(8,128)(2,1)S(1)}) custom-call(f32[512,256]{1,0:T(8,128)S(1)} %get-tuple-element.43.refs_0_, f32[512,256]{1,0:T(8,128)S(1)} %get-tuple-element.45.refs_1_, bf16[256,256]{1,0:T(8,128)(2,1)S(1)} %collective-permute-done.7.refs_2_, ...), custom_call_target="tpu_custom_call" | custom-call | flops 1048576 | bytes 7380000 | tf_op jit(solution)/shard_map/pallas_call | solution.py:366
  36.8 0.1 collective-permute-start.9
  36.9 0.1 collective-permute-start.10
  37.0 0.1 collective-permute-start.12
  37.1 1.2 %collective-permute-start.14 = (bf16[256,256]{1,0:T(8,128)(2,1)S(1)}, bf16[256,256]{1,0:T(8,128)(2,1)S(1)}, u32[]{:S(2)}, u32[]{:S(2)}) collective-permute-start(bf16[256,256]{1,0:T(8,128)(2,1)S(1)} %shard_map.112), channel_id=1, source_target_pairs={{0,4},{4,8},{8,12},{12,16},{16,20},{20,24},{24,28},{28,0},{1,5},{5... | collective-permute-start | bytes 393224 | tf_op jit(solution)/shard_map/ppermute | solution.py:315
  38.3 3.0 %shard_map.109 = (f32[512,256]{1,0:T(8,128)S(1)}, f32[512,256]{1,0:T(8,128)S(1)}, f32[256,256]{1,0:T(8,128)S(1)}, f32[256,256]{1,0:T(8,128)S(1)}) custom-call(bf16[256,256]{1,0:T(8,128)(2,1)S(1)} %get-tuple-element.46.k_ref, bf16[256,256]{1,0:T(8,128)(2,1)} %v_ref.1, bf16[256,1024]{1,0:T(8,128)(2,1)S(1)} %get-tuple-element.36.refs_2_.refs_3_.refs_4_.qr_ref, ...), custom_call_target="tpu_custom_call" | custom-call | flops 1048576 | bytes 11070000 | tf_op jit(solution)/shard_map/pallas_call | solution.py:382
  41.4 3.6 %collective-permute-done.9.refs_4_ = bf16[256,256]{1,0:T(8,128)(2,1)S(1)} collective-permute-done((bf16[256,256]{1,0:T(8,128)(2,1)S(1)}, bf16[256,256]{1,0:T(8,128)(2,1)S(1)}, u32[]{:S(2)}, u32[]{:S(2)}) %collective-permute-start.9) | collective-permute-done | bytes 131104 | tf_op jit(solution)/shard_map/ppermute | solution.py:315
  45.0 1.4 %collective-permute-done.10.refs_5_ = bf16[256,256]{1,0:T(8,128)(2,1)S(1)} collective-permute-done((bf16[256,256]{1,0:T(8,128)(2,1)S(1)}, bf16[256,256]{1,0:T(8,128)(2,1)S(1)}, u32[]{:S(2)}, u32[]{:S(2)}) %collective-permute-start.10) | collective-permute-done | bytes 131104 | tf_op jit(solution)/shard_map/ppermute | solution.py:315
  46.4 1.1 %shard_map.110 = (bf16[256,1024]{1,0:T(8,128)(2,1)}, f32[256,256]{1,0:T(8,128)S(1)}, f32[256,256]{1,0:T(8,128)S(1)}) custom-call(f32[128,256]{1,0:T(8,128)S(1)} %get-tuple-element.34.tables_ref, f32[512,256]{1,0:T(8,128)S(1)} %get-tuple-element.50.refs_0_, f32[512,256]{1,0:T(8,128)S(1)} %get-tuple-element.51.refs_1_, ...), custom_call_target="tpu_custom_call" | custom-call | flops 1048576 | bytes 3690000 | tf_op jit(solution)/shard_map/pallas_call | solution.py:389
  47.5 0.9 %shard_map.113 = (bf16[256,256]{1,0:T(8,128)(2,1)}, bf16[256,256]{1,0:T(8,128)(2,1)}) custom-call(f32[128,256]{1,0:T(8,128)S(1)} %get-tuple-element.34.tables_ref, f32[256,256]{1,0:T(8,128)S(1)} %get-tuple-element.57.refs_0_, f32[256,256]{1,0:T(8,128)S(1)} %get-tuple-element.58.refs_1_, bf16[256,256]{1,0:T(8,128)(2,1)S(1)} %collective-permute-done.12.refs_2_, ...), custom_call_target="tpu_custom_call" | custom-call | flops 1048576 | bytes 3690000 | tf_op jit(solution)/shard_map/pallas_call | solution.py:399
  (11 shorter events, 0.1 us)
Async XLA Ops:
  0.6 9.3 %collective-permute-start.1 = (s32[3,64]{1,0:T(4,128)}, s32[3,64]{1,0:T(4,128)S(1)}, u32[]{:S(2)}, u32[]{:S(2)}) collective-permute-start(s32[3,64]{1,0:T(4,128)} %own_ref.1), channel_id=1, source_target_pairs={{0,2},{1,3},{2,0},{3,1},{4,6},{5,7},{6,4},{7,5},{8,10},{9,11},{10,... | collective-permute-start | bytes 2312 | tf_op jit(solution)/shard_map/ppermute | solution.py:315
  3.6 6.3 %collective-permute-start = (s32[3,64]{1,0:T(4,128)}, s32[3,64]{1,0:T(4,128)S(1)}, u32[]{:S(2)}, u32[]{:S(2)}) collective-permute-start(s32[3,64]{1,0:T(4,128)} %own_ref.1), channel_id=1, source_target_pairs={{0,1},{1,2},{2,3},{3,0},{4,5},{5,6},{6,7},{7,4},{8,9},{9,10},{10,1... | collective-permute-start | bytes 2312 | tf_op jit(solution)/shard_map/ppermute | solution.py:315
  3.6 6.3 %collective-permute-start.2 = (s32[3,64]{1,0:T(4,128)}, s32[3,64]{1,0:T(4,128)S(1)}, u32[]{:S(2)}, u32[]{:S(2)}) collective-permute-start(s32[3,64]{1,0:T(4,128)} %own_ref.1), channel_id=1, source_target_pairs={{0,3},{1,0},{2,1},{3,2},{4,7},{5,4},{6,5},{7,6},{8,11},{9,8},{10,9... | collective-permute-start | bytes 2312 | tf_op jit(solution)/shard_map/ppermute | solution.py:315
  5.4 9.9 %collective-permute-start.4 = (bf16[256,256]{1,0:T(8,128)(2,1)}, bf16[256,256]{1,0:T(8,128)(2,1)S(1)}, u32[]{:S(2)}, u32[]{:S(2)}) collective-permute-start(bf16[256,256]{1,0:T(8,128)(2,1)} %v_ref.1), channel_id=1, source_target_pairs={{0,28},{4,0},{8,4},{12,8},{16,12},{20,16},{24,20},{28,24},{1,29},{... | collective-permute-start | bytes 393224 | tf_op jit(solution)/shard_map/ppermute | solution.py:315
  11.2 5.1 %collective-permute-start.3 = (bf16[256,256]{1,0:T(8,128)(2,1)S(1)}, bf16[256,256]{1,0:T(8,128)(2,1)S(1)}, u32[]{:S(2)}, u32[]{:S(2)}) collective-permute-start(bf16[256,256]{1,0:T(8,128)(2,1)S(1)} %get-tuple-element.46.k_ref), channel_id=1, source_target_pairs={{0,28},{4,0},{8,4},{12,8},{16,12},{20,16},{24,20},{28,24},{1,29},{... | collective-permute-start | bytes 393224 | tf_op jit(solution)/shard_map/ppermute | solution.py:315
  12.7 5.5 %copy-start = (bf16[256,256]{1,0:T(8,128)(2,1)S(1)}, bf16[256,256]{1,0:T(8,128)(2,1)}, u32[]{:S(2)}) copy-start(bf16[256,256]{1,0:T(8,128)(2,1)} %v_ref.1) | copy-start | bytes 393220
  15.3 6.7 %collective-permute-start.6 = (bf16[256,256]{1,0:T(8,128)(2,1)S(1)}, bf16[256,256]{1,0:T(8,128)(2,1)S(1)}, u32[]{:S(2)}, u32[]{:S(2)}) collective-permute-start(bf16[256,256]{1,0:T(8,128)(2,1)S(1)} %collective-permute-done.4.refs_1_), channel_id=1, source_target_pairs={{0,24},{4,28},{8,0},{12,4},{16,8},{20,12},{24,16},{28,20},{1,25},{... | collective-permute-start | bytes 393224 | tf_op jit(solution)/shard_map/ppermute | solution.py:315
  16.3 8.2 %collective-permute-start.5 = (bf16[256,256]{1,0:T(8,128)(2,1)S(1)}, bf16[256,256]{1,0:T(8,128)(2,1)S(1)}, u32[]{:S(2)}, u32[]{:S(2)}) collective-permute-start(bf16[256,256]{1,0:T(8,128)(2,1)S(1)} %collective-permute-done.3.refs_0_), channel_id=1, source_target_pairs={{0,24},{4,28},{8,0},{12,4},{16,8},{20,12},{24,16},{28,20},{1,25},{... | collective-permute-start | bytes 393224 | tf_op jit(solution)/shard_map/ppermute | solution.py:315
  17.8 9.5 %collective-permute-start.7 = (bf16[256,256]{1,0:T(8,128)(2,1)S(1)}, bf16[256,256]{1,0:T(8,128)(2,1)S(1)}, u32[]{:S(2)}, u32[]{:S(2)}) collective-permute-start(bf16[256,256]{1,0:T(8,128)(2,1)S(1)} %get-tuple-element.46.k_ref), channel_id=1, source_target_pairs={{0,24},{4,28},{8,0},{12,4},{16,8},{20,12},{24,16},{28,20},{1,25},{... | collective-permute-start | bytes 393224 | tf_op jit(solution)/shard_map/ppermute | solution.py:315
  18.3 16.9 %collective-permute-start.8 = (bf16[256,256]{1,0:T(8,128)(2,1)S(1)}, bf16[256,256]{1,0:T(8,128)(2,1)S(1)}, u32[]{:S(2)}, u32[]{:S(2)}) collective-permute-start(bf16[256,256]{1,0:T(8,128)(2,1)S(1)} %copy-done), channel_id=1, source_target_pairs={{0,24},{4,28},{8,0},{12,4},{16,8},{20,12},{24,16},{28,20},{1,25},{... | collective-permute-start | bytes 393224 | tf_op jit(solution)/shard_map/ppermute | solution.py:315
  25.4 11.5 %collective-permute-start.11 = (bf16[256,256]{1,0:T(8,128)(2,1)S(1)}, bf16[256,256]{1,0:T(8,128)(2,1)S(1)}, u32[]{:S(2)}, u32[]{:S(2)}) collective-permute-start(bf16[256,256]{1,0:T(8,128)(2,1)S(1)} %get-tuple-element.60), channel_id=1, source_target_pairs={{0,8},{4,12},{8,16},{12,20},{16,24},{20,28},{24,0},{28,4},{1,9},{5... | collective-permute-start | bytes 393224 | tf_op jit(solution)/shard_map/ppermute | solution.py:315
  26.4 10.6 %collective-permute-start.13 = (bf16[256,256]{1,0:T(8,128)(2,1)S(1)}, bf16[256,256]{1,0:T(8,128)(2,1)S(1)}, u32[]{:S(2)}, u32[]{:S(2)}) collective-permute-start(bf16[256,256]{1,0:T(8,128)(2,1)S(1)} %get-tuple-element.62), channel_id=1, source_target_pairs={{0,8},{4,12},{8,16},{12,20},{16,24},{20,28},{24,0},{28,4},{1,9},{5... | collective-permute-start | bytes 393224 | tf_op jit(solution)/shard_map/ppermute | solution.py:315
  36.8 8.2 %collective-permute-start.9 = (bf16[256,256]{1,0:T(8,128)(2,1)S(1)}, bf16[256,256]{1,0:T(8,128)(2,1)S(1)}, u32[]{:S(2)}, u32[]{:S(2)}) collective-permute-start(bf16[256,256]{1,0:T(8,128)(2,1)S(1)} %get-tuple-element.54), channel_id=1, source_target_pairs={{0,8},{4,12},{8,16},{12,20},{16,24},{20,28},{24,0},{28,4},{1,9},{5... | collective-permute-start | bytes 393224 | tf_op jit(solution)/shard_map/ppermute | solution.py:315
  36.9 9.5 %collective-permute-start.10 = (bf16[256,256]{1,0:T(8,128)(2,1)S(1)}, bf16[256,256]{1,0:T(8,128)(2,1)S(1)}, u32[]{:S(2)}, u32[]{:S(2)}) collective-permute-start(bf16[256,256]{1,0:T(8,128)(2,1)S(1)} %get-tuple-element.55), channel_id=1, source_target_pairs={{0,8},{4,12},{8,16},{12,20},{16,24},{20,28},{24,0},{28,4},{1,9},{5... | collective-permute-start | bytes 393224 | tf_op jit(solution)/shard_map/ppermute | solution.py:315
  37.0 10.5 %collective-permute-start.12 = (bf16[256,256]{1,0:T(8,128)(2,1)S(1)}, bf16[256,256]{1,0:T(8,128)(2,1)S(1)}, u32[]{:S(2)}, u32[]{:S(2)}) collective-permute-start(bf16[256,256]{1,0:T(8,128)(2,1)S(1)} %shard_map.111), channel_id=1, source_target_pairs={{0,4},{4,8},{8,12},{12,16},{16,20},{20,24},{24,28},{28,0},{1,5},{5... | collective-permute-start | bytes 393224 | tf_op jit(solution)/shard_map/ppermute | solution.py:315
  37.1 10.4 %collective-permute-start.14 = (bf16[256,256]{1,0:T(8,128)(2,1)S(1)}, bf16[256,256]{1,0:T(8,128)(2,1)S(1)}, u32[]{:S(2)}, u32[]{:S(2)}) collective-permute-start(bf16[256,256]{1,0:T(8,128)(2,1)S(1)} %shard_map.112), channel_id=1, source_target_pairs={{0,4},{4,8},{8,12},{12,16},{16,20},{20,24},{24,28},{28,0},{1,5},{5... | collective-permute-start | bytes 393224 | tf_op jit(solution)/shard_map/ppermute | solution.py:315

commit v25 on v20

--- a/solution.py
+++ b/solution.py
@@ -362,6 +362,8 @@
     )(span_map, tables, lse, q, do, at)
     v1, _ = lax.optimization_barrier((v1, shared[3]))
     v3 = shifted(v1, -2)
+    v_far, _ = lax.optimization_barrier((v, shared[3]))
+    v2 = shifted(v_far, -2)
     k3 = shifted(k1, -2)
     dqs = []
     dq_out = ((wide_q // groups, rows), F32)
@@ -386,9 +388,8 @@
 
     (part1,) = hop(1, every, k1, v1, joined=True)
     swapped = exchanged(part1)
-    kr2, v_far, _ = lax.optimization_barrier((kr, v, part1))
+    kr2, _ = lax.optimization_barrier((kr, part1))
     k2 = shifted(kr2, -2)
-    v2 = shifted(v_far, -2)
     moved = [shifted(*hop(3, (g,), k3, v3), 1) for g in every]
     parts2 = hop(2, every, k2, v2)
     results = call(

time: 45.4 us -> 45.3 us (level)
  no operation moved by 1% of the time
where the time goes in v25:
time: 45.3 us; the launch traced here: 45.1 us
  starting transfers between devices  24.9 us (55%)
  Pallas kernels  13.9 us (31%)
  waiting for transfers between devices  5.61 us (12%)
  between operations  0.7 us (2%)
    ppermute x13, starting transfers between devices, shifted(): return lax.ppermute(value, axis, pairs)  20.5 us
    ppermute x13, waiting for transfers between devices, shifted(): return lax.ppermute(value, axis, pairs)  5.61 us
    pallas_call x4, Pallas kernels, hop(): call(functools.partial(hop_kernel, step, wanted, started, joined), [dq_ou...  5.12 us
    ppermute x1, starting transfers between devices, exchanged(): lax.ppermute(value, 'ctx', [(source, source ^ 1) for source in range(coun...  4.37 us
    pallas_call x1, Pallas kernels, shards(): call(functools.partial(own_kernel, groups), [dq_out] * groups + [((rows,...  3.05 us
    pallas_call x1, Pallas kernels, shards(): call(functools.partial(prep_kernel, groups), [((rows, wide_q), BF16)] * 2...  2.41 us
    pallas_call x1, Pallas kernels, shards(): call(key_kernel, [((rows, wide_k), BF16), ((HEAD, rows), F32)], [VMEM] * 5)  1.24 us
    pallas_call x1, Pallas kernels, shards(): call(functools.partial(query_kernel, groups), [((rows, wide_q), BF16)] +...  1.1 us
  transfers between devices with their start and end apart: 14, of which 5 were waited for; matrix products, arithmetic and copies ran while one was open for 0% of the time, Pallas kernels for 29%

profile of v25, /device:TPU:0, one launch (start us, length us, event | category | flops | bytes accessed | tf_op | source)
XLA Modules:
  0.0 45.1 jit_solution(17216831766370743937)
XLA Ops:
  0.6 0.5 %collective-permute-start = (s32[3,64]{1,0:T(4,128)}, s32[3,64]{1,0:T(4,128)S(1)}, u32[]{:S(2)}, u32[]{:S(2)}) collective-permute-start(s32[3,64]{1,0:T(4,128)} %own_ref.1), channel_id=1, source_target_pairs={{0,1},{1,2},{2,3},{3,0},{4,5},{5,6},{6,7},{7,4},{8,9},{9,10},{10,1... | collective-permute-start | bytes 2312 | tf_op jit(solution)/shard_map/ppermute | solution.py:321
  1.1 2.6 %collective-permute-start.1 = (s32[3,64]{1,0:T(4,128)}, s32[3,64]{1,0:T(4,128)S(1)}, u32[]{:S(2)}, u32[]{:S(2)}) collective-permute-start(s32[3,64]{1,0:T(4,128)} %own_ref.1), channel_id=1, source_target_pairs={{0,2},{1,3},{2,0},{3,1},{4,6},{5,7},{6,4},{7,5},{8,10},{9,11},{10,... | collective-permute-start | bytes 2312 | tf_op jit(solution)/shard_map/ppermute | solution.py:321
  3.7 1.4 %collective-permute-start.2 = (s32[3,64]{1,0:T(4,128)}, s32[3,64]{1,0:T(4,128)S(1)}, u32[]{:S(2)}, u32[]{:S(2)}) collective-permute-start(s32[3,64]{1,0:T(4,128)} %own_ref.1), channel_id=1, source_target_pairs={{0,3},{1,0},{2,1},{3,2},{4,7},{5,4},{6,5},{7,6},{8,11},{9,8},{10,9... | collective-permute-start | bytes 2312 | tf_op jit(solution)/shard_map/ppermute | solution.py:321
  5.1 4.6 %collective-permute-start.4 = (bf16[256,256]{1,0:T(8,128)(2,1)}, bf16[256,256]{1,0:T(8,128)(2,1)S(1)}, u32[]{:S(2)}, u32[]{:S(2)}) collective-permute-start(bf16[256,256]{1,0:T(8,128)(2,1)} %v_ref.1), channel_id=1, source_target_pairs={{0,28},{4,0},{8,4},{12,8},{16,12},{20,16},{24,20},{28,24},{1,29},{... | collective-permute-start | bytes 393224 | tf_op jit(solution)/shard_map/ppermute | solution.py:321
  9.6 0.0 collective-permute-done.p1_ref
  9.6 0.0 collective-permute-done.1.p2_ref
  9.7 0.0 collective-permute-done.2.p3_ref
  9.7 1.2 %shard_map.103 = (bf16[256,256]{1,0:T(8,128)(2,1)S(1)}, f32[128,256]{1,0:T(8,128)S(1)}) custom-call(s32[3,64]{1,0:T(4,128)} %own_ref.1, s32[3,64]{1,0:T(4,128)S(1)} %collective-permute-done.p1_ref, s32[3,64]{1,0:T(4,128)S(1)} %collective-permute-done.1.p2_ref, s32[3,64]{1,0:T(4,128)S(1)} %collective-permute-done.2.p3_ref, bf16[256,256]{1,0:T(8,128)(2,1)} %k_ref.1), custom_call_target="tpu_custom_call" | custom-call | flops 1048576 | bytes 3690000 | tf_op jit(solution)/shard_map/pallas_call | solution.py:347
  10.9 1.6 %collective-permute-start.3 = (bf16[256,256]{1,0:T(8,128)(2,1)S(1)}, bf16[256,256]{1,0:T(8,128)(2,1)S(1)}, u32[]{:S(2)}, u32[]{:S(2)}) collective-permute-start(bf16[256,256]{1,0:T(8,128)(2,1)S(1)} %get-tuple-element.46.k_ref), channel_id=1, source_target_pairs={{0,28},{4,0},{8,4},{12,8},{16,12},{20,16},{24,20},{28,24},{1,29},{... | collective-permute-start | bytes 393224 | tf_op jit(solution)/shard_map/ppermute | solution.py:321
  12.5 2.4 %shard_map.104 = (bf16[256,1024]{1,0:T(8,128)(2,1)S(1)}, bf16[256,1024]{1,0:T(8,128)(2,1)S(1)}, f32[8,256]{1,0:T(8,128)S(1)}, f32[8,256]{1,0:T(8,128)S(1)}, s32[8,128]{1,0:T(8,128)S(1)}) custom-call(s32[8]{0:T(128)} %span_ref.1, f32[128,256]{1,0:T(8,128)S(1)} %get-tuple-element.33.tables_ref, f32[8,256]{1,0:T(8,128)} %lse_hbm.1, bf16[256,1024]{1,0:T(8,128)(2,1)} %q_hbm.1, ...), custom_call_target="tpu_custom_call" | custom-call | flops 1048576 | bytes 7380000 | tf_op jit(solution)/shard_map/pallas_call | solution.py:351
  14.9 0.5 %collective-permute-start.6 = (bf16[256,256]{1,0:T(8,128)(2,1)S(1)}, bf16[256,256]{1,0:T(8,128)(2,1)S(1)}, u32[]{:S(2)}, u32[]{:S(2)}) collective-permute-start(bf16[256,256]{1,0:T(8,128)(2,1)S(1)} %collective-permute-done.4.refs_1_), channel_id=1, source_target_pairs={{0,24},{4,28},{8,0},{12,4},{16,8},{20,12},{24,16},{28,20},{1,25},{... | collective-permute-start | bytes 393224 | tf_op jit(solution)/shard_map/ppermute | solution.py:321
  15.4 0.7 %collective-permute-done.3.refs_0_ = bf16[256,256]{1,0:T(8,128)(2,1)S(1)} collective-permute-done((bf16[256,256]{1,0:T(8,128)(2,1)S(1)}, bf16[256,256]{1,0:T(8,128)(2,1)S(1)}, u32[]{:S(2)}, u32[]{:S(2)}) %collective-permute-start.3) | collective-permute-done | bytes 131104 | tf_op jit(solution)/shard_map/ppermute | solution.py:321
  16.1 1.4 %collective-permute-start.5 = (bf16[256,256]{1,0:T(8,128)(2,1)S(1)}, bf16[256,256]{1,0:T(8,128)(2,1)S(1)}, u32[]{:S(2)}, u32[]{:S(2)}) collective-permute-start(bf16[256,256]{1,0:T(8,128)(2,1)S(1)} %collective-permute-done.3.refs_0_), channel_id=1, source_target_pairs={{0,24},{4,28},{8,0},{12,4},{16,8},{20,12},{24,16},{28,20},{1,25},{... | collective-permute-start | bytes 393224 | tf_op jit(solution)/shard_map/ppermute | solution.py:321
  17.5 1.6 %shard_map.105 = (f32[512,256]{1,0:T(8,128)S(1)}, f32[512,256]{1,0:T(8,128)S(1)}, bf16[256,512]{1,0:T(8,128)(2,1)S(1)}) custom-call(bf16[256,256]{1,0:T(8,128)(2,1)S(1)} %collective-permute-done.3.refs_0_, bf16[256,256]{1,0:T(8,128)(2,1)S(1)} %collective-permute-done.4.refs_1_, bf16[256,1024]{1,0:T(8,128)(2,1)S(1)} %get-tuple-element.35.refs_2_.refs_3_.refs_4_.qr_ref, ...), custom_call_target="tpu_custom_call" | custom-call | flops 1048576 | bytes 7380000 | tf_op jit(solution)/shard_map/pallas_call | solution.py:376
  19.2 4.4 %collective-permute-start.9 = (bf16[256,512]{1,0:T(8,128)(2,1)S(1)}, bf16[256,512]{1,0:T(8,128)(2,1)S(1)}, u32[]{:S(2)}, u32[]{:S(2)}) collective-permute-start(bf16[256,512]{1,0:T(8,128)(2,1)S(1)} %get-tuple-element.45), channel_id=1, source_target_pairs={{0,4},{4,0},{8,12},{12,8},{16,20},{20,16},{24,28},{28,24},{1,5},{5... | collective-permute-start | bytes 786440 | tf_op jit(solution)/shard_map/ppermute | solution.py:326
  23.5 0.0 collective-permute-start.7
  23.6 0.9 %shard_map.107 = (f32[512,256]{1,0:T(8,128)S(1)}, bf16[256,256]{1,0:T(8,128)(2,1)S(1)}) custom-call(f32[512,256]{1,0:T(8,128)S(1)} %get-tuple-element.43.refs_0_, bf16[256,256]{1,0:T(8,128)(2,1)S(1)} %collective-permute-done.5.refs_1_, bf16[256,256]{1,0:T(8,128)(2,1)S(1)} %collective-permute-done.6.refs_2_, ...), custom_call_target="tpu_custom_call" | custom-call | flops 1048576 | bytes 3690000 | tf_op jit(solution)/shard_map/pallas_call | solution.py:376
  24.5 2.0 %collective-permute-start.12 = (bf16[256,256]{1,0:T(8,128)(2,1)S(1)}, bf16[256,256]{1,0:T(8,128)(2,1)S(1)}, u32[]{:S(2)}, u32[]{:S(2)}) collective-permute-start(bf16[256,256]{1,0:T(8,128)(2,1)S(1)} %get-tuple-element.60), channel_id=1, source_target_pairs={{0,4},{4,8},{8,12},{12,16},{16,20},{20,24},{24,28},{28,0},{1,5},{5... | collective-permute-start | bytes 393224 | tf_op jit(solution)/shard_map/ppermute | solution.py:321
  26.5 0.9 %shard_map.106 = (f32[512,256]{1,0:T(8,128)S(1)}, bf16[256,256]{1,0:T(8,128)(2,1)S(1)}) custom-call(f32[512,256]{1,0:T(8,128)S(1)} %get-tuple-element.41.refs_0_, bf16[256,256]{1,0:T(8,128)(2,1)S(1)} %collective-permute-done.5.refs_1_, bf16[256,256]{1,0:T(8,128)(2,1)S(1)} %collective-permute-done.6.refs_2_, ...), custom_call_target="tpu_custom_call" | custom-call | flops 1048576 | bytes 3690000 | tf_op jit(solution)/shard_map/pallas_call | solution.py:376
  27.5 1.6 %collective-permute-start.10 = (bf16[256,256]{1,0:T(8,128)(2,1)S(1)}, bf16[256,256]{1,0:T(8,128)(2,1)S(1)}, u32[]{:S(2)}, u32[]{:S(2)}) collective-permute-start(bf16[256,256]{1,0:T(8,128)(2,1)S(1)} %get-tuple-element.58), channel_id=1, source_target_pairs={{0,4},{4,8},{8,12},{12,16},{16,20},{20,24},{24,28},{28,0},{1,5},{5... | collective-permute-start | bytes 393224 | tf_op jit(solution)/shard_map/ppermute | solution.py:321
  29.0 0.5 %collective-permute-done.8.refs_3_ = bf16[256,256]{1,0:T(8,128)(2,1)S(1)} collective-permute-done((bf16[256,256]{1,0:T(8,128)(2,1)S(1)}, bf16[256,256]{1,0:T(8,128)(2,1)S(1)}, u32[]{:S(2)}, u32[]{:S(2)}) %collective-permute-start.8) | collective-permute-done | bytes 131104 | tf_op jit(solution)/shard_map/ppermute | solution.py:321
  29.5 1.4 %collective-permute-done.7.refs_2_ = bf16[256,256]{1,0:T(8,128)(2,1)S(1)} collective-permute-done((bf16[256,256]{1,0:T(8,128)(2,1)S(1)}, bf16[256,256]{1,0:T(8,128)(2,1)S(1)}, u32[]{:S(2)}, u32[]{:S(2)}) %collective-permute-start.7) | collective-permute-done | bytes 131104 | tf_op jit(solution)/shard_map/ppermute | solution.py:321
  30.9 1.6 %shard_map.108 = (f32[512,256]{1,0:T(8,128)S(1)}, f32[512,256]{1,0:T(8,128)S(1)}, bf16[256,256]{1,0:T(8,128)(2,1)S(1)}, bf16[256,256]{1,0:T(8,128)(2,1)S(1)}) custom-call(f32[512,256]{1,0:T(8,128)S(1)} %get-tuple-element.42.refs_0_, f32[512,256]{1,0:T(8,128)S(1)} %get-tuple-element.44.refs_1_, bf16[256,256]{1,0:T(8,128)(2,1)S(1)} %collective-permute-done.7.refs_2_, ...), custom_call_target="tpu_custom_call" | custom-call | flops 1048576 | bytes 7380000 | tf_op jit(solution)/shard_map/pallas_call | solution.py:376
  32.6 2.0 %collective-permute-done.12.three_ref = bf16[256,256]{1,0:T(8,128)(2,1)S(1)} collective-permute-done((bf16[256,256]{1,0:T(8,128)(2,1)S(1)}, bf16[256,256]{1,0:T(8,128)(2,1)S(1)}, u32[]{:S(2)}, u32[]{:S(2)}) %collective-permute-start.12) | collective-permute-done | bytes 131104 | tf_op jit(solution)/shard_map/ppermute | solution.py:321
  34.5 0.1 shard_map.112
  34.6 1.4 %collective-permute-start.13 = (bf16[256,256]{1,0:T(8,128)(2,1)S(1)}, bf16[256,256]{1,0:T(8,128)(2,1)S(1)}, u32[]{:S(2)}, u32[]{:S(2)}) collective-permute-start(bf16[256,256]{1,0:T(8,128)(2,1)S(1)} %shard_map.112), channel_id=1, source_target_pairs={{0,8},{4,12},{8,16},{12,20},{16,24},{20,28},{24,0},{28,4},{1,9},{5... | collective-permute-start | bytes 393224 | tf_op jit(solution)/shard_map/ppermute | solution.py:321
  36.1 0.1 shard_map.111
  36.1 2.9 %collective-permute-start.11 = (bf16[256,256]{1,0:T(8,128)(2,1)S(1)}, bf16[256,256]{1,0:T(8,128)(2,1)S(1)}, u32[]{:S(2)}, u32[]{:S(2)}) collective-permute-start(bf16[256,256]{1,0:T(8,128)(2,1)S(1)} %shard_map.111), channel_id=1, source_target_pairs={{0,8},{4,12},{8,16},{12,20},{16,24},{20,28},{24,0},{28,4},{1,9},{5... | collective-permute-start | bytes 393224 | tf_op jit(solution)/shard_map/ppermute | solution.py:321
  39.0 3.0 %shard_map.109 = (f32[512,256]{1,0:T(8,128)S(1)}, f32[512,256]{1,0:T(8,128)S(1)}, f32[256,256]{1,0:T(8,128)S(1)}, f32[256,256]{1,0:T(8,128)S(1)}) custom-call(bf16[256,256]{1,0:T(8,128)(2,1)S(1)} %get-tuple-element.46.k_ref, bf16[256,256]{1,0:T(8,128)(2,1)} %v_ref.1, bf16[256,1024]{1,0:T(8,128)(2,1)S(1)} %get-tuple-element.35.refs_2_.refs_3_.refs_4_.qr_ref, ...), custom_call_target="tpu_custom_call" | custom-call | flops 1048576 | bytes 11070000 | tf_op jit(solution)/shard_map/pallas_call | solution.py:395
  42.1 1.1 %shard_map.110 = (bf16[256,1024]{1,0:T(8,128)(2,1)}, f32[256,256]{1,0:T(8,128)S(1)}, f32[256,256]{1,0:T(8,128)S(1)}) custom-call(f32[128,256]{1,0:T(8,128)S(1)} %get-tuple-element.33.tables_ref, f32[512,256]{1,0:T(8,128)S(1)} %get-tuple-element.50.refs_0_, f32[512,256]{1,0:T(8,128)S(1)} %get-tuple-element.51.refs_1_, ...), custom_call_target="tpu_custom_call" | custom-call | flops 1048576 | bytes 3690000 | tf_op jit(solution)/shard_map/pallas_call | solution.py:402
  43.2 1.0 %collective-permute-done.11.refs_2_ = bf16[256,256]{1,0:T(8,128)(2,1)S(1)} collective-permute-done((bf16[256,256]{1,0:T(8,128)(2,1)S(1)}, bf16[256,256]{1,0:T(8,128)(2,1)S(1)}, u32[]{:S(2)}, u32[]{:S(2)}) %collective-permute-start.11) | collective-permute-done | bytes 131104 | tf_op jit(solution)/shard_map/ppermute | solution.py:321
  44.2 0.9 %shard_map.113 = (bf16[256,256]{1,0:T(8,128)(2,1)}, bf16[256,256]{1,0:T(8,128)(2,1)}) custom-call(f32[128,256]{1,0:T(8,128)S(1)} %get-tuple-element.33.tables_ref, f32[256,256]{1,0:T(8,128)S(1)} %get-tuple-element.55.refs_0_, f32[256,256]{1,0:T(8,128)S(1)} %get-tuple-element.56.refs_1_, bf16[256,256]{1,0:T(8,128)(2,1)S(1)} %collective-permute-done.11.refs_2_, ...), custom_call_target="tpu_custom_call" | custom-call | flops 1048576 | bytes 3690000 | tf_op jit(solution)/shard_map/pallas_call | solution.py:414
  (9 shorter events, 0.0 us)
Async XLA Ops:
  0.6 9.0 %collective-permute-start = (s32[3,64]{1,0:T(4,128)}, s32[3,64]{1,0:T(4,128)S(1)}, u32[]{:S(2)}, u32[]{:S(2)}) collective-permute-start(s32[3,64]{1,0:T(4,128)} %own_ref.1), channel_id=1, source_target_pairs={{0,1},{1,2},{2,3},{3,0},{4,5},{5,6},{6,7},{7,4},{8,9},{9,10},{10,1... | collective-permute-start | bytes 2312 | tf_op jit(solution)/shard_map/ppermute | solution.py:321
  1.1 8.5 %collective-permute-start.1 = (s32[3,64]{1,0:T(4,128)}, s32[3,64]{1,0:T(4,128)S(1)}, u32[]{:S(2)}, u32[]{:S(2)}) collective-permute-start(s32[3,64]{1,0:T(4,128)} %own_ref.1), channel_id=1, source_target_pairs={{0,2},{1,3},{2,0},{3,1},{4,6},{5,7},{6,4},{7,5},{8,10},{9,11},{10,... | collective-permute-start | bytes 2312 | tf_op jit(solution)/shard_map/ppermute | solution.py:321
  3.7 6.0 %collective-permute-start.2 = (s32[3,64]{1,0:T(4,128)}, s32[3,64]{1,0:T(4,128)S(1)}, u32[]{:S(2)}, u32[]{:S(2)}) collective-permute-start(s32[3,64]{1,0:T(4,128)} %own_ref.1), channel_id=1, source_target_pairs={{0,3},{1,0},{2,1},{3,2},{4,7},{5,4},{6,5},{7,6},{8,11},{9,8},{10,9... | collective-permute-start | bytes 2312 | tf_op jit(solution)/shard_map/ppermute | solution.py:321
  5.1 9.8 %collective-permute-start.4 = (bf16[256,256]{1,0:T(8,128)(2,1)}, bf16[256,256]{1,0:T(8,128)(2,1)S(1)}, u32[]{:S(2)}, u32[]{:S(2)}) collective-permute-start(bf16[256,256]{1,0:T(8,128)(2,1)} %v_ref.1), channel_id=1, source_target_pairs={{0,28},{4,0},{8,4},{12,8},{16,12},{20,16},{24,20},{28,24},{1,29},{... | collective-permute-start | bytes 393224 | tf_op jit(solution)/shard_map/ppermute | solution.py:321
  10.9 5.2 %collective-permute-start.3 = (bf16[256,256]{1,0:T(8,128)(2,1)S(1)}, bf16[256,256]{1,0:T(8,128)(2,1)S(1)}, u32[]{:S(2)}, u32[]{:S(2)}) collective-permute-start(bf16[256,256]{1,0:T(8,128)(2,1)S(1)} %get-tuple-element.46.k_ref), channel_id=1, source_target_pairs={{0,28},{4,0},{8,4},{12,8},{16,12},{20,16},{24,20},{28,24},{1,29},{... | collective-permute-start | bytes 393224 | tf_op jit(solution)/shard_map/ppermute | solution.py:321
  14.9 8.7 %collective-permute-start.6 = (bf16[256,256]{1,0:T(8,128)(2,1)S(1)}, bf16[256,256]{1,0:T(8,128)(2,1)S(1)}, u32[]{:S(2)}, u32[]{:S(2)}) collective-permute-start(bf16[256,256]{1,0:T(8,128)(2,1)S(1)} %collective-permute-done.4.refs_1_), channel_id=1, source_target_pairs={{0,24},{4,28},{8,0},{12,4},{16,8},{20,12},{24,16},{28,20},{1,25},{... | collective-permute-start | bytes 393224 | tf_op jit(solution)/shard_map/ppermute | solution.py:321
  16.1 7.5 %collective-permute-start.5 = (bf16[256,256]{1,0:T(8,128)(2,1)S(1)}, bf16[256,256]{1,0:T(8,128)(2,1)S(1)}, u32[]{:S(2)}, u32[]{:S(2)}) collective-permute-start(bf16[256,256]{1,0:T(8,128)(2,1)S(1)} %collective-permute-done.3.refs_0_), channel_id=1, source_target_pairs={{0,24},{4,28},{8,0},{12,4},{16,8},{20,12},{24,16},{28,20},{1,25},{... | collective-permute-start | bytes 393224 | tf_op jit(solution)/shard_map/ppermute | solution.py:321
  17.5 6.0 %copy-start = (bf16[256,256]{1,0:T(8,128)(2,1)S(1)}, bf16[256,256]{1,0:T(8,128)(2,1)}, u32[]{:S(2)}) copy-start(bf16[256,256]{1,0:T(8,128)(2,1)} %v_ref.1) | copy-start | bytes 393220
  19.2 15.4 %collective-permute-start.9 = (bf16[256,512]{1,0:T(8,128)(2,1)S(1)}, bf16[256,512]{1,0:T(8,128)(2,1)S(1)}, u32[]{:S(2)}, u32[]{:S(2)}) collective-permute-start(bf16[256,512]{1,0:T(8,128)(2,1)S(1)} %get-tuple-element.45), channel_id=1, source_target_pairs={{0,4},{4,0},{8,12},{12,8},{16,20},{20,16},{24,28},{28,24},{1,5},{5... | collective-permute-start | bytes 786440 | tf_op jit(solution)/shard_map/ppermute | solution.py:326
  23.5 6.0 %collective-permute-start.8 = (bf16[256,256]{1,0:T(8,128)(2,1)S(1)}, bf16[256,256]{1,0:T(8,128)(2,1)S(1)}, u32[]{:S(2)}, u32[]{:S(2)}) collective-permute-start(bf16[256,256]{1,0:T(8,128)(2,1)S(1)} %copy-done), channel_id=1, source_target_pairs={{0,24},{4,28},{8,0},{12,4},{16,8},{20,12},{24,16},{28,20},{1,25},{... | collective-permute-start | bytes 393224 | tf_op jit(solution)/shard_map/ppermute | solution.py:321
  23.5 7.4 %collective-permute-start.7 = (bf16[256,256]{1,0:T(8,128)(2,1)S(1)}, bf16[256,256]{1,0:T(8,128)(2,1)S(1)}, u32[]{:S(2)}, u32[]{:S(2)}) collective-permute-start(bf16[256,256]{1,0:T(8,128)(2,1)S(1)} %get-tuple-element.46.k_ref), channel_id=1, source_target_pairs={{0,24},{4,28},{8,0},{12,4},{16,8},{20,12},{24,16},{28,20},{1,25},{... | collective-permute-start | bytes 393224 | tf_op jit(solution)/shard_map/ppermute | solution.py:321
  24.5 10.0 %collective-permute-start.12 = (bf16[256,256]{1,0:T(8,128)(2,1)S(1)}, bf16[256,256]{1,0:T(8,128)(2,1)S(1)}, u32[]{:S(2)}, u32[]{:S(2)}) collective-permute-start(bf16[256,256]{1,0:T(8,128)(2,1)S(1)} %get-tuple-element.60), channel_id=1, source_target_pairs={{0,4},{4,8},{8,12},{12,16},{16,20},{20,24},{24,28},{28,0},{1,5},{5... | collective-permute-start | bytes 393224 | tf_op jit(solution)/shard_map/ppermute | solution.py:321
  27.5 8.6 %collective-permute-start.10 = (bf16[256,256]{1,0:T(8,128)(2,1)S(1)}, bf16[256,256]{1,0:T(8,128)(2,1)S(1)}, u32[]{:S(2)}, u32[]{:S(2)}) collective-permute-start(bf16[256,256]{1,0:T(8,128)(2,1)S(1)} %get-tuple-element.58), channel_id=1, source_target_pairs={{0,4},{4,8},{8,12},{12,16},{16,20},{20,24},{24,28},{28,0},{1,5},{5... | collective-permute-start | bytes 393224 | tf_op jit(solution)/shard_map/ppermute | solution.py:321
  34.6 8.6 %collective-permute-start.13 = (bf16[256,256]{1,0:T(8,128)(2,1)S(1)}, bf16[256,256]{1,0:T(8,128)(2,1)S(1)}, u32[]{:S(2)}, u32[]{:S(2)}) collective-permute-start(bf16[256,256]{1,0:T(8,128)(2,1)S(1)} %shard_map.112), channel_id=1, source_target_pairs={{0,8},{4,12},{8,16},{12,20},{16,24},{20,28},{24,0},{28,4},{1,9},{5... | collective-permute-start | bytes 393224 | tf_op jit(solution)/shard_map/ppermute | solution.py:321
  36.1 8.1 %collective-permute-start.11 = (bf16[256,256]{1,0:T(8,128)(2,1)S(1)}, bf16[256,256]{1,0:T(8,128)(2,1)S(1)}, u32[]{:S(2)}, u32[]{:S(2)}) collective-permute-start(bf16[256,256]{1,0:T(8,128)(2,1)S(1)} %shard_map.111), channel_id=1, source_target_pairs={{0,8},{4,12},{8,16},{12,20},{16,24},{20,28},{24,0},{28,4},{1,9},{5... | collective-permute-start | bytes 393224 | tf_op jit(solution)/shard_map/ppermute | solution.py:321
